TPU v7x, 32 devices: a whole 2x2x4 slice. The times are simulated.
32 devices in a mesh: grp: 4 (over x, core), vocab: 8 (over z, y).
Axes of the slice: x: 2, y: 2, z: 4, core: 2. Of those that a mesh axis runs over, the one named last changes fastest.
Arguments:
- hidden: bfloat16 [512, 3584], P('grp'), may hold values from -300 to 300
- token_ids: int32 [512], P('grp'), may hold values from 0 to 16383
- serving: int32 [512], replicated, may hold values from 0 to 511, each once
- head_weight: bfloat16 [3584, 16384], P(None, ('grp', 'vocab')), may hold values from -0.3125 to 0.3125
- teacher_logits: bfloat16 [512, 4, 4096], P('grp', None, 'vocab'), may hold values from -300 to 300
Outputs:
- grad_hidden: float32 [512, 3584], P(('grp', 'vocab'))
- grad_head: bfloat16 [3584, 16384], P(None, ('grp', 'vocab'))
All inputs are finite; a program needn't handle non-finite values.
Results may differ from a plain program's by a relative error of at most 0.012.
Values may be sent and summed in bfloat16 or wider, within the bound.
No kernel may reach another device: no remote copies, remote signals or barrier semaphores. Data moves between devices by JAX's collectives and lax.ppermute only.
A program may use at most 128 MiB of HBM per device.

v0:
```python
import jax
import jax.numpy as jnp
from jax import lax
from jax.sharding import PartitionSpec as P

smoothing_divisor = 2.0
imitation_mixing_coefficient = 0.5
objective_scaling_factor = 32.0


def body(hidden, token_ids, serving, head_weight, teacher_logits):
    rows_all, ids_all = (
        lax.all_gather(hidden, "grp", axis=0, tiled=True),
        lax.all_gather(token_ids, "grp", axis=0, tiled=True),
    )
    groups = lax.axis_size("grp")
    shards = lax.axis_size("vocab")
    arrived = lax.all_to_all(teacher_logits, "grp", split_axis=1, concat_axis=0, tiled=True)
    per_group = arrived.shape[0] // groups
    shard_cols = head_weight.shape[1]
    mentor_activations = arrived.reshape(groups * per_group, shard_cols)[serving].astype(
        jnp.float32
    )
    logits = jnp.dot(rows_all, head_weight, preferred_element_type=jnp.float32)
    local_peak = jnp.max(logits, axis=1)
    local_tpeak = jnp.max(mentor_activations, axis=1)
    student_peak, mentor_peak_activation = lax.pmax((local_peak, local_tpeak), ("grp", "vocab"))
    shifted_pupil_activations = logits - student_peak[:, None]
    mentor_shifted_activations = (
        mentor_activations - mentor_peak_activation[:, None]
    ) / smoothing_divisor
    sum_hard, mentor_component_accumulated, mentor_exponential_summed = lax.psum(
        (
            jnp.sum(jnp.exp(shifted_pupil_activations), axis=1),
            jnp.sum(jnp.exp(shifted_pupil_activations / smoothing_divisor), axis=1),
            jnp.sum(jnp.exp(mentor_shifted_activations), axis=1),
        ),
        ("grp", "vocab"),
    )
    first_col = (lax.axis_index("grp") * shards + lax.axis_index("vocab")) * shard_cols
    columns = first_col + jnp.arange(shard_cols, dtype=jnp.int32)
    labels = (ids_all[:, None] == columns[None, :]).astype(jnp.float32)
    mentor_match_component = (
        jnp.exp(shifted_pupil_activations / smoothing_divisor)
        / mentor_component_accumulated[:, None]
        - jnp.exp(mentor_shifted_activations) / mentor_exponential_summed[:, None]
    )
    ground_truth_component = jnp.exp(shifted_pupil_activations) / sum_hard[:, None] - labels
    activation_derivative = (
        objective_scaling_factor
        * (
            imitation_mixing_coefficient * smoothing_divisor * mentor_match_component
            + (1.0 - imitation_mixing_coefficient) * ground_truth_component
        )
    ).astype(jnp.bfloat16)
    grad_head = lax.dot_general(
        rows_all,
        activation_derivative,
        (((0,), (0,)), ((), ())),
        preferred_element_type=jnp.float32,
    ).astype(jnp.bfloat16)
    grad_hidden = lax.psum_scatter(
        lax.dot_general(
            activation_derivative,
            head_weight,
            (((1,), (1,)), ((), ())),
            preferred_element_type=jnp.float32,
        ),
        ("grp", "vocab"),
        scatter_dimension=0,
        tiled=True,
    )
    return (grad_hidden, grad_head)


def solution(mesh):
    placed = (P("grp", None), P("grp"), P(), P(None, ("grp", "vocab")), P("grp", None, "vocab"))
    return jax.shard_map(
        body,
        mesh=mesh,
        in_specs=placed,
        out_specs=(P(("grp", "vocab"), None), P(None, ("grp", "vocab"))),
        check_vma=False,
    )
```

profile of v0, /device:TPU:0, one launch (start us, length us, event | category | flops | bytes accessed | tf_op | source)
XLA Modules:
  0.0 309.5 jit_solution(3984622040751088887)
XLA Ops:
  7.2 0.0 all-gather.3.cloned.1.call-start
  7.2 0.7 all-gather.3.cloned.1.call-update
  7.9 1.9 copy.10
  9.8 4.2 %all-to-all-start = ((bf16[128,4,512]{2,0,1:T(8,128)(2,1)}), bf16[128,4,512]{2,0,1:T(8,128)(2,1)S(1)}, u32[]{:S(2)}, u32[]{:S(2)}) async-start(bf16[128,4,512]{2,0,1:T(8,128)(2,1)} %copy.10), calls=%async_computation | async-start | bytes 1048576 | tf_op jit(solution)/shard_map/all_to_all | solution.py:18
  14.0 0.0 reduce-scatter.2.cloned.1.call-start
  14.0 10.3 %all-gather = s32[4,1,128]{2,1,0:T(1,128)S(1)} all-gather(s32[1,1,128]{2,1,0:T(1,128)} %bitcast.16), channel_id=1, replica_groups=mesh['grp'=4,'vocab'=8] {'grp'}, dimensions={0}, use_global_device_ids=true | all-gather | bytes 2560 | tf_op jit(solution)/shard_map/all_gather | solution.py:14
  24.3 0.7 compare_select_fusion
  25.0 0.0 all-to-all-done
  25.0 2.0 gather_fusion
  27.0 0.2 copy.11
  27.2 0.2 reduce_max.24
  27.4 16.8 %all-gather.3.cloned.1.call-done = bf16[512,3584]{1,0:T(8,128)(2,1)} async-done(((bf16[128,3584]{1,0:T(8,128)(2,1)}), bf16[512,3584]{1,0:T(8,128)(2,1)}) %all-gather.3.cloned.1.call-update) | async-done | bytes 3670032 | tf_op jit(solution)/shard_map/all_gather | solution.py:13
  44.1 5.3 %fusion.4 = (f32[512]{0:T(512)S(1)}, f32[512,512]{0,1:T(8,128)S(1)}) fusion(bf16[512,3584]{1,0:T(8,128)(2,1)} %all-gather.3.cloned.1.call-done, bf16[3584,512]{1,0:T(8,128)(2,1)} %param.8), kind=kOutput, calls=%fused_computation.13 | convolution fusion | flops 1879309824 | bytes 8390656 | tf_op jit(solution)/shard_map/dot_general | solution.py:24
  49.4 40.3 %all-reduce.1 = (f32[512]{0:T(512)S(1)}, f32[512]{0:T(512)S(1)}) all-reduce(f32[512]{0:T(512)S(1)} %get-tuple-element.13, bf16[512]{0:T(512)(128)(2,1)S(1)} %reduce_max.24), channel_id=1, replica_groups=mesh['grp'=4,'vocab'=8] {'grp','vocab'}, use_global_device_ids=true, to_apply=%region_1.0 | all-reduce | flops 1024 | bytes 7168 | tf_op jit(solution)/shard_map/pmax | solution.py:27
  89.7 0.5 fusion.2
  90.2 41.1 %all-reduce = (f32[512]{0:T(512)S(1)}, f32[512]{0:T(512)S(1)}, f32[512]{0:T(512)S(1)}) all-reduce(f32[512]{0:T(512)S(1)} %get-tuple-element.7, f32[512]{0:T(512)S(1)} %get-tuple-element.15, f32[512]{0:T(512)S(1)} %get-tuple-element.6), channel_id=1, replica_groups=mesh['grp'=4,'vocab'=8] {'grp','vocab'}, use_global_device_ids=true, to_apply=%region_9.0 | all-reduce | flops 1536 | bytes 12288 | tf_op jit(solution)/shard_map/psum | solution.py:32
  131.3 7.7 %fusion.3 = f32[512,3584]{1,0:T(8,128)} fusion(bf16[3584,512]{1,0:T(8,128)(2,1)} %param.8, bf16[512,512]{0,1:T(8,128)(2,1)S(1)} %copy.11, f32[512,512]{0,1:T(8,128)S(1)} %get-tuple-element.14, s32[512]{0:T(512)S(1)} %bitcast.14, f32[512]{0:T(512)S(1)} %get-tuple-element.8, f32[512]{0:T(512)S(1)} %get-tuple-element.9, f32[512]{0:T(512)S(1)} %get-tuple-element.12, ...), kind=kOutput, calls=%fused_computation.12 | convolution fusion | flops 1883242496 | bytes 12597248 | tf_op jit(solution)/shard_map/dot_general | solution.py:63
  139.0 0.0 reduce-scatter.2.cloned.1.call-update
  139.0 6.6 %fusion = bf16[3584,512]{0,1:T(8,128)(2,1)} fusion(bf16[512,3584]{1,0:T(8,128)(2,1)} %all-gather.3.cloned.1.call-done, bf16[512,512]{0,1:T(8,128)(2,1)S(1)} %copy.11, f32[512,512]{0,1:T(8,128)S(1)} %get-tuple-element.14, s32[512]{0:T(512)S(1)} %bitcast.15, f32[512]{0:T(512)S(1)} %get-tuple-element.8, f32[512]{0:T(512)S(1)} %get-tuple-element.9, ...), kind=kOutput, calls=%fused_computation.2 | convolution fusion | flops 1885077504 | bytes 8927232 | tf_op jit(solution)/shard_map/dot_general | solution.py:56
  145.6 5.9 %copy.12 = bf16[3584,512]{1,0:T(8,128)(2,1)} copy(bf16[3584,512]{0,1:T(8,128)(2,1)} %fusion) | data formatting | bytes 7340032
  151.5 151.1 %reduce-scatter.2.cloned.1.call-done = f32[16,3584]{1,0:T(8,128)} async-done(((f32[512,3584]{1,0:T(8,128)}), f32[16,3584]{1,0:T(8,128)}) %reduce-scatter.2.cloned.1.call-update) | async-done | bytes 229392 | tf_op jit(solution)/shard_map/reduce_scatter | solution.py:62
  (2 shorter events, 0.0 us)
Async XLA Ops:
  7.2 37.0 %all-gather.3.cloned.1.call-start = ((), (), s32[]{:S(2)}) async-start(), calls=%async_computation.2 | async-start | bytes 4587520 | tf_op jit(solution)/shard_map/all_gather | solution.py:13
  9.8 15.2 %all-to-all-start = ((bf16[128,4,512]{2,0,1:T(8,128)(2,1)}), bf16[128,4,512]{2,0,1:T(8,128)(2,1)S(1)}, u32[]{:S(2)}, u32[]{:S(2)}) async-start(bf16[128,4,512]{2,0,1:T(8,128)(2,1)} %copy.10), calls=%async_computation | async-start | bytes 1048576 | tf_op jit(solution)/shard_map/all_to_all | solution.py:18
  14.0 288.6 %reduce-scatter.2.cloned.1.call-start = ((), (), s32[]{:S(2)}) async-start(), calls=%async_computation.3 | async-start | bytes 7569408 | tf_op jit(solution)/shard_map/reduce_scatter | solution.py:62
Sparse Core Ops, SparseCore 0:
  9.6 34.5 all-gather.2
  139.1 163.4 reduce-scatter.1
where the time goes:
time: 310 us
  waiting for transfers between devices  169 us (55%)
  blocking collectives  91.7 us (30%)
  matrix products  19.6 us (6%)
  between operations  14.1 us (5%)
  local copies, waits for them, and re-layouts  10 us (3%)
  starting transfers between devices  4.25 us (1%)
    reduce_scatter x1, waiting for transfers between devices, body(): lax.psum_scatter(lax.dot_general(activation_derivative, head_weight, (((1...  151 us
    psum x1, blocking collectives, body(): lax.psum((jnp.sum(jnp.exp(shifted_pupil_activations), axis=1), jnp.sum(jn...  41.1 us
    pmax x1, blocking collectives, body(): lax.pmax((local_peak, local_tpeak), ('grp', 'vocab'))  40.3 us
    all_gather x1, waiting for transfers between devices, body(): lax.all_gather(hidden, 'grp', axis=0, tiled=True)  16.8 us
    all_gather x1, blocking collectives, body(): lax.all_gather(token_ids, 'grp', axis=0, tiled=True)  10.3 us
    unnamed x2, local copies, waits for them, and re-layouts  7.85 us
    dot_general x1, matrix products, body(): lax.dot_general(activation_derivative, head_weight, (((1,), (1,)), ((), (...  7.69 us
    dot_general x1, matrix products, body(): lax.dot_general(rows_all, activation_derivative, (((0,), (0,)), ((), ()))...  6.6 us
  transfers between devices with their start and end apart: 3, of which 2 were waited for; matrix products, arithmetic and copies ran while one was open for 6% of the time, Pallas kernels for 0%

commit v1 on v0

v1 whole, which is shorter than its diff:
```python
import jax
import jax.numpy as jnp
from jax import lax
from jax.sharding import PartitionSpec as P

BF16 = jnp.bfloat16
F32 = jnp.float32


def swap(value, axis, mask):
    count = lax.axis_size(axis)
    return lax.ppermute(value, axis, [(i, i ^ mask) for i in range(count)])


def body(hidden, token_ids, serving, head_weight, teacher_logits):
    groups = lax.axis_size("grp")
    shards = lax.axis_size("vocab")
    me_g = lax.axis_index("grp")
    me_v = lax.axis_index("vocab")
    per = hidden.shape[0]
    depth = hidden.shape[1]
    cols = head_weight.shape[1]

    arrived = lax.all_to_all(teacher_logits, "grp", split_axis=1, concat_axis=0, tiled=True)
    from_x = swap(hidden, "grp", 2)
    from_core = swap(hidden, "grp", 1)
    from_diag = swap(from_x, "grp", 1)
    ids_x = swap(token_ids, "grp", 2)
    ids_pair = jnp.concatenate([token_ids, ids_x])
    ids_core = swap(ids_pair, "grp", 1)
    ids = jnp.concatenate([token_ids, ids_core[:per], ids_x, ids_core[per:]])
    rows = [hidden, from_core, from_x, from_diag]

    order = me_g ^ jnp.arange(groups, dtype=jnp.int32)
    serving_rel = serving.reshape(groups, per)[order].reshape(-1)
    aligned = arrived.reshape(groups * per, cols)[serving_rel].astype(F32)

    logits = jnp.concatenate(
        [jnp.dot(block, head_weight, preferred_element_type=F32) for block in rows]
    )
    peak = jnp.max(logits, axis=1)
    tpeak = jnp.max(aligned, axis=1)
    shifted = logits - peak[:, None]
    tshifted = (aligned - tpeak[:, None]) * 0.5
    stats = jnp.stack(
        [
            peak,
            jnp.sum(jnp.exp(shifted), axis=1),
            jnp.sum(jnp.exp(shifted * 0.5), axis=1),
            tpeak,
            jnp.sum(jnp.exp(tshifted), axis=1),
        ]
    )
    stats = stats.reshape(5, groups, per).swapaxes(0, 1)[order]
    everyone = lax.all_to_all(
        jnp.broadcast_to(stats[None], (groups * shards,) + stats.shape),
        ("grp", "vocab"),
        split_axis=0,
        concat_axis=0,
        tiled=True,
    )
    everyone = everyone[:, order]
    peaks, hards, softs, tpeaks, tsums = [
        everyone[:, :, k].reshape(groups * shards, groups * per) for k in range(5)
    ]
    top = jnp.max(peaks, axis=0)
    ttop = jnp.max(tpeaks, axis=0)
    hard = jnp.sum(hards * jnp.exp(peaks - top), axis=0)
    soft = jnp.sum(softs * jnp.exp((peaks - top) * 0.5), axis=0)
    tsum = jnp.sum(tsums * jnp.exp((tpeaks - ttop) * 0.5), axis=0)

    first = (me_g * shards + me_v) * cols
    columns = first + jnp.arange(cols, dtype=jnp.int32)
    labels = (ids[:, None] == columns[None, :]).astype(F32)
    moved = logits - top[:, None]
    grad = (
        32.0
        * (
            jnp.exp(moved * 0.5) / soft[:, None]
            - jnp.exp((aligned - ttop[:, None]) * 0.5) / tsum[:, None]
            + 0.5 * (jnp.exp(moved) / hard[:, None] - labels)
        )
    ).astype(BF16)

    blocks = grad.reshape(groups, per, cols)

    def back(j):
        return lax.dot_general(
            blocks[j], head_weight, (((1,), (1,)), ((), ())), preferred_element_type=F32
        )

    far = swap(back(3).astype(BF16), "grp", 1)
    near = swap(back(1).astype(BF16), "grp", 1)
    across = swap((back(2) + far.astype(F32)).astype(BF16), "grp", 2)
    mine = (back(0) + near.astype(F32) + across.astype(F32)).astype(BF16)
    parts = lax.all_to_all(
        mine.reshape(shards, per // shards, depth), "vocab", split_axis=0, concat_axis=0, tiled=True
    )
    grad_hidden = jnp.sum(parts.astype(F32), axis=0)

    grad_head = lax.dot_general(
        jnp.concatenate(rows),
        grad,
        (((0,), (0,)), ((), ())),
        preferred_element_type=F32,
    ).astype(BF16)
    return (grad_hidden, grad_head)


def solution(mesh):
    placed = (P("grp", None), P("grp"), P(), P(None, ("grp", "vocab")), P("grp", None, "vocab"))
    return jax.shard_map(
        body,
        mesh=mesh,
        in_specs=placed,
        out_specs=(P(("grp", "vocab"), None), P(None, ("grp", "vocab"))),
        check_vma=False,
    )
```

time: 310 us -> 119 us (0.38)
  waiting for transfers between devices: 169 us -> 65.6 us
  blocking collectives: 91.7 us -> 0 us
  starting transfers between devices: 4.25 us -> 19.2 us
  between operations: 14.1 us -> 0.97 us
  local copies, waits for them, and re-layouts: 10 us -> 6.45 us
  other arithmetic: 1.34 us -> 4.77 us
    reduce_scatter x1 -> x0, waiting for transfers between devices: 151 us -> none  [body(): lax.psum_scatter(lax.dot_general(activation_derivative, head_weight, (((1...]
    psum x1 -> x0, blocking collectives: 41.1 us -> none  [body(): lax.psum((jnp.sum(jnp.exp(shifted_pupil_activations), axis=1), jnp.sum(jn...]
    pmax x1 -> x0, blocking collectives: 40.3 us -> none  [body(): lax.pmax((local_peak, local_tpeak), ('grp', 'vocab'))]
    ppermute x0 -> x8, waiting for transfers between devices: none -> 36.7 us  [swap(): return lax.ppermute(value, axis, [(i, i ^ mask) for i in range(count)])]
    all_to_all x0 -> x2, waiting for transfers between devices: none -> 24.2 us  [the longest x1 17.1 us: body(): lax.all_to_all(mine.reshape(shards, per // shards, depth), 'vocab', split...]
    all_gather x1 -> x0, waiting for transfers between devices: 16.8 us -> none  [body(): lax.all_gather(hidden, 'grp', axis=0, tiled=True)]
    all_gather x1 -> x0, blocking collectives: 10.3 us -> none  [body(): lax.all_gather(token_ids, 'grp', axis=0, tiled=True)]
    all_to_all x0 -> x2, starting transfers between devices: none -> 9.66 us  [the longest x1 6.11 us: body(): lax.all_to_all(jnp.broadcast_to(stats[None], (groups * shards,) + stats.s...]
  transfers between devices with their start and end apart: 3 -> 11, of which waited for: 2 -> 8; matrix products, arithmetic and copies ran while one was open for 6% -> 18% of each run, Pallas kernels for 0% -> 0%
where the time goes in v1:
time: 119 us; the launch traced here: 118 us
  waiting for transfers between devices  65.6 us (55%)
  matrix products  21.3 us (18%)
  starting transfers between devices  19.2 us (16%)
  local copies, waits for them, and re-layouts  6.45 us (5%)
  other arithmetic  4.77 us (4%)
    ppermute x8, waiting for transfers between devices, swap(): return lax.ppermute(value, axis, [(i, i ^ mask) for i in range(count)])  36.7 us
    all_to_all x1, waiting for transfers between devices, body(): lax.all_to_all(mine.reshape(shards, per // shards, depth), 'vocab', split...  17.1 us
    dot_general x4, matrix products, body(): jnp.dot(block, head_weight, preferred_element_type=F32)  8.3 us
    dot_general x4, matrix products, back(): lax.dot_general(blocks[j], head_weight, (((1,), (1,)), ((), ())), preferr...  7.29 us
    all_to_all x1, waiting for transfers between devices, body(): lax.all_to_all(jnp.broadcast_to(stats[None], (groups * shards,) + stats.s...  7.06 us
    all_to_all x1, starting transfers between devices, body(): lax.all_to_all(jnp.broadcast_to(stats[None], (groups * shards,) + stats.s...  6.11 us
    ppermute x8, starting transfers between devices, swap(): return lax.ppermute(value, axis, [(i, i ^ mask) for i in range(count)])  6.08 us
    dot_general x1, matrix products, body(): lax.dot_general(jnp.concatenate(rows), grad, (((0,), (0,)), ((), ())), pr...  5.69 us
  transfers between devices with their start and end apart: 11, of which 8 were waited for; matrix products, arithmetic and copies ran while one was open for 18% of the time, Pallas kernels for 0%

profile of v1, /device:TPU:0, one launch (start us, length us, event | category | flops | bytes accessed | tf_op | source)
XLA Modules:
  0.0 118.3 jit_solution(12402256498382676165)
XLA Ops:
  0.6 0.0 copy-start
  0.6 3.0 %collective-permute-start.1 = (bf16[128,3584]{1,0:T(8,128)(2,1)}, bf16[128,3584]{1,0:T(8,128)(2,1)S(1)}, u32[]{:S(2)}, u32[]{:S(2)}) collective-permute-start(bf16[128,3584]{1,0:T(8,128)(2,1)} %param.5), channel_id=1, source_target_pairs={{0,16},{8,24},{16,0},{24,8},{1,17},{9,25},{17,1},{25,9},{2,18},{10... | collective-permute-start | bytes 2752520 | tf_op jit(solution)/shard_map/ppermute | solution.py:12
  3.6 0.0 collective-permute-start
  3.7 1.9 %copy.12 = bf16[128,4,512]{2,0,1:T(8,128)(2,1)} copy(bf16[128,4,512]{2,1,0:T(4,128)(2,1)} %param.9) | data formatting | bytes 1048576 | tf_op args[4]
  5.6 3.5 %all-to-all-start = ((bf16[128,4,512]{2,0,1:T(8,128)(2,1)}), bf16[128,4,512]{2,0,1:T(8,128)(2,1)S(1)}, u32[]{:S(2)}, u32[]{:S(2)}) async-start(bf16[128,4,512]{2,0,1:T(8,128)(2,1)} %copy.12), calls=%async_computation | async-start | bytes 1048576 | tf_op jit(solution)/shard_map/all_to_all | solution.py:24
  9.1 3.0 %fusion.32 = f32[128,512]{1,0:T(8,128)S(1)} fusion(bf16[128,3584]{1,0:T(8,128)(2,1)} %param.5, bf16[3584,512]{1,0:T(8,128)(2,1)} %param.8), kind=kOutput, calls=%fused_computation.58 | convolution fusion | flops 469762048 | bytes 4849664 | tf_op jit(solution)/shard_map/dot_general | solution.py:39
  12.1 0.0 copy-done
  12.1 0.6 gather_fusion
  12.6 12.4 %collective-permute-done.1 = bf16[128,3584]{1,0:T(8,128)(2,1)S(1)} collective-permute-done((bf16[128,3584]{1,0:T(8,128)(2,1)}, bf16[128,3584]{1,0:T(8,128)(2,1)S(1)}, u32[]{:S(2)}, u32[]{:S(2)}) %collective-permute-start.1) | collective-permute-done | bytes 917536 | tf_op jit(solution)/shard_map/ppermute | solution.py:12
  25.0 0.0 copy-start.4
  25.0 0.0 collective-permute-start.2
  25.1 4.8 %all-to-all-done = bf16[128,4,512]{2,0,1:T(8,128)(2,1)S(1)} async-done(((bf16[128,4,512]{2,0,1:T(8,128)(2,1)}), bf16[128,4,512]{2,0,1:T(8,128)(2,1)S(1)}, u32[]{:S(2)}, u32[]{:S(2)}) %all-to-all-start) | async-done | bytes 524320 | tf_op jit(solution)/shard_map/all_to_all | solution.py:24
  29.8 2.0 %gather_fusion.1 = bf16[512,512]{1,0:T(8,128)(2,1)S(1)} fusion(bf16[512,512]{1,0:T(8,128)(2,1)S(1)} %bitcast.37, s32[1024]{0:T(1024)S(1)} %pad_clamp_fusion), kind=kCustom, calls=%fused_computation.1 | custom fusion | bytes 1050624 | tf_op jit(solution)/shard_map/gather | solution.py:36
  31.8 0.2 reduce_max.46
  32.0 0.0 copy-start.1
  32.0 0.4 fusion.9
  32.4 2.9 %fusion.34 = f32[128,512]{1,0:T(8,128)S(1)} fusion(bf16[128,3584]{1,0:T(8,128)(2,1)S(1)} %collective-permute-done.1, bf16[3584,512]{1,0:T(8,128)(2,1)} %param.8), kind=kOutput, calls=%fused_computation.60 | convolution fusion | flops 469762048 | bytes 4849664 | tf_op jit(solution)/shard_map/dot_general | solution.py:39
  35.3 0.0 collective-permute-done
  35.3 0.0 copy-done.1
  35.3 0.0 copy-start.5
  35.3 0.6 fusion.33
  35.9 0.0 copy-done.4
  35.9 0.0 copy-start.6
  36.0 0.0 collective-permute-done.2
  36.0 1.8 %fusion.35 = f32[128,512]{1,0:T(8,128)S(1)} fusion(bf16[128,3584]{1,0:T(8,128)(2,1)} %collective-permute-done.2, bf16[3584,512]{1,0:T(8,128)(2,1)S(1)} %copy-done.1), kind=kOutput, calls=%fused_computation.61 | convolution fusion | flops 469762048 | bytes 4849664 | tf_op jit(solution)/shard_map/dot_general | solution.py:39
  37.8 0.1 fusion.30
  37.9 0.6 exponential_reduce_fusion
  38.6 0.6 gather_fusion.2
  39.2 0.8 broadcast_in_dim.2
  39.9 6.1 %all-to-all-start.1 = ((f32[32,4,5,128]{3,1,2,0:T(4,128)}), f32[32,4,5,128]{3,1,2,0:T(4,128)S(1)}, u32[]{:S(2)}, u32[]{:S(2)}) async-start(f32[32,4,5,128]{3,1,2,0:T(4,128)} %broadcast_in_dim.2), calls=%async_computation.1 | async-start | bytes 655360 | tf_op jit(solution)/shard_map/all_to_all | solution.py:55
  46.1 0.0 copy-done.6
  46.1 1.8 %collective-permute-start.3 = (s32[128]{0:T(128)S(1)}, s32[128]{0:T(128)S(1)}, u32[]{:S(2)}, u32[]{:S(2)}) collective-permute-start(s32[128]{0:T(128)S(1)} %copy-done.6), channel_id=1, source_target_pairs={{0,16},{8,24},{16,0},{24,8},{1,17},{9,25},{17,1},{25,9},{2,18},{10... | collective-permute-start | bytes 1544 | tf_op jit(solution)/shard_map/ppermute | solution.py:12
  47.9 2.1 %collective-permute-done.3 = s32[128]{0:T(128)S(1)} collective-permute-done((s32[128]{0:T(128)S(1)}, s32[128]{0:T(128)S(1)}, u32[]{:S(2)}, u32[]{:S(2)}) %collective-permute-start.3) | collective-permute-done | bytes 544 | tf_op jit(solution)/shard_map/ppermute | solution.py:12
  50.0 0.0 collective-permute-start.4
  50.0 1.1 collective-permute-done.4
  51.1 7.1 %all-to-all-done.1 = f32[32,4,5,128]{3,1,2,0:T(4,128)S(1)} async-done(((f32[32,4,5,128]{3,1,2,0:T(4,128)}), f32[32,4,5,128]{3,1,2,0:T(4,128)S(1)}, u32[]{:S(2)}, u32[]{:S(2)}) %all-to-all-start.1) | async-done | bytes 327712 | tf_op jit(solution)/shard_map/all_to_all | solution.py:55
  58.2 0.6 gather_fusion.3
  58.8 0.0 copy-start.2
  58.9 0.1 fusion.27
  58.9 1.2 %fusion.16 = bf16[512,512]{1,0:T(8,128)(2,1)S(1)} fusion(bf16[512,512]{1,0:T(8,128)(2,1)S(1)} %gather_fusion.1, s32[512]{0:T(512)S(1)} %iota_add_fusion, f32[512]{0:T(512)S(1)} %bitcast.46, f32[512]{0:T(512)S(1)} %bitcast.47, f32[512]{0:T(512)S(1)} %bitcast.41, f32[512]{0:T(512)S(1)} %bitcast.45, f32[512]{0:T(512)S(1)} %bitcast.42, s32[512]{0:T(512)S(1)} %pad_add_fusion, ...), kind=kLoop, calls=%fused_computation.31 | loop fusion | flops 4980736 | bytes 2111488 | tf_op jit(solution)/shard_map/convert_element_type | solution.py:83
  60.2 3.3 %convolution_convert_fusion.1 = bf16[128,3584]{1,0:T(8,128)(2,1)S(1)} fusion(bf16[3584,512]{1,0:T(8,128)(2,1)} %param.8, bf16[512,512]{1,0:T(8,128)(2,1)S(1)} %fusion.16), kind=kOutput, calls=%fused_computation.5 | convolution fusion | flops 470220800 | bytes 4718592 | tf_op jit(solution)/shard_map/dot_general | solution.py:88
  63.5 0.1 collective-permute-start.6
  63.6 0.0 copy-done.2
  63.6 1.3 %convolution_convert_fusion.2 = bf16[128,3584]{1,0:T(8,128)(2,1)S(1)} fusion(bf16[3584,512]{1,0:T(8,128)(2,1)S(1)} %copy-done.2, bf16[512,512]{1,0:T(8,128)(2,1)S(1)} %fusion.16), kind=kOutput, calls=%fused_computation.6 | convolution fusion | flops 470220800 | bytes 4718592 | tf_op jit(solution)/shard_map/dot_general | solution.py:88
  64.9 0.0 copy-done.5
  64.9 0.6 collective-permute-start.5
  65.5 0.6 collective-permute-done.6
  66.1 1.3 %add_convert_fusion.1 = bf16[128,3584]{1,0:T(8,128)(2,1)S(1)} fusion(bf16[128,3584]{1,0:T(8,128)(2,1)S(1)} %collective-permute-done.6, bf16[3584,512]{1,0:T(8,128)(2,1)S(1)} %copy-done.2, bf16[512,512]{1,0:T(8,128)(2,1)S(1)} %fusion.16), kind=kOutput, calls=%fused_computation.16 | convolution fusion | flops 471138304 | bytes 5636096 | tf_op jit(solution)/shard_map/dot_general | solution.py:88
  67.4 0.6 collective-permute-start.7
  68.0 1.3 %fusion.23 = f32[128,3584]{1,0:T(8,128)S(1)} fusion(bf16[3584,512]{1,0:T(8,128)(2,1)S(1)} %copy-done.2, bf16[512,512]{1,0:T(8,128)(2,1)S(1)} %fusion.16), kind=kOutput, calls=%fused_computation.36 | convolution fusion | flops 469762048 | bytes 5636096 | tf_op jit(solution)/shard_map/dot_general | solution.py:88
  69.3 0.0 copy-start.3
  69.3 0.0 collective-permute-done.5
  69.3 20.5 %collective-permute-done.7 = bf16[128,3584]{1,0:T(8,128)(2,1)S(1)} collective-permute-done((bf16[128,3584]{1,0:T(8,128)(2,1)S(1)}, bf16[128,3584]{1,0:T(8,128)(2,1)S(1)}, u32[]{:S(2)}, u32[]{:S(2)}) %collective-permute-start.7) | collective-permute-done | bytes 917536 | tf_op jit(solution)/shard_map/ppermute | solution.py:12
  89.9 1.2 %add_convert_fusion = bf16[128,3584]{1,0:T(8,128)(2,1)} fusion(bf16[128,3584]{1,0:T(8,128)(2,1)S(1)} %collective-permute-done.7, f32[128,3584]{1,0:T(8,128)S(1)} %fusion.23, bf16[128,3584]{1,0:T(8,128)(2,1)S(1)} %collective-permute-done.5), kind=kLoop, calls=%fused_computation.15 | loop fusion | flops 2293760 | bytes 4587520 | tf_op jit(solution)/shard_map/convert_element_type | solution.py:95
  91.1 3.6 %all-to-all-start.2 = ((bf16[8,16,3584]{2,1,0:T(8,128)(2,1)}), bf16[8,16,3584]{2,1,0:T(8,128)(2,1)S(1)}, u32[]{:S(2)}, u32[]{:S(2)}) async-start(bf16[8,16,3584]{2,1,0:T(8,128)(2,1)} %bitcast.19), calls=%async_computation.2 | async-start | bytes 1835008 | tf_op jit(solution)/shard_map/all_to_all | solution.py:96
  94.7 0.0 copy-done.3
  94.7 5.7 %convolution_convert_fusion = bf16[3584,512]{1,0:T(8,128)(2,1)} fusion(bf16[512,512]{1,0:T(8,128)(2,1)S(1)} %fusion.16, bf16[128,3584]{1,0:T(8,128)(2,1)} %collective-permute-done.2, bf16[128,3584]{1,0:T(8,128)(2,1)} %copy-done.4, bf16[128,3584]{1,0:T(8,128)(2,1)} %copy-done.5, bf16[128,3584]{1,0:T(8,128)(2,1)S(1)} %copy-done.3), kind=kOutput, calls=%fused_computation.4 | convolution fusion | flops 1895563264 | bytes 7864320 | tf_op jit(solution)/shard_map/dot_general | solution.py:101
  100.3 17.1 %all-to-all-done.2 = bf16[8,16,3584]{2,1,0:T(8,128)(2,1)S(1)} async-done(((bf16[8,16,3584]{2,1,0:T(8,128)(2,1)}), bf16[8,16,3584]{2,1,0:T(8,128)(2,1)S(1)}, u32[]{:S(2)}, u32[]{:S(2)}) %all-to-all-start.2) | async-done | bytes 917536 | tf_op jit(solution)/shard_map/all_to_all | solution.py:96
  117.5 0.8 convert_reduce_fusion
  (13 shorter events, 0.1 us)
Async XLA Ops:
  0.6 11.4 %copy-start = (s32[512]{0:T(512)S(1)}, s32[512]{0:T(512)}, u32[]{:S(2)}) copy-start(s32[512]{0:T(512)} %param.7) | copy-start | bytes 6148
  0.6 24.4 %collective-permute-start.1 = (bf16[128,3584]{1,0:T(8,128)(2,1)}, bf16[128,3584]{1,0:T(8,128)(2,1)S(1)}, u32[]{:S(2)}, u32[]{:S(2)}) collective-permute-start(bf16[128,3584]{1,0:T(8,128)(2,1)} %param.5), channel_id=1, source_target_pairs={{0,16},{8,24},{16,0},{24,8},{1,17},{9,25},{17,1},{25,9},{2,18},{10... | collective-permute-start | bytes 2752520 | tf_op jit(solution)/shard_map/ppermute | solution.py:12
  3.6 31.6 %collective-permute-start = (bf16[128,3584]{1,0:T(8,128)(2,1)}, bf16[128,3584]{1,0:T(8,128)(2,1)S(1)}, u32[]{:S(2)}, u32[]{:S(2)}) collective-permute-start(bf16[128,3584]{1,0:T(8,128)(2,1)} %param.5), channel_id=1, source_target_pairs={{0,8},{8,0},{16,24},{24,16},{1,9},{9,1},{17,25},{25,17},{2,10},{10... | collective-permute-start | bytes 2752520 | tf_op jit(solution)/shard_map/ppermute | solution.py:12
  5.6 24.3 %all-to-all-start = ((bf16[128,4,512]{2,0,1:T(8,128)(2,1)}), bf16[128,4,512]{2,0,1:T(8,128)(2,1)S(1)}, u32[]{:S(2)}, u32[]{:S(2)}) async-start(bf16[128,4,512]{2,0,1:T(8,128)(2,1)} %copy.12), calls=%async_computation | async-start | bytes 1048576 | tf_op jit(solution)/shard_map/all_to_all | solution.py:24
  25.0 10.9 %copy-start.4 = (bf16[128,3584]{1,0:T(8,128)(2,1)}, bf16[128,3584]{1,0:T(8,128)(2,1)S(1)}, u32[]{:S(2)}) copy-start(bf16[128,3584]{1,0:T(8,128)(2,1)S(1)} %collective-permute-done.1) | copy-start | bytes 2752516
  25.0 10.9 %collective-permute-start.2 = (bf16[128,3584]{1,0:T(8,128)(2,1)S(1)}, bf16[128,3584]{1,0:T(8,128)(2,1)}, u32[]{:S(2)}, u32[]{:S(2)}) collective-permute-start(bf16[128,3584]{1,0:T(8,128)(2,1)S(1)} %collective-permute-done.1), channel_id=1, source_target_pairs={{0,8},{8,0},{16,24},{24,16},{1,9},{9,1},{17,25},{25,17},{2,10},{10... | collective-permute-start | bytes 2752520 | tf_op jit(solution)/shard_map/ppermute | solution.py:12
  32.0 3.3 %copy-start.1 = (bf16[3584,512]{1,0:T(8,128)(2,1)S(1)}, bf16[3584,512]{1,0:T(8,128)(2,1)}, u32[]{:S(2)}) copy-start(bf16[3584,512]{1,0:T(8,128)(2,1)} %param.8) | copy-start | bytes 11010052
  35.3 29.7 %copy-start.5 = (bf16[128,3584]{1,0:T(8,128)(2,1)}, bf16[128,3584]{1,0:T(8,128)(2,1)S(1)}, u32[]{:S(2)}) copy-start(bf16[128,3584]{1,0:T(8,128)(2,1)S(1)} %collective-permute-done) | copy-start | bytes 2752516
  35.9 10.1 %copy-start.6 = (s32[128]{0:T(128)S(1)}, s32[128]{0:T(128)}, u32[]{:S(2)}) copy-start(s32[128]{0:T(128)} %param.6) | copy-start | bytes 1540
  39.9 18.3 %all-to-all-start.1 = ((f32[32,4,5,128]{3,1,2,0:T(4,128)}), f32[32,4,5,128]{3,1,2,0:T(4,128)S(1)}, u32[]{:S(2)}, u32[]{:S(2)}) async-start(f32[32,4,5,128]{3,1,2,0:T(4,128)} %broadcast_in_dim.2), calls=%async_computation.1 | async-start | bytes 655360 | tf_op jit(solution)/shard_map/all_to_all | solution.py:55
  46.1 3.9 %collective-permute-start.3 = (s32[128]{0:T(128)S(1)}, s32[128]{0:T(128)S(1)}, u32[]{:S(2)}, u32[]{:S(2)}) collective-permute-start(s32[128]{0:T(128)S(1)} %copy-done.6), channel_id=1, source_target_pairs={{0,16},{8,24},{16,0},{24,8},{1,17},{9,25},{17,1},{25,9},{2,18},{10... | collective-permute-start | bytes 1544 | tf_op jit(solution)/shard_map/ppermute | solution.py:12
  50.0 1.1 collective-permute-start.4
  58.8 4.8 %copy-start.2 = (bf16[3584,512]{1,0:T(8,128)(2,1)S(1)}, bf16[3584,512]{1,0:T(8,128)(2,1)}, u32[]{:S(2)}) copy-start(bf16[3584,512]{1,0:T(8,128)(2,1)} %param.8) | copy-start | bytes 11010052
  63.5 2.5 %collective-permute-start.6 = (bf16[128,3584]{1,0:T(8,128)(2,1)S(1)}, bf16[128,3584]{1,0:T(8,128)(2,1)S(1)}, u32[]{:S(2)}, u32[]{:S(2)}) collective-permute-start(bf16[128,3584]{1,0:T(8,128)(2,1)S(1)} %convolution_convert_fusion.1), channel_id=1, source_target_pairs={{0,8},{8,0},{16,24},{24,16},{1,9},{9,1},{17,25},{25,17},{2,10},{10... | collective-permute-start | bytes 2752520 | tf_op jit(solution)/shard_map/ppermute | solution.py:12
  64.9 4.4 %collective-permute-start.5 = (bf16[128,3584]{1,0:T(8,128)(2,1)S(1)}, bf16[128,3584]{1,0:T(8,128)(2,1)S(1)}, u32[]{:S(2)}, u32[]{:S(2)}) collective-permute-start(bf16[128,3584]{1,0:T(8,128)(2,1)S(1)} %convolution_convert_fusion.2), channel_id=1, source_target_pairs={{0,8},{8,0},{16,24},{24,16},{1,9},{9,1},{17,25},{25,17},{2,10},{10... | collective-permute-start | bytes 2752520 | tf_op jit(solution)/shard_map/ppermute | solution.py:12
  67.4 22.5 %collective-permute-start.7 = (bf16[128,3584]{1,0:T(8,128)(2,1)S(1)}, bf16[128,3584]{1,0:T(8,128)(2,1)S(1)}, u32[]{:S(2)}, u32[]{:S(2)}) collective-permute-start(bf16[128,3584]{1,0:T(8,128)(2,1)S(1)} %add_convert_fusion.1), channel_id=1, source_target_pairs={{0,16},{8,24},{16,0},{24,8},{1,17},{9,25},{17,1},{25,9},{2,18},{10... | collective-permute-start | bytes 2752520 | tf_op jit(solution)/shard_map/ppermute | solution.py:12
  69.3 25.3 %copy-start.3 = (bf16[128,3584]{1,0:T(8,128)(2,1)S(1)}, bf16[128,3584]{1,0:T(8,128)(2,1)}, u32[]{:S(2)}) copy-start(bf16[128,3584]{1,0:T(8,128)(2,1)} %param.5) | copy-start | bytes 2752516
  91.1 26.4 %all-to-all-start.2 = ((bf16[8,16,3584]{2,1,0:T(8,128)(2,1)}), bf16[8,16,3584]{2,1,0:T(8,128)(2,1)S(1)}, u32[]{:S(2)}, u32[]{:S(2)}) async-start(bf16[8,16,3584]{2,1,0:T(8,128)(2,1)} %bitcast.19), calls=%async_computation.2 | async-start | bytes 1835008 | tf_op jit(solution)/shard_map/all_to_all | solution.py:96

commit v2 on v0

v2 whole, which is shorter than its diff:
```python
import jax
import jax.numpy as jnp
from jax import lax
from jax.experimental import pallas as pl
from jax.experimental.pallas import tpu as pltpu
from jax.sharding import PartitionSpec as P

BF16 = jnp.bfloat16
F32 = jnp.float32
AXES = ("grp", "vocab")
VMEM = pl.BlockSpec(memory_space=pltpu.VMEM)
SMEM = pl.BlockSpec(memory_space=pltpu.SMEM)
ANY = pl.BlockSpec(memory_space=pl.ANY)
PARAMS = pltpu.CompilerParams(vmem_limit_bytes=40 * 2**20)
STAT_ROWS = 8


def columns_to_rows(columns):
    count = columns[0].shape[0]
    lane = lax.broadcasted_iota(jnp.int32, (count, 128), 1)
    wide = jnp.zeros((count, 128), F32)
    for k, column in enumerate(columns):
        wide = jnp.where(lane == k, column, wide)
    return wide.T[:STAT_ROWS]


def teacher_kernel(me_ref, serving_ref, arrived_ref, aligned_ref, stats_ref):
    me = me_ref[0]
    groups, _, per = serving_ref.shape
    total = arrived_ref.shape[0]
    for j in range(groups):
        wanted = serving_ref[me ^ j]
        pick = (lax.broadcasted_iota(jnp.int32, (total, per), 0) == wanted).astype(BF16)
        rows = lax.dot_general(
            pick, arrived_ref[...], (((0,), (0,)), ((), ())), preferred_element_type=F32
        )
        aligned_ref[j] = rows.astype(BF16)
        peak = jnp.max(rows, axis=1, keepdims=True)
        part = jnp.sum(jnp.exp((rows - peak) * 0.5), axis=1, keepdims=True)
        stats_ref[:, j * per : (j + 1) * per] = columns_to_rows([peak, part])


def teacher_rows(me, serving, arrived, groups):
    total, cols = arrived.shape
    per = total // groups
    return pl.pallas_call(
        teacher_kernel,
        out_shape=(
            jax.ShapeDtypeStruct((groups, per, cols), BF16),
            jax.ShapeDtypeStruct((STAT_ROWS, total), F32),
        ),
        in_specs=[SMEM, VMEM, VMEM],
        out_specs=(VMEM, VMEM),
        compiler_params=PARAMS,
        cost_estimate=pl.CostEstimate(
            flops=2 * total * total * cols, bytes_accessed=2 * total * cols * 2, transcendentals=total * cols
        ),
        name="teacher_rows",
    )(me, serving.reshape(groups, 1, per), arrived)


def place_copies(pieces, places, full, sems):
    copies = []
    for k, (piece, place) in enumerate(zip(pieces, places)):
        count = piece.shape[0]
        start = place if isinstance(place, int) else pl.multiple_of(place, 16)
        copy = pltpu.make_async_copy(piece, full.at[pl.ds(start, count)], sems.at[k])
        copy.start()
        copies.append(copy)
    return copies


def logits_kernel(spots, splits, *refs):
    n = len(spots)
    at_ref, pieces, (w_ref, logits_ref, stats_ref, full, weights, sems, wsems) = (
        refs[0],
        refs[1 : 1 + n],
        refs[1 + n :],
    )
    places = [spot if isinstance(spot, int) else at_ref[spot[0]] for spot in spots]
    copies = place_copies(pieces, places, full, sems)
    depth = w_ref.shape[0]
    step = depth // splits
    wcopies = []
    for c in range(splits):
        part = pl.ds(c * step, step)
        copy = pltpu.make_async_copy(w_ref.at[part], weights.at[part], wsems.at[c])
        copy.start()
        wcopies.append(copy)
    for copy in copies:
        copy.wait()
    total = None
    for c in range(splits):
        wcopies[c].wait()
        term = jnp.dot(
            full[:, c * step : (c + 1) * step],
            weights[c * step : (c + 1) * step, :],
            preferred_element_type=F32,
        )
        total = term if total is None else total + term
    logits_ref[...] = total
    peak = jnp.max(total, axis=1, keepdims=True)
    soft = jnp.exp((total - peak) * 0.5)
    stats_ref[...] = columns_to_rows(
        [
            peak,
            jnp.sum(soft * soft, axis=1, keepdims=True),
            jnp.sum(soft, axis=1, keepdims=True),
        ]
    )


def student_logits(at, pieces, spots, head_weight):
    depth, cols = head_weight.shape
    rows = sum(piece.shape[0] for piece in pieces)
    splits = 7 if depth % (7 * 128) == 0 else 1
    return pl.pallas_call(
        lambda *refs: logits_kernel(spots, splits, *refs),
        out_shape=(
            jax.ShapeDtypeStruct((rows, cols), F32),
            jax.ShapeDtypeStruct((STAT_ROWS, rows), F32),
        ),
        in_specs=[SMEM] + [ANY] * (len(pieces) + 1),
        out_specs=(VMEM, VMEM),
        scratch_shapes=[
            pltpu.VMEM((rows, depth), BF16),
            pltpu.VMEM((depth, cols), BF16),
            pltpu.SemaphoreType.DMA((len(pieces),)),
            pltpu.SemaphoreType.DMA((splits,)),
        ],
        compiler_params=PARAMS,
        cost_estimate=pl.CostEstimate(
            flops=2 * rows * depth * cols,
            bytes_accessed=(rows + cols) * depth * 2 + rows * cols * 4,
            transcendentals=rows * cols,
        ),
        name="student_logits",
    )(at, *pieces, head_weight)


def back_kernel(chunk, at_ref, top_ref, low_ref, aligned_ref, stats_ref, w_ref, grad_ref, back_ref, mixed, weights, wsem):
    copy = pltpu.make_async_copy(w_ref, weights, wsem)
    copy.start()
    first = at_ref[0]
    flip = at_ref[1]
    per, cols = top_ref.shape
    turn = (
        lax.broadcasted_iota(jnp.int32, (per, per), 1)
        == (lax.broadcasted_iota(jnp.int32, (per, per), 0) ^ flip)
    ).astype(BF16)
    column = first + lax.broadcasted_iota(jnp.int32, (per, cols), 1)
    for k, logits_ref in enumerate((top_ref, low_ref)):
        stats = jnp.concatenate([stats_ref[k, 0], jnp.zeros((128 - STAT_ROWS, per), F32)]).T
        peak, hard, soft, tpeak, tsum, ids = [stats[:, i : i + 1] for i in range(6)]
        half = jnp.exp((logits_ref[...] - peak) * 0.5)
        taught = jnp.exp((aligned_ref[k, 0].astype(F32) - tpeak) * 0.5)
        label = jnp.where(column == ids.astype(jnp.int32), 16.0, 0.0)
        grad = (half * (32.0 / soft) - taught * (32.0 / tsum)) + (half * half * (16.0 / hard) - label)
        grad = grad.astype(BF16)
        grad_ref[k] = grad
        mixed[k * per : (k + 1) * per, :] = jnp.dot(turn, grad, preferred_element_type=F32).astype(BF16)
    copy.wait()
    depth = weights.shape[0]
    rows = mixed[...]
    for c in range(depth // chunk):
        part = slice(c * chunk, (c + 1) * chunk)
        out = lax.dot_general(
            rows, weights[part, :], (((1,), (1,)), ((), ())), preferred_element_type=F32
        ).astype(BF16)
        back_ref[0, :, part] = out[:per]
        back_ref[1, :, part] = out[per:]


def back_rows(at, near, far, aligned, stats, head_weight, which):
    depth, cols = head_weight.shape
    per = near.shape[0] // 2
    chunk = 512 if depth % 512 == 0 else depth
    paired = lambda i: (0, which, 0, 0)
    return pl.pallas_call(
        lambda *refs: back_kernel(chunk, *refs),
        grid=(1,),
        out_shape=(
            jax.ShapeDtypeStruct((2, per, cols), BF16),
            jax.ShapeDtypeStruct((2, per, depth), BF16),
        ),
        in_specs=[
            SMEM,
            pl.BlockSpec((per, cols), lambda i: (which, 0)),
            pl.BlockSpec((per, cols), lambda i: (which, 0)),
            pl.BlockSpec((2, 1, per, cols), paired),
            pl.BlockSpec((2, 1, STAT_ROWS, per), paired),
            ANY,
        ],
        out_specs=(
            pl.BlockSpec((2, per, cols), lambda i: (0, 0, 0)),
            pl.BlockSpec((2, per, depth), lambda i: (0, 0, 0)),
        ),
        scratch_shapes=[
            pltpu.VMEM((2 * per, cols), BF16),
            pltpu.VMEM((depth, cols), BF16),
            pltpu.SemaphoreType.DMA,
        ],
        compiler_params=PARAMS,
        cost_estimate=pl.CostEstimate(
            flops=4 * per * depth * cols,
            bytes_accessed=depth * cols * 2 + 4 * per * depth,
            transcendentals=4 * per * cols,
        ),
        name="back_rows",
    )(at, near, far, aligned, stats, head_weight)


def head_kernel(spots, *refs):
    n = len(spots)
    at_ref, pieces, (even_ref, odd_ref, out_ref, full, sems) = refs[0], refs[1 : 1 + n], refs[1 + n :]
    step = pl.program_id(0)

    @pl.when(step == 0)
    def _():
        places = [spot if isinstance(spot, int) else at_ref[spot[0]] for spot in spots]
        for copy in place_copies(pieces, places, full, sems):
            copy.wait()

    tile = out_ref.shape[0]
    part = pl.ds(pl.multiple_of(step * tile, tile), tile)
    grads = jnp.concatenate([even_ref[0], odd_ref[0], even_ref[1], odd_ref[1]])
    out_ref[...] = lax.dot_general(
        full[:, part], grads, (((0,), (0,)), ((), ())), preferred_element_type=F32
    ).astype(BF16)


def head_gradient(at, pieces, spots, even, odd):
    depth = pieces[0].shape[1]
    rows = sum(piece.shape[0] for piece in pieces)
    _, per, cols = even.shape
    tile = 512 if depth % 512 == 0 else depth
    whole = pl.BlockSpec((2, per, cols), lambda i: (0, 0, 0))
    return pl.pallas_call(
        lambda *refs: head_kernel(spots, *refs),
        grid=(depth // tile,),
        out_shape=jax.ShapeDtypeStruct((depth, cols), BF16),
        in_specs=[SMEM] + [ANY] * len(pieces) + [whole, whole],
        out_specs=pl.BlockSpec((tile, cols), lambda i: (i, 0)),
        scratch_shapes=[
            pltpu.VMEM((rows, depth), BF16),
            pltpu.SemaphoreType.DMA((len(pieces),)),
        ],
        compiler_params=PARAMS,
        cost_estimate=pl.CostEstimate(
            flops=2 * rows * depth * cols,
            bytes_accessed=(rows + cols) * depth * 2 + rows * cols * 2,
            transcendentals=0,
        ),
        name="head_gradient",
    )(at, *pieces, even, odd)


def flip_groups(stats, mask):
    groups = stats.shape[1]
    return jnp.stack([stats[:, j ^ mask] for j in range(groups)], axis=1)


def merge(parts):
    peak, tpeak = parts[0][0], parts[0][3]
    ids = parts[0][5]
    for part in parts[1:]:
        peak, tpeak = jnp.maximum(peak, part[0]), jnp.maximum(tpeak, part[3])
        ids = jnp.maximum(ids, part[5])
    hard = soft = tsum = 0.0
    for part in parts:
        shrink = jnp.exp((part[0] - peak) * 0.5)
        hard = hard + part[1] * (shrink * shrink)
        soft = soft + part[2] * shrink
        tsum = tsum + part[4] * jnp.exp((part[3] - tpeak) * 0.5)
    return jnp.stack([peak, hard, soft, tpeak, tsum, ids])


def body(hidden, token_ids, serving, head_weight, teacher_logits):
    groups = lax.axis_size("grp")
    shards = lax.axis_size("vocab")
    me_g = lax.axis_index("grp")
    me_v = lax.axis_index("vocab")
    per, depth = hidden.shape
    cols = head_weight.shape[1]
    owned = per // shards
    CORE, X = shards, 2 * shards
    Y, W = 1, 2
    count = groups * shards

    def swap(value, mask):
        return lax.ppermute(value, AXES, [(i, i ^ mask) for i in range(count)])

    quarter_rows = per // 4
    half_rows = quarter_rows // 2
    quarter = me_v & 3
    x0 = swap(lax.dynamic_slice_in_dim(hidden, quarter * quarter_rows, quarter_rows, 0), X)
    from_core = swap(hidden, CORE)
    arrived = lax.all_to_all(teacher_logits, "grp", split_axis=1, concat_axis=0, tiled=True)
    x1 = swap(x0, Y)
    x2 = swap(x0, W)
    x3a = swap(x2[:half_rows], Y)
    x3b = swap(x1[half_rows:], W)
    xs = [x0, x1, x2, x3a, x3b]
    ds = [swap(piece, CORE) for piece in xs]
    starts = [
        (quarter ^ k) * quarter_rows + extra
        for k, extra in ((0, 0), (1, 0), (2, 0), (3, 0), (3, half_rows))
    ]
    late_at = jnp.stack([s for s in starts] + [per + s for s in starts]).astype(jnp.int32)
    all_at = late_at + 2 * per
    late = xs + ds
    late_spots = [(k,) for k in range(10)]

    near_logits, near_stats = student_logits(late_at, [hidden, from_core], [0, per], head_weight)
    aligned, tstats = teacher_rows(
        me_g.astype(jnp.int32).reshape(1), serving, arrived.reshape(groups * per, cols), groups
    )
    far_logits, far_stats = student_logits(late_at, late, late_spots, head_weight)

    mine = jnp.concatenate([near_stats[:3], far_stats[:3]], axis=1)
    ids = jnp.concatenate([token_ids.astype(F32), jnp.zeros(((groups - 1) * per,), F32)])
    stats = jnp.concatenate([mine, tstats[:2], ids[None]]).reshape(6, groups, per)
    stats = merge([stats, flip_groups(swap(stats, CORE), 1)])
    stats = merge(
        [
            stats,
            flip_groups(swap(stats, X), 2),
            swap(stats, Y),
            flip_groups(swap(stats, X + Y), 2),
        ]
    )
    mask = W
    while mask < shards:
        masks = [mask, 2 * mask, 3 * mask] if 2 * mask < shards else [mask]
        stats = merge([stats] + [swap(stats, m) for m in masks])
        mask *= 4
    stats = jnp.concatenate([stats, jnp.zeros((STAT_ROWS - 6, groups, per), F32)])
    stats = stats.swapaxes(0, 1).reshape(2, 2, STAT_ROWS, per)

    at = jnp.stack([(me_g * shards + me_v) * cols, me_v * owned]).astype(jnp.int32)
    pairs = aligned.reshape(2, 2, per, cols)
    odd, away = back_rows(at, near_logits, far_logits, pairs, stats, head_weight, 1)
    recv = swap(away, CORE)
    even, keep = back_rows(at, near_logits, far_logits, pairs, stats, head_weight, 0)

    bits = shards.bit_length() - 1
    shape = (2,) * (1 + bits) + (owned, depth)
    held = [keep.reshape(shape), recv.reshape(shape)]
    masks = {0: X}
    for b in range(bits):
        masks[1 + b] = shards >> (1 + b)
    ydim, wdim = bits, bits - 1
    units = depth // 128
    third = units // 3
    edges = [0, third * 128, 2 * third * 128, depth]
    orders = [(0, ydim, wdim), (ydim, wdim, 0), (wdim, 0, ydim)]
    parts = []
    for p, order in enumerate(orders):
        terms = [h[..., edges[p] : edges[p + 1]] for h in held]
        for dim in order:
            sent = sum(lax.index_in_dim(t, 1, dim).astype(F32) for t in terms).astype(BF16)
            got = swap(sent, masks[dim])
            terms = [lax.index_in_dim(t, 0, dim) for t in terms] + [got]
        parts.append(terms)
    parts = [
        sum(t.astype(F32) for t in terms) for terms in parts
    ]
    total = jnp.concatenate(parts, axis=-1)
    for dim in range(1, wdim):
        got = swap(lax.index_in_dim(total, 1, dim).astype(BF16), masks[dim])
        total = lax.index_in_dim(total, 0, dim) + got.astype(F32)
    grad_hidden = total.reshape(owned, depth)

    grad_head = head_gradient(
        all_at, [hidden, from_core] + late, [0, per] + late_spots, even, odd
    )
    return (grad_hidden, grad_head)


def solution(mesh):
    placed = (P("grp", None), P("grp"), P(), P(None, ("grp", "vocab")), P("grp", None, "vocab"))
    return jax.shard_map(
        body,
        mesh=mesh,
        in_specs=placed,
        out_specs=(P(("grp", "vocab"), None), P(None, ("grp", "vocab"))),
        check_vma=False,
    )
```

time: 310 us -> 115 us (0.37)
  waiting for transfers between devices: 169 us -> 28.2 us
  blocking collectives: 91.7 us -> 0 us
  starting transfers between devices: 4.25 us -> 33 us
  Pallas kernels: 0 us -> 22.6 us
  matrix products: 19.6 us -> 0 us
  between operations: 14.1 us -> 1.09 us
  other arithmetic: 1.34 us -> 12.5 us
  local copies, waits for them, and re-layouts: 10 us -> 17 us
    reduce_scatter x1 -> x0, waiting for transfers between devices: 151 us -> none  [body(): lax.psum_scatter(lax.dot_general(activation_derivative, head_weight, (((1...]
    psum x1 -> x0, blocking collectives: 41.1 us -> none  [body(): lax.psum((jnp.sum(jnp.exp(shifted_pupil_activations), axis=1), jnp.sum(jn...]
    pmax x1 -> x0, blocking collectives: 40.3 us -> none  [body(): lax.pmax((local_peak, local_tpeak), ('grp', 'vocab'))]
    ppermute x0 -> x29, starting transfers between devices: none -> 29.5 us  [swap(): return lax.ppermute(value, AXES, [(i, i ^ mask) for i in range(count)])]
    ppermute x0 -> x29, waiting for transfers between devices: none -> 28.2 us  [swap(): return lax.ppermute(value, AXES, [(i, i ^ mask) for i in range(count)])]
    pallas_call x0 -> x6, Pallas kernels: none -> 22.6 us  [the longest x1 8.64 us: head_gradient(): pl.pallas_call(lambda *refs: head_kernel(spots, *refs), grid=(depth // ti...]
    dot_general x3 -> x0, matrix products: 19.6 us -> none  [the longest x1 7.69 us: body(): lax.dot_general(activation_derivative, head_weight, (((1,), (1,)), ((), (...]
    all_gather x1 -> x0, waiting for transfers between devices: 16.8 us -> none  [body(): lax.all_gather(hidden, 'grp', axis=0, tiled=True)]
  transfers between devices with their start and end apart: 3 -> 30, of which waited for: 2 -> 15; matrix products, arithmetic and copies ran while one was open for 6% -> 7% of each run, Pallas kernels for 0% -> 15%
where the time goes in v2:
time: 115 us; the launch traced here: 114 us
  starting transfers between devices  33 us (29%)
  waiting for transfers between devices  28.2 us (25%)
  Pallas kernels  22.6 us (20%)
  local copies, waits for them, and re-layouts  17 us (15%)
  other arithmetic  12.5 us (11%)
    ppermute x29, starting transfers between devices, swap(): return lax.ppermute(value, AXES, [(i, i ^ mask) for i in range(count)])  29.5 us
    ppermute x29, waiting for transfers between devices, swap(): return lax.ppermute(value, AXES, [(i, i ^ mask) for i in range(count)])  28.2 us
    unnamed x59, local copies, waits for them, and re-layouts  11.3 us
    pallas_call x1, Pallas kernels, head_gradient(): pl.pallas_call(lambda *refs: head_kernel(spots, *refs), grid=(depth // ti...  8.64 us
    pallas_call x2, Pallas kernels, student_logits(): pl.pallas_call(lambda *refs: logits_kernel(spots, splits, *refs), out_sha...  7.92 us
    unnamed x10, other arithmetic  7.13 us
    pallas_call x2, Pallas kernels, back_rows(): pl.pallas_call(lambda *refs: back_kernel(chunk, *refs), grid=(1,), out_sh...  5.27 us
    all_to_all x1, starting transfers between devices, body(): lax.all_to_all(teacher_logits, 'grp', split_axis=1, concat_axis=0, tiled=...  3.47 us
  transfers between devices with their start and end apart: 30, of which 15 were waited for; matrix products, arithmetic and copies ran while one was open for 7% of the time, Pallas kernels for 15%

profile of v2, /device:TPU:0, one launch (start us, length us, event | category | flops | bytes accessed | tf_op | source)
XLA Modules:
  0.0 114.5 jit_solution(4182632069091031644)
XLA Ops:
  1.2 1.0 constant_dynamic-slice_fusion
  2.1 2.6 %collective-permute-start.1 = (bf16[32,3584]{1,0:T(8,128)(2,1)S(1)}, bf16[32,3584]{1,0:T(8,128)(2,1)S(1)}, u32[]{:S(2)}, u32[]{:S(2)}) collective-permute-start(bf16[32,3584]{1,0:T(8,128)(2,1)S(1)} %constant_dynamic-slice_fusion), channel_id=1, source_target_pairs={{0,16},{1,17},{2,18},{3,19},{4,20},{5,21},{6,22},{7,23},{8,24},{9,... | collective-permute-start | bytes 688136 | tf_op jit(solution)/shard_map/ppermute | solution.py:291
  4.7 1.9 %copy.27 = bf16[128,4,512]{2,0,1:T(8,128)(2,1)} copy(bf16[128,4,512]{2,1,0:T(4,128)(2,1)} %param.9) | data formatting | bytes 1048576 | tf_op args[4]
  6.6 3.5 %all-to-all-start = ((bf16[128,4,512]{2,0,1:T(8,128)(2,1)}), bf16[128,4,512]{2,0,1:T(8,128)(2,1)S(1)}, u32[]{:S(2)}, u32[]{:S(2)}) async-start(bf16[128,4,512]{2,0,1:T(8,128)(2,1)} %copy.27), calls=%async_computation | async-start | bytes 1048576 | tf_op jit(solution)/shard_map/all_to_all | solution.py:298
  10.1 0.8 collective-permute-done.1.refs_1_.refs_3_
  11.0 1.8 %collective-permute-start.3 = (bf16[32,3584]{1,0:T(8,128)(2,1)S(1)}, bf16[32,3584]{1,0:T(8,128)(2,1)S(1)}, u32[]{:S(2)}, u32[]{:S(2)}) collective-permute-start(bf16[32,3584]{1,0:T(8,128)(2,1)S(1)} %collective-permute-done.1.refs_1_.refs_3_), channel_id=1, source_target_pairs={{0,2},{1,3},{2,0},{3,1},{4,6},{5,7},{6,4},{7,5},{8,10},{9,11},{10,... | collective-permute-start | bytes 688136 | tf_op jit(solution)/shard_map/ppermute | solution.py:291
  12.8 1.5 %collective-permute-start.2 = (bf16[32,3584]{1,0:T(8,128)(2,1)S(1)}, bf16[32,3584]{1,0:T(8,128)(2,1)S(1)}, u32[]{:S(2)}, u32[]{:S(2)}) collective-permute-start(bf16[32,3584]{1,0:T(8,128)(2,1)S(1)} %collective-permute-done.1.refs_1_.refs_3_), channel_id=1, source_target_pairs={{0,1},{1,0},{2,3},{3,2},{4,5},{5,4},{6,7},{7,6},{8,9},{9,8},{10,11... | collective-permute-start | bytes 688136 | tf_op jit(solution)/shard_map/ppermute | solution.py:291
  14.4 4.0 %collective-permute-done.3.refs_3_.refs_5_ = bf16[32,3584]{1,0:T(8,128)(2,1)S(1)} collective-permute-done((bf16[32,3584]{1,0:T(8,128)(2,1)S(1)}, bf16[32,3584]{1,0:T(8,128)(2,1)S(1)}, u32[]{:S(2)}, u32[]{:S(2)}) %collective-permute-start.3) | collective-permute-done | bytes 229408 | tf_op jit(solution)/shard_map/ppermute | solution.py:291
  18.4 0.7 slice.506
  19.1 1.6 %collective-permute-start.4 = (bf16[16,3584]{1,0:T(8,128)(2,1)}, bf16[16,3584]{1,0:T(8,128)(2,1)S(1)}, u32[]{:S(2)}, u32[]{:S(2)}) collective-permute-start(bf16[16,3584]{1,0:T(8,128)(2,1)} %slice.506), channel_id=1, source_target_pairs={{0,1},{1,0},{2,3},{3,2},{4,5},{5,4},{6,7},{7,6},{8,9},{9,8},{10,11... | collective-permute-start | bytes 344072 | tf_op jit(solution)/shard_map/ppermute | solution.py:291
  20.6 0.7 slice.507
  21.3 1.6 %collective-permute-start.5 = (bf16[16,3584]{1,0:T(8,128)(2,1)}, bf16[16,3584]{1,0:T(8,128)(2,1)}, u32[]{:S(2)}, u32[]{:S(2)}) collective-permute-start(bf16[16,3584]{1,0:T(8,128)(2,1)} %slice.507), channel_id=1, source_target_pairs={{0,2},{1,3},{2,0},{3,1},{4,6},{5,7},{6,4},{7,5},{8,10},{9,11},{10,... | collective-permute-start | bytes 344072 | tf_op jit(solution)/shard_map/ppermute | solution.py:291
  24.0 0.8 teacher_rows.1
  24.8 0.6 concatenate.24
  25.5 1.0 collective-permute-done.5.refs_5_.refs_7_
  27.0 0.7 copy-done.14
  27.7 0.7 copy-done.17
  28.5 2.1 %copy-done = bf16[3584,512]{1,0:T(8,128)(2,1)S(1)} copy-done((bf16[3584,512]{1,0:T(8,128)(2,1)S(1)}, bf16[3584,512]{1,0:T(8,128)(2,1)}, u32[]{:S(2)}) %copy-start) | copy-done | bytes 3670040
  30.5 0.9 copy-done.9
  31.5 0.9 copy-done.12
  32.4 0.9 copy-done.15
  33.4 0.9 copy-done.18
  34.3 4.9 %student_logits.3 = (f32[256,512]{1,0:T(8,128)S(1)}, f32[8,256]{1,0:T(8,128)S(1)}) custom-call(s32[10]{0:T(128)S(1)} %stack.90.refs_0_, bf16[32,3584]{1,0:T(8,128)(2,1)S(1)} %copy-done.9, bf16[32,3584]{1,0:T(8,128)(2,1)S(1)} %collective-permute-done.2.refs_2_.refs_4_, bf16[32,3584]{1,0:T(8,128)(2,1)S(1)} %collective-permute-done.3.refs_3_.refs_5_, ...), custom_call_target="tpu_custom_call" | custom-call | flops 939524096 | bytes 6029312 | tf_op jit(solution)/shard_map/student_logits/pallas_call | solution.py:117
  39.3 3.0 %student_logits.2 = (f32[256,512]{1,0:T(8,128)S(1)}, f32[8,256]{1,0:T(8,128)S(1)}) custom-call(s32[10]{0:T(128)S(1)} %stack.90.refs_0_, bf16[128,3584]{1,0:T(8,128)(2,1)S(1)} %copy-done.3, bf16[128,3584]{1,0:T(8,128)(2,1)S(1)} %collective-permute-done.refs_2_, bf16[3584,512]{1,0:T(8,128)(2,1)S(1)} %copy-done.1), custom_call_target="tpu_custom_call" | custom-call | flops 939524096 | bytes 6029312 | tf_op jit(solution)/shard_map/student_logits/pallas_call | solution.py:117
  42.4 0.7 pad_maximum_fusion.1
  43.6 0.8 collective-permute-done.11
  44.4 0.6 constant_dynamic-update-slice_fusion.5
  45.0 0.6 constant_dynamic-update-slice_fusion.4
  45.6 0.6 constant_dynamic-update-slice_fusion.3
  46.8 1.2 %constant_dynamic-update-slice_fusion.1 = f32[6,4,128]{2,1,0:T(4,128)} fusion(f32[6,4,128]{2,1,0:T(4,128)} %constant_dynamic-update-slice_fusion.2, f32[6,4,128]{2,1,0:T(4,128)S(1)} %pad_maximum_fusion.2, f32[1,4,128]{2,1,0:T(4,128)} %bitcast.81, f32[1,4,128]{2,1,0:T(4,128)S(1)} %bitcast.76), kind=kLoop, calls=%fused_computation.17 | loop fusion | flops 4096 | bytes 10240
  48.1 1.3 %constant_dynamic-update-slice_fusion = f32[6,4,128]{2,1,0:T(4,128)} fusion(f32[6,4,128]{2,1,0:T(4,128)} %constant_dynamic-update-slice_fusion.1, f32[6,4,128]{2,1,0:T(4,128)S(1)} %pad_maximum_fusion.2, f32[128]{0:T(128)} %copy-done.27), kind=kLoop, calls=%fused_computation.16 | loop fusion | flops 512 | bytes 4608 | tf_op jit(solution)/shard_map/stack | solution.py:275
  49.3 1.5 %collective-permute-start.14 = (f32[6,4,128]{2,1,0:T(4,128)}, f32[6,4,128]{2,1,0:T(4,128)}, u32[]{:S(2)}, u32[]{:S(2)}) collective-permute-start(f32[6,4,128]{2,1,0:T(4,128)} %constant_dynamic-update-slice_fusion), channel_id=1, source_target_pairs={{0,17},{1,16},{2,19},{3,18},{4,21},{5,20},{6,23},{7,22},{8,25},{9,... | collective-permute-start | bytes 36872 | tf_op jit(solution)/shard_map/ppermute | solution.py:291
  50.9 1.4 %collective-permute-start.13 = (f32[6,4,128]{2,1,0:T(4,128)}, f32[6,4,128]{2,1,0:T(4,128)S(1)}, u32[]{:S(2)}, u32[]{:S(2)}) collective-permute-start(f32[6,4,128]{2,1,0:T(4,128)} %constant_dynamic-update-slice_fusion), channel_id=1, source_target_pairs={{0,1},{1,0},{2,3},{3,2},{4,5},{5,4},{6,7},{7,6},{8,9},{9,8},{10,11... | collective-permute-start | bytes 36872 | tf_op jit(solution)/shard_map/ppermute | solution.py:291
  52.8 1.4 %collective-permute-done.14 = f32[6,4,128]{2,1,0:T(4,128)} collective-permute-done((f32[6,4,128]{2,1,0:T(4,128)}, f32[6,4,128]{2,1,0:T(4,128)}, u32[]{:S(2)}, u32[]{:S(2)}) %collective-permute-start.14) | collective-permute-done | bytes 12320 | tf_op jit(solution)/shard_map/ppermute | solution.py:291
  54.2 0.8 fusion.51
  55.0 1.2 %collective-permute-done.12 = f32[6,4,128]{2,1,0:T(4,128)S(1)} collective-permute-done((f32[6,4,128]{2,1,0:T(4,128)}, f32[6,4,128]{2,1,0:T(4,128)S(1)}, u32[]{:S(2)}, u32[]{:S(2)}) %collective-permute-start.12) | collective-permute-done | bytes 12320 | tf_op jit(solution)/shard_map/ppermute | solution.py:291
  56.2 0.7 constant_dynamic-update-slice_fusion.11
  56.9 0.7 constant_dynamic-update-slice_fusion.10
  57.6 0.7 constant_dynamic-update-slice_fusion.9
  58.3 0.7 constant_dynamic-update-slice_fusion.8
  59.0 0.7 constant_dynamic-update-slice_fusion.7
  59.7 0.7 constant_dynamic-update-slice_fusion.6
  60.4 3.7 %collective-permute-start.17 = (f32[6,4,128]{2,1,0:T(4,128)S(1)}, f32[6,4,128]{2,1,0:T(4,128)S(1)}, u32[]{:S(2)}, u32[]{:S(2)}) collective-permute-start(f32[6,4,128]{2,1,0:T(4,128)S(1)} %get-tuple-element.26), channel_id=1, source_target_pairs={{0,6},{1,7},{2,4},{3,5},{4,2},{5,3},{6,0},{7,1},{8,14},{9,15},{10,... | collective-permute-start | bytes 36872 | tf_op jit(solution)/shard_map/ppermute | solution.py:291
  64.1 0.8 collective-permute-start.15
  64.9 1.0 collective-permute-done.17
  66.0 2.7 %collective-permute-done.16 = f32[6,4,128]{2,1,0:T(4,128)S(1)} collective-permute-done((f32[6,4,128]{2,1,0:T(4,128)S(1)}, f32[6,4,128]{2,1,0:T(4,128)S(1)}, u32[]{:S(2)}, u32[]{:S(2)}) %collective-permute-start.16) | collective-permute-done | bytes 12320 | tf_op jit(solution)/shard_map/ppermute | solution.py:291
  68.7 0.6 fusion.32
  69.9 0.7 concatenate.28
  70.6 2.0 %copy-done.2 = bf16[3584,512]{1,0:T(8,128)(2,1)S(1)} copy-done((bf16[3584,512]{1,0:T(8,128)(2,1)S(1)}, bf16[3584,512]{1,0:T(8,128)(2,1)}, u32[]{:S(2)}) %copy-start.2) | copy-done | bytes 3670040
  72.6 2.6 %back_rows.3 = (bf16[2,128,512]{2,1,0:T(8,128)(2,1)S(1)}, bf16[2,128,3584]{2,1,0:T(8,128)(2,1)S(1)}) custom-call(s32[2]{0:T(128)S(1)} %pad_add_fusion.refs_0_, f32[256,512]{1,0:T(8,128)S(1)} %get-tuple-element.12.refs_1_, f32[256,512]{1,0:T(8,128)S(1)} %get-tuple-element.13.refs_2_, bf16[2,2,128,512]{3,2,1,0:T(8,128)(2,1)S(1)} %bitcast.45, ...), custom_call_target="tpu_custom_call" | custom-call | flops 939524096 | bytes 5505024 | tf_op jit(solution)/shard_map/back_rows/pallas_call | solution.py:179
  75.4 2.6 %back_rows.2 = (bf16[2,128,512]{2,1,0:T(8,128)(2,1)S(1)}, bf16[2,128,3584]{2,1,0:T(8,128)(2,1)S(1)}) custom-call(s32[2]{0:T(128)S(1)} %pad_add_fusion.refs_0_, f32[256,512]{1,0:T(8,128)S(1)} %get-tuple-element.12.refs_1_, f32[256,512]{1,0:T(8,128)S(1)} %get-tuple-element.13.refs_2_, bf16[2,2,128,512]{3,2,1,0:T(8,128)(2,1)S(1)} %bitcast.46, ...), custom_call_target="tpu_custom_call" | custom-call | flops 939524096 | bytes 5505024 | tf_op jit(solution)/shard_map/back_rows/pallas_call | solution.py:179
  78.0 1.1 collective-permute-done.18
  80.6 7.9 %collective-permute-done.19 = bf16[1,2,2,2,16,1152]{5,4,3,2,1,0:T(8,128)(2,1)S(1)} collective-permute-done((bf16[1,2,2,2,16,1152]{5,4,3,2,1,0:T(8,128)(2,1)S(1)}, bf16[1,2,2,2,16,1152]{5,4,3,2,1,0:T(8,128)(2,1)S(1)}, u32[]{:S(2)}, u32[]{:S(2)}) %collective-permute-start.19) | collective-permute-done | bytes 294944 | tf_op jit(solution)/shard_map/ppermute | solution.py:291
  89.2 1.7 %collective-permute-start.23 = (bf16[2,2,1,1,16,1152]{5,4,3,2,1,0:T(8,128)(2,1)S(1)}, bf16[2,2,1,1,16,1152]{5,4,3,2,1,0:T(8,128)(2,1)S(1)}, u32[]{:S(2)}, u32[]{:S(2)}) collective-permute-start(bf16[2,2,1,1,16,1152]{5,4,3,2,1,0:T(8,128)(2,1)S(1)} %add_convert_fusion.4), channel_id=1, source_target_pairs={{0,2},{1,3},{2,0},{3,1},{4,6},{5,7},{6,4},{7,5},{8,10},{9,11},{10,... | collective-permute-start | bytes 442376 | tf_op jit(solution)/shard_map/ppermute | solution.py:291
  91.0 1.3 %collective-permute-start.26 = (bf16[1,2,1,2,16,1280]{5,4,3,2,1,0:T(8,128)(2,1)S(1)}, bf16[1,2,1,2,16,1280]{5,4,3,2,1,0:T(8,128)(2,1)S(1)}, u32[]{:S(2)}, u32[]{:S(2)}) collective-permute-start(bf16[1,2,1,2,16,1280]{5,4,3,2,1,0:T(8,128)(2,1)S(1)} %add_convert_fusion.3), channel_id=1, source_target_pairs={{0,16},{1,17},{2,18},{3,19},{4,20},{5,21},{6,22},{7,23},{8,24},{9,... | collective-permute-start | bytes 491528 | tf_op jit(solution)/shard_map/ppermute | solution.py:291
  92.3 1.5 %collective-permute-done.20 = bf16[1,2,2,1,16,1152]{5,4,3,2,1,0:T(8,128)(2,1)S(1)} collective-permute-done((bf16[1,2,2,1,16,1152]{5,4,3,2,1,0:T(8,128)(2,1)S(1)}, bf16[1,2,2,1,16,1152]{5,4,3,2,1,0:T(8,128)(2,1)S(1)}, u32[]{:S(2)}, u32[]{:S(2)}) %collective-permute-start.20) | collective-permute-done | bytes 147488 | tf_op jit(solution)/shard_map/ppermute | solution.py:291
  93.9 1.7 %collective-permute-start.21 = (bf16[1,2,1,1,16,1152]{5,4,3,2,1,0:T(8,128)(2,1)S(1)}, bf16[1,2,1,1,16,1152]{5,4,3,2,1,0:T(8,128)(2,1)S(1)}, u32[]{:S(2)}, u32[]{:S(2)}) collective-permute-start(bf16[1,2,1,1,16,1152]{5,4,3,2,1,0:T(8,128)(2,1)S(1)} %add_convert_fusion.8), channel_id=1, source_target_pairs={{0,2},{1,3},{2,0},{3,1},{4,6},{5,7},{6,4},{7,5},{8,10},{9,11},{10,... | collective-permute-start | bytes 221192 | tf_op jit(solution)/shard_map/ppermute | solution.py:291
  95.6 0.8 collective-permute-done.26
  96.4 1.6 %collective-permute-start.27 = (bf16[1,2,1,1,16,1280]{5,4,3,2,1,0:T(8,128)(2,1)S(1)}, bf16[1,2,1,1,16,1280]{5,4,3,2,1,0:T(8,128)(2,1)S(1)}, u32[]{:S(2)}, u32[]{:S(2)}) collective-permute-start(bf16[1,2,1,1,16,1280]{5,4,3,2,1,0:T(8,128)(2,1)S(1)} %add_convert_fusion.6), channel_id=1, source_target_pairs={{0,1},{1,0},{2,3},{3,2},{4,5},{5,4},{6,7},{7,6},{8,9},{9,8},{10,11... | collective-permute-start | bytes 245768 | tf_op jit(solution)/shard_map/ppermute | solution.py:291
  99.0 1.9 %collective-permute-done.27 = bf16[1,2,1,1,16,1280]{5,4,3,2,1,0:T(8,128)(2,1)S(1)} collective-permute-done((bf16[1,2,1,1,16,1280]{5,4,3,2,1,0:T(8,128)(2,1)S(1)}, bf16[1,2,1,1,16,1280]{5,4,3,2,1,0:T(8,128)(2,1)S(1)}, u32[]{:S(2)}, u32[]{:S(2)}) %collective-permute-start.27) | collective-permute-done | bytes 81952 | tf_op jit(solution)/shard_map/ppermute | solution.py:291
  101.0 1.8 %collective-permute-done.24 = bf16[1,2,1,1,16,1152]{5,4,3,2,1,0:T(8,128)(2,1)S(1)} collective-permute-done((bf16[1,2,1,1,16,1152]{5,4,3,2,1,0:T(8,128)(2,1)S(1)}, bf16[1,2,1,1,16,1152]{5,4,3,2,1,0:T(8,128)(2,1)S(1)}, u32[]{:S(2)}, u32[]{:S(2)}) %collective-permute-start.24) | collective-permute-done | bytes 73760 | tf_op jit(solution)/shard_map/ppermute | solution.py:291
  102.9 2.1 %collective-permute-start.28 = (bf16[1,1,1,1,16,3584]{5,4,3,2,1,0:T(8,128)(2,1)S(1)}, bf16[1,1,1,1,16,3584]{5,4,3,2,1,0:T(8,128)(2,1)S(1)}, u32[]{:S(2)}, u32[]{:S(2)}) collective-permute-start(bf16[1,1,1,1,16,3584]{5,4,3,2,1,0:T(8,128)(2,1)S(1)} %slice.938), channel_id=1, source_target_pairs={{0,4},{1,5},{2,6},{3,7},{4,0},{5,1},{6,2},{7,3},{8,12},{9,13},{10,... | collective-permute-start | bytes 344072 | tf_op jit(solution)/shard_map/ppermute | solution.py:291
  105.1 8.6 %head_gradient.1 = bf16[3584,512]{1,0:T(8,128)(2,1)} custom-call(s32[10]{0:T(128)S(1)} %broadcast_add_fusion.refs_0_, bf16[128,3584]{1,0:T(8,128)(2,1)S(1)} %copy-done.3, bf16[128,3584]{1,0:T(8,128)(2,1)S(1)} %collective-permute-done.refs_2_, bf16[32,3584]{1,0:T(8,128)(2,1)S(1)} %copy-done.10, bf16[32,3584]{1,0:T(8,128)(2,1)S(1)} %copy-done.7, ...), custom_call_target="tpu_custom_call" | custom-call | flops 1879048192 | bytes 7864320 | tf_op jit(solution)/shard_map/head_gradient/pallas_call | solution.py:238
  113.8 0.7 fusion
  (112 shorter events, 8.4 us)
Async XLA Ops:
  0.6 13.7 %copy-start.28 = (s32[128]{0:T(128)S(1)}, s32[128]{0:T(128)}, u32[]{:S(2)}) copy-start(s32[128]{0:T(128)} %param.6) | copy-start | bytes 1540
  0.6 23.4 %copy-start.24 = (s32[512]{0:T(512)S(1)}, s32[512]{0:T(512)}, u32[]{:S(2)}) copy-start(s32[512]{0:T(512)} %param.7) | copy-start | bytes 6148
  0.6 38.6 %collective-permute-start = (bf16[128,3584]{1,0:T(8,128)(2,1)}, bf16[128,3584]{1,0:T(8,128)(2,1)S(1)}, u32[]{:S(2)}, u32[]{:S(2)}) collective-permute-start(bf16[128,3584]{1,0:T(8,128)(2,1)} %refs_1_.3), channel_id=1, source_target_pairs={{0,8},{1,9},{2,10},{3,11},{4,12},{5,13},{6,14},{7,15},{8,0},{9,1},... | collective-permute-start | bytes 2752520 | tf_op jit(solution)/shard_map/ppermute | solution.py:291
  2.1 8.8 %collective-permute-start.1 = (bf16[32,3584]{1,0:T(8,128)(2,1)S(1)}, bf16[32,3584]{1,0:T(8,128)(2,1)S(1)}, u32[]{:S(2)}, u32[]{:S(2)}) collective-permute-start(bf16[32,3584]{1,0:T(8,128)(2,1)S(1)} %constant_dynamic-slice_fusion), channel_id=1, source_target_pairs={{0,16},{1,17},{2,18},{3,19},{4,20},{5,21},{6,22},{7,23},{8,24},{9,... | collective-permute-start | bytes 688136 | tf_op jit(solution)/shard_map/ppermute | solution.py:291
  6.6 17.4 %all-to-all-start = ((bf16[128,4,512]{2,0,1:T(8,128)(2,1)}), bf16[128,4,512]{2,0,1:T(8,128)(2,1)S(1)}, u32[]{:S(2)}, u32[]{:S(2)}) async-start(bf16[128,4,512]{2,0,1:T(8,128)(2,1)} %copy.27), calls=%async_computation | async-start | bytes 1048576 | tf_op jit(solution)/shard_map/all_to_all | solution.py:298
  11.0 17.5 %copy-start.8 = (bf16[32,3584]{1,0:T(8,128)(2,1)}, bf16[32,3584]{1,0:T(8,128)(2,1)S(1)}, u32[]{:S(2)}) copy-start(bf16[32,3584]{1,0:T(8,128)(2,1)S(1)} %collective-permute-done.1.refs_1_.refs_3_) | copy-start | bytes 688132
  11.0 7.4 %collective-permute-start.3 = (bf16[32,3584]{1,0:T(8,128)(2,1)S(1)}, bf16[32,3584]{1,0:T(8,128)(2,1)S(1)}, u32[]{:S(2)}, u32[]{:S(2)}) collective-permute-start(bf16[32,3584]{1,0:T(8,128)(2,1)S(1)} %collective-permute-done.1.refs_1_.refs_3_), channel_id=1, source_target_pairs={{0,2},{1,3},{2,0},{3,1},{4,6},{5,7},{6,4},{7,5},{8,10},{9,11},{10,... | collective-permute-start | bytes 688136 | tf_op jit(solution)/shard_map/ppermute | solution.py:291
  12.8 7.8 %collective-permute-start.2 = (bf16[32,3584]{1,0:T(8,128)(2,1)S(1)}, bf16[32,3584]{1,0:T(8,128)(2,1)S(1)}, u32[]{:S(2)}, u32[]{:S(2)}) collective-permute-start(bf16[32,3584]{1,0:T(8,128)(2,1)S(1)} %collective-permute-done.1.refs_1_.refs_3_), channel_id=1, source_target_pairs={{0,1},{1,0},{2,3},{3,2},{4,5},{5,4},{6,7},{7,6},{8,9},{9,8},{10,11... | collective-permute-start | bytes 688136 | tf_op jit(solution)/shard_map/ppermute | solution.py:291
  14.3 9.2 %collective-permute-start.6 = (bf16[32,3584]{1,0:T(8,128)(2,1)S(1)}, bf16[32,3584]{1,0:T(8,128)(2,1)S(1)}, u32[]{:S(2)}, u32[]{:S(2)}) collective-permute-start(bf16[32,3584]{1,0:T(8,128)(2,1)S(1)} %collective-permute-done.1.refs_1_.refs_3_), channel_id=1, source_target_pairs={{0,8},{1,9},{2,10},{3,11},{4,12},{5,13},{6,14},{7,15},{8,0},{9,1},... | collective-permute-start | bytes 688136 | tf_op jit(solution)/shard_map/ppermute | solution.py:291
  14.3 9.7 %copy-start.27 = (f32[128]{0:T(128)}, f32[128]{0:T(128)S(1)}, u32[]{:S(2)}) copy-start(f32[128]{0:T(128)S(1)} %convert_element_type.160) | copy-start | bytes 1540
  18.4 20.9 %copy-start.4 = (bf16[32,3584]{1,0:T(8,128)(2,1)}, bf16[32,3584]{1,0:T(8,128)(2,1)S(1)}, u32[]{:S(2)}) copy-start(bf16[32,3584]{1,0:T(8,128)(2,1)S(1)} %collective-permute-done.3.refs_3_.refs_5_) | copy-start | bytes 688132
  19.1 6.3 %collective-permute-start.4 = (bf16[16,3584]{1,0:T(8,128)(2,1)}, bf16[16,3584]{1,0:T(8,128)(2,1)S(1)}, u32[]{:S(2)}, u32[]{:S(2)}) collective-permute-start(bf16[16,3584]{1,0:T(8,128)(2,1)} %slice.506), channel_id=1, source_target_pairs={{0,1},{1,0},{2,3},{3,2},{4,5},{5,4},{6,7},{7,6},{8,9},{9,8},{10,11... | collective-permute-start | bytes 344072 | tf_op jit(solution)/shard_map/ppermute | solution.py:291
  20.6 18.6 %copy-start.6 = (bf16[32,3584]{1,0:T(8,128)(2,1)}, bf16[32,3584]{1,0:T(8,128)(2,1)S(1)}, u32[]{:S(2)}) copy-start(bf16[32,3584]{1,0:T(8,128)(2,1)S(1)} %collective-permute-done.2.refs_2_.refs_4_) | copy-start | bytes 688132
  21.3 5.1 %collective-permute-start.5 = (bf16[16,3584]{1,0:T(8,128)(2,1)}, bf16[16,3584]{1,0:T(8,128)(2,1)}, u32[]{:S(2)}, u32[]{:S(2)}) collective-permute-start(bf16[16,3584]{1,0:T(8,128)(2,1)} %slice.507), channel_id=1, source_target_pairs={{0,2},{1,3},{2,0},{3,1},{4,6},{5,7},{6,4},{7,5},{8,10},{9,11},{10,... | collective-permute-start | bytes 344072 | tf_op jit(solution)/shard_map/ppermute | solution.py:291
  23.5 3.6 %collective-permute-start.7 = (bf16[32,3584]{1,0:T(8,128)(2,1)S(1)}, bf16[32,3584]{1,0:T(8,128)(2,1)S(1)}, u32[]{:S(2)}, u32[]{:S(2)}) collective-permute-start(bf16[32,3584]{1,0:T(8,128)(2,1)S(1)} %collective-permute-done.2.refs_2_.refs_4_), channel_id=1, source_target_pairs={{0,8},{1,9},{2,10},{3,11},{4,12},{5,13},{6,14},{7,15},{8,0},{9,1},... | collective-permute-start | bytes 688136 | tf_op jit(solution)/shard_map/ppermute | solution.py:291
  23.5 4.9 %copy-start.11 = (bf16[32,3584]{1,0:T(8,128)(2,1)}, bf16[32,3584]{1,0:T(8,128)(2,1)S(1)}, u32[]{:S(2)}) copy-start(bf16[32,3584]{1,0:T(8,128)(2,1)S(1)} %collective-permute-done.6.refs_6_.refs_8_) | copy-start | bytes 688132
  23.5 4.2 %collective-permute-start.8 = (bf16[32,3584]{1,0:T(8,128)(2,1)S(1)}, bf16[32,3584]{1,0:T(8,128)(2,1)S(1)}, u32[]{:S(2)}, u32[]{:S(2)}) collective-permute-start(bf16[32,3584]{1,0:T(8,128)(2,1)S(1)} %collective-permute-done.3.refs_3_.refs_5_), channel_id=1, source_target_pairs={{0,8},{1,9},{2,10},{3,11},{4,12},{5,13},{6,14},{7,15},{8,0},{9,1},... | collective-permute-start | bytes 688136 | tf_op jit(solution)/shard_map/ppermute | solution.py:291
  25.4 3.0 %collective-permute-start.9 = (bf16[16,3584]{1,0:T(8,128)(2,1)S(1)}, bf16[16,3584]{1,0:T(8,128)(2,1)S(1)}, u32[]{:S(2)}, u32[]{:S(2)}) collective-permute-start(bf16[16,3584]{1,0:T(8,128)(2,1)S(1)} %collective-permute-done.4.refs_4_.refs_6_), channel_id=1, source_target_pairs={{0,8},{1,9},{2,10},{3,11},{4,12},{5,13},{6,14},{7,15},{8,0},{9,1},... | collective-permute-start | bytes 344072 | tf_op jit(solution)/shard_map/ppermute | solution.py:291
  26.4 2.0 %collective-permute-start.10 = (bf16[16,3584]{1,0:T(8,128)(2,1)}, bf16[16,3584]{1,0:T(8,128)(2,1)S(1)}, u32[]{:S(2)}, u32[]{:S(2)}) collective-permute-start(bf16[16,3584]{1,0:T(8,128)(2,1)} %collective-permute-done.5.refs_5_.refs_7_), channel_id=1, source_target_pairs={{0,8},{1,9},{2,10},{3,11},{4,12},{5,13},{6,14},{7,15},{8,0},{9,1},... | collective-permute-start | bytes 344072 | tf_op jit(solution)/shard_map/ppermute | solution.py:291
  27.0 0.7 copy-start.14
  27.7 0.7 copy-start.17
  28.4 10.8 %copy-start.20 = (bf16[16,3584]{1,0:T(8,128)(2,1)}, bf16[16,3584]{1,0:T(8,128)(2,1)S(1)}, u32[]{:S(2)}) copy-start(bf16[16,3584]{1,0:T(8,128)(2,1)S(1)} %collective-permute-done.9.refs_9_.refs_11_) | copy-start | bytes 344068
  28.5 2.1 %copy-start = (bf16[3584,512]{1,0:T(8,128)(2,1)S(1)}, bf16[3584,512]{1,0:T(8,128)(2,1)}, u32[]{:S(2)}) copy-start(bf16[3584,512]{1,0:T(8,128)(2,1)} %refs_5_.3) | copy-start | bytes 11010052
  30.5 0.9 copy-start.9
  31.5 0.9 copy-start.12
  32.4 0.9 copy-start.15
  33.4 0.9 copy-start.18
  34.3 5.0 %copy-start.22 = (bf16[16,3584]{1,0:T(8,128)(2,1)}, bf16[16,3584]{1,0:T(8,128)(2,1)S(1)}, u32[]{:S(2)}) copy-start(bf16[16,3584]{1,0:T(8,128)(2,1)S(1)} %collective-permute-done.10.refs_10_.refs_12_) | copy-start | bytes 344068
  34.3 5.0 %copy-start.1 = (bf16[3584,512]{1,0:T(8,128)(2,1)S(1)}, bf16[3584,512]{1,0:T(8,128)(2,1)}, u32[]{:S(2)}) copy-start(bf16[3584,512]{1,0:T(8,128)(2,1)} %refs_5_.3) | copy-start | bytes 11010052
  34.3 5.0 %copy-start.3 = (bf16[128,3584]{1,0:T(8,128)(2,1)S(1)}, bf16[128,3584]{1,0:T(8,128)(2,1)}, u32[]{:S(2)}) copy-start(bf16[128,3584]{1,0:T(8,128)(2,1)} %refs_1_.3) | copy-start | bytes 2752516
  39.3 7.0 %copy-start.26 = (f32[1,512]{1,0:T(1,128)S(1)}, f32[1,512]{1,0:T(1,128)}, u32[]{:S(2)}) copy-start(f32[1,512]{1,0:T(1,128)} %get-tuple-element.49) | copy-start | bytes 6148
  43.1 1.3 %collective-permute-start.11 = (f32[6,4,128]{2,1,0:T(4,128)S(1)}, f32[6,4,128]{2,1,0:T(4,128)S(1)}, u32[]{:S(2)}, u32[]{:S(2)}) collective-permute-start(f32[6,4,128]{2,1,0:T(4,128)S(1)} %pad_maximum_fusion.1), channel_id=1, source_target_pairs={{0,8},{1,9},{2,10},{3,11},{4,12},{5,13},{6,14},{7,15},{8,0},{9,1},... | collective-permute-start | bytes 36872 | tf_op jit(solution)/shard_map/ppermute | solution.py:291
  45.0 7.8 %copy-start.25 = (f32[1,4,128]{2,1,0:T(4,128)}, f32[1,4,128]{2,1,0:T(4,128)S(1)}, u32[]{:S(2)}) copy-start(f32[1,4,128]{2,1,0:T(4,128)S(1)} %get-tuple-element.43) | copy-start | bytes 6148
  49.3 4.9 %collective-permute-start.14 = (f32[6,4,128]{2,1,0:T(4,128)}, f32[6,4,128]{2,1,0:T(4,128)}, u32[]{:S(2)}, u32[]{:S(2)}) collective-permute-start(f32[6,4,128]{2,1,0:T(4,128)} %constant_dynamic-update-slice_fusion), channel_id=1, source_target_pairs={{0,17},{1,16},{2,19},{3,18},{4,21},{5,20},{6,23},{7,22},{8,25},{9,... | collective-permute-start | bytes 36872 | tf_op jit(solution)/shard_map/ppermute | solution.py:291
  50.9 5.3 %collective-permute-start.13 = (f32[6,4,128]{2,1,0:T(4,128)}, f32[6,4,128]{2,1,0:T(4,128)S(1)}, u32[]{:S(2)}, u32[]{:S(2)}) collective-permute-start(f32[6,4,128]{2,1,0:T(4,128)} %constant_dynamic-update-slice_fusion), channel_id=1, source_target_pairs={{0,1},{1,0},{2,3},{3,2},{4,5},{5,4},{6,7},{7,6},{8,9},{9,8},{10,11... | collective-permute-start | bytes 36872 | tf_op jit(solution)/shard_map/ppermute | solution.py:291
  52.3 3.9 %collective-permute-start.12 = (f32[6,4,128]{2,1,0:T(4,128)}, f32[6,4,128]{2,1,0:T(4,128)S(1)}, u32[]{:S(2)}, u32[]{:S(2)}) collective-permute-start(f32[6,4,128]{2,1,0:T(4,128)} %constant_dynamic-update-slice_fusion), channel_id=1, source_target_pairs={{0,16},{1,17},{2,18},{3,19},{4,20},{5,21},{6,22},{7,23},{8,24},{9,... | collective-permute-start | bytes 36872 | tf_op jit(solution)/shard_map/ppermute | solution.py:291
  60.4 5.6 %collective-permute-start.17 = (f32[6,4,128]{2,1,0:T(4,128)S(1)}, f32[6,4,128]{2,1,0:T(4,128)S(1)}, u32[]{:S(2)}, u32[]{:S(2)}) collective-permute-start(f32[6,4,128]{2,1,0:T(4,128)S(1)} %get-tuple-element.26), channel_id=1, source_target_pairs={{0,6},{1,7},{2,4},{3,5},{4,2},{5,3},{6,0},{7,1},{8,14},{9,15},{10,... | collective-permute-start | bytes 36872 | tf_op jit(solution)/shard_map/ppermute | solution.py:291
  64.1 4.6 %collective-permute-start.16 = (f32[6,4,128]{2,1,0:T(4,128)S(1)}, f32[6,4,128]{2,1,0:T(4,128)S(1)}, u32[]{:S(2)}, u32[]{:S(2)}) collective-permute-start(f32[6,4,128]{2,1,0:T(4,128)S(1)} %get-tuple-element.26), channel_id=1, source_target_pairs={{0,4},{1,5},{2,6},{3,7},{4,0},{5,1},{6,2},{7,3},{8,12},{9,13},{10,... | collective-permute-start | bytes 36872 | tf_op jit(solution)/shard_map/ppermute | solution.py:291
  64.1 4.6 %collective-permute-start.15 = (f32[6,4,128]{2,1,0:T(4,128)S(1)}, f32[6,4,128]{2,1,0:T(4,128)S(1)}, u32[]{:S(2)}, u32[]{:S(2)}) collective-permute-start(f32[6,4,128]{2,1,0:T(4,128)S(1)} %get-tuple-element.26), channel_id=1, source_target_pairs={{0,2},{1,3},{2,0},{3,1},{4,6},{5,7},{6,4},{7,5},{8,10},{9,11},{10,... | collective-permute-start | bytes 36872 | tf_op jit(solution)/shard_map/ppermute | solution.py:291
  70.6 2.0 %copy-start.2 = (bf16[3584,512]{1,0:T(8,128)(2,1)S(1)}, bf16[3584,512]{1,0:T(8,128)(2,1)}, u32[]{:S(2)}) copy-start(bf16[3584,512]{1,0:T(8,128)(2,1)} %refs_5_.3) | copy-start | bytes 11010052
  75.3 3.9 %collective-permute-start.18 = (bf16[2,128,3584]{2,1,0:T(8,128)(2,1)S(1)}, bf16[2,128,3584]{2,1,0:T(8,128)(2,1)S(1)}, u32[]{:S(2)}, u32[]{:S(2)}) collective-permute-start(bf16[2,128,3584]{2,1,0:T(8,128)(2,1)S(1)} %get-tuple-element.19), channel_id=1, source_target_pairs={{0,8},{1,9},{2,10},{3,11},{4,12},{5,13},{6,14},{7,15},{8,0},{9,1},... | collective-permute-start | bytes 5505032 | tf_op jit(solution)/shard_map/ppermute | solution.py:291
  79.3 11.6 %collective-permute-start.25 = (bf16[2,2,1,2,16,1280]{5,4,3,2,1,0:T(8,128)(2,1)S(1)}, bf16[2,2,1,2,16,1280]{5,4,3,2,1,0:T(8,128)(2,1)S(1)}, u32[]{:S(2)}, u32[]{:S(2)}) collective-permute-start(bf16[2,2,1,2,16,1280]{5,4,3,2,1,0:T(8,128)(2,1)S(1)} %add_convert_fusion), channel_id=1, source_target_pairs={{0,2},{1,3},{2,0},{3,1},{4,6},{5,7},{6,4},{7,5},{8,10},{9,11},{10,... | collective-permute-start | bytes 983048 | tf_op jit(solution)/shard_map/ppermute | solution.py:291
  79.4 9.1 %collective-permute-start.19 = (bf16[1,2,2,2,16,1152]{5,4,3,2,1,0:T(8,128)(2,1)S(1)}, bf16[1,2,2,2,16,1152]{5,4,3,2,1,0:T(8,128)(2,1)S(1)}, u32[]{:S(2)}, u32[]{:S(2)}) collective-permute-start(bf16[1,2,2,2,16,1152]{5,4,3,2,1,0:T(8,128)(2,1)S(1)} %add_convert_fusion.2), channel_id=1, source_target_pairs={{0,16},{1,17},{2,18},{3,19},{4,20},{5,21},{6,22},{7,23},{8,24},{9,... | collective-permute-start | bytes 884744 | tf_op jit(solution)/shard_map/ppermute | solution.py:291
  80.1 9.1 %collective-permute-start.22 = (bf16[2,2,2,1,16,1152]{5,4,3,2,1,0:T(8,128)(2,1)S(1)}, bf16[2,2,2,1,16,1152]{5,4,3,2,1,0:T(8,128)(2,1)S(1)}, u32[]{:S(2)}, u32[]{:S(2)}) collective-permute-start(bf16[2,2,2,1,16,1152]{5,4,3,2,1,0:T(8,128)(2,1)S(1)} %add_convert_fusion.1), channel_id=1, source_target_pairs={{0,1},{1,0},{2,3},{3,2},{4,5},{5,4},{6,7},{7,6},{8,9},{9,8},{10,11... | collective-permute-start | bytes 884744 | tf_op jit(solution)/shard_map/ppermute | solution.py:291
  88.6 5.2 %collective-permute-start.20 = (bf16[1,2,2,1,16,1152]{5,4,3,2,1,0:T(8,128)(2,1)S(1)}, bf16[1,2,2,1,16,1152]{5,4,3,2,1,0:T(8,128)(2,1)S(1)}, u32[]{:S(2)}, u32[]{:S(2)}) collective-permute-start(bf16[1,2,2,1,16,1152]{5,4,3,2,1,0:T(8,128)(2,1)S(1)} %add_convert_fusion.5), channel_id=1, source_target_pairs={{0,1},{1,0},{2,3},{3,2},{4,5},{5,4},{6,7},{7,6},{8,9},{9,8},{10,11... | collective-permute-start | bytes 442376 | tf_op jit(solution)/shard_map/ppermute | solution.py:291
  89.2 8.8 %collective-permute-start.23 = (bf16[2,2,1,1,16,1152]{5,4,3,2,1,0:T(8,128)(2,1)S(1)}, bf16[2,2,1,1,16,1152]{5,4,3,2,1,0:T(8,128)(2,1)S(1)}, u32[]{:S(2)}, u32[]{:S(2)}) collective-permute-start(bf16[2,2,1,1,16,1152]{5,4,3,2,1,0:T(8,128)(2,1)S(1)} %add_convert_fusion.4), channel_id=1, source_target_pairs={{0,2},{1,3},{2,0},{3,1},{4,6},{5,7},{6,4},{7,5},{8,10},{9,11},{10,... | collective-permute-start | bytes 442376 | tf_op jit(solution)/shard_map/ppermute | solution.py:291
  91.0 5.4 %collective-permute-start.26 = (bf16[1,2,1,2,16,1280]{5,4,3,2,1,0:T(8,128)(2,1)S(1)}, bf16[1,2,1,2,16,1280]{5,4,3,2,1,0:T(8,128)(2,1)S(1)}, u32[]{:S(2)}, u32[]{:S(2)}) collective-permute-start(bf16[1,2,1,2,16,1280]{5,4,3,2,1,0:T(8,128)(2,1)S(1)} %add_convert_fusion.3), channel_id=1, source_target_pairs={{0,16},{1,17},{2,18},{3,19},{4,20},{5,21},{6,22},{7,23},{8,24},{9,... | collective-permute-start | bytes 491528 | tf_op jit(solution)/shard_map/ppermute | solution.py:291
  93.8 11.2 %copy-start.5 = (bf16[32,3584]{1,0:T(8,128)(2,1)S(1)}, bf16[32,3584]{1,0:T(8,128)(2,1)}, u32[]{:S(2)}) copy-start(bf16[32,3584]{1,0:T(8,128)(2,1)} %copy-done.4) | copy-start | bytes 688132
  93.8 11.2 %copy-start.7 = (bf16[32,3584]{1,0:T(8,128)(2,1)S(1)}, bf16[32,3584]{1,0:T(8,128)(2,1)}, u32[]{:S(2)}) copy-start(bf16[32,3584]{1,0:T(8,128)(2,1)} %copy-done.6) | copy-start | bytes 688132
  93.8 11.2 %copy-start.10 = (bf16[32,3584]{1,0:T(8,128)(2,1)S(1)}, bf16[32,3584]{1,0:T(8,128)(2,1)}, u32[]{:S(2)}) copy-start(bf16[32,3584]{1,0:T(8,128)(2,1)} %copy-done.8) | copy-start | bytes 688132
  93.9 11.2 %copy-start.13 = (bf16[32,3584]{1,0:T(8,128)(2,1)S(1)}, bf16[32,3584]{1,0:T(8,128)(2,1)}, u32[]{:S(2)}) copy-start(bf16[32,3584]{1,0:T(8,128)(2,1)} %copy-done.11) | copy-start | bytes 688132
  93.9 11.2 %copy-start.16 = (bf16[32,3584]{1,0:T(8,128)(2,1)S(1)}, bf16[32,3584]{1,0:T(8,128)(2,1)}, u32[]{:S(2)}) copy-start(bf16[32,3584]{1,0:T(8,128)(2,1)} %copy-done.14) | copy-start | bytes 688132
  93.9 11.2 %copy-start.19 = (bf16[32,3584]{1,0:T(8,128)(2,1)S(1)}, bf16[32,3584]{1,0:T(8,128)(2,1)}, u32[]{:S(2)}) copy-start(bf16[32,3584]{1,0:T(8,128)(2,1)} %copy-done.17) | copy-start | bytes 688132
  93.9 11.2 %copy-start.21 = (bf16[16,3584]{1,0:T(8,128)(2,1)S(1)}, bf16[16,3584]{1,0:T(8,128)(2,1)}, u32[]{:S(2)}) copy-start(bf16[16,3584]{1,0:T(8,128)(2,1)} %copy-done.20) | copy-start | bytes 344068
  93.9 11.2 %copy-start.23 = (bf16[16,3584]{1,0:T(8,128)(2,1)S(1)}, bf16[16,3584]{1,0:T(8,128)(2,1)}, u32[]{:S(2)}) copy-start(bf16[16,3584]{1,0:T(8,128)(2,1)} %copy-done.22) | copy-start | bytes 344068
  93.9 4.4 %collective-permute-start.21 = (bf16[1,2,1,1,16,1152]{5,4,3,2,1,0:T(8,128)(2,1)S(1)}, bf16[1,2,1,1,16,1152]{5,4,3,2,1,0:T(8,128)(2,1)S(1)}, u32[]{:S(2)}, u32[]{:S(2)}) collective-permute-start(bf16[1,2,1,1,16,1152]{5,4,3,2,1,0:T(8,128)(2,1)S(1)} %add_convert_fusion.8), channel_id=1, source_target_pairs={{0,2},{1,3},{2,0},{3,1},{4,6},{5,7},{6,4},{7,5},{8,10},{9,11},{10,... | collective-permute-start | bytes 221192 | tf_op jit(solution)/shard_map/ppermute | solution.py:291
  96.4 4.5 %collective-permute-start.27 = (bf16[1,2,1,1,16,1280]{5,4,3,2,1,0:T(8,128)(2,1)S(1)}, bf16[1,2,1,1,16,1280]{5,4,3,2,1,0:T(8,128)(2,1)S(1)}, u32[]{:S(2)}, u32[]{:S(2)}) collective-permute-start(bf16[1,2,1,1,16,1280]{5,4,3,2,1,0:T(8,128)(2,1)S(1)} %add_convert_fusion.6), channel_id=1, source_target_pairs={{0,1},{1,0},{2,3},{3,2},{4,5},{5,4},{6,7},{7,6},{8,9},{9,8},{10,11... | collective-permute-start | bytes 245768 | tf_op jit(solution)/shard_map/ppermute | solution.py:291
  98.4 4.4 %collective-permute-start.24 = (bf16[1,2,1,1,16,1152]{5,4,3,2,1,0:T(8,128)(2,1)S(1)}, bf16[1,2,1,1,16,1152]{5,4,3,2,1,0:T(8,128)(2,1)S(1)}, u32[]{:S(2)}, u32[]{:S(2)}) collective-permute-start(bf16[1,2,1,1,16,1152]{5,4,3,2,1,0:T(8,128)(2,1)S(1)} %get-tuple-element.45), channel_id=1, source_target_pairs={{0,16},{1,17},{2,18},{3,19},{4,20},{5,21},{6,22},{7,23},{8,24},{9,... | collective-permute-start | bytes 221192 | tf_op jit(solution)/shard_map/ppermute | solution.py:291
  102.9 10.8 %collective-permute-start.28 = (bf16[1,1,1,1,16,3584]{5,4,3,2,1,0:T(8,128)(2,1)S(1)}, bf16[1,1,1,1,16,3584]{5,4,3,2,1,0:T(8,128)(2,1)S(1)}, u32[]{:S(2)}, u32[]{:S(2)}) collective-permute-start(bf16[1,1,1,1,16,3584]{5,4,3,2,1,0:T(8,128)(2,1)S(1)} %slice.938), channel_id=1, source_target_pairs={{0,4},{1,5},{2,6},{3,7},{4,0},{5,1},{6,2},{7,3},{8,12},{9,13},{10,... | collective-permute-start | bytes 344072 | tf_op jit(solution)/shard_map/ppermute | solution.py:291

commit v3 on v2

--- a/solution.py
+++ b/solution.py
@@ -10,7 +10,7 @@
 AXES = ("grp", "vocab")
 VMEM = pl.BlockSpec(memory_space=pltpu.VMEM)
 SMEM = pl.BlockSpec(memory_space=pltpu.SMEM)
-ANY = pl.BlockSpec(memory_space=pl.ANY)
+HBM = pl.BlockSpec(memory_space=pltpu.HBM)
 PARAMS = pltpu.CompilerParams(vmem_limit_bytes=40 * 2**20)
 STAT_ROWS = 8
 
@@ -72,11 +72,8 @@
 
 def logits_kernel(spots, splits, *refs):
     n = len(spots)
-    at_ref, pieces, (w_ref, logits_ref, stats_ref, full, weights, sems, wsems) = (
-        refs[0],
-        refs[1 : 1 + n],
-        refs[1 + n :],
-    )
+    at_ref, pieces, rest = refs[0], refs[1 : 1 + n], refs[1 + n :]
+    w_ref, logits_ref, stats_ref, rows_ref, full, weights, sems, wsems, osem = rest
     places = [spot if isinstance(spot, int) else at_ref[spot[0]] for spot in spots]
     copies = place_copies(pieces, places, full, sems)
     depth = w_ref.shape[0]
@@ -89,6 +86,8 @@
         wcopies.append(copy)
     for copy in copies:
         copy.wait()
+    out = pltpu.make_async_copy(full, rows_ref, osem)
+    out.start()
     total = None
     for c in range(splits):
         wcopies[c].wait()
@@ -108,6 +107,7 @@
             jnp.sum(soft, axis=1, keepdims=True),
         ]
     )
+    out.wait()
 
 
 def student_logits(at, pieces, spots, head_weight):
@@ -119,14 +119,16 @@
         out_shape=(
             jax.ShapeDtypeStruct((rows, cols), F32),
             jax.ShapeDtypeStruct((STAT_ROWS, rows), F32),
-        ),
-        in_specs=[SMEM] + [ANY] * (len(pieces) + 1),
-        out_specs=(VMEM, VMEM),
+            jax.ShapeDtypeStruct((rows, depth), BF16),
+        ),
+        in_specs=[SMEM] + [HBM] * (len(pieces) + 1),
+        out_specs=(VMEM, VMEM, HBM),
         scratch_shapes=[
             pltpu.VMEM((rows, depth), BF16),
             pltpu.VMEM((depth, cols), BF16),
             pltpu.SemaphoreType.DMA((len(pieces),)),
             pltpu.SemaphoreType.DMA((splits,)),
+            pltpu.SemaphoreType.DMA,
         ],
         compiler_params=PARAMS,
         cost_estimate=pl.CostEstimate(
@@ -138,9 +140,14 @@
     )(at, *pieces, head_weight)
 
 
-def back_kernel(chunk, at_ref, top_ref, low_ref, aligned_ref, stats_ref, w_ref, grad_ref, back_ref, mixed, weights, wsem):
-    copy = pltpu.make_async_copy(w_ref, weights, wsem)
-    copy.start()
+def back_kernel(chunk, at_ref, top_ref, low_ref, aligned_ref, stats_ref, w_ref, grad_ref, back_ref, mixed, weights, wsems):
+    depth = weights.shape[0]
+    copies = []
+    for c in range(depth // chunk):
+        part = pl.ds(c * chunk, chunk)
+        copy = pltpu.make_async_copy(w_ref.at[part], weights.at[part], wsems.at[c])
+        copy.start()
+        copies.append(copy)
     first = at_ref[0]
     flip = at_ref[1]
     per, cols = top_ref.shape
@@ -150,7 +157,7 @@
     ).astype(BF16)
     column = first + lax.broadcasted_iota(jnp.int32, (per, cols), 1)
     for k, logits_ref in enumerate((top_ref, low_ref)):
-        stats = jnp.concatenate([stats_ref[k, 0], jnp.zeros((128 - STAT_ROWS, per), F32)]).T
+        stats = jnp.concatenate([stats_ref[k], jnp.zeros((128 - STAT_ROWS, per), F32)]).T
         peak, hard, soft, tpeak, tsum, ids = [stats[:, i : i + 1] for i in range(6)]
         half = jnp.exp((logits_ref[...] - peak) * 0.5)
         taught = jnp.exp((aligned_ref[k, 0].astype(F32) - tpeak) * 0.5)
@@ -159,11 +166,10 @@
         grad = grad.astype(BF16)
         grad_ref[k] = grad
         mixed[k * per : (k + 1) * per, :] = jnp.dot(turn, grad, preferred_element_type=F32).astype(BF16)
-    copy.wait()
-    depth = weights.shape[0]
     rows = mixed[...]
     for c in range(depth // chunk):
         part = slice(c * chunk, (c + 1) * chunk)
+        copies[c].wait()
         out = lax.dot_general(
             rows, weights[part, :], (((1,), (1,)), ((), ())), preferred_element_type=F32
         ).astype(BF16)
@@ -188,8 +194,8 @@
             pl.BlockSpec((per, cols), lambda i: (which, 0)),
             pl.BlockSpec((per, cols), lambda i: (which, 0)),
             pl.BlockSpec((2, 1, per, cols), paired),
-            pl.BlockSpec((2, 1, STAT_ROWS, per), paired),
-            ANY,
+            pl.BlockSpec((2, STAT_ROWS, per), lambda i: (0, 0, which)),
+            HBM,
         ],
         out_specs=(
             pl.BlockSpec((2, per, cols), lambda i: (0, 0, 0)),
@@ -198,7 +204,7 @@
         scratch_shapes=[
             pltpu.VMEM((2 * per, cols), BF16),
             pltpu.VMEM((depth, cols), BF16),
-            pltpu.SemaphoreType.DMA,
+            pltpu.SemaphoreType.DMA((depth // chunk,)),
         ],
         compiler_params=PARAMS,
         cost_estimate=pl.CostEstimate(
@@ -210,69 +216,95 @@
     )(at, near, far, aligned, stats, head_weight)
 
 
-def head_kernel(spots, *refs):
-    n = len(spots)
-    at_ref, pieces, (even_ref, odd_ref, out_ref, full, sems) = refs[0], refs[1 : 1 + n], refs[1 + n :]
-    step = pl.program_id(0)
-
-    @pl.when(step == 0)
+def head_kernel(near_ref, far_ref, even_ref, odd_ref, out_ref, grads):
+    @pl.when(pl.program_id(0) == 0)
     def _():
-        places = [spot if isinstance(spot, int) else at_ref[spot[0]] for spot in spots]
-        for copy in place_copies(pieces, places, full, sems):
-            copy.wait()
-
-    tile = out_ref.shape[0]
-    part = pl.ds(pl.multiple_of(step * tile, tile), tile)
-    grads = jnp.concatenate([even_ref[0], odd_ref[0], even_ref[1], odd_ref[1]])
+        per = even_ref.shape[1]
+        for k, block in enumerate((even_ref[0], odd_ref[0], even_ref[1], odd_ref[1])):
+            grads[k * per : (k + 1) * per, :] = block
+
+    rows = jnp.concatenate([near_ref[...], far_ref[...]])
     out_ref[...] = lax.dot_general(
-        full[:, part], grads, (((0,), (0,)), ((), ())), preferred_element_type=F32
+        rows, grads[...], (((0,), (0,)), ((), ())), preferred_element_type=F32
     ).astype(BF16)
 
 
-def head_gradient(at, pieces, spots, even, odd):
-    depth = pieces[0].shape[1]
-    rows = sum(piece.shape[0] for piece in pieces)
+def head_gradient(near, far, even, odd):
+    rows, depth = near.shape
     _, per, cols = even.shape
     tile = 512 if depth % 512 == 0 else depth
     whole = pl.BlockSpec((2, per, cols), lambda i: (0, 0, 0))
-    return pl.pallas_call(
-        lambda *refs: head_kernel(spots, *refs),
+    slab = pl.BlockSpec((rows, tile), lambda i: (0, i))
+    return pl.pallas_call(
+        head_kernel,
         grid=(depth // tile,),
         out_shape=jax.ShapeDtypeStruct((depth, cols), BF16),
-        in_specs=[SMEM] + [ANY] * len(pieces) + [whole, whole],
+        in_specs=[slab, slab, whole, whole],
         out_specs=pl.BlockSpec((tile, cols), lambda i: (i, 0)),
-        scratch_shapes=[
-            pltpu.VMEM((rows, depth), BF16),
-            pltpu.SemaphoreType.DMA((len(pieces),)),
-        ],
+        scratch_shapes=[pltpu.VMEM((4 * per, cols), BF16)],
         compiler_params=PARAMS,
         cost_estimate=pl.CostEstimate(
-            flops=2 * rows * depth * cols,
-            bytes_accessed=(rows + cols) * depth * 2 + rows * cols * 2,
+            flops=4 * rows * depth * cols,
+            bytes_accessed=(2 * rows + cols) * depth * 2 + 2 * rows * cols * 2,
             transcendentals=0,
         ),
         name="head_gradient",
-    )(at, *pieces, even, odd)
-
-
-def flip_groups(stats, mask):
-    groups = stats.shape[1]
-    return jnp.stack([stats[:, j ^ mask] for j in range(groups)], axis=1)
-
-
-def merge(parts):
-    peak, tpeak = parts[0][0], parts[0][3]
-    ids = parts[0][5]
-    for part in parts[1:]:
-        peak, tpeak = jnp.maximum(peak, part[0]), jnp.maximum(tpeak, part[3])
-        ids = jnp.maximum(ids, part[5])
-    hard = soft = tsum = 0.0
-    for part in parts:
-        shrink = jnp.exp((part[0] - peak) * 0.5)
-        hard = hard + part[1] * (shrink * shrink)
-        soft = soft + part[2] * shrink
-        tsum = tsum + part[4] * jnp.exp((part[3] - tpeak) * 0.5)
-    return jnp.stack([peak, hard, soft, tpeak, tsum, ids])
+    )(near, far, even, odd)
+
+
+def merge_rows(a, b):
+    top = jnp.maximum(a, b)
+    peak, tpeak = top[0:1], top[3:4]
+    shrink = []
+    for part in (a, b):
+        s = jnp.exp((part[0:1] - peak) * 0.5)
+        t = jnp.exp((part[3:4] - tpeak) * 0.5)
+        shrink.append((part[1:2] * (s * s), part[2:3] * s, part[4:5] * t))
+    hard, soft, tsum = [p + q for p, q in zip(*shrink)]
+    return jnp.concatenate([peak, hard, soft, tpeak, tsum, top[5:]])
+
+
+def merge_kernel(order, mine_ref, got_ref, out_ref):
+    per = mine_ref.shape[2]
+    for p in range(2):
+        for i in range(2):
+            here = (p, slice(None), slice(i * per // 2, (i + 1) * per // 2))
+            q, j = order(p, i)
+            there = (q, slice(None), slice(j * per // 2, (j + 1) * per // 2))
+            out_ref[here] = merge_rows(mine_ref[here], got_ref[there])
+
+
+def merge(mine, got, mask):
+    order = lambda p, i: (p ^ (mask >> 1), i ^ (mask & 1))
+    return pl.pallas_call(
+        lambda *refs: merge_kernel(order, *refs),
+        out_shape=jax.ShapeDtypeStruct(mine.shape, F32),
+        in_specs=[VMEM, VMEM],
+        out_specs=VMEM,
+        cost_estimate=pl.CostEstimate(flops=0, bytes_accessed=3 * mine.size * 4, transcendentals=0),
+        name="merge_stats",
+    )(mine, got)
+
+
+def gather_kernel(near_ref, far_ref, tstats_ref, ids_ref, out_ref):
+    per2 = near_ref.shape[1]
+    per = per2 // 2
+    for p, ref in enumerate((near_ref, far_ref)):
+        out_ref[p, 0:3, :] = ref[0:3, :]
+        out_ref[p, 3:5, :] = tstats_ref[0:2, p * per2 : (p + 1) * per2]
+        out_ref[p, 5:8, :] = jnp.zeros((3, per2), F32)
+    out_ref[0, 5:6, 0:per] = ids_ref[...].astype(F32)
+
+
+def first_stats(near, far, tstats, ids):
+    return pl.pallas_call(
+        gather_kernel,
+        out_shape=jax.ShapeDtypeStruct((2,) + near.shape, F32),
+        in_specs=[VMEM] * 4,
+        out_specs=VMEM,
+        cost_estimate=pl.CostEstimate(flops=0, bytes_accessed=2 * near.size * 8, transcendentals=0),
+        name="first_stats",
+    )(near, far, tstats, ids.reshape(1, -1))
 
 
 def body(hidden, token_ids, serving, head_weight, teacher_logits):
@@ -291,51 +323,37 @@
         return lax.ppermute(value, AXES, [(i, i ^ mask) for i in range(count)])
 
     quarter_rows = per // 4
-    half_rows = quarter_rows // 2
     quarter = me_v & 3
-    x0 = swap(lax.dynamic_slice_in_dim(hidden, quarter * quarter_rows, quarter_rows, 0), X)
+    starts = [(quarter ^ k) * quarter_rows for k in range(4)]
+    first = lax.dynamic_slice_in_dim(hidden, starts[0], quarter_rows, 0)
+    second = lax.dynamic_slice_in_dim(hidden, starts[3], quarter_rows, 0)
+    x0 = swap(first, X)
+    x3 = swap(second, X)
     from_core = swap(hidden, CORE)
     arrived = lax.all_to_all(teacher_logits, "grp", split_axis=1, concat_axis=0, tiled=True)
     x1 = swap(x0, Y)
     x2 = swap(x0, W)
-    x3a = swap(x2[:half_rows], Y)
-    x3b = swap(x1[half_rows:], W)
-    xs = [x0, x1, x2, x3a, x3b]
-    ds = [swap(piece, CORE) for piece in xs]
-    starts = [
-        (quarter ^ k) * quarter_rows + extra
-        for k, extra in ((0, 0), (1, 0), (2, 0), (3, 0), (3, half_rows))
-    ]
-    late_at = jnp.stack([s for s in starts] + [per + s for s in starts]).astype(jnp.int32)
-    all_at = late_at + 2 * per
-    late = xs + ds
-    late_spots = [(k,) for k in range(10)]
-
-    near_logits, near_stats = student_logits(late_at, [hidden, from_core], [0, per], head_weight)
+    late_at = jnp.stack(starts + [per + s for s in starts]).astype(jnp.int32)
+    near_logits, near_stats, near_rows = student_logits(
+        late_at, [hidden, from_core], [0, per], head_weight
+    )
     aligned, tstats = teacher_rows(
         me_g.astype(jnp.int32).reshape(1), serving, arrived.reshape(groups * per, cols), groups
     )
-    far_logits, far_stats = student_logits(late_at, late, late_spots, head_weight)
-
-    mine = jnp.concatenate([near_stats[:3], far_stats[:3]], axis=1)
-    ids = jnp.concatenate([token_ids.astype(F32), jnp.zeros(((groups - 1) * per,), F32)])
-    stats = jnp.concatenate([mine, tstats[:2], ids[None]]).reshape(6, groups, per)
-    stats = merge([stats, flip_groups(swap(stats, CORE), 1)])
-    stats = merge(
-        [
-            stats,
-            flip_groups(swap(stats, X), 2),
-            swap(stats, Y),
-            flip_groups(swap(stats, X + Y), 2),
-        ]
+    x1, near_logits = lax.optimization_barrier((x1, near_logits))
+    xs = [x0, x1, x2, x3]
+    ds = [swap(piece, CORE) for piece in xs]
+    far_logits, far_stats, far_rows = student_logits(
+        late_at, xs + ds, [(k,) for k in range(8)], head_weight
     )
-    mask = W
+
+    stats = first_stats(near_stats, far_stats, tstats, token_ids)
+    stats = merge(stats, swap(stats, CORE), 1)
+    stats = merge(stats, swap(stats, X), 2)
+    mask = Y
     while mask < shards:
-        masks = [mask, 2 * mask, 3 * mask] if 2 * mask < shards else [mask]
-        stats = merge([stats] + [swap(stats, m) for m in masks])
-        mask *= 4
-    stats = jnp.concatenate([stats, jnp.zeros((STAT_ROWS - 6, groups, per), F32)])
-    stats = stats.swapaxes(0, 1).reshape(2, 2, STAT_ROWS, per)
+        stats = merge(stats, swap(stats, mask), 0)
+        mask *= 2
 
     at = jnp.stack([(me_g * shards + me_v) * cols, me_v * owned]).astype(jnp.int32)
     pairs = aligned.reshape(2, 2, per, cols)
@@ -354,27 +372,24 @@
     third = units // 3
     edges = [0, third * 128, 2 * third * 128, depth]
     orders = [(0, ydim, wdim), (ydim, wdim, 0), (wdim, 0, ydim)]
-    parts = []
-    for p, order in enumerate(orders):
-        terms = [h[..., edges[p] : edges[p + 1]] for h in held]
-        for dim in order:
-            sent = sum(lax.index_in_dim(t, 1, dim).astype(F32) for t in terms).astype(BF16)
-            got = swap(sent, masks[dim])
-            terms = [lax.index_in_dim(t, 0, dim) for t in terms] + [got]
-        parts.append(terms)
-    parts = [
-        sum(t.astype(F32) for t in terms) for terms in parts
-    ]
-    total = jnp.concatenate(parts, axis=-1)
+    parts = [[h[..., edges[p] : edges[p + 1]] for h in held] for p in range(3)]
+    grad_head = None
+    for stage in range(3):
+        sents = [
+            sum(lax.index_in_dim(t, 1, orders[p][stage]).astype(F32) for t in parts[p]).astype(BF16)
+            for p in range(3)
+        ]
+        gots = [swap(sents[p], masks[orders[p][stage]]) for p in range(3)]
+        if stage == 0:
+            grad_head = head_gradient(near_rows, far_rows, even, odd)
+            grad_head, *gots = lax.optimization_barrier((grad_head, *gots))
+        for p in range(3):
+            parts[p] = [lax.index_in_dim(t, 0, orders[p][stage]) for t in parts[p]] + [gots[p]]
+    total = jnp.concatenate([sum(t.astype(F32) for t in terms) for terms in parts], axis=-1)
     for dim in range(1, wdim):
         got = swap(lax.index_in_dim(total, 1, dim).astype(BF16), masks[dim])
         total = lax.index_in_dim(total, 0, dim) + got.astype(F32)
-    grad_hidden = total.reshape(owned, depth)
-
-    grad_head = head_gradient(
-        all_at, [hidden, from_core] + late, [0, per] + late_spots, even, odd
-    )
-    return (grad_hidden, grad_head)
+    return (total.reshape(owned, depth), grad_head)
 
 
 def solution(mesh):

time: 115 us -> 117 us (1.017)
  other arithmetic: 12.5 us -> 1.49 us
  waiting for transfers between devices: 28.2 us -> 36.4 us
  Pallas kernels: 22.6 us -> 30.1 us
  starting transfers between devices: 33 us -> 28.1 us
  local copies, waits for them, and re-layouts: 17 us -> 19.1 us
    ppermute x29 -> x25, waiting for transfers between devices: 28.2 us -> 36 us  [swap(): return lax.ppermute(value, AXES, [(i, i ^ mask) for i in range(count)])]
    unnamed x10 -> x0, other arithmetic: 7.13 us -> none
    unnamed x59 -> x43, local copies, waits for them, and re-layouts: 11.3 us -> 17.9 us
    ppermute x29 -> x25, starting transfers between devices: 29.5 us -> 23.9 us  [swap(): return lax.ppermute(value, AXES, [(i, i ^ mask) for i in range(count)])]
    pallas_call x1 -> x7, Pallas kernels: 8.64 us -> 13.4 us  [the longest x5 6.8 us: merge(): pl.pallas_call(lambda *refs: merge_kernel(order, *refs), out_shape=jax.Sh...]
    slice x9 -> x0, local copies, waits for them, and re-layouts: 2.79 us -> none  [the longest x3 0.8 us: flip_groups(): return jnp.stack([stats[:, j ^ mask] for j in range(groups)], axis=1)]
    pallas_call x2, Pallas kernels: 5.27 us -> 7.79 us  [back_rows(): pl.pallas_call(lambda *refs: back_kernel(chunk, *refs), grid=(1,), out_sh...]
    another operation x3 -> x0, other arithmetic: 1.98 us -> none  [the longest x2 1.96 us: merge(): return jnp.stack([peak, hard, soft, tpeak, tsum, ids])]
  transfers between devices with their start and end apart: 30 -> 26, of which waited for: 15 -> 14; matrix products, arithmetic and copies ran while one was open for 7% -> 3% of each run, Pallas kernels for 15% -> 12%
where the time goes in v3:
time: 117 us; the launch traced here: 116 us
  waiting for transfers between devices  36.4 us (31%)
  Pallas kernels  30.1 us (26%)
  starting transfers between devices  28.1 us (24%)
  local copies, waits for them, and re-layouts  19.1 us (16%)
  other arithmetic  1.49 us (1%)
    ppermute x25, waiting for transfers between devices, swap(): return lax.ppermute(value, AXES, [(i, i ^ mask) for i in range(count)])  36 us
    ppermute x25, starting transfers between devices, swap(): return lax.ppermute(value, AXES, [(i, i ^ mask) for i in range(count)])  23.9 us
    unnamed x43, local copies, waits for them, and re-layouts  17.9 us
    pallas_call x2, Pallas kernels, back_rows(): pl.pallas_call(lambda *refs: back_kernel(chunk, *refs), grid=(1,), out_sh...  7.79 us
    pallas_call x2, Pallas kernels, student_logits(): pl.pallas_call(lambda *refs: logits_kernel(spots, splits, *refs), out_sha...  7.15 us
    pallas_call x5, Pallas kernels, merge(): pl.pallas_call(lambda *refs: merge_kernel(order, *refs), out_shape=jax.Sh...  6.8 us
    pallas_call x1, Pallas kernels, head_gradient(): pl.pallas_call(head_kernel, grid=(depth // tile,), out_shape=jax.ShapeDty...  5.24 us
    all_to_all x1, starting transfers between devices, body(): lax.all_to_all(teacher_logits, 'grp', split_axis=1, concat_axis=0, tiled=...  4.14 us
  transfers between devices with their start and end apart: 26, of which 14 were waited for; matrix products, arithmetic and copies ran while one was open for 3% of the time, Pallas kernels for 12%

profile of v3, /device:TPU:0, one launch (start us, length us, event | category | flops | bytes accessed | tf_op | source)
XLA Modules:
  0.0 116.1 jit_solution(6608101961658335333)
XLA Ops:
  0.6 0.5 collective-permute-start.2
  1.2 1.1 constant_dynamic-slice_fusion
  2.2 2.6 %collective-permute-start = (bf16[32,3584]{1,0:T(8,128)(2,1)S(1)}, bf16[32,3584]{1,0:T(8,128)(2,1)}, u32[]{:S(2)}, u32[]{:S(2)}) collective-permute-start(bf16[32,3584]{1,0:T(8,128)(2,1)S(1)} %get-tuple-element.41), channel_id=1, source_target_pairs={{0,16},{1,17},{2,18},{3,19},{4,20},{5,21},{6,22},{7,23},{8,24},{9,... | collective-permute-start | bytes 688136 | tf_op jit(solution)/shard_map/ppermute | solution.py:323
  5.0 6.5 %collective-permute-done.refs_1_ = bf16[32,3584]{1,0:T(8,128)(2,1)} collective-permute-done((bf16[32,3584]{1,0:T(8,128)(2,1)S(1)}, bf16[32,3584]{1,0:T(8,128)(2,1)}, u32[]{:S(2)}, u32[]{:S(2)}) %collective-permute-start) | collective-permute-done | bytes 229408 | tf_op jit(solution)/shard_map/ppermute | solution.py:323
  11.4 2.0 %collective-permute-start.3 = (bf16[32,3584]{1,0:T(8,128)(2,1)}, bf16[32,3584]{1,0:T(8,128)(2,1)}, u32[]{:S(2)}, u32[]{:S(2)}) collective-permute-start(bf16[32,3584]{1,0:T(8,128)(2,1)} %collective-permute-done.refs_1_), channel_id=1, source_target_pairs={{0,2},{1,3},{2,0},{3,1},{4,6},{5,7},{6,4},{7,5},{8,10},{9,11},{10,... | collective-permute-start | bytes 688136 | tf_op jit(solution)/shard_map/ppermute | solution.py:323
  13.5 1.5 %collective-permute-start.1 = (bf16[32,3584]{1,0:T(8,128)(2,1)}, bf16[32,3584]{1,0:T(8,128)(2,1)}, u32[]{:S(2)}, u32[]{:S(2)}) collective-permute-start(bf16[32,3584]{1,0:T(8,128)(2,1)} %collective-permute-done.refs_1_), channel_id=1, source_target_pairs={{0,1},{1,0},{2,3},{3,2},{4,5},{5,4},{6,7},{7,6},{8,9},{9,8},{10,11... | collective-permute-start | bytes 688136 | tf_op jit(solution)/shard_map/ppermute | solution.py:323
  15.0 1.9 %copy.8 = bf16[128,4,512]{2,0,1:T(8,128)(2,1)} copy(bf16[128,4,512]{2,1,0:T(4,128)(2,1)} %param.9) | data formatting | bytes 1048576 | tf_op args[4]
  16.9 4.1 %all-to-all-start = ((bf16[128,4,512]{2,0,1:T(8,128)(2,1)}), bf16[128,4,512]{2,0,1:T(8,128)(2,1)}, u32[]{:S(2)}, u32[]{:S(2)}) async-start(bf16[128,4,512]{2,0,1:T(8,128)(2,1)} %copy.8), calls=%async_computation | async-start | bytes 1048576 | tf_op jit(solution)/shard_map/all_to_all | solution.py:333
  21.2 0.4 collective-permute-start.5
  21.7 0.4 collective-permute-start.7
  22.2 0.9 copy-done.6
  23.1 2.0 %copy-done = bf16[3584,512]{1,0:T(8,128)(2,1)S(1)} copy-done((bf16[3584,512]{1,0:T(8,128)(2,1)S(1)}, bf16[3584,512]{1,0:T(8,128)(2,1)}, u32[]{:S(2)}) %copy-start) | copy-done | bytes 3670040
  25.1 1.2 %copy-done.7 = bf16[128,3584]{1,0:T(8,128)(2,1)S(1)} copy-done((bf16[128,3584]{1,0:T(8,128)(2,1)S(1)}, bf16[128,3584]{1,0:T(8,128)(2,1)}, u32[]{:S(2)}) %copy-start.7) | copy-done | bytes 917528
  26.3 3.1 %student_logits.2 = (f32[256,512]{1,0:T(8,128)S(1)}, f32[8,256]{1,0:T(8,128)S(1)}, bf16[256,3584]{1,0:T(8,128)(2,1)S(1)}) custom-call(s32[8]{0:T(128)S(1)} %stack.47.refs_0_, bf16[128,3584]{1,0:T(8,128)(2,1)S(1)} %copy-done.3, bf16[128,3584]{1,0:T(8,128)(2,1)S(1)} %copy-done.7, bf16[3584,512]{1,0:T(8,128)(2,1)S(1)} %copy-done), custom_call_target="tpu_custom_call" | custom-call | flops 939524096 | bytes 6029312 | tf_op jit(solution)/shard_map/student_logits/pallas_call | solution.py:117
  29.6 0.4 all-to-all-done
  30.0 1.8 %teacher_rows.1 = (bf16[4,128,512]{2,1,0:T(8,128)(2,1)S(1)}, f32[8,512]{1,0:T(8,128)S(1)}) custom-call(s32[1]{0:T(128)} %bitcast.10.me_ref, s32[4,1,128]{2,1,0:T(1,128)S(1)} %bitcast.36, bf16[512,512]{1,0:T(8,128)(2,1)} %bitcast.14.arrived_ref), custom_call_target="tpu_custom_call" | custom-call | flops 268435456 | bytes 1048576 | tf_op jit(solution)/shard_map/teacher_rows/pallas_call | solution.py:46
  31.8 0.6 copy-done.12
  32.4 0.7 copy-done.8
  33.1 2.0 %copy-done.1 = bf16[3584,512]{1,0:T(8,128)(2,1)S(1)} copy-done((bf16[3584,512]{1,0:T(8,128)(2,1)S(1)}, bf16[3584,512]{1,0:T(8,128)(2,1)}, u32[]{:S(2)}) %copy-start.1) | copy-done | bytes 3670040
  35.2 0.9 copy-done.9
  36.1 4.0 %student_logits.3 = (f32[256,512]{1,0:T(8,128)S(1)}, f32[8,256]{1,0:T(8,128)S(1)}, bf16[256,3584]{1,0:T(8,128)(2,1)S(1)}) custom-call(s32[8]{0:T(128)S(1)} %stack.47.refs_0_, bf16[32,3584]{1,0:T(8,128)(2,1)} %collective-permute-done.refs_1_, bf16[32,3584]{1,0:T(8,128)(2,1)} %collective-permute-done.1.refs_2_, ...), custom_call_target="tpu_custom_call" | custom-call | flops 939524096 | bytes 6029312 | tf_op jit(solution)/shard_map/student_logits/pallas_call | solution.py:117
  40.2 1.2 %copy-done.4 = bf16[256,3584]{1,0:T(8,128)(2,1)} copy-done((bf16[256,3584]{1,0:T(8,128)(2,1)}, bf16[256,3584]{1,0:T(8,128)(2,1)S(1)}, u32[]{:S(2)}) %copy-start.4) | copy-done | bytes 1835032
  41.4 0.6 copy-done.14
  42.0 1.4 %first_stats.1.refs_0_ = f32[2,8,256]{2,1,0:T(8,128)} custom-call(f32[8,256]{1,0:T(8,128)} %copy-done.13, f32[8,256]{1,0:T(8,128)} %copy-done.14, f32[8,512]{1,0:T(8,128)} %copy-done.12, s32[1,128]{1,0:T(1,128)} %bitcast.48), custom_call_target="tpu_custom_call" | custom-call | bytes 32768 | tf_op jit(solution)/shard_map/first_stats/pallas_call | solution.py:300
  43.4 1.4 %collective-permute-done.9.refs_1_ = f32[2,8,256]{2,1,0:T(8,128)S(1)} collective-permute-done((f32[2,8,256]{2,1,0:T(8,128)}, f32[2,8,256]{2,1,0:T(8,128)S(1)}, u32[]{:S(2)}, u32[]{:S(2)}) %collective-permute-start.9) | collective-permute-done | bytes 16416 | tf_op jit(solution)/shard_map/ppermute | solution.py:323
  44.7 0.6 copy-done.18
  45.3 1.4 %merge_stats.5.refs_0_ = f32[2,8,256]{2,1,0:T(8,128)} custom-call(f32[2,8,256]{2,1,0:T(8,128)} %first_stats.1.refs_0_, f32[2,8,256]{2,1,0:T(8,128)} %copy-done.18), custom_call_target="tpu_custom_call" | custom-call | bytes 49152 | tf_op jit(solution)/shard_map/merge_stats/pallas_call | solution.py:279
  46.7 1.5 %collective-permute-start.10 = (f32[2,8,256]{2,1,0:T(8,128)}, f32[2,8,256]{2,1,0:T(8,128)S(1)}, u32[]{:S(2)}, u32[]{:S(2)}) collective-permute-start(f32[2,8,256]{2,1,0:T(8,128)} %merge_stats.5.refs_0_), channel_id=1, source_target_pairs={{0,16},{1,17},{2,18},{3,19},{4,20},{5,21},{6,22},{7,23},{8,24},{9,... | collective-permute-start | bytes 49160 | tf_op jit(solution)/shard_map/ppermute | solution.py:323
  48.2 2.4 %collective-permute-done.10.refs_1_ = f32[2,8,256]{2,1,0:T(8,128)S(1)} collective-permute-done((f32[2,8,256]{2,1,0:T(8,128)}, f32[2,8,256]{2,1,0:T(8,128)S(1)}, u32[]{:S(2)}, u32[]{:S(2)}) %collective-permute-start.10) | collective-permute-done | bytes 16416 | tf_op jit(solution)/shard_map/ppermute | solution.py:323
  50.6 0.6 copy-done.19
  51.2 1.4 %merge_stats.6.refs_0_ = f32[2,8,256]{2,1,0:T(8,128)} custom-call(f32[2,8,256]{2,1,0:T(8,128)} %merge_stats.5.refs_0_, f32[2,8,256]{2,1,0:T(8,128)} %copy-done.19), custom_call_target="tpu_custom_call" | custom-call | bytes 49152 | tf_op jit(solution)/shard_map/merge_stats/pallas_call | solution.py:279
  52.6 0.5 collective-permute-start.11
  53.1 3.4 %collective-permute-done.11.refs_1_ = f32[2,8,256]{2,1,0:T(8,128)S(1)} collective-permute-done((f32[2,8,256]{2,1,0:T(8,128)}, f32[2,8,256]{2,1,0:T(8,128)S(1)}, u32[]{:S(2)}, u32[]{:S(2)}) %collective-permute-start.11) | collective-permute-done | bytes 16416 | tf_op jit(solution)/shard_map/ppermute | solution.py:323
  56.6 0.6 copy-done.20
  57.2 1.4 %merge_stats.7.refs_0_ = f32[2,8,256]{2,1,0:T(8,128)} custom-call(f32[2,8,256]{2,1,0:T(8,128)} %merge_stats.6.refs_0_, f32[2,8,256]{2,1,0:T(8,128)} %copy-done.20), custom_call_target="tpu_custom_call" | custom-call | bytes 49152 | tf_op jit(solution)/shard_map/merge_stats/pallas_call | solution.py:279
  58.5 0.4 collective-permute-start.12
  59.0 3.5 %collective-permute-done.12.refs_1_ = f32[2,8,256]{2,1,0:T(8,128)S(1)} collective-permute-done((f32[2,8,256]{2,1,0:T(8,128)}, f32[2,8,256]{2,1,0:T(8,128)S(1)}, u32[]{:S(2)}, u32[]{:S(2)}) %collective-permute-start.12) | collective-permute-done | bytes 16416 | tf_op jit(solution)/shard_map/ppermute | solution.py:323
  62.5 0.6 copy-done.16
  63.1 1.4 %merge_stats.8.refs_0_ = f32[2,8,256]{2,1,0:T(8,128)} custom-call(f32[2,8,256]{2,1,0:T(8,128)} %merge_stats.7.refs_0_, f32[2,8,256]{2,1,0:T(8,128)} %copy-done.16), custom_call_target="tpu_custom_call" | custom-call | bytes 49152 | tf_op jit(solution)/shard_map/merge_stats/pallas_call | solution.py:279
  64.4 2.6 %collective-permute-start.13 = (f32[2,8,256]{2,1,0:T(8,128)}, f32[2,8,256]{2,1,0:T(8,128)S(1)}, u32[]{:S(2)}, u32[]{:S(2)}) collective-permute-start(f32[2,8,256]{2,1,0:T(8,128)} %merge_stats.8.refs_0_), channel_id=1, source_target_pairs={{0,4},{1,5},{2,6},{3,7},{4,0},{5,1},{6,2},{7,3},{8,12},{9,13},{10,... | collective-permute-start | bytes 49160 | tf_op jit(solution)/shard_map/ppermute | solution.py:323
  67.1 2.2 %collective-permute-done.13.refs_1_ = f32[2,8,256]{2,1,0:T(8,128)S(1)} collective-permute-done((f32[2,8,256]{2,1,0:T(8,128)}, f32[2,8,256]{2,1,0:T(8,128)S(1)}, u32[]{:S(2)}, u32[]{:S(2)}) %collective-permute-start.13) | collective-permute-done | bytes 16416 | tf_op jit(solution)/shard_map/ppermute | solution.py:323
  69.3 0.6 copy-done.17
  69.9 1.4 %merge_stats.9.refs_4_ = f32[2,8,256]{2,1,0:T(8,128)} custom-call(f32[2,8,256]{2,1,0:T(8,128)} %merge_stats.8.refs_0_, f32[2,8,256]{2,1,0:T(8,128)} %copy-done.17), custom_call_target="tpu_custom_call" | custom-call | bytes 49152 | tf_op jit(solution)/shard_map/merge_stats/pallas_call | solution.py:279
  71.3 2.0 %copy-done.2 = bf16[3584,512]{1,0:T(8,128)(2,1)S(1)} copy-done((bf16[3584,512]{1,0:T(8,128)(2,1)S(1)}, bf16[3584,512]{1,0:T(8,128)(2,1)}, u32[]{:S(2)}) %copy-start.2) | copy-done | bytes 3670040
  73.3 0.7 copy-done.10
  74.1 3.9 %back_rows.3 = (bf16[2,128,512]{2,1,0:T(8,128)(2,1)S(1)}, bf16[2,128,3584]{2,1,0:T(8,128)(2,1)S(1)}) custom-call(s32[2]{0:T(128)S(1)} %pad_add_fusion.refs_0_, f32[256,512]{1,0:T(8,128)S(1)} %get-tuple-element.21.refs_1_, f32[256,512]{1,0:T(8,128)S(1)} %get-tuple-element.23.refs_2_, bf16[2,2,128,512]{3,2,1,0:T(8,128)(2,1)S(1)} %bitcast.23, ...), custom_call_target="tpu_custom_call" | custom-call | flops 939524096 | bytes 5505024 | tf_op jit(solution)/shard_map/back_rows/pallas_call | solution.py:185
  78.1 3.9 %back_rows.2 = (bf16[2,128,512]{2,1,0:T(8,128)(2,1)S(1)}, bf16[2,128,3584]{2,1,0:T(8,128)(2,1)S(1)}) custom-call(s32[2]{0:T(128)S(1)} %pad_add_fusion.refs_0_, f32[256,512]{1,0:T(8,128)S(1)} %get-tuple-element.21.refs_1_, f32[256,512]{1,0:T(8,128)S(1)} %get-tuple-element.23.refs_2_, bf16[2,2,128,512]{3,2,1,0:T(8,128)(2,1)S(1)} %bitcast.24, ...), custom_call_target="tpu_custom_call" | custom-call | flops 939524096 | bytes 5505024 | tf_op jit(solution)/shard_map/back_rows/pallas_call | solution.py:185
  82.1 0.5 collective-permute-start.17
  82.7 1.6 %collective-permute-start.15 = (bf16[1,2,2,2,16,1152]{5,4,3,2,1,0:T(8,128)(2,1)S(1)}, bf16[1,2,2,2,16,1152]{5,4,3,2,1,0:T(8,128)(2,1)S(1)}, u32[]{:S(2)}, u32[]{:S(2)}) collective-permute-start(bf16[1,2,2,2,16,1152]{5,4,3,2,1,0:T(8,128)(2,1)S(1)} %add_convert_fusion.2), channel_id=1, source_target_pairs={{0,16},{1,17},{2,18},{3,19},{4,20},{5,21},{6,22},{7,23},{8,24},{9,... | collective-permute-start | bytes 884744 | tf_op jit(solution)/shard_map/ppermute | solution.py:323
  84.5 5.2 %head_gradient.1 = bf16[3584,512]{1,0:T(8,128)(2,1)} custom-call(bf16[256,3584]{1,0:T(8,128)(2,1)S(1)} %get-tuple-element.30.near_ref, bf16[256,3584]{1,0:T(8,128)(2,1)S(1)} %copy-done.5, bf16[2,128,512]{2,1,0:T(8,128)(2,1)S(1)} %get-tuple-element.32.even_ref, bf16[2,128,512]{2,1,0:T(8,128)(2,1)S(1)} %get-tuple-element.33.odd_ref), custom_call_target="tpu_custom_call" | custom-call | flops 1879048192 | bytes 7864320 | tf_op jit(solution)/shard_map/head_gradient/pallas_call | solution.py:238
  89.7 2.1 %collective-permute-done.15 = bf16[1,2,2,2,16,1152]{5,4,3,2,1,0:T(8,128)(2,1)S(1)} collective-permute-done((bf16[1,2,2,2,16,1152]{5,4,3,2,1,0:T(8,128)(2,1)S(1)}, bf16[1,2,2,2,16,1152]{5,4,3,2,1,0:T(8,128)(2,1)S(1)}, u32[]{:S(2)}, u32[]{:S(2)}) %collective-permute-start.15) | collective-permute-done | bytes 294944 | tf_op jit(solution)/shard_map/ppermute | solution.py:323
  91.9 1.3 %collective-permute-done.16 = bf16[2,2,2,1,16,1152]{5,4,3,2,1,0:T(8,128)(2,1)S(1)} collective-permute-done((bf16[2,2,2,1,16,1152]{5,4,3,2,1,0:T(8,128)(2,1)S(1)}, bf16[2,2,2,1,16,1152]{5,4,3,2,1,0:T(8,128)(2,1)S(1)}, u32[]{:S(2)}, u32[]{:S(2)}) %collective-permute-start.16) | collective-permute-done | bytes 294944 | tf_op jit(solution)/shard_map/ppermute | solution.py:323
  93.2 0.8 collective-permute-start.22
  94.1 0.5 collective-permute-start.18
  94.6 1.4 %collective-permute-start.20 = (bf16[2,2,1,1,16,1152]{5,4,3,2,1,0:T(8,128)(2,1)S(1)}, bf16[2,2,1,1,16,1152]{5,4,3,2,1,0:T(8,128)(2,1)S(1)}, u32[]{:S(2)}, u32[]{:S(2)}) collective-permute-start(bf16[2,2,1,1,16,1152]{5,4,3,2,1,0:T(8,128)(2,1)S(1)} %add_convert_fusion.4), channel_id=1, source_target_pairs={{0,2},{1,3},{2,0},{3,1},{4,6},{5,7},{6,4},{7,5},{8,10},{9,11},{10,... | collective-permute-start | bytes 442376 | tf_op jit(solution)/shard_map/ppermute | solution.py:323
  96.1 3.2 %collective-permute-done.18 = bf16[1,2,2,1,16,1152]{5,4,3,2,1,0:T(8,128)(2,1)S(1)} collective-permute-done((bf16[1,2,2,1,16,1152]{5,4,3,2,1,0:T(8,128)(2,1)S(1)}, bf16[1,2,2,1,16,1152]{5,4,3,2,1,0:T(8,128)(2,1)S(1)}, u32[]{:S(2)}, u32[]{:S(2)}) %collective-permute-start.18) | collective-permute-done | bytes 147488 | tf_op jit(solution)/shard_map/ppermute | solution.py:323
  99.4 1.4 %collective-permute-start.19 = (bf16[1,2,1,1,16,1152]{5,4,3,2,1,0:T(8,128)(2,1)S(1)}, bf16[1,2,1,1,16,1152]{5,4,3,2,1,0:T(8,128)(2,1)S(1)}, u32[]{:S(2)}, u32[]{:S(2)}) collective-permute-start(bf16[1,2,1,1,16,1152]{5,4,3,2,1,0:T(8,128)(2,1)S(1)} %add_convert_fusion.8), channel_id=1, source_target_pairs={{0,2},{1,3},{2,0},{3,1},{4,6},{5,7},{6,4},{7,5},{8,10},{9,11},{10,... | collective-permute-start | bytes 221192 | tf_op jit(solution)/shard_map/ppermute | solution.py:323
  100.8 0.5 collective-permute-start.23
  101.3 2.5 %collective-permute-done.19 = bf16[1,2,1,1,16,1152]{5,4,3,2,1,0:T(8,128)(2,1)S(1)} collective-permute-done((bf16[1,2,1,1,16,1152]{5,4,3,2,1,0:T(8,128)(2,1)S(1)}, bf16[1,2,1,1,16,1152]{5,4,3,2,1,0:T(8,128)(2,1)S(1)}, u32[]{:S(2)}, u32[]{:S(2)}) %collective-permute-start.19) | collective-permute-done | bytes 73760 | tf_op jit(solution)/shard_map/ppermute | solution.py:323
  103.9 1.3 %collective-permute-start.21 = (bf16[1,2,1,1,16,1152]{5,4,3,2,1,0:T(8,128)(2,1)S(1)}, bf16[1,2,1,1,16,1152]{5,4,3,2,1,0:T(8,128)(2,1)S(1)}, u32[]{:S(2)}, u32[]{:S(2)}) collective-permute-start(bf16[1,2,1,1,16,1152]{5,4,3,2,1,0:T(8,128)(2,1)S(1)} %get-tuple-element.39), channel_id=1, source_target_pairs={{0,16},{1,17},{2,18},{3,19},{4,20},{5,21},{6,22},{7,23},{8,24},{9,... | collective-permute-start | bytes 221192 | tf_op jit(solution)/shard_map/ppermute | solution.py:323
  105.4 2.9 %collective-permute-done.21 = bf16[1,2,1,1,16,1152]{5,4,3,2,1,0:T(8,128)(2,1)S(1)} collective-permute-done((bf16[1,2,1,1,16,1152]{5,4,3,2,1,0:T(8,128)(2,1)S(1)}, bf16[1,2,1,1,16,1152]{5,4,3,2,1,0:T(8,128)(2,1)S(1)}, u32[]{:S(2)}, u32[]{:S(2)}) %collective-permute-start.21) | collective-permute-done | bytes 73760 | tf_op jit(solution)/shard_map/ppermute | solution.py:323
  108.4 2.6 %collective-permute-start.24 = (bf16[1,1,1,1,16,3584]{5,4,3,2,1,0:T(8,128)(2,1)S(1)}, bf16[1,1,1,1,16,3584]{5,4,3,2,1,0:T(8,128)(2,1)S(1)}, u32[]{:S(2)}, u32[]{:S(2)}) collective-permute-start(bf16[1,1,1,1,16,3584]{5,4,3,2,1,0:T(8,128)(2,1)S(1)} %slice.303), channel_id=1, source_target_pairs={{0,4},{1,5},{2,6},{3,7},{4,0},{5,1},{6,2},{7,3},{8,12},{9,13},{10,... | collective-permute-start | bytes 344072 | tf_op jit(solution)/shard_map/ppermute | solution.py:323
  111.0 4.4 %collective-permute-done.24 = bf16[1,1,1,1,16,3584]{5,4,3,2,1,0:T(8,128)(2,1)S(1)} collective-permute-done((bf16[1,1,1,1,16,3584]{5,4,3,2,1,0:T(8,128)(2,1)S(1)}, bf16[1,1,1,1,16,3584]{5,4,3,2,1,0:T(8,128)(2,1)S(1)}, u32[]{:S(2)}, u32[]{:S(2)}) %collective-permute-start.24) | collective-permute-done | bytes 114720 | tf_op jit(solution)/shard_map/ppermute | solution.py:323
  115.4 0.7 fusion
  (60 shorter events, 1.7 us)
Async XLA Ops:
  0.6 22.4 %copy-start.3 = (bf16[128,3584]{1,0:T(8,128)(2,1)S(1)}, bf16[128,3584]{1,0:T(8,128)(2,1)}, u32[]{:S(2)}) copy-start(bf16[128,3584]{1,0:T(8,128)(2,1)} %refs_1_.1) | copy-start | bytes 2752516
  0.6 21.5 %collective-permute-start.2 = (bf16[128,3584]{1,0:T(8,128)(2,1)}, bf16[128,3584]{1,0:T(8,128)(2,1)S(1)}, u32[]{:S(2)}, u32[]{:S(2)}) collective-permute-start(bf16[128,3584]{1,0:T(8,128)(2,1)} %refs_1_.1), channel_id=1, source_target_pairs={{0,8},{1,9},{2,10},{3,11},{4,12},{5,13},{6,14},{7,15},{8,0},{9,1},... | collective-permute-start | bytes 2752520 | tf_op jit(solution)/shard_map/ppermute | solution.py:323
  2.2 9.2 %collective-permute-start = (bf16[32,3584]{1,0:T(8,128)(2,1)S(1)}, bf16[32,3584]{1,0:T(8,128)(2,1)}, u32[]{:S(2)}, u32[]{:S(2)}) collective-permute-start(bf16[32,3584]{1,0:T(8,128)(2,1)S(1)} %get-tuple-element.41), channel_id=1, source_target_pairs={{0,16},{1,17},{2,18},{3,19},{4,20},{5,21},{6,22},{7,23},{8,24},{9,... | collective-permute-start | bytes 688136 | tf_op jit(solution)/shard_map/ppermute | solution.py:323
  4.9 16.7 %collective-permute-start.4 = (bf16[32,3584]{1,0:T(8,128)(2,1)S(1)}, bf16[32,3584]{1,0:T(8,128)(2,1)}, u32[]{:S(2)}, u32[]{:S(2)}) collective-permute-start(bf16[32,3584]{1,0:T(8,128)(2,1)S(1)} %get-tuple-element.40), channel_id=1, source_target_pairs={{0,16},{1,17},{2,18},{3,19},{4,20},{5,21},{6,22},{7,23},{8,24},{9,... | collective-permute-start | bytes 688136 | tf_op jit(solution)/shard_map/ppermute | solution.py:323
  11.4 10.3 %collective-permute-start.3 = (bf16[32,3584]{1,0:T(8,128)(2,1)}, bf16[32,3584]{1,0:T(8,128)(2,1)}, u32[]{:S(2)}, u32[]{:S(2)}) collective-permute-start(bf16[32,3584]{1,0:T(8,128)(2,1)} %collective-permute-done.refs_1_), channel_id=1, source_target_pairs={{0,2},{1,3},{2,0},{3,1},{4,6},{5,7},{6,4},{7,5},{8,10},{9,11},{10,... | collective-permute-start | bytes 688136 | tf_op jit(solution)/shard_map/ppermute | solution.py:323
  13.5 15.9 %collective-permute-start.1 = (bf16[32,3584]{1,0:T(8,128)(2,1)}, bf16[32,3584]{1,0:T(8,128)(2,1)}, u32[]{:S(2)}, u32[]{:S(2)}) collective-permute-start(bf16[32,3584]{1,0:T(8,128)(2,1)} %collective-permute-done.refs_1_), channel_id=1, source_target_pairs={{0,1},{1,0},{2,3},{3,2},{4,5},{5,4},{6,7},{7,6},{8,9},{9,8},{10,11... | collective-permute-start | bytes 688136 | tf_op jit(solution)/shard_map/ppermute | solution.py:323
  16.9 13.1 %all-to-all-start = ((bf16[128,4,512]{2,0,1:T(8,128)(2,1)}), bf16[128,4,512]{2,0,1:T(8,128)(2,1)}, u32[]{:S(2)}, u32[]{:S(2)}) async-start(bf16[128,4,512]{2,0,1:T(8,128)(2,1)} %copy.8), calls=%async_computation | async-start | bytes 1048576 | tf_op jit(solution)/shard_map/all_to_all | solution.py:333
  21.1 8.9 %copy-start.15 = (s32[512]{0:T(512)S(1)}, s32[512]{0:T(512)}, u32[]{:S(2)}) copy-start(s32[512]{0:T(512)} %param.7) | copy-start | bytes 6148
  21.2 11.2 %collective-permute-start.5 = (bf16[32,3584]{1,0:T(8,128)(2,1)}, bf16[32,3584]{1,0:T(8,128)(2,1)}, u32[]{:S(2)}, u32[]{:S(2)}) collective-permute-start(bf16[32,3584]{1,0:T(8,128)(2,1)} %collective-permute-done.refs_1_), channel_id=1, source_target_pairs={{0,8},{1,9},{2,10},{3,11},{4,12},{5,13},{6,14},{7,15},{8,0},{9,1},... | collective-permute-start | bytes 688136 | tf_op jit(solution)/shard_map/ppermute | solution.py:323
  21.6 10.8 %collective-permute-start.8 = (bf16[32,3584]{1,0:T(8,128)(2,1)}, bf16[32,3584]{1,0:T(8,128)(2,1)}, u32[]{:S(2)}, u32[]{:S(2)}) collective-permute-start(bf16[32,3584]{1,0:T(8,128)(2,1)} %collective-permute-done.4.refs_4_), channel_id=1, source_target_pairs={{0,8},{1,9},{2,10},{3,11},{4,12},{5,13},{6,14},{7,15},{8,0},{9,1},... | collective-permute-start | bytes 688136 | tf_op jit(solution)/shard_map/ppermute | solution.py:323
  21.7 10.7 %collective-permute-start.7 = (bf16[32,3584]{1,0:T(8,128)(2,1)}, bf16[32,3584]{1,0:T(8,128)(2,1)}, u32[]{:S(2)}, u32[]{:S(2)}) collective-permute-start(bf16[32,3584]{1,0:T(8,128)(2,1)} %collective-permute-done.3.refs_3_), channel_id=1, source_target_pairs={{0,8},{1,9},{2,10},{3,11},{4,12},{5,13},{6,14},{7,15},{8,0},{9,1},... | collective-permute-start | bytes 688136 | tf_op jit(solution)/shard_map/ppermute | solution.py:323
  22.2 0.9 copy-start.6
  23.1 2.0 %copy-start = (bf16[3584,512]{1,0:T(8,128)(2,1)S(1)}, bf16[3584,512]{1,0:T(8,128)(2,1)}, u32[]{:S(2)}) copy-start(bf16[3584,512]{1,0:T(8,128)(2,1)} %refs_5_.3) | copy-start | bytes 11010052
  25.1 1.2 %copy-start.7 = (bf16[128,3584]{1,0:T(8,128)(2,1)S(1)}, bf16[128,3584]{1,0:T(8,128)(2,1)}, u32[]{:S(2)}) copy-start(bf16[128,3584]{1,0:T(8,128)(2,1)} %copy-done.6) | copy-start | bytes 2752516
  29.4 3.0 %copy-start.13 = (f32[8,256]{1,0:T(8,128)}, f32[8,256]{1,0:T(8,128)S(1)}, u32[]{:S(2)}) copy-start(f32[8,256]{1,0:T(8,128)S(1)} %get-tuple-element.25.near_ref) | copy-start | bytes 24580
  29.4 3.0 %collective-permute-start.6 = (bf16[32,3584]{1,0:T(8,128)(2,1)}, bf16[32,3584]{1,0:T(8,128)(2,1)S(1)}, u32[]{:S(2)}, u32[]{:S(2)}) collective-permute-start(bf16[32,3584]{1,0:T(8,128)(2,1)} %collective-permute-done.1.refs_2_), channel_id=1, source_target_pairs={{0,8},{1,9},{2,10},{3,11},{4,12},{5,13},{6,14},{7,15},{8,0},{9,1},... | collective-permute-start | bytes 688136 | tf_op jit(solution)/shard_map/ppermute | solution.py:323
  31.8 0.6 copy-start.12
  32.4 0.7 copy-start.8
  33.1 2.0 %copy-start.1 = (bf16[3584,512]{1,0:T(8,128)(2,1)S(1)}, bf16[3584,512]{1,0:T(8,128)(2,1)}, u32[]{:S(2)}) copy-start(bf16[3584,512]{1,0:T(8,128)(2,1)} %refs_5_.3) | copy-start | bytes 11010052
  35.2 0.9 copy-start.9
  40.1 1.2 %copy-start.4 = (bf16[256,3584]{1,0:T(8,128)(2,1)}, bf16[256,3584]{1,0:T(8,128)(2,1)S(1)}, u32[]{:S(2)}) copy-start(bf16[256,3584]{1,0:T(8,128)(2,1)S(1)} %get-tuple-element.31.far_ref) | copy-start | bytes 5505028
  41.4 0.6 copy-start.14
  43.3 1.4 %collective-permute-start.9 = (f32[2,8,256]{2,1,0:T(8,128)}, f32[2,8,256]{2,1,0:T(8,128)S(1)}, u32[]{:S(2)}, u32[]{:S(2)}) collective-permute-start(f32[2,8,256]{2,1,0:T(8,128)} %first_stats.1.refs_0_), channel_id=1, source_target_pairs={{0,8},{1,9},{2,10},{3,11},{4,12},{5,13},{6,14},{7,15},{8,0},{9,1},... | collective-permute-start | bytes 49160 | tf_op jit(solution)/shard_map/ppermute | solution.py:323
  44.7 0.6 copy-start.18
  46.7 3.9 %collective-permute-start.10 = (f32[2,8,256]{2,1,0:T(8,128)}, f32[2,8,256]{2,1,0:T(8,128)S(1)}, u32[]{:S(2)}, u32[]{:S(2)}) collective-permute-start(f32[2,8,256]{2,1,0:T(8,128)} %merge_stats.5.refs_0_), channel_id=1, source_target_pairs={{0,16},{1,17},{2,18},{3,19},{4,20},{5,21},{6,22},{7,23},{8,24},{9,... | collective-permute-start | bytes 49160 | tf_op jit(solution)/shard_map/ppermute | solution.py:323
  50.6 0.6 copy-start.19
  52.6 3.9 %collective-permute-start.11 = (f32[2,8,256]{2,1,0:T(8,128)}, f32[2,8,256]{2,1,0:T(8,128)S(1)}, u32[]{:S(2)}, u32[]{:S(2)}) collective-permute-start(f32[2,8,256]{2,1,0:T(8,128)} %merge_stats.6.refs_0_), channel_id=1, source_target_pairs={{0,1},{1,0},{2,3},{3,2},{4,5},{5,4},{6,7},{7,6},{8,9},{9,8},{10,11... | collective-permute-start | bytes 49160 | tf_op jit(solution)/shard_map/ppermute | solution.py:323
  56.6 0.6 copy-start.20
  58.5 3.9 %collective-permute-start.12 = (f32[2,8,256]{2,1,0:T(8,128)}, f32[2,8,256]{2,1,0:T(8,128)S(1)}, u32[]{:S(2)}, u32[]{:S(2)}) collective-permute-start(f32[2,8,256]{2,1,0:T(8,128)} %merge_stats.7.refs_0_), channel_id=1, source_target_pairs={{0,2},{1,3},{2,0},{3,1},{4,6},{5,7},{6,4},{7,5},{8,10},{9,11},{10,... | collective-permute-start | bytes 49160 | tf_op jit(solution)/shard_map/ppermute | solution.py:323
  62.5 0.6 copy-start.16
  64.4 4.9 %collective-permute-start.13 = (f32[2,8,256]{2,1,0:T(8,128)}, f32[2,8,256]{2,1,0:T(8,128)S(1)}, u32[]{:S(2)}, u32[]{:S(2)}) collective-permute-start(f32[2,8,256]{2,1,0:T(8,128)} %merge_stats.8.refs_0_), channel_id=1, source_target_pairs={{0,4},{1,5},{2,6},{3,7},{4,0},{5,1},{6,2},{7,3},{8,12},{9,13},{10,... | collective-permute-start | bytes 49160 | tf_op jit(solution)/shard_map/ppermute | solution.py:323
  69.3 0.6 copy-start.17
  71.3 2.0 %copy-start.2 = (bf16[3584,512]{1,0:T(8,128)(2,1)S(1)}, bf16[3584,512]{1,0:T(8,128)(2,1)}, u32[]{:S(2)}) copy-start(bf16[3584,512]{1,0:T(8,128)(2,1)} %refs_5_.3) | copy-start | bytes 11010052
  73.3 0.7 copy-start.10
  74.1 4.0 %copy-start.11 = (f32[2,8,256]{2,1,0:T(8,128)S(1)}, f32[2,8,256]{2,1,0:T(8,128)}, u32[]{:S(2)}) copy-start(f32[2,8,256]{2,1,0:T(8,128)} %merge_stats.9.refs_4_) | copy-start | bytes 49156
  78.0 4.0 %collective-permute-start.14 = (bf16[2,128,3584]{2,1,0:T(8,128)(2,1)S(1)}, bf16[2,128,3584]{2,1,0:T(8,128)(2,1)S(1)}, u32[]{:S(2)}, u32[]{:S(2)}) collective-permute-start(bf16[2,128,3584]{2,1,0:T(8,128)(2,1)S(1)} %get-tuple-element.29), channel_id=1, source_target_pairs={{0,8},{1,9},{2,10},{3,11},{4,12},{5,13},{6,14},{7,15},{8,0},{9,1},... | collective-permute-start | bytes 5505032 | tf_op jit(solution)/shard_map/ppermute | solution.py:323
  82.0 2.5 %copy-start.5 = (bf16[256,3584]{1,0:T(8,128)(2,1)S(1)}, bf16[256,3584]{1,0:T(8,128)(2,1)}, u32[]{:S(2)}) copy-start(bf16[256,3584]{1,0:T(8,128)(2,1)} %copy-done.4) | copy-start | bytes 5505028
  82.1 11.0 %collective-permute-start.17 = (bf16[2,2,1,2,16,1280]{5,4,3,2,1,0:T(8,128)(2,1)S(1)}, bf16[2,2,1,2,16,1280]{5,4,3,2,1,0:T(8,128)(2,1)S(1)}, u32[]{:S(2)}, u32[]{:S(2)}) collective-permute-start(bf16[2,2,1,2,16,1280]{5,4,3,2,1,0:T(8,128)(2,1)S(1)} %add_convert_fusion), channel_id=1, source_target_pairs={{0,2},{1,3},{2,0},{3,1},{4,6},{5,7},{6,4},{7,5},{8,10},{9,11},{10,... | collective-permute-start | bytes 983048 | tf_op jit(solution)/shard_map/ppermute | solution.py:323
  82.7 9.2 %collective-permute-start.15 = (bf16[1,2,2,2,16,1152]{5,4,3,2,1,0:T(8,128)(2,1)S(1)}, bf16[1,2,2,2,16,1152]{5,4,3,2,1,0:T(8,128)(2,1)S(1)}, u32[]{:S(2)}, u32[]{:S(2)}) collective-permute-start(bf16[1,2,2,2,16,1152]{5,4,3,2,1,0:T(8,128)(2,1)S(1)} %add_convert_fusion.2), channel_id=1, source_target_pairs={{0,16},{1,17},{2,18},{3,19},{4,20},{5,21},{6,22},{7,23},{8,24},{9,... | collective-permute-start | bytes 884744 | tf_op jit(solution)/shard_map/ppermute | solution.py:323
  84.3 8.8 %collective-permute-start.16 = (bf16[2,2,2,1,16,1152]{5,4,3,2,1,0:T(8,128)(2,1)S(1)}, bf16[2,2,2,1,16,1152]{5,4,3,2,1,0:T(8,128)(2,1)S(1)}, u32[]{:S(2)}, u32[]{:S(2)}) collective-permute-start(bf16[2,2,2,1,16,1152]{5,4,3,2,1,0:T(8,128)(2,1)S(1)} %add_convert_fusion.1), channel_id=1, source_target_pairs={{0,1},{1,0},{2,3},{3,2},{4,5},{5,4},{6,7},{7,6},{8,9},{9,8},{10,11... | collective-permute-start | bytes 884744 | tf_op jit(solution)/shard_map/ppermute | solution.py:323
  93.2 7.6 %collective-permute-start.22 = (bf16[1,2,1,2,16,1280]{5,4,3,2,1,0:T(8,128)(2,1)S(1)}, bf16[1,2,1,2,16,1280]{5,4,3,2,1,0:T(8,128)(2,1)S(1)}, u32[]{:S(2)}, u32[]{:S(2)}) collective-permute-start(bf16[1,2,1,2,16,1280]{5,4,3,2,1,0:T(8,128)(2,1)S(1)} %add_convert_fusion.3), channel_id=1, source_target_pairs={{0,16},{1,17},{2,18},{3,19},{4,20},{5,21},{6,22},{7,23},{8,24},{9,... | collective-permute-start | bytes 491528 | tf_op jit(solution)/shard_map/ppermute | solution.py:323
  94.1 5.2 %collective-permute-start.18 = (bf16[1,2,2,1,16,1152]{5,4,3,2,1,0:T(8,128)(2,1)S(1)}, bf16[1,2,2,1,16,1152]{5,4,3,2,1,0:T(8,128)(2,1)S(1)}, u32[]{:S(2)}, u32[]{:S(2)}) collective-permute-start(bf16[1,2,2,1,16,1152]{5,4,3,2,1,0:T(8,128)(2,1)S(1)} %add_convert_fusion.5), channel_id=1, source_target_pairs={{0,1},{1,0},{2,3},{3,2},{4,5},{5,4},{6,7},{7,6},{8,9},{9,8},{10,11... | collective-permute-start | bytes 442376 | tf_op jit(solution)/shard_map/ppermute | solution.py:323
  94.6 6.7 %collective-permute-start.20 = (bf16[2,2,1,1,16,1152]{5,4,3,2,1,0:T(8,128)(2,1)S(1)}, bf16[2,2,1,1,16,1152]{5,4,3,2,1,0:T(8,128)(2,1)S(1)}, u32[]{:S(2)}, u32[]{:S(2)}) collective-permute-start(bf16[2,2,1,1,16,1152]{5,4,3,2,1,0:T(8,128)(2,1)S(1)} %add_convert_fusion.4), channel_id=1, source_target_pairs={{0,2},{1,3},{2,0},{3,1},{4,6},{5,7},{6,4},{7,5},{8,10},{9,11},{10,... | collective-permute-start | bytes 442376 | tf_op jit(solution)/shard_map/ppermute | solution.py:323
  99.4 4.4 %collective-permute-start.19 = (bf16[1,2,1,1,16,1152]{5,4,3,2,1,0:T(8,128)(2,1)S(1)}, bf16[1,2,1,1,16,1152]{5,4,3,2,1,0:T(8,128)(2,1)S(1)}, u32[]{:S(2)}, u32[]{:S(2)}) collective-permute-start(bf16[1,2,1,1,16,1152]{5,4,3,2,1,0:T(8,128)(2,1)S(1)} %add_convert_fusion.8), channel_id=1, source_target_pairs={{0,2},{1,3},{2,0},{3,1},{4,6},{5,7},{6,4},{7,5},{8,10},{9,11},{10,... | collective-permute-start | bytes 221192 | tf_op jit(solution)/shard_map/ppermute | solution.py:323
  100.8 4.5 %collective-permute-start.23 = (bf16[1,2,1,1,16,1280]{5,4,3,2,1,0:T(8,128)(2,1)S(1)}, bf16[1,2,1,1,16,1280]{5,4,3,2,1,0:T(8,128)(2,1)S(1)}, u32[]{:S(2)}, u32[]{:S(2)}) collective-permute-start(bf16[1,2,1,1,16,1280]{5,4,3,2,1,0:T(8,128)(2,1)S(1)} %add_convert_fusion.6), channel_id=1, source_target_pairs={{0,1},{1,0},{2,3},{3,2},{4,5},{5,4},{6,7},{7,6},{8,9},{9,8},{10,11... | collective-permute-start | bytes 245768 | tf_op jit(solution)/shard_map/ppermute | solution.py:323
  103.9 4.4 %collective-permute-start.21 = (bf16[1,2,1,1,16,1152]{5,4,3,2,1,0:T(8,128)(2,1)S(1)}, bf16[1,2,1,1,16,1152]{5,4,3,2,1,0:T(8,128)(2,1)S(1)}, u32[]{:S(2)}, u32[]{:S(2)}) collective-permute-start(bf16[1,2,1,1,16,1152]{5,4,3,2,1,0:T(8,128)(2,1)S(1)} %get-tuple-element.39), channel_id=1, source_target_pairs={{0,16},{1,17},{2,18},{3,19},{4,20},{5,21},{6,22},{7,23},{8,24},{9,... | collective-permute-start | bytes 221192 | tf_op jit(solution)/shard_map/ppermute | solution.py:323
  108.4 7.0 %collective-permute-start.24 = (bf16[1,1,1,1,16,3584]{5,4,3,2,1,0:T(8,128)(2,1)S(1)}, bf16[1,1,1,1,16,3584]{5,4,3,2,1,0:T(8,128)(2,1)S(1)}, u32[]{:S(2)}, u32[]{:S(2)}) collective-permute-start(bf16[1,1,1,1,16,3584]{5,4,3,2,1,0:T(8,128)(2,1)S(1)} %slice.303), channel_id=1, source_target_pairs={{0,4},{1,5},{2,6},{3,7},{4,0},{5,1},{6,2},{7,3},{8,12},{9,13},{10,... | collective-permute-start | bytes 344072 | tf_op jit(solution)/shard_map/ppermute | solution.py:323

commit v4 on v0

v4 whole, which is shorter than its diff:
```python
import jax
import jax.numpy as jnp
from jax import lax
from jax.experimental import pallas as pl
from jax.experimental.pallas import tpu as pltpu
from jax.sharding import PartitionSpec as P

BF16 = jnp.bfloat16
F32 = jnp.float32
AXES = ("grp", "vocab")
VMEM = pl.BlockSpec(memory_space=pltpu.VMEM)
SMEM = pl.BlockSpec(memory_space=pltpu.SMEM)
STAT_ROWS = 8
MIB = 2**20


def params(mib):
    return pltpu.CompilerParams(vmem_limit_bytes=mib * MIB)


def cost(flops, nbytes, exps=0):
    return pl.CostEstimate(flops=flops, bytes_accessed=nbytes, transcendentals=exps)


def shape(dims, dtype):
    return jax.ShapeDtypeStruct(dims, dtype)


def columns_to_rows(columns):
    count = columns[0].shape[0]
    lane = lax.broadcasted_iota(jnp.int32, (count, 128), 1)
    wide = jnp.zeros((count, 128), F32)
    for k, column in enumerate(columns):
        wide = jnp.where(lane == k, column, wide)
    return wide.T[:STAT_ROWS]


def teacher_kernel(at_ref, serving_ref, a0, a1, a2, a3, aligned_ref, stats_ref):
    me, core = at_ref[0], at_ref[1]
    _, per, cols = a0.shape
    for j in range(2):
        wanted = serving_ref[me ^ (2 * j)]
        sums = [0.0, 0.0]
        for k, arrived in enumerate((a0, a1, a2, a3)):
            row = lax.broadcasted_iota(jnp.int32, (per, per), 0) + (me ^ k) * per
            pick = (row == wanted).astype(BF16)
            for c in range(2):
                sums[c] += lax.dot_general(
                    pick, arrived[core ^ c], (((0,), (0,)), ((), ())), preferred_element_type=F32
                )
        peak = jnp.maximum(*[jnp.max(s, axis=1, keepdims=True) for s in sums])
        total = sum(jnp.sum(jnp.exp((s - peak) * 0.5), axis=1, keepdims=True) for s in sums)
        for c in range(2):
            aligned_ref[j, :, c * cols : (c + 1) * cols] = sums[c].astype(BF16)
        stats_ref[j] = columns_to_rows([peak, total])


def teacher_rows(at, serving, arrived):
    _, per, cols = arrived[0].shape
    groups = serving.shape[0] // per
    return pl.pallas_call(
        teacher_kernel,
        out_shape=(shape((2, per, 2 * cols), BF16), shape((2, STAT_ROWS, per), F32)),
        in_specs=[SMEM] + [VMEM] * 5,
        out_specs=(VMEM, VMEM),
        compiler_params=params(10),
        cost_estimate=cost(32 * per * per * cols, 12 * per * cols * 2, 4 * per * cols),
        name="teacher_rows",
    )(at, serving.reshape(groups, 1, per), *arrived)


def logits_of(rows, own_ref, other_ref, logits_ref):
    cols = own_ref.shape[1]
    a = jnp.dot(rows, own_ref[...], preferred_element_type=F32)
    b = jnp.dot(rows, other_ref[...], preferred_element_type=F32)
    logits_ref[:, :cols] = a
    logits_ref[:, cols:] = b
    peak = jnp.maximum(jnp.max(a, axis=1, keepdims=True), jnp.max(b, axis=1, keepdims=True))
    a = jnp.exp((a - peak) * 0.5)
    b = jnp.exp((b - peak) * 0.5)
    hard = jnp.sum(a * a, axis=1, keepdims=True) + jnp.sum(b * b, axis=1, keepdims=True)
    soft = jnp.sum(a, axis=1, keepdims=True) + jnp.sum(b, axis=1, keepdims=True)
    return columns_to_rows([peak, hard, soft])


def near_kernel(rows_ref, own_ref, other_ref, logits_ref, stats_ref):
    stats_ref[...] = logits_of(rows_ref[...], own_ref, other_ref, logits_ref)


def near_logits(rows, own, other):
    per, depth = rows.shape
    cols = own.shape[1]
    return pl.pallas_call(
        near_kernel,
        out_shape=(shape((per, 2 * cols), F32), shape((STAT_ROWS, per), F32)),
        in_specs=[VMEM] * 3,
        out_specs=(VMEM, VMEM),
        compiler_params=params(16),
        cost_estimate=cost(4 * per * depth * cols, (per + 2 * cols) * depth * 2, 2 * per * cols),
        name="near_logits",
    )(rows, own, other)


def far_kernel(spots_ref, x0, x1, x2, x3, own_ref, other_ref, near_ref, taught_ref, ids_ref, logits_ref, rows_ref, out_ref):
    count = x0.shape[0]
    for k, piece in enumerate((x0, x1, x2, x3)):
        rows_ref[pl.ds(pl.multiple_of(spots_ref[k], 16), count), :] = piece[...]
    stats = logits_of(rows_ref[...], own_ref, other_ref, logits_ref)
    per = rows_ref.shape[0]
    for j, student in enumerate((near_ref[...], stats)):
        out_ref[j, 0:3, :] = student[0:3]
        out_ref[j, 3:5, :] = taught_ref[j, 0:2, :]
        out_ref[j, 5:8, :] = jnp.zeros((3, per), F32)
    out_ref[0, 5:6, :] = ids_ref[...].astype(F32)


def far_logits(spots, pieces, own, other, near_stats, taught, ids):
    depth, cols = own.shape
    per = sum(piece.shape[0] for piece in pieces)
    return pl.pallas_call(
        far_kernel,
        out_shape=(
            shape((per, 2 * cols), F32),
            shape((per, depth), BF16),
            shape((2, STAT_ROWS, per), F32),
        ),
        in_specs=[SMEM] + [VMEM] * 9,
        out_specs=(VMEM, VMEM, VMEM),
        compiler_params=params(20),
        cost_estimate=cost(4 * per * depth * cols, (per + 2 * cols) * depth * 2, 2 * per * cols),
        name="far_logits",
    )(spots, *pieces, own, other, near_stats, taught, ids.reshape(1, per))


def merged(parts):
    top = parts[0]
    for part in parts[1:]:
        top = jnp.maximum(top, part)
    hard = soft = total = 0.0
    for part in parts:
        s = jnp.exp((part[0:1] - top[0:1]) * 0.5)
        t = jnp.exp((part[3:4] - top[3:4]) * 0.5)
        hard += part[1:2] * (s * s)
        soft += part[2:3] * s
        total += part[4:5] * t
    return top[0:1], hard, soft, top[3:4], total, top[5:]


def merge_kernel(flips, *refs):
    out_ref = refs[-1]
    for j in range(2):
        out_ref[j] = jnp.concatenate(merged([ref[j ^ f] for ref, f in zip(refs, flips)]))


def merge(parts, flips):
    return pl.pallas_call(
        lambda *refs: merge_kernel(flips, *refs),
        out_shape=shape(parts[0].shape, F32),
        in_specs=[VMEM] * len(parts),
        out_specs=VMEM,
        compiler_params=params(2),
        cost_estimate=cost(0, 5 * parts[0].size * 4),
        name="merge_stats",
    )(*parts)


def picker(bit, side, flip, total):
    row = lax.broadcasted_iota(jnp.int32, (total // 2, total), 0)
    low = row & ((1 << bit) - 1)
    row = ((row >> bit) << (bit + 1)) + (side << bit) + low
    return (lax.broadcasted_iota(jnp.int32, (total // 2, total), 1) == (row ^ flip)).astype(BF16)


def push_back(bits, edges, side, flip, own, other, wown_ref, wother_ref, out_refs):
    for p, out_ref in enumerate(out_refs):
        pick = picker(bits[p], side, flip, own.shape[0])
        part = slice(edges[p], edges[p + 1])
        total = 0.0
        for grad, w_ref in ((own, wown_ref), (other, wother_ref)):
            rows = jnp.dot(pick, grad, preferred_element_type=F32).astype(BF16)
            total += lax.dot_general(
                rows, w_ref[part, :], (((1,), (1,)), ((), ())), preferred_element_type=F32
            )
        out_ref[...] = total.astype(out_ref.dtype)


def send_kernel(bits, edges, n, at_ref, *refs):
    stats_refs = refs[:n]
    near_ref, far_ref, aligned_ref, wown_ref, wother_ref = refs[n : n + 5]
    gown_ref, gother_ref = refs[n + 5 : n + 7]
    out_refs = refs[n + 7 :]
    flip = at_ref[0]
    per, wide = near_ref.shape
    cols = wide // 2
    for j, logits_ref in enumerate((near_ref, far_ref)):
        rows = merged([ref[j] for ref in stats_refs])
        stats = jnp.concatenate(rows + (jnp.zeros((128 - STAT_ROWS, per), F32),)).T
        peak, hard, soft, tpeak, total, ids = [stats[:, i : i + 1] for i in range(6)]
        ids = ids.astype(jnp.int32)
        hard, soft, total = 16.0 / hard, 32.0 / soft, 32.0 / total
        for c, g_ref in enumerate((gown_ref, gother_ref)):
            part = slice(c * cols, (c + 1) * cols)
            column = at_ref[1 + c] + lax.broadcasted_iota(jnp.int32, (per, cols), 1)
            half = jnp.exp((logits_ref[:, part] - peak) * 0.5)
            taught = jnp.exp((aligned_ref[j, :, part].astype(F32) - tpeak) * 0.5)
            label = jnp.where(column == ids, 16.0, 0.0)
            grad = (half * soft - taught * total) + (half * half * hard - label)
            g_ref[j * per : (j + 1) * per, :] = grad.astype(BF16)
    push_back(bits, edges, 1, flip, gown_ref[...], gother_ref[...], wown_ref, wother_ref, out_refs)


def keep_kernel(bits, edges, at_ref, gown_ref, gother_ref, wown_ref, wother_ref, *out_refs):
    push_back(bits, edges, 0, at_ref[0], gown_ref[...], gother_ref[...], wown_ref, wother_ref, out_refs)


def send_rows(at, stats, near, far, aligned, own, other, bits, edges):
    depth, cols = own.shape
    per = near.shape[0]
    outs = [shape((per, edges[p + 1] - edges[p]), BF16) for p in range(3)]
    got = pl.pallas_call(
        lambda *refs: send_kernel(bits, edges, len(stats), *refs),
        out_shape=[shape((2 * per, cols), BF16)] * 2 + outs,
        in_specs=[SMEM] + [VMEM] * (len(stats) + 5),
        out_specs=[VMEM] * 5,
        compiler_params=params(20),
        cost_estimate=cost(4 * per * depth * cols, 2 * cols * depth * 2, 4 * per * cols),
        name="send_rows",
    )(at, *stats, near, far, aligned, own, other)
    return got[0], got[1], got[2:]


def keep_rows(at, gown, gother, own, other, bits, edges):
    depth, cols = own.shape
    per = gown.shape[0] // 2
    outs = [shape((per, edges[p + 1] - edges[p]), F32) for p in range(3)]
    return pl.pallas_call(
        lambda *refs: keep_kernel(bits, edges, *refs),
        out_shape=outs,
        in_specs=[SMEM] + [VMEM] * 4,
        out_specs=[VMEM] * 3,
        compiler_params=params(20),
        cost_estimate=cost(4 * per * depth * cols, 2 * cols * depth * 2),
        name="keep_rows",
    )(at, gown, gother, own, other)


def head_kernel(r0, r1, r2, r3, mine_ref, theirs_ref, out_ref):
    rows = jnp.concatenate([r0[...], r1[...], r2[...], r3[...]])
    grads = jnp.concatenate([mine_ref[...], theirs_ref[...]])
    out_ref[...] = lax.dot_general(
        rows, grads, (((0,), (0,)), ((), ())), preferred_element_type=F32
    ).astype(BF16)


def head_gradient(rows, mine, theirs):
    per, depth = rows[0].shape
    cols = mine.shape[1]
    tile = 512 if depth % 512 == 0 else depth
    whole = pl.BlockSpec((2 * per, cols), lambda i: (0, 0))
    slab = pl.BlockSpec((per, tile), lambda i: (0, i))
    return pl.pallas_call(
        head_kernel,
        grid=(depth // tile,),
        out_shape=shape((depth, cols), BF16),
        in_specs=[slab] * 4 + [whole] * 2,
        out_specs=pl.BlockSpec((tile, cols), lambda i: (i, 0)),
        compiler_params=params(12),
        cost_estimate=cost(8 * per * depth * cols, (4 * per + cols) * depth * 2),
        name="head_gradient",
    )(*rows, mine, theirs)


def body(hidden, token_ids, serving, head_weight, teacher_logits):
    groups = lax.axis_size("grp")
    shards = lax.axis_size("vocab")
    me_g = lax.axis_index("grp")
    me_v = lax.axis_index("vocab")
    per, depth = hidden.shape
    cols = head_weight.shape[1]
    owned = per // shards
    CORE, X = shards, 2 * shards
    Y, W = 1, 2
    count = groups * shards

    def swap(value, mask):
        return lax.ppermute(value, AXES, [(i, i ^ mask) for i in range(count)])

    def tie(*values):
        return lax.optimization_barrier(values)

    def ints(*values):
        return jnp.stack([jnp.asarray(v, jnp.int32) for v in values])

    quarter_rows = per // 4
    quarter = me_v & 3
    starts = [(quarter ^ k) * quarter_rows for k in range(4)]
    x0 = swap(lax.dynamic_slice_in_dim(hidden, starts[0], quarter_rows, 0), X)
    other_weight = swap(head_weight, CORE)
    second = lax.dynamic_slice_in_dim(hidden, starts[3], quarter_rows, 0)
    chip = me_g >> 1
    kept = lax.dynamic_slice_in_dim(teacher_logits, 2 * chip, 2, 1).swapaxes(0, 1)
    gone = lax.dynamic_slice_in_dim(teacher_logits, 2 * (chip ^ 1), 2, 1).swapaxes(0, 1)
    x0, second, kept, gone, near_in = tie(x0, second, kept, gone, hidden)
    x1 = swap(x0, Y)
    x2 = swap(x0, W)
    x3 = swap(second, X)
    taught_x = swap(gone, X)
    taught_core = swap(kept, CORE)
    logits0, stats0 = near_logits(near_in, head_weight, other_weight)
    taught_far = swap(taught_x, CORE)
    aligned, taught_stats = teacher_rows(
        ints(me_g, me_g & 1), serving, [kept, taught_core, taught_x, taught_far]
    )
    logits1, x_rows, stats = far_logits(
        ints(*starts), [x0, x1, x2, x3], head_weight, other_weight, stats0, taught_stats, token_ids
    )

    stats = merge([stats, swap(stats, X), swap(stats, Y), swap(stats, X + Y)], (0, 1, 0, 1))
    core_rows = swap(hidden, CORE)
    stats, x_sent = tie(stats, x_rows)
    core_x_rows = swap(x_sent, CORE)
    mask = W
    while True:
        masks = [mask, 2 * mask, 3 * mask] if 2 * mask < shards else [mask]
        parts = [stats] + [swap(stats, m) for m in masks]
        mask *= 4
        if mask >= shards:
            break
        stats = merge(parts, (0,) * len(parts))

    bits = shards.bit_length() - 1
    masks = {0: X}
    for b in range(bits):
        masks[1 + b] = shards >> (1 + b)
    ydim, wdim = bits, bits - 1
    third = depth // 128 // 3 * 128
    edges = (0, third, 2 * third, depth)
    orders = [(0, ydim, wdim), (ydim, wdim, 0), (wdim, 0, ydim)]
    low = owned.bit_length() - 1
    row_bit = {0: low + bits, ydim: low, wdim: low + 1}
    first_bits = tuple(row_bit[order[0]] for order in orders)
    at = ints(
        me_v * owned, (me_g * shards + me_v) * cols, ((me_g ^ 1) * shards + me_v) * cols
    )
    gown, gother, sents = send_rows(
        at, parts, logits0, logits1, aligned, head_weight, other_weight, first_bits, edges
    )
    gots = [swap(sents[p], masks[orders[p][0]]) for p in range(3)]
    theirs = swap(gother, CORE)
    keeps = keep_rows(at, gown, gother, head_weight, other_weight, first_bits, edges)
    grad_head = head_gradient([hidden, x_rows, core_rows, core_x_rows], gown, theirs)
    grad_head, *gots = tie(grad_head, *gots)

    def folded(value, p):
        dims = [2] * (1 + bits)
        dims[orders[p][0]] = 1
        return value.reshape(*dims, owned, value.shape[-1])

    terms = [[folded(keeps[p], p), folded(gots[p], p)] for p in range(3)]
    for stage in (1, 2):
        sents = [
            sum(lax.index_in_dim(t, 1, orders[p][stage]).astype(F32) for t in terms[p]).astype(BF16)
            for p in range(3)
        ]
        gots = [swap(sents[p], masks[orders[p][stage]]) for p in range(3)]
        for p in range(3):
            terms[p] = [lax.index_in_dim(t, 0, orders[p][stage]) for t in terms[p]] + [gots[p]]
    total = jnp.concatenate([sum(t.astype(F32) for t in ts) for ts in terms], axis=-1)
    for dim in range(1, wdim):
        got = swap(lax.index_in_dim(total, 1, dim).astype(BF16), masks[dim])
        total = lax.index_in_dim(total, 0, dim) + got.astype(F32)
    return (total.reshape(owned, depth), grad_head)


def solution(mesh):
    placed = (P("grp", None), P("grp"), P(), P(None, ("grp", "vocab")), P("grp", None, "vocab"))
    return jax.shard_map(
        body,
        mesh=mesh,
        in_specs=placed,
        out_specs=(P(("grp", "vocab"), None), P(None, ("grp", "vocab"))),
        check_vma=False,
    )
```

time: 310 us -> 97.1 us (0.31)
  waiting for transfers between devices: 169 us -> 26.9 us
  blocking collectives: 91.7 us -> 0 us
  Pallas kernels: 0 us -> 26.8 us
  starting transfers between devices: 4.25 us -> 28.6 us
  matrix products: 19.6 us -> 0 us
  between operations: 14.1 us -> 0.84 us
    reduce_scatter x1 -> x0, waiting for transfers between devices: 151 us -> none  [body(): lax.psum_scatter(lax.dot_general(activation_derivative, head_weight, (((1...]
    psum x1 -> x0, blocking collectives: 41.1 us -> none  [body(): lax.psum((jnp.sum(jnp.exp(shifted_pupil_activations), axis=1), jnp.sum(jn...]
    pmax x1 -> x0, blocking collectives: 40.3 us -> none  [body(): lax.pmax((local_peak, local_tpeak), ('grp', 'vocab'))]
    ppermute x0 -> x27, starting transfers between devices: none -> 28.6 us  [swap(): return lax.ppermute(value, AXES, [(i, i ^ mask) for i in range(count)])]
    ppermute x0 -> x27, waiting for transfers between devices: none -> 26.9 us  [swap(): return lax.ppermute(value, AXES, [(i, i ^ mask) for i in range(count)])]
    pallas_call x0 -> x7, Pallas kernels: none -> 26.8 us  [the longest x1 6.94 us: head_gradient(): pl.pallas_call(head_kernel, grid=(depth // tile,), out_shape=shape((depth...]
    dot_general x3 -> x0, matrix products: 19.6 us -> none  [the longest x1 7.69 us: body(): lax.dot_general(activation_derivative, head_weight, (((1,), (1,)), ((), (...]
    all_gather x1 -> x0, waiting for transfers between devices: 16.8 us -> none  [body(): lax.all_gather(hidden, 'grp', axis=0, tiled=True)]
  transfers between devices with their start and end apart: 3 -> 27, of which waited for: 2 -> 13; matrix products, arithmetic and copies ran while one was open for 6% -> 4% of each run, Pallas kernels for 0% -> 28%
where the time goes in v4:
time: 97.1 us; the launch traced here: 96.6 us
  starting transfers between devices  28.6 us (29%)
  waiting for transfers between devices  26.9 us (28%)
  Pallas kernels  26.8 us (28%)
  local copies, waits for them, and re-layouts  12.1 us (12%)
  other arithmetic  1.3 us (1%)
    ppermute x27, starting transfers between devices, swap(): return lax.ppermute(value, AXES, [(i, i ^ mask) for i in range(count)])  28.6 us
    ppermute x27, waiting for transfers between devices, swap(): return lax.ppermute(value, AXES, [(i, i ^ mask) for i in range(count)])  26.9 us
    unnamed x20, local copies, waits for them, and re-layouts  8.47 us
    pallas_call x1, Pallas kernels, head_gradient(): pl.pallas_call(head_kernel, grid=(depth // tile,), out_shape=shape((depth...  6.94 us
    pallas_call x1, Pallas kernels, send_rows(): pl.pallas_call(lambda *refs: send_kernel(bits, edges, len(stats), *refs),...  5.85 us
    pallas_call x1, Pallas kernels, keep_rows(): pl.pallas_call(lambda *refs: keep_kernel(bits, edges, *refs), out_shape=o...  5.02 us
    pallas_call x1, Pallas kernels, far_logits(): pl.pallas_call(far_kernel, out_shape=(shape((per, 2 * cols), F32), shape(...  3.92 us
    pallas_call x1, Pallas kernels, near_logits(): pl.pallas_call(near_kernel, out_shape=(shape((per, 2 * cols), F32), shape...  3.58 us
  transfers between devices with their start and end apart: 27, of which 13 were waited for; matrix products, arithmetic and copies ran while one was open for 4% of the time, Pallas kernels for 28%

profile of v4, /device:TPU:0, one launch (start us, length us, event | category | flops | bytes accessed | tf_op | source)
XLA Modules:
  0.0 96.6 jit_solution(11739867530509313053)
XLA Ops:
  0.6 0.0 copy-start.3
  0.6 0.5 collective-permute-start.4
  1.2 1.8 %constant_dynamic-slice_fusion.2 = (bf16[32,3584]{1,0:T(8,128)(2,1)}, bf16[32,3584]{1,0:T(8,128)(2,1)S(1)}) fusion(bf16[128,3584]{1,0:T(8,128)(2,1)} %r0.1, s32[]{:T(128)S(6)} %select_n.13, s32[]{:T(128)S(6)} %select_n.12), kind=kLoop, calls=%fused_computation.31 | loop fusion | bytes 917512 | tf_op jit(solution)/shard_map/dynamic_slice | solution.py:299
  2.9 2.6 %collective-permute-start = (bf16[32,3584]{1,0:T(8,128)(2,1)S(1)}, bf16[32,3584]{1,0:T(8,128)(2,1)}, u32[]{:S(2)}, u32[]{:S(2)}) collective-permute-start(bf16[32,3584]{1,0:T(8,128)(2,1)S(1)} %get-tuple-element.55), channel_id=1, source_target_pairs={{0,16},{1,17},{2,18},{3,19},{4,20},{5,21},{6,22},{7,23},{8,24},{9,... | collective-permute-start | bytes 688136 | tf_op jit(solution)/shard_map/ppermute | solution.py:286
  5.5 1.7 %constant_dynamic-slice_fusion = (bf16[128,2,512]{2,1,0:T(2,128)(2,1)S(1)}, bf16[128,2,512]{2,1,0:T(2,128)(2,1)S(1)}) fusion(bf16[128,4,512]{2,1,0:T(4,128)(2,1)} %param.9, s32[]{:T(128)S(6)} %select_n.15, s32[]{:T(128)S(6)} %select_n.14), kind=kLoop, calls=%fused_computation.29 | loop fusion | bytes 1048584 | tf_op jit(solution)/shard_map/dynamic_slice | solution.py:302
  7.3 0.1 copy_bitcast_fusion
  7.3 4.5 %collective-permute-done.x0 = bf16[32,3584]{1,0:T(8,128)(2,1)} collective-permute-done((bf16[32,3584]{1,0:T(8,128)(2,1)S(1)}, bf16[32,3584]{1,0:T(8,128)(2,1)}, u32[]{:S(2)}, u32[]{:S(2)}) %collective-permute-start) | collective-permute-done | bytes 229408 | tf_op jit(solution)/shard_map/ppermute | solution.py:286
  11.8 1.8 %collective-permute-start.6 = (bf16[2,128,512]{2,1,0:T(8,128)(2,1)S(1)}, bf16[2,128,512]{2,1,0:T(8,128)(2,1)S(1)}, u32[]{:S(2)}, u32[]{:S(2)}) collective-permute-start(bf16[2,128,512]{2,1,0:T(8,128)(2,1)S(1)} %get-tuple-element.33), channel_id=1, source_target_pairs={{0,16},{1,17},{2,18},{3,19},{4,20},{5,21},{6,22},{7,23},{8,24},{9,... | collective-permute-start | bytes 786440 | tf_op jit(solution)/shard_map/ppermute | solution.py:286
  13.6 0.0 collective-permute-start.5
  13.6 6.3 %collective-permute-done.6.a2 = bf16[2,128,512]{2,1,0:T(8,128)(2,1)S(1)} collective-permute-done((bf16[2,128,512]{2,1,0:T(8,128)(2,1)S(1)}, bf16[2,128,512]{2,1,0:T(8,128)(2,1)S(1)}, u32[]{:S(2)}, u32[]{:S(2)}) %collective-permute-start.6) | collective-permute-done | bytes 262176 | tf_op jit(solution)/shard_map/ppermute | solution.py:286
  19.8 1.6 %collective-permute-start.2 = (bf16[32,3584]{1,0:T(8,128)(2,1)}, bf16[32,3584]{1,0:T(8,128)(2,1)}, u32[]{:S(2)}, u32[]{:S(2)}) collective-permute-start(bf16[32,3584]{1,0:T(8,128)(2,1)} %collective-permute-done.x0), channel_id=1, source_target_pairs={{0,2},{1,3},{2,0},{3,1},{4,6},{5,7},{6,4},{7,5},{8,10},{9,11},{10,... | collective-permute-start | bytes 688136 | tf_op jit(solution)/shard_map/ppermute | solution.py:286
  21.5 1.5 %collective-permute-start.1 = (bf16[32,3584]{1,0:T(8,128)(2,1)}, bf16[32,3584]{1,0:T(8,128)(2,1)}, u32[]{:S(2)}, u32[]{:S(2)}) collective-permute-start(bf16[32,3584]{1,0:T(8,128)(2,1)} %collective-permute-done.x0), channel_id=1, source_target_pairs={{0,1},{1,0},{2,3},{3,2},{4,5},{5,4},{6,7},{7,6},{8,9},{9,8},{10,11... | collective-permute-start | bytes 688136 | tf_op jit(solution)/shard_map/ppermute | solution.py:286
  23.0 0.0 collective-permute-done.5.a1
  23.0 1.5 %collective-permute-start.3 = (bf16[32,3584]{1,0:T(8,128)(2,1)}, bf16[32,3584]{1,0:T(8,128)(2,1)}, u32[]{:S(2)}, u32[]{:S(2)}) collective-permute-start(bf16[32,3584]{1,0:T(8,128)(2,1)} %get-tuple-element.29), channel_id=1, source_target_pairs={{0,16},{1,17},{2,18},{3,19},{4,20},{5,21},{6,22},{7,23},{8,24},{9,... | collective-permute-start | bytes 688136 | tf_op jit(solution)/shard_map/ppermute | solution.py:286
  24.5 0.1 pad_add_fusion.2.at_ref
  24.6 0.1 pad_add_fusion.1.spots_ref
  24.7 0.0 collective-permute-done.7.a3
  24.7 0.0 collective-permute-start.14
  24.7 0.0 copy-start.8
  24.7 0.7 copy-done.8
  25.4 1.5 %teacher_rows.1 = (bf16[2,128,1024]{2,1,0:T(8,128)(2,1)S(1)}, f32[2,8,128]{2,1,0:T(8,128)S(1)}) custom-call(s32[2]{0:T(128)S(1)} %pad_add_fusion.2.at_ref, s32[4,1,128]{2,1,0:T(1,128)S(1)} %bitcast.40, bf16[2,128,512]{2,1,0:T(8,128)(2,1)S(1)} %get-tuple-element.32.a0, bf16[2,128,512]{2,1,0:T(8,128)(2,1)S(1)} %collective-permute-done.5.a1, ...), custom_call_target="tpu_custom_call" | custom-call | flops 268435456 | bytes 1572864 | tf_op jit(solution)/shard_map/teacher_rows/pallas_call | solution.py:61
  26.9 2.0 %copy-done = bf16[3584,512]{1,0:T(8,128)(2,1)S(1)} copy-done((bf16[3584,512]{1,0:T(8,128)(2,1)S(1)}, bf16[3584,512]{1,0:T(8,128)(2,1)}, u32[]{:S(2)}) %copy-start) | copy-done | bytes 3670040
  28.9 3.6 %near_logits.1 = (f32[128,1024]{1,0:T(8,128)S(1)}, f32[8,128]{1,0:T(8,128)S(1)}) custom-call(bf16[128,3584]{1,0:T(8,128)(2,1)S(1)} %copy-done.3, bf16[3584,512]{1,0:T(8,128)(2,1)S(1)} %copy-done, bf16[3584,512]{1,0:T(8,128)(2,1)} %collective-permute-done.4.other_ref.refs_9_.refs_4_), custom_call_target="tpu_custom_call" | custom-call | flops 939524096 | bytes 8257536 | tf_op jit(solution)/shard_map/near_logits/pallas_call | solution.py:93
  32.5 0.8 copy-done.4
  33.4 3.9 %far_logits.1 = (f32[128,1024]{1,0:T(8,128)S(1)}, bf16[128,3584]{1,0:T(8,128)(2,1)S(1)}, f32[2,8,128]{2,1,0:T(8,128)S(1)}) custom-call(s32[4]{0:T(128)S(1)} %pad_add_fusion.1.spots_ref, bf16[32,3584]{1,0:T(8,128)(2,1)} %collective-permute-done.x0, bf16[32,3584]{1,0:T(8,128)(2,1)} %collective-permute-done.1.x1, bf16[32,3584]{1,0:T(8,128)(2,1)} %collective-permute-done.2.x2, ...), custom_call_target="tpu_custom_call" | custom-call | flops 939524096 | bytes 8257536 | tf_op jit(solution)/shard_map/far_logits/pallas_call | solution.py:120
  37.3 0.8 copy-done.6
  38.1 0.5 collective-permute-start.10
  38.6 1.5 %collective-permute-start.9 = (f32[2,8,128]{2,1,0:T(8,128)S(1)}, f32[2,8,128]{2,1,0:T(8,128)S(1)}, u32[]{:S(2)}, u32[]{:S(2)}) collective-permute-start(f32[2,8,128]{2,1,0:T(8,128)S(1)} %get-tuple-element.35.refs_0_), channel_id=1, source_target_pairs={{0,1},{1,0},{2,3},{3,2},{4,5},{5,4},{6,7},{7,6},{8,9},{9,8},{10,11... | collective-permute-start | bytes 24584 | tf_op jit(solution)/shard_map/ppermute | solution.py:286
  40.1 1.5 %collective-permute-start.8 = (f32[2,8,128]{2,1,0:T(8,128)S(1)}, f32[2,8,128]{2,1,0:T(8,128)S(1)}, u32[]{:S(2)}, u32[]{:S(2)}) collective-permute-start(f32[2,8,128]{2,1,0:T(8,128)S(1)} %get-tuple-element.35.refs_0_), channel_id=1, source_target_pairs={{0,16},{1,17},{2,18},{3,19},{4,20},{5,21},{6,22},{7,23},{8,24},{9,... | collective-permute-start | bytes 24584 | tf_op jit(solution)/shard_map/ppermute | solution.py:286
  41.6 1.1 %collective-permute-done.10.refs_3_ = f32[2,8,128]{2,1,0:T(8,128)S(1)} collective-permute-done((f32[2,8,128]{2,1,0:T(8,128)S(1)}, f32[2,8,128]{2,1,0:T(8,128)S(1)}, u32[]{:S(2)}, u32[]{:S(2)}) %collective-permute-start.10) | collective-permute-done | bytes 8224 | tf_op jit(solution)/shard_map/ppermute | solution.py:286
  42.7 1.0 %collective-permute-done.8.refs_1_ = f32[2,8,128]{2,1,0:T(8,128)S(1)} collective-permute-done((f32[2,8,128]{2,1,0:T(8,128)S(1)}, f32[2,8,128]{2,1,0:T(8,128)S(1)}, u32[]{:S(2)}, u32[]{:S(2)}) %collective-permute-start.8) | collective-permute-done | bytes 8224 | tf_op jit(solution)/shard_map/ppermute | solution.py:286
  43.8 0.1 collective-permute-start.15
  43.9 2.6 %collective-permute-start.13 = (f32[2,8,128]{2,1,0:T(8,128)S(1)}, f32[2,8,128]{2,1,0:T(8,128)S(1)}, u32[]{:S(2)}, u32[]{:S(2)}) collective-permute-start(f32[2,8,128]{2,1,0:T(8,128)S(1)} %merge_stats.1.refs_1_), channel_id=1, source_target_pairs={{0,6},{1,7},{2,4},{3,5},{4,2},{5,3},{6,0},{7,1},{8,14},{9,15},{10,... | collective-permute-start | bytes 24584 | tf_op jit(solution)/shard_map/ppermute | solution.py:286
  46.4 0.2 collective-permute-start.12
  46.6 1.7 %collective-permute-start.11 = (f32[2,8,128]{2,1,0:T(8,128)S(1)}, f32[2,8,128]{2,1,0:T(8,128)S(1)}, u32[]{:S(2)}, u32[]{:S(2)}) collective-permute-start(f32[2,8,128]{2,1,0:T(8,128)S(1)} %merge_stats.1.refs_1_), channel_id=1, source_target_pairs={{0,2},{1,3},{2,0},{3,1},{4,6},{5,7},{6,4},{7,5},{8,10},{9,11},{10,... | collective-permute-start | bytes 24584 | tf_op jit(solution)/shard_map/ppermute | solution.py:286
  48.3 0.1 pad_add_fusion.refs_0_
  48.4 1.0 %collective-permute-done.13.refs_4_ = f32[2,8,128]{2,1,0:T(8,128)S(1)} collective-permute-done((f32[2,8,128]{2,1,0:T(8,128)S(1)}, f32[2,8,128]{2,1,0:T(8,128)S(1)}, u32[]{:S(2)}, u32[]{:S(2)}) %collective-permute-start.13) | collective-permute-done | bytes 8224 | tf_op jit(solution)/shard_map/ppermute | solution.py:286
  49.4 1.5 %collective-permute-done.12.refs_3_ = f32[2,8,128]{2,1,0:T(8,128)S(1)} collective-permute-done((f32[2,8,128]{2,1,0:T(8,128)S(1)}, f32[2,8,128]{2,1,0:T(8,128)S(1)}, u32[]{:S(2)}, u32[]{:S(2)}) %collective-permute-start.12) | collective-permute-done | bytes 8224 | tf_op jit(solution)/shard_map/ppermute | solution.py:286
  51.0 2.0 %copy-done.2 = bf16[3584,512]{1,0:T(8,128)(2,1)S(1)} copy-done((bf16[3584,512]{1,0:T(8,128)(2,1)S(1)}, bf16[3584,512]{1,0:T(8,128)(2,1)}, u32[]{:S(2)}) %copy-start.2) | copy-done | bytes 3670040
  53.0 1.0 %copy-done.5 = f32[128,1024]{1,0:T(8,128)S(1)} copy-done((f32[128,1024]{1,0:T(8,128)S(1)}, f32[128,1024]{1,0:T(8,128)}, u32[]{:S(2)}) %copy-start.5) | copy-done | bytes 524312
  54.1 1.0 %copy-done.7 = f32[128,1024]{1,0:T(8,128)S(1)} copy-done((f32[128,1024]{1,0:T(8,128)S(1)}, f32[128,1024]{1,0:T(8,128)}, u32[]{:S(2)}) %copy-start.7) | copy-done | bytes 524312
  55.1 5.8 %send_rows.1 = (bf16[256,512]{1,0:T(8,128)(2,1)S(1)}, bf16[256,512]{1,0:T(8,128)(2,1)S(1)}, bf16[128,1152]{1,0:T(8,128)(2,1)S(1)}, bf16[128,1152]{1,0:T(8,128)(2,1)S(1)}, bf16[128,1280]{1,0:T(8,128)(2,1)S(1)}) custom-call(s32[3]{0:T(128)S(1)} %pad_add_fusion.refs_0_, f32[2,8,128]{2,1,0:T(8,128)S(1)} %merge_stats.1.refs_1_, ...), custom_call_target="tpu_custom_call" | custom-call | flops 939524096 | bytes 7340032 | tf_op jit(solution)/shard_map/send_rows/pallas_call | solution.py:220
  60.9 0.1 collective-permute-start.16
  61.0 1.1 %collective-permute-start.19 = (bf16[128,1280]{1,0:T(8,128)(2,1)S(1)}, bf16[128,1280]{1,0:T(8,128)(2,1)S(1)}, u32[]{:S(2)}, u32[]{:S(2)}) collective-permute-start(bf16[128,1280]{1,0:T(8,128)(2,1)S(1)} %get-tuple-element.47), channel_id=1, source_target_pairs={{0,2},{1,3},{2,0},{3,1},{4,6},{5,7},{6,4},{7,5},{8,10},{9,11},{10,... | collective-permute-start | bytes 983048 | tf_op jit(solution)/shard_map/ppermute | solution.py:286
  62.1 1.5 %collective-permute-start.17 = (bf16[128,1152]{1,0:T(8,128)(2,1)S(1)}, bf16[128,1152]{1,0:T(8,128)(2,1)S(1)}, u32[]{:S(2)}, u32[]{:S(2)}) collective-permute-start(bf16[128,1152]{1,0:T(8,128)(2,1)S(1)} %get-tuple-element.45), channel_id=1, source_target_pairs={{0,16},{1,17},{2,18},{3,19},{4,20},{5,21},{6,22},{7,23},{8,24},{9,... | collective-permute-start | bytes 884744 | tf_op jit(solution)/shard_map/ppermute | solution.py:286
  63.6 0.5 collective-permute-start.18
  64.1 5.0 %keep_rows.1 = (f32[128,1152]{1,0:T(8,128)S(1)}, f32[128,1152]{1,0:T(8,128)S(1)}, f32[128,1280]{1,0:T(8,128)S(1)}) custom-call(s32[3]{0:T(128)S(1)} %pad_add_fusion.refs_0_, bf16[256,512]{1,0:T(8,128)(2,1)S(1)} %get-tuple-element.41.refs_1_.mine_ref, bf16[256,512]{1,0:T(8,128)(2,1)S(1)} %get-tuple-element.42.refs_2_, bf16[3584,512]{1,0:T(8,128)(2,1)S(1)} %copy-done.2, ...), custom_call_target="tpu_custom_call" | custom-call | flops 939524096 | bytes 7340032 | tf_op jit(solution)/shard_map/keep_rows/pallas_call | solution.py:236
  69.1 6.9 %head_gradient.1 = bf16[3584,512]{1,0:T(8,128)(2,1)} custom-call(bf16[128,3584]{1,0:T(8,128)(2,1)S(1)} %copy-done.3, bf16[128,3584]{1,0:T(8,128)(2,1)S(1)} %get-tuple-element.44.r1, bf16[128,3584]{1,0:T(8,128)(2,1)S(1)} %collective-permute-done.14.r2, bf16[128,3584]{1,0:T(8,128)(2,1)} %collective-permute-done.15.r3, ...), custom_call_target="tpu_custom_call" | custom-call | flops 1879048192 | bytes 7340032 | tf_op jit(solution)/shard_map/head_gradient/pallas_call | solution.py:261
  76.1 1.6 %collective-permute-start.20 = (bf16[1,2,2,1,16,1152]{5,4,3,2,1,0:T(8,128)(2,1)S(1)}, bf16[1,2,2,1,16,1152]{5,4,3,2,1,0:T(8,128)(2,1)S(1)}, u32[]{:S(2)}, u32[]{:S(2)}) collective-permute-start(bf16[1,2,2,1,16,1152]{5,4,3,2,1,0:T(8,128)(2,1)S(1)} %fusion.1), channel_id=1, source_target_pairs={{0,1},{1,0},{2,3},{3,2},{4,5},{5,4},{6,7},{7,6},{8,9},{9,8},{10,11... | collective-permute-start | bytes 442376 | tf_op jit(solution)/shard_map/ppermute | solution.py:286
  77.7 0.1 add_convert_fusion
  77.8 1.1 %collective-permute-start.22 = (bf16[2,2,1,1,16,1152]{5,4,3,2,1,0:T(8,128)(2,1)S(1)}, bf16[2,2,1,1,16,1152]{5,4,3,2,1,0:T(8,128)(2,1)S(1)}, u32[]{:S(2)}, u32[]{:S(2)}) collective-permute-start(bf16[2,2,1,1,16,1152]{5,4,3,2,1,0:T(8,128)(2,1)S(1)} %fusion), channel_id=1, source_target_pairs={{0,2},{1,3},{2,0},{3,1},{4,6},{5,7},{6,4},{7,5},{8,10},{9,11},{10,... | collective-permute-start | bytes 442376 | tf_op jit(solution)/shard_map/ppermute | solution.py:286
  78.9 0.5 collective-permute-start.24
  79.5 2.1 %collective-permute-done.20 = bf16[1,2,2,1,16,1152]{5,4,3,2,1,0:T(8,128)(2,1)S(1)} collective-permute-done((bf16[1,2,2,1,16,1152]{5,4,3,2,1,0:T(8,128)(2,1)S(1)}, bf16[1,2,2,1,16,1152]{5,4,3,2,1,0:T(8,128)(2,1)S(1)}, u32[]{:S(2)}, u32[]{:S(2)}) %collective-permute-start.20) | collective-permute-done | bytes 147488 | tf_op jit(solution)/shard_map/ppermute | solution.py:286
  81.6 1.1 %collective-permute-start.21 = (bf16[1,2,1,1,16,1152]{5,4,3,2,1,0:T(8,128)(2,1)S(1)}, bf16[1,2,1,1,16,1152]{5,4,3,2,1,0:T(8,128)(2,1)S(1)}, u32[]{:S(2)}, u32[]{:S(2)}) collective-permute-start(bf16[1,2,1,1,16,1152]{5,4,3,2,1,0:T(8,128)(2,1)S(1)} %fusion.12), channel_id=1, source_target_pairs={{0,2},{1,3},{2,0},{3,1},{4,6},{5,7},{6,4},{7,5},{8,10},{9,11},{10,... | collective-permute-start | bytes 221192 | tf_op jit(solution)/shard_map/ppermute | solution.py:286
  82.7 0.4 collective-permute-done.22
  83.1 0.6 collective-permute-start.23
  83.7 0.6 collective-permute-done.24
  84.3 0.7 collective-permute-start.25
  85.0 1.1 %collective-permute-done.21 = bf16[1,2,1,1,16,1152]{5,4,3,2,1,0:T(8,128)(2,1)S(1)} collective-permute-done((bf16[1,2,1,1,16,1152]{5,4,3,2,1,0:T(8,128)(2,1)S(1)}, bf16[1,2,1,1,16,1152]{5,4,3,2,1,0:T(8,128)(2,1)S(1)}, u32[]{:S(2)}, u32[]{:S(2)}) %collective-permute-start.21) | collective-permute-done | bytes 73760 | tf_op jit(solution)/shard_map/ppermute | solution.py:286
  86.1 1.5 %collective-permute-done.23 = bf16[1,2,1,1,16,1152]{5,4,3,2,1,0:T(8,128)(2,1)S(1)} collective-permute-done((bf16[1,2,1,1,16,1152]{5,4,3,2,1,0:T(8,128)(2,1)S(1)}, bf16[1,2,1,1,16,1152]{5,4,3,2,1,0:T(8,128)(2,1)S(1)}, u32[]{:S(2)}, u32[]{:S(2)}) %collective-permute-start.23) | collective-permute-done | bytes 73760 | tf_op jit(solution)/shard_map/ppermute | solution.py:286
  87.6 1.2 %collective-permute-done.25 = bf16[1,2,1,1,16,1280]{5,4,3,2,1,0:T(8,128)(2,1)S(1)} collective-permute-done((bf16[1,2,1,1,16,1280]{5,4,3,2,1,0:T(8,128)(2,1)S(1)}, bf16[1,2,1,1,16,1280]{5,4,3,2,1,0:T(8,128)(2,1)S(1)}, u32[]{:S(2)}, u32[]{:S(2)}) %collective-permute-start.25) | collective-permute-done | bytes 81952 | tf_op jit(solution)/shard_map/ppermute | solution.py:286
  88.9 2.4 %collective-permute-start.26 = (bf16[1,1,1,1,16,3584]{5,4,3,2,1,0:T(8,128)(2,1)S(1)}, bf16[1,1,1,1,16,3584]{5,4,3,2,1,0:T(8,128)(2,1)S(1)}, u32[]{:S(2)}, u32[]{:S(2)}) collective-permute-start(bf16[1,1,1,1,16,3584]{5,4,3,2,1,0:T(8,128)(2,1)S(1)} %slice.215), channel_id=1, source_target_pairs={{0,4},{1,5},{2,6},{3,7},{4,0},{5,1},{6,2},{7,3},{8,12},{9,13},{10,... | collective-permute-start | bytes 344072 | tf_op jit(solution)/shard_map/ppermute | solution.py:286
  91.3 4.6 %collective-permute-done.26 = bf16[1,1,1,1,16,3584]{5,4,3,2,1,0:T(8,128)(2,1)S(1)} collective-permute-done((bf16[1,1,1,1,16,3584]{5,4,3,2,1,0:T(8,128)(2,1)S(1)}, bf16[1,1,1,1,16,3584]{5,4,3,2,1,0:T(8,128)(2,1)S(1)}, u32[]{:S(2)}, u32[]{:S(2)}) %collective-permute-start.26) | collective-permute-done | bytes 114720 | tf_op jit(solution)/shard_map/ppermute | solution.py:286
  95.9 0.7 fusion.2
  (36 shorter events, 0.4 us)
Async XLA Ops:
  0.6 26.3 %copy-start.3 = (bf16[128,3584]{1,0:T(8,128)(2,1)S(1)}, bf16[128,3584]{1,0:T(8,128)(2,1)}, u32[]{:S(2)}) copy-start(bf16[128,3584]{1,0:T(8,128)(2,1)} %r0.1) | copy-start | bytes 2752516
  0.6 26.2 %collective-permute-start.4 = (bf16[3584,512]{1,0:T(8,128)(2,1)}, bf16[3584,512]{1,0:T(8,128)(2,1)}, u32[]{:S(2)}, u32[]{:S(2)}) collective-permute-start(bf16[3584,512]{1,0:T(8,128)(2,1)} %refs_3_.1), channel_id=1, source_target_pairs={{0,8},{1,9},{2,10},{3,11},{4,12},{5,13},{6,14},{7,15},{8,0},{9,1},... | collective-permute-start | bytes 11010056 | tf_op jit(solution)/shard_map/ppermute | solution.py:286
  2.9 8.9 %collective-permute-start = (bf16[32,3584]{1,0:T(8,128)(2,1)S(1)}, bf16[32,3584]{1,0:T(8,128)(2,1)}, u32[]{:S(2)}, u32[]{:S(2)}) collective-permute-start(bf16[32,3584]{1,0:T(8,128)(2,1)S(1)} %get-tuple-element.55), channel_id=1, source_target_pairs={{0,16},{1,17},{2,18},{3,19},{4,20},{5,21},{6,22},{7,23},{8,24},{9,... | collective-permute-start | bytes 688136 | tf_op jit(solution)/shard_map/ppermute | solution.py:286
  11.8 8.0 %collective-permute-start.6 = (bf16[2,128,512]{2,1,0:T(8,128)(2,1)S(1)}, bf16[2,128,512]{2,1,0:T(8,128)(2,1)S(1)}, u32[]{:S(2)}, u32[]{:S(2)}) collective-permute-start(bf16[2,128,512]{2,1,0:T(8,128)(2,1)S(1)} %get-tuple-element.33), channel_id=1, source_target_pairs={{0,16},{1,17},{2,18},{3,19},{4,20},{5,21},{6,22},{7,23},{8,24},{9,... | collective-permute-start | bytes 786440 | tf_op jit(solution)/shard_map/ppermute | solution.py:286
  13.6 9.5 %collective-permute-start.5 = (bf16[2,128,512]{2,1,0:T(8,128)(2,1)S(1)}, bf16[2,128,512]{2,1,0:T(8,128)(2,1)S(1)}, u32[]{:S(2)}, u32[]{:S(2)}) collective-permute-start(bf16[2,128,512]{2,1,0:T(8,128)(2,1)S(1)} %get-tuple-element.32.a0), channel_id=1, source_target_pairs={{0,8},{1,9},{2,10},{3,11},{4,12},{5,13},{6,14},{7,15},{8,0},{9,1},... | collective-permute-start | bytes 786440 | tf_op jit(solution)/shard_map/ppermute | solution.py:286
  19.8 4.8 %collective-permute-start.7 = (bf16[2,128,512]{2,1,0:T(8,128)(2,1)S(1)}, bf16[2,128,512]{2,1,0:T(8,128)(2,1)S(1)}, u32[]{:S(2)}, u32[]{:S(2)}) collective-permute-start(bf16[2,128,512]{2,1,0:T(8,128)(2,1)S(1)} %collective-permute-done.6.a2), channel_id=1, source_target_pairs={{0,8},{1,9},{2,10},{3,11},{4,12},{5,13},{6,14},{7,15},{8,0},{9,1},... | collective-permute-start | bytes 786440 | tf_op jit(solution)/shard_map/ppermute | solution.py:286
  19.8 13.5 %collective-permute-start.2 = (bf16[32,3584]{1,0:T(8,128)(2,1)}, bf16[32,3584]{1,0:T(8,128)(2,1)}, u32[]{:S(2)}, u32[]{:S(2)}) collective-permute-start(bf16[32,3584]{1,0:T(8,128)(2,1)} %collective-permute-done.x0), channel_id=1, source_target_pairs={{0,2},{1,3},{2,0},{3,1},{4,6},{5,7},{6,4},{7,5},{8,10},{9,11},{10,... | collective-permute-start | bytes 688136 | tf_op jit(solution)/shard_map/ppermute | solution.py:286
  21.5 11.8 %collective-permute-start.1 = (bf16[32,3584]{1,0:T(8,128)(2,1)}, bf16[32,3584]{1,0:T(8,128)(2,1)}, u32[]{:S(2)}, u32[]{:S(2)}) collective-permute-start(bf16[32,3584]{1,0:T(8,128)(2,1)} %collective-permute-done.x0), channel_id=1, source_target_pairs={{0,1},{1,0},{2,3},{3,2},{4,5},{5,4},{6,7},{7,6},{8,9},{9,8},{10,11... | collective-permute-start | bytes 688136 | tf_op jit(solution)/shard_map/ppermute | solution.py:286
  23.0 10.3 %collective-permute-start.3 = (bf16[32,3584]{1,0:T(8,128)(2,1)}, bf16[32,3584]{1,0:T(8,128)(2,1)}, u32[]{:S(2)}, u32[]{:S(2)}) collective-permute-start(bf16[32,3584]{1,0:T(8,128)(2,1)} %get-tuple-element.29), channel_id=1, source_target_pairs={{0,16},{1,17},{2,18},{3,19},{4,20},{5,21},{6,22},{7,23},{8,24},{9,... | collective-permute-start | bytes 688136 | tf_op jit(solution)/shard_map/ppermute | solution.py:286
  24.7 38.9 %collective-permute-start.14 = (bf16[128,3584]{1,0:T(8,128)(2,1)}, bf16[128,3584]{1,0:T(8,128)(2,1)S(1)}, u32[]{:S(2)}, u32[]{:S(2)}) collective-permute-start(bf16[128,3584]{1,0:T(8,128)(2,1)} %r0.1), channel_id=1, source_target_pairs={{0,8},{1,9},{2,10},{3,11},{4,12},{5,13},{6,14},{7,15},{8,0},{9,1},... | collective-permute-start | bytes 2752520 | tf_op jit(solution)/shard_map/ppermute | solution.py:286
  24.7 0.7 copy-start.8
  26.9 2.1 %copy-start = (bf16[3584,512]{1,0:T(8,128)(2,1)S(1)}, bf16[3584,512]{1,0:T(8,128)(2,1)}, u32[]{:S(2)}) copy-start(bf16[3584,512]{1,0:T(8,128)(2,1)} %refs_3_.1) | copy-start | bytes 11010052
  28.9 4.4 %copy-start.1 = (bf16[3584,512]{1,0:T(8,128)(2,1)S(1)}, bf16[3584,512]{1,0:T(8,128)(2,1)}, u32[]{:S(2)}) copy-start(bf16[3584,512]{1,0:T(8,128)(2,1)} %refs_3_.1) | copy-start | bytes 11010052
  28.9 4.4 %copy-start.9 = (s32[128]{0:T(128)S(1)}, s32[128]{0:T(128)}, u32[]{:S(2)}) copy-start(s32[128]{0:T(128)} %param.6) | copy-start | bytes 1540
  32.5 0.8 copy-start.4
  37.3 0.8 copy-start.6
  38.1 4.6 %collective-permute-start.10 = (f32[2,8,128]{2,1,0:T(8,128)S(1)}, f32[2,8,128]{2,1,0:T(8,128)S(1)}, u32[]{:S(2)}, u32[]{:S(2)}) collective-permute-start(f32[2,8,128]{2,1,0:T(8,128)S(1)} %get-tuple-element.35.refs_0_), channel_id=1, source_target_pairs={{0,17},{1,16},{2,19},{3,18},{4,21},{5,20},{6,23},{7,22},{8,25},{9,... | collective-permute-start | bytes 24584 | tf_op jit(solution)/shard_map/ppermute | solution.py:286
  38.6 4.1 %collective-permute-start.9 = (f32[2,8,128]{2,1,0:T(8,128)S(1)}, f32[2,8,128]{2,1,0:T(8,128)S(1)}, u32[]{:S(2)}, u32[]{:S(2)}) collective-permute-start(f32[2,8,128]{2,1,0:T(8,128)S(1)} %get-tuple-element.35.refs_0_), channel_id=1, source_target_pairs={{0,1},{1,0},{2,3},{3,2},{4,5},{5,4},{6,7},{7,6},{8,9},{9,8},{10,11... | collective-permute-start | bytes 24584 | tf_op jit(solution)/shard_map/ppermute | solution.py:286
  40.1 3.7 %collective-permute-start.8 = (f32[2,8,128]{2,1,0:T(8,128)S(1)}, f32[2,8,128]{2,1,0:T(8,128)S(1)}, u32[]{:S(2)}, u32[]{:S(2)}) collective-permute-start(f32[2,8,128]{2,1,0:T(8,128)S(1)} %get-tuple-element.35.refs_0_), channel_id=1, source_target_pairs={{0,16},{1,17},{2,18},{3,19},{4,20},{5,21},{6,22},{7,23},{8,24},{9,... | collective-permute-start | bytes 24584 | tf_op jit(solution)/shard_map/ppermute | solution.py:286
  43.8 25.4 %collective-permute-start.15 = (bf16[128,3584]{1,0:T(8,128)(2,1)S(1)}, bf16[128,3584]{1,0:T(8,128)(2,1)}, u32[]{:S(2)}, u32[]{:S(2)}) collective-permute-start(bf16[128,3584]{1,0:T(8,128)(2,1)S(1)} %get-tuple-element.44.r1), channel_id=1, source_target_pairs={{0,8},{1,9},{2,10},{3,11},{4,12},{5,13},{6,14},{7,15},{8,0},{9,1},... | collective-permute-start | bytes 2752520 | tf_op jit(solution)/shard_map/ppermute | solution.py:286
  43.9 5.6 %collective-permute-start.13 = (f32[2,8,128]{2,1,0:T(8,128)S(1)}, f32[2,8,128]{2,1,0:T(8,128)S(1)}, u32[]{:S(2)}, u32[]{:S(2)}) collective-permute-start(f32[2,8,128]{2,1,0:T(8,128)S(1)} %merge_stats.1.refs_1_), channel_id=1, source_target_pairs={{0,6},{1,7},{2,4},{3,5},{4,2},{5,3},{6,0},{7,1},{8,14},{9,15},{10,... | collective-permute-start | bytes 24584 | tf_op jit(solution)/shard_map/ppermute | solution.py:286
  46.4 4.5 %collective-permute-start.12 = (f32[2,8,128]{2,1,0:T(8,128)S(1)}, f32[2,8,128]{2,1,0:T(8,128)S(1)}, u32[]{:S(2)}, u32[]{:S(2)}) collective-permute-start(f32[2,8,128]{2,1,0:T(8,128)S(1)} %merge_stats.1.refs_1_), channel_id=1, source_target_pairs={{0,4},{1,5},{2,6},{3,7},{4,0},{5,1},{6,2},{7,3},{8,12},{9,13},{10,... | collective-permute-start | bytes 24584 | tf_op jit(solution)/shard_map/ppermute | solution.py:286
  46.6 4.4 %collective-permute-start.11 = (f32[2,8,128]{2,1,0:T(8,128)S(1)}, f32[2,8,128]{2,1,0:T(8,128)S(1)}, u32[]{:S(2)}, u32[]{:S(2)}) collective-permute-start(f32[2,8,128]{2,1,0:T(8,128)S(1)} %merge_stats.1.refs_1_), channel_id=1, source_target_pairs={{0,2},{1,3},{2,0},{3,1},{4,6},{5,7},{6,4},{7,5},{8,10},{9,11},{10,... | collective-permute-start | bytes 24584 | tf_op jit(solution)/shard_map/ppermute | solution.py:286
  51.0 2.0 %copy-start.2 = (bf16[3584,512]{1,0:T(8,128)(2,1)S(1)}, bf16[3584,512]{1,0:T(8,128)(2,1)}, u32[]{:S(2)}) copy-start(bf16[3584,512]{1,0:T(8,128)(2,1)} %refs_3_.1) | copy-start | bytes 11010052
  53.0 1.0 %copy-start.5 = (f32[128,1024]{1,0:T(8,128)S(1)}, f32[128,1024]{1,0:T(8,128)}, u32[]{:S(2)}) copy-start(f32[128,1024]{1,0:T(8,128)} %copy-done.4) | copy-start | bytes 1572868
  54.1 1.0 %copy-start.7 = (f32[128,1024]{1,0:T(8,128)S(1)}, f32[128,1024]{1,0:T(8,128)}, u32[]{:S(2)}) copy-start(f32[128,1024]{1,0:T(8,128)} %copy-done.6) | copy-start | bytes 1572868
  60.9 8.2 %collective-permute-start.16 = (bf16[256,512]{1,0:T(8,128)(2,1)S(1)}, bf16[256,512]{1,0:T(8,128)(2,1)S(1)}, u32[]{:S(2)}, u32[]{:S(2)}) collective-permute-start(bf16[256,512]{1,0:T(8,128)(2,1)S(1)} %get-tuple-element.42.refs_2_), channel_id=1, source_target_pairs={{0,8},{1,9},{2,10},{3,11},{4,12},{5,13},{6,14},{7,15},{8,0},{9,1},... | collective-permute-start | bytes 786440 | tf_op jit(solution)/shard_map/ppermute | solution.py:286
  61.0 15.1 %collective-permute-start.19 = (bf16[128,1280]{1,0:T(8,128)(2,1)S(1)}, bf16[128,1280]{1,0:T(8,128)(2,1)S(1)}, u32[]{:S(2)}, u32[]{:S(2)}) collective-permute-start(bf16[128,1280]{1,0:T(8,128)(2,1)S(1)} %get-tuple-element.47), channel_id=1, source_target_pairs={{0,2},{1,3},{2,0},{3,1},{4,6},{5,7},{6,4},{7,5},{8,10},{9,11},{10,... | collective-permute-start | bytes 983048 | tf_op jit(solution)/shard_map/ppermute | solution.py:286
  62.1 14.0 %collective-permute-start.17 = (bf16[128,1152]{1,0:T(8,128)(2,1)S(1)}, bf16[128,1152]{1,0:T(8,128)(2,1)S(1)}, u32[]{:S(2)}, u32[]{:S(2)}) collective-permute-start(bf16[128,1152]{1,0:T(8,128)(2,1)S(1)} %get-tuple-element.45), channel_id=1, source_target_pairs={{0,16},{1,17},{2,18},{3,19},{4,20},{5,21},{6,22},{7,23},{8,24},{9,... | collective-permute-start | bytes 884744 | tf_op jit(solution)/shard_map/ppermute | solution.py:286
  63.6 12.5 %collective-permute-start.18 = (bf16[128,1152]{1,0:T(8,128)(2,1)S(1)}, bf16[128,1152]{1,0:T(8,128)(2,1)S(1)}, u32[]{:S(2)}, u32[]{:S(2)}) collective-permute-start(bf16[128,1152]{1,0:T(8,128)(2,1)S(1)} %get-tuple-element.46), channel_id=1, source_target_pairs={{0,1},{1,0},{2,3},{3,2},{4,5},{5,4},{6,7},{7,6},{8,9},{9,8},{10,11... | collective-permute-start | bytes 884744 | tf_op jit(solution)/shard_map/ppermute | solution.py:286
  76.1 5.4 %collective-permute-start.20 = (bf16[1,2,2,1,16,1152]{5,4,3,2,1,0:T(8,128)(2,1)S(1)}, bf16[1,2,2,1,16,1152]{5,4,3,2,1,0:T(8,128)(2,1)S(1)}, u32[]{:S(2)}, u32[]{:S(2)}) collective-permute-start(bf16[1,2,2,1,16,1152]{5,4,3,2,1,0:T(8,128)(2,1)S(1)} %fusion.1), channel_id=1, source_target_pairs={{0,1},{1,0},{2,3},{3,2},{4,5},{5,4},{6,7},{7,6},{8,9},{9,8},{10,11... | collective-permute-start | bytes 442376 | tf_op jit(solution)/shard_map/ppermute | solution.py:286
  77.8 5.2 %collective-permute-start.22 = (bf16[2,2,1,1,16,1152]{5,4,3,2,1,0:T(8,128)(2,1)S(1)}, bf16[2,2,1,1,16,1152]{5,4,3,2,1,0:T(8,128)(2,1)S(1)}, u32[]{:S(2)}, u32[]{:S(2)}) collective-permute-start(bf16[2,2,1,1,16,1152]{5,4,3,2,1,0:T(8,128)(2,1)S(1)} %fusion), channel_id=1, source_target_pairs={{0,2},{1,3},{2,0},{3,1},{4,6},{5,7},{6,4},{7,5},{8,10},{9,11},{10,... | collective-permute-start | bytes 442376 | tf_op jit(solution)/shard_map/ppermute | solution.py:286
  78.9 5.3 %collective-permute-start.24 = (bf16[1,2,1,2,16,1280]{5,4,3,2,1,0:T(8,128)(2,1)S(1)}, bf16[1,2,1,2,16,1280]{5,4,3,2,1,0:T(8,128)(2,1)S(1)}, u32[]{:S(2)}, u32[]{:S(2)}) collective-permute-start(bf16[1,2,1,2,16,1280]{5,4,3,2,1,0:T(8,128)(2,1)S(1)} %bitcast.52), channel_id=1, source_target_pairs={{0,16},{1,17},{2,18},{3,19},{4,20},{5,21},{6,22},{7,23},{8,24},{9,... | collective-permute-start | bytes 491528 | tf_op jit(solution)/shard_map/ppermute | solution.py:286
  81.6 4.4 %collective-permute-start.21 = (bf16[1,2,1,1,16,1152]{5,4,3,2,1,0:T(8,128)(2,1)S(1)}, bf16[1,2,1,1,16,1152]{5,4,3,2,1,0:T(8,128)(2,1)S(1)}, u32[]{:S(2)}, u32[]{:S(2)}) collective-permute-start(bf16[1,2,1,1,16,1152]{5,4,3,2,1,0:T(8,128)(2,1)S(1)} %fusion.12), channel_id=1, source_target_pairs={{0,2},{1,3},{2,0},{3,1},{4,6},{5,7},{6,4},{7,5},{8,10},{9,11},{10,... | collective-permute-start | bytes 221192 | tf_op jit(solution)/shard_map/ppermute | solution.py:286
  83.1 4.4 %collective-permute-start.23 = (bf16[1,2,1,1,16,1152]{5,4,3,2,1,0:T(8,128)(2,1)S(1)}, bf16[1,2,1,1,16,1152]{5,4,3,2,1,0:T(8,128)(2,1)S(1)}, u32[]{:S(2)}, u32[]{:S(2)}) collective-permute-start(bf16[1,2,1,1,16,1152]{5,4,3,2,1,0:T(8,128)(2,1)S(1)} %fusion.8), channel_id=1, source_target_pairs={{0,16},{1,17},{2,18},{3,19},{4,20},{5,21},{6,22},{7,23},{8,24},{9,... | collective-permute-start | bytes 221192 | tf_op jit(solution)/shard_map/ppermute | solution.py:286
  84.3 4.5 %collective-permute-start.25 = (bf16[1,2,1,1,16,1280]{5,4,3,2,1,0:T(8,128)(2,1)S(1)}, bf16[1,2,1,1,16,1280]{5,4,3,2,1,0:T(8,128)(2,1)S(1)}, u32[]{:S(2)}, u32[]{:S(2)}) collective-permute-start(bf16[1,2,1,1,16,1280]{5,4,3,2,1,0:T(8,128)(2,1)S(1)} %fusion.4), channel_id=1, source_target_pairs={{0,1},{1,0},{2,3},{3,2},{4,5},{5,4},{6,7},{7,6},{8,9},{9,8},{10,11... | collective-permute-start | bytes 245768 | tf_op jit(solution)/shard_map/ppermute | solution.py:286
  88.9 7.0 %collective-permute-start.26 = (bf16[1,1,1,1,16,3584]{5,4,3,2,1,0:T(8,128)(2,1)S(1)}, bf16[1,1,1,1,16,3584]{5,4,3,2,1,0:T(8,128)(2,1)S(1)}, u32[]{:S(2)}, u32[]{:S(2)}) collective-permute-start(bf16[1,1,1,1,16,3584]{5,4,3,2,1,0:T(8,128)(2,1)S(1)} %slice.215), channel_id=1, source_target_pairs={{0,4},{1,5},{2,6},{3,7},{4,0},{5,1},{6,2},{7,3},{8,12},{9,13},{10,... | collective-permute-start | bytes 344072 | tf_op jit(solution)/shard_map/ppermute | solution.py:286

commit v5 on v4

v5 whole, which is shorter than its diff:
```python
import jax
import jax.numpy as jnp
from jax import lax
from jax.experimental import pallas as pl
from jax.experimental.pallas import tpu as pltpu
from jax.sharding import PartitionSpec as P

BF16 = jnp.bfloat16
F32 = jnp.float32
AXES = ("grp", "vocab")
VMEM = pl.BlockSpec(memory_space=pltpu.VMEM)
SMEM = pl.BlockSpec(memory_space=pltpu.SMEM)
STAT_ROWS = 8
MIB = 2**20


def params(mib):
    return pltpu.CompilerParams(vmem_limit_bytes=mib * MIB)


def cost(flops, nbytes, exps=0):
    return pl.CostEstimate(flops=flops, bytes_accessed=nbytes, transcendentals=exps)


def shape(dims, dtype):
    return jax.ShapeDtypeStruct(dims, dtype)


def columns_to_rows(columns):
    count = columns[0].shape[0]
    lane = lax.broadcasted_iota(jnp.int32, (count, 128), 1)
    wide = jnp.zeros((count, 128), F32)
    for k, column in enumerate(columns):
        wide = jnp.where(lane == k, column, wide)
    return wide.T[:STAT_ROWS]


def taught_kernel(kept_ref, gone_ref, out_ref):
    parts = [ref[c].astype(F32) for ref in (kept_ref, gone_ref) for c in range(2)]
    top = parts[0]
    for part in parts[1:]:
        top = jnp.maximum(top, part)
    peak = jnp.max(top, axis=1, keepdims=True)
    total = sum(jnp.exp((part - peak) * 0.5) for part in parts)
    out_ref[...] = columns_to_rows([peak, jnp.sum(total, axis=1, keepdims=True)])


def taught_stats(kept, gone):
    _, per, cols = kept.shape
    return pl.pallas_call(
        taught_kernel,
        out_shape=shape((STAT_ROWS, per), F32),
        in_specs=[VMEM] * 2,
        out_specs=VMEM,
        compiler_params=params(6),
        cost_estimate=cost(0, 4 * per * cols * 2, 4 * per * cols),
        name="taught_stats",
    )(kept, gone)


def teacher_kernel(at_ref, serving_ref, a0, a1, a2, a3, aligned_ref):
    me, core = at_ref[0], at_ref[1]
    _, per, cols = a0.shape
    for j in range(2):
        wanted = serving_ref[me ^ (2 * j)]
        sums = [0.0, 0.0]
        for k, arrived in enumerate((a0, a1, a2, a3)):
            row = lax.broadcasted_iota(jnp.int32, (per, per), 0) + (me ^ k) * per
            pick = (row == wanted).astype(BF16)
            for c in range(2):
                sums[c] += lax.dot_general(
                    pick, arrived[core ^ c], (((0,), (0,)), ((), ())), preferred_element_type=F32
                )
        for c in range(2):
            aligned_ref[j, :, c * cols : (c + 1) * cols] = sums[c].astype(BF16)


def teacher_rows(at, serving, arrived):
    _, per, cols = arrived[0].shape
    return pl.pallas_call(
        teacher_kernel,
        out_shape=shape((2, per, 2 * cols), BF16),
        in_specs=[SMEM] + [VMEM] * 5,
        out_specs=VMEM,
        compiler_params=params(10),
        cost_estimate=cost(32 * per * per * cols, 12 * per * cols * 2),
        name="teacher_rows",
    )(at, serving, *arrived)


def student_stats(logits_ref, a, b):
    cols = a.shape[1]
    logits_ref[:, :cols] = a
    logits_ref[:, cols:] = b
    peak = jnp.max(jnp.maximum(a, b), axis=1, keepdims=True)
    a = jnp.exp((a - peak) * 0.5)
    b = jnp.exp((b - peak) * 0.5)
    hard = jnp.sum(a * a + b * b, axis=1, keepdims=True)
    soft = jnp.sum(a + b, axis=1, keepdims=True)
    return columns_to_rows([peak, hard, soft])


def near_kernel(splits, rows_ref, w_ref, other_ref, logits_ref, stats_ref, own_ref, sems):
    step = w_ref.shape[0] // splits
    copies = []
    for c in range(splits):
        part = pl.ds(c * step, step)
        copies.append(pltpu.make_async_copy(w_ref.at[part], own_ref.at[part], sems.at[c]))
        copies[c].start()
    b = jnp.dot(rows_ref[...], other_ref[...], preferred_element_type=F32)
    a = 0.0
    for c in range(splits):
        copies[c].wait()
        part = slice(c * step, (c + 1) * step)
        a += jnp.dot(rows_ref[:, part], own_ref[part, :], preferred_element_type=F32)
    stats_ref[...] = student_stats(logits_ref, a, b)


def near_logits(rows, own, other):
    per, depth = rows.shape
    cols = own.shape[1]
    splits = 2 if depth % 256 == 0 else 1
    return pl.pallas_call(
        lambda *refs: near_kernel(splits, *refs),
        out_shape=(
            shape((per, 2 * cols), F32),
            shape((STAT_ROWS, per), F32),
            shape((depth, cols), BF16),
        ),
        in_specs=[VMEM, pl.BlockSpec(memory_space=pl.ANY), VMEM],
        out_specs=(VMEM, VMEM, VMEM),
        scratch_shapes=[pltpu.SemaphoreType.DMA((splits,))],
        compiler_params=params(16),
        cost_estimate=cost(4 * per * depth * cols, (per + 2 * cols) * depth * 2, 2 * per * cols),
        name="near_logits",
    )(rows, own, other)


NOTHING = -3.0e38


def far_kernel(spots_ref, x0, x1, x2, x3, own_ref, other_ref, near_ref, taught_ref, taught_core_ref, ids_ref, logits_ref, rows_ref, out_ref):
    count = x0.shape[0]
    for k, piece in enumerate((x0, x1, x2, x3)):
        rows_ref[pl.ds(pl.multiple_of(spots_ref[k], 16), count), :] = piece[...]
    per = rows_ref.shape[0]
    a = jnp.dot(rows_ref[...], own_ref[...], preferred_element_type=F32)
    b = jnp.dot(rows_ref[...], other_ref[...], preferred_element_type=F32)
    out_ref[0, 0:3, :] = near_ref[0:3, :]
    out_ref[0, 3:4, :] = ids_ref[...].astype(F32)
    out_ref[0, 4:6, :] = taught_ref[0:2, :]
    out_ref[0, 6:8, :] = taught_core_ref[0:2, :]
    out_ref[1, 0:3, :] = student_stats(logits_ref, a, b)[0:3]
    row = lax.broadcasted_iota(jnp.int32, (5, per), 0)
    out_ref[1, 3:8, :] = jnp.where((row == 1) | (row == 3), NOTHING, 0.0)


def far_logits(spots, pieces, own, other, near_stats, taught, taught_core, ids):
    depth, cols = own.shape
    per = sum(piece.shape[0] for piece in pieces)
    return pl.pallas_call(
        far_kernel,
        out_shape=(
            shape((per, 2 * cols), F32),
            shape((per, depth), BF16),
            shape((2, STAT_ROWS, per), F32),
        ),
        in_specs=[SMEM] + [VMEM] * 10,
        out_specs=(VMEM, VMEM, VMEM),
        compiler_params=params(20),
        cost_estimate=cost(4 * per * depth * cols, (per + 2 * cols) * depth * 2, 2 * per * cols),
        name="far_logits",
    )(spots, *pieces, own, other, near_stats, taught, taught_core, ids)


def merged(parts):
    top = parts[0]
    for part in parts[1:]:
        top = jnp.maximum(top, part)
    hard = soft = taught0 = taught1 = 0.0
    for part in parts:
        shrink = jnp.exp((part - top) * 0.5)
        s = shrink[0:1]
        hard += part[1:2] * (s * s)
        soft += part[2:3] * s
        taught0 += part[5:6] * shrink[4:5]
        taught1 += part[7:8] * shrink[6:7]
    return top[0:1], hard, soft, top[3:4], top[4:5], taught0, top[6:7], taught1


def merge_kernel(flips, *refs):
    out_ref = refs[-1]
    for j in range(2):
        out_ref[j] = jnp.concatenate(merged([ref[j ^ f] for ref, f in zip(refs, flips)]))


def merge(parts, flips, held):
    return pl.pallas_call(
        lambda *refs: merge_kernel(flips, *refs),
        out_shape=shape(parts[0].shape, F32),
        in_specs=[VMEM] * (len(parts) + len(held)),
        out_specs=VMEM,
        compiler_params=params(6),
        cost_estimate=cost(0, 5 * parts[0].size * 4),
        name="merge_stats",
    )(*parts, *held)


def picker(bit, flip, total):
    half = total // 2
    row = lax.broadcasted_iota(jnp.int32, (total, total), 0)
    side = jnp.where(row < half, 1 << bit, 0)
    row = row & (half - 1)
    row = ((row >> bit) << (bit + 1)) + side + (row & ((1 << bit) - 1))
    return (lax.broadcasted_iota(jnp.int32, (total, total), 1) == (row ^ flip)).astype(BF16)


def back_kernel(bits, edges, n, at_ref, *refs):
    stats_refs = refs[:n]
    serving_ref, near_ref, far_ref, aligned_ref, wown_ref, wother_ref = refs[n : n + 6]
    gown_ref, gother_ref = refs[n + 6 : n + 8]
    send_refs, keep_refs = refs[n + 8 : n + 11], refs[n + 11 :]
    flip, me = at_ref[0], at_ref[3]
    per, wide = near_ref.shape
    cols = wide // 2
    stats = [merged([ref[j] for ref in stats_refs]) for j in range(2)]
    lane = lax.broadcasted_iota(jnp.int32, (per, per), 1)
    for j, logits_ref in enumerate((near_ref, far_ref)):
        rows = stats[j][:4] + (serving_ref[me ^ (2 * j)].astype(F32),)
        columns = jnp.concatenate(rows + (jnp.zeros((128 - len(rows), per), F32),)).T
        peak, hard, soft, ids, wanted = [columns[:, i : i + 1] for i in range(len(rows))]
        ids, wanted = ids.astype(jnp.int32), wanted.astype(jnp.int32)
        tpeak = total = 0.0
        for k in range(4):
            here = wanted - (me ^ k) * per == lane
            taught = stats[k // 2][4 + 2 * (k % 2) : 6 + 2 * (k % 2)]
            tpeak += jnp.sum(jnp.where(here, taught[0], 0.0), axis=1, keepdims=True)
            total += jnp.sum(jnp.where(here, taught[1], 0.0), axis=1, keepdims=True)
        hard, soft, total = 16.0 / hard, 32.0 / soft, 32.0 / total
        for c, g_ref in enumerate((gown_ref, gother_ref)):
            part = slice(c * cols, (c + 1) * cols)
            column = at_ref[1 + c] + lax.broadcasted_iota(jnp.int32, (per, cols), 1)
            half = jnp.exp((logits_ref[:, part] - peak) * 0.5)
            taught = jnp.exp((aligned_ref[j, :, part].astype(F32) - tpeak) * 0.5)
            label = jnp.where(column == ids, 16.0, 0.0)
            grad = (half * soft - taught * total) + (half * half * hard - label)
            g_ref[j * per : (j + 1) * per, :] = grad.astype(BF16)
    for p in range(3):
        pick = picker(bits[p], flip, 2 * per)
        part = slice(edges[p], edges[p + 1])
        back = 0.0
        for g_ref, w_ref in ((gown_ref, wown_ref), (gother_ref, wother_ref)):
            rows = jnp.dot(pick, g_ref[...], preferred_element_type=F32).astype(BF16)
            back += lax.dot_general(
                rows, w_ref[part, :], (((1,), (1,)), ((), ())), preferred_element_type=F32
            )
        send_refs[p][...] = back[:per].astype(BF16)
        keep_refs[p][...] = back[per:]


def back_rows(at, stats, serving, near, far, aligned, own, other, bits, edges):
    depth, cols = own.shape
    per = near.shape[0]
    sends = [shape((per, edges[p + 1] - edges[p]), BF16) for p in range(3)]
    keeps = [shape((per, edges[p + 1] - edges[p]), F32) for p in range(3)]
    got = pl.pallas_call(
        lambda *refs: back_kernel(bits, edges, len(stats), *refs),
        out_shape=[shape((2 * per, cols), BF16)] * 2 + sends + keeps,
        in_specs=[SMEM] + [VMEM] * (len(stats) + 6),
        out_specs=[VMEM] * 8,
        compiler_params=params(24),
        cost_estimate=cost(8 * per * depth * cols, 2 * cols * depth * 2, 4 * per * cols),
        name="back_rows",
    )(at, *stats, serving, near, far, aligned, own, other)
    return got[0], got[1], got[2:5], got[5:8]


def head_kernel(r0, r1, r2, r3, mine_ref, theirs_ref, out_ref):
    rows = jnp.concatenate([r0[...], r1[...], r2[...], r3[...]])
    grads = jnp.concatenate([mine_ref[...], theirs_ref[...]])
    out_ref[...] = lax.dot_general(
        rows, grads, (((0,), (0,)), ((), ())), preferred_element_type=F32
    ).astype(BF16)


def head_gradient(rows, mine, theirs):
    per, depth = rows[0].shape
    cols = mine.shape[1]
    tile = 512 if depth % 512 == 0 else depth
    whole = pl.BlockSpec((2 * per, cols), lambda i: (0, 0))
    slab = pl.BlockSpec((per, tile), lambda i: (0, i))
    return pl.pallas_call(
        head_kernel,
        grid=(depth // tile,),
        out_shape=shape((depth, cols), BF16),
        in_specs=[slab] * 4 + [whole] * 2,
        out_specs=pl.BlockSpec((tile, cols), lambda i: (i, 0)),
        compiler_params=params(12),
        cost_estimate=cost(8 * per * depth * cols, (4 * per + cols) * depth * 2),
        name="head_gradient",
    )(*rows, mine, theirs)


def body(hidden, token_ids, serving, head_weight, teacher_logits):
    groups = lax.axis_size("grp")
    shards = lax.axis_size("vocab")
    me_g = lax.axis_index("grp")
    me_v = lax.axis_index("vocab")
    per, depth = hidden.shape
    cols = head_weight.shape[1]
    owned = per // shards
    CORE, X = shards, 2 * shards
    Y, W = 1, 2
    count = groups * shards

    def swap(value, mask):
        return lax.ppermute(value, AXES, [(i, i ^ mask) for i in range(count)])

    def tie(*values):
        return lax.optimization_barrier(values)

    def ints(*values):
        return jnp.stack([jnp.asarray(v, jnp.int32) for v in values])

    quarter_rows = per // 4
    quarter = me_v & 3
    starts = [(quarter ^ k) * quarter_rows for k in range(4)]
    x0 = swap(lax.dynamic_slice_in_dim(hidden, starts[0], quarter_rows, 0), X)
    other_weight = swap(head_weight, CORE)
    second = lax.dynamic_slice_in_dim(hidden, starts[3], quarter_rows, 0)
    chip = me_g >> 1
    kept = lax.dynamic_slice_in_dim(teacher_logits, 2 * chip, 2, 1).swapaxes(0, 1)
    gone = lax.dynamic_slice_in_dim(teacher_logits, 2 * (chip ^ 1), 2, 1).swapaxes(0, 1)
    taught = taught_stats(kept, gone)
    taught_core = swap(taught, CORE)
    x0, second, near_in = tie(x0, second, hidden)
    x1 = swap(x0, Y)
    x2 = swap(x0, W)
    x3 = swap(second, X)
    logits0, stats0, own_weight = near_logits(near_in, head_weight, other_weight)
    x3, gone, logits0 = tie(x3, gone, logits0)
    logits1, x_rows, stats = far_logits(
        ints(*starts),
        [x0, x1, x2, x3],
        own_weight,
        other_weight,
        stats0,
        taught,
        taught_core,
        token_ids.reshape(1, per),
    )

    served = serving.reshape(groups, 1, per)
    taught_x = swap(gone, X)
    arrived = [kept, swap(kept, CORE), taught_x, swap(taught_x, CORE)]
    aligned = teacher_rows(ints(me_g, me_g & 1), served, arrived)

    held = [logits0, logits1]
    stats = merge([stats, swap(stats, X), swap(stats, Y), swap(stats, X + Y)], (0, 1, 0, 1), held)
    core_rows = swap(hidden, CORE)
    stats, x_sent = tie(stats, x_rows)
    core_x_rows = swap(x_sent, CORE)
    mask = W
    while True:
        masks = [mask, 2 * mask, 3 * mask] if 2 * mask < shards else [mask]
        parts = [stats] + [swap(stats, m) for m in masks]
        mask *= 4
        if mask >= shards:
            break
        stats = merge(parts, (0,) * len(parts), held)

    bits = shards.bit_length() - 1
    masks = {0: X}
    for b in range(bits):
        masks[1 + b] = shards >> (1 + b)
    ydim, wdim = bits, bits - 1
    third = depth // 128 // 3 * 128
    edges = (0, third, 2 * third, depth)
    orders = [(0, ydim, wdim), (ydim, wdim, 0), (wdim, 0, ydim)]
    low = owned.bit_length() - 1
    row_bit = {0: low + bits, ydim: low, wdim: low + 1}
    first_bits = tuple(row_bit[order[0]] for order in orders)
    at = ints(
        me_v * owned, (me_g * shards + me_v) * cols, ((me_g ^ 1) * shards + me_v) * cols, me_g
    )
    gown, gother, sents, keeps = back_rows(
        at, parts, served, logits0, logits1, aligned, own_weight, other_weight, first_bits, edges
    )
    gots = [swap(sents[p], masks[orders[p][0]]) for p in range(3)]
    theirs = swap(gother, CORE)
    grad_head = head_gradient([hidden, x_rows, core_rows, core_x_rows], gown, theirs)
    grad_head, *gots = tie(grad_head, *gots)

    def folded(value, p):
        dims = [2] * (1 + bits)
        dims[orders[p][0]] = 1
        return value.reshape(*dims, owned, value.shape[-1])

    terms = [[folded(keeps[p], p), folded(gots[p], p)] for p in range(3)]
    for stage in (1, 2):
        sents = [
            sum(lax.index_in_dim(t, 1, orders[p][stage]).astype(F32) for t in terms[p]).astype(BF16)
            for p in range(3)
        ]
        gots = [swap(sents[p], masks[orders[p][stage]]) for p in range(3)]
        for p in range(3):
            terms[p] = [lax.index_in_dim(t, 0, orders[p][stage]) for t in terms[p]] + [gots[p]]
    total = jnp.concatenate([sum(t.astype(F32) for t in ts) for ts in terms], axis=-1)
    for dim in range(1, wdim):
        got = swap(lax.index_in_dim(total, 1, dim).astype(BF16), masks[dim])
        total = lax.index_in_dim(total, 0, dim) + got.astype(F32)
    return (total.reshape(owned, depth), grad_head)


def solution(mesh):
    placed = (P("grp", None), P("grp"), P(), P(None, ("grp", "vocab")), P("grp", None, "vocab"))
    return jax.shard_map(
        body,
        mesh=mesh,
        in_specs=placed,
        out_specs=(P(("grp", "vocab"), None), P(None, ("grp", "vocab"))),
        check_vma=False,
    )
```

time: 97.1 us -> 88.5 us (0.911)
  waiting for transfers between devices: 26.9 us -> 22.3 us
  Pallas kernels: 26.8 us -> 23.3 us
  local copies, waits for them, and re-layouts: 12.1 us -> 10.7 us
    ppermute x27 -> x28, waiting for transfers between devices: 26.9 us -> 22.3 us  [swap(): return lax.ppermute(value, AXES, [(i, i ^ mask) for i in range(count)])]
    pallas_call x4, Pallas kernels: 16 us -> 12.4 us  [the longest x1 6.18 us: back_rows(): pl.pallas_call(lambda *refs: back_kernel(bits, edges, len(stats), *refs),...]
    unnamed x20 -> x22, local copies, waits for them, and re-layouts: 8.47 us -> 7.18 us
    ppermute x27 -> x28, starting transfers between devices: 28.6 us -> 29.5 us  [swap(): return lax.ppermute(value, AXES, [(i, i ^ mask) for i in range(count)])]
  transfers between devices with their start and end apart: 27 -> 28, of which waited for: 13 -> 13; matrix products, arithmetic and copies ran while one was open for 4% -> 5% of each run, Pallas kernels for 28% -> 27%
where the time goes in v5:
time: 88.5 us; the launch traced here: 87.9 us
  starting transfers between devices  29.5 us (33%)
  Pallas kernels  23.3 us (26%)
  waiting for transfers between devices  22.3 us (25%)
  local copies, waits for them, and re-layouts  10.7 us (12%)
  other arithmetic  1.3 us (1%)
    ppermute x28, starting transfers between devices, swap(): return lax.ppermute(value, AXES, [(i, i ^ mask) for i in range(count)])  29.5 us
    ppermute x28, waiting for transfers between devices, swap(): return lax.ppermute(value, AXES, [(i, i ^ mask) for i in range(count)])  22.3 us
    pallas_call x1, Pallas kernels, head_gradient(): pl.pallas_call(head_kernel, grid=(depth // tile,), out_shape=shape((depth...  7.22 us
    unnamed x22, local copies, waits for them, and re-layouts  7.18 us
    pallas_call x1, Pallas kernels, back_rows(): pl.pallas_call(lambda *refs: back_kernel(bits, edges, len(stats), *refs),...  6.18 us
    pallas_call x1, Pallas kernels, near_logits(): pl.pallas_call(lambda *refs: near_kernel(splits, *refs), out_shape=(shape...  4.02 us
    pallas_call x1, Pallas kernels, far_logits(): pl.pallas_call(far_kernel, out_shape=(shape((per, 2 * cols), F32), shape(...  3.73 us
    pallas_call x1, Pallas kernels, teacher_rows(): pl.pallas_call(teacher_kernel, out_shape=shape((2, per, 2 * cols), BF16),...  1.78 us
  transfers between devices with their start and end apart: 28, of which 13 were waited for; matrix products, arithmetic and copies ran while one was open for 5% of the time, Pallas kernels for 27%

profile of v5, /device:TPU:0, one launch (start us, length us, event | category | flops | bytes accessed | tf_op | source)
XLA Modules:
  0.0 87.9 jit_solution(13272435628379200406)
XLA Ops:
  0.6 0.0 copy-start.2
  0.6 0.5 collective-permute-start.4
  1.2 1.8 %constant_dynamic-slice_fusion.2 = (bf16[32,3584]{1,0:T(8,128)(2,1)}, bf16[32,3584]{1,0:T(8,128)(2,1)S(1)}) fusion(bf16[128,3584]{1,0:T(8,128)(2,1)} %r0.1, s32[]{:T(128)S(6)} %select_n.13, s32[]{:T(128)S(6)} %select_n.12), kind=kLoop, calls=%fused_computation.31 | loop fusion | bytes 917512 | tf_op jit(solution)/shard_map/dynamic_slice | solution.py:330
  2.9 2.6 %collective-permute-start = (bf16[32,3584]{1,0:T(8,128)(2,1)S(1)}, bf16[32,3584]{1,0:T(8,128)(2,1)S(1)}, u32[]{:S(2)}, u32[]{:S(2)}) collective-permute-start(bf16[32,3584]{1,0:T(8,128)(2,1)S(1)} %get-tuple-element.55), channel_id=1, source_target_pairs={{0,16},{1,17},{2,18},{3,19},{4,20},{5,21},{6,22},{7,23},{8,24},{9,... | collective-permute-start | bytes 688136 | tf_op jit(solution)/shard_map/ppermute | solution.py:317
  5.5 0.1 collective-permute-start.15
  5.7 6.0 %collective-permute-done.x0 = bf16[32,3584]{1,0:T(8,128)(2,1)S(1)} collective-permute-done((bf16[32,3584]{1,0:T(8,128)(2,1)S(1)}, bf16[32,3584]{1,0:T(8,128)(2,1)S(1)}, u32[]{:S(2)}, u32[]{:S(2)}) %collective-permute-start) | collective-permute-done | bytes 229408 | tf_op jit(solution)/shard_map/ppermute | solution.py:317
  11.7 1.8 %collective-permute-start.1 = (bf16[32,3584]{1,0:T(8,128)(2,1)S(1)}, bf16[32,3584]{1,0:T(8,128)(2,1)S(1)}, u32[]{:S(2)}, u32[]{:S(2)}) collective-permute-start(bf16[32,3584]{1,0:T(8,128)(2,1)S(1)} %collective-permute-done.x0), channel_id=1, source_target_pairs={{0,1},{1,0},{2,3},{3,2},{4,5},{5,4},{6,7},{7,6},{8,9},{9,8},{10,11... | collective-permute-start | bytes 688136 | tf_op jit(solution)/shard_map/ppermute | solution.py:317
  13.5 1.6 %collective-permute-start.2 = (bf16[32,3584]{1,0:T(8,128)(2,1)S(1)}, bf16[32,3584]{1,0:T(8,128)(2,1)}, u32[]{:S(2)}, u32[]{:S(2)}) collective-permute-start(bf16[32,3584]{1,0:T(8,128)(2,1)S(1)} %collective-permute-done.x0), channel_id=1, source_target_pairs={{0,2},{1,3},{2,0},{3,1},{4,6},{5,7},{6,4},{7,5},{8,10},{9,11},{10,... | collective-permute-start | bytes 688136 | tf_op jit(solution)/shard_map/ppermute | solution.py:317
  15.1 1.5 %collective-permute-start.3 = (bf16[32,3584]{1,0:T(8,128)(2,1)}, bf16[32,3584]{1,0:T(8,128)(2,1)}, u32[]{:S(2)}, u32[]{:S(2)}) collective-permute-start(bf16[32,3584]{1,0:T(8,128)(2,1)} %get-tuple-element.29), channel_id=1, source_target_pairs={{0,16},{1,17},{2,18},{3,19},{4,20},{5,21},{6,22},{7,23},{8,24},{9,... | collective-permute-start | bytes 688136 | tf_op jit(solution)/shard_map/ppermute | solution.py:317
  16.5 1.7 %constant_dynamic-slice_fusion = (bf16[128,2,512]{2,1,0:T(2,128)(2,1)S(1)}, bf16[128,2,512]{2,1,0:T(2,128)(2,1)S(1)}) fusion(bf16[128,4,512]{2,1,0:T(4,128)(2,1)} %param.9, s32[]{:T(128)S(6)} %select_n.15, s32[]{:T(128)S(6)} %select_n.14), kind=kLoop, calls=%fused_computation.29 | loop fusion | bytes 1048584 | tf_op jit(solution)/shard_map/dynamic_slice | solution.py:332
  18.4 0.4 taught_stats.1.taught_ref
  18.8 0.1 pad_add_fusion.1.spots_ref
  18.9 0.0 collective-permute-start.5
  18.9 0.0 copy-start.3
  18.9 2.0 %copy-done.3 = bf16[3584,512]{1,0:T(8,128)(2,1)S(1)} copy-done((bf16[3584,512]{1,0:T(8,128)(2,1)S(1)}, bf16[3584,512]{1,0:T(8,128)(2,1)}, u32[]{:S(2)}) %copy-start.3) | copy-done | bytes 3670040
  20.9 4.0 %near_logits.1 = (f32[128,1024]{1,0:T(8,128)S(1)}, f32[8,128]{1,0:T(8,128)S(1)}, bf16[3584,512]{1,0:T(8,128)(2,1)S(1)}) custom-call(bf16[128,3584]{1,0:T(8,128)(2,1)S(1)} %copy-done.2, bf16[3584,512]{1,0:T(8,128)(2,1)S(1)} %copy-done.3, bf16[3584,512]{1,0:T(8,128)(2,1)} %collective-permute-done.4.refs_2_.other_ref.refs_10_), custom_call_target="tpu_custom_call" | custom-call | flops 939524096 | bytes 8257536 | tf_op jit(solution)/shard_map/near_logits/pallas_call | solution.py:123
  25.0 0.0 copy-start
  25.0 0.0 collective-permute-done.3.x3
  25.0 0.6 collective-permute-start.13
  25.6 0.0 collective-permute-done.1.x1
  25.6 1.1 %copy-done.6 = bf16[32,3584]{1,0:T(8,128)(2,1)} copy-done((bf16[32,3584]{1,0:T(8,128)(2,1)}, bf16[32,3584]{1,0:T(8,128)(2,1)S(1)}, u32[]{:S(2)}) %copy-start.6) | copy-done | bytes 229400
  26.8 0.0 collective-permute-done.2.x2
  26.8 0.9 %copy-done.5 = bf16[32,3584]{1,0:T(8,128)(2,1)S(1)} copy-done((bf16[32,3584]{1,0:T(8,128)(2,1)S(1)}, bf16[32,3584]{1,0:T(8,128)(2,1)}, u32[]{:S(2)}) %copy-start.5) | copy-done | bytes 229400
  27.7 0.9 %copy-done.7 = bf16[32,3584]{1,0:T(8,128)(2,1)S(1)} copy-done((bf16[32,3584]{1,0:T(8,128)(2,1)S(1)}, bf16[32,3584]{1,0:T(8,128)(2,1)}, u32[]{:S(2)}) %copy-start.7) | copy-done | bytes 229400
  28.6 3.7 %far_logits.1 = (f32[128,1024]{1,0:T(8,128)S(1)}, bf16[128,3584]{1,0:T(8,128)(2,1)}, f32[2,8,128]{2,1,0:T(8,128)S(1)}) custom-call(s32[4]{0:T(128)S(1)} %pad_add_fusion.1.spots_ref, bf16[32,3584]{1,0:T(8,128)(2,1)S(1)} %copy-done.5, bf16[32,3584]{1,0:T(8,128)(2,1)S(1)} %copy-done.7, bf16[32,3584]{1,0:T(8,128)(2,1)} %collective-permute-done.2.x2, ...), custom_call_target="tpu_custom_call" | custom-call | flops 939524096 | bytes 8257536 | tf_op jit(solution)/shard_map/far_logits/pallas_call | solution.py:161
  32.4 1.1 %collective-permute-start.6 = (f32[2,8,128]{2,1,0:T(8,128)S(1)}, f32[2,8,128]{2,1,0:T(8,128)S(1)}, u32[]{:S(2)}, u32[]{:S(2)}) collective-permute-start(f32[2,8,128]{2,1,0:T(8,128)S(1)} %get-tuple-element.35.refs_0_), channel_id=1, source_target_pairs={{0,16},{1,17},{2,18},{3,19},{4,20},{5,21},{6,22},{7,23},{8,24},{9,... | collective-permute-start | bytes 24584 | tf_op jit(solution)/shard_map/ppermute | solution.py:317
  33.5 0.5 collective-permute-start.7
  34.0 1.9 %collective-permute-start.8 = (f32[2,8,128]{2,1,0:T(8,128)S(1)}, f32[2,8,128]{2,1,0:T(8,128)S(1)}, u32[]{:S(2)}, u32[]{:S(2)}) collective-permute-start(f32[2,8,128]{2,1,0:T(8,128)S(1)} %get-tuple-element.35.refs_0_), channel_id=1, source_target_pairs={{0,17},{1,16},{2,19},{3,18},{4,21},{5,20},{6,23},{7,22},{8,25},{9,... | collective-permute-start | bytes 24584 | tf_op jit(solution)/shard_map/ppermute | solution.py:317
  35.9 0.2 collective-permute-done.6.refs_1_
  36.1 1.1 %collective-permute-done.7.refs_2_ = f32[2,8,128]{2,1,0:T(8,128)S(1)} collective-permute-done((f32[2,8,128]{2,1,0:T(8,128)S(1)}, f32[2,8,128]{2,1,0:T(8,128)S(1)}, u32[]{:S(2)}, u32[]{:S(2)}) %collective-permute-start.7) | collective-permute-done | bytes 8224 | tf_op jit(solution)/shard_map/ppermute | solution.py:317
  37.1 1.4 %collective-permute-done.8.refs_3_ = f32[2,8,128]{2,1,0:T(8,128)S(1)} collective-permute-done((f32[2,8,128]{2,1,0:T(8,128)S(1)}, f32[2,8,128]{2,1,0:T(8,128)S(1)}, u32[]{:S(2)}, u32[]{:S(2)}) %collective-permute-start.8) | collective-permute-done | bytes 8224 | tf_op jit(solution)/shard_map/ppermute | solution.py:317
  38.5 0.1 collective-permute-start.16
  38.6 0.5 collective-permute-start.12
  39.1 0.1 collective-permute-start.14
  39.2 0.1 pad_add_fusion.2.at_ref
  39.3 0.1 pad_add_fusion.refs_0_
  39.4 2.6 %collective-permute-start.10 = (f32[2,8,128]{2,1,0:T(8,128)S(1)}, f32[2,8,128]{2,1,0:T(8,128)S(1)}, u32[]{:S(2)}, u32[]{:S(2)}) collective-permute-start(f32[2,8,128]{2,1,0:T(8,128)S(1)} %merge_stats.1.refs_1_), channel_id=1, source_target_pairs={{0,4},{1,5},{2,6},{3,7},{4,0},{5,1},{6,2},{7,3},{8,12},{9,13},{10,... | collective-permute-start | bytes 24584 | tf_op jit(solution)/shard_map/ppermute | solution.py:317
  41.9 2.1 %collective-permute-start.11 = (f32[2,8,128]{2,1,0:T(8,128)S(1)}, f32[2,8,128]{2,1,0:T(8,128)S(1)}, u32[]{:S(2)}, u32[]{:S(2)}) collective-permute-start(f32[2,8,128]{2,1,0:T(8,128)S(1)} %merge_stats.1.refs_1_), channel_id=1, source_target_pairs={{0,6},{1,7},{2,4},{3,5},{4,2},{5,3},{6,0},{7,1},{8,14},{9,15},{10,... | collective-permute-start | bytes 24584 | tf_op jit(solution)/shard_map/ppermute | solution.py:317
  44.1 0.7 collective-permute-start.9
  44.8 1.8 %teacher_rows.1.refs_8_ = bf16[2,128,1024]{2,1,0:T(8,128)(2,1)S(1)} custom-call(s32[2]{0:T(128)S(1)} %pad_add_fusion.2.at_ref, s32[4,1,128]{2,1,0:T(1,128)S(1)} %bitcast.47, bf16[2,128,512]{2,1,0:T(8,128)(2,1)S(1)} %bitcast.38, bf16[2,128,512]{2,1,0:T(8,128)(2,1)} %collective-permute-done.12.a1, bf16[2,128,512]{2,1,0:T(8,128)(2,1)} %collective-permute-done.13.a2, ...), custom_call_target="tpu_custom_call" | custom-call | flops 268435456 | bytes 1572864 | tf_op jit(solution)/shard_map/teacher_rows/pallas_call | solution.py:80
  46.6 0.8 collective-permute-done.11.refs_4_
  47.4 0.4 collective-permute-done.9.refs_2_
  47.8 2.0 %copy-done.1 = bf16[3584,512]{1,0:T(8,128)(2,1)S(1)} copy-done((bf16[3584,512]{1,0:T(8,128)(2,1)S(1)}, bf16[3584,512]{1,0:T(8,128)(2,1)}, u32[]{:S(2)}) %copy-start.1) | copy-done | bytes 3670040
  49.8 6.2 %back_rows.1 = (bf16[256,512]{1,0:T(8,128)(2,1)S(1)}, bf16[256,512]{1,0:T(8,128)(2,1)S(1)}, bf16[128,1152]{1,0:T(8,128)(2,1)S(1)}, bf16[128,1152]{1,0:T(8,128)(2...) custom-call(s32[4]{0:T(128)S(1)} %pad_add_fusion.refs_0_, ...), custom_call_target="tpu_custom_call" | custom-call | flops 1879048192 | bytes 7340032 | tf_op jit(solution)/shard_map/back_rows/pallas_call | solution.py:266
  56.0 0.1 collective-permute-start.17
  56.1 0.7 collective-permute-start.20
  56.8 1.0 %collective-permute-start.18 = (bf16[128,1152]{1,0:T(8,128)(2,1)S(1)}, bf16[128,1152]{1,0:T(8,128)(2,1)S(1)}, u32[]{:S(2)}, u32[]{:S(2)}) collective-permute-start(bf16[128,1152]{1,0:T(8,128)(2,1)S(1)} %get-tuple-element.45), channel_id=1, source_target_pairs={{0,16},{1,17},{2,18},{3,19},{4,20},{5,21},{6,22},{7,23},{8,24},{9,... | collective-permute-start | bytes 884744 | tf_op jit(solution)/shard_map/ppermute | solution.py:317
  57.8 1.5 %collective-permute-start.19 = (bf16[128,1152]{1,0:T(8,128)(2,1)S(1)}, bf16[128,1152]{1,0:T(8,128)(2,1)S(1)}, u32[]{:S(2)}, u32[]{:S(2)}) collective-permute-start(bf16[128,1152]{1,0:T(8,128)(2,1)S(1)} %get-tuple-element.46), channel_id=1, source_target_pairs={{0,1},{1,0},{2,3},{3,2},{4,5},{5,4},{6,7},{7,6},{8,9},{9,8},{10,11... | collective-permute-start | bytes 884744 | tf_op jit(solution)/shard_map/ppermute | solution.py:317
  59.3 7.2 %head_gradient.1 = bf16[3584,512]{1,0:T(8,128)(2,1)} custom-call(bf16[128,3584]{1,0:T(8,128)(2,1)S(1)} %copy-done.2, bf16[128,3584]{1,0:T(8,128)(2,1)} %get-tuple-element.42.r1, bf16[128,3584]{1,0:T(8,128)(2,1)S(1)} %collective-permute-done.15.r2, bf16[128,3584]{1,0:T(8,128)(2,1)} %collective-permute-done.16.r3, ...), custom_call_target="tpu_custom_call" | custom-call | flops 1879048192 | bytes 7340032 | tf_op jit(solution)/shard_map/head_gradient/pallas_call | solution.py:292
  66.5 0.1 collective-permute-done.19
  66.7 1.6 %collective-permute-start.21 = (bf16[1,2,2,1,16,1152]{5,4,3,2,1,0:T(8,128)(2,1)S(1)}, bf16[1,2,2,1,16,1152]{5,4,3,2,1,0:T(8,128)(2,1)S(1)}, u32[]{:S(2)}, u32[]{:S(2)}) collective-permute-start(bf16[1,2,2,1,16,1152]{5,4,3,2,1,0:T(8,128)(2,1)S(1)} %fusion.1), channel_id=1, source_target_pairs={{0,1},{1,0},{2,3},{3,2},{4,5},{5,4},{6,7},{7,6},{8,9},{9,8},{10,11... | collective-permute-start | bytes 442376 | tf_op jit(solution)/shard_map/ppermute | solution.py:317
  68.2 1.4 %collective-permute-start.23 = (bf16[2,2,1,1,16,1152]{5,4,3,2,1,0:T(8,128)(2,1)S(1)}, bf16[2,2,1,1,16,1152]{5,4,3,2,1,0:T(8,128)(2,1)S(1)}, u32[]{:S(2)}, u32[]{:S(2)}) collective-permute-start(bf16[2,2,1,1,16,1152]{5,4,3,2,1,0:T(8,128)(2,1)S(1)} %fusion), channel_id=1, source_target_pairs={{0,2},{1,3},{2,0},{3,1},{4,6},{5,7},{6,4},{7,5},{8,10},{9,11},{10,... | collective-permute-start | bytes 442376 | tf_op jit(solution)/shard_map/ppermute | solution.py:317
  69.7 1.1 %collective-permute-start.25 = (bf16[1,2,1,2,16,1280]{5,4,3,2,1,0:T(8,128)(2,1)S(1)}, bf16[1,2,1,2,16,1280]{5,4,3,2,1,0:T(8,128)(2,1)S(1)}, u32[]{:S(2)}, u32[]{:S(2)}) collective-permute-start(bf16[1,2,1,2,16,1280]{5,4,3,2,1,0:T(8,128)(2,1)S(1)} %bitcast.60), channel_id=1, source_target_pairs={{0,16},{1,17},{2,18},{3,19},{4,20},{5,21},{6,22},{7,23},{8,24},{9,... | collective-permute-start | bytes 491528 | tf_op jit(solution)/shard_map/ppermute | solution.py:317
  70.8 1.2 %collective-permute-done.21 = bf16[1,2,2,1,16,1152]{5,4,3,2,1,0:T(8,128)(2,1)S(1)} collective-permute-done((bf16[1,2,2,1,16,1152]{5,4,3,2,1,0:T(8,128)(2,1)S(1)}, bf16[1,2,2,1,16,1152]{5,4,3,2,1,0:T(8,128)(2,1)S(1)}, u32[]{:S(2)}, u32[]{:S(2)}) %collective-permute-start.21) | collective-permute-done | bytes 147488 | tf_op jit(solution)/shard_map/ppermute | solution.py:317
  72.1 1.4 %collective-permute-start.22 = (bf16[1,2,1,1,16,1152]{5,4,3,2,1,0:T(8,128)(2,1)S(1)}, bf16[1,2,1,1,16,1152]{5,4,3,2,1,0:T(8,128)(2,1)S(1)}, u32[]{:S(2)}, u32[]{:S(2)}) collective-permute-start(bf16[1,2,1,1,16,1152]{5,4,3,2,1,0:T(8,128)(2,1)S(1)} %fusion.12), channel_id=1, source_target_pairs={{0,2},{1,3},{2,0},{3,1},{4,6},{5,7},{6,4},{7,5},{8,10},{9,11},{10,... | collective-permute-start | bytes 221192 | tf_op jit(solution)/shard_map/ppermute | solution.py:317
  73.5 1.1 %collective-permute-start.24 = (bf16[1,2,1,1,16,1152]{5,4,3,2,1,0:T(8,128)(2,1)S(1)}, bf16[1,2,1,1,16,1152]{5,4,3,2,1,0:T(8,128)(2,1)S(1)}, u32[]{:S(2)}, u32[]{:S(2)}) collective-permute-start(bf16[1,2,1,1,16,1152]{5,4,3,2,1,0:T(8,128)(2,1)S(1)} %fusion.8), channel_id=1, source_target_pairs={{0,16},{1,17},{2,18},{3,19},{4,20},{5,21},{6,22},{7,23},{8,24},{9,... | collective-permute-start | bytes 221192 | tf_op jit(solution)/shard_map/ppermute | solution.py:317
  74.6 1.0 %collective-permute-done.25 = bf16[1,2,1,2,16,1280]{5,4,3,2,1,0:T(8,128)(2,1)S(1)} collective-permute-done((bf16[1,2,1,2,16,1280]{5,4,3,2,1,0:T(8,128)(2,1)S(1)}, bf16[1,2,1,2,16,1280]{5,4,3,2,1,0:T(8,128)(2,1)S(1)}, u32[]{:S(2)}, u32[]{:S(2)}) %collective-permute-start.25) | collective-permute-done | bytes 163872 | tf_op jit(solution)/shard_map/ppermute | solution.py:317
  75.7 0.5 collective-permute-start.26
  76.2 0.3 collective-permute-done.22
  76.5 1.4 %collective-permute-done.24 = bf16[1,2,1,1,16,1152]{5,4,3,2,1,0:T(8,128)(2,1)S(1)} collective-permute-done((bf16[1,2,1,1,16,1152]{5,4,3,2,1,0:T(8,128)(2,1)S(1)}, bf16[1,2,1,1,16,1152]{5,4,3,2,1,0:T(8,128)(2,1)S(1)}, u32[]{:S(2)}, u32[]{:S(2)}) %collective-permute-start.24) | collective-permute-done | bytes 73760 | tf_op jit(solution)/shard_map/ppermute | solution.py:317
  78.0 2.2 %collective-permute-done.26 = bf16[1,2,1,1,16,1280]{5,4,3,2,1,0:T(8,128)(2,1)S(1)} collective-permute-done((bf16[1,2,1,1,16,1280]{5,4,3,2,1,0:T(8,128)(2,1)S(1)}, bf16[1,2,1,1,16,1280]{5,4,3,2,1,0:T(8,128)(2,1)S(1)}, u32[]{:S(2)}, u32[]{:S(2)}) %collective-permute-start.26) | collective-permute-done | bytes 81952 | tf_op jit(solution)/shard_map/ppermute | solution.py:317
  80.3 0.7 collective-permute-start.27
  81.0 6.2 %collective-permute-done.27 = bf16[1,1,1,1,16,3584]{5,4,3,2,1,0:T(8,128)(2,1)S(1)} collective-permute-done((bf16[1,1,1,1,16,3584]{5,4,3,2,1,0:T(8,128)(2,1)S(1)}, bf16[1,1,1,1,16,3584]{5,4,3,2,1,0:T(8,128)(2,1)S(1)}, u32[]{:S(2)}, u32[]{:S(2)}) %collective-permute-start.27) | collective-permute-done | bytes 114720 | tf_op jit(solution)/shard_map/ppermute | solution.py:317
  87.2 0.7 fusion.2
  (39 shorter events, 0.5 us)
Async XLA Ops:
  0.6 18.3 %copy-start.2 = (bf16[128,3584]{1,0:T(8,128)(2,1)S(1)}, bf16[128,3584]{1,0:T(8,128)(2,1)}, u32[]{:S(2)}) copy-start(bf16[128,3584]{1,0:T(8,128)(2,1)} %r0.1) | copy-start | bytes 2752516
  0.6 18.2 %collective-permute-start.4 = (bf16[3584,512]{1,0:T(8,128)(2,1)}, bf16[3584,512]{1,0:T(8,128)(2,1)}, u32[]{:S(2)}, u32[]{:S(2)}) collective-permute-start(bf16[3584,512]{1,0:T(8,128)(2,1)} %refs_1_.1), channel_id=1, source_target_pairs={{0,8},{1,9},{2,10},{3,11},{4,12},{5,13},{6,14},{7,15},{8,0},{9,1},... | collective-permute-start | bytes 11010056 | tf_op jit(solution)/shard_map/ppermute | solution.py:317
  2.9 8.8 %collective-permute-start = (bf16[32,3584]{1,0:T(8,128)(2,1)S(1)}, bf16[32,3584]{1,0:T(8,128)(2,1)S(1)}, u32[]{:S(2)}, u32[]{:S(2)}) collective-permute-start(bf16[32,3584]{1,0:T(8,128)(2,1)S(1)} %get-tuple-element.55), channel_id=1, source_target_pairs={{0,16},{1,17},{2,18},{3,19},{4,20},{5,21},{6,22},{7,23},{8,24},{9,... | collective-permute-start | bytes 688136 | tf_op jit(solution)/shard_map/ppermute | solution.py:317
  5.5 52.3 %collective-permute-start.15 = (bf16[128,3584]{1,0:T(8,128)(2,1)}, bf16[128,3584]{1,0:T(8,128)(2,1)S(1)}, u32[]{:S(2)}, u32[]{:S(2)}) collective-permute-start(bf16[128,3584]{1,0:T(8,128)(2,1)} %r0.1), channel_id=1, source_target_pairs={{0,8},{1,9},{2,10},{3,11},{4,12},{5,13},{6,14},{7,15},{8,0},{9,1},... | collective-permute-start | bytes 2752520 | tf_op jit(solution)/shard_map/ppermute | solution.py:317
  11.7 13.3 %copy-start.4 = (bf16[32,3584]{1,0:T(8,128)(2,1)}, bf16[32,3584]{1,0:T(8,128)(2,1)S(1)}, u32[]{:S(2)}) copy-start(bf16[32,3584]{1,0:T(8,128)(2,1)S(1)} %collective-permute-done.x0) | copy-start | bytes 688132
  11.7 13.9 %collective-permute-start.1 = (bf16[32,3584]{1,0:T(8,128)(2,1)S(1)}, bf16[32,3584]{1,0:T(8,128)(2,1)S(1)}, u32[]{:S(2)}, u32[]{:S(2)}) collective-permute-start(bf16[32,3584]{1,0:T(8,128)(2,1)S(1)} %collective-permute-done.x0), channel_id=1, source_target_pairs={{0,1},{1,0},{2,3},{3,2},{4,5},{5,4},{6,7},{7,6},{8,9},{9,8},{10,11... | collective-permute-start | bytes 688136 | tf_op jit(solution)/shard_map/ppermute | solution.py:317
  13.5 13.3 %collective-permute-start.2 = (bf16[32,3584]{1,0:T(8,128)(2,1)S(1)}, bf16[32,3584]{1,0:T(8,128)(2,1)}, u32[]{:S(2)}, u32[]{:S(2)}) collective-permute-start(bf16[32,3584]{1,0:T(8,128)(2,1)S(1)} %collective-permute-done.x0), channel_id=1, source_target_pairs={{0,2},{1,3},{2,0},{3,1},{4,6},{5,7},{6,4},{7,5},{8,10},{9,11},{10,... | collective-permute-start | bytes 688136 | tf_op jit(solution)/shard_map/ppermute | solution.py:317
  15.1 9.9 %collective-permute-start.3 = (bf16[32,3584]{1,0:T(8,128)(2,1)}, bf16[32,3584]{1,0:T(8,128)(2,1)}, u32[]{:S(2)}, u32[]{:S(2)}) collective-permute-start(bf16[32,3584]{1,0:T(8,128)(2,1)} %get-tuple-element.29), channel_id=1, source_target_pairs={{0,16},{1,17},{2,18},{3,19},{4,20},{5,21},{6,22},{7,23},{8,24},{9,... | collective-permute-start | bytes 688136 | tf_op jit(solution)/shard_map/ppermute | solution.py:317
  18.7 8.0 %copy-start.9 = (s32[128]{0:T(128)S(1)}, s32[128]{0:T(128)}, u32[]{:S(2)}) copy-start(s32[128]{0:T(128)} %param.6) | copy-start | bytes 1540
  18.9 6.7 %collective-permute-start.5 = (f32[8,128]{1,0:T(8,128)S(1)}, f32[8,128]{1,0:T(8,128)S(1)}, u32[]{:S(2)}, u32[]{:S(2)}) collective-permute-start(f32[8,128]{1,0:T(8,128)S(1)} %taught_stats.1.taught_ref), channel_id=1, source_target_pairs={{0,8},{1,9},{2,10},{3,11},{4,12},{5,13},{6,14},{7,15},{8,0},{9,1},... | collective-permute-start | bytes 12296 | tf_op jit(solution)/shard_map/ppermute | solution.py:317
  18.9 2.0 %copy-start.3 = (bf16[3584,512]{1,0:T(8,128)(2,1)S(1)}, bf16[3584,512]{1,0:T(8,128)(2,1)}, u32[]{:S(2)}) copy-start(bf16[3584,512]{1,0:T(8,128)(2,1)} %refs_1_.1) | copy-start | bytes 11010052
  25.0 7.4 %copy-start = (bf16[3584,512]{1,0:T(8,128)(2,1)}, bf16[3584,512]{1,0:T(8,128)(2,1)S(1)}, u32[]{:S(2)}) copy-start(bf16[3584,512]{1,0:T(8,128)(2,1)S(1)} %get-tuple-element.33.own_ref.refs_9_) | copy-start | bytes 11010052
  25.0 14.1 %collective-permute-start.13 = (bf16[2,128,512]{2,1,0:T(8,128)(2,1)S(1)}, bf16[2,128,512]{2,1,0:T(8,128)(2,1)}, u32[]{:S(2)}, u32[]{:S(2)}) collective-permute-start(bf16[2,128,512]{2,1,0:T(8,128)(2,1)S(1)} %bitcast.40), channel_id=1, source_target_pairs={{0,16},{1,17},{2,18},{3,19},{4,20},{5,21},{6,22},{7,23},{8,24},{9,... | collective-permute-start | bytes 786440 | tf_op jit(solution)/shard_map/ppermute | solution.py:317
  25.6 1.1 %copy-start.6 = (bf16[32,3584]{1,0:T(8,128)(2,1)}, bf16[32,3584]{1,0:T(8,128)(2,1)S(1)}, u32[]{:S(2)}) copy-start(bf16[32,3584]{1,0:T(8,128)(2,1)S(1)} %collective-permute-done.1.x1) | copy-start | bytes 688132
  26.8 0.9 %copy-start.5 = (bf16[32,3584]{1,0:T(8,128)(2,1)S(1)}, bf16[32,3584]{1,0:T(8,128)(2,1)}, u32[]{:S(2)}) copy-start(bf16[32,3584]{1,0:T(8,128)(2,1)} %copy-done.4) | copy-start | bytes 688132
  27.7 0.9 %copy-start.7 = (bf16[32,3584]{1,0:T(8,128)(2,1)S(1)}, bf16[32,3584]{1,0:T(8,128)(2,1)}, u32[]{:S(2)}) copy-start(bf16[32,3584]{1,0:T(8,128)(2,1)} %copy-done.6) | copy-start | bytes 688132
  28.6 16.1 %copy-start.8 = (s32[512]{0:T(512)S(1)}, s32[512]{0:T(512)}, u32[]{:S(2)}) copy-start(s32[512]{0:T(512)} %param.7) | copy-start | bytes 6148
  32.4 3.7 %collective-permute-start.6 = (f32[2,8,128]{2,1,0:T(8,128)S(1)}, f32[2,8,128]{2,1,0:T(8,128)S(1)}, u32[]{:S(2)}, u32[]{:S(2)}) collective-permute-start(f32[2,8,128]{2,1,0:T(8,128)S(1)} %get-tuple-element.35.refs_0_), channel_id=1, source_target_pairs={{0,16},{1,17},{2,18},{3,19},{4,20},{5,21},{6,22},{7,23},{8,24},{9,... | collective-permute-start | bytes 24584 | tf_op jit(solution)/shard_map/ppermute | solution.py:317
  33.5 3.7 %collective-permute-start.7 = (f32[2,8,128]{2,1,0:T(8,128)S(1)}, f32[2,8,128]{2,1,0:T(8,128)S(1)}, u32[]{:S(2)}, u32[]{:S(2)}) collective-permute-start(f32[2,8,128]{2,1,0:T(8,128)S(1)} %get-tuple-element.35.refs_0_), channel_id=1, source_target_pairs={{0,1},{1,0},{2,3},{3,2},{4,5},{5,4},{6,7},{7,6},{8,9},{9,8},{10,11... | collective-permute-start | bytes 24584 | tf_op jit(solution)/shard_map/ppermute | solution.py:317
  34.0 4.5 %collective-permute-start.8 = (f32[2,8,128]{2,1,0:T(8,128)S(1)}, f32[2,8,128]{2,1,0:T(8,128)S(1)}, u32[]{:S(2)}, u32[]{:S(2)}) collective-permute-start(f32[2,8,128]{2,1,0:T(8,128)S(1)} %get-tuple-element.35.refs_0_), channel_id=1, source_target_pairs={{0,17},{1,16},{2,19},{3,18},{4,21},{5,20},{6,23},{7,22},{8,25},{9,... | collective-permute-start | bytes 24584 | tf_op jit(solution)/shard_map/ppermute | solution.py:317
  38.5 20.8 %collective-permute-start.16 = (bf16[128,3584]{1,0:T(8,128)(2,1)}, bf16[128,3584]{1,0:T(8,128)(2,1)}, u32[]{:S(2)}, u32[]{:S(2)}) collective-permute-start(bf16[128,3584]{1,0:T(8,128)(2,1)} %get-tuple-element.42.r1), channel_id=1, source_target_pairs={{0,8},{1,9},{2,10},{3,11},{4,12},{5,13},{6,14},{7,15},{8,0},{9,1},... | collective-permute-start | bytes 2752520 | tf_op jit(solution)/shard_map/ppermute | solution.py:317
  38.6 3.3 %collective-permute-start.12 = (bf16[2,128,512]{2,1,0:T(8,128)(2,1)S(1)}, bf16[2,128,512]{2,1,0:T(8,128)(2,1)}, u32[]{:S(2)}, u32[]{:S(2)}) collective-permute-start(bf16[2,128,512]{2,1,0:T(8,128)(2,1)S(1)} %bitcast.37), channel_id=1, source_target_pairs={{0,8},{1,9},{2,10},{3,11},{4,12},{5,13},{6,14},{7,15},{8,0},{9,1},... | collective-permute-start | bytes 786440 | tf_op jit(solution)/shard_map/ppermute | solution.py:317
  39.1 5.0 %collective-permute-start.14 = (bf16[2,128,512]{2,1,0:T(8,128)(2,1)}, bf16[2,128,512]{2,1,0:T(8,128)(2,1)S(1)}, u32[]{:S(2)}, u32[]{:S(2)}) collective-permute-start(bf16[2,128,512]{2,1,0:T(8,128)(2,1)} %collective-permute-done.13.a2), channel_id=1, source_target_pairs={{0,8},{1,9},{2,10},{3,11},{4,12},{5,13},{6,14},{7,15},{8,0},{9,1},... | collective-permute-start | bytes 786440 | tf_op jit(solution)/shard_map/ppermute | solution.py:317
  39.4 7.2 %collective-permute-start.10 = (f32[2,8,128]{2,1,0:T(8,128)S(1)}, f32[2,8,128]{2,1,0:T(8,128)S(1)}, u32[]{:S(2)}, u32[]{:S(2)}) collective-permute-start(f32[2,8,128]{2,1,0:T(8,128)S(1)} %merge_stats.1.refs_1_), channel_id=1, source_target_pairs={{0,4},{1,5},{2,6},{3,7},{4,0},{5,1},{6,2},{7,3},{8,12},{9,13},{10,... | collective-permute-start | bytes 24584 | tf_op jit(solution)/shard_map/ppermute | solution.py:317
  41.9 5.4 %collective-permute-start.11 = (f32[2,8,128]{2,1,0:T(8,128)S(1)}, f32[2,8,128]{2,1,0:T(8,128)S(1)}, u32[]{:S(2)}, u32[]{:S(2)}) collective-permute-start(f32[2,8,128]{2,1,0:T(8,128)S(1)} %merge_stats.1.refs_1_), channel_id=1, source_target_pairs={{0,6},{1,7},{2,4},{3,5},{4,2},{5,3},{6,0},{7,1},{8,14},{9,15},{10,... | collective-permute-start | bytes 24584 | tf_op jit(solution)/shard_map/ppermute | solution.py:317
  44.1 3.7 %collective-permute-start.9 = (f32[2,8,128]{2,1,0:T(8,128)S(1)}, f32[2,8,128]{2,1,0:T(8,128)S(1)}, u32[]{:S(2)}, u32[]{:S(2)}) collective-permute-start(f32[2,8,128]{2,1,0:T(8,128)S(1)} %merge_stats.1.refs_1_), channel_id=1, source_target_pairs={{0,2},{1,3},{2,0},{3,1},{4,6},{5,7},{6,4},{7,5},{8,10},{9,11},{10,... | collective-permute-start | bytes 24584 | tf_op jit(solution)/shard_map/ppermute | solution.py:317
  47.8 2.0 %copy-start.1 = (bf16[3584,512]{1,0:T(8,128)(2,1)S(1)}, bf16[3584,512]{1,0:T(8,128)(2,1)}, u32[]{:S(2)}) copy-start(bf16[3584,512]{1,0:T(8,128)(2,1)} %copy-done) | copy-start | bytes 11010052
  56.0 3.3 %collective-permute-start.17 = (bf16[256,512]{1,0:T(8,128)(2,1)S(1)}, bf16[256,512]{1,0:T(8,128)(2,1)S(1)}, u32[]{:S(2)}, u32[]{:S(2)}) collective-permute-start(bf16[256,512]{1,0:T(8,128)(2,1)S(1)} %get-tuple-element.44), channel_id=1, source_target_pairs={{0,8},{1,9},{2,10},{3,11},{4,12},{5,13},{6,14},{7,15},{8,0},{9,1},... | collective-permute-start | bytes 786440 | tf_op jit(solution)/shard_map/ppermute | solution.py:317
  56.1 10.6 %collective-permute-start.20 = (bf16[128,1280]{1,0:T(8,128)(2,1)S(1)}, bf16[128,1280]{1,0:T(8,128)(2,1)S(1)}, u32[]{:S(2)}, u32[]{:S(2)}) collective-permute-start(bf16[128,1280]{1,0:T(8,128)(2,1)S(1)} %get-tuple-element.47), channel_id=1, source_target_pairs={{0,2},{1,3},{2,0},{3,1},{4,6},{5,7},{6,4},{7,5},{8,10},{9,11},{10,... | collective-permute-start | bytes 983048 | tf_op jit(solution)/shard_map/ppermute | solution.py:317
  56.8 9.8 %collective-permute-start.18 = (bf16[128,1152]{1,0:T(8,128)(2,1)S(1)}, bf16[128,1152]{1,0:T(8,128)(2,1)S(1)}, u32[]{:S(2)}, u32[]{:S(2)}) collective-permute-start(bf16[128,1152]{1,0:T(8,128)(2,1)S(1)} %get-tuple-element.45), channel_id=1, source_target_pairs={{0,16},{1,17},{2,18},{3,19},{4,20},{5,21},{6,22},{7,23},{8,24},{9,... | collective-permute-start | bytes 884744 | tf_op jit(solution)/shard_map/ppermute | solution.py:317
  57.8 8.8 %collective-permute-start.19 = (bf16[128,1152]{1,0:T(8,128)(2,1)S(1)}, bf16[128,1152]{1,0:T(8,128)(2,1)S(1)}, u32[]{:S(2)}, u32[]{:S(2)}) collective-permute-start(bf16[128,1152]{1,0:T(8,128)(2,1)S(1)} %get-tuple-element.46), channel_id=1, source_target_pairs={{0,1},{1,0},{2,3},{3,2},{4,5},{5,4},{6,7},{7,6},{8,9},{9,8},{10,11... | collective-permute-start | bytes 884744 | tf_op jit(solution)/shard_map/ppermute | solution.py:317
  66.7 5.4 %collective-permute-start.21 = (bf16[1,2,2,1,16,1152]{5,4,3,2,1,0:T(8,128)(2,1)S(1)}, bf16[1,2,2,1,16,1152]{5,4,3,2,1,0:T(8,128)(2,1)S(1)}, u32[]{:S(2)}, u32[]{:S(2)}) collective-permute-start(bf16[1,2,2,1,16,1152]{5,4,3,2,1,0:T(8,128)(2,1)S(1)} %fusion.1), channel_id=1, source_target_pairs={{0,1},{1,0},{2,3},{3,2},{4,5},{5,4},{6,7},{7,6},{8,9},{9,8},{10,11... | collective-permute-start | bytes 442376 | tf_op jit(solution)/shard_map/ppermute | solution.py:317
  68.2 5.2 %collective-permute-start.23 = (bf16[2,2,1,1,16,1152]{5,4,3,2,1,0:T(8,128)(2,1)S(1)}, bf16[2,2,1,1,16,1152]{5,4,3,2,1,0:T(8,128)(2,1)S(1)}, u32[]{:S(2)}, u32[]{:S(2)}) collective-permute-start(bf16[2,2,1,1,16,1152]{5,4,3,2,1,0:T(8,128)(2,1)S(1)} %fusion), channel_id=1, source_target_pairs={{0,2},{1,3},{2,0},{3,1},{4,6},{5,7},{6,4},{7,5},{8,10},{9,11},{10,... | collective-permute-start | bytes 442376 | tf_op jit(solution)/shard_map/ppermute | solution.py:317
  69.7 5.9 %collective-permute-start.25 = (bf16[1,2,1,2,16,1280]{5,4,3,2,1,0:T(8,128)(2,1)S(1)}, bf16[1,2,1,2,16,1280]{5,4,3,2,1,0:T(8,128)(2,1)S(1)}, u32[]{:S(2)}, u32[]{:S(2)}) collective-permute-start(bf16[1,2,1,2,16,1280]{5,4,3,2,1,0:T(8,128)(2,1)S(1)} %bitcast.60), channel_id=1, source_target_pairs={{0,16},{1,17},{2,18},{3,19},{4,20},{5,21},{6,22},{7,23},{8,24},{9,... | collective-permute-start | bytes 491528 | tf_op jit(solution)/shard_map/ppermute | solution.py:317
  72.1 4.4 %collective-permute-start.22 = (bf16[1,2,1,1,16,1152]{5,4,3,2,1,0:T(8,128)(2,1)S(1)}, bf16[1,2,1,1,16,1152]{5,4,3,2,1,0:T(8,128)(2,1)S(1)}, u32[]{:S(2)}, u32[]{:S(2)}) collective-permute-start(bf16[1,2,1,1,16,1152]{5,4,3,2,1,0:T(8,128)(2,1)S(1)} %fusion.12), channel_id=1, source_target_pairs={{0,2},{1,3},{2,0},{3,1},{4,6},{5,7},{6,4},{7,5},{8,10},{9,11},{10,... | collective-permute-start | bytes 221192 | tf_op jit(solution)/shard_map/ppermute | solution.py:317
  73.5 4.4 %collective-permute-start.24 = (bf16[1,2,1,1,16,1152]{5,4,3,2,1,0:T(8,128)(2,1)S(1)}, bf16[1,2,1,1,16,1152]{5,4,3,2,1,0:T(8,128)(2,1)S(1)}, u32[]{:S(2)}, u32[]{:S(2)}) collective-permute-start(bf16[1,2,1,1,16,1152]{5,4,3,2,1,0:T(8,128)(2,1)S(1)} %fusion.8), channel_id=1, source_target_pairs={{0,16},{1,17},{2,18},{3,19},{4,20},{5,21},{6,22},{7,23},{8,24},{9,... | collective-permute-start | bytes 221192 | tf_op jit(solution)/shard_map/ppermute | solution.py:317
  75.7 4.5 %collective-permute-start.26 = (bf16[1,2,1,1,16,1280]{5,4,3,2,1,0:T(8,128)(2,1)S(1)}, bf16[1,2,1,1,16,1280]{5,4,3,2,1,0:T(8,128)(2,1)S(1)}, u32[]{:S(2)}, u32[]{:S(2)}) collective-permute-start(bf16[1,2,1,1,16,1280]{5,4,3,2,1,0:T(8,128)(2,1)S(1)} %fusion.4), channel_id=1, source_target_pairs={{0,1},{1,0},{2,3},{3,2},{4,5},{5,4},{6,7},{7,6},{8,9},{9,8},{10,11... | collective-permute-start | bytes 245768 | tf_op jit(solution)/shard_map/ppermute | solution.py:317
  80.3 6.9 %collective-permute-start.27 = (bf16[1,1,1,1,16,3584]{5,4,3,2,1,0:T(8,128)(2,1)S(1)}, bf16[1,1,1,1,16,3584]{5,4,3,2,1,0:T(8,128)(2,1)S(1)}, u32[]{:S(2)}, u32[]{:S(2)}) collective-permute-start(bf16[1,1,1,1,16,3584]{5,4,3,2,1,0:T(8,128)(2,1)S(1)} %slice.215), channel_id=1, source_target_pairs={{0,4},{1,5},{2,6},{3,7},{4,0},{5,1},{6,2},{7,3},{8,12},{9,13},{10,... | collective-permute-start | bytes 344072 | tf_op jit(solution)/shard_map/ppermute | solution.py:317

commit v6 on v5

--- a/solution.py
+++ b/solution.py
@@ -88,89 +88,115 @@
     )(at, serving, *arrived)
 
 
-def student_stats(logits_ref, a, b):
-    cols = a.shape[1]
-    logits_ref[:, :cols] = a
-    logits_ref[:, cols:] = b
-    peak = jnp.max(jnp.maximum(a, b), axis=1, keepdims=True)
-    a = jnp.exp((a - peak) * 0.5)
-    b = jnp.exp((b - peak) * 0.5)
-    hard = jnp.sum(a * a + b * b, axis=1, keepdims=True)
-    soft = jnp.sum(a + b, axis=1, keepdims=True)
-    return columns_to_rows([peak, hard, soft])
-
-
-def near_kernel(splits, rows_ref, w_ref, other_ref, logits_ref, stats_ref, own_ref, sems):
+def student_stats(logits):
+    peak = jnp.max(logits, axis=1, keepdims=True)
+    soft = jnp.exp((logits - peak) * 0.5)
+    hard = jnp.sum(soft * soft, axis=1, keepdims=True)
+    return columns_to_rows([peak, hard, jnp.sum(soft, axis=1, keepdims=True)])
+
+
+def own_kernel(splits, rows_ref, w_ref, logits_ref, stats_ref, own_ref, sems):
     step = w_ref.shape[0] // splits
     copies = []
     for c in range(splits):
         part = pl.ds(c * step, step)
         copies.append(pltpu.make_async_copy(w_ref.at[part], own_ref.at[part], sems.at[c]))
         copies[c].start()
-    b = jnp.dot(rows_ref[...], other_ref[...], preferred_element_type=F32)
-    a = 0.0
+    logits = 0.0
     for c in range(splits):
         copies[c].wait()
         part = slice(c * step, (c + 1) * step)
-        a += jnp.dot(rows_ref[:, part], own_ref[part, :], preferred_element_type=F32)
-    stats_ref[...] = student_stats(logits_ref, a, b)
-
-
-def near_logits(rows, own, other):
+        logits += jnp.dot(rows_ref[:, part], own_ref[part, :], preferred_element_type=F32)
+    logits_ref[...] = logits
+    stats_ref[...] = student_stats(logits)
+
+
+def own_logits(rows, own):
     per, depth = rows.shape
     cols = own.shape[1]
-    splits = 2 if depth % 256 == 0 else 1
-    return pl.pallas_call(
-        lambda *refs: near_kernel(splits, *refs),
+    splits = 4 if depth % 512 == 0 else 1
+    return pl.pallas_call(
+        lambda *refs: own_kernel(splits, *refs),
         out_shape=(
-            shape((per, 2 * cols), F32),
+            shape((per, cols), F32),
             shape((STAT_ROWS, per), F32),
             shape((depth, cols), BF16),
         ),
-        in_specs=[VMEM, pl.BlockSpec(memory_space=pl.ANY), VMEM],
+        in_specs=[VMEM, pl.BlockSpec(memory_space=pl.ANY)],
         out_specs=(VMEM, VMEM, VMEM),
         scratch_shapes=[pltpu.SemaphoreType.DMA((splits,))],
-        compiler_params=params(16),
-        cost_estimate=cost(4 * per * depth * cols, (per + 2 * cols) * depth * 2, 2 * per * cols),
-        name="near_logits",
-    )(rows, own, other)
+        compiler_params=params(10),
+        cost_estimate=cost(2 * per * depth * cols, (per + 2 * cols) * depth * 2, per * cols),
+        name="own_logits",
+    )(rows, own)
+
+
+def core_kernel(rows_ref, w_ref, held_ref, logits_ref, stats_ref):
+    logits = jnp.dot(rows_ref[...], w_ref[...], preferred_element_type=F32)
+    logits_ref[...] = logits
+    stats_ref[...] = student_stats(logits)
+
+
+def core_logits(rows, other, held):
+    per, depth = rows.shape
+    cols = other.shape[1]
+    return pl.pallas_call(
+        core_kernel,
+        out_shape=(shape((per, cols), F32), shape((STAT_ROWS, per), F32)),
+        in_specs=[VMEM] * 3,
+        out_specs=(VMEM, VMEM),
+        compiler_params=params(10),
+        cost_estimate=cost(2 * per * depth * cols, (per + cols) * depth * 2, per * cols),
+        name="core_logits",
+    )(rows, other, held)
 
 
 NOTHING = -3.0e38
 
 
-def far_kernel(spots_ref, x0, x1, x2, x3, own_ref, other_ref, near_ref, taught_ref, taught_core_ref, ids_ref, logits_ref, rows_ref, out_ref):
+def both(a, b):
+    peak = jnp.maximum(a[0:1], b[0:1])
+    ea, eb = jnp.exp((a[0:1] - peak) * 0.5), jnp.exp((b[0:1] - peak) * 0.5)
+    return jnp.concatenate(
+        [peak, a[1:2] * (ea * ea) + b[1:2] * (eb * eb), a[2:3] * ea + b[2:3] * eb]
+    )
+
+
+def far_kernel(spots_ref, x0, x1, x2, x3, own_ref, other_ref, stats_a, stats_b, taught_ref, taught_core_ref, ids_ref, a_ref, b_ref, rows_ref, out_ref):
     count = x0.shape[0]
     for k, piece in enumerate((x0, x1, x2, x3)):
         rows_ref[pl.ds(pl.multiple_of(spots_ref[k], 16), count), :] = piece[...]
     per = rows_ref.shape[0]
     a = jnp.dot(rows_ref[...], own_ref[...], preferred_element_type=F32)
     b = jnp.dot(rows_ref[...], other_ref[...], preferred_element_type=F32)
-    out_ref[0, 0:3, :] = near_ref[0:3, :]
+    a_ref[...] = a
+    b_ref[...] = b
+    out_ref[0, 0:3, :] = both(stats_a[...], stats_b[...])
     out_ref[0, 3:4, :] = ids_ref[...].astype(F32)
     out_ref[0, 4:6, :] = taught_ref[0:2, :]
     out_ref[0, 6:8, :] = taught_core_ref[0:2, :]
-    out_ref[1, 0:3, :] = student_stats(logits_ref, a, b)[0:3]
+    out_ref[1, 0:3, :] = both(student_stats(a), student_stats(b))
     row = lax.broadcasted_iota(jnp.int32, (5, per), 0)
     out_ref[1, 3:8, :] = jnp.where((row == 1) | (row == 3), NOTHING, 0.0)
 
 
-def far_logits(spots, pieces, own, other, near_stats, taught, taught_core, ids):
+def far_logits(spots, pieces, own, other, stats_a, stats_b, taught, taught_core, ids):
     depth, cols = own.shape
     per = sum(piece.shape[0] for piece in pieces)
     return pl.pallas_call(
         far_kernel,
         out_shape=(
-            shape((per, 2 * cols), F32),
+            shape((per, cols), F32),
+            shape((per, cols), F32),
             shape((per, depth), BF16),
             shape((2, STAT_ROWS, per), F32),
         ),
-        in_specs=[SMEM] + [VMEM] * 10,
-        out_specs=(VMEM, VMEM, VMEM),
+        in_specs=[SMEM] + [VMEM] * 11,
+        out_specs=(VMEM, VMEM, VMEM, VMEM),
         compiler_params=params(20),
         cost_estimate=cost(4 * per * depth * cols, (per + 2 * cols) * depth * 2, 2 * per * cols),
         name="far_logits",
-    )(spots, *pieces, own, other, near_stats, taught, taught_core, ids)
+    )(spots, *pieces, own, other, stats_a, stats_b, taught, taught_core, ids)
 
 
 def merged(parts):
@@ -200,7 +226,7 @@
         out_shape=shape(parts[0].shape, F32),
         in_specs=[VMEM] * (len(parts) + len(held)),
         out_specs=VMEM,
-        compiler_params=params(6),
+        compiler_params=params(14),
         cost_estimate=cost(0, 5 * parts[0].size * 4),
         name="merge_stats",
     )(*parts, *held)
@@ -217,15 +243,15 @@
 
 def back_kernel(bits, edges, n, at_ref, *refs):
     stats_refs = refs[:n]
-    serving_ref, near_ref, far_ref, aligned_ref, wown_ref, wother_ref = refs[n : n + 6]
-    gown_ref, gother_ref = refs[n + 6 : n + 8]
-    send_refs, keep_refs = refs[n + 8 : n + 11], refs[n + 11 :]
+    logits_refs = refs[n : n + 4]
+    serving_ref, aligned_ref, wown_ref, wother_ref = refs[n + 4 : n + 8]
+    gown_ref, gother_ref = refs[n + 8 : n + 10]
+    send_refs, keep_refs = refs[n + 10 : n + 13], refs[n + 13 :]
     flip, me = at_ref[0], at_ref[3]
-    per, wide = near_ref.shape
-    cols = wide // 2
+    per, cols = logits_refs[0].shape
     stats = [merged([ref[j] for ref in stats_refs]) for j in range(2)]
     lane = lax.broadcasted_iota(jnp.int32, (per, per), 1)
-    for j, logits_ref in enumerate((near_ref, far_ref)):
+    for j in range(2):
         rows = stats[j][:4] + (serving_ref[me ^ (2 * j)].astype(F32),)
         columns = jnp.concatenate(rows + (jnp.zeros((128 - len(rows), per), F32),)).T
         peak, hard, soft, ids, wanted = [columns[:, i : i + 1] for i in range(len(rows))]
@@ -240,7 +266,7 @@
         for c, g_ref in enumerate((gown_ref, gother_ref)):
             part = slice(c * cols, (c + 1) * cols)
             column = at_ref[1 + c] + lax.broadcasted_iota(jnp.int32, (per, cols), 1)
-            half = jnp.exp((logits_ref[:, part] - peak) * 0.5)
+            half = jnp.exp((logits_refs[2 * j + c][...] - peak) * 0.5)
             taught = jnp.exp((aligned_ref[j, :, part].astype(F32) - tpeak) * 0.5)
             label = jnp.where(column == ids, 16.0, 0.0)
             grad = (half * soft - taught * total) + (half * half * hard - label)
@@ -252,26 +278,27 @@
         for g_ref, w_ref in ((gown_ref, wown_ref), (gother_ref, wother_ref)):
             rows = jnp.dot(pick, g_ref[...], preferred_element_type=F32).astype(BF16)
             back += lax.dot_general(
-                rows, w_ref[part, :], (((1,), (1,)), ((), ())), preferred_element_type=F32
+                w_ref[part, :], rows, (((1,), (1,)), ((), ())), preferred_element_type=F32
             )
+        back = back.T
         send_refs[p][...] = back[:per].astype(BF16)
         keep_refs[p][...] = back[per:]
 
 
-def back_rows(at, stats, serving, near, far, aligned, own, other, bits, edges):
+def back_rows(at, stats, logits, serving, aligned, own, other, bits, edges):
     depth, cols = own.shape
-    per = near.shape[0]
+    per = logits[0].shape[0]
     sends = [shape((per, edges[p + 1] - edges[p]), BF16) for p in range(3)]
     keeps = [shape((per, edges[p + 1] - edges[p]), F32) for p in range(3)]
     got = pl.pallas_call(
         lambda *refs: back_kernel(bits, edges, len(stats), *refs),
         out_shape=[shape((2 * per, cols), BF16)] * 2 + sends + keeps,
-        in_specs=[SMEM] + [VMEM] * (len(stats) + 6),
+        in_specs=[SMEM] + [VMEM] * (len(stats) + 8),
         out_specs=[VMEM] * 8,
         compiler_params=params(24),
         cost_estimate=cost(8 * per * depth * cols, 2 * cols * depth * 2, 4 * per * cols),
         name="back_rows",
-    )(at, *stats, serving, near, far, aligned, own, other)
+    )(at, *stats, *logits, serving, aligned, own, other)
     return got[0], got[1], got[2:5], got[5:8]
 
 
@@ -325,41 +352,51 @@
     quarter_rows = per // 4
     quarter = me_v & 3
     starts = [(quarter ^ k) * quarter_rows for k in range(4)]
-    x0 = swap(lax.dynamic_slice_in_dim(hidden, starts[0], quarter_rows, 0), X)
     other_weight = swap(head_weight, CORE)
-    second = lax.dynamic_slice_in_dim(hidden, starts[3], quarter_rows, 0)
+    first = lax.dynamic_slice_in_dim(hidden, starts[0], quarter_rows, 0)
+    x0 = swap(first, X)
+    _, rows, teacher = tie(first, hidden, teacher_logits)
+    second = lax.dynamic_slice_in_dim(rows, starts[3], quarter_rows, 0)
     chip = me_g >> 1
-    kept = lax.dynamic_slice_in_dim(teacher_logits, 2 * chip, 2, 1).swapaxes(0, 1)
-    gone = lax.dynamic_slice_in_dim(teacher_logits, 2 * (chip ^ 1), 2, 1).swapaxes(0, 1)
+    kept = lax.dynamic_slice_in_dim(teacher, 2 * chip, 2, 1).swapaxes(0, 1)
+    gone = lax.dynamic_slice_in_dim(teacher, 2 * (chip ^ 1), 2, 1).swapaxes(0, 1)
     taught = taught_stats(kept, gone)
-    taught_core = swap(taught, CORE)
-    x0, second, near_in = tie(x0, second, hidden)
+    near_a, stats_a, own_weight = own_logits(rows, head_weight)
+    x0, second, kept, gone, taught, near_a, rows = tie(
+        x0, second, kept, gone, taught, near_a, rows
+    )
     x1 = swap(x0, Y)
     x2 = swap(x0, W)
     x3 = swap(second, X)
-    logits0, stats0, own_weight = near_logits(near_in, head_weight, other_weight)
-    x3, gone, logits0 = tie(x3, gone, logits0)
-    logits1, x_rows, stats = far_logits(
+    taught_core = swap(taught, CORE)
+    kept_core = swap(kept, CORE)
+    near_b, stats_b = core_logits(rows, other_weight, x0)
+    x1, x2, x3, gone, near_b, kept_core, taught_core = tie(
+        x1, x2, x3, gone, near_b, kept_core, taught_core
+    )
+    taught_x = swap(gone, X)
+    far_a, far_b, x_rows, stats = far_logits(
         ints(*starts),
         [x0, x1, x2, x3],
         own_weight,
         other_weight,
-        stats0,
+        stats_a,
+        stats_b,
         taught,
         taught_core,
         token_ids.reshape(1, per),
     )
 
     served = serving.reshape(groups, 1, per)
-    taught_x = swap(gone, X)
-    arrived = [kept, swap(kept, CORE), taught_x, swap(taught_x, CORE)]
-    aligned = teacher_rows(ints(me_g, me_g & 1), served, arrived)
-
-    held = [logits0, logits1]
+    logits = [near_a, near_b, far_a, far_b]
+    held = logits + [own_weight]
     stats = merge([stats, swap(stats, X), swap(stats, Y), swap(stats, X + Y)], (0, 1, 0, 1), held)
-    core_rows = swap(hidden, CORE)
-    stats, x_sent = tie(stats, x_rows)
-    core_x_rows = swap(x_sent, CORE)
+    _, taught_x, rows, x_sent = tie(stats, taught_x, rows, x_rows)
+    core_rows = [swap(rows, CORE), swap(x_sent, CORE)]
+    aligned = teacher_rows(
+        ints(me_g, me_g & 1), served, [kept, kept_core, taught_x, swap(taught_x, CORE)]
+    )
+    aligned, *core_rows = tie(aligned, *core_rows)
     mask = W
     while True:
         masks = [mask, 2 * mask, 3 * mask] if 2 * mask < shards else [mask]
@@ -384,11 +421,11 @@
         me_v * owned, (me_g * shards + me_v) * cols, ((me_g ^ 1) * shards + me_v) * cols, me_g
     )
     gown, gother, sents, keeps = back_rows(
-        at, parts, served, logits0, logits1, aligned, own_weight, other_weight, first_bits, edges
+        at, parts, logits, served, aligned, own_weight, other_weight, first_bits, edges
     )
     gots = [swap(sents[p], masks[orders[p][0]]) for p in range(3)]
     theirs = swap(gother, CORE)
-    grad_head = head_gradient([hidden, x_rows, core_rows, core_x_rows], gown, theirs)
+    grad_head = head_gradient([hidden, x_rows] + core_rows, gown, theirs)
     grad_head, *gots = tie(grad_head, *gots)
 
     def folded(value, p):

time: 88.5 us -> 90.4 us (1.021)
  local copies, waits for them, and re-layouts: 10.7 us -> 18.6 us
  waiting for transfers between devices: 22.3 us -> 15.4 us
    unnamed x22 -> x34, local copies, waits for them, and re-layouts: 7.18 us -> 15.5 us
    ppermute x28, waiting for transfers between devices: 22.3 us -> 15.4 us  [swap(): return lax.ppermute(value, AXES, [(i, i ^ mask) for i in range(count)])]
    dynamic_slice x2, local copies, waits for them, and re-layouts: 3.51 us -> 1.91 us  [the longest x1 0.95 us: body(): first = lax.dynamic_slice_in_dim(hidden, starts[0], quarter_rows, 0)]
    optimization_barrier x0 -> x1, local copies, waits for them, and re-layouts: none -> 1.14 us  [tie(): return lax.optimization_barrier(values)]
    pallas_call x2 -> x3, Pallas kernels: 7.75 us -> 8.43 us  [the longest x1 3.46 us: far_logits(): pl.pallas_call(far_kernel, out_shape=(shape((per, cols), F32), shape((per...]
  transfers between devices with their start and end apart: 28 -> 28, of which waited for: 13 -> 12; matrix products, arithmetic and copies ran while one was open for 5% -> 4% of each run, Pallas kernels for 27% -> 20%
where the time goes in v6:
time: 90.4 us; the launch traced here: 89.7 us
  starting transfers between devices  29.7 us (33%)
  Pallas kernels  23.8 us (26%)
  local copies, waits for them, and re-layouts  18.6 us (21%)
  waiting for transfers between devices  15.4 us (17%)
  other arithmetic  1.3 us (1%)
    ppermute x28, starting transfers between devices, swap(): return lax.ppermute(value, AXES, [(i, i ^ mask) for i in range(count)])  29.7 us
    unnamed x34, local copies, waits for them, and re-layouts  15.5 us
    ppermute x28, waiting for transfers between devices, swap(): return lax.ppermute(value, AXES, [(i, i ^ mask) for i in range(count)])  15.4 us
    pallas_call x1, Pallas kernels, head_gradient(): pl.pallas_call(head_kernel, grid=(depth // tile,), out_shape=shape((depth...  7.23 us
    pallas_call x1, Pallas kernels, back_rows(): pl.pallas_call(lambda *refs: back_kernel(bits, edges, len(stats), *refs),...  6.04 us
    pallas_call x1, Pallas kernels, far_logits(): pl.pallas_call(far_kernel, out_shape=(shape((per, cols), F32), shape((per...  3.46 us
    pallas_call x1, Pallas kernels, core_logits(): pl.pallas_call(core_kernel, out_shape=(shape((per, cols), F32), shape((ST...  2.9 us
    pallas_call x1, Pallas kernels, own_logits(): pl.pallas_call(lambda *refs: own_kernel(splits, *refs), out_shape=(shape(...  2.06 us
  transfers between devices with their start and end apart: 28, of which 12 were waited for; matrix products, arithmetic and copies ran while one was open for 4% of the time, Pallas kernels for 20%

profile of v6, /device:TPU:0, one launch (start us, length us, event | category | flops | bytes accessed | tf_op | source)
XLA Modules:
  0.0 89.7 jit_solution(1646523007238073907)
XLA Ops:
  0.6 0.5 collective-permute-start.4
  1.2 1.0 %constant_dynamic-slice_fusion.1 = bf16[32,3584]{1,0:T(8,128)(2,1)S(1)} fusion(bf16[128,3584]{1,0:T(8,128)(2,1)} %r0.1, s32[]{:T(128)S(6)} %select_n.12), kind=kLoop, calls=%fused_computation.30 | loop fusion | bytes 458756 | tf_op jit(solution)/shard_map/dynamic_slice | solution.py:356
  2.1 2.6 %collective-permute-start = (bf16[32,3584]{1,0:T(8,128)(2,1)S(1)}, bf16[32,3584]{1,0:T(8,128)(2,1)S(1)}, u32[]{:S(2)}, u32[]{:S(2)}) collective-permute-start(bf16[32,3584]{1,0:T(8,128)(2,1)S(1)} %constant_dynamic-slice_fusion.1), channel_id=1, source_target_pairs={{0,16},{1,17},{2,18},{3,19},{4,20},{5,21},{6,22},{7,23},{8,24},{9,... | collective-permute-start | bytes 688136 | tf_op jit(solution)/shard_map/ppermute | solution.py:344
  4.8 1.0 %constant_dynamic-slice_fusion = bf16[32,3584]{1,0:T(8,128)(2,1)S(1)} fusion(bf16[128,3584]{1,0:T(8,128)(2,1)} %r0.1, s32[]{:T(128)S(6)} %select_n.13), kind=kLoop, calls=%fused_computation.29 | loop fusion | bytes 458756 | tf_op jit(solution)/shard_map/dynamic_slice | solution.py:359
  5.7 1.1 %copy.7 = bf16[128,4,512]{2,0,1:T(8,128)(2,1)S(1)} copy(bf16[128,4,512]{2,1,0:T(4,128)(2,1)} %param.9) | data formatting | bytes 1048576 | tf_op jit(solution)/shard_map/optimization_barrier | solution.py:347
  6.9 0.4 taught_stats.1.taught_ref
  7.3 2.1 %copy-done.4 = bf16[3584,512]{1,0:T(8,128)(2,1)S(1)} copy-done((bf16[3584,512]{1,0:T(8,128)(2,1)S(1)}, bf16[3584,512]{1,0:T(8,128)(2,1)}, u32[]{:S(2)}) %copy-start.4) | copy-done | bytes 3670040
  9.4 2.1 %own_logits.1 = (f32[128,512]{1,0:T(8,128)S(1)}, f32[8,128]{1,0:T(8,128)S(1)}, bf16[3584,512]{1,0:T(8,128)(2,1)S(1)}) custom-call(bf16[128,3584]{1,0:T(8,128)(2,1)S(1)} %copy-done.3, bf16[3584,512]{1,0:T(8,128)(2,1)S(1)} %copy-done.4), custom_call_target="tpu_custom_call" | custom-call | flops 469762048 | bytes 8257536 | tf_op jit(solution)/shard_map/own_logits/pallas_call | solution.py:118
  11.5 1.8 %copy-done = bf16[3584,512]{1,0:T(8,128)(2,1)} copy-done((bf16[3584,512]{1,0:T(8,128)(2,1)}, bf16[3584,512]{1,0:T(8,128)(2,1)S(1)}, u32[]{:S(2)}) %copy-start) | copy-done | bytes 3670040
  13.3 0.1 collective-permute-start.5
  13.4 0.3 collective-permute-start.3
  13.7 1.8 %collective-permute-start.2 = (bf16[32,3584]{1,0:T(8,128)(2,1)S(1)}, bf16[32,3584]{1,0:T(8,128)(2,1)S(1)}, u32[]{:S(2)}, u32[]{:S(2)}) collective-permute-start(bf16[32,3584]{1,0:T(8,128)(2,1)S(1)} %collective-permute-done.held_ref.x0), channel_id=1, source_target_pairs={{0,2},{1,3},{2,0},{3,1},{4,6},{5,7},{6,4},{7,5},{8,10},{9,11},{10,... | collective-permute-start | bytes 688136 | tf_op jit(solution)/shard_map/ppermute | solution.py:344
  15.6 1.5 %collective-permute-start.1 = (bf16[32,3584]{1,0:T(8,128)(2,1)S(1)}, bf16[32,3584]{1,0:T(8,128)(2,1)S(1)}, u32[]{:S(2)}, u32[]{:S(2)}) collective-permute-start(bf16[32,3584]{1,0:T(8,128)(2,1)S(1)} %collective-permute-done.held_ref.x0), channel_id=1, source_target_pairs={{0,1},{1,0},{2,3},{3,2},{4,5},{5,4},{6,7},{7,6},{8,9},{9,8},{10,11... | collective-permute-start | bytes 688136 | tf_op jit(solution)/shard_map/ppermute | solution.py:344
  17.1 2.9 %core_logits.1 = (f32[128,512]{1,0:T(8,128)S(1)}, f32[8,128]{1,0:T(8,128)S(1)}) custom-call(bf16[128,3584]{1,0:T(8,128)(2,1)S(1)} %copy-done.3, bf16[3584,512]{1,0:T(8,128)(2,1)} %collective-permute-done.4.w_ref.other_ref.refs_12_, bf16[32,3584]{1,0:T(8,128)(2,1)S(1)} %collective-permute-done.held_ref.x0), custom_call_target="tpu_custom_call" | custom-call | flops 469762048 | bytes 4587520 | tf_op jit(solution)/shard_map/core_logits/pallas_call | solution.py:143
  20.0 1.3 %collective-permute-done.3.x3 = bf16[32,3584]{1,0:T(8,128)(2,1)S(1)} collective-permute-done((bf16[32,3584]{1,0:T(8,128)(2,1)S(1)}, bf16[32,3584]{1,0:T(8,128)(2,1)S(1)}, u32[]{:S(2)}, u32[]{:S(2)}) %collective-permute-start.3) | collective-permute-done | bytes 229408 | tf_op jit(solution)/shard_map/ppermute | solution.py:344
  21.3 0.7 copy-done.9
  22.0 0.7 copy-done.11
  22.7 0.1 collective-permute-done.1.x1
  22.9 0.7 copy-done.13
  23.6 0.7 copy-done.7
  24.3 1.5 %collective-permute-start.13 = (bf16[2,128,512]{2,1,0:T(8,128)(2,1)S(1)}, bf16[2,128,512]{2,1,0:T(8,128)(2,1)}, u32[]{:S(2)}, u32[]{:S(2)}) collective-permute-start(bf16[2,128,512]{2,1,0:T(8,128)(2,1)S(1)} %get-tuple-element.68.gone_ref), channel_id=1, source_target_pairs={{0,16},{1,17},{2,18},{3,19},{4,20},{5,21},{6,22},{7,23},{8,24},{9,... | collective-permute-start | bytes 786440 | tf_op jit(solution)/shard_map/ppermute | solution.py:344
  25.8 0.1 pad_add_fusion.1.spots_ref
  25.8 2.0 %copy-done.1 = bf16[3584,512]{1,0:T(8,128)(2,1)S(1)} copy-done((bf16[3584,512]{1,0:T(8,128)(2,1)S(1)}, bf16[3584,512]{1,0:T(8,128)(2,1)}, u32[]{:S(2)}) %copy-start.1) | copy-done | bytes 3670040
  27.9 0.9 %copy-done.6 = bf16[32,3584]{1,0:T(8,128)(2,1)S(1)} copy-done((bf16[32,3584]{1,0:T(8,128)(2,1)S(1)}, bf16[32,3584]{1,0:T(8,128)(2,1)}, u32[]{:S(2)}) %copy-start.6) | copy-done | bytes 229400
  28.8 0.9 %copy-done.10 = bf16[32,3584]{1,0:T(8,128)(2,1)S(1)} copy-done((bf16[32,3584]{1,0:T(8,128)(2,1)S(1)}, bf16[32,3584]{1,0:T(8,128)(2,1)}, u32[]{:S(2)}) %copy-start.10) | copy-done | bytes 229400
  29.8 0.9 %copy-done.12 = bf16[32,3584]{1,0:T(8,128)(2,1)S(1)} copy-done((bf16[32,3584]{1,0:T(8,128)(2,1)S(1)}, bf16[32,3584]{1,0:T(8,128)(2,1)}, u32[]{:S(2)}) %copy-start.12) | copy-done | bytes 229400
  30.7 0.9 %copy-done.14 = bf16[32,3584]{1,0:T(8,128)(2,1)S(1)} copy-done((bf16[32,3584]{1,0:T(8,128)(2,1)S(1)}, bf16[32,3584]{1,0:T(8,128)(2,1)}, u32[]{:S(2)}) %copy-start.14) | copy-done | bytes 229400
  31.6 3.5 %far_logits.1 = (f32[128,512]{1,0:T(8,128)S(1)}, f32[128,512]{1,0:T(8,128)S(1)}, bf16[128,3584]{1,0:T(8,128)(2,1)S(1)}, f32[2,8,128]{2,1,0:T(8,128)S(1)}) custom-call(s32[4]{0:T(128)S(1)} %pad_add_fusion.1.spots_ref, bf16[32,3584]{1,0:T(8,128)(2,1)S(1)} %copy-done.6, bf16[32,3584]{1,0:T(8,128)(2,1)S(1)} %copy-done.14, bf16[32,3584]{1,0:T(8,128)(2,1)S(1)} %copy-done.12, ...), custom_call_target="tpu_custom_call" | custom-call | flops 939524096 | bytes 8257536 | tf_op jit(solution)/shard_map/far_logits/pallas_call | solution.py:186
  35.1 1.6 %collective-permute-start.9 = (f32[2,8,128]{2,1,0:T(8,128)S(1)}, f32[2,8,128]{2,1,0:T(8,128)S(1)}, u32[]{:S(2)}, u32[]{:S(2)}) collective-permute-start(f32[2,8,128]{2,1,0:T(8,128)S(1)} %get-tuple-element.62.refs_0_), channel_id=1, source_target_pairs={{0,17},{1,16},{2,19},{3,18},{4,21},{5,20},{6,23},{7,22},{8,25},{9,... | collective-permute-start | bytes 24584 | tf_op jit(solution)/shard_map/ppermute | solution.py:344
  36.7 0.5 collective-permute-start.8
  37.2 1.5 %collective-permute-start.7 = (f32[2,8,128]{2,1,0:T(8,128)S(1)}, f32[2,8,128]{2,1,0:T(8,128)S(1)}, u32[]{:S(2)}, u32[]{:S(2)}) collective-permute-start(f32[2,8,128]{2,1,0:T(8,128)S(1)} %get-tuple-element.62.refs_0_), channel_id=1, source_target_pairs={{0,16},{1,17},{2,18},{3,19},{4,20},{5,21},{6,22},{7,23},{8,24},{9,... | collective-permute-start | bytes 24584 | tf_op jit(solution)/shard_map/ppermute | solution.py:344
  38.7 1.1 %collective-permute-done.9.refs_3_ = f32[2,8,128]{2,1,0:T(8,128)S(1)} collective-permute-done((f32[2,8,128]{2,1,0:T(8,128)S(1)}, f32[2,8,128]{2,1,0:T(8,128)S(1)}, u32[]{:S(2)}, u32[]{:S(2)}) %collective-permute-start.9) | collective-permute-done | bytes 8224 | tf_op jit(solution)/shard_map/ppermute | solution.py:344
  39.7 0.6 collective-permute-done.8.refs_2_
  40.3 0.5 collective-permute-done.7.refs_1_
  40.9 0.1 collective-permute-start.15
  41.0 0.5 collective-permute-start.16
  41.5 0.1 collective-permute-start.14
  41.5 0.1 pad_add_fusion.2.at_ref
  41.6 0.1 pad_add_fusion.refs_0_
  41.7 3.5 %collective-permute-start.12 = (f32[2,8,128]{2,1,0:T(8,128)S(1)}, f32[2,8,128]{2,1,0:T(8,128)S(1)}, u32[]{:S(2)}, u32[]{:S(2)}) collective-permute-start(f32[2,8,128]{2,1,0:T(8,128)S(1)} %merge_stats.1.refs_1_), channel_id=1, source_target_pairs={{0,6},{1,7},{2,4},{3,5},{4,2},{5,3},{6,0},{7,1},{8,14},{9,15},{10,... | collective-permute-start | bytes 24584 | tf_op jit(solution)/shard_map/ppermute | solution.py:344
  45.2 0.9 %collective-permute-start.10 = (f32[2,8,128]{2,1,0:T(8,128)S(1)}, f32[2,8,128]{2,1,0:T(8,128)S(1)}, u32[]{:S(2)}, u32[]{:S(2)}) collective-permute-start(f32[2,8,128]{2,1,0:T(8,128)S(1)} %merge_stats.1.refs_1_), channel_id=1, source_target_pairs={{0,2},{1,3},{2,0},{3,1},{4,6},{5,7},{6,4},{7,5},{8,10},{9,11},{10,... | collective-permute-start | bytes 24584 | tf_op jit(solution)/shard_map/ppermute | solution.py:344
  46.1 0.9 %copy-done.8 = bf16[2,128,512]{2,1,0:T(8,128)(2,1)S(1)} copy-done((bf16[2,128,512]{2,1,0:T(8,128)(2,1)S(1)}, bf16[2,128,512]{2,1,0:T(8,128)(2,1)}, u32[]{:S(2)}) %copy-start.8) | copy-done | bytes 262168
  47.0 1.7 %teacher_rows.1.refs_10_ = bf16[2,128,1024]{2,1,0:T(8,128)(2,1)S(1)} custom-call(s32[2]{0:T(128)S(1)} %pad_add_fusion.2.at_ref, s32[4,1,128]{2,1,0:T(1,128)S(1)} %bitcast.40, bf16[2,128,512]{2,1,0:T(8,128)(2,1)S(1)} %get-tuple-element.53.kept_ref.a0, bf16[2,128,512]{2,1,0:T(8,128)(2,1)S(1)} %copy-done.8, bf16[2,128,512]{2,1,0:T(8,128)(2,1)} %collective-permute-done.13.a2, ...), custom_call_target="tpu_custom_call" | custom-call | flops 268435456 | bytes 1572864 | tf_op jit(solution)/shard_map/teacher_rows/pallas_call | solution.py:80
  48.8 0.9 %collective-permute-done.11.refs_3_ = f32[2,8,128]{2,1,0:T(8,128)S(1)} collective-permute-done((f32[2,8,128]{2,1,0:T(8,128)S(1)}, f32[2,8,128]{2,1,0:T(8,128)S(1)}, u32[]{:S(2)}, u32[]{:S(2)}) %collective-permute-start.11) | collective-permute-done | bytes 8224 | tf_op jit(solution)/shard_map/ppermute | solution.py:344
  49.7 2.0 %copy-done.2 = bf16[3584,512]{1,0:T(8,128)(2,1)S(1)} copy-done((bf16[3584,512]{1,0:T(8,128)(2,1)S(1)}, bf16[3584,512]{1,0:T(8,128)(2,1)}, u32[]{:S(2)}) %copy-start.2) | copy-done | bytes 3670040
  51.8 6.0 %back_rows.1 = (bf16[256,512]{1,0:T(8,128)(2,1)S(1)}, bf16[256,512]{1,0:T(8,128)(2,1)S(1)}, bf16[128,1152]{1,0:T(8,128)(2,1)S(1)}, bf16[128,1152]{1,0:T(8,128)(2...) custom-call(s32[4]{0:T(128)S(1)} %pad_add_fusion.refs_0_, ...), custom_call_target="tpu_custom_call" | custom-call | flops 1879048192 | bytes 7340032 | tf_op jit(solution)/shard_map/back_rows/pallas_call | solution.py:293
  57.9 0.2 collective-permute-start.20
  58.1 1.3 %collective-permute-start.18 = (bf16[128,1152]{1,0:T(8,128)(2,1)S(1)}, bf16[128,1152]{1,0:T(8,128)(2,1)S(1)}, u32[]{:S(2)}, u32[]{:S(2)}) collective-permute-start(bf16[128,1152]{1,0:T(8,128)(2,1)S(1)} %get-tuple-element.79), channel_id=1, source_target_pairs={{0,16},{1,17},{2,18},{3,19},{4,20},{5,21},{6,22},{7,23},{8,24},{9,... | collective-permute-start | bytes 884744 | tf_op jit(solution)/shard_map/ppermute | solution.py:344
  59.4 1.5 %collective-permute-start.19 = (bf16[128,1152]{1,0:T(8,128)(2,1)S(1)}, bf16[128,1152]{1,0:T(8,128)(2,1)S(1)}, u32[]{:S(2)}, u32[]{:S(2)}) collective-permute-start(bf16[128,1152]{1,0:T(8,128)(2,1)S(1)} %get-tuple-element.80), channel_id=1, source_target_pairs={{0,1},{1,0},{2,3},{3,2},{4,5},{5,4},{6,7},{7,6},{8,9},{9,8},{10,11... | collective-permute-start | bytes 884744 | tf_op jit(solution)/shard_map/ppermute | solution.py:344
  61.0 7.2 %head_gradient.1 = bf16[3584,512]{1,0:T(8,128)(2,1)} custom-call(bf16[128,3584]{1,0:T(8,128)(2,1)S(1)} %copy-done.3, bf16[128,3584]{1,0:T(8,128)(2,1)S(1)} %get-tuple-element.72.r1, bf16[128,3584]{1,0:T(8,128)(2,1)} %collective-permute-done.15.r2, bf16[128,3584]{1,0:T(8,128)(2,1)} %collective-permute-done.16.r3, ...), custom_call_target="tpu_custom_call" | custom-call | flops 1879048192 | bytes 7340032 | tf_op jit(solution)/shard_map/head_gradient/pallas_call | solution.py:319
  68.3 1.6 %collective-permute-start.21 = (bf16[1,2,2,1,16,1152]{5,4,3,2,1,0:T(8,128)(2,1)S(1)}, bf16[1,2,2,1,16,1152]{5,4,3,2,1,0:T(8,128)(2,1)S(1)}, u32[]{:S(2)}, u32[]{:S(2)}) collective-permute-start(bf16[1,2,2,1,16,1152]{5,4,3,2,1,0:T(8,128)(2,1)S(1)} %fusion.1), channel_id=1, source_target_pairs={{0,1},{1,0},{2,3},{3,2},{4,5},{5,4},{6,7},{7,6},{8,9},{9,8},{10,11... | collective-permute-start | bytes 442376 | tf_op jit(solution)/shard_map/ppermute | solution.py:344
  70.0 1.6 %collective-permute-start.23 = (bf16[2,2,1,1,16,1152]{5,4,3,2,1,0:T(8,128)(2,1)S(1)}, bf16[2,2,1,1,16,1152]{5,4,3,2,1,0:T(8,128)(2,1)S(1)}, u32[]{:S(2)}, u32[]{:S(2)}) collective-permute-start(bf16[2,2,1,1,16,1152]{5,4,3,2,1,0:T(8,128)(2,1)S(1)} %fusion), channel_id=1, source_target_pairs={{0,2},{1,3},{2,0},{3,1},{4,6},{5,7},{6,4},{7,5},{8,10},{9,11},{10,... | collective-permute-start | bytes 442376 | tf_op jit(solution)/shard_map/ppermute | solution.py:344
  71.6 1.0 %collective-permute-start.25 = (bf16[1,2,1,2,16,1280]{5,4,3,2,1,0:T(8,128)(2,1)S(1)}, bf16[1,2,1,2,16,1280]{5,4,3,2,1,0:T(8,128)(2,1)S(1)}, u32[]{:S(2)}, u32[]{:S(2)}) collective-permute-start(bf16[1,2,1,2,16,1280]{5,4,3,2,1,0:T(8,128)(2,1)S(1)} %bitcast.53), channel_id=1, source_target_pairs={{0,16},{1,17},{2,18},{3,19},{4,20},{5,21},{6,22},{7,23},{8,24},{9,... | collective-permute-start | bytes 491528 | tf_op jit(solution)/shard_map/ppermute | solution.py:344
  72.6 1.1 %collective-permute-done.21 = bf16[1,2,2,1,16,1152]{5,4,3,2,1,0:T(8,128)(2,1)S(1)} collective-permute-done((bf16[1,2,2,1,16,1152]{5,4,3,2,1,0:T(8,128)(2,1)S(1)}, bf16[1,2,2,1,16,1152]{5,4,3,2,1,0:T(8,128)(2,1)S(1)}, u32[]{:S(2)}, u32[]{:S(2)}) %collective-permute-start.21) | collective-permute-done | bytes 147488 | tf_op jit(solution)/shard_map/ppermute | solution.py:344
  73.7 1.6 %collective-permute-start.22 = (bf16[1,2,1,1,16,1152]{5,4,3,2,1,0:T(8,128)(2,1)S(1)}, bf16[1,2,1,1,16,1152]{5,4,3,2,1,0:T(8,128)(2,1)S(1)}, u32[]{:S(2)}, u32[]{:S(2)}) collective-permute-start(bf16[1,2,1,1,16,1152]{5,4,3,2,1,0:T(8,128)(2,1)S(1)} %fusion.12), channel_id=1, source_target_pairs={{0,2},{1,3},{2,0},{3,1},{4,6},{5,7},{6,4},{7,5},{8,10},{9,11},{10,... | collective-permute-start | bytes 221192 | tf_op jit(solution)/shard_map/ppermute | solution.py:344
  75.4 1.0 %collective-permute-start.24 = (bf16[1,2,1,1,16,1152]{5,4,3,2,1,0:T(8,128)(2,1)S(1)}, bf16[1,2,1,1,16,1152]{5,4,3,2,1,0:T(8,128)(2,1)S(1)}, u32[]{:S(2)}, u32[]{:S(2)}) collective-permute-start(bf16[1,2,1,1,16,1152]{5,4,3,2,1,0:T(8,128)(2,1)S(1)} %fusion.8), channel_id=1, source_target_pairs={{0,16},{1,17},{2,18},{3,19},{4,20},{5,21},{6,22},{7,23},{8,24},{9,... | collective-permute-start | bytes 221192 | tf_op jit(solution)/shard_map/ppermute | solution.py:344
  76.4 0.9 %collective-permute-done.25 = bf16[1,2,1,2,16,1280]{5,4,3,2,1,0:T(8,128)(2,1)S(1)} collective-permute-done((bf16[1,2,1,2,16,1280]{5,4,3,2,1,0:T(8,128)(2,1)S(1)}, bf16[1,2,1,2,16,1280]{5,4,3,2,1,0:T(8,128)(2,1)S(1)}, u32[]{:S(2)}, u32[]{:S(2)}) %collective-permute-start.25) | collective-permute-done | bytes 163872 | tf_op jit(solution)/shard_map/ppermute | solution.py:344
  77.4 0.5 collective-permute-start.26
  77.9 0.2 collective-permute-done.22
  78.2 1.6 %collective-permute-done.24 = bf16[1,2,1,1,16,1152]{5,4,3,2,1,0:T(8,128)(2,1)S(1)} collective-permute-done((bf16[1,2,1,1,16,1152]{5,4,3,2,1,0:T(8,128)(2,1)S(1)}, bf16[1,2,1,1,16,1152]{5,4,3,2,1,0:T(8,128)(2,1)S(1)}, u32[]{:S(2)}, u32[]{:S(2)}) %collective-permute-start.24) | collective-permute-done | bytes 73760 | tf_op jit(solution)/shard_map/ppermute | solution.py:344
  79.8 2.1 %collective-permute-done.26 = bf16[1,2,1,1,16,1280]{5,4,3,2,1,0:T(8,128)(2,1)S(1)} collective-permute-done((bf16[1,2,1,1,16,1280]{5,4,3,2,1,0:T(8,128)(2,1)S(1)}, bf16[1,2,1,1,16,1280]{5,4,3,2,1,0:T(8,128)(2,1)S(1)}, u32[]{:S(2)}, u32[]{:S(2)}) %collective-permute-start.26) | collective-permute-done | bytes 81952 | tf_op jit(solution)/shard_map/ppermute | solution.py:344
  82.0 2.1 %collective-permute-start.27 = (bf16[1,1,1,1,16,3584]{5,4,3,2,1,0:T(8,128)(2,1)S(1)}, bf16[1,1,1,1,16,3584]{5,4,3,2,1,0:T(8,128)(2,1)S(1)}, u32[]{:S(2)}, u32[]{:S(2)}) collective-permute-start(bf16[1,1,1,1,16,3584]{5,4,3,2,1,0:T(8,128)(2,1)S(1)} %slice.215), channel_id=1, source_target_pairs={{0,4},{1,5},{2,6},{3,7},{4,0},{5,1},{6,2},{7,3},{8,12},{9,13},{10,... | collective-permute-start | bytes 344072 | tf_op jit(solution)/shard_map/ppermute | solution.py:344
  84.1 4.9 %collective-permute-done.27 = bf16[1,1,1,1,16,3584]{5,4,3,2,1,0:T(8,128)(2,1)S(1)} collective-permute-done((bf16[1,1,1,1,16,3584]{5,4,3,2,1,0:T(8,128)(2,1)S(1)}, bf16[1,1,1,1,16,3584]{5,4,3,2,1,0:T(8,128)(2,1)S(1)}, u32[]{:S(2)}, u32[]{:S(2)}) %collective-permute-start.27) | collective-permute-done | bytes 114720 | tf_op jit(solution)/shard_map/ppermute | solution.py:344
  89.0 0.7 fusion.2
  (54 shorter events, 0.7 us)
Async XLA Ops:
  0.6 6.7 %copy-start.3 = (bf16[128,3584]{1,0:T(8,128)(2,1)S(1)}, bf16[128,3584]{1,0:T(8,128)(2,1)}, u32[]{:S(2)}) copy-start(bf16[128,3584]{1,0:T(8,128)(2,1)} %r0.1) | copy-start | bytes 2752516
  0.6 16.4 %collective-permute-start.4 = (bf16[3584,512]{1,0:T(8,128)(2,1)}, bf16[3584,512]{1,0:T(8,128)(2,1)}, u32[]{:S(2)}, u32[]{:S(2)}) collective-permute-start(bf16[3584,512]{1,0:T(8,128)(2,1)} %refs_1_.1), channel_id=1, source_target_pairs={{0,8},{1,9},{2,10},{3,11},{4,12},{5,13},{6,14},{7,15},{8,0},{9,1},... | collective-permute-start | bytes 11010056 | tf_op jit(solution)/shard_map/ppermute | solution.py:344
  2.1 11.2 %collective-permute-start = (bf16[32,3584]{1,0:T(8,128)(2,1)S(1)}, bf16[32,3584]{1,0:T(8,128)(2,1)S(1)}, u32[]{:S(2)}, u32[]{:S(2)}) collective-permute-start(bf16[32,3584]{1,0:T(8,128)(2,1)S(1)} %constant_dynamic-slice_fusion.1), channel_id=1, source_target_pairs={{0,16},{1,17},{2,18},{3,19},{4,20},{5,21},{6,22},{7,23},{8,24},{9,... | collective-permute-start | bytes 688136 | tf_op jit(solution)/shard_map/ppermute | solution.py:344
  7.3 2.1 %copy-start.4 = (bf16[3584,512]{1,0:T(8,128)(2,1)S(1)}, bf16[3584,512]{1,0:T(8,128)(2,1)}, u32[]{:S(2)}) copy-start(bf16[3584,512]{1,0:T(8,128)(2,1)} %refs_1_.1) | copy-start | bytes 11010052
  9.4 16.5 %copy-start.16 = (s32[128]{0:T(128)S(1)}, s32[128]{0:T(128)}, u32[]{:S(2)}) copy-start(s32[128]{0:T(128)} %param.6) | copy-start | bytes 1540
  11.4 1.8 %copy-start = (bf16[3584,512]{1,0:T(8,128)(2,1)}, bf16[3584,512]{1,0:T(8,128)(2,1)S(1)}, u32[]{:S(2)}) copy-start(bf16[3584,512]{1,0:T(8,128)(2,1)S(1)} %get-tuple-element.58.own_ref.refs_8_.refs_11_) | copy-start | bytes 11010052
  13.3 12.5 %copy-start.5 = (bf16[32,3584]{1,0:T(8,128)(2,1)}, bf16[32,3584]{1,0:T(8,128)(2,1)S(1)}, u32[]{:S(2)}) copy-start(bf16[32,3584]{1,0:T(8,128)(2,1)S(1)} %collective-permute-done.held_ref.x0) | copy-start | bytes 688132
  13.3 10.3 %collective-permute-start.5 = (bf16[2,128,512]{2,1,0:T(8,128)(2,1)S(1)}, bf16[2,128,512]{2,1,0:T(8,128)(2,1)S(1)}, u32[]{:S(2)}, u32[]{:S(2)}) collective-permute-start(bf16[2,128,512]{2,1,0:T(8,128)(2,1)S(1)} %get-tuple-element.53.kept_ref.a0), channel_id=1, source_target_pairs={{0,8},{1,9},{2,10},{3,11},{4,12},{5,13},{6,14},{7,15},{8,0},{9,1},... | collective-permute-start | bytes 786440 | tf_op jit(solution)/shard_map/ppermute | solution.py:344
  13.4 7.9 %collective-permute-start.3 = (bf16[32,3584]{1,0:T(8,128)(2,1)S(1)}, bf16[32,3584]{1,0:T(8,128)(2,1)S(1)}, u32[]{:S(2)}, u32[]{:S(2)}) collective-permute-start(bf16[32,3584]{1,0:T(8,128)(2,1)S(1)} %constant_dynamic-slice_fusion), channel_id=1, source_target_pairs={{0,16},{1,17},{2,18},{3,19},{4,20},{5,21},{6,22},{7,23},{8,24},{9,... | collective-permute-start | bytes 688136 | tf_op jit(solution)/shard_map/ppermute | solution.py:344
  13.7 8.3 %collective-permute-start.2 = (bf16[32,3584]{1,0:T(8,128)(2,1)S(1)}, bf16[32,3584]{1,0:T(8,128)(2,1)S(1)}, u32[]{:S(2)}, u32[]{:S(2)}) collective-permute-start(bf16[32,3584]{1,0:T(8,128)(2,1)S(1)} %collective-permute-done.held_ref.x0), channel_id=1, source_target_pairs={{0,2},{1,3},{2,0},{3,1},{4,6},{5,7},{6,4},{7,5},{8,10},{9,11},{10,... | collective-permute-start | bytes 688136 | tf_op jit(solution)/shard_map/ppermute | solution.py:344
  15.6 7.3 %collective-permute-start.1 = (bf16[32,3584]{1,0:T(8,128)(2,1)S(1)}, bf16[32,3584]{1,0:T(8,128)(2,1)S(1)}, u32[]{:S(2)}, u32[]{:S(2)}) collective-permute-start(bf16[32,3584]{1,0:T(8,128)(2,1)S(1)} %collective-permute-done.held_ref.x0), channel_id=1, source_target_pairs={{0,1},{1,0},{2,3},{3,2},{4,5},{5,4},{6,7},{7,6},{8,9},{9,8},{10,11... | collective-permute-start | bytes 688136 | tf_op jit(solution)/shard_map/ppermute | solution.py:344
  17.1 2.9 %collective-permute-start.6 = (f32[8,128]{1,0:T(8,128)S(1)}, f32[8,128]{1,0:T(8,128)S(1)}, u32[]{:S(2)}, u32[]{:S(2)}) collective-permute-start(f32[8,128]{1,0:T(8,128)S(1)} %taught_stats.1.taught_ref), channel_id=1, source_target_pairs={{0,8},{1,9},{2,10},{3,11},{4,12},{5,13},{6,14},{7,15},{8,0},{9,1},... | collective-permute-start | bytes 12296 | tf_op jit(solution)/shard_map/ppermute | solution.py:344
  21.3 0.7 copy-start.9
  22.0 0.7 copy-start.11
  22.9 0.7 copy-start.13
  23.5 0.7 copy-start.7
  24.3 16.6 %collective-permute-start.13 = (bf16[2,128,512]{2,1,0:T(8,128)(2,1)S(1)}, bf16[2,128,512]{2,1,0:T(8,128)(2,1)}, u32[]{:S(2)}, u32[]{:S(2)}) collective-permute-start(bf16[2,128,512]{2,1,0:T(8,128)(2,1)S(1)} %get-tuple-element.68.gone_ref), channel_id=1, source_target_pairs={{0,16},{1,17},{2,18},{3,19},{4,20},{5,21},{6,22},{7,23},{8,24},{9,... | collective-permute-start | bytes 786440 | tf_op jit(solution)/shard_map/ppermute | solution.py:344
  25.8 2.0 %copy-start.1 = (bf16[3584,512]{1,0:T(8,128)(2,1)S(1)}, bf16[3584,512]{1,0:T(8,128)(2,1)}, u32[]{:S(2)}) copy-start(bf16[3584,512]{1,0:T(8,128)(2,1)} %copy-done) | copy-start | bytes 11010052
  27.9 0.9 %copy-start.6 = (bf16[32,3584]{1,0:T(8,128)(2,1)S(1)}, bf16[32,3584]{1,0:T(8,128)(2,1)}, u32[]{:S(2)}) copy-start(bf16[32,3584]{1,0:T(8,128)(2,1)} %copy-done.5) | copy-start | bytes 688132
  28.8 0.9 %copy-start.10 = (bf16[32,3584]{1,0:T(8,128)(2,1)S(1)}, bf16[32,3584]{1,0:T(8,128)(2,1)}, u32[]{:S(2)}) copy-start(bf16[32,3584]{1,0:T(8,128)(2,1)} %copy-done.9) | copy-start | bytes 688132
  29.8 0.9 %copy-start.12 = (bf16[32,3584]{1,0:T(8,128)(2,1)S(1)}, bf16[32,3584]{1,0:T(8,128)(2,1)}, u32[]{:S(2)}) copy-start(bf16[32,3584]{1,0:T(8,128)(2,1)} %copy-done.11) | copy-start | bytes 688132
  30.7 0.9 %copy-start.14 = (bf16[32,3584]{1,0:T(8,128)(2,1)S(1)}, bf16[32,3584]{1,0:T(8,128)(2,1)}, u32[]{:S(2)}) copy-start(bf16[32,3584]{1,0:T(8,128)(2,1)} %copy-done.13) | copy-start | bytes 688132
  35.1 11.0 %copy-start.15 = (s32[512]{0:T(512)S(1)}, s32[512]{0:T(512)}, u32[]{:S(2)}) copy-start(s32[512]{0:T(512)} %param.7) | copy-start | bytes 6148
  35.1 4.6 %collective-permute-start.9 = (f32[2,8,128]{2,1,0:T(8,128)S(1)}, f32[2,8,128]{2,1,0:T(8,128)S(1)}, u32[]{:S(2)}, u32[]{:S(2)}) collective-permute-start(f32[2,8,128]{2,1,0:T(8,128)S(1)} %get-tuple-element.62.refs_0_), channel_id=1, source_target_pairs={{0,17},{1,16},{2,19},{3,18},{4,21},{5,20},{6,23},{7,22},{8,25},{9,... | collective-permute-start | bytes 24584 | tf_op jit(solution)/shard_map/ppermute | solution.py:344
  36.7 3.7 %collective-permute-start.8 = (f32[2,8,128]{2,1,0:T(8,128)S(1)}, f32[2,8,128]{2,1,0:T(8,128)S(1)}, u32[]{:S(2)}, u32[]{:S(2)}) collective-permute-start(f32[2,8,128]{2,1,0:T(8,128)S(1)} %get-tuple-element.62.refs_0_), channel_id=1, source_target_pairs={{0,1},{1,0},{2,3},{3,2},{4,5},{5,4},{6,7},{7,6},{8,9},{9,8},{10,11... | collective-permute-start | bytes 24584 | tf_op jit(solution)/shard_map/ppermute | solution.py:344
  37.2 3.7 %collective-permute-start.7 = (f32[2,8,128]{2,1,0:T(8,128)S(1)}, f32[2,8,128]{2,1,0:T(8,128)S(1)}, u32[]{:S(2)}, u32[]{:S(2)}) collective-permute-start(f32[2,8,128]{2,1,0:T(8,128)S(1)} %get-tuple-element.62.refs_0_), channel_id=1, source_target_pairs={{0,16},{1,17},{2,18},{3,19},{4,20},{5,21},{6,22},{7,23},{8,24},{9,... | collective-permute-start | bytes 24584 | tf_op jit(solution)/shard_map/ppermute | solution.py:344
  40.9 7.9 %collective-permute-start.15 = (bf16[128,3584]{1,0:T(8,128)(2,1)S(1)}, bf16[128,3584]{1,0:T(8,128)(2,1)}, u32[]{:S(2)}, u32[]{:S(2)}) collective-permute-start(bf16[128,3584]{1,0:T(8,128)(2,1)S(1)} %copy-done.3), channel_id=1, source_target_pairs={{0,8},{1,9},{2,10},{3,11},{4,12},{5,13},{6,14},{7,15},{8,0},{9,1},... | collective-permute-start | bytes 2752520 | tf_op jit(solution)/shard_map/ppermute | solution.py:344
  41.0 7.8 %collective-permute-start.16 = (bf16[128,3584]{1,0:T(8,128)(2,1)S(1)}, bf16[128,3584]{1,0:T(8,128)(2,1)}, u32[]{:S(2)}, u32[]{:S(2)}) collective-permute-start(bf16[128,3584]{1,0:T(8,128)(2,1)S(1)} %get-tuple-element.72.r1), channel_id=1, source_target_pairs={{0,8},{1,9},{2,10},{3,11},{4,12},{5,13},{6,14},{7,15},{8,0},{9,1},... | collective-permute-start | bytes 2752520 | tf_op jit(solution)/shard_map/ppermute | solution.py:344
  41.5 3.7 %collective-permute-start.14 = (bf16[2,128,512]{2,1,0:T(8,128)(2,1)}, bf16[2,128,512]{2,1,0:T(8,128)(2,1)S(1)}, u32[]{:S(2)}, u32[]{:S(2)}) collective-permute-start(bf16[2,128,512]{2,1,0:T(8,128)(2,1)} %collective-permute-done.13.a2), channel_id=1, source_target_pairs={{0,8},{1,9},{2,10},{3,11},{4,12},{5,13},{6,14},{7,15},{8,0},{9,1},... | collective-permute-start | bytes 786440 | tf_op jit(solution)/shard_map/ppermute | solution.py:344
  41.7 7.1 %collective-permute-start.12 = (f32[2,8,128]{2,1,0:T(8,128)S(1)}, f32[2,8,128]{2,1,0:T(8,128)S(1)}, u32[]{:S(2)}, u32[]{:S(2)}) collective-permute-start(f32[2,8,128]{2,1,0:T(8,128)S(1)} %merge_stats.1.refs_1_), channel_id=1, source_target_pairs={{0,6},{1,7},{2,4},{3,5},{4,2},{5,3},{6,0},{7,1},{8,14},{9,15},{10,... | collective-permute-start | bytes 24584 | tf_op jit(solution)/shard_map/ppermute | solution.py:344
  45.2 4.5 %collective-permute-start.11 = (f32[2,8,128]{2,1,0:T(8,128)S(1)}, f32[2,8,128]{2,1,0:T(8,128)S(1)}, u32[]{:S(2)}, u32[]{:S(2)}) collective-permute-start(f32[2,8,128]{2,1,0:T(8,128)S(1)} %merge_stats.1.refs_1_), channel_id=1, source_target_pairs={{0,4},{1,5},{2,6},{3,7},{4,0},{5,1},{6,2},{7,3},{8,12},{9,13},{10,... | collective-permute-start | bytes 24584 | tf_op jit(solution)/shard_map/ppermute | solution.py:344
  45.2 4.5 %collective-permute-start.10 = (f32[2,8,128]{2,1,0:T(8,128)S(1)}, f32[2,8,128]{2,1,0:T(8,128)S(1)}, u32[]{:S(2)}, u32[]{:S(2)}) collective-permute-start(f32[2,8,128]{2,1,0:T(8,128)S(1)} %merge_stats.1.refs_1_), channel_id=1, source_target_pairs={{0,2},{1,3},{2,0},{3,1},{4,6},{5,7},{6,4},{7,5},{8,10},{9,11},{10,... | collective-permute-start | bytes 24584 | tf_op jit(solution)/shard_map/ppermute | solution.py:344
  46.1 1.0 %copy-start.8 = (bf16[2,128,512]{2,1,0:T(8,128)(2,1)S(1)}, bf16[2,128,512]{2,1,0:T(8,128)(2,1)}, u32[]{:S(2)}) copy-start(bf16[2,128,512]{2,1,0:T(8,128)(2,1)} %copy-done.7) | copy-start | bytes 786436
  49.7 2.0 %copy-start.2 = (bf16[3584,512]{1,0:T(8,128)(2,1)S(1)}, bf16[3584,512]{1,0:T(8,128)(2,1)}, u32[]{:S(2)}) copy-start(bf16[3584,512]{1,0:T(8,128)(2,1)} %copy-done) | copy-start | bytes 11010052
  57.8 3.2 %collective-permute-start.17 = (bf16[256,512]{1,0:T(8,128)(2,1)S(1)}, bf16[256,512]{1,0:T(8,128)(2,1)S(1)}, u32[]{:S(2)}, u32[]{:S(2)}) collective-permute-start(bf16[256,512]{1,0:T(8,128)(2,1)S(1)} %get-tuple-element.78), channel_id=1, source_target_pairs={{0,8},{1,9},{2,10},{3,11},{4,12},{5,13},{6,14},{7,15},{8,0},{9,1},... | collective-permute-start | bytes 786440 | tf_op jit(solution)/shard_map/ppermute | solution.py:344
  57.9 10.4 %collective-permute-start.20 = (bf16[128,1280]{1,0:T(8,128)(2,1)S(1)}, bf16[128,1280]{1,0:T(8,128)(2,1)S(1)}, u32[]{:S(2)}, u32[]{:S(2)}) collective-permute-start(bf16[128,1280]{1,0:T(8,128)(2,1)S(1)} %get-tuple-element.81), channel_id=1, source_target_pairs={{0,2},{1,3},{2,0},{3,1},{4,6},{5,7},{6,4},{7,5},{8,10},{9,11},{10,... | collective-permute-start | bytes 983048 | tf_op jit(solution)/shard_map/ppermute | solution.py:344
  58.1 10.1 %collective-permute-start.18 = (bf16[128,1152]{1,0:T(8,128)(2,1)S(1)}, bf16[128,1152]{1,0:T(8,128)(2,1)S(1)}, u32[]{:S(2)}, u32[]{:S(2)}) collective-permute-start(bf16[128,1152]{1,0:T(8,128)(2,1)S(1)} %get-tuple-element.79), channel_id=1, source_target_pairs={{0,16},{1,17},{2,18},{3,19},{4,20},{5,21},{6,22},{7,23},{8,24},{9,... | collective-permute-start | bytes 884744 | tf_op jit(solution)/shard_map/ppermute | solution.py:344
  59.4 8.8 %collective-permute-start.19 = (bf16[128,1152]{1,0:T(8,128)(2,1)S(1)}, bf16[128,1152]{1,0:T(8,128)(2,1)S(1)}, u32[]{:S(2)}, u32[]{:S(2)}) collective-permute-start(bf16[128,1152]{1,0:T(8,128)(2,1)S(1)} %get-tuple-element.80), channel_id=1, source_target_pairs={{0,1},{1,0},{2,3},{3,2},{4,5},{5,4},{6,7},{7,6},{8,9},{9,8},{10,11... | collective-permute-start | bytes 884744 | tf_op jit(solution)/shard_map/ppermute | solution.py:344
  68.3 5.4 %collective-permute-start.21 = (bf16[1,2,2,1,16,1152]{5,4,3,2,1,0:T(8,128)(2,1)S(1)}, bf16[1,2,2,1,16,1152]{5,4,3,2,1,0:T(8,128)(2,1)S(1)}, u32[]{:S(2)}, u32[]{:S(2)}) collective-permute-start(bf16[1,2,2,1,16,1152]{5,4,3,2,1,0:T(8,128)(2,1)S(1)} %fusion.1), channel_id=1, source_target_pairs={{0,1},{1,0},{2,3},{3,2},{4,5},{5,4},{6,7},{7,6},{8,9},{9,8},{10,11... | collective-permute-start | bytes 442376 | tf_op jit(solution)/shard_map/ppermute | solution.py:344
  70.0 5.4 %collective-permute-start.23 = (bf16[2,2,1,1,16,1152]{5,4,3,2,1,0:T(8,128)(2,1)S(1)}, bf16[2,2,1,1,16,1152]{5,4,3,2,1,0:T(8,128)(2,1)S(1)}, u32[]{:S(2)}, u32[]{:S(2)}) collective-permute-start(bf16[2,2,1,1,16,1152]{5,4,3,2,1,0:T(8,128)(2,1)S(1)} %fusion), channel_id=1, source_target_pairs={{0,2},{1,3},{2,0},{3,1},{4,6},{5,7},{6,4},{7,5},{8,10},{9,11},{10,... | collective-permute-start | bytes 442376 | tf_op jit(solution)/shard_map/ppermute | solution.py:344
  71.6 5.8 %collective-permute-start.25 = (bf16[1,2,1,2,16,1280]{5,4,3,2,1,0:T(8,128)(2,1)S(1)}, bf16[1,2,1,2,16,1280]{5,4,3,2,1,0:T(8,128)(2,1)S(1)}, u32[]{:S(2)}, u32[]{:S(2)}) collective-permute-start(bf16[1,2,1,2,16,1280]{5,4,3,2,1,0:T(8,128)(2,1)S(1)} %bitcast.53), channel_id=1, source_target_pairs={{0,16},{1,17},{2,18},{3,19},{4,20},{5,21},{6,22},{7,23},{8,24},{9,... | collective-permute-start | bytes 491528 | tf_op jit(solution)/shard_map/ppermute | solution.py:344
  73.7 4.4 %collective-permute-start.22 = (bf16[1,2,1,1,16,1152]{5,4,3,2,1,0:T(8,128)(2,1)S(1)}, bf16[1,2,1,1,16,1152]{5,4,3,2,1,0:T(8,128)(2,1)S(1)}, u32[]{:S(2)}, u32[]{:S(2)}) collective-permute-start(bf16[1,2,1,1,16,1152]{5,4,3,2,1,0:T(8,128)(2,1)S(1)} %fusion.12), channel_id=1, source_target_pairs={{0,2},{1,3},{2,0},{3,1},{4,6},{5,7},{6,4},{7,5},{8,10},{9,11},{10,... | collective-permute-start | bytes 221192 | tf_op jit(solution)/shard_map/ppermute | solution.py:344
  75.4 4.4 %collective-permute-start.24 = (bf16[1,2,1,1,16,1152]{5,4,3,2,1,0:T(8,128)(2,1)S(1)}, bf16[1,2,1,1,16,1152]{5,4,3,2,1,0:T(8,128)(2,1)S(1)}, u32[]{:S(2)}, u32[]{:S(2)}) collective-permute-start(bf16[1,2,1,1,16,1152]{5,4,3,2,1,0:T(8,128)(2,1)S(1)} %fusion.8), channel_id=1, source_target_pairs={{0,16},{1,17},{2,18},{3,19},{4,20},{5,21},{6,22},{7,23},{8,24},{9,... | collective-permute-start | bytes 221192 | tf_op jit(solution)/shard_map/ppermute | solution.py:344
  77.4 4.5 %collective-permute-start.26 = (bf16[1,2,1,1,16,1280]{5,4,3,2,1,0:T(8,128)(2,1)S(1)}, bf16[1,2,1,1,16,1280]{5,4,3,2,1,0:T(8,128)(2,1)S(1)}, u32[]{:S(2)}, u32[]{:S(2)}) collective-permute-start(bf16[1,2,1,1,16,1280]{5,4,3,2,1,0:T(8,128)(2,1)S(1)} %fusion.4), channel_id=1, source_target_pairs={{0,1},{1,0},{2,3},{3,2},{4,5},{5,4},{6,7},{7,6},{8,9},{9,8},{10,11... | collective-permute-start | bytes 245768 | tf_op jit(solution)/shard_map/ppermute | solution.py:344
  82.0 7.0 %collective-permute-start.27 = (bf16[1,1,1,1,16,3584]{5,4,3,2,1,0:T(8,128)(2,1)S(1)}, bf16[1,1,1,1,16,3584]{5,4,3,2,1,0:T(8,128)(2,1)S(1)}, u32[]{:S(2)}, u32[]{:S(2)}) collective-permute-start(bf16[1,1,1,1,16,3584]{5,4,3,2,1,0:T(8,128)(2,1)S(1)} %slice.215), channel_id=1, source_target_pairs={{0,4},{1,5},{2,6},{3,7},{4,0},{5,1},{6,2},{7,3},{8,12},{9,13},{10,... | collective-permute-start | bytes 344072 | tf_op jit(solution)/shard_map/ppermute | solution.py:344

commit v7 on v6

--- a/solution.py
+++ b/solution.py
@@ -52,7 +52,7 @@
         out_shape=shape((STAT_ROWS, per), F32),
         in_specs=[VMEM] * 2,
         out_specs=VMEM,
-        compiler_params=params(6),
+        compiler_params=params(4),
         cost_estimate=cost(0, 4 * per * cols * 2, 4 * per * cols),
         name="taught_stats",
     )(kept, gone)
@@ -82,7 +82,7 @@
         out_shape=shape((2, per, 2 * cols), BF16),
         in_specs=[SMEM] + [VMEM] * 5,
         out_specs=VMEM,
-        compiler_params=params(10),
+        compiler_params=params(5),
         cost_estimate=cost(32 * per * per * cols, 12 * per * cols * 2),
         name="teacher_rows",
     )(at, serving, *arrived)
@@ -125,7 +125,7 @@
         in_specs=[VMEM, pl.BlockSpec(memory_space=pl.ANY)],
         out_specs=(VMEM, VMEM, VMEM),
         scratch_shapes=[pltpu.SemaphoreType.DMA((splits,))],
-        compiler_params=params(10),
+        compiler_params=params(6),
         cost_estimate=cost(2 * per * depth * cols, (per + 2 * cols) * depth * 2, per * cols),
         name="own_logits",
     )(rows, own)
@@ -145,7 +145,7 @@
         out_shape=(shape((per, cols), F32), shape((STAT_ROWS, per), F32)),
         in_specs=[VMEM] * 3,
         out_specs=(VMEM, VMEM),
-        compiler_params=params(10),
+        compiler_params=params(6),
         cost_estimate=cost(2 * per * depth * cols, (per + cols) * depth * 2, per * cols),
         name="core_logits",
     )(rows, other, held)
@@ -193,7 +193,7 @@
         ),
         in_specs=[SMEM] + [VMEM] * 11,
         out_specs=(VMEM, VMEM, VMEM, VMEM),
-        compiler_params=params(20),
+        compiler_params=params(11),
         cost_estimate=cost(4 * per * depth * cols, (per + 2 * cols) * depth * 2, 2 * per * cols),
         name="far_logits",
     )(spots, *pieces, own, other, stats_a, stats_b, taught, taught_core, ids)
@@ -226,7 +226,7 @@
         out_shape=shape(parts[0].shape, F32),
         in_specs=[VMEM] * (len(parts) + len(held)),
         out_specs=VMEM,
-        compiler_params=params(14),
+        compiler_params=params(6),
         cost_estimate=cost(0, 5 * parts[0].size * 4),
         name="merge_stats",
     )(*parts, *held)
@@ -295,7 +295,7 @@
         out_shape=[shape((2 * per, cols), BF16)] * 2 + sends + keeps,
         in_specs=[SMEM] + [VMEM] * (len(stats) + 8),
         out_specs=[VMEM] * 8,
-        compiler_params=params(24),
+        compiler_params=params(18),
         cost_estimate=cost(8 * per * depth * cols, 2 * cols * depth * 2, 4 * per * cols),
         name="back_rows",
     )(at, *stats, *logits, serving, aligned, own, other)
@@ -322,7 +322,7 @@
         out_shape=shape((depth, cols), BF16),
         in_specs=[slab] * 4 + [whole] * 2,
         out_specs=pl.BlockSpec((tile, cols), lambda i: (i, 0)),
-        compiler_params=params(12),
+        compiler_params=params(6),
         cost_estimate=cost(8 * per * depth * cols, (4 * per + cols) * depth * 2),
         name="head_gradient",
     )(*rows, mine, theirs)
@@ -353,6 +353,7 @@
     quarter = me_v & 3
     starts = [(quarter ^ k) * quarter_rows for k in range(4)]
     other_weight = swap(head_weight, CORE)
+    core_hidden = swap(hidden, CORE)
     first = lax.dynamic_slice_in_dim(hidden, starts[0], quarter_rows, 0)
     x0 = swap(first, X)
     _, rows, teacher = tie(first, hidden, teacher_logits)
@@ -371,8 +372,8 @@
     taught_core = swap(taught, CORE)
     kept_core = swap(kept, CORE)
     near_b, stats_b = core_logits(rows, other_weight, x0)
-    x1, x2, x3, gone, near_b, kept_core, taught_core = tie(
-        x1, x2, x3, gone, near_b, kept_core, taught_core
+    x1, x2, x3, gone, near_b, kept_core, core_hidden = tie(
+        x1, x2, x3, gone, near_b, kept_core, core_hidden
     )
     taught_x = swap(gone, X)
     far_a, far_b, x_rows, stats = far_logits(
@@ -388,15 +389,16 @@
     )
 
     served = serving.reshape(groups, 1, per)
+    _, taught_x = tie(stats, taught_x)
+    taught_far = swap(taught_x, CORE)
     logits = [near_a, near_b, far_a, far_b]
     held = logits + [own_weight]
     stats = merge([stats, swap(stats, X), swap(stats, Y), swap(stats, X + Y)], (0, 1, 0, 1), held)
-    _, taught_x, rows, x_sent = tie(stats, taught_x, rows, x_rows)
-    core_rows = [swap(rows, CORE), swap(x_sent, CORE)]
+    _, taught_far = tie(stats, taught_far)
     aligned = teacher_rows(
-        ints(me_g, me_g & 1), served, [kept, kept_core, taught_x, swap(taught_x, CORE)]
-    )
-    aligned, *core_rows = tie(aligned, *core_rows)
+        ints(me_g, me_g & 1), served, [kept, kept_core, taught_x, taught_far]
+    )
+    core_x = swap(x_rows, CORE)
     mask = W
     while True:
         masks = [mask, 2 * mask, 3 * mask] if 2 * mask < shards else [mask]
@@ -425,7 +427,7 @@
     )
     gots = [swap(sents[p], masks[orders[p][0]]) for p in range(3)]
     theirs = swap(gother, CORE)
-    grad_head = head_gradient([hidden, x_rows] + core_rows, gown, theirs)
+    grad_head = head_gradient([hidden, x_rows, core_hidden, core_x], gown, theirs)
     grad_head, *gots = tie(grad_head, *gots)
 
     def folded(value, p):
@@ -442,10 +444,11 @@
         gots = [swap(sents[p], masks[orders[p][stage]]) for p in range(3)]
         for p in range(3):
             terms[p] = [lax.index_in_dim(t, 0, orders[p][stage]) for t in terms[p]] + [gots[p]]
+    for dim in range(1, wdim):
+        for p in range(3):
+            sent = sum(lax.index_in_dim(t, 1, dim).astype(F32) for t in terms[p]).astype(BF16)
+            terms[p] = [lax.index_in_dim(t, 0, dim) for t in terms[p]] + [swap(sent, masks[dim])]
     total = jnp.concatenate([sum(t.astype(F32) for t in ts) for ts in terms], axis=-1)
-    for dim in range(1, wdim):
-        got = swap(lax.index_in_dim(total, 1, dim).astype(BF16), masks[dim])
-        total = lax.index_in_dim(total, 0, dim) + got.astype(F32)
     return (total.reshape(owned, depth), grad_head)
 
 

time: 90.4 us -> 90.3 us (level)
  local copies, waits for them, and re-layouts: 18.6 us -> 13 us
  starting transfers between devices: 29.7 us -> 32.2 us
  waiting for transfers between devices: 15.4 us -> 17.4 us
  Pallas kernels: 23.8 us -> 25 us
    unnamed x34 -> x30, local copies, waits for them, and re-layouts: 15.5 us -> 9.26 us
    ppermute x28 -> x30, starting transfers between devices: 29.7 us -> 32.2 us  [swap(): return lax.ppermute(value, AXES, [(i, i ^ mask) for i in range(count)])]
    ppermute x28 -> x30, waiting for transfers between devices: 15.4 us -> 17.4 us  [swap(): return lax.ppermute(value, AXES, [(i, i ^ mask) for i in range(count)])]
    pallas_call x1, Pallas kernels: 3.46 us -> 4.51 us  [far_logits(): pl.pallas_call(far_kernel, out_shape=(shape((per, cols), F32), shape((per...]
  transfers between devices with their start and end apart: 28 -> 30, of which waited for: 12 -> 16; matrix products, arithmetic and copies ran while one was open for 4% -> 5% of each run, Pallas kernels for 20% -> 28%
where the time goes in v7:
time: 90.3 us; the launch traced here: 89.7 us
  starting transfers between devices  32.2 us (36%)
  Pallas kernels  25 us (28%)
  waiting for transfers between devices  17.4 us (19%)
  local copies, waits for them, and re-layouts  13 us (14%)
  other arithmetic  1.3 us (1%)
    ppermute x30, starting transfers between devices, swap(): return lax.ppermute(value, AXES, [(i, i ^ mask) for i in range(count)])  32.2 us
    ppermute x30, waiting for transfers between devices, swap(): return lax.ppermute(value, AXES, [(i, i ^ mask) for i in range(count)])  17.4 us
    unnamed x30, local copies, waits for them, and re-layouts  9.26 us
    pallas_call x1, Pallas kernels, head_gradient(): pl.pallas_call(head_kernel, grid=(depth // tile,), out_shape=shape((depth...  7.23 us
    pallas_call x1, Pallas kernels, back_rows(): pl.pallas_call(lambda *refs: back_kernel(bits, edges, len(stats), *refs),...  6.04 us
    pallas_call x1, Pallas kernels, far_logits(): pl.pallas_call(far_kernel, out_shape=(shape((per, cols), F32), shape((per...  4.51 us
    pallas_call x1, Pallas kernels, core_logits(): pl.pallas_call(core_kernel, out_shape=(shape((per, cols), F32), shape((ST...  3.05 us
    pallas_call x1, Pallas kernels, own_logits(): pl.pallas_call(lambda *refs: own_kernel(splits, *refs), out_shape=(shape(...  2.05 us
  transfers between devices with their start and end apart: 30, of which 16 were waited for; matrix products, arithmetic and copies ran while one was open for 5% of the time, Pallas kernels for 28%

profile of v7, /device:TPU:0, one launch (start us, length us, event | category | flops | bytes accessed | tf_op | source)
XLA Modules:
  0.0 89.7 jit_solution(8985436530238004381)
XLA Ops:
  0.6 0.5 collective-permute-start.4
  1.2 0.1 collective-permute-start.6
  1.2 1.0 %constant_dynamic-slice_fusion.1 = bf16[32,3584]{1,0:T(8,128)(2,1)S(1)} fusion(bf16[128,3584]{1,0:T(8,128)(2,1)} %r0.1, s32[]{:T(128)S(6)} %select_n.12), kind=kLoop, calls=%fused_computation.42 | loop fusion | bytes 458756 | tf_op jit(solution)/shard_map/dynamic_slice | solution.py:357
  2.2 3.0 %collective-permute-start = (bf16[32,3584]{1,0:T(8,128)(2,1)S(1)}, bf16[32,3584]{1,0:T(8,128)(2,1)S(1)}, u32[]{:S(2)}, u32[]{:S(2)}) collective-permute-start(bf16[32,3584]{1,0:T(8,128)(2,1)S(1)} %constant_dynamic-slice_fusion.1), channel_id=1, source_target_pairs={{0,16},{1,17},{2,18},{3,19},{4,20},{5,21},{6,22},{7,23},{8,24},{9,... | collective-permute-start | bytes 688136 | tf_op jit(solution)/shard_map/ppermute | solution.py:344
  5.2 1.6 %constant_dynamic-slice_fusion = bf16[32,3584]{1,0:T(8,128)(2,1)} fusion(bf16[128,3584]{1,0:T(8,128)(2,1)} %r0.1, s32[]{:T(128)S(6)} %select_n.13), kind=kLoop, calls=%fused_computation.41 | loop fusion | bytes 458756 | tf_op jit(solution)/shard_map/dynamic_slice | solution.py:360
  6.8 1.1 %copy.7 = bf16[128,4,512]{2,0,1:T(8,128)(2,1)S(1)} copy(bf16[128,4,512]{2,1,0:T(4,128)(2,1)} %param.9) | data formatting | bytes 1048576 | tf_op jit(solution)/shard_map/optimization_barrier | solution.py:347
  8.0 0.4 taught_stats.1.taught_ref
  8.4 2.1 %copy-done.5 = bf16[3584,512]{1,0:T(8,128)(2,1)S(1)} copy-done((bf16[3584,512]{1,0:T(8,128)(2,1)S(1)}, bf16[3584,512]{1,0:T(8,128)(2,1)}, u32[]{:S(2)}) %copy-start.5) | copy-done | bytes 3670040
  10.5 2.1 %own_logits.1 = (f32[128,512]{1,0:T(8,128)S(1)}, f32[8,128]{1,0:T(8,128)S(1)}, bf16[3584,512]{1,0:T(8,128)(2,1)S(1)}) custom-call(bf16[128,3584]{1,0:T(8,128)(2,1)S(1)} %copy-done.4, bf16[3584,512]{1,0:T(8,128)(2,1)S(1)} %copy-done.5), custom_call_target="tpu_custom_call" | custom-call | flops 469762048 | bytes 8257536 | tf_op jit(solution)/shard_map/own_logits/pallas_call | solution.py:118
  12.5 1.8 %copy-done = bf16[3584,512]{1,0:T(8,128)(2,1)} copy-done((bf16[3584,512]{1,0:T(8,128)(2,1)}, bf16[3584,512]{1,0:T(8,128)(2,1)S(1)}, u32[]{:S(2)}) %copy-start) | copy-done | bytes 3670040
  14.4 0.1 collective-permute-start.3
  14.5 0.1 collective-permute-start.5
  14.5 2.0 %collective-permute-start.2 = (bf16[32,3584]{1,0:T(8,128)(2,1)S(1)}, bf16[32,3584]{1,0:T(8,128)(2,1)}, u32[]{:S(2)}, u32[]{:S(2)}) collective-permute-start(bf16[32,3584]{1,0:T(8,128)(2,1)S(1)} %collective-permute-done.held_ref.x0), channel_id=1, source_target_pairs={{0,2},{1,3},{2,0},{3,1},{4,6},{5,7},{6,4},{7,5},{8,10},{9,11},{10,... | collective-permute-start | bytes 688136 | tf_op jit(solution)/shard_map/ppermute | solution.py:344
  16.6 5.2 %collective-permute-done.3.x3 = bf16[32,3584]{1,0:T(8,128)(2,1)S(1)} collective-permute-done((bf16[32,3584]{1,0:T(8,128)(2,1)S(1)}, bf16[32,3584]{1,0:T(8,128)(2,1)S(1)}, u32[]{:S(2)}, u32[]{:S(2)}) %collective-permute-start.3) | collective-permute-done | bytes 229408 | tf_op jit(solution)/shard_map/ppermute | solution.py:344
  21.8 0.7 copy-done.10
  22.5 1.5 %collective-permute-start.1 = (bf16[32,3584]{1,0:T(8,128)(2,1)S(1)}, bf16[32,3584]{1,0:T(8,128)(2,1)}, u32[]{:S(2)}, u32[]{:S(2)}) collective-permute-start(bf16[32,3584]{1,0:T(8,128)(2,1)S(1)} %collective-permute-done.held_ref.x0), channel_id=1, source_target_pairs={{0,1},{1,0},{2,3},{3,2},{4,5},{5,4},{6,7},{7,6},{8,9},{9,8},{10,11... | collective-permute-start | bytes 688136 | tf_op jit(solution)/shard_map/ppermute | solution.py:344
  24.0 0.1 pad_add_fusion.1.spots_ref
  24.1 0.0 collective-permute-start.7
  24.1 3.0 %core_logits.1 = (f32[128,512]{1,0:T(8,128)S(1)}, f32[8,128]{1,0:T(8,128)S(1)}) custom-call(bf16[128,3584]{1,0:T(8,128)(2,1)S(1)} %copy-done.4, bf16[3584,512]{1,0:T(8,128)(2,1)} %collective-permute-done.4.w_ref.other_ref.refs_12_, bf16[32,3584]{1,0:T(8,128)(2,1)S(1)} %collective-permute-done.held_ref.x0), custom_call_target="tpu_custom_call" | custom-call | flops 469762048 | bytes 4587520 | tf_op jit(solution)/shard_map/core_logits/pallas_call | solution.py:143
  27.1 2.0 %collective-permute-done.1.x1 = bf16[32,3584]{1,0:T(8,128)(2,1)} collective-permute-done((bf16[32,3584]{1,0:T(8,128)(2,1)S(1)}, bf16[32,3584]{1,0:T(8,128)(2,1)}, u32[]{:S(2)}, u32[]{:S(2)}) %collective-permute-start.1) | collective-permute-done | bytes 229408 | tf_op jit(solution)/shard_map/ppermute | solution.py:344
  29.1 0.7 copy-done.8
  29.8 0.6 collective-permute-start.14
  30.5 0.9 %copy-done.7 = bf16[32,3584]{1,0:T(8,128)(2,1)S(1)} copy-done((bf16[32,3584]{1,0:T(8,128)(2,1)S(1)}, bf16[32,3584]{1,0:T(8,128)(2,1)}, u32[]{:S(2)}) %copy-start.7) | copy-done | bytes 229400
  31.4 4.5 %far_logits.1 = (f32[128,512]{1,0:T(8,128)S(1)}, f32[128,512]{1,0:T(8,128)S(1)}, bf16[128,3584]{1,0:T(8,128)(2,1)}, f32[2,8,128]{2,1,0:T(8,128)S(1)}) custom-call(s32[4]{0:T(128)S(1)} %pad_add_fusion.1.spots_ref, bf16[32,3584]{1,0:T(8,128)(2,1)S(1)} %copy-done.7, bf16[32,3584]{1,0:T(8,128)(2,1)} %collective-permute-done.1.x1, ...), custom_call_target="tpu_custom_call" | custom-call | flops 939524096 | bytes 8257536 | tf_op jit(solution)/shard_map/far_logits/pallas_call | solution.py:186
  35.9 0.6 collective-permute-done.14.a2
  36.5 0.1 pad_add_fusion.2.at_ref
  36.6 2.3 %collective-permute-start.10 = (f32[2,8,128]{2,1,0:T(8,128)S(1)}, f32[2,8,128]{2,1,0:T(8,128)S(1)}, u32[]{:S(2)}, u32[]{:S(2)}) collective-permute-start(f32[2,8,128]{2,1,0:T(8,128)S(1)} %get-tuple-element.57.refs_0_), channel_id=1, source_target_pairs={{0,17},{1,16},{2,19},{3,18},{4,21},{5,20},{6,23},{7,22},{8,25},{9,... | collective-permute-start | bytes 24584 | tf_op jit(solution)/shard_map/ppermute | solution.py:344
  38.9 0.5 collective-permute-start.9
  39.4 0.7 collective-permute-start.8
  40.1 0.1 pad_add_fusion.refs_0_
  40.2 1.0 %collective-permute-done.10.refs_3_ = f32[2,8,128]{2,1,0:T(8,128)S(1)} collective-permute-done((f32[2,8,128]{2,1,0:T(8,128)S(1)}, f32[2,8,128]{2,1,0:T(8,128)S(1)}, u32[]{:S(2)}, u32[]{:S(2)}) %collective-permute-start.10) | collective-permute-done | bytes 8224 | tf_op jit(solution)/shard_map/ppermute | solution.py:344
  41.2 1.4 %collective-permute-done.9.refs_2_ = f32[2,8,128]{2,1,0:T(8,128)S(1)} collective-permute-done((f32[2,8,128]{2,1,0:T(8,128)S(1)}, f32[2,8,128]{2,1,0:T(8,128)S(1)}, u32[]{:S(2)}, u32[]{:S(2)}) %collective-permute-start.9) | collective-permute-done | bytes 8224 | tf_op jit(solution)/shard_map/ppermute | solution.py:344
  42.5 0.5 collective-permute-done.8.refs_1_
  43.0 2.0 %copy-done.2 = bf16[3584,512]{1,0:T(8,128)(2,1)S(1)} copy-done((bf16[3584,512]{1,0:T(8,128)(2,1)S(1)}, bf16[3584,512]{1,0:T(8,128)(2,1)}, u32[]{:S(2)}) %copy-start.2) | copy-done | bytes 3670040
  45.1 3.7 %collective-permute-start.13 = (f32[2,8,128]{2,1,0:T(8,128)S(1)}, f32[2,8,128]{2,1,0:T(8,128)S(1)}, u32[]{:S(2)}, u32[]{:S(2)}) collective-permute-start(f32[2,8,128]{2,1,0:T(8,128)S(1)} %merge_stats.1.refs_1_), channel_id=1, source_target_pairs={{0,6},{1,7},{2,4},{3,5},{4,2},{5,3},{6,0},{7,1},{8,14},{9,15},{10,... | collective-permute-start | bytes 24584 | tf_op jit(solution)/shard_map/ppermute | solution.py:344
  48.8 0.8 collective-permute-start.11
  49.6 0.9 %copy-done.9 = bf16[2,128,512]{2,1,0:T(8,128)(2,1)S(1)} copy-done((bf16[2,128,512]{2,1,0:T(8,128)(2,1)S(1)}, bf16[2,128,512]{2,1,0:T(8,128)(2,1)}, u32[]{:S(2)}) %copy-start.9) | copy-done | bytes 262168
  50.5 1.7 %teacher_rows.1.refs_10_ = bf16[2,128,1024]{2,1,0:T(8,128)(2,1)S(1)} custom-call(s32[2]{0:T(128)S(1)} %pad_add_fusion.2.at_ref, s32[4,1,128]{2,1,0:T(1,128)S(1)} %bitcast.42, bf16[2,128,512]{2,1,0:T(8,128)(2,1)S(1)} %get-tuple-element.49.kept_ref.a0, bf16[2,128,512]{2,1,0:T(8,128)(2,1)S(1)} %copy-done.9, bf16[2,128,512]{2,1,0:T(8,128)(2,1)} %collective-permute-done.14.a2, ...), custom_call_target="tpu_custom_call" | custom-call | flops 268435456 | bytes 1572864 | tf_op jit(solution)/shard_map/teacher_rows/pallas_call | solution.py:80
  52.2 1.1 %collective-permute-done.12.refs_3_ = f32[2,8,128]{2,1,0:T(8,128)S(1)} collective-permute-done((f32[2,8,128]{2,1,0:T(8,128)S(1)}, f32[2,8,128]{2,1,0:T(8,128)S(1)}, u32[]{:S(2)}, u32[]{:S(2)}) %collective-permute-start.12) | collective-permute-done | bytes 8224 | tf_op jit(solution)/shard_map/ppermute | solution.py:344
  53.3 6.0 %back_rows.1 = (bf16[256,512]{1,0:T(8,128)(2,1)S(1)}, bf16[256,512]{1,0:T(8,128)(2,1)S(1)}, bf16[128,1152]{1,0:T(8,128)(2,1)S(1)}, bf16[128,1152]{1,0:T(8,128)(2...) custom-call(s32[4]{0:T(128)S(1)} %pad_add_fusion.refs_0_, ...), custom_call_target="tpu_custom_call" | custom-call | flops 1879048192 | bytes 7340032 | tf_op jit(solution)/shard_map/back_rows/pallas_call | solution.py:293
  59.4 0.1 collective-permute-start.17
  59.5 0.3 collective-permute-start.20
  59.7 0.7 collective-permute-start.18
  60.4 1.3 %collective-permute-start.19 = (bf16[128,1152]{1,0:T(8,128)(2,1)S(1)}, bf16[128,1152]{1,0:T(8,128)(2,1)S(1)}, u32[]{:S(2)}, u32[]{:S(2)}) collective-permute-start(bf16[128,1152]{1,0:T(8,128)(2,1)S(1)} %get-tuple-element.72), channel_id=1, source_target_pairs={{0,1},{1,0},{2,3},{3,2},{4,5},{5,4},{6,7},{7,6},{8,9},{9,8},{10,11... | collective-permute-start | bytes 884744 | tf_op jit(solution)/shard_map/ppermute | solution.py:344
  61.8 7.2 %head_gradient.1 = bf16[3584,512]{1,0:T(8,128)(2,1)} custom-call(bf16[128,3584]{1,0:T(8,128)(2,1)S(1)} %copy-done.4, bf16[128,3584]{1,0:T(8,128)(2,1)} %get-tuple-element.67.r1, bf16[128,3584]{1,0:T(8,128)(2,1)S(1)} %collective-permute-done.6.r2, bf16[128,3584]{1,0:T(8,128)(2,1)} %collective-permute-done.16.r3, ...), custom_call_target="tpu_custom_call" | custom-call | flops 1879048192 | bytes 7340032 | tf_op jit(solution)/shard_map/head_gradient/pallas_call | solution.py:319
  69.0 0.3 collective-permute-done.19
  69.3 0.3 collective-permute-done.20
  69.6 1.6 %collective-permute-start.21 = (bf16[1,2,2,1,16,1152]{5,4,3,2,1,0:T(8,128)(2,1)S(1)}, bf16[1,2,2,1,16,1152]{5,4,3,2,1,0:T(8,128)(2,1)S(1)}, u32[]{:S(2)}, u32[]{:S(2)}) collective-permute-start(bf16[1,2,2,1,16,1152]{5,4,3,2,1,0:T(8,128)(2,1)S(1)} %fusion.1), channel_id=1, source_target_pairs={{0,1},{1,0},{2,3},{3,2},{4,5},{5,4},{6,7},{7,6},{8,9},{9,8},{10,11... | collective-permute-start | bytes 442376 | tf_op jit(solution)/shard_map/ppermute | solution.py:344
  71.3 1.4 %collective-permute-start.24 = (bf16[2,2,1,1,16,1152]{5,4,3,2,1,0:T(8,128)(2,1)S(1)}, bf16[2,2,1,1,16,1152]{5,4,3,2,1,0:T(8,128)(2,1)S(1)}, u32[]{:S(2)}, u32[]{:S(2)}) collective-permute-start(bf16[2,2,1,1,16,1152]{5,4,3,2,1,0:T(8,128)(2,1)S(1)} %fusion), channel_id=1, source_target_pairs={{0,2},{1,3},{2,0},{3,1},{4,6},{5,7},{6,4},{7,5},{8,10},{9,11},{10,... | collective-permute-start | bytes 442376 | tf_op jit(solution)/shard_map/ppermute | solution.py:344
  72.7 1.5 %collective-permute-start.27 = (bf16[1,2,1,2,16,1280]{5,4,3,2,1,0:T(8,128)(2,1)S(1)}, bf16[1,2,1,2,16,1280]{5,4,3,2,1,0:T(8,128)(2,1)S(1)}, u32[]{:S(2)}, u32[]{:S(2)}) collective-permute-start(bf16[1,2,1,2,16,1280]{5,4,3,2,1,0:T(8,128)(2,1)S(1)} %bitcast.59), channel_id=1, source_target_pairs={{0,16},{1,17},{2,18},{3,19},{4,20},{5,21},{6,22},{7,23},{8,24},{9,... | collective-permute-start | bytes 491528 | tf_op jit(solution)/shard_map/ppermute | solution.py:344
  74.2 0.9 %collective-permute-done.21 = bf16[1,2,2,1,16,1152]{5,4,3,2,1,0:T(8,128)(2,1)S(1)} collective-permute-done((bf16[1,2,2,1,16,1152]{5,4,3,2,1,0:T(8,128)(2,1)S(1)}, bf16[1,2,2,1,16,1152]{5,4,3,2,1,0:T(8,128)(2,1)S(1)}, u32[]{:S(2)}, u32[]{:S(2)}) %collective-permute-start.21) | collective-permute-done | bytes 147488 | tf_op jit(solution)/shard_map/ppermute | solution.py:344
  75.1 1.3 %collective-permute-start.22 = (bf16[1,2,1,1,16,1152]{5,4,3,2,1,0:T(8,128)(2,1)S(1)}, bf16[1,2,1,1,16,1152]{5,4,3,2,1,0:T(8,128)(2,1)S(1)}, u32[]{:S(2)}, u32[]{:S(2)}) collective-permute-start(bf16[1,2,1,1,16,1152]{5,4,3,2,1,0:T(8,128)(2,1)S(1)} %fusion.7), channel_id=1, source_target_pairs={{0,2},{1,3},{2,0},{3,1},{4,6},{5,7},{6,4},{7,5},{8,10},{9,11},{10,... | collective-permute-start | bytes 221192 | tf_op jit(solution)/shard_map/ppermute | solution.py:344
  76.4 0.1 collective-permute-done.24
  76.6 1.5 %collective-permute-start.25 = (bf16[1,2,1,1,16,1152]{5,4,3,2,1,0:T(8,128)(2,1)S(1)}, bf16[1,2,1,1,16,1152]{5,4,3,2,1,0:T(8,128)(2,1)S(1)}, u32[]{:S(2)}, u32[]{:S(2)}) collective-permute-start(bf16[1,2,1,1,16,1152]{5,4,3,2,1,0:T(8,128)(2,1)S(1)} %fusion.5), channel_id=1, source_target_pairs={{0,16},{1,17},{2,18},{3,19},{4,20},{5,21},{6,22},{7,23},{8,24},{9,... | collective-permute-start | bytes 221192 | tf_op jit(solution)/shard_map/ppermute | solution.py:344
  78.0 0.1 collective-permute-done.27
  78.2 1.3 %collective-permute-start.28 = (bf16[1,2,1,1,16,1280]{5,4,3,2,1,0:T(8,128)(2,1)S(1)}, bf16[1,2,1,1,16,1280]{5,4,3,2,1,0:T(8,128)(2,1)S(1)}, u32[]{:S(2)}, u32[]{:S(2)}) collective-permute-start(bf16[1,2,1,1,16,1280]{5,4,3,2,1,0:T(8,128)(2,1)S(1)} %fusion.3), channel_id=1, source_target_pairs={{0,1},{1,0},{2,3},{3,2},{4,5},{5,4},{6,7},{7,6},{8,9},{9,8},{10,11... | collective-permute-start | bytes 245768 | tf_op jit(solution)/shard_map/ppermute | solution.py:344
  79.4 0.1 collective-permute-done.22
  79.6 2.3 %collective-permute-start.23 = (bf16[1,1,1,1,16,1152]{5,4,3,2,1,0:T(8,128)(2,1)S(1)}, bf16[1,1,1,1,16,1152]{5,4,3,2,1,0:T(8,128)(2,1)S(1)}, u32[]{:S(2)}, u32[]{:S(2)}) collective-permute-start(bf16[1,1,1,1,16,1152]{5,4,3,2,1,0:T(8,128)(2,1)S(1)} %fusion.22), channel_id=1, source_target_pairs={{0,4},{1,5},{2,6},{3,7},{4,0},{5,1},{6,2},{7,3},{8,12},{9,13},{10,... | collective-permute-start | bytes 110600 | tf_op jit(solution)/shard_map/ppermute | solution.py:344
  82.0 2.0 %collective-permute-start.26 = (bf16[1,1,1,1,16,1152]{5,4,3,2,1,0:T(8,128)(2,1)S(1)}, bf16[1,1,1,1,16,1152]{5,4,3,2,1,0:T(8,128)(2,1)S(1)}, u32[]{:S(2)}, u32[]{:S(2)}) collective-permute-start(bf16[1,1,1,1,16,1152]{5,4,3,2,1,0:T(8,128)(2,1)S(1)} %fusion.16), channel_id=1, source_target_pairs={{0,4},{1,5},{2,6},{3,7},{4,0},{5,1},{6,2},{7,3},{8,12},{9,13},{10,... | collective-permute-start | bytes 110600 | tf_op jit(solution)/shard_map/ppermute | solution.py:344
  84.0 1.2 %collective-permute-start.29 = (bf16[1,1,1,1,16,1280]{5,4,3,2,1,0:T(8,128)(2,1)S(1)}, bf16[1,1,1,1,16,1280]{5,4,3,2,1,0:T(8,128)(2,1)S(1)}, u32[]{:S(2)}, u32[]{:S(2)}) collective-permute-start(bf16[1,1,1,1,16,1280]{5,4,3,2,1,0:T(8,128)(2,1)S(1)} %fusion.10), channel_id=1, source_target_pairs={{0,4},{1,5},{2,6},{3,7},{4,0},{5,1},{6,2},{7,3},{8,12},{9,13},{10,... | collective-permute-start | bytes 122888 | tf_op jit(solution)/shard_map/ppermute | solution.py:344
  85.2 0.5 collective-permute-done.23
  85.7 1.2 %collective-permute-done.26 = bf16[1,1,1,1,16,1152]{5,4,3,2,1,0:T(8,128)(2,1)S(1)} collective-permute-done((bf16[1,1,1,1,16,1152]{5,4,3,2,1,0:T(8,128)(2,1)S(1)}, bf16[1,1,1,1,16,1152]{5,4,3,2,1,0:T(8,128)(2,1)S(1)}, u32[]{:S(2)}, u32[]{:S(2)}) %collective-permute-start.26) | collective-permute-done | bytes 36896 | tf_op jit(solution)/shard_map/ppermute | solution.py:344
  86.9 2.1 %collective-permute-done.29 = bf16[1,1,1,1,16,1280]{5,4,3,2,1,0:T(8,128)(2,1)S(1)} collective-permute-done((bf16[1,1,1,1,16,1280]{5,4,3,2,1,0:T(8,128)(2,1)S(1)}, bf16[1,1,1,1,16,1280]{5,4,3,2,1,0:T(8,128)(2,1)S(1)}, u32[]{:S(2)}, u32[]{:S(2)}) %collective-permute-start.29) | collective-permute-done | bytes 40992 | tf_op jit(solution)/shard_map/ppermute | solution.py:344
  89.0 0.7 maximum_bitcast_fusion
  (55 shorter events, 0.5 us)
Async XLA Ops:
  0.6 7.8 %copy-start.4 = (bf16[128,3584]{1,0:T(8,128)(2,1)S(1)}, bf16[128,3584]{1,0:T(8,128)(2,1)}, u32[]{:S(2)}) copy-start(bf16[128,3584]{1,0:T(8,128)(2,1)} %r0.1) | copy-start | bytes 2752516
  0.6 23.4 %collective-permute-start.4 = (bf16[3584,512]{1,0:T(8,128)(2,1)}, bf16[3584,512]{1,0:T(8,128)(2,1)}, u32[]{:S(2)}, u32[]{:S(2)}) collective-permute-start(bf16[3584,512]{1,0:T(8,128)(2,1)} %refs_1_.1), channel_id=1, source_target_pairs={{0,8},{1,9},{2,10},{3,11},{4,12},{5,13},{6,14},{7,15},{8,0},{9,1},... | collective-permute-start | bytes 11010056 | tf_op jit(solution)/shard_map/ppermute | solution.py:344
  1.2 28.7 %collective-permute-start.6 = (bf16[128,3584]{1,0:T(8,128)(2,1)}, bf16[128,3584]{1,0:T(8,128)(2,1)S(1)}, u32[]{:S(2)}, u32[]{:S(2)}) collective-permute-start(bf16[128,3584]{1,0:T(8,128)(2,1)} %r0.1), channel_id=1, source_target_pairs={{0,8},{1,9},{2,10},{3,11},{4,12},{5,13},{6,14},{7,15},{8,0},{9,1},... | collective-permute-start | bytes 2752520 | tf_op jit(solution)/shard_map/ppermute | solution.py:344
  2.2 12.2 %collective-permute-start = (bf16[32,3584]{1,0:T(8,128)(2,1)S(1)}, bf16[32,3584]{1,0:T(8,128)(2,1)S(1)}, u32[]{:S(2)}, u32[]{:S(2)}) collective-permute-start(bf16[32,3584]{1,0:T(8,128)(2,1)S(1)} %constant_dynamic-slice_fusion.1), channel_id=1, source_target_pairs={{0,16},{1,17},{2,18},{3,19},{4,20},{5,21},{6,22},{7,23},{8,24},{9,... | collective-permute-start | bytes 688136 | tf_op jit(solution)/shard_map/ppermute | solution.py:344
  8.0 6.4 %copy-start.14 = (bf16[32,3584]{1,0:T(8,128)(2,1)S(1)}, bf16[32,3584]{1,0:T(8,128)(2,1)}, u32[]{:S(2)}) copy-start(bf16[32,3584]{1,0:T(8,128)(2,1)} %constant_dynamic-slice_fusion) | copy-start | bytes 688132
  8.4 2.1 %copy-start.5 = (bf16[3584,512]{1,0:T(8,128)(2,1)S(1)}, bf16[3584,512]{1,0:T(8,128)(2,1)}, u32[]{:S(2)}) copy-start(bf16[3584,512]{1,0:T(8,128)(2,1)} %refs_1_.1) | copy-start | bytes 11010052
  10.5 20.0 %copy-start.13 = (s32[128]{0:T(128)S(1)}, s32[128]{0:T(128)}, u32[]{:S(2)}) copy-start(s32[128]{0:T(128)} %param.6) | copy-start | bytes 1540
  12.5 1.8 %copy-start = (bf16[3584,512]{1,0:T(8,128)(2,1)}, bf16[3584,512]{1,0:T(8,128)(2,1)S(1)}, u32[]{:S(2)}) copy-start(bf16[3584,512]{1,0:T(8,128)(2,1)S(1)} %get-tuple-element.53.own_ref.refs_8_.refs_11_) | copy-start | bytes 11010052
  14.4 16.1 %copy-start.6 = (bf16[32,3584]{1,0:T(8,128)(2,1)}, bf16[32,3584]{1,0:T(8,128)(2,1)S(1)}, u32[]{:S(2)}) copy-start(bf16[32,3584]{1,0:T(8,128)(2,1)S(1)} %collective-permute-done.held_ref.x0) | copy-start | bytes 688132
  14.4 7.4 %collective-permute-start.3 = (bf16[32,3584]{1,0:T(8,128)(2,1)S(1)}, bf16[32,3584]{1,0:T(8,128)(2,1)S(1)}, u32[]{:S(2)}, u32[]{:S(2)}) collective-permute-start(bf16[32,3584]{1,0:T(8,128)(2,1)S(1)} %copy-done.14), channel_id=1, source_target_pairs={{0,16},{1,17},{2,18},{3,19},{4,20},{5,21},{6,22},{7,23},{8,24},{9,... | collective-permute-start | bytes 688136 | tf_op jit(solution)/shard_map/ppermute | solution.py:344
  14.5 14.6 %collective-permute-start.5 = (bf16[2,128,512]{2,1,0:T(8,128)(2,1)S(1)}, bf16[2,128,512]{2,1,0:T(8,128)(2,1)S(1)}, u32[]{:S(2)}, u32[]{:S(2)}) collective-permute-start(bf16[2,128,512]{2,1,0:T(8,128)(2,1)S(1)} %get-tuple-element.49.kept_ref.a0), channel_id=1, source_target_pairs={{0,8},{1,9},{2,10},{3,11},{4,12},{5,13},{6,14},{7,15},{8,0},{9,1},... | collective-permute-start | bytes 786440 | tf_op jit(solution)/shard_map/ppermute | solution.py:344
  14.5 12.6 %collective-permute-start.2 = (bf16[32,3584]{1,0:T(8,128)(2,1)S(1)}, bf16[32,3584]{1,0:T(8,128)(2,1)}, u32[]{:S(2)}, u32[]{:S(2)}) collective-permute-start(bf16[32,3584]{1,0:T(8,128)(2,1)S(1)} %collective-permute-done.held_ref.x0), channel_id=1, source_target_pairs={{0,2},{1,3},{2,0},{3,1},{4,6},{5,7},{6,4},{7,5},{8,10},{9,11},{10,... | collective-permute-start | bytes 688136 | tf_op jit(solution)/shard_map/ppermute | solution.py:344
  21.8 0.7 copy-start.10
  22.5 6.7 %collective-permute-start.1 = (bf16[32,3584]{1,0:T(8,128)(2,1)S(1)}, bf16[32,3584]{1,0:T(8,128)(2,1)}, u32[]{:S(2)}, u32[]{:S(2)}) collective-permute-start(bf16[32,3584]{1,0:T(8,128)(2,1)S(1)} %collective-permute-done.held_ref.x0), channel_id=1, source_target_pairs={{0,1},{1,0},{2,3},{3,2},{4,5},{5,4},{6,7},{7,6},{8,9},{9,8},{10,11... | collective-permute-start | bytes 688136 | tf_op jit(solution)/shard_map/ppermute | solution.py:344
  24.0 6.5 %copy-start.1 = (bf16[3584,512]{1,0:T(8,128)(2,1)S(1)}, bf16[3584,512]{1,0:T(8,128)(2,1)}, u32[]{:S(2)}) copy-start(bf16[3584,512]{1,0:T(8,128)(2,1)} %copy-done) | copy-start | bytes 11010052
  24.0 6.5 %copy-start.11 = (bf16[32,3584]{1,0:T(8,128)(2,1)S(1)}, bf16[32,3584]{1,0:T(8,128)(2,1)}, u32[]{:S(2)}) copy-start(bf16[32,3584]{1,0:T(8,128)(2,1)} %copy-done.10) | copy-start | bytes 688132
  24.1 6.4 %collective-permute-start.7 = (f32[8,128]{1,0:T(8,128)S(1)}, f32[8,128]{1,0:T(8,128)S(1)}, u32[]{:S(2)}, u32[]{:S(2)}) collective-permute-start(f32[8,128]{1,0:T(8,128)S(1)} %taught_stats.1.taught_ref), channel_id=1, source_target_pairs={{0,8},{1,9},{2,10},{3,11},{4,12},{5,13},{6,14},{7,15},{8,0},{9,1},... | collective-permute-start | bytes 12296 | tf_op jit(solution)/shard_map/ppermute | solution.py:344
  29.1 0.7 copy-start.8
  29.8 6.7 %collective-permute-start.14 = (bf16[2,128,512]{2,1,0:T(8,128)(2,1)S(1)}, bf16[2,128,512]{2,1,0:T(8,128)(2,1)}, u32[]{:S(2)}, u32[]{:S(2)}) collective-permute-start(bf16[2,128,512]{2,1,0:T(8,128)(2,1)S(1)} %get-tuple-element.63.gone_ref), channel_id=1, source_target_pairs={{0,16},{1,17},{2,18},{3,19},{4,20},{5,21},{6,22},{7,23},{8,24},{9,... | collective-permute-start | bytes 786440 | tf_op jit(solution)/shard_map/ppermute | solution.py:344
  30.5 0.9 %copy-start.7 = (bf16[32,3584]{1,0:T(8,128)(2,1)S(1)}, bf16[32,3584]{1,0:T(8,128)(2,1)}, u32[]{:S(2)}) copy-start(bf16[32,3584]{1,0:T(8,128)(2,1)} %copy-done.6) | copy-start | bytes 688132
  35.9 13.7 %copy-start.12 = (s32[512]{0:T(512)S(1)}, s32[512]{0:T(512)}, u32[]{:S(2)}) copy-start(s32[512]{0:T(512)} %param.7) | copy-start | bytes 6148
  35.9 25.8 %collective-permute-start.16 = (bf16[128,3584]{1,0:T(8,128)(2,1)}, bf16[128,3584]{1,0:T(8,128)(2,1)}, u32[]{:S(2)}, u32[]{:S(2)}) collective-permute-start(bf16[128,3584]{1,0:T(8,128)(2,1)} %get-tuple-element.67.r1), channel_id=1, source_target_pairs={{0,8},{1,9},{2,10},{3,11},{4,12},{5,13},{6,14},{7,15},{8,0},{9,1},... | collective-permute-start | bytes 2752520 | tf_op jit(solution)/shard_map/ppermute | solution.py:344
  36.5 13.1 %collective-permute-start.15 = (bf16[2,128,512]{2,1,0:T(8,128)(2,1)}, bf16[2,128,512]{2,1,0:T(8,128)(2,1)S(1)}, u32[]{:S(2)}, u32[]{:S(2)}) collective-permute-start(bf16[2,128,512]{2,1,0:T(8,128)(2,1)} %collective-permute-done.14.a2), channel_id=1, source_target_pairs={{0,8},{1,9},{2,10},{3,11},{4,12},{5,13},{6,14},{7,15},{8,0},{9,1},... | collective-permute-start | bytes 786440 | tf_op jit(solution)/shard_map/ppermute | solution.py:344
  36.6 4.6 %collective-permute-start.10 = (f32[2,8,128]{2,1,0:T(8,128)S(1)}, f32[2,8,128]{2,1,0:T(8,128)S(1)}, u32[]{:S(2)}, u32[]{:S(2)}) collective-permute-start(f32[2,8,128]{2,1,0:T(8,128)S(1)} %get-tuple-element.57.refs_0_), channel_id=1, source_target_pairs={{0,17},{1,16},{2,19},{3,18},{4,21},{5,20},{6,23},{7,22},{8,25},{9,... | collective-permute-start | bytes 24584 | tf_op jit(solution)/shard_map/ppermute | solution.py:344
  38.9 3.7 %collective-permute-start.9 = (f32[2,8,128]{2,1,0:T(8,128)S(1)}, f32[2,8,128]{2,1,0:T(8,128)S(1)}, u32[]{:S(2)}, u32[]{:S(2)}) collective-permute-start(f32[2,8,128]{2,1,0:T(8,128)S(1)} %get-tuple-element.57.refs_0_), channel_id=1, source_target_pairs={{0,1},{1,0},{2,3},{3,2},{4,5},{5,4},{6,7},{7,6},{8,9},{9,8},{10,11... | collective-permute-start | bytes 24584 | tf_op jit(solution)/shard_map/ppermute | solution.py:344
  39.4 3.7 %collective-permute-start.8 = (f32[2,8,128]{2,1,0:T(8,128)S(1)}, f32[2,8,128]{2,1,0:T(8,128)S(1)}, u32[]{:S(2)}, u32[]{:S(2)}) collective-permute-start(f32[2,8,128]{2,1,0:T(8,128)S(1)} %get-tuple-element.57.refs_0_), channel_id=1, source_target_pairs={{0,16},{1,17},{2,18},{3,19},{4,20},{5,21},{6,22},{7,23},{8,24},{9,... | collective-permute-start | bytes 24584 | tf_op jit(solution)/shard_map/ppermute | solution.py:344
  43.0 2.0 %copy-start.2 = (bf16[3584,512]{1,0:T(8,128)(2,1)S(1)}, bf16[3584,512]{1,0:T(8,128)(2,1)}, u32[]{:S(2)}) copy-start(bf16[3584,512]{1,0:T(8,128)(2,1)} %copy-done) | copy-start | bytes 11010052
  45.1 8.2 %copy-start.3 = (bf16[3584,512]{1,0:T(8,128)(2,1)S(1)}, bf16[3584,512]{1,0:T(8,128)(2,1)}, u32[]{:S(2)}) copy-start(bf16[3584,512]{1,0:T(8,128)(2,1)} %copy-done) | copy-start | bytes 11010052
  45.1 7.1 %collective-permute-start.13 = (f32[2,8,128]{2,1,0:T(8,128)S(1)}, f32[2,8,128]{2,1,0:T(8,128)S(1)}, u32[]{:S(2)}, u32[]{:S(2)}) collective-permute-start(f32[2,8,128]{2,1,0:T(8,128)S(1)} %merge_stats.1.refs_1_), channel_id=1, source_target_pairs={{0,6},{1,7},{2,4},{3,5},{4,2},{5,3},{6,0},{7,1},{8,14},{9,15},{10,... | collective-permute-start | bytes 24584 | tf_op jit(solution)/shard_map/ppermute | solution.py:344
  48.8 4.5 %collective-permute-start.12 = (f32[2,8,128]{2,1,0:T(8,128)S(1)}, f32[2,8,128]{2,1,0:T(8,128)S(1)}, u32[]{:S(2)}, u32[]{:S(2)}) collective-permute-start(f32[2,8,128]{2,1,0:T(8,128)S(1)} %merge_stats.1.refs_1_), channel_id=1, source_target_pairs={{0,4},{1,5},{2,6},{3,7},{4,0},{5,1},{6,2},{7,3},{8,12},{9,13},{10,... | collective-permute-start | bytes 24584 | tf_op jit(solution)/shard_map/ppermute | solution.py:344
  48.8 4.5 %collective-permute-start.11 = (f32[2,8,128]{2,1,0:T(8,128)S(1)}, f32[2,8,128]{2,1,0:T(8,128)S(1)}, u32[]{:S(2)}, u32[]{:S(2)}) collective-permute-start(f32[2,8,128]{2,1,0:T(8,128)S(1)} %merge_stats.1.refs_1_), channel_id=1, source_target_pairs={{0,2},{1,3},{2,0},{3,1},{4,6},{5,7},{6,4},{7,5},{8,10},{9,11},{10,... | collective-permute-start | bytes 24584 | tf_op jit(solution)/shard_map/ppermute | solution.py:344
  49.6 1.0 %copy-start.9 = (bf16[2,128,512]{2,1,0:T(8,128)(2,1)S(1)}, bf16[2,128,512]{2,1,0:T(8,128)(2,1)}, u32[]{:S(2)}) copy-start(bf16[2,128,512]{2,1,0:T(8,128)(2,1)} %copy-done.8) | copy-start | bytes 786436
  59.4 2.4 %collective-permute-start.17 = (bf16[256,512]{1,0:T(8,128)(2,1)S(1)}, bf16[256,512]{1,0:T(8,128)(2,1)S(1)}, u32[]{:S(2)}, u32[]{:S(2)}) collective-permute-start(bf16[256,512]{1,0:T(8,128)(2,1)S(1)} %get-tuple-element.70), channel_id=1, source_target_pairs={{0,8},{1,9},{2,10},{3,11},{4,12},{5,13},{6,14},{7,15},{8,0},{9,1},... | collective-permute-start | bytes 786440 | tf_op jit(solution)/shard_map/ppermute | solution.py:344
  59.5 10.1 %collective-permute-start.20 = (bf16[128,1280]{1,0:T(8,128)(2,1)S(1)}, bf16[128,1280]{1,0:T(8,128)(2,1)S(1)}, u32[]{:S(2)}, u32[]{:S(2)}) collective-permute-start(bf16[128,1280]{1,0:T(8,128)(2,1)S(1)} %get-tuple-element.73), channel_id=1, source_target_pairs={{0,2},{1,3},{2,0},{3,1},{4,6},{5,7},{6,4},{7,5},{8,10},{9,11},{10,... | collective-permute-start | bytes 983048 | tf_op jit(solution)/shard_map/ppermute | solution.py:344
  59.7 9.3 %collective-permute-start.18 = (bf16[128,1152]{1,0:T(8,128)(2,1)S(1)}, bf16[128,1152]{1,0:T(8,128)(2,1)S(1)}, u32[]{:S(2)}, u32[]{:S(2)}) collective-permute-start(bf16[128,1152]{1,0:T(8,128)(2,1)S(1)} %get-tuple-element.71), channel_id=1, source_target_pairs={{0,16},{1,17},{2,18},{3,19},{4,20},{5,21},{6,22},{7,23},{8,24},{9,... | collective-permute-start | bytes 884744 | tf_op jit(solution)/shard_map/ppermute | solution.py:344
  60.4 8.9 %collective-permute-start.19 = (bf16[128,1152]{1,0:T(8,128)(2,1)S(1)}, bf16[128,1152]{1,0:T(8,128)(2,1)S(1)}, u32[]{:S(2)}, u32[]{:S(2)}) collective-permute-start(bf16[128,1152]{1,0:T(8,128)(2,1)S(1)} %get-tuple-element.72), channel_id=1, source_target_pairs={{0,1},{1,0},{2,3},{3,2},{4,5},{5,4},{6,7},{7,6},{8,9},{9,8},{10,11... | collective-permute-start | bytes 884744 | tf_op jit(solution)/shard_map/ppermute | solution.py:344
  69.6 5.5 %collective-permute-start.21 = (bf16[1,2,2,1,16,1152]{5,4,3,2,1,0:T(8,128)(2,1)S(1)}, bf16[1,2,2,1,16,1152]{5,4,3,2,1,0:T(8,128)(2,1)S(1)}, u32[]{:S(2)}, u32[]{:S(2)}) collective-permute-start(bf16[1,2,2,1,16,1152]{5,4,3,2,1,0:T(8,128)(2,1)S(1)} %fusion.1), channel_id=1, source_target_pairs={{0,1},{1,0},{2,3},{3,2},{4,5},{5,4},{6,7},{7,6},{8,9},{9,8},{10,11... | collective-permute-start | bytes 442376 | tf_op jit(solution)/shard_map/ppermute | solution.py:344
  71.3 5.2 %collective-permute-start.24 = (bf16[2,2,1,1,16,1152]{5,4,3,2,1,0:T(8,128)(2,1)S(1)}, bf16[2,2,1,1,16,1152]{5,4,3,2,1,0:T(8,128)(2,1)S(1)}, u32[]{:S(2)}, u32[]{:S(2)}) collective-permute-start(bf16[2,2,1,1,16,1152]{5,4,3,2,1,0:T(8,128)(2,1)S(1)} %fusion), channel_id=1, source_target_pairs={{0,2},{1,3},{2,0},{3,1},{4,6},{5,7},{6,4},{7,5},{8,10},{9,11},{10,... | collective-permute-start | bytes 442376 | tf_op jit(solution)/shard_map/ppermute | solution.py:344
  72.7 5.5 %collective-permute-start.27 = (bf16[1,2,1,2,16,1280]{5,4,3,2,1,0:T(8,128)(2,1)S(1)}, bf16[1,2,1,2,16,1280]{5,4,3,2,1,0:T(8,128)(2,1)S(1)}, u32[]{:S(2)}, u32[]{:S(2)}) collective-permute-start(bf16[1,2,1,2,16,1280]{5,4,3,2,1,0:T(8,128)(2,1)S(1)} %bitcast.59), channel_id=1, source_target_pairs={{0,16},{1,17},{2,18},{3,19},{4,20},{5,21},{6,22},{7,23},{8,24},{9,... | collective-permute-start | bytes 491528 | tf_op jit(solution)/shard_map/ppermute | solution.py:344
  75.1 4.4 %collective-permute-start.22 = (bf16[1,2,1,1,16,1152]{5,4,3,2,1,0:T(8,128)(2,1)S(1)}, bf16[1,2,1,1,16,1152]{5,4,3,2,1,0:T(8,128)(2,1)S(1)}, u32[]{:S(2)}, u32[]{:S(2)}) collective-permute-start(bf16[1,2,1,1,16,1152]{5,4,3,2,1,0:T(8,128)(2,1)S(1)} %fusion.7), channel_id=1, source_target_pairs={{0,2},{1,3},{2,0},{3,1},{4,6},{5,7},{6,4},{7,5},{8,10},{9,11},{10,... | collective-permute-start | bytes 221192 | tf_op jit(solution)/shard_map/ppermute | solution.py:344
  76.6 5.4 %collective-permute-start.25 = (bf16[1,2,1,1,16,1152]{5,4,3,2,1,0:T(8,128)(2,1)S(1)}, bf16[1,2,1,1,16,1152]{5,4,3,2,1,0:T(8,128)(2,1)S(1)}, u32[]{:S(2)}, u32[]{:S(2)}) collective-permute-start(bf16[1,2,1,1,16,1152]{5,4,3,2,1,0:T(8,128)(2,1)S(1)} %fusion.5), channel_id=1, source_target_pairs={{0,16},{1,17},{2,18},{3,19},{4,20},{5,21},{6,22},{7,23},{8,24},{9,... | collective-permute-start | bytes 221192 | tf_op jit(solution)/shard_map/ppermute | solution.py:344
  78.2 5.8 %collective-permute-start.28 = (bf16[1,2,1,1,16,1280]{5,4,3,2,1,0:T(8,128)(2,1)S(1)}, bf16[1,2,1,1,16,1280]{5,4,3,2,1,0:T(8,128)(2,1)S(1)}, u32[]{:S(2)}, u32[]{:S(2)}) collective-permute-start(bf16[1,2,1,1,16,1280]{5,4,3,2,1,0:T(8,128)(2,1)S(1)} %fusion.3), channel_id=1, source_target_pairs={{0,1},{1,0},{2,3},{3,2},{4,5},{5,4},{6,7},{7,6},{8,9},{9,8},{10,11... | collective-permute-start | bytes 245768 | tf_op jit(solution)/shard_map/ppermute | solution.py:344
  79.6 6.1 %collective-permute-start.23 = (bf16[1,1,1,1,16,1152]{5,4,3,2,1,0:T(8,128)(2,1)S(1)}, bf16[1,1,1,1,16,1152]{5,4,3,2,1,0:T(8,128)(2,1)S(1)}, u32[]{:S(2)}, u32[]{:S(2)}) collective-permute-start(bf16[1,1,1,1,16,1152]{5,4,3,2,1,0:T(8,128)(2,1)S(1)} %fusion.22), channel_id=1, source_target_pairs={{0,4},{1,5},{2,6},{3,7},{4,0},{5,1},{6,2},{7,3},{8,12},{9,13},{10,... | collective-permute-start | bytes 110600 | tf_op jit(solution)/shard_map/ppermute | solution.py:344
  82.0 4.9 %collective-permute-start.26 = (bf16[1,1,1,1,16,1152]{5,4,3,2,1,0:T(8,128)(2,1)S(1)}, bf16[1,1,1,1,16,1152]{5,4,3,2,1,0:T(8,128)(2,1)S(1)}, u32[]{:S(2)}, u32[]{:S(2)}) collective-permute-start(bf16[1,1,1,1,16,1152]{5,4,3,2,1,0:T(8,128)(2,1)S(1)} %fusion.16), channel_id=1, source_target_pairs={{0,4},{1,5},{2,6},{3,7},{4,0},{5,1},{6,2},{7,3},{8,12},{9,13},{10,... | collective-permute-start | bytes 110600 | tf_op jit(solution)/shard_map/ppermute | solution.py:344
  84.0 5.0 %collective-permute-start.29 = (bf16[1,1,1,1,16,1280]{5,4,3,2,1,0:T(8,128)(2,1)S(1)}, bf16[1,1,1,1,16,1280]{5,4,3,2,1,0:T(8,128)(2,1)S(1)}, u32[]{:S(2)}, u32[]{:S(2)}) collective-permute-start(bf16[1,1,1,1,16,1280]{5,4,3,2,1,0:T(8,128)(2,1)S(1)} %fusion.10), channel_id=1, source_target_pairs={{0,4},{1,5},{2,6},{3,7},{4,0},{5,1},{6,2},{7,3},{8,12},{9,13},{10,... | collective-permute-start | bytes 122888 | tf_op jit(solution)/shard_map/ppermute | solution.py:344

commit v8 on v7

--- a/solution.py
+++ b/solution.py
@@ -352,15 +352,29 @@
     quarter_rows = per // 4
     quarter = me_v & 3
     starts = [(quarter ^ k) * quarter_rows for k in range(4)]
-    other_weight = swap(head_weight, CORE)
-    core_hidden = swap(hidden, CORE)
-    first = lax.dynamic_slice_in_dim(hidden, starts[0], quarter_rows, 0)
+    chip = me_g >> 1
+    spots = ints(*starts)
+    at = ints(
+        me_v * owned, (me_g * shards + me_v) * cols, ((me_g ^ 1) * shards + me_v) * cols, me_g
+    )
+    who = ints(me_g, me_g & 1)
+    unsigned = [jnp.asarray(v, jnp.uint32) for v in (starts[0], starts[3], 2 * chip, 2 * (chip ^ 1))]
+    rows, weight, spots, at, who, *unsigned = tie(hidden, head_weight, spots, at, who, *unsigned)
+    zero = jnp.uint32(0)
+
+    def cut(value, start, size, dim):
+        indices = [start if d == dim else zero for d in range(value.ndim)]
+        sizes = [size if d == dim else n for d, n in enumerate(value.shape)]
+        return lax.dynamic_slice(value, indices, sizes)
+
+    other_weight = swap(weight, CORE)
+    core_hidden = swap(rows, CORE)
+    first = cut(rows, unsigned[0], quarter_rows, 0)
     x0 = swap(first, X)
-    _, rows, teacher = tie(first, hidden, teacher_logits)
-    second = lax.dynamic_slice_in_dim(rows, starts[3], quarter_rows, 0)
-    chip = me_g >> 1
-    kept = lax.dynamic_slice_in_dim(teacher, 2 * chip, 2, 1).swapaxes(0, 1)
-    gone = lax.dynamic_slice_in_dim(teacher, 2 * (chip ^ 1), 2, 1).swapaxes(0, 1)
+    _, rows, teacher = tie(first, rows, teacher_logits)
+    second = cut(rows, unsigned[1], quarter_rows, 0)
+    kept = cut(teacher, unsigned[2], 2, 1).swapaxes(0, 1)
+    gone = cut(teacher, unsigned[3], 2, 1).swapaxes(0, 1)
     taught = taught_stats(kept, gone)
     near_a, stats_a, own_weight = own_logits(rows, head_weight)
     x0, second, kept, gone, taught, near_a, rows = tie(
@@ -372,12 +386,13 @@
     taught_core = swap(taught, CORE)
     kept_core = swap(kept, CORE)
     near_b, stats_b = core_logits(rows, other_weight, x0)
-    x1, x2, x3, gone, near_b, kept_core, core_hidden = tie(
-        x1, x2, x3, gone, near_b, kept_core, core_hidden
-    )
+    x1, x2, x3, gone, near_b, kept_core, taught_core = tie(
+        x1, x2, x3, gone, near_b, kept_core, taught_core
+    )
+    spots, core_hidden = tie(spots, core_hidden)
     taught_x = swap(gone, X)
     far_a, far_b, x_rows, stats = far_logits(
-        ints(*starts),
+        spots,
         [x0, x1, x2, x3],
         own_weight,
         other_weight,
@@ -395,9 +410,7 @@
     held = logits + [own_weight]
     stats = merge([stats, swap(stats, X), swap(stats, Y), swap(stats, X + Y)], (0, 1, 0, 1), held)
     _, taught_far = tie(stats, taught_far)
-    aligned = teacher_rows(
-        ints(me_g, me_g & 1), served, [kept, kept_core, taught_x, taught_far]
-    )
+    aligned = teacher_rows(who, served, [kept, kept_core, taught_x, taught_far])
     core_x = swap(x_rows, CORE)
     mask = W
     while True:
@@ -419,9 +432,6 @@
     low = owned.bit_length() - 1
     row_bit = {0: low + bits, ydim: low, wdim: low + 1}
     first_bits = tuple(row_bit[order[0]] for order in orders)
-    at = ints(
-        me_v * owned, (me_g * shards + me_v) * cols, ((me_g ^ 1) * shards + me_v) * cols, me_g
-    )
     gown, gother, sents, keeps = back_rows(
         at, parts, logits, served, aligned, own_weight, other_weight, first_bits, edges
     )

time: 90.3 us -> 77.5 us (0.86)
  Pallas kernels: 25 us -> 16.3 us
  local copies, waits for them, and re-layouts: 13 us -> 5.29 us
  waiting for transfers between devices: 17.4 us -> 21.7 us
    unnamed x30 -> x8, local copies, waits for them, and re-layouts: 9.26 us -> 2.08 us
    ppermute x30, waiting for transfers between devices: 17.4 us -> 21.7 us  [swap(): return lax.ppermute(value, AXES, [(i, i ^ mask) for i in range(count)])]
    pallas_call x1, Pallas kernels: 4.51 us -> 1.96 us  [far_logits(): pl.pallas_call(far_kernel, out_shape=(shape((per, cols), F32), shape((per...]
    pallas_call x1, Pallas kernels: 3.05 us -> 0.86 us  [core_logits(): pl.pallas_call(core_kernel, out_shape=(shape((per, cols), F32), shape((ST...]
    pallas_call x1, Pallas kernels: 7.23 us -> 5.23 us  [head_gradient(): pl.pallas_call(head_kernel, grid=(depth // tile,), out_shape=shape((depth...]
    pallas_call x1, Pallas kernels: 6.04 us -> 4.53 us  [back_rows(): pl.pallas_call(lambda *refs: back_kernel(bits, edges, len(stats), *refs),...]
  transfers between devices with their start and end apart: 30 -> 30, of which waited for: 16 -> 19; matrix products, arithmetic and copies ran while one was open for 5% -> 5% of each run, Pallas kernels for 28% -> 21%
where the time goes in v8:
time: 77.5 us; the launch traced here: 77.3 us
  starting transfers between devices  32 us (41%)
  waiting for transfers between devices  21.7 us (28%)
  Pallas kernels  16.3 us (21%)
  local copies, waits for them, and re-layouts  5.29 us (7%)
  other arithmetic  1.2 us (2%)
  between operations  0.85 us (1%)
    ppermute x30, starting transfers between devices, swap(): return lax.ppermute(value, AXES, [(i, i ^ mask) for i in range(count)])  32 us
    ppermute x30, waiting for transfers between devices, swap(): return lax.ppermute(value, AXES, [(i, i ^ mask) for i in range(count)])  21.7 us
    pallas_call x1, Pallas kernels, head_gradient(): pl.pallas_call(head_kernel, grid=(depth // tile,), out_shape=shape((depth...  5.23 us
    pallas_call x1, Pallas kernels, back_rows(): pl.pallas_call(lambda *refs: back_kernel(bits, edges, len(stats), *refs),...  4.53 us
    unnamed x8, local copies, waits for them, and re-layouts  2.08 us
    pallas_call x1, Pallas kernels, own_logits(): pl.pallas_call(lambda *refs: own_kernel(splits, *refs), out_shape=(shape(...  2.04 us
    dynamic_slice x2, local copies, waits for them, and re-layouts, cut(): return lax.dynamic_slice(value, indices, sizes)  2.01 us
    pallas_call x1, Pallas kernels, far_logits(): pl.pallas_call(far_kernel, out_shape=(shape((per, cols), F32), shape((per...  1.96 us
  transfers between devices with their start and end apart: 30, of which 19 were waited for; matrix products, arithmetic and copies ran while one was open for 5% of the time, Pallas kernels for 21%

profile of v8, /device:TPU:0, one launch (start us, length us, event | category | flops | bytes accessed | tf_op | source)
XLA Modules:
  0.0 77.3 jit_solution(12531558899885711922)
XLA Ops:
  0.6 0.0 copy-start
  0.7 0.1 pad_add_fusion.2.at_ref
  0.7 0.1 pad_add_fusion
  0.8 0.5 collective-permute-start.5
  1.3 0.1 collective-permute-start
  1.4 1.0 %constant_dynamic-slice_fusion.1 = bf16[32,3584]{1,0:T(8,128)(2,1)S(1)} fusion(bf16[128,3584]{1,0:T(8,128)(2,1)} %r0.1, u32[]{:T(128)S(6)} %convert_element_type.149), kind=kLoop, calls=%fused_computation.42 | loop fusion | bytes 458756 | tf_op jit(solution)/shard_map/dynamic_slice | solution.py:368
  2.4 3.0 %collective-permute-start.1 = (bf16[32,3584]{1,0:T(8,128)(2,1)S(1)}, bf16[32,3584]{1,0:T(8,128)(2,1)S(1)}, u32[]{:S(2)}, u32[]{:S(2)}) collective-permute-start(bf16[32,3584]{1,0:T(8,128)(2,1)S(1)} %constant_dynamic-slice_fusion.1), channel_id=1, source_target_pairs={{0,16},{1,17},{2,18},{3,19},{4,20},{5,21},{6,22},{7,23},{8,24},{9,... | collective-permute-start | bytes 688136 | tf_op jit(solution)/shard_map/ppermute | solution.py:344
  5.4 1.0 %constant_dynamic-slice_fusion = bf16[32,3584]{1,0:T(8,128)(2,1)S(1)} fusion(bf16[128,3584]{1,0:T(8,128)(2,1)} %r0.1, u32[]{:T(128)S(6)} %convert_element_type.150), kind=kLoop, calls=%fused_computation.41 | loop fusion | bytes 458756 | tf_op jit(solution)/shard_map/dynamic_slice | solution.py:368
  6.4 1.1 %copy.7 = bf16[128,4,512]{2,0,1:T(8,128)(2,1)S(1)} copy(bf16[128,4,512]{2,1,0:T(4,128)(2,1)} %param.9) | data formatting | bytes 1048576 | tf_op jit(solution)/shard_map/optimization_barrier | solution.py:347
  7.5 0.4 taught_stats.1.taught_ref
  7.9 2.1 %copy-done.1 = bf16[3584,512]{1,0:T(8,128)(2,1)S(1)} copy-done((bf16[3584,512]{1,0:T(8,128)(2,1)S(1)}, bf16[3584,512]{1,0:T(8,128)(2,1)}, u32[]{:S(2)}) %copy-start.1) | copy-done | bytes 3670040
  10.0 2.0 %own_logits.1 = (f32[128,512]{1,0:T(8,128)S(1)}, f32[8,128]{1,0:T(8,128)S(1)}, bf16[3584,512]{1,0:T(8,128)(2,1)S(1)}) custom-call(bf16[128,3584]{1,0:T(8,128)(2,1)S(1)} %copy-done, bf16[3584,512]{1,0:T(8,128)(2,1)S(1)} %copy-done.1), custom_call_target="tpu_custom_call" | custom-call | flops 469762048 | bytes 8257536 | tf_op jit(solution)/shard_map/own_logits/pallas_call | solution.py:118
  12.0 0.0 collective-permute-done.1.held_ref.x0
  12.1 0.1 collective-permute-start.6
  12.1 0.8 %collective-permute-start.4 = (bf16[32,3584]{1,0:T(8,128)(2,1)S(1)}, bf16[32,3584]{1,0:T(8,128)(2,1)S(1)}, u32[]{:S(2)}, u32[]{:S(2)}) collective-permute-start(bf16[32,3584]{1,0:T(8,128)(2,1)S(1)} %constant_dynamic-slice_fusion), channel_id=1, source_target_pairs={{0,16},{1,17},{2,18},{3,19},{4,20},{5,21},{6,22},{7,23},{8,24},{9,... | collective-permute-start | bytes 688136 | tf_op jit(solution)/shard_map/ppermute | solution.py:344
  13.0 1.6 %collective-permute-start.3 = (bf16[32,3584]{1,0:T(8,128)(2,1)S(1)}, bf16[32,3584]{1,0:T(8,128)(2,1)S(1)}, u32[]{:S(2)}, u32[]{:S(2)}) collective-permute-start(bf16[32,3584]{1,0:T(8,128)(2,1)S(1)} %collective-permute-done.1.held_ref.x0), channel_id=1, source_target_pairs={{0,2},{1,3},{2,0},{3,1},{4,6},{5,7},{6,4},{7,5},{8,10},{9,11},{10,... | collective-permute-start | bytes 688136 | tf_op jit(solution)/shard_map/ppermute | solution.py:344
  14.5 1.5 %collective-permute-start.2 = (bf16[32,3584]{1,0:T(8,128)(2,1)S(1)}, bf16[32,3584]{1,0:T(8,128)(2,1)S(1)}, u32[]{:S(2)}, u32[]{:S(2)}) collective-permute-start(bf16[32,3584]{1,0:T(8,128)(2,1)S(1)} %collective-permute-done.1.held_ref.x0), channel_id=1, source_target_pairs={{0,1},{1,0},{2,3},{3,2},{4,5},{5,4},{6,7},{7,6},{8,9},{9,8},{10,11... | collective-permute-start | bytes 688136 | tf_op jit(solution)/shard_map/ppermute | solution.py:344
  16.0 0.9 %core_logits.1 = (f32[128,512]{1,0:T(8,128)S(1)}, f32[8,128]{1,0:T(8,128)S(1)}) custom-call(bf16[128,3584]{1,0:T(8,128)(2,1)S(1)} %copy-done, bf16[3584,512]{1,0:T(8,128)(2,1)S(1)} %collective-permute-done.5.w_ref.other_ref.refs_12_, bf16[32,3584]{1,0:T(8,128)(2,1)S(1)} %collective-permute-done.1.held_ref.x0), custom_call_target="tpu_custom_call" | custom-call | flops 469762048 | bytes 4587520 | tf_op jit(solution)/shard_map/core_logits/pallas_call | solution.py:143
  16.9 0.3 collective-permute-done.7.taught_core_ref
  17.2 3.0 %collective-permute-done.4.x3 = bf16[32,3584]{1,0:T(8,128)(2,1)S(1)} collective-permute-done((bf16[32,3584]{1,0:T(8,128)(2,1)S(1)}, bf16[32,3584]{1,0:T(8,128)(2,1)S(1)}, u32[]{:S(2)}, u32[]{:S(2)}) %collective-permute-start.4) | collective-permute-done | bytes 229408 | tf_op jit(solution)/shard_map/ppermute | solution.py:344
  20.2 0.5 collective-permute-done.3.x2
  20.7 1.3 %collective-permute-done.2.x1 = bf16[32,3584]{1,0:T(8,128)(2,1)S(1)} collective-permute-done((bf16[32,3584]{1,0:T(8,128)(2,1)S(1)}, bf16[32,3584]{1,0:T(8,128)(2,1)S(1)}, u32[]{:S(2)}, u32[]{:S(2)}) %collective-permute-start.2) | collective-permute-done | bytes 229408 | tf_op jit(solution)/shard_map/ppermute | solution.py:344
  22.0 1.2 %collective-permute-start.14 = (bf16[2,128,512]{2,1,0:T(8,128)(2,1)S(1)}, bf16[2,128,512]{2,1,0:T(8,128)(2,1)S(1)}, u32[]{:S(2)}, u32[]{:S(2)}) collective-permute-start(bf16[2,128,512]{2,1,0:T(8,128)(2,1)S(1)} %get-tuple-element.85.gone_ref), channel_id=1, source_target_pairs={{0,16},{1,17},{2,18},{3,19},{4,20},{5,21},{6,22},{7,23},{8,24},{9,... | collective-permute-start | bytes 786440 | tf_op jit(solution)/shard_map/ppermute | solution.py:344
  23.2 2.0 %far_logits.1 = (f32[128,512]{1,0:T(8,128)S(1)}, f32[128,512]{1,0:T(8,128)S(1)}, bf16[128,3584]{1,0:T(8,128)(2,1)S(1)}, f32[2,8,128]{2,1,0:T(8,128)S(1)}) custom-call(s32[4]{0:T(128)S(1)} %get-tuple-element.55.spots_ref, bf16[32,3584]{1,0:T(8,128)(2,1)S(1)} %collective-permute-done.1.held_ref.x0, bf16[32,3584]{1,0:T(8,128)(2,1)S(1)} %collective-permute-done.2.x1, ...), custom_call_target="tpu_custom_call" | custom-call | flops 939524096 | bytes 8257536 | tf_op jit(solution)/shard_map/far_logits/pallas_call | solution.py:186
  25.2 0.0 copy-start.2
  25.2 0.1 collective-permute-start.16
  25.3 4.0 %collective-permute-done.14.a2 = bf16[2,128,512]{2,1,0:T(8,128)(2,1)S(1)} collective-permute-done((bf16[2,128,512]{2,1,0:T(8,128)(2,1)S(1)}, bf16[2,128,512]{2,1,0:T(8,128)(2,1)S(1)}, u32[]{:S(2)}, u32[]{:S(2)}) %collective-permute-start.14) | collective-permute-done | bytes 262176 | tf_op jit(solution)/shard_map/ppermute | solution.py:344
  29.3 2.1 %collective-permute-start.10 = (f32[2,8,128]{2,1,0:T(8,128)S(1)}, f32[2,8,128]{2,1,0:T(8,128)S(1)}, u32[]{:S(2)}, u32[]{:S(2)}) collective-permute-start(f32[2,8,128]{2,1,0:T(8,128)S(1)} %get-tuple-element.78.refs_0_), channel_id=1, source_target_pairs={{0,17},{1,16},{2,19},{3,18},{4,21},{5,20},{6,23},{7,22},{8,25},{9,... | collective-permute-start | bytes 24584 | tf_op jit(solution)/shard_map/ppermute | solution.py:344
  31.4 0.5 collective-permute-start.9
  31.9 0.9 %collective-permute-start.8 = (f32[2,8,128]{2,1,0:T(8,128)S(1)}, f32[2,8,128]{2,1,0:T(8,128)S(1)}, u32[]{:S(2)}, u32[]{:S(2)}) collective-permute-start(f32[2,8,128]{2,1,0:T(8,128)S(1)} %get-tuple-element.78.refs_0_), channel_id=1, source_target_pairs={{0,16},{1,17},{2,18},{3,19},{4,20},{5,21},{6,22},{7,23},{8,24},{9,... | collective-permute-start | bytes 24584 | tf_op jit(solution)/shard_map/ppermute | solution.py:344
  32.8 1.1 %collective-permute-done.10.refs_3_ = f32[2,8,128]{2,1,0:T(8,128)S(1)} collective-permute-done((f32[2,8,128]{2,1,0:T(8,128)S(1)}, f32[2,8,128]{2,1,0:T(8,128)S(1)}, u32[]{:S(2)}, u32[]{:S(2)}) %collective-permute-start.10) | collective-permute-done | bytes 8224 | tf_op jit(solution)/shard_map/ppermute | solution.py:344
  33.8 1.2 %collective-permute-done.9.refs_2_ = f32[2,8,128]{2,1,0:T(8,128)S(1)} collective-permute-done((f32[2,8,128]{2,1,0:T(8,128)S(1)}, f32[2,8,128]{2,1,0:T(8,128)S(1)}, u32[]{:S(2)}, u32[]{:S(2)}) %collective-permute-start.9) | collective-permute-done | bytes 8224 | tf_op jit(solution)/shard_map/ppermute | solution.py:344
  35.0 0.5 collective-permute-done.8.refs_1_
  35.6 2.7 %collective-permute-start.13 = (f32[2,8,128]{2,1,0:T(8,128)S(1)}, f32[2,8,128]{2,1,0:T(8,128)S(1)}, u32[]{:S(2)}, u32[]{:S(2)}) collective-permute-start(f32[2,8,128]{2,1,0:T(8,128)S(1)} %merge_stats.1.refs_1_), channel_id=1, source_target_pairs={{0,6},{1,7},{2,4},{3,5},{4,2},{5,3},{6,0},{7,1},{8,14},{9,15},{10,... | collective-permute-start | bytes 24584 | tf_op jit(solution)/shard_map/ppermute | solution.py:344
  38.3 0.0 collective-permute-start.12
  38.3 1.7 %collective-permute-start.11 = (f32[2,8,128]{2,1,0:T(8,128)S(1)}, f32[2,8,128]{2,1,0:T(8,128)S(1)}, u32[]{:S(2)}, u32[]{:S(2)}) collective-permute-start(f32[2,8,128]{2,1,0:T(8,128)S(1)} %merge_stats.1.refs_1_), channel_id=1, source_target_pairs={{0,2},{1,3},{2,0},{3,1},{4,6},{5,7},{6,4},{7,5},{8,10},{9,11},{10,... | collective-permute-start | bytes 24584 | tf_op jit(solution)/shard_map/ppermute | solution.py:344
  40.1 1.3 %teacher_rows.1.refs_10_ = bf16[2,128,1024]{2,1,0:T(8,128)(2,1)S(1)} custom-call(s32[2]{0:T(128)S(1)} %pad_add_fusion.2.at_ref, s32[4,1,128]{2,1,0:T(1,128)S(1)} %bitcast.42, bf16[2,128,512]{2,1,0:T(8,128)(2,1)S(1)} %get-tuple-element.69.kept_ref.a0, bf16[2,128,512]{2,1,0:T(8,128)(2,1)S(1)} %collective-permute-done.6.a1, ...), custom_call_target="tpu_custom_call" | custom-call | flops 268435456 | bytes 1572864 | tf_op jit(solution)/shard_map/teacher_rows/pallas_call | solution.py:80
  41.4 1.5 %collective-permute-done.12.refs_3_ = f32[2,8,128]{2,1,0:T(8,128)S(1)} collective-permute-done((f32[2,8,128]{2,1,0:T(8,128)S(1)}, f32[2,8,128]{2,1,0:T(8,128)S(1)}, u32[]{:S(2)}, u32[]{:S(2)}) %collective-permute-start.12) | collective-permute-done | bytes 8224 | tf_op jit(solution)/shard_map/ppermute | solution.py:344
  42.9 4.5 %back_rows.1 = (bf16[256,512]{1,0:T(8,128)(2,1)S(1)}, bf16[256,512]{1,0:T(8,128)(2,1)S(1)}, bf16[128,1152]{1,0:T(8,128)(2,1)S(1)}, bf16[128,1152]{1,0:T(8,128)(2...) custom-call(s32[4]{0:T(128)S(1)} %get-tuple-element.52.refs_0_, ...), custom_call_target="tpu_custom_call" | custom-call | flops 1879048192 | bytes 7340032 | tf_op jit(solution)/shard_map/back_rows/pallas_call | solution.py:293
  47.4 0.1 collective-permute-start.17
  47.5 0.9 %collective-permute-start.20 = (bf16[128,1280]{1,0:T(8,128)(2,1)S(1)}, bf16[128,1280]{1,0:T(8,128)(2,1)S(1)}, u32[]{:S(2)}, u32[]{:S(2)}) collective-permute-start(bf16[128,1280]{1,0:T(8,128)(2,1)S(1)} %get-tuple-element.95), channel_id=1, source_target_pairs={{0,2},{1,3},{2,0},{3,1},{4,6},{5,7},{6,4},{7,5},{8,10},{9,11},{10,... | collective-permute-start | bytes 983048 | tf_op jit(solution)/shard_map/ppermute | solution.py:344
  48.4 0.9 %collective-permute-start.18 = (bf16[128,1152]{1,0:T(8,128)(2,1)S(1)}, bf16[128,1152]{1,0:T(8,128)(2,1)S(1)}, u32[]{:S(2)}, u32[]{:S(2)}) collective-permute-start(bf16[128,1152]{1,0:T(8,128)(2,1)S(1)} %get-tuple-element.93), channel_id=1, source_target_pairs={{0,16},{1,17},{2,18},{3,19},{4,20},{5,21},{6,22},{7,23},{8,24},{9,... | collective-permute-start | bytes 884744 | tf_op jit(solution)/shard_map/ppermute | solution.py:344
  49.3 1.5 %collective-permute-start.19 = (bf16[128,1152]{1,0:T(8,128)(2,1)S(1)}, bf16[128,1152]{1,0:T(8,128)(2,1)S(1)}, u32[]{:S(2)}, u32[]{:S(2)}) collective-permute-start(bf16[128,1152]{1,0:T(8,128)(2,1)S(1)} %get-tuple-element.94), channel_id=1, source_target_pairs={{0,1},{1,0},{2,3},{3,2},{4,5},{5,4},{6,7},{7,6},{8,9},{9,8},{10,11... | collective-permute-start | bytes 884744 | tf_op jit(solution)/shard_map/ppermute | solution.py:344
  50.8 5.2 %head_gradient.1 = bf16[3584,512]{1,0:T(8,128)(2,1)} custom-call(bf16[128,3584]{1,0:T(8,128)(2,1)S(1)} %copy-done, bf16[128,3584]{1,0:T(8,128)(2,1)S(1)} %get-tuple-element.89.r1, bf16[128,3584]{1,0:T(8,128)(2,1)S(1)} %collective-permute-done.r2, bf16[128,3584]{1,0:T(8,128)(2,1)S(1)} %collective-permute-done.16.r3, ...), custom_call_target="tpu_custom_call" | custom-call | flops 1879048192 | bytes 7340032 | tf_op jit(solution)/shard_map/head_gradient/pallas_call | solution.py:319
  56.0 1.5 %collective-permute-done.18 = bf16[128,1152]{1,0:T(8,128)(2,1)S(1)} collective-permute-done((bf16[128,1152]{1,0:T(8,128)(2,1)S(1)}, bf16[128,1152]{1,0:T(8,128)(2,1)S(1)}, u32[]{:S(2)}, u32[]{:S(2)}) %collective-permute-start.18) | collective-permute-done | bytes 294944 | tf_op jit(solution)/shard_map/ppermute | solution.py:344
  57.5 0.6 collective-permute-done.19
  58.1 1.6 %collective-permute-start.21 = (bf16[1,2,2,1,16,1152]{5,4,3,2,1,0:T(8,128)(2,1)S(1)}, bf16[1,2,2,1,16,1152]{5,4,3,2,1,0:T(8,128)(2,1)S(1)}, u32[]{:S(2)}, u32[]{:S(2)}) collective-permute-start(bf16[1,2,2,1,16,1152]{5,4,3,2,1,0:T(8,128)(2,1)S(1)} %fusion.1), channel_id=1, source_target_pairs={{0,1},{1,0},{2,3},{3,2},{4,5},{5,4},{6,7},{7,6},{8,9},{9,8},{10,11... | collective-permute-start | bytes 442376 | tf_op jit(solution)/shard_map/ppermute | solution.py:344
  59.8 1.3 %collective-permute-start.24 = (bf16[2,2,1,1,16,1152]{5,4,3,2,1,0:T(8,128)(2,1)S(1)}, bf16[2,2,1,1,16,1152]{5,4,3,2,1,0:T(8,128)(2,1)S(1)}, u32[]{:S(2)}, u32[]{:S(2)}) collective-permute-start(bf16[2,2,1,1,16,1152]{5,4,3,2,1,0:T(8,128)(2,1)S(1)} %fusion), channel_id=1, source_target_pairs={{0,2},{1,3},{2,0},{3,1},{4,6},{5,7},{6,4},{7,5},{8,10},{9,11},{10,... | collective-permute-start | bytes 442376 | tf_op jit(solution)/shard_map/ppermute | solution.py:344
  61.0 1.2 %collective-permute-start.27 = (bf16[1,2,1,2,16,1280]{5,4,3,2,1,0:T(8,128)(2,1)S(1)}, bf16[1,2,1,2,16,1280]{5,4,3,2,1,0:T(8,128)(2,1)S(1)}, u32[]{:S(2)}, u32[]{:S(2)}) collective-permute-start(bf16[1,2,1,2,16,1280]{5,4,3,2,1,0:T(8,128)(2,1)S(1)} %bitcast.59), channel_id=1, source_target_pairs={{0,16},{1,17},{2,18},{3,19},{4,20},{5,21},{6,22},{7,23},{8,24},{9,... | collective-permute-start | bytes 491528 | tf_op jit(solution)/shard_map/ppermute | solution.py:344
  62.2 1.1 %collective-permute-done.21 = bf16[1,2,2,1,16,1152]{5,4,3,2,1,0:T(8,128)(2,1)S(1)} collective-permute-done((bf16[1,2,2,1,16,1152]{5,4,3,2,1,0:T(8,128)(2,1)S(1)}, bf16[1,2,2,1,16,1152]{5,4,3,2,1,0:T(8,128)(2,1)S(1)}, u32[]{:S(2)}, u32[]{:S(2)}) %collective-permute-start.21) | collective-permute-done | bytes 147488 | tf_op jit(solution)/shard_map/ppermute | solution.py:344
  63.3 1.3 %collective-permute-start.22 = (bf16[1,2,1,1,16,1152]{5,4,3,2,1,0:T(8,128)(2,1)S(1)}, bf16[1,2,1,1,16,1152]{5,4,3,2,1,0:T(8,128)(2,1)S(1)}, u32[]{:S(2)}, u32[]{:S(2)}) collective-permute-start(bf16[1,2,1,1,16,1152]{5,4,3,2,1,0:T(8,128)(2,1)S(1)} %fusion.7), channel_id=1, source_target_pairs={{0,2},{1,3},{2,0},{3,1},{4,6},{5,7},{6,4},{7,5},{8,10},{9,11},{10,... | collective-permute-start | bytes 221192 | tf_op jit(solution)/shard_map/ppermute | solution.py:344
  64.6 1.1 %collective-permute-done.24 = bf16[2,2,1,1,16,1152]{5,4,3,2,1,0:T(8,128)(2,1)S(1)} collective-permute-done((bf16[2,2,1,1,16,1152]{5,4,3,2,1,0:T(8,128)(2,1)S(1)}, bf16[2,2,1,1,16,1152]{5,4,3,2,1,0:T(8,128)(2,1)S(1)}, u32[]{:S(2)}, u32[]{:S(2)}) %collective-permute-start.24) | collective-permute-done | bytes 147488 | tf_op jit(solution)/shard_map/ppermute | solution.py:344
  65.8 1.2 %collective-permute-start.25 = (bf16[1,2,1,1,16,1152]{5,4,3,2,1,0:T(8,128)(2,1)S(1)}, bf16[1,2,1,1,16,1152]{5,4,3,2,1,0:T(8,128)(2,1)S(1)}, u32[]{:S(2)}, u32[]{:S(2)}) collective-permute-start(bf16[1,2,1,1,16,1152]{5,4,3,2,1,0:T(8,128)(2,1)S(1)} %fusion.5), channel_id=1, source_target_pairs={{0,16},{1,17},{2,18},{3,19},{4,20},{5,21},{6,22},{7,23},{8,24},{9,... | collective-permute-start | bytes 221192 | tf_op jit(solution)/shard_map/ppermute | solution.py:344
  67.1 0.4 collective-permute-start.28
  67.5 0.3 collective-permute-done.22
  67.8 1.9 %collective-permute-start.23 = (bf16[1,1,1,1,16,1152]{5,4,3,2,1,0:T(8,128)(2,1)S(1)}, bf16[1,1,1,1,16,1152]{5,4,3,2,1,0:T(8,128)(2,1)S(1)}, u32[]{:S(2)}, u32[]{:S(2)}) collective-permute-start(bf16[1,1,1,1,16,1152]{5,4,3,2,1,0:T(8,128)(2,1)S(1)} %fusion.22), channel_id=1, source_target_pairs={{0,4},{1,5},{2,6},{3,7},{4,0},{5,1},{6,2},{7,3},{8,12},{9,13},{10,... | collective-permute-start | bytes 110600 | tf_op jit(solution)/shard_map/ppermute | solution.py:344
  69.7 0.6 collective-permute-done.25
  70.2 1.2 %collective-permute-start.26 = (bf16[1,1,1,1,16,1152]{5,4,3,2,1,0:T(8,128)(2,1)S(1)}, bf16[1,1,1,1,16,1152]{5,4,3,2,1,0:T(8,128)(2,1)S(1)}, u32[]{:S(2)}, u32[]{:S(2)}) collective-permute-start(bf16[1,1,1,1,16,1152]{5,4,3,2,1,0:T(8,128)(2,1)S(1)} %fusion.16), channel_id=1, source_target_pairs={{0,4},{1,5},{2,6},{3,7},{4,0},{5,1},{6,2},{7,3},{8,12},{9,13},{10,... | collective-permute-start | bytes 110600 | tf_op jit(solution)/shard_map/ppermute | solution.py:344
  71.4 0.2 collective-permute-done.28
  71.6 2.0 %collective-permute-start.29 = (bf16[1,1,1,1,16,1280]{5,4,3,2,1,0:T(8,128)(2,1)S(1)}, bf16[1,1,1,1,16,1280]{5,4,3,2,1,0:T(8,128)(2,1)S(1)}, u32[]{:S(2)}, u32[]{:S(2)}) collective-permute-start(bf16[1,1,1,1,16,1280]{5,4,3,2,1,0:T(8,128)(2,1)S(1)} %fusion.10), channel_id=1, source_target_pairs={{0,4},{1,5},{2,6},{3,7},{4,0},{5,1},{6,2},{7,3},{8,12},{9,13},{10,... | collective-permute-start | bytes 122888 | tf_op jit(solution)/shard_map/ppermute | solution.py:344
  73.5 0.3 collective-permute-done.23
  73.8 1.3 %collective-permute-done.26 = bf16[1,1,1,1,16,1152]{5,4,3,2,1,0:T(8,128)(2,1)S(1)} collective-permute-done((bf16[1,1,1,1,16,1152]{5,4,3,2,1,0:T(8,128)(2,1)S(1)}, bf16[1,1,1,1,16,1152]{5,4,3,2,1,0:T(8,128)(2,1)S(1)}, u32[]{:S(2)}, u32[]{:S(2)}) %collective-permute-start.26) | collective-permute-done | bytes 36896 | tf_op jit(solution)/shard_map/ppermute | solution.py:344
  75.2 1.4 %collective-permute-done.29 = bf16[1,1,1,1,16,1280]{5,4,3,2,1,0:T(8,128)(2,1)S(1)} collective-permute-done((bf16[1,1,1,1,16,1280]{5,4,3,2,1,0:T(8,128)(2,1)S(1)}, bf16[1,1,1,1,16,1280]{5,4,3,2,1,0:T(8,128)(2,1)S(1)}, u32[]{:S(2)}, u32[]{:S(2)}) %collective-permute-start.29) | collective-permute-done | bytes 40992 | tf_op jit(solution)/shard_map/ppermute | solution.py:344
  76.6 0.7 maximum_bitcast_fusion
  (32 shorter events, 0.5 us)
Async XLA Ops:
  0.6 7.3 %copy-start = (bf16[128,3584]{1,0:T(8,128)(2,1)S(1)}, bf16[128,3584]{1,0:T(8,128)(2,1)}, u32[]{:S(2)}) copy-start(bf16[128,3584]{1,0:T(8,128)(2,1)} %r0.1) | copy-start | bytes 2752516
  0.8 15.2 %collective-permute-start.5 = (bf16[3584,512]{1,0:T(8,128)(2,1)}, bf16[3584,512]{1,0:T(8,128)(2,1)S(1)}, u32[]{:S(2)}, u32[]{:S(2)}) collective-permute-start(bf16[3584,512]{1,0:T(8,128)(2,1)} %refs_1_.1), channel_id=1, source_target_pairs={{0,8},{1,9},{2,10},{3,11},{4,12},{5,13},{6,14},{7,15},{8,0},{9,1},... | collective-permute-start | bytes 11010056 | tf_op jit(solution)/shard_map/ppermute | solution.py:344
  1.3 13.3 %collective-permute-start = (bf16[128,3584]{1,0:T(8,128)(2,1)}, bf16[128,3584]{1,0:T(8,128)(2,1)S(1)}, u32[]{:S(2)}, u32[]{:S(2)}) collective-permute-start(bf16[128,3584]{1,0:T(8,128)(2,1)} %r0.1), channel_id=1, source_target_pairs={{0,8},{1,9},{2,10},{3,11},{4,12},{5,13},{6,14},{7,15},{8,0},{9,1},... | collective-permute-start | bytes 2752520 | tf_op jit(solution)/shard_map/ppermute | solution.py:344
  2.4 9.7 %collective-permute-start.1 = (bf16[32,3584]{1,0:T(8,128)(2,1)S(1)}, bf16[32,3584]{1,0:T(8,128)(2,1)S(1)}, u32[]{:S(2)}, u32[]{:S(2)}) collective-permute-start(bf16[32,3584]{1,0:T(8,128)(2,1)S(1)} %constant_dynamic-slice_fusion.1), channel_id=1, source_target_pairs={{0,16},{1,17},{2,18},{3,19},{4,20},{5,21},{6,22},{7,23},{8,24},{9,... | collective-permute-start | bytes 688136 | tf_op jit(solution)/shard_map/ppermute | solution.py:344
  7.9 2.1 %copy-start.1 = (bf16[3584,512]{1,0:T(8,128)(2,1)S(1)}, bf16[3584,512]{1,0:T(8,128)(2,1)}, u32[]{:S(2)}) copy-start(bf16[3584,512]{1,0:T(8,128)(2,1)} %refs_1_.1) | copy-start | bytes 11010052
  10.0 13.2 %copy-start.3 = (s32[128]{0:T(128)S(1)}, s32[128]{0:T(128)}, u32[]{:S(2)}) copy-start(s32[128]{0:T(128)} %param.6) | copy-start | bytes 1540
  12.1 9.9 %collective-permute-start.6 = (bf16[2,128,512]{2,1,0:T(8,128)(2,1)S(1)}, bf16[2,128,512]{2,1,0:T(8,128)(2,1)S(1)}, u32[]{:S(2)}, u32[]{:S(2)}) collective-permute-start(bf16[2,128,512]{2,1,0:T(8,128)(2,1)S(1)} %get-tuple-element.69.kept_ref.a0), channel_id=1, source_target_pairs={{0,8},{1,9},{2,10},{3,11},{4,12},{5,13},{6,14},{7,15},{8,0},{9,1},... | collective-permute-start | bytes 786440 | tf_op jit(solution)/shard_map/ppermute | solution.py:344
  12.1 8.0 %collective-permute-start.4 = (bf16[32,3584]{1,0:T(8,128)(2,1)S(1)}, bf16[32,3584]{1,0:T(8,128)(2,1)S(1)}, u32[]{:S(2)}, u32[]{:S(2)}) collective-permute-start(bf16[32,3584]{1,0:T(8,128)(2,1)S(1)} %constant_dynamic-slice_fusion), channel_id=1, source_target_pairs={{0,16},{1,17},{2,18},{3,19},{4,20},{5,21},{6,22},{7,23},{8,24},{9,... | collective-permute-start | bytes 688136 | tf_op jit(solution)/shard_map/ppermute | solution.py:344
  13.0 7.7 %collective-permute-start.3 = (bf16[32,3584]{1,0:T(8,128)(2,1)S(1)}, bf16[32,3584]{1,0:T(8,128)(2,1)S(1)}, u32[]{:S(2)}, u32[]{:S(2)}) collective-permute-start(bf16[32,3584]{1,0:T(8,128)(2,1)S(1)} %collective-permute-done.1.held_ref.x0), channel_id=1, source_target_pairs={{0,2},{1,3},{2,0},{3,1},{4,6},{5,7},{6,4},{7,5},{8,10},{9,11},{10,... | collective-permute-start | bytes 688136 | tf_op jit(solution)/shard_map/ppermute | solution.py:344
  14.5 7.5 %collective-permute-start.2 = (bf16[32,3584]{1,0:T(8,128)(2,1)S(1)}, bf16[32,3584]{1,0:T(8,128)(2,1)S(1)}, u32[]{:S(2)}, u32[]{:S(2)}) collective-permute-start(bf16[32,3584]{1,0:T(8,128)(2,1)S(1)} %collective-permute-done.1.held_ref.x0), channel_id=1, source_target_pairs={{0,1},{1,0},{2,3},{3,2},{4,5},{5,4},{6,7},{7,6},{8,9},{9,8},{10,11... | collective-permute-start | bytes 688136 | tf_op jit(solution)/shard_map/ppermute | solution.py:344
  16.0 1.2 %collective-permute-start.7 = (f32[8,128]{1,0:T(8,128)S(1)}, f32[8,128]{1,0:T(8,128)S(1)}, u32[]{:S(2)}, u32[]{:S(2)}) collective-permute-start(f32[8,128]{1,0:T(8,128)S(1)} %taught_stats.1.taught_ref), channel_id=1, source_target_pairs={{0,8},{1,9},{2,10},{3,11},{4,12},{5,13},{6,14},{7,15},{8,0},{9,1},... | collective-permute-start | bytes 12296 | tf_op jit(solution)/shard_map/ppermute | solution.py:344
  22.0 7.3 %collective-permute-start.14 = (bf16[2,128,512]{2,1,0:T(8,128)(2,1)S(1)}, bf16[2,128,512]{2,1,0:T(8,128)(2,1)S(1)}, u32[]{:S(2)}, u32[]{:S(2)}) collective-permute-start(bf16[2,128,512]{2,1,0:T(8,128)(2,1)S(1)} %get-tuple-element.85.gone_ref), channel_id=1, source_target_pairs={{0,16},{1,17},{2,18},{3,19},{4,20},{5,21},{6,22},{7,23},{8,24},{9,... | collective-permute-start | bytes 786440 | tf_op jit(solution)/shard_map/ppermute | solution.py:344
  25.2 14.9 %copy-start.2 = (s32[512]{0:T(512)S(1)}, s32[512]{0:T(512)}, u32[]{:S(2)}) copy-start(s32[512]{0:T(512)} %param.7) | copy-start | bytes 6148
  25.2 25.6 %collective-permute-start.16 = (bf16[128,3584]{1,0:T(8,128)(2,1)S(1)}, bf16[128,3584]{1,0:T(8,128)(2,1)S(1)}, u32[]{:S(2)}, u32[]{:S(2)}) collective-permute-start(bf16[128,3584]{1,0:T(8,128)(2,1)S(1)} %get-tuple-element.89.r1), channel_id=1, source_target_pairs={{0,8},{1,9},{2,10},{3,11},{4,12},{5,13},{6,14},{7,15},{8,0},{9,1},... | collective-permute-start | bytes 2752520 | tf_op jit(solution)/shard_map/ppermute | solution.py:344
  29.3 10.8 %collective-permute-start.15 = (bf16[2,128,512]{2,1,0:T(8,128)(2,1)S(1)}, bf16[2,128,512]{2,1,0:T(8,128)(2,1)S(1)}, u32[]{:S(2)}, u32[]{:S(2)}) collective-permute-start(bf16[2,128,512]{2,1,0:T(8,128)(2,1)S(1)} %collective-permute-done.14.a2), channel_id=1, source_target_pairs={{0,8},{1,9},{2,10},{3,11},{4,12},{5,13},{6,14},{7,15},{8,0},{9,1},... | collective-permute-start | bytes 786440 | tf_op jit(solution)/shard_map/ppermute | solution.py:344
  29.3 4.6 %collective-permute-start.10 = (f32[2,8,128]{2,1,0:T(8,128)S(1)}, f32[2,8,128]{2,1,0:T(8,128)S(1)}, u32[]{:S(2)}, u32[]{:S(2)}) collective-permute-start(f32[2,8,128]{2,1,0:T(8,128)S(1)} %get-tuple-element.78.refs_0_), channel_id=1, source_target_pairs={{0,17},{1,16},{2,19},{3,18},{4,21},{5,20},{6,23},{7,22},{8,25},{9,... | collective-permute-start | bytes 24584 | tf_op jit(solution)/shard_map/ppermute | solution.py:344
  31.4 3.7 %collective-permute-start.9 = (f32[2,8,128]{2,1,0:T(8,128)S(1)}, f32[2,8,128]{2,1,0:T(8,128)S(1)}, u32[]{:S(2)}, u32[]{:S(2)}) collective-permute-start(f32[2,8,128]{2,1,0:T(8,128)S(1)} %get-tuple-element.78.refs_0_), channel_id=1, source_target_pairs={{0,1},{1,0},{2,3},{3,2},{4,5},{5,4},{6,7},{7,6},{8,9},{9,8},{10,11... | collective-permute-start | bytes 24584 | tf_op jit(solution)/shard_map/ppermute | solution.py:344
  31.9 3.7 %collective-permute-start.8 = (f32[2,8,128]{2,1,0:T(8,128)S(1)}, f32[2,8,128]{2,1,0:T(8,128)S(1)}, u32[]{:S(2)}, u32[]{:S(2)}) collective-permute-start(f32[2,8,128]{2,1,0:T(8,128)S(1)} %get-tuple-element.78.refs_0_), channel_id=1, source_target_pairs={{0,16},{1,17},{2,18},{3,19},{4,20},{5,21},{6,22},{7,23},{8,24},{9,... | collective-permute-start | bytes 24584 | tf_op jit(solution)/shard_map/ppermute | solution.py:344
  35.6 5.7 %collective-permute-start.13 = (f32[2,8,128]{2,1,0:T(8,128)S(1)}, f32[2,8,128]{2,1,0:T(8,128)S(1)}, u32[]{:S(2)}, u32[]{:S(2)}) collective-permute-start(f32[2,8,128]{2,1,0:T(8,128)S(1)} %merge_stats.1.refs_1_), channel_id=1, source_target_pairs={{0,6},{1,7},{2,4},{3,5},{4,2},{5,3},{6,0},{7,1},{8,14},{9,15},{10,... | collective-permute-start | bytes 24584 | tf_op jit(solution)/shard_map/ppermute | solution.py:344
  38.3 4.6 %collective-permute-start.12 = (f32[2,8,128]{2,1,0:T(8,128)S(1)}, f32[2,8,128]{2,1,0:T(8,128)S(1)}, u32[]{:S(2)}, u32[]{:S(2)}) collective-permute-start(f32[2,8,128]{2,1,0:T(8,128)S(1)} %merge_stats.1.refs_1_), channel_id=1, source_target_pairs={{0,4},{1,5},{2,6},{3,7},{4,0},{5,1},{6,2},{7,3},{8,12},{9,13},{10,... | collective-permute-start | bytes 24584 | tf_op jit(solution)/shard_map/ppermute | solution.py:344
  38.3 4.6 %collective-permute-start.11 = (f32[2,8,128]{2,1,0:T(8,128)S(1)}, f32[2,8,128]{2,1,0:T(8,128)S(1)}, u32[]{:S(2)}, u32[]{:S(2)}) collective-permute-start(f32[2,8,128]{2,1,0:T(8,128)S(1)} %merge_stats.1.refs_1_), channel_id=1, source_target_pairs={{0,2},{1,3},{2,0},{3,1},{4,6},{5,7},{6,4},{7,5},{8,10},{9,11},{10,... | collective-permute-start | bytes 24584 | tf_op jit(solution)/shard_map/ppermute | solution.py:344
  47.4 3.3 %collective-permute-start.17 = (bf16[256,512]{1,0:T(8,128)(2,1)S(1)}, bf16[256,512]{1,0:T(8,128)(2,1)S(1)}, u32[]{:S(2)}, u32[]{:S(2)}) collective-permute-start(bf16[256,512]{1,0:T(8,128)(2,1)S(1)} %get-tuple-element.92), channel_id=1, source_target_pairs={{0,8},{1,9},{2,10},{3,11},{4,12},{5,13},{6,14},{7,15},{8,0},{9,1},... | collective-permute-start | bytes 786440 | tf_op jit(solution)/shard_map/ppermute | solution.py:344
  47.5 10.5 %collective-permute-start.20 = (bf16[128,1280]{1,0:T(8,128)(2,1)S(1)}, bf16[128,1280]{1,0:T(8,128)(2,1)S(1)}, u32[]{:S(2)}, u32[]{:S(2)}) collective-permute-start(bf16[128,1280]{1,0:T(8,128)(2,1)S(1)} %get-tuple-element.95), channel_id=1, source_target_pairs={{0,2},{1,3},{2,0},{3,1},{4,6},{5,7},{6,4},{7,5},{8,10},{9,11},{10,... | collective-permute-start | bytes 983048 | tf_op jit(solution)/shard_map/ppermute | solution.py:344
  48.4 9.1 %collective-permute-start.18 = (bf16[128,1152]{1,0:T(8,128)(2,1)S(1)}, bf16[128,1152]{1,0:T(8,128)(2,1)S(1)}, u32[]{:S(2)}, u32[]{:S(2)}) collective-permute-start(bf16[128,1152]{1,0:T(8,128)(2,1)S(1)} %get-tuple-element.93), channel_id=1, source_target_pairs={{0,16},{1,17},{2,18},{3,19},{4,20},{5,21},{6,22},{7,23},{8,24},{9,... | collective-permute-start | bytes 884744 | tf_op jit(solution)/shard_map/ppermute | solution.py:344
  49.3 8.8 %collective-permute-start.19 = (bf16[128,1152]{1,0:T(8,128)(2,1)S(1)}, bf16[128,1152]{1,0:T(8,128)(2,1)S(1)}, u32[]{:S(2)}, u32[]{:S(2)}) collective-permute-start(bf16[128,1152]{1,0:T(8,128)(2,1)S(1)} %get-tuple-element.94), channel_id=1, source_target_pairs={{0,1},{1,0},{2,3},{3,2},{4,5},{5,4},{6,7},{7,6},{8,9},{9,8},{10,11... | collective-permute-start | bytes 884744 | tf_op jit(solution)/shard_map/ppermute | solution.py:344
  58.1 5.2 %collective-permute-start.21 = (bf16[1,2,2,1,16,1152]{5,4,3,2,1,0:T(8,128)(2,1)S(1)}, bf16[1,2,2,1,16,1152]{5,4,3,2,1,0:T(8,128)(2,1)S(1)}, u32[]{:S(2)}, u32[]{:S(2)}) collective-permute-start(bf16[1,2,2,1,16,1152]{5,4,3,2,1,0:T(8,128)(2,1)S(1)} %fusion.1), channel_id=1, source_target_pairs={{0,1},{1,0},{2,3},{3,2},{4,5},{5,4},{6,7},{7,6},{8,9},{9,8},{10,11... | collective-permute-start | bytes 442376 | tf_op jit(solution)/shard_map/ppermute | solution.py:344
  59.8 6.0 %collective-permute-start.24 = (bf16[2,2,1,1,16,1152]{5,4,3,2,1,0:T(8,128)(2,1)S(1)}, bf16[2,2,1,1,16,1152]{5,4,3,2,1,0:T(8,128)(2,1)S(1)}, u32[]{:S(2)}, u32[]{:S(2)}) collective-permute-start(bf16[2,2,1,1,16,1152]{5,4,3,2,1,0:T(8,128)(2,1)S(1)} %fusion), channel_id=1, source_target_pairs={{0,2},{1,3},{2,0},{3,1},{4,6},{5,7},{6,4},{7,5},{8,10},{9,11},{10,... | collective-permute-start | bytes 442376 | tf_op jit(solution)/shard_map/ppermute | solution.py:344
  61.0 6.0 %collective-permute-start.27 = (bf16[1,2,1,2,16,1280]{5,4,3,2,1,0:T(8,128)(2,1)S(1)}, bf16[1,2,1,2,16,1280]{5,4,3,2,1,0:T(8,128)(2,1)S(1)}, u32[]{:S(2)}, u32[]{:S(2)}) collective-permute-start(bf16[1,2,1,2,16,1280]{5,4,3,2,1,0:T(8,128)(2,1)S(1)} %bitcast.59), channel_id=1, source_target_pairs={{0,16},{1,17},{2,18},{3,19},{4,20},{5,21},{6,22},{7,23},{8,24},{9,... | collective-permute-start | bytes 491528 | tf_op jit(solution)/shard_map/ppermute | solution.py:344
  63.3 4.4 %collective-permute-start.22 = (bf16[1,2,1,1,16,1152]{5,4,3,2,1,0:T(8,128)(2,1)S(1)}, bf16[1,2,1,1,16,1152]{5,4,3,2,1,0:T(8,128)(2,1)S(1)}, u32[]{:S(2)}, u32[]{:S(2)}) collective-permute-start(bf16[1,2,1,1,16,1152]{5,4,3,2,1,0:T(8,128)(2,1)S(1)} %fusion.7), channel_id=1, source_target_pairs={{0,2},{1,3},{2,0},{3,1},{4,6},{5,7},{6,4},{7,5},{8,10},{9,11},{10,... | collective-permute-start | bytes 221192 | tf_op jit(solution)/shard_map/ppermute | solution.py:344
  65.8 4.4 %collective-permute-start.25 = (bf16[1,2,1,1,16,1152]{5,4,3,2,1,0:T(8,128)(2,1)S(1)}, bf16[1,2,1,1,16,1152]{5,4,3,2,1,0:T(8,128)(2,1)S(1)}, u32[]{:S(2)}, u32[]{:S(2)}) collective-permute-start(bf16[1,2,1,1,16,1152]{5,4,3,2,1,0:T(8,128)(2,1)S(1)} %fusion.5), channel_id=1, source_target_pairs={{0,16},{1,17},{2,18},{3,19},{4,20},{5,21},{6,22},{7,23},{8,24},{9,... | collective-permute-start | bytes 221192 | tf_op jit(solution)/shard_map/ppermute | solution.py:344
  67.1 4.5 %collective-permute-start.28 = (bf16[1,2,1,1,16,1280]{5,4,3,2,1,0:T(8,128)(2,1)S(1)}, bf16[1,2,1,1,16,1280]{5,4,3,2,1,0:T(8,128)(2,1)S(1)}, u32[]{:S(2)}, u32[]{:S(2)}) collective-permute-start(bf16[1,2,1,1,16,1280]{5,4,3,2,1,0:T(8,128)(2,1)S(1)} %fusion.3), channel_id=1, source_target_pairs={{0,1},{1,0},{2,3},{3,2},{4,5},{5,4},{6,7},{7,6},{8,9},{9,8},{10,11... | collective-permute-start | bytes 245768 | tf_op jit(solution)/shard_map/ppermute | solution.py:344
  67.8 6.0 %collective-permute-start.23 = (bf16[1,1,1,1,16,1152]{5,4,3,2,1,0:T(8,128)(2,1)S(1)}, bf16[1,1,1,1,16,1152]{5,4,3,2,1,0:T(8,128)(2,1)S(1)}, u32[]{:S(2)}, u32[]{:S(2)}) collective-permute-start(bf16[1,1,1,1,16,1152]{5,4,3,2,1,0:T(8,128)(2,1)S(1)} %fusion.22), channel_id=1, source_target_pairs={{0,4},{1,5},{2,6},{3,7},{4,0},{5,1},{6,2},{7,3},{8,12},{9,13},{10,... | collective-permute-start | bytes 110600 | tf_op jit(solution)/shard_map/ppermute | solution.py:344
  70.2 4.9 %collective-permute-start.26 = (bf16[1,1,1,1,16,1152]{5,4,3,2,1,0:T(8,128)(2,1)S(1)}, bf16[1,1,1,1,16,1152]{5,4,3,2,1,0:T(8,128)(2,1)S(1)}, u32[]{:S(2)}, u32[]{:S(2)}) collective-permute-start(bf16[1,1,1,1,16,1152]{5,4,3,2,1,0:T(8,128)(2,1)S(1)} %fusion.16), channel_id=1, source_target_pairs={{0,4},{1,5},{2,6},{3,7},{4,0},{5,1},{6,2},{7,3},{8,12},{9,13},{10,... | collective-permute-start | bytes 110600 | tf_op jit(solution)/shard_map/ppermute | solution.py:344
  71.6 5.0 %collective-permute-start.29 = (bf16[1,1,1,1,16,1280]{5,4,3,2,1,0:T(8,128)(2,1)S(1)}, bf16[1,1,1,1,16,1280]{5,4,3,2,1,0:T(8,128)(2,1)S(1)}, u32[]{:S(2)}, u32[]{:S(2)}) collective-permute-start(bf16[1,1,1,1,16,1280]{5,4,3,2,1,0:T(8,128)(2,1)S(1)} %fusion.10), channel_id=1, source_target_pairs={{0,4},{1,5},{2,6},{3,7},{4,0},{5,1},{6,2},{7,3},{8,12},{9,13},{10,... | collective-permute-start | bytes 122888 | tf_op jit(solution)/shard_map/ppermute | solution.py:344

commit v9 on v8

--- a/solution.py
+++ b/solution.py
@@ -95,60 +95,25 @@
     return columns_to_rows([peak, hard, jnp.sum(soft, axis=1, keepdims=True)])
 
 
-def own_kernel(splits, rows_ref, w_ref, logits_ref, stats_ref, own_ref, sems):
-    step = w_ref.shape[0] // splits
-    copies = []
-    for c in range(splits):
-        part = pl.ds(c * step, step)
-        copies.append(pltpu.make_async_copy(w_ref.at[part], own_ref.at[part], sems.at[c]))
-        copies[c].start()
-    logits = 0.0
-    for c in range(splits):
-        copies[c].wait()
-        part = slice(c * step, (c + 1) * step)
-        logits += jnp.dot(rows_ref[:, part], own_ref[part, :], preferred_element_type=F32)
-    logits_ref[...] = logits
-    stats_ref[...] = student_stats(logits)
-
-
-def own_logits(rows, own):
-    per, depth = rows.shape
-    cols = own.shape[1]
-    splits = 4 if depth % 512 == 0 else 1
-    return pl.pallas_call(
-        lambda *refs: own_kernel(splits, *refs),
-        out_shape=(
-            shape((per, cols), F32),
-            shape((STAT_ROWS, per), F32),
-            shape((depth, cols), BF16),
-        ),
-        in_specs=[VMEM, pl.BlockSpec(memory_space=pl.ANY)],
-        out_specs=(VMEM, VMEM, VMEM),
-        scratch_shapes=[pltpu.SemaphoreType.DMA((splits,))],
-        compiler_params=params(6),
-        cost_estimate=cost(2 * per * depth * cols, (per + 2 * cols) * depth * 2, per * cols),
-        name="own_logits",
-    )(rows, own)
-
-
-def core_kernel(rows_ref, w_ref, held_ref, logits_ref, stats_ref):
+def near_kernel(rows_ref, w_ref, *refs):
+    logits_ref, stats_ref = refs[-2:]
     logits = jnp.dot(rows_ref[...], w_ref[...], preferred_element_type=F32)
     logits_ref[...] = logits
     stats_ref[...] = student_stats(logits)
 
 
-def core_logits(rows, other, held):
+def near_logits(rows, weight, *held):
     per, depth = rows.shape
-    cols = other.shape[1]
-    return pl.pallas_call(
-        core_kernel,
+    cols = weight.shape[1]
+    return pl.pallas_call(
+        near_kernel,
         out_shape=(shape((per, cols), F32), shape((STAT_ROWS, per), F32)),
-        in_specs=[VMEM] * 3,
+        in_specs=[VMEM] * (2 + len(held)),
         out_specs=(VMEM, VMEM),
         compiler_params=params(6),
         cost_estimate=cost(2 * per * depth * cols, (per + cols) * depth * 2, per * cols),
-        name="core_logits",
-    )(rows, other, held)
+        name="near_logits",
+    )(rows, weight, *held)
 
 
 NOTHING = -3.0e38
@@ -162,10 +127,12 @@
     )
 
 
-def far_kernel(spots_ref, x0, x1, x2, x3, own_ref, other_ref, stats_a, stats_b, taught_ref, taught_core_ref, ids_ref, a_ref, b_ref, rows_ref, out_ref):
-    count = x0.shape[0]
-    for k, piece in enumerate((x0, x1, x2, x3)):
-        rows_ref[pl.ds(pl.multiple_of(spots_ref[k], 16), count), :] = piece[...]
+def far_kernel(n, spots_ref, *refs):
+    pieces, refs = refs[:n], refs[n:]
+    own_ref, other_ref, stats_a, stats_b, taught_ref, taught_core_ref, ids_ref = refs[:7]
+    a_ref, b_ref, rows_ref, out_ref = refs[7:]
+    for k, piece in enumerate(pieces):
+        rows_ref[pl.ds(pl.multiple_of(spots_ref[k], 16), piece.shape[0]), :] = piece[...]
     per = rows_ref.shape[0]
     a = jnp.dot(rows_ref[...], own_ref[...], preferred_element_type=F32)
     b = jnp.dot(rows_ref[...], other_ref[...], preferred_element_type=F32)
@@ -180,23 +147,23 @@
     out_ref[1, 3:8, :] = jnp.where((row == 1) | (row == 3), NOTHING, 0.0)
 
 
-def far_logits(spots, pieces, own, other, stats_a, stats_b, taught, taught_core, ids):
+def far_logits(spots, pieces, own, other, *small):
     depth, cols = own.shape
     per = sum(piece.shape[0] for piece in pieces)
     return pl.pallas_call(
-        far_kernel,
+        lambda *refs: far_kernel(len(pieces), *refs),
         out_shape=(
             shape((per, cols), F32),
             shape((per, cols), F32),
             shape((per, depth), BF16),
             shape((2, STAT_ROWS, per), F32),
         ),
-        in_specs=[SMEM] + [VMEM] * 11,
+        in_specs=[SMEM] + [VMEM] * (len(pieces) + 2 + len(small)),
         out_specs=(VMEM, VMEM, VMEM, VMEM),
-        compiler_params=params(11),
+        compiler_params=params(12),
         cost_estimate=cost(4 * per * depth * cols, (per + 2 * cols) * depth * 2, 2 * per * cols),
         name="far_logits",
-    )(spots, *pieces, own, other, stats_a, stats_b, taught, taught_core, ids)
+    )(spots, *pieces, own, other, *small)
 
 
 def merged(parts):
@@ -241,13 +208,11 @@
     return (lax.broadcasted_iota(jnp.int32, (total, total), 1) == (row ^ flip)).astype(BF16)
 
 
-def back_kernel(bits, edges, n, at_ref, *refs):
-    stats_refs = refs[:n]
-    logits_refs = refs[n : n + 4]
-    serving_ref, aligned_ref, wown_ref, wother_ref = refs[n + 4 : n + 8]
-    gown_ref, gother_ref = refs[n + 8 : n + 10]
-    send_refs, keep_refs = refs[n + 10 : n + 13], refs[n + 13 :]
-    flip, me = at_ref[0], at_ref[3]
+def grads_kernel(n, at_ref, *refs):
+    stats_refs, logits_refs = refs[:n], refs[n : n + 4]
+    serving_ref, aligned_ref = refs[n + 4 : n + 6]
+    g_refs = refs[n + 6 :]
+    me = at_ref[3]
     per, cols = logits_refs[0].shape
     stats = [merged([ref[j] for ref in stats_refs]) for j in range(2)]
     lane = lax.broadcasted_iota(jnp.int32, (per, per), 1)
@@ -260,10 +225,12 @@
         for k in range(4):
             here = wanted - (me ^ k) * per == lane
             taught = stats[k // 2][4 + 2 * (k % 2) : 6 + 2 * (k % 2)]
-            tpeak += jnp.sum(jnp.where(here, taught[0], 0.0), axis=1, keepdims=True)
-            total += jnp.sum(jnp.where(here, taught[1], 0.0), axis=1, keepdims=True)
+            tpeak += jnp.where(here, taught[0], 0.0)
+            total += jnp.where(here, taught[1], 0.0)
+        tpeak = jnp.sum(tpeak, axis=1, keepdims=True)
+        total = jnp.sum(total, axis=1, keepdims=True)
         hard, soft, total = 16.0 / hard, 32.0 / soft, 32.0 / total
-        for c, g_ref in enumerate((gown_ref, gother_ref)):
+        for c, g_ref in enumerate(g_refs):
             part = slice(c * cols, (c + 1) * cols)
             column = at_ref[1 + c] + lax.broadcasted_iota(jnp.int32, (per, cols), 1)
             half = jnp.exp((logits_refs[2 * j + c][...] - peak) * 0.5)
@@ -271,35 +238,63 @@
             label = jnp.where(column == ids, 16.0, 0.0)
             grad = (half * soft - taught * total) + (half * half * hard - label)
             g_ref[j * per : (j + 1) * per, :] = grad.astype(BF16)
-    for p in range(3):
-        pick = picker(bits[p], flip, 2 * per)
-        part = slice(edges[p], edges[p + 1])
-        back = 0.0
-        for g_ref, w_ref in ((gown_ref, wown_ref), (gother_ref, wother_ref)):
-            rows = jnp.dot(pick, g_ref[...], preferred_element_type=F32).astype(BF16)
-            back += lax.dot_general(
-                w_ref[part, :], rows, (((1,), (1,)), ((), ())), preferred_element_type=F32
-            )
-        back = back.T
-        send_refs[p][...] = back[:per].astype(BF16)
-        keep_refs[p][...] = back[per:]
-
-
-def back_rows(at, stats, logits, serving, aligned, own, other, bits, edges):
+
+
+def push_back(bit, first, flip, g_refs, w_refs, send_ref, keep_ref):
+    per, width = send_ref.shape
+    pick = picker(bit, flip, 2 * per)
+    back = 0.0
+    for g_ref, w_ref in zip(g_refs, w_refs):
+        rows = jnp.dot(pick, g_ref[...], preferred_element_type=F32).astype(BF16)
+        back += lax.dot_general(
+            w_ref[first : first + width, :],
+            rows,
+            (((1,), (1,)), ((), ())),
+            preferred_element_type=F32,
+        )
+    back = back.T
+    send_ref[...] = back[:per].astype(BF16)
+    keep_ref[...] = back[per:]
+
+
+def back_kernel(bit, first, n, at_ref, *refs):
+    w_refs, refs = refs[:2], refs[2:]
+    g_refs, (send_ref, keep_ref) = refs[-4:-2], refs[-2:]
+    if n:
+        grads_kernel(n, at_ref, *refs[:-2])
+    push_back(bit, first, at_ref[0], g_refs, w_refs, send_ref, keep_ref)
+
+
+def back_outs(own, per, first, last):
+    return [shape((per, last - first), BF16), shape((per, last - first), F32)]
+
+
+def grads_and_back(at, own, other, stats, logits, serving, aligned, bit, first, last):
     depth, cols = own.shape
     per = logits[0].shape[0]
-    sends = [shape((per, edges[p + 1] - edges[p]), BF16) for p in range(3)]
-    keeps = [shape((per, edges[p + 1] - edges[p]), F32) for p in range(3)]
-    got = pl.pallas_call(
-        lambda *refs: back_kernel(bits, edges, len(stats), *refs),
-        out_shape=[shape((2 * per, cols), BF16)] * 2 + sends + keeps,
-        in_specs=[SMEM] + [VMEM] * (len(stats) + 8),
-        out_specs=[VMEM] * 8,
-        compiler_params=params(18),
-        cost_estimate=cost(8 * per * depth * cols, 2 * cols * depth * 2, 4 * per * cols),
-        name="back_rows",
-    )(at, *stats, *logits, serving, aligned, own, other)
-    return got[0], got[1], got[2:5], got[5:8]
+    return pl.pallas_call(
+        lambda *refs: back_kernel(bit, first, len(stats), *refs),
+        out_shape=[shape((2 * per, cols), BF16)] * 2 + back_outs(own, per, first, last),
+        in_specs=[SMEM] + [VMEM] * (2 + len(stats) + 6),
+        out_specs=[VMEM] * 4,
+        compiler_params=params(16),
+        cost_estimate=cost(8 * per * (last - first) * cols, 2 * cols * depth * 2, 4 * per * cols),
+        name="grads_and_back",
+    )(at, own, other, *stats, *logits, serving, aligned)
+
+
+def back_only(at, own, other, gown, gother, bit, first, last):
+    depth, cols = own.shape
+    per = gown.shape[0] // 2
+    return pl.pallas_call(
+        lambda *refs: back_kernel(bit, first, 0, *refs),
+        out_shape=back_outs(own, per, first, last),
+        in_specs=[SMEM] + [VMEM] * 4,
+        out_specs=[VMEM] * 2,
+        compiler_params=params(16),
+        cost_estimate=cost(8 * per * (last - first) * cols, 2 * cols * depth * 2),
+        name="back_only",
+    )(at, own, other, gown, gother)
 
 
 def head_kernel(r0, r1, r2, r3, mine_ref, theirs_ref, out_ref):
@@ -358,7 +353,10 @@
         me_v * owned, (me_g * shards + me_v) * cols, ((me_g ^ 1) * shards + me_v) * cols, me_g
     )
     who = ints(me_g, me_g & 1)
-    unsigned = [jnp.asarray(v, jnp.uint32) for v in (starts[0], starts[3], 2 * chip, 2 * (chip ^ 1))]
+    unsigned = [
+        jnp.asarray(v, jnp.uint32)
+        for v in (starts[0], starts[3], 2 * chip, 2 * (chip ^ 1))
+    ]
     rows, weight, spots, at, who, *unsigned = tie(hidden, head_weight, spots, at, who, *unsigned)
     zero = jnp.uint32(0)
 
@@ -372,29 +370,24 @@
     first = cut(rows, unsigned[0], quarter_rows, 0)
     x0 = swap(first, X)
     _, rows, teacher = tie(first, rows, teacher_logits)
-    second = cut(rows, unsigned[1], quarter_rows, 0)
+    x3 = swap(cut(rows, unsigned[1], quarter_rows, 0), X)
     kept = cut(teacher, unsigned[2], 2, 1).swapaxes(0, 1)
     gone = cut(teacher, unsigned[3], 2, 1).swapaxes(0, 1)
     taught = taught_stats(kept, gone)
-    near_a, stats_a, own_weight = own_logits(rows, head_weight)
-    x0, second, kept, gone, taught, near_a, rows = tie(
-        x0, second, kept, gone, taught, near_a, rows
-    )
+    near_a, stats_a = near_logits(rows, weight)
+    x0, kept, gone, taught, near_a, rows = tie(x0, kept, gone, taught, near_a, rows)
     x1 = swap(x0, Y)
     x2 = swap(x0, W)
-    x3 = swap(second, X)
     taught_core = swap(taught, CORE)
     kept_core = swap(kept, CORE)
-    near_b, stats_b = core_logits(rows, other_weight, x0)
-    x1, x2, x3, gone, near_b, kept_core, taught_core = tie(
-        x1, x2, x3, gone, near_b, kept_core, taught_core
-    )
-    spots, core_hidden = tie(spots, core_hidden)
+    near_b, stats_b = near_logits(rows, other_weight, x0)
+    *pieces, gone, near_b = tie(x0, x1, x2, x3, gone, near_b)
     taught_x = swap(gone, X)
+    spots, core_hidden, kept_core = tie(spots, core_hidden, kept_core)
     far_a, far_b, x_rows, stats = far_logits(
         spots,
-        [x0, x1, x2, x3],
-        own_weight,
+        pieces,
+        weight,
         other_weight,
         stats_a,
         stats_b,
@@ -404,14 +397,12 @@
     )
 
     served = serving.reshape(groups, 1, per)
+    logits = [near_a, near_b, far_a, far_b]
+    held = logits + [weight]
+    stats = merge([stats, swap(stats, X), swap(stats, Y), swap(stats, X + Y)], (0, 1, 0, 1), held)
     _, taught_x = tie(stats, taught_x)
     taught_far = swap(taught_x, CORE)
-    logits = [near_a, near_b, far_a, far_b]
-    held = logits + [own_weight]
-    stats = merge([stats, swap(stats, X), swap(stats, Y), swap(stats, X + Y)], (0, 1, 0, 1), held)
-    _, taught_far = tie(stats, taught_far)
     aligned = teacher_rows(who, served, [kept, kept_core, taught_x, taught_far])
-    core_x = swap(x_rows, CORE)
     mask = W
     while True:
         masks = [mask, 2 * mask, 3 * mask] if 2 * mask < shards else [mask]
@@ -432,12 +423,19 @@
     low = owned.bit_length() - 1
     row_bit = {0: low + bits, ydim: low, wdim: low + 1}
     first_bits = tuple(row_bit[order[0]] for order in orders)
-    gown, gother, sents, keeps = back_rows(
-        at, parts, logits, served, aligned, own_weight, other_weight, first_bits, edges
+    gown, gother, sent, keep = grads_and_back(
+        at, weight, other_weight, parts, logits, served, aligned, first_bits[0], *edges[:2]
     )
-    gots = [swap(sents[p], masks[orders[p][0]]) for p in range(3)]
+    gots, keeps = [swap(sent, masks[orders[0][0]])], [keep]
+    for p in (1, 2):
+        sent, keep = back_only(
+            at, weight, other_weight, gown, gother, first_bits[p], *edges[p : p + 2]
+        )
+        gots.append(swap(sent, masks[orders[p][0]]))
+        keeps.append(keep)
     theirs = swap(gother, CORE)
-    grad_head = head_gradient([hidden, x_rows, core_hidden, core_x], gown, theirs)
+    _, x_sent = tie(gother, x_rows)
+    grad_head = head_gradient([hidden, x_rows, core_hidden, swap(x_sent, CORE)], gown, theirs)
     grad_head, *gots = tie(grad_head, *gots)
 
     def folded(value, p):

time: 77.5 us -> 75.2 us (0.970)
  waiting for transfers between devices: 21.7 us -> 18.7 us
    ppermute x30, waiting for transfers between devices: 21.7 us -> 18.7 us  [swap(): return lax.ppermute(value, AXES, [(i, i ^ mask) for i in range(count)])]
    pallas_call x4 -> x6, Pallas kernels: 9.39 us -> 9.86 us  [the longest x2 3.41 us: back_only(): pl.pallas_call(lambda *refs: back_kernel(bit, first, 0, *refs), out_shape...]
    unnamed x8 -> x10, local copies, waits for them, and re-layouts: 2.08 us -> 2.09 us
  transfers between devices with their start and end apart: 30 -> 30, of which waited for: 19 -> 16; matrix products, arithmetic and copies ran while one was open for 5% -> 5% of each run, Pallas kernels for 21% -> 19%
where the time goes in v9:
time: 75.2 us; the launch traced here: 75 us
  starting transfers between devices  32.3 us (43%)
  waiting for transfers between devices  18.7 us (25%)
  Pallas kernels  16.8 us (22%)
  local copies, waits for them, and re-layouts  5.29 us (7%)
  other arithmetic  1.18 us (2%)
  between operations  0.84 us (1%)
    ppermute x30, starting transfers between devices, swap(): return lax.ppermute(value, AXES, [(i, i ^ mask) for i in range(count)])  32.3 us
    ppermute x30, waiting for transfers between devices, swap(): return lax.ppermute(value, AXES, [(i, i ^ mask) for i in range(count)])  18.7 us
    pallas_call x1, Pallas kernels, head_gradient(): pl.pallas_call(head_kernel, grid=(depth // tile,), out_shape=shape((depth...  5.23 us
    pallas_call x2, Pallas kernels, back_only(): pl.pallas_call(lambda *refs: back_kernel(bit, first, 0, *refs), out_shape...  3.41 us
    pallas_call x1, Pallas kernels, grads_and_back(): pl.pallas_call(lambda *refs: back_kernel(bit, first, len(stats), *refs),...  2.77 us
    unnamed x10, local copies, waits for them, and re-layouts  2.09 us
    dynamic_slice x2, local copies, waits for them, and re-layouts, cut(): return lax.dynamic_slice(value, indices, sizes)  2.01 us
    pallas_call x1, Pallas kernels, far_logits(): pl.pallas_call(lambda *refs: far_kernel(len(pieces), *refs), out_shape=(s...  1.95 us
  transfers between devices with their start and end apart: 30, of which 16 were waited for; matrix products, arithmetic and copies ran while one was open for 5% of the time, Pallas kernels for 19%

profile of v9, /device:TPU:0, one launch (start us, length us, event | category | flops | bytes accessed | tf_op | source)
XLA Modules:
  0.0 75.0 jit_solution(12383142965225393032)
XLA Ops:
  0.6 0.0 copy-start.2
  0.7 0.1 pad_add_fusion.2.at_ref
  0.7 0.1 pad_add_fusion
  0.8 0.5 collective-permute-start
  1.3 0.1 collective-permute-start.1
  1.4 1.0 %constant_dynamic-slice_fusion.1 = bf16[32,3584]{1,0:T(8,128)(2,1)S(1)} fusion(bf16[128,3584]{1,0:T(8,128)(2,1)} %r0.1, u32[]{:T(128)S(6)} %convert_element_type.149), kind=kLoop, calls=%fused_computation.42 | loop fusion | bytes 458756 | tf_op jit(solution)/shard_map/dynamic_slice | solution.py:366
  2.4 3.0 %collective-permute-start.2 = (bf16[32,3584]{1,0:T(8,128)(2,1)S(1)}, bf16[32,3584]{1,0:T(8,128)(2,1)S(1)}, u32[]{:S(2)}, u32[]{:S(2)}) collective-permute-start(bf16[32,3584]{1,0:T(8,128)(2,1)S(1)} %constant_dynamic-slice_fusion.1), channel_id=1, source_target_pairs={{0,16},{1,17},{2,18},{3,19},{4,20},{5,21},{6,22},{7,23},{8,24},{9,... | collective-permute-start | bytes 688136 | tf_op jit(solution)/shard_map/ppermute | solution.py:339
  5.4 1.0 %constant_dynamic-slice_fusion = bf16[32,3584]{1,0:T(8,128)(2,1)S(1)} fusion(bf16[128,3584]{1,0:T(8,128)(2,1)} %r0.1, u32[]{:T(128)S(6)} %convert_element_type.150), kind=kLoop, calls=%fused_computation.41 | loop fusion | bytes 458756 | tf_op jit(solution)/shard_map/dynamic_slice | solution.py:366
  6.4 0.1 collective-permute-start.6
  6.4 1.1 %copy.7 = bf16[128,4,512]{2,0,1:T(8,128)(2,1)S(1)} copy(bf16[128,4,512]{2,1,0:T(4,128)(2,1)} %param.9) | data formatting | bytes 1048576 | tf_op jit(solution)/shard_map/optimization_barrier | solution.py:342
  7.6 0.4 taught_stats.1.refs_9_
  8.0 2.1 %copy-done = bf16[3584,512]{1,0:T(8,128)(2,1)S(1)} copy-done((bf16[3584,512]{1,0:T(8,128)(2,1)S(1)}, bf16[3584,512]{1,0:T(8,128)(2,1)}, u32[]{:S(2)}) %copy-start) | copy-done | bytes 3670040
  10.1 0.9 %near_logits.2 = (f32[128,512]{1,0:T(8,128)S(1)}, f32[8,128]{1,0:T(8,128)S(1)}) custom-call(bf16[128,3584]{1,0:T(8,128)(2,1)S(1)} %copy-done.2, bf16[3584,512]{1,0:T(8,128)(2,1)S(1)} %copy-done), custom_call_target="tpu_custom_call" | custom-call | flops 469762048 | bytes 4587520 | tf_op jit(solution)/shard_map/near_logits/pallas_call | solution.py:108
  10.9 0.8 %collective-permute-done.2.refs_0_.refs_1_ = bf16[32,3584]{1,0:T(8,128)(2,1)S(1)} collective-permute-done((bf16[32,3584]{1,0:T(8,128)(2,1)S(1)}, bf16[32,3584]{1,0:T(8,128)(2,1)S(1)}, u32[]{:S(2)}, u32[]{:S(2)}) %collective-permute-start.2) | collective-permute-done | bytes 229408 | tf_op jit(solution)/shard_map/ppermute | solution.py:339
  11.8 2.1 %collective-permute-start.5 = (bf16[32,3584]{1,0:T(8,128)(2,1)S(1)}, bf16[32,3584]{1,0:T(8,128)(2,1)S(1)}, u32[]{:S(2)}, u32[]{:S(2)}) collective-permute-start(bf16[32,3584]{1,0:T(8,128)(2,1)S(1)} %collective-permute-done.2.refs_0_.refs_1_), channel_id=1, source_target_pairs={{0,2},{1,3},{2,0},{3,1},{4,6},{5,7},{6,4},{7,5},{8,10},{9,11},{10,... | collective-permute-start | bytes 688136 | tf_op jit(solution)/shard_map/ppermute | solution.py:339
  13.9 1.5 %collective-permute-start.4 = (bf16[32,3584]{1,0:T(8,128)(2,1)S(1)}, bf16[32,3584]{1,0:T(8,128)(2,1)S(1)}, u32[]{:S(2)}, u32[]{:S(2)}) collective-permute-start(bf16[32,3584]{1,0:T(8,128)(2,1)S(1)} %collective-permute-done.2.refs_0_.refs_1_), channel_id=1, source_target_pairs={{0,1},{1,0},{2,3},{3,2},{4,5},{5,4},{6,7},{7,6},{8,9},{9,8},{10,11... | collective-permute-start | bytes 688136 | tf_op jit(solution)/shard_map/ppermute | solution.py:339
  15.4 0.9 %near_logits.3 = (f32[128,512]{1,0:T(8,128)S(1)}, f32[8,128]{1,0:T(8,128)S(1)}) custom-call(bf16[128,3584]{1,0:T(8,128)(2,1)S(1)} %copy-done.2, bf16[3584,512]{1,0:T(8,128)(2,1)S(1)} %collective-permute-done.w_ref.refs_6_.refs_2_, bf16[32,3584]{1,0:T(8,128)(2,1)S(1)} %collective-permute-done.2.refs_0_.refs_1_), custom_call_target="tpu_custom_call" | custom-call | flops 469762048 | bytes 4587520 | tf_op jit(solution)/shard_map/near_logits/pallas_call | solution.py:108
  16.3 0.0 collective-permute-done.6.refs_4_
  16.3 2.1 %collective-permute-done.5.refs_3_ = bf16[32,3584]{1,0:T(8,128)(2,1)S(1)} collective-permute-done((bf16[32,3584]{1,0:T(8,128)(2,1)S(1)}, bf16[32,3584]{1,0:T(8,128)(2,1)S(1)}, u32[]{:S(2)}, u32[]{:S(2)}) %collective-permute-start.5) | collective-permute-done | bytes 229408 | tf_op jit(solution)/shard_map/ppermute | solution.py:339
  18.4 1.5 %collective-permute-done.4.refs_2_ = bf16[32,3584]{1,0:T(8,128)(2,1)S(1)} collective-permute-done((bf16[32,3584]{1,0:T(8,128)(2,1)S(1)}, bf16[32,3584]{1,0:T(8,128)(2,1)S(1)}, u32[]{:S(2)}, u32[]{:S(2)}) %collective-permute-start.4) | collective-permute-done | bytes 229408 | tf_op jit(solution)/shard_map/ppermute | solution.py:339
  19.9 1.5 %collective-permute-start.14 = (bf16[2,128,512]{2,1,0:T(8,128)(2,1)S(1)}, bf16[2,128,512]{2,1,0:T(8,128)(2,1)S(1)}, u32[]{:S(2)}, u32[]{:S(2)}) collective-permute-start(bf16[2,128,512]{2,1,0:T(8,128)(2,1)S(1)} %get-tuple-element.81.gone_ref), channel_id=1, source_target_pairs={{0,16},{1,17},{2,18},{3,19},{4,20},{5,21},{6,22},{7,23},{8,24},{9,... | collective-permute-start | bytes 786440 | tf_op jit(solution)/shard_map/ppermute | solution.py:339
  21.4 1.2 %collective-permute-done.7.refs_10_ = f32[8,128]{1,0:T(8,128)S(1)} collective-permute-done((f32[8,128]{1,0:T(8,128)S(1)}, f32[8,128]{1,0:T(8,128)S(1)}, u32[]{:S(2)}, u32[]{:S(2)}) %collective-permute-start.7) | collective-permute-done | bytes 4128 | tf_op jit(solution)/shard_map/ppermute | solution.py:339
  22.6 2.0 %far_logits.1 = (f32[128,512]{1,0:T(8,128)S(1)}, f32[128,512]{1,0:T(8,128)S(1)}, bf16[128,3584]{1,0:T(8,128)(2,1)S(1)}, f32[2,8,128]{2,1,0:T(8,128)S(1)}) custom-call(s32[4]{0:T(128)S(1)} %get-tuple-element.61.refs_0_, bf16[32,3584]{1,0:T(8,128)(2,1)S(1)} %collective-permute-done.2.refs_0_.refs_1_, bf16[32,3584]{1,0:T(8,128)(2,1)S(1)} %collective-permute-done.4.refs_2_, ...), custom_call_target="tpu_custom_call" | custom-call | flops 939524096 | bytes 8257536 | tf_op jit(solution)/shard_map/far_logits/pallas_call | solution.py:153
  24.6 0.0 copy-start.3
  24.6 1.5 %collective-permute-start.10 = (f32[2,8,128]{2,1,0:T(8,128)S(1)}, f32[2,8,128]{2,1,0:T(8,128)S(1)}, u32[]{:S(2)}, u32[]{:S(2)}) collective-permute-start(f32[2,8,128]{2,1,0:T(8,128)S(1)} %get-tuple-element.74.refs_0_), channel_id=1, source_target_pairs={{0,17},{1,16},{2,19},{3,18},{4,21},{5,20},{6,23},{7,22},{8,25},{9,... | collective-permute-start | bytes 24584 | tf_op jit(solution)/shard_map/ppermute | solution.py:339
  26.1 0.5 collective-permute-start.9
  26.6 1.5 %collective-permute-start.8 = (f32[2,8,128]{2,1,0:T(8,128)S(1)}, f32[2,8,128]{2,1,0:T(8,128)S(1)}, u32[]{:S(2)}, u32[]{:S(2)}) collective-permute-start(f32[2,8,128]{2,1,0:T(8,128)S(1)} %get-tuple-element.74.refs_0_), channel_id=1, source_target_pairs={{0,16},{1,17},{2,18},{3,19},{4,20},{5,21},{6,22},{7,23},{8,24},{9,... | collective-permute-start | bytes 24584 | tf_op jit(solution)/shard_map/ppermute | solution.py:339
  28.1 1.1 %collective-permute-done.10.refs_3_ = f32[2,8,128]{2,1,0:T(8,128)S(1)} collective-permute-done((f32[2,8,128]{2,1,0:T(8,128)S(1)}, f32[2,8,128]{2,1,0:T(8,128)S(1)}, u32[]{:S(2)}, u32[]{:S(2)}) %collective-permute-start.10) | collective-permute-done | bytes 8224 | tf_op jit(solution)/shard_map/ppermute | solution.py:339
  29.2 0.6 collective-permute-done.9.refs_2_
  29.8 0.5 collective-permute-done.8.refs_1_
  30.3 0.1 collective-permute-start.15
  30.4 2.5 %collective-permute-start.13 = (f32[2,8,128]{2,1,0:T(8,128)S(1)}, f32[2,8,128]{2,1,0:T(8,128)S(1)}, u32[]{:S(2)}, u32[]{:S(2)}) collective-permute-start(f32[2,8,128]{2,1,0:T(8,128)S(1)} %merge_stats.1.refs_3_), channel_id=1, source_target_pairs={{0,6},{1,7},{2,4},{3,5},{4,2},{5,3},{6,0},{7,1},{8,14},{9,15},{10,... | collective-permute-start | bytes 24584 | tf_op jit(solution)/shard_map/ppermute | solution.py:339
  32.9 0.2 collective-permute-start.12
  33.1 1.7 %collective-permute-start.11 = (f32[2,8,128]{2,1,0:T(8,128)S(1)}, f32[2,8,128]{2,1,0:T(8,128)S(1)}, u32[]{:S(2)}, u32[]{:S(2)}) collective-permute-start(f32[2,8,128]{2,1,0:T(8,128)S(1)} %merge_stats.1.refs_3_), channel_id=1, source_target_pairs={{0,2},{1,3},{2,0},{3,1},{4,6},{5,7},{6,4},{7,5},{8,10},{9,11},{10,... | collective-permute-start | bytes 24584 | tf_op jit(solution)/shard_map/ppermute | solution.py:339
  34.9 1.3 %teacher_rows.1.refs_12_ = bf16[2,128,1024]{2,1,0:T(8,128)(2,1)S(1)} custom-call(s32[2]{0:T(128)S(1)} %pad_add_fusion.2.at_ref, s32[4,1,128]{2,1,0:T(1,128)S(1)} %bitcast.42, bf16[2,128,512]{2,1,0:T(8,128)(2,1)S(1)} %get-tuple-element.60.kept_ref.a0, bf16[2,128,512]{2,1,0:T(8,128)(2,1)S(1)} %collective-permute-done.3.a1, ...), custom_call_target="tpu_custom_call" | custom-call | flops 268435456 | bytes 1572864 | tf_op jit(solution)/shard_map/teacher_rows/pallas_call | solution.py:80
  36.1 0.0 collective-permute-done.13.refs_6_
  36.2 1.3 %collective-permute-done.12.refs_5_ = f32[2,8,128]{2,1,0:T(8,128)S(1)} collective-permute-done((f32[2,8,128]{2,1,0:T(8,128)S(1)}, f32[2,8,128]{2,1,0:T(8,128)S(1)}, u32[]{:S(2)}, u32[]{:S(2)}) %collective-permute-start.12) | collective-permute-done | bytes 8224 | tf_op jit(solution)/shard_map/ppermute | solution.py:339
  37.5 2.8 %grads_and_back.1 = (bf16[256,512]{1,0:T(8,128)(2,1)S(1)}, bf16[256,512]{1,0:T(8,128)(2,1)S(1)}, bf16[128,1152]{1,0:T(8,128)(2,1)S(1)}, f32[128,1152]{1,0:T(8,128)S(1)}) custom-call(s32[4]{0:T(128)S(1)} %get-tuple-element.50.refs_0_, bf16[3584,512]{1,0:T(8,128)(2,1)S(1)} %copy-done.1, bf16[3584,512]{1,0:T(8,128)(2,1)S(1)} %collective-permute-done.w_ref.refs_6_.refs_2_, ...), custom_call_target="tpu_custom_call" | custom-call | flops 603979776 | bytes 7340032 | tf_op jit(solution)/shard_map/grads_and_back/pallas_call | solution.py:275
  40.3 0.1 collective-permute-start.16
  40.4 0.5 collective-permute-start.17
  40.9 1.5 %collective-permute-start.18 = (bf16[128,1152]{1,0:T(8,128)(2,1)S(1)}, bf16[128,1152]{1,0:T(8,128)(2,1)S(1)}, u32[]{:S(2)}, u32[]{:S(2)}) collective-permute-start(bf16[128,1152]{1,0:T(8,128)(2,1)S(1)} %get-tuple-element.89), channel_id=1, source_target_pairs={{0,16},{1,17},{2,18},{3,19},{4,20},{5,21},{6,22},{7,23},{8,24},{9,... | collective-permute-start | bytes 884744 | tf_op jit(solution)/shard_map/ppermute | solution.py:339
  42.3 1.7 %back_only.3 = (bf16[128,1280]{1,0:T(8,128)(2,1)S(1)}, f32[128,1280]{1,0:T(8,128)S(1)}) custom-call(s32[4]{0:T(128)S(1)} %get-tuple-element.50.refs_0_, bf16[3584,512]{1,0:T(8,128)(2,1)S(1)} %copy-done.1, bf16[3584,512]{1,0:T(8,128)(2,1)S(1)} %collective-permute-done.w_ref.refs_6_.refs_2_, bf16[256,512]{1,0:T(8,128)(2,1)S(1)} %get-tuple-element.88.mine_ref.refs_3_, ...), custom_call_target="tpu_custom_call" | custom-call | flops 671088640 | bytes 7340032 | tf_op jit(solution)/shard_map/back_only/pallas_call | solution.py:289
  44.1 1.1 %collective-permute-start.20 = (bf16[128,1280]{1,0:T(8,128)(2,1)S(1)}, bf16[128,1280]{1,0:T(8,128)(2,1)S(1)}, u32[]{:S(2)}, u32[]{:S(2)}) collective-permute-start(bf16[128,1280]{1,0:T(8,128)(2,1)S(1)} %get-tuple-element.91), channel_id=1, source_target_pairs={{0,2},{1,3},{2,0},{3,1},{4,6},{5,7},{6,4},{7,5},{8,10},{9,11},{10,... | collective-permute-start | bytes 983048 | tf_op jit(solution)/shard_map/ppermute | solution.py:339
  45.1 1.7 %back_only.2 = (bf16[128,1152]{1,0:T(8,128)(2,1)S(1)}, f32[128,1152]{1,0:T(8,128)S(1)}) custom-call(s32[4]{0:T(128)S(1)} %get-tuple-element.50.refs_0_, bf16[3584,512]{1,0:T(8,128)(2,1)S(1)} %copy-done.1, bf16[3584,512]{1,0:T(8,128)(2,1)S(1)} %collective-permute-done.w_ref.refs_6_.refs_2_, bf16[256,512]{1,0:T(8,128)(2,1)S(1)} %get-tuple-element.88.mine_ref.refs_3_, ...), custom_call_target="tpu_custom_call" | custom-call | flops 603979776 | bytes 7340032 | tf_op jit(solution)/shard_map/back_only/pallas_call | solution.py:289
  46.8 1.6 %collective-permute-start.19 = (bf16[128,1152]{1,0:T(8,128)(2,1)S(1)}, bf16[128,1152]{1,0:T(8,128)(2,1)S(1)}, u32[]{:S(2)}, u32[]{:S(2)}) collective-permute-start(bf16[128,1152]{1,0:T(8,128)(2,1)S(1)} %get-tuple-element.90), channel_id=1, source_target_pairs={{0,1},{1,0},{2,3},{3,2},{4,5},{5,4},{6,7},{7,6},{8,9},{9,8},{10,11... | collective-permute-start | bytes 884744 | tf_op jit(solution)/shard_map/ppermute | solution.py:339
  48.4 5.2 %head_gradient.1 = bf16[3584,512]{1,0:T(8,128)(2,1)} custom-call(bf16[128,3584]{1,0:T(8,128)(2,1)S(1)} %copy-done.2, bf16[128,3584]{1,0:T(8,128)(2,1)S(1)} %get-tuple-element.87.r1, bf16[128,3584]{1,0:T(8,128)(2,1)S(1)} %collective-permute-done.1.r2, bf16[128,3584]{1,0:T(8,128)(2,1)S(1)} %collective-permute-done.16.r3, ...), custom_call_target="tpu_custom_call" | custom-call | flops 1879048192 | bytes 7340032 | tf_op jit(solution)/shard_map/head_gradient/pallas_call | solution.py:314
  53.6 1.7 %collective-permute-done.19 = bf16[128,1152]{1,0:T(8,128)(2,1)S(1)} collective-permute-done((bf16[128,1152]{1,0:T(8,128)(2,1)S(1)}, bf16[128,1152]{1,0:T(8,128)(2,1)S(1)}, u32[]{:S(2)}, u32[]{:S(2)}) %collective-permute-start.19) | collective-permute-done | bytes 294944 | tf_op jit(solution)/shard_map/ppermute | solution.py:339
  55.3 1.6 %collective-permute-start.21 = (bf16[1,2,2,1,16,1152]{5,4,3,2,1,0:T(8,128)(2,1)S(1)}, bf16[1,2,2,1,16,1152]{5,4,3,2,1,0:T(8,128)(2,1)S(1)}, u32[]{:S(2)}, u32[]{:S(2)}) collective-permute-start(bf16[1,2,2,1,16,1152]{5,4,3,2,1,0:T(8,128)(2,1)S(1)} %fusion.1), channel_id=1, source_target_pairs={{0,1},{1,0},{2,3},{3,2},{4,5},{5,4},{6,7},{7,6},{8,9},{9,8},{10,11... | collective-permute-start | bytes 442376 | tf_op jit(solution)/shard_map/ppermute | solution.py:339
  57.0 1.1 %collective-permute-start.24 = (bf16[2,2,1,1,16,1152]{5,4,3,2,1,0:T(8,128)(2,1)S(1)}, bf16[2,2,1,1,16,1152]{5,4,3,2,1,0:T(8,128)(2,1)S(1)}, u32[]{:S(2)}, u32[]{:S(2)}) collective-permute-start(bf16[2,2,1,1,16,1152]{5,4,3,2,1,0:T(8,128)(2,1)S(1)} %fusion), channel_id=1, source_target_pairs={{0,2},{1,3},{2,0},{3,1},{4,6},{5,7},{6,4},{7,5},{8,10},{9,11},{10,... | collective-permute-start | bytes 442376 | tf_op jit(solution)/shard_map/ppermute | solution.py:339
  58.1 0.5 collective-permute-start.27
  58.7 1.9 %collective-permute-done.21 = bf16[1,2,2,1,16,1152]{5,4,3,2,1,0:T(8,128)(2,1)S(1)} collective-permute-done((bf16[1,2,2,1,16,1152]{5,4,3,2,1,0:T(8,128)(2,1)S(1)}, bf16[1,2,2,1,16,1152]{5,4,3,2,1,0:T(8,128)(2,1)S(1)}, u32[]{:S(2)}, u32[]{:S(2)}) %collective-permute-start.21) | collective-permute-done | bytes 147488 | tf_op jit(solution)/shard_map/ppermute | solution.py:339
  60.6 1.1 %collective-permute-start.22 = (bf16[1,2,1,1,16,1152]{5,4,3,2,1,0:T(8,128)(2,1)S(1)}, bf16[1,2,1,1,16,1152]{5,4,3,2,1,0:T(8,128)(2,1)S(1)}, u32[]{:S(2)}, u32[]{:S(2)}) collective-permute-start(bf16[1,2,1,1,16,1152]{5,4,3,2,1,0:T(8,128)(2,1)S(1)} %fusion.7), channel_id=1, source_target_pairs={{0,2},{1,3},{2,0},{3,1},{4,6},{5,7},{6,4},{7,5},{8,10},{9,11},{10,... | collective-permute-start | bytes 221192 | tf_op jit(solution)/shard_map/ppermute | solution.py:339
  61.7 1.4 %collective-permute-done.24 = bf16[2,2,1,1,16,1152]{5,4,3,2,1,0:T(8,128)(2,1)S(1)} collective-permute-done((bf16[2,2,1,1,16,1152]{5,4,3,2,1,0:T(8,128)(2,1)S(1)}, bf16[2,2,1,1,16,1152]{5,4,3,2,1,0:T(8,128)(2,1)S(1)}, u32[]{:S(2)}, u32[]{:S(2)}) %collective-permute-start.24) | collective-permute-done | bytes 147488 | tf_op jit(solution)/shard_map/ppermute | solution.py:339
  63.0 0.6 collective-permute-start.25
  63.7 0.6 collective-permute-done.27
  64.3 0.6 collective-permute-start.28
  64.8 0.2 collective-permute-done.22
  65.0 1.9 %collective-permute-start.23 = (bf16[1,1,1,1,16,1152]{5,4,3,2,1,0:T(8,128)(2,1)S(1)}, bf16[1,1,1,1,16,1152]{5,4,3,2,1,0:T(8,128)(2,1)S(1)}, u32[]{:S(2)}, u32[]{:S(2)}) collective-permute-start(bf16[1,1,1,1,16,1152]{5,4,3,2,1,0:T(8,128)(2,1)S(1)} %fusion.22), channel_id=1, source_target_pairs={{0,4},{1,5},{2,6},{3,7},{4,0},{5,1},{6,2},{7,3},{8,12},{9,13},{10,... | collective-permute-start | bytes 110600 | tf_op jit(solution)/shard_map/ppermute | solution.py:339
  67.0 0.5 collective-permute-done.25
  67.5 1.8 %collective-permute-start.26 = (bf16[1,1,1,1,16,1152]{5,4,3,2,1,0:T(8,128)(2,1)S(1)}, bf16[1,1,1,1,16,1152]{5,4,3,2,1,0:T(8,128)(2,1)S(1)}, u32[]{:S(2)}, u32[]{:S(2)}) collective-permute-start(bf16[1,1,1,1,16,1152]{5,4,3,2,1,0:T(8,128)(2,1)S(1)} %fusion.16), channel_id=1, source_target_pairs={{0,4},{1,5},{2,6},{3,7},{4,0},{5,1},{6,2},{7,3},{8,12},{9,13},{10,... | collective-permute-start | bytes 110600 | tf_op jit(solution)/shard_map/ppermute | solution.py:339
  69.3 1.6 %collective-permute-start.29 = (bf16[1,1,1,1,16,1280]{5,4,3,2,1,0:T(8,128)(2,1)S(1)}, bf16[1,1,1,1,16,1280]{5,4,3,2,1,0:T(8,128)(2,1)S(1)}, u32[]{:S(2)}, u32[]{:S(2)}) collective-permute-start(bf16[1,1,1,1,16,1280]{5,4,3,2,1,0:T(8,128)(2,1)S(1)} %fusion.10), channel_id=1, source_target_pairs={{0,4},{1,5},{2,6},{3,7},{4,0},{5,1},{6,2},{7,3},{8,12},{9,13},{10,... | collective-permute-start | bytes 122888 | tf_op jit(solution)/shard_map/ppermute | solution.py:339
  70.9 1.5 %collective-permute-done.26 = bf16[1,1,1,1,16,1152]{5,4,3,2,1,0:T(8,128)(2,1)S(1)} collective-permute-done((bf16[1,1,1,1,16,1152]{5,4,3,2,1,0:T(8,128)(2,1)S(1)}, bf16[1,1,1,1,16,1152]{5,4,3,2,1,0:T(8,128)(2,1)S(1)}, u32[]{:S(2)}, u32[]{:S(2)}) %collective-permute-start.26) | collective-permute-done | bytes 36896 | tf_op jit(solution)/shard_map/ppermute | solution.py:339
  72.4 1.8 %collective-permute-done.29 = bf16[1,1,1,1,16,1280]{5,4,3,2,1,0:T(8,128)(2,1)S(1)} collective-permute-done((bf16[1,1,1,1,16,1280]{5,4,3,2,1,0:T(8,128)(2,1)S(1)}, bf16[1,1,1,1,16,1280]{5,4,3,2,1,0:T(8,128)(2,1)S(1)}, u32[]{:S(2)}, u32[]{:S(2)}) %collective-permute-start.29) | collective-permute-done | bytes 40992 | tf_op jit(solution)/shard_map/ppermute | solution.py:339
  74.3 0.7 maximum_bitcast_fusion
  (36 shorter events, 0.5 us)
Async XLA Ops:
  0.6 7.4 %copy-start.2 = (bf16[128,3584]{1,0:T(8,128)(2,1)S(1)}, bf16[128,3584]{1,0:T(8,128)(2,1)}, u32[]{:S(2)}) copy-start(bf16[128,3584]{1,0:T(8,128)(2,1)} %r0.1) | copy-start | bytes 2752516
  0.8 14.6 %collective-permute-start = (bf16[3584,512]{1,0:T(8,128)(2,1)}, bf16[3584,512]{1,0:T(8,128)(2,1)S(1)}, u32[]{:S(2)}, u32[]{:S(2)}) collective-permute-start(bf16[3584,512]{1,0:T(8,128)(2,1)} %refs_1_.2), channel_id=1, source_target_pairs={{0,8},{1,9},{2,10},{3,11},{4,12},{5,13},{6,14},{7,15},{8,0},{9,1},... | collective-permute-start | bytes 11010056 | tf_op jit(solution)/shard_map/ppermute | solution.py:339
  1.3 20.2 %collective-permute-start.1 = (bf16[128,3584]{1,0:T(8,128)(2,1)}, bf16[128,3584]{1,0:T(8,128)(2,1)S(1)}, u32[]{:S(2)}, u32[]{:S(2)}) collective-permute-start(bf16[128,3584]{1,0:T(8,128)(2,1)} %r0.1), channel_id=1, source_target_pairs={{0,8},{1,9},{2,10},{3,11},{4,12},{5,13},{6,14},{7,15},{8,0},{9,1},... | collective-permute-start | bytes 2752520 | tf_op jit(solution)/shard_map/ppermute | solution.py:339
  2.4 9.4 %collective-permute-start.2 = (bf16[32,3584]{1,0:T(8,128)(2,1)S(1)}, bf16[32,3584]{1,0:T(8,128)(2,1)S(1)}, u32[]{:S(2)}, u32[]{:S(2)}) collective-permute-start(bf16[32,3584]{1,0:T(8,128)(2,1)S(1)} %constant_dynamic-slice_fusion.1), channel_id=1, source_target_pairs={{0,16},{1,17},{2,18},{3,19},{4,20},{5,21},{6,22},{7,23},{8,24},{9,... | collective-permute-start | bytes 688136 | tf_op jit(solution)/shard_map/ppermute | solution.py:339
  6.4 9.9 %collective-permute-start.6 = (bf16[32,3584]{1,0:T(8,128)(2,1)S(1)}, bf16[32,3584]{1,0:T(8,128)(2,1)S(1)}, u32[]{:S(2)}, u32[]{:S(2)}) collective-permute-start(bf16[32,3584]{1,0:T(8,128)(2,1)S(1)} %constant_dynamic-slice_fusion), channel_id=1, source_target_pairs={{0,16},{1,17},{2,18},{3,19},{4,20},{5,21},{6,22},{7,23},{8,24},{9,... | collective-permute-start | bytes 688136 | tf_op jit(solution)/shard_map/ppermute | solution.py:339
  8.0 2.1 %copy-start = (bf16[3584,512]{1,0:T(8,128)(2,1)S(1)}, bf16[3584,512]{1,0:T(8,128)(2,1)}, u32[]{:S(2)}) copy-start(bf16[3584,512]{1,0:T(8,128)(2,1)} %refs_1_.2) | copy-start | bytes 11010052
  10.1 12.5 %copy-start.1 = (bf16[3584,512]{1,0:T(8,128)(2,1)S(1)}, bf16[3584,512]{1,0:T(8,128)(2,1)}, u32[]{:S(2)}) copy-start(bf16[3584,512]{1,0:T(8,128)(2,1)} %refs_1_.2) | copy-start | bytes 11010052
  10.1 12.5 %copy-start.4 = (s32[128]{0:T(128)S(1)}, s32[128]{0:T(128)}, u32[]{:S(2)}) copy-start(s32[128]{0:T(128)} %param.6) | copy-start | bytes 1540
  11.8 6.6 %collective-permute-start.5 = (bf16[32,3584]{1,0:T(8,128)(2,1)S(1)}, bf16[32,3584]{1,0:T(8,128)(2,1)S(1)}, u32[]{:S(2)}, u32[]{:S(2)}) collective-permute-start(bf16[32,3584]{1,0:T(8,128)(2,1)S(1)} %collective-permute-done.2.refs_0_.refs_1_), channel_id=1, source_target_pairs={{0,2},{1,3},{2,0},{3,1},{4,6},{5,7},{6,4},{7,5},{8,10},{9,11},{10,... | collective-permute-start | bytes 688136 | tf_op jit(solution)/shard_map/ppermute | solution.py:339
  13.9 6.0 %collective-permute-start.4 = (bf16[32,3584]{1,0:T(8,128)(2,1)S(1)}, bf16[32,3584]{1,0:T(8,128)(2,1)S(1)}, u32[]{:S(2)}, u32[]{:S(2)}) collective-permute-start(bf16[32,3584]{1,0:T(8,128)(2,1)S(1)} %collective-permute-done.2.refs_0_.refs_1_), channel_id=1, source_target_pairs={{0,1},{1,0},{2,3},{3,2},{4,5},{5,4},{6,7},{7,6},{8,9},{9,8},{10,11... | collective-permute-start | bytes 688136 | tf_op jit(solution)/shard_map/ppermute | solution.py:339
  15.4 6.0 %collective-permute-start.3 = (bf16[2,128,512]{2,1,0:T(8,128)(2,1)S(1)}, bf16[2,128,512]{2,1,0:T(8,128)(2,1)S(1)}, u32[]{:S(2)}, u32[]{:S(2)}) collective-permute-start(bf16[2,128,512]{2,1,0:T(8,128)(2,1)S(1)} %get-tuple-element.60.kept_ref.a0), channel_id=1, source_target_pairs={{0,8},{1,9},{2,10},{3,11},{4,12},{5,13},{6,14},{7,15},{8,0},{9,1},... | collective-permute-start | bytes 786440 | tf_op jit(solution)/shard_map/ppermute | solution.py:339
  19.9 10.4 %collective-permute-start.14 = (bf16[2,128,512]{2,1,0:T(8,128)(2,1)S(1)}, bf16[2,128,512]{2,1,0:T(8,128)(2,1)S(1)}, u32[]{:S(2)}, u32[]{:S(2)}) collective-permute-start(bf16[2,128,512]{2,1,0:T(8,128)(2,1)S(1)} %get-tuple-element.81.gone_ref), channel_id=1, source_target_pairs={{0,16},{1,17},{2,18},{3,19},{4,20},{5,21},{6,22},{7,23},{8,24},{9,... | collective-permute-start | bytes 786440 | tf_op jit(solution)/shard_map/ppermute | solution.py:339
  21.4 1.2 %collective-permute-start.7 = (f32[8,128]{1,0:T(8,128)S(1)}, f32[8,128]{1,0:T(8,128)S(1)}, u32[]{:S(2)}, u32[]{:S(2)}) collective-permute-start(f32[8,128]{1,0:T(8,128)S(1)} %taught_stats.1.refs_9_), channel_id=1, source_target_pairs={{0,8},{1,9},{2,10},{3,11},{4,12},{5,13},{6,14},{7,15},{8,0},{9,1},... | collective-permute-start | bytes 12296 | tf_op jit(solution)/shard_map/ppermute | solution.py:339
  24.6 10.3 %copy-start.3 = (s32[512]{0:T(512)S(1)}, s32[512]{0:T(512)}, u32[]{:S(2)}) copy-start(s32[512]{0:T(512)} %param.7) | copy-start | bytes 6148
  24.6 4.6 %collective-permute-start.10 = (f32[2,8,128]{2,1,0:T(8,128)S(1)}, f32[2,8,128]{2,1,0:T(8,128)S(1)}, u32[]{:S(2)}, u32[]{:S(2)}) collective-permute-start(f32[2,8,128]{2,1,0:T(8,128)S(1)} %get-tuple-element.74.refs_0_), channel_id=1, source_target_pairs={{0,17},{1,16},{2,19},{3,18},{4,21},{5,20},{6,23},{7,22},{8,25},{9,... | collective-permute-start | bytes 24584 | tf_op jit(solution)/shard_map/ppermute | solution.py:339
  26.1 3.7 %collective-permute-start.9 = (f32[2,8,128]{2,1,0:T(8,128)S(1)}, f32[2,8,128]{2,1,0:T(8,128)S(1)}, u32[]{:S(2)}, u32[]{:S(2)}) collective-permute-start(f32[2,8,128]{2,1,0:T(8,128)S(1)} %get-tuple-element.74.refs_0_), channel_id=1, source_target_pairs={{0,1},{1,0},{2,3},{3,2},{4,5},{5,4},{6,7},{7,6},{8,9},{9,8},{10,11... | collective-permute-start | bytes 24584 | tf_op jit(solution)/shard_map/ppermute | solution.py:339
  26.6 3.7 %collective-permute-start.8 = (f32[2,8,128]{2,1,0:T(8,128)S(1)}, f32[2,8,128]{2,1,0:T(8,128)S(1)}, u32[]{:S(2)}, u32[]{:S(2)}) collective-permute-start(f32[2,8,128]{2,1,0:T(8,128)S(1)} %get-tuple-element.74.refs_0_), channel_id=1, source_target_pairs={{0,16},{1,17},{2,18},{3,19},{4,20},{5,21},{6,22},{7,23},{8,24},{9,... | collective-permute-start | bytes 24584 | tf_op jit(solution)/shard_map/ppermute | solution.py:339
  30.3 4.5 %collective-permute-start.15 = (bf16[2,128,512]{2,1,0:T(8,128)(2,1)S(1)}, bf16[2,128,512]{2,1,0:T(8,128)(2,1)S(1)}, u32[]{:S(2)}, u32[]{:S(2)}) collective-permute-start(bf16[2,128,512]{2,1,0:T(8,128)(2,1)S(1)} %collective-permute-done.14.a2), channel_id=1, source_target_pairs={{0,8},{1,9},{2,10},{3,11},{4,12},{5,13},{6,14},{7,15},{8,0},{9,1},... | collective-permute-start | bytes 786440 | tf_op jit(solution)/shard_map/ppermute | solution.py:339
  30.4 5.7 %collective-permute-start.13 = (f32[2,8,128]{2,1,0:T(8,128)S(1)}, f32[2,8,128]{2,1,0:T(8,128)S(1)}, u32[]{:S(2)}, u32[]{:S(2)}) collective-permute-start(f32[2,8,128]{2,1,0:T(8,128)S(1)} %merge_stats.1.refs_3_), channel_id=1, source_target_pairs={{0,6},{1,7},{2,4},{3,5},{4,2},{5,3},{6,0},{7,1},{8,14},{9,15},{10,... | collective-permute-start | bytes 24584 | tf_op jit(solution)/shard_map/ppermute | solution.py:339
  32.9 4.5 %collective-permute-start.12 = (f32[2,8,128]{2,1,0:T(8,128)S(1)}, f32[2,8,128]{2,1,0:T(8,128)S(1)}, u32[]{:S(2)}, u32[]{:S(2)}) collective-permute-start(f32[2,8,128]{2,1,0:T(8,128)S(1)} %merge_stats.1.refs_3_), channel_id=1, source_target_pairs={{0,4},{1,5},{2,6},{3,7},{4,0},{5,1},{6,2},{7,3},{8,12},{9,13},{10,... | collective-permute-start | bytes 24584 | tf_op jit(solution)/shard_map/ppermute | solution.py:339
  33.1 4.4 %collective-permute-start.11 = (f32[2,8,128]{2,1,0:T(8,128)S(1)}, f32[2,8,128]{2,1,0:T(8,128)S(1)}, u32[]{:S(2)}, u32[]{:S(2)}) collective-permute-start(f32[2,8,128]{2,1,0:T(8,128)S(1)} %merge_stats.1.refs_3_), channel_id=1, source_target_pairs={{0,2},{1,3},{2,0},{3,1},{4,6},{5,7},{6,4},{7,5},{8,10},{9,11},{10,... | collective-permute-start | bytes 24584 | tf_op jit(solution)/shard_map/ppermute | solution.py:339
  40.3 8.1 %collective-permute-start.16 = (bf16[128,3584]{1,0:T(8,128)(2,1)S(1)}, bf16[128,3584]{1,0:T(8,128)(2,1)S(1)}, u32[]{:S(2)}, u32[]{:S(2)}) collective-permute-start(bf16[128,3584]{1,0:T(8,128)(2,1)S(1)} %get-tuple-element.87.r1), channel_id=1, source_target_pairs={{0,8},{1,9},{2,10},{3,11},{4,12},{5,13},{6,14},{7,15},{8,0},{9,1},... | collective-permute-start | bytes 2752520 | tf_op jit(solution)/shard_map/ppermute | solution.py:339
  40.4 8.0 %collective-permute-start.17 = (bf16[256,512]{1,0:T(8,128)(2,1)S(1)}, bf16[256,512]{1,0:T(8,128)(2,1)S(1)}, u32[]{:S(2)}, u32[]{:S(2)}) collective-permute-start(bf16[256,512]{1,0:T(8,128)(2,1)S(1)} %get-tuple-element.86.refs_4_), channel_id=1, source_target_pairs={{0,8},{1,9},{2,10},{3,11},{4,12},{5,13},{6,14},{7,15},{8,0},{9,1},... | collective-permute-start | bytes 786440 | tf_op jit(solution)/shard_map/ppermute | solution.py:339
  40.9 12.8 %collective-permute-start.18 = (bf16[128,1152]{1,0:T(8,128)(2,1)S(1)}, bf16[128,1152]{1,0:T(8,128)(2,1)S(1)}, u32[]{:S(2)}, u32[]{:S(2)}) collective-permute-start(bf16[128,1152]{1,0:T(8,128)(2,1)S(1)} %get-tuple-element.89), channel_id=1, source_target_pairs={{0,16},{1,17},{2,18},{3,19},{4,20},{5,21},{6,22},{7,23},{8,24},{9,... | collective-permute-start | bytes 884744 | tf_op jit(solution)/shard_map/ppermute | solution.py:339
  44.1 11.2 %collective-permute-start.20 = (bf16[128,1280]{1,0:T(8,128)(2,1)S(1)}, bf16[128,1280]{1,0:T(8,128)(2,1)S(1)}, u32[]{:S(2)}, u32[]{:S(2)}) collective-permute-start(bf16[128,1280]{1,0:T(8,128)(2,1)S(1)} %get-tuple-element.91), channel_id=1, source_target_pairs={{0,2},{1,3},{2,0},{3,1},{4,6},{5,7},{6,4},{7,5},{8,10},{9,11},{10,... | collective-permute-start | bytes 983048 | tf_op jit(solution)/shard_map/ppermute | solution.py:339
  46.8 8.5 %collective-permute-start.19 = (bf16[128,1152]{1,0:T(8,128)(2,1)S(1)}, bf16[128,1152]{1,0:T(8,128)(2,1)S(1)}, u32[]{:S(2)}, u32[]{:S(2)}) collective-permute-start(bf16[128,1152]{1,0:T(8,128)(2,1)S(1)} %get-tuple-element.90), channel_id=1, source_target_pairs={{0,1},{1,0},{2,3},{3,2},{4,5},{5,4},{6,7},{7,6},{8,9},{9,8},{10,11... | collective-permute-start | bytes 884744 | tf_op jit(solution)/shard_map/ppermute | solution.py:339
  55.3 5.2 %collective-permute-start.21 = (bf16[1,2,2,1,16,1152]{5,4,3,2,1,0:T(8,128)(2,1)S(1)}, bf16[1,2,2,1,16,1152]{5,4,3,2,1,0:T(8,128)(2,1)S(1)}, u32[]{:S(2)}, u32[]{:S(2)}) collective-permute-start(bf16[1,2,2,1,16,1152]{5,4,3,2,1,0:T(8,128)(2,1)S(1)} %fusion.1), channel_id=1, source_target_pairs={{0,1},{1,0},{2,3},{3,2},{4,5},{5,4},{6,7},{7,6},{8,9},{9,8},{10,11... | collective-permute-start | bytes 442376 | tf_op jit(solution)/shard_map/ppermute | solution.py:339
  57.0 6.0 %collective-permute-start.24 = (bf16[2,2,1,1,16,1152]{5,4,3,2,1,0:T(8,128)(2,1)S(1)}, bf16[2,2,1,1,16,1152]{5,4,3,2,1,0:T(8,128)(2,1)S(1)}, u32[]{:S(2)}, u32[]{:S(2)}) collective-permute-start(bf16[2,2,1,1,16,1152]{5,4,3,2,1,0:T(8,128)(2,1)S(1)} %fusion), channel_id=1, source_target_pairs={{0,2},{1,3},{2,0},{3,1},{4,6},{5,7},{6,4},{7,5},{8,10},{9,11},{10,... | collective-permute-start | bytes 442376 | tf_op jit(solution)/shard_map/ppermute | solution.py:339
  58.1 6.1 %collective-permute-start.27 = (bf16[1,2,1,2,16,1280]{5,4,3,2,1,0:T(8,128)(2,1)S(1)}, bf16[1,2,1,2,16,1280]{5,4,3,2,1,0:T(8,128)(2,1)S(1)}, u32[]{:S(2)}, u32[]{:S(2)}) collective-permute-start(bf16[1,2,1,2,16,1280]{5,4,3,2,1,0:T(8,128)(2,1)S(1)} %bitcast.59), channel_id=1, source_target_pairs={{0,16},{1,17},{2,18},{3,19},{4,20},{5,21},{6,22},{7,23},{8,24},{9,... | collective-permute-start | bytes 491528 | tf_op jit(solution)/shard_map/ppermute | solution.py:339
  60.6 4.4 %collective-permute-start.22 = (bf16[1,2,1,1,16,1152]{5,4,3,2,1,0:T(8,128)(2,1)S(1)}, bf16[1,2,1,1,16,1152]{5,4,3,2,1,0:T(8,128)(2,1)S(1)}, u32[]{:S(2)}, u32[]{:S(2)}) collective-permute-start(bf16[1,2,1,1,16,1152]{5,4,3,2,1,0:T(8,128)(2,1)S(1)} %fusion.7), channel_id=1, source_target_pairs={{0,2},{1,3},{2,0},{3,1},{4,6},{5,7},{6,4},{7,5},{8,10},{9,11},{10,... | collective-permute-start | bytes 221192 | tf_op jit(solution)/shard_map/ppermute | solution.py:339
  63.0 4.4 %collective-permute-start.25 = (bf16[1,2,1,1,16,1152]{5,4,3,2,1,0:T(8,128)(2,1)S(1)}, bf16[1,2,1,1,16,1152]{5,4,3,2,1,0:T(8,128)(2,1)S(1)}, u32[]{:S(2)}, u32[]{:S(2)}) collective-permute-start(bf16[1,2,1,1,16,1152]{5,4,3,2,1,0:T(8,128)(2,1)S(1)} %fusion.5), channel_id=1, source_target_pairs={{0,16},{1,17},{2,18},{3,19},{4,20},{5,21},{6,22},{7,23},{8,24},{9,... | collective-permute-start | bytes 221192 | tf_op jit(solution)/shard_map/ppermute | solution.py:339
  64.3 5.0 %collective-permute-start.28 = (bf16[1,2,1,1,16,1280]{5,4,3,2,1,0:T(8,128)(2,1)S(1)}, bf16[1,2,1,1,16,1280]{5,4,3,2,1,0:T(8,128)(2,1)S(1)}, u32[]{:S(2)}, u32[]{:S(2)}) collective-permute-start(bf16[1,2,1,1,16,1280]{5,4,3,2,1,0:T(8,128)(2,1)S(1)} %fusion.3), channel_id=1, source_target_pairs={{0,1},{1,0},{2,3},{3,2},{4,5},{5,4},{6,7},{7,6},{8,9},{9,8},{10,11... | collective-permute-start | bytes 245768 | tf_op jit(solution)/shard_map/ppermute | solution.py:339
  65.0 5.9 %collective-permute-start.23 = (bf16[1,1,1,1,16,1152]{5,4,3,2,1,0:T(8,128)(2,1)S(1)}, bf16[1,1,1,1,16,1152]{5,4,3,2,1,0:T(8,128)(2,1)S(1)}, u32[]{:S(2)}, u32[]{:S(2)}) collective-permute-start(bf16[1,1,1,1,16,1152]{5,4,3,2,1,0:T(8,128)(2,1)S(1)} %fusion.22), channel_id=1, source_target_pairs={{0,4},{1,5},{2,6},{3,7},{4,0},{5,1},{6,2},{7,3},{8,12},{9,13},{10,... | collective-permute-start | bytes 110600 | tf_op jit(solution)/shard_map/ppermute | solution.py:339
  67.5 4.9 %collective-permute-start.26 = (bf16[1,1,1,1,16,1152]{5,4,3,2,1,0:T(8,128)(2,1)S(1)}, bf16[1,1,1,1,16,1152]{5,4,3,2,1,0:T(8,128)(2,1)S(1)}, u32[]{:S(2)}, u32[]{:S(2)}) collective-permute-start(bf16[1,1,1,1,16,1152]{5,4,3,2,1,0:T(8,128)(2,1)S(1)} %fusion.16), channel_id=1, source_target_pairs={{0,4},{1,5},{2,6},{3,7},{4,0},{5,1},{6,2},{7,3},{8,12},{9,13},{10,... | collective-permute-start | bytes 110600 | tf_op jit(solution)/shard_map/ppermute | solution.py:339
  69.3 5.0 %collective-permute-start.29 = (bf16[1,1,1,1,16,1280]{5,4,3,2,1,0:T(8,128)(2,1)S(1)}, bf16[1,1,1,1,16,1280]{5,4,3,2,1,0:T(8,128)(2,1)S(1)}, u32[]{:S(2)}, u32[]{:S(2)}) collective-permute-start(bf16[1,1,1,1,16,1280]{5,4,3,2,1,0:T(8,128)(2,1)S(1)} %fusion.10), channel_id=1, source_target_pairs={{0,4},{1,5},{2,6},{3,7},{4,0},{5,1},{6,2},{7,3},{8,12},{9,13},{10,... | collective-permute-start | bytes 122888 | tf_op jit(solution)/shard_map/ppermute | solution.py:339

commit v10 on v9

--- a/solution.py
+++ b/solution.py
@@ -181,22 +181,24 @@
     return top[0:1], hard, soft, top[3:4], top[4:5], taught0, top[6:7], taught1
 
 
-def merge_kernel(flips, *refs):
+def merge_kernel(mine_ref, got_ref, *refs):
     out_ref = refs[-1]
     for j in range(2):
-        out_ref[j] = jnp.concatenate(merged([ref[j ^ f] for ref, f in zip(refs, flips)]))
-
-
-def merge(parts, flips, held):
-    return pl.pallas_call(
-        lambda *refs: merge_kernel(flips, *refs),
-        out_shape=shape(parts[0].shape, F32),
-        in_specs=[VMEM] * (len(parts) + len(held)),
+        rows = jnp.concatenate(merged([mine_ref[j], got_ref[j ^ 1]]))
+        for copy in range(out_ref.shape[0]):
+            out_ref[copy, j] = rows
+
+
+def merge(mine, got, held, copies):
+    return pl.pallas_call(
+        merge_kernel,
+        out_shape=shape((copies,) + mine.shape, F32),
+        in_specs=[VMEM] * (2 + len(held)),
         out_specs=VMEM,
         compiler_params=params(6),
-        cost_estimate=cost(0, 5 * parts[0].size * 4),
+        cost_estimate=cost(0, (copies + 2) * mine.size * 4),
         name="merge_stats",
-    )(*parts, *held)
+    )(mine, got, *held)
 
 
 def picker(bit, flip, total):
@@ -208,13 +210,11 @@
     return (lax.broadcasted_iota(jnp.int32, (total, total), 1) == (row ^ flip)).astype(BF16)
 
 
-def grads_kernel(n, at_ref, *refs):
-    stats_refs, logits_refs = refs[:n], refs[n : n + 4]
-    serving_ref, aligned_ref = refs[n + 4 : n + 6]
-    g_refs = refs[n + 6 :]
+def grads_kernel(at_ref, stats_ref, *refs):
+    logits_refs, (serving_ref, aligned_ref), g_refs = refs[:4], refs[4:6], refs[6:]
     me = at_ref[3]
     per, cols = logits_refs[0].shape
-    stats = [merged([ref[j] for ref in stats_refs]) for j in range(2)]
+    stats = [merged([stats_ref[i, j] for i in range(stats_ref.shape[0])]) for j in range(2)]
     lane = lax.broadcasted_iota(jnp.int32, (per, per), 1)
     for j in range(2):
         rows = stats[j][:4] + (serving_ref[me ^ (2 * j)].astype(F32),)
@@ -240,61 +240,42 @@
             g_ref[j * per : (j + 1) * per, :] = grad.astype(BF16)
 
 
-def push_back(bit, first, flip, g_refs, w_refs, send_ref, keep_ref):
-    per, width = send_ref.shape
-    pick = picker(bit, flip, 2 * per)
-    back = 0.0
-    for g_ref, w_ref in zip(g_refs, w_refs):
-        rows = jnp.dot(pick, g_ref[...], preferred_element_type=F32).astype(BF16)
-        back += lax.dot_general(
-            w_ref[first : first + width, :],
-            rows,
-            (((1,), (1,)), ((), ())),
-            preferred_element_type=F32,
-        )
-    back = back.T
-    send_ref[...] = back[:per].astype(BF16)
-    keep_ref[...] = back[per:]
-
-
-def back_kernel(bit, first, n, at_ref, *refs):
-    w_refs, refs = refs[:2], refs[2:]
-    g_refs, (send_ref, keep_ref) = refs[-4:-2], refs[-2:]
-    if n:
-        grads_kernel(n, at_ref, *refs[:-2])
-    push_back(bit, first, at_ref[0], g_refs, w_refs, send_ref, keep_ref)
-
-
-def back_outs(own, per, first, last):
-    return [shape((per, last - first), BF16), shape((per, last - first), F32)]
-
-
-def grads_and_back(at, own, other, stats, logits, serving, aligned, bit, first, last):
+def back_kernel(bits, edges, at_ref, *refs):
+    w_refs, g_refs, send_refs, keep_refs = refs[:2], refs[-8:-6], refs[-6:-3], refs[-3:]
+    grads_kernel(at_ref, *refs[2:-6])
+    for p in range(3):
+        per = send_refs[p].shape[0]
+        pick = picker(bits[p], at_ref[0], 2 * per)
+        back = 0.0
+        for g_ref, w_ref in zip(g_refs, w_refs):
+            rows = jnp.dot(pick, g_ref[...], preferred_element_type=F32).astype(BF16)
+            back += lax.dot_general(
+                w_ref[edges[p] : edges[p + 1], :],
+                rows,
+                (((1,), (1,)), ((), ())),
+                preferred_element_type=F32,
+            )
+        back = back.T
+        send_refs[p][...] = back[:per].astype(BF16)
+        keep_refs[p][...] = back[per:]
+
+
+def back_rows(at, own, other, stats, logits, serving, aligned, bits, edges):
     depth, cols = own.shape
     per = logits[0].shape[0]
-    return pl.pallas_call(
-        lambda *refs: back_kernel(bit, first, len(stats), *refs),
-        out_shape=[shape((2 * per, cols), BF16)] * 2 + back_outs(own, per, first, last),
-        in_specs=[SMEM] + [VMEM] * (2 + len(stats) + 6),
-        out_specs=[VMEM] * 4,
-        compiler_params=params(16),
-        cost_estimate=cost(8 * per * (last - first) * cols, 2 * cols * depth * 2, 4 * per * cols),
-        name="grads_and_back",
-    )(at, own, other, *stats, *logits, serving, aligned)
-
-
-def back_only(at, own, other, gown, gother, bit, first, last):
-    depth, cols = own.shape
-    per = gown.shape[0] // 2
-    return pl.pallas_call(
-        lambda *refs: back_kernel(bit, first, 0, *refs),
-        out_shape=back_outs(own, per, first, last),
-        in_specs=[SMEM] + [VMEM] * 4,
-        out_specs=[VMEM] * 2,
-        compiler_params=params(16),
-        cost_estimate=cost(8 * per * (last - first) * cols, 2 * cols * depth * 2),
-        name="back_only",
-    )(at, own, other, gown, gother)
+    parts = [(per, edges[p + 1] - edges[p]) for p in range(3)]
+    got = pl.pallas_call(
+        lambda *refs: back_kernel(bits, edges, *refs),
+        out_shape=[shape((2 * per, cols), BF16)] * 2
+        + [shape(part, BF16) for part in parts]
+        + [shape(part, F32) for part in parts],
+        in_specs=[SMEM] + [VMEM] * 9,
+        out_specs=[VMEM] * 8,
+        compiler_params=params(20),
+        cost_estimate=cost(8 * per * depth * cols, 2 * cols * depth * 2, 4 * per * cols),
+        name="back_rows",
+    )(at, own, other, stats, *logits, serving, aligned)
+    return got[0], got[1], got[2:5], got[5:8]
 
 
 def head_kernel(r0, r1, r2, r3, mine_ref, theirs_ref, out_ref):
@@ -365,20 +346,22 @@
         sizes = [size if d == dim else n for d, n in enumerate(value.shape)]
         return lax.dynamic_slice(value, indices, sizes)
 
+    first = cut(rows, unsigned[0], quarter_rows, 0)
+    x0 = swap(first, X)
+    _, rows, weight, teacher = tie(first, rows, weight, teacher_logits)
     other_weight = swap(weight, CORE)
     core_hidden = swap(rows, CORE)
-    first = cut(rows, unsigned[0], quarter_rows, 0)
-    x0 = swap(first, X)
-    _, rows, teacher = tie(first, rows, teacher_logits)
     x3 = swap(cut(rows, unsigned[1], quarter_rows, 0), X)
     kept = cut(teacher, unsigned[2], 2, 1).swapaxes(0, 1)
     gone = cut(teacher, unsigned[3], 2, 1).swapaxes(0, 1)
     taught = taught_stats(kept, gone)
+    taught_core = swap(taught, CORE)
     near_a, stats_a = near_logits(rows, weight)
-    x0, kept, gone, taught, near_a, rows = tie(x0, kept, gone, taught, near_a, rows)
+    x0, kept, gone, taught, taught_core, near_a, rows = tie(
+        x0, kept, gone, taught, taught_core, near_a, rows
+    )
     x1 = swap(x0, Y)
     x2 = swap(x0, W)
-    taught_core = swap(taught, CORE)
     kept_core = swap(kept, CORE)
     near_b, stats_b = near_logits(rows, other_weight, x0)
     *pieces, gone, near_b = tie(x0, x1, x2, x3, gone, near_b)
@@ -399,18 +382,11 @@
     served = serving.reshape(groups, 1, per)
     logits = [near_a, near_b, far_a, far_b]
     held = logits + [weight]
-    stats = merge([stats, swap(stats, X), swap(stats, Y), swap(stats, X + Y)], (0, 1, 0, 1), held)
+    stats = merge(stats, swap(stats, X), held, shards)
     _, taught_x = tie(stats, taught_x)
     taught_far = swap(taught_x, CORE)
     aligned = teacher_rows(who, served, [kept, kept_core, taught_x, taught_far])
-    mask = W
-    while True:
-        masks = [mask, 2 * mask, 3 * mask] if 2 * mask < shards else [mask]
-        parts = [stats] + [swap(stats, m) for m in masks]
-        mask *= 4
-        if mask >= shards:
-            break
-        stats = merge(parts, (0,) * len(parts), held)
+    stats = lax.all_to_all(stats, "vocab", split_axis=0, concat_axis=0, tiled=True)
 
     bits = shards.bit_length() - 1
     masks = {0: X}
@@ -423,16 +399,10 @@
     low = owned.bit_length() - 1
     row_bit = {0: low + bits, ydim: low, wdim: low + 1}
     first_bits = tuple(row_bit[order[0]] for order in orders)
-    gown, gother, sent, keep = grads_and_back(
-        at, weight, other_weight, parts, logits, served, aligned, first_bits[0], *edges[:2]
-    )
-    gots, keeps = [swap(sent, masks[orders[0][0]])], [keep]
-    for p in (1, 2):
-        sent, keep = back_only(
-            at, weight, other_weight, gown, gother, first_bits[p], *edges[p : p + 2]
-        )
-        gots.append(swap(sent, masks[orders[p][0]]))
-        keeps.append(keep)
+    gown, gother, sents, keeps = back_rows(
+        at, weight, other_weight, stats, logits, served, aligned, first_bits, edges
+    )
+    gots = [swap(sents[p], masks[orders[p][0]]) for p in range(3)]
     theirs = swap(gother, CORE)
     _, x_sent = tie(gother, x_rows)
     grad_head = head_gradient([hidden, x_rows, core_hidden, swap(x_sent, CORE)], gown, theirs)

time: 75.2 us -> 79 us (1.051)
  local copies, waits for them, and re-layouts: 5.29 us -> 12 us
  starting transfers between devices: 32.3 us -> 27.9 us
  waiting for transfers between devices: 18.7 us -> 21 us
  Pallas kernels: 16.8 us -> 15.6 us
    ppermute x30 -> x25, starting transfers between devices: 32.3 us -> 23.1 us  [swap(): return lax.ppermute(value, AXES, [(i, i ^ mask) for i in range(count)])]
    unnamed x10 -> x28, local copies, waits for them, and re-layouts: 2.09 us -> 8.73 us
    all_to_all x0 -> x1, starting transfers between devices: none -> 4.81 us  [body(): lax.all_to_all(stats, 'vocab', split_axis=0, concat_axis=0, tiled=True)]
    all_to_all x0 -> x1, waiting for transfers between devices: none -> 3.97 us  [body(): lax.all_to_all(stats, 'vocab', split_axis=0, concat_axis=0, tiled=True)]
    ppermute x30 -> x25, waiting for transfers between devices: 18.7 us -> 17 us  [swap(): return lax.ppermute(value, AXES, [(i, i ^ mask) for i in range(count)])]
    pallas_call x4 -> x2, Pallas kernels: 6.21 us -> 5.04 us  [the longest x1 4.39 us: back_rows(): pl.pallas_call(lambda *refs: back_kernel(bits, edges, *refs), out_shape=[...]
  transfers between devices with their start and end apart: 30 -> 26, of which waited for: 16 -> 15; matrix products, arithmetic and copies ran while one was open for 5% -> 3% of each run, Pallas kernels for 19% -> 14%
where the time goes in v10:
time: 79 us; the launch traced here: 78.5 us
  starting transfers between devices  27.9 us (35%)
  waiting for transfers between devices  21 us (27%)
  Pallas kernels  15.6 us (20%)
  local copies, waits for them, and re-layouts  12 us (15%)
  other arithmetic  1.21 us (2%)
  between operations  0.85 us (1%)
    ppermute x25, starting transfers between devices, swap(): return lax.ppermute(value, AXES, [(i, i ^ mask) for i in range(count)])  23.1 us
    ppermute x25, waiting for transfers between devices, swap(): return lax.ppermute(value, AXES, [(i, i ^ mask) for i in range(count)])  17 us
    unnamed x28, local copies, waits for them, and re-layouts  8.73 us
    pallas_call x1, Pallas kernels, head_gradient(): pl.pallas_call(head_kernel, grid=(depth // tile,), out_shape=shape((depth...  5.23 us
    all_to_all x1, starting transfers between devices, body(): lax.all_to_all(stats, 'vocab', split_axis=0, concat_axis=0, tiled=True)  4.81 us
    pallas_call x1, Pallas kernels, back_rows(): pl.pallas_call(lambda *refs: back_kernel(bits, edges, *refs), out_shape=[...  4.39 us
    all_to_all x1, waiting for transfers between devices, body(): lax.all_to_all(stats, 'vocab', split_axis=0, concat_axis=0, tiled=True)  3.97 us
    dynamic_slice x2, local copies, waits for them, and re-layouts, cut(): return lax.dynamic_slice(value, indices, sizes)  2.1 us
  transfers between devices with their start and end apart: 26, of which 15 were waited for; matrix products, arithmetic and copies ran while one was open for 3% of the time, Pallas kernels for 14%

profile of v10, /device:TPU:0, one launch (start us, length us, event | category | flops | bytes accessed | tf_op | source)
XLA Modules:
  0.0 78.5 jit_solution(15646264836113817423)
XLA Ops:
  0.6 0.0 copy-start.5
  0.7 0.1 pad_add_fusion.2.at_ref
  0.7 0.1 pad_add_fusion
  0.8 1.1 %constant_dynamic-slice_fusion.1 = bf16[32,3584]{1,0:T(8,128)(2,1)S(1)} fusion(bf16[128,3584]{1,0:T(8,128)(2,1)} %r0.1, u32[]{:T(128)S(6)} %convert_element_type.149), kind=kLoop, calls=%fused_computation.42 | loop fusion | bytes 458756 | tf_op jit(solution)/shard_map/dynamic_slice | solution.py:347
  1.9 0.5 collective-permute-start
  2.4 2.6 %collective-permute-start.2 = (bf16[32,3584]{1,0:T(8,128)(2,1)S(1)}, bf16[32,3584]{1,0:T(8,128)(2,1)S(1)}, u32[]{:S(2)}, u32[]{:S(2)}) collective-permute-start(bf16[32,3584]{1,0:T(8,128)(2,1)S(1)} %constant_dynamic-slice_fusion.1), channel_id=1, source_target_pairs={{0,16},{1,17},{2,18},{3,19},{4,20},{5,21},{6,22},{7,23},{8,24},{9,... | collective-permute-start | bytes 688136 | tf_op jit(solution)/shard_map/ppermute | solution.py:320
  5.0 0.2 collective-permute-start.1
  5.2 1.0 %constant_dynamic-slice_fusion = bf16[32,3584]{1,0:T(8,128)(2,1)S(1)} fusion(bf16[128,3584]{1,0:T(8,128)(2,1)} %r0.1, u32[]{:T(128)S(6)} %convert_element_type.150), kind=kLoop, calls=%fused_computation.41 | loop fusion | bytes 458756 | tf_op jit(solution)/shard_map/dynamic_slice | solution.py:347
  6.2 0.3 collective-permute-start.7
  6.5 1.1 %copy.7 = bf16[128,4,512]{2,0,1:T(8,128)(2,1)S(1)} copy(bf16[128,4,512]{2,1,0:T(4,128)(2,1)} %param.9) | data formatting | bytes 1048576 | tf_op jit(solution)/shard_map/optimization_barrier | solution.py:323
  7.7 0.4 taught_stats.1.refs_9_
  8.1 0.1 collective-permute-start.3
  8.2 2.0 %copy-done = bf16[3584,512]{1,0:T(8,128)(2,1)S(1)} copy-done((bf16[3584,512]{1,0:T(8,128)(2,1)S(1)}, bf16[3584,512]{1,0:T(8,128)(2,1)}, u32[]{:S(2)}) %copy-start) | copy-done | bytes 3670040
  10.2 0.9 %near_logits.2 = (f32[128,512]{1,0:T(8,128)S(1)}, f32[8,128]{1,0:T(8,128)S(1)}) custom-call(bf16[128,3584]{1,0:T(8,128)(2,1)S(1)} %copy-done.5, bf16[3584,512]{1,0:T(8,128)(2,1)S(1)} %copy-done), custom_call_target="tpu_custom_call" | custom-call | flops 469762048 | bytes 4587520 | tf_op jit(solution)/shard_map/near_logits/pallas_call | solution.py:108
  11.1 0.4 collective-permute-done.2.refs_0_.refs_1_
  11.5 2.0 %collective-permute-start.6 = (bf16[32,3584]{1,0:T(8,128)(2,1)S(1)}, bf16[32,3584]{1,0:T(8,128)(2,1)S(1)}, u32[]{:S(2)}, u32[]{:S(2)}) collective-permute-start(bf16[32,3584]{1,0:T(8,128)(2,1)S(1)} %collective-permute-done.2.refs_0_.refs_1_), channel_id=1, source_target_pairs={{0,2},{1,3},{2,0},{3,1},{4,6},{5,7},{6,4},{7,5},{8,10},{9,11},{10,... | collective-permute-start | bytes 688136 | tf_op jit(solution)/shard_map/ppermute | solution.py:320
  13.5 1.5 %collective-permute-start.5 = (bf16[32,3584]{1,0:T(8,128)(2,1)S(1)}, bf16[32,3584]{1,0:T(8,128)(2,1)S(1)}, u32[]{:S(2)}, u32[]{:S(2)}) collective-permute-start(bf16[32,3584]{1,0:T(8,128)(2,1)S(1)} %collective-permute-done.2.refs_0_.refs_1_), channel_id=1, source_target_pairs={{0,1},{1,0},{2,3},{3,2},{4,5},{5,4},{6,7},{7,6},{8,9},{9,8},{10,11... | collective-permute-start | bytes 688136 | tf_op jit(solution)/shard_map/ppermute | solution.py:320
  15.0 0.9 %near_logits.3 = (f32[128,512]{1,0:T(8,128)S(1)}, f32[8,128]{1,0:T(8,128)S(1)}) custom-call(bf16[128,3584]{1,0:T(8,128)(2,1)S(1)} %copy-done.5, bf16[3584,512]{1,0:T(8,128)(2,1)S(1)} %collective-permute-done.w_ref.refs_6_.refs_2_, bf16[32,3584]{1,0:T(8,128)(2,1)S(1)} %collective-permute-done.2.refs_0_.refs_1_), custom_call_target="tpu_custom_call" | custom-call | flops 469762048 | bytes 4587520 | tf_op jit(solution)/shard_map/near_logits/pallas_call | solution.py:108
  15.9 0.2 collective-permute-done.7.refs_4_
  16.1 3.1 %collective-permute-done.6.refs_3_ = bf16[32,3584]{1,0:T(8,128)(2,1)S(1)} collective-permute-done((bf16[32,3584]{1,0:T(8,128)(2,1)S(1)}, bf16[32,3584]{1,0:T(8,128)(2,1)S(1)}, u32[]{:S(2)}, u32[]{:S(2)}) %collective-permute-start.6) | collective-permute-done | bytes 229408 | tf_op jit(solution)/shard_map/ppermute | solution.py:320
  19.2 1.5 %collective-permute-done.5.refs_2_ = bf16[32,3584]{1,0:T(8,128)(2,1)S(1)} collective-permute-done((bf16[32,3584]{1,0:T(8,128)(2,1)S(1)}, bf16[32,3584]{1,0:T(8,128)(2,1)S(1)}, u32[]{:S(2)}, u32[]{:S(2)}) %collective-permute-start.5) | collective-permute-done | bytes 229408 | tf_op jit(solution)/shard_map/ppermute | solution.py:320
  20.7 1.5 %collective-permute-start.9 = (bf16[2,128,512]{2,1,0:T(8,128)(2,1)S(1)}, bf16[2,128,512]{2,1,0:T(8,128)(2,1)S(1)}, u32[]{:S(2)}, u32[]{:S(2)}) collective-permute-start(bf16[2,128,512]{2,1,0:T(8,128)(2,1)S(1)} %get-tuple-element.85.gone_ref), channel_id=1, source_target_pairs={{0,16},{1,17},{2,18},{3,19},{4,20},{5,21},{6,22},{7,23},{8,24},{9,... | collective-permute-start | bytes 786440 | tf_op jit(solution)/shard_map/ppermute | solution.py:320
  22.2 0.9 %copy-done.6 = bf16[128,3584]{1,0:T(8,128)(2,1)} copy-done((bf16[128,3584]{1,0:T(8,128)(2,1)}, bf16[128,3584]{1,0:T(8,128)(2,1)S(1)}, u32[]{:S(2)}) %copy-start.6) | copy-done | bytes 917528
  23.1 2.0 %far_logits.1 = (f32[128,512]{1,0:T(8,128)S(1)}, f32[128,512]{1,0:T(8,128)S(1)}, bf16[128,3584]{1,0:T(8,128)(2,1)S(1)}, f32[2,8,128]{2,1,0:T(8,128)S(1)}) custom-call(s32[4]{0:T(128)S(1)} %get-tuple-element.64.refs_0_, bf16[32,3584]{1,0:T(8,128)(2,1)S(1)} %collective-permute-done.2.refs_0_.refs_1_, bf16[32,3584]{1,0:T(8,128)(2,1)S(1)} %collective-permute-done.5.refs_2_, ...), custom_call_target="tpu_custom_call" | custom-call | flops 939524096 | bytes 8257536 | tf_op jit(solution)/shard_map/far_logits/pallas_call | solution.py:153
  25.1 0.0 copy-start.12
  25.1 0.6 collective-permute-start.8
  25.7 3.1 %collective-permute-done.8.got_ref = f32[2,8,128]{2,1,0:T(8,128)S(1)} collective-permute-done((f32[2,8,128]{2,1,0:T(8,128)S(1)}, f32[2,8,128]{2,1,0:T(8,128)S(1)}, u32[]{:S(2)}, u32[]{:S(2)}) %collective-permute-start.8) | collective-permute-done | bytes 8224 | tf_op jit(solution)/shard_map/ppermute | solution.py:320
  28.8 0.7 merge_stats.1
  29.5 0.0 collective-permute-done.9.a2
  29.5 4.8 %all-to-all-start = ((f32[8,2,8,128]{3,2,1,0:T(8,128)}), f32[8,2,8,128]{3,2,1,0:T(8,128)S(1)}, u32[]{:S(2)}, u32[]{:S(2)}) async-start(f32[8,2,8,128]{3,2,1,0:T(8,128)} %merge_stats.1), calls=%async_computation | async-start | bytes 131072 | tf_op jit(solution)/shard_map/all_to_all | solution.py:389
  34.3 0.0 collective-permute-done.10.a3
  34.3 0.7 copy-done.10
  35.0 0.9 %copy-done.11 = bf16[2,128,512]{2,1,0:T(8,128)(2,1)S(1)} copy-done((bf16[2,128,512]{2,1,0:T(8,128)(2,1)S(1)}, bf16[2,128,512]{2,1,0:T(8,128)(2,1)}, u32[]{:S(2)}) %copy-start.11) | copy-done | bytes 262168
  36.0 1.3 %teacher_rows.1.refs_9_ = bf16[2,128,1024]{2,1,0:T(8,128)(2,1)S(1)} custom-call(s32[2]{0:T(128)S(1)} %pad_add_fusion.2.at_ref, s32[4,1,128]{2,1,0:T(1,128)S(1)} %bitcast.42, bf16[2,128,512]{2,1,0:T(8,128)(2,1)S(1)} %get-tuple-element.63.kept_ref.a0, bf16[2,128,512]{2,1,0:T(8,128)(2,1)S(1)} %collective-permute-done.4.a1, ...), custom_call_target="tpu_custom_call" | custom-call | flops 268435456 | bytes 1572864 | tf_op jit(solution)/shard_map/teacher_rows/pallas_call | solution.py:80
  37.2 4.0 %all-to-all-done.refs_3_ = f32[8,2,8,128]{3,2,1,0:T(8,128)S(1)} async-done(((f32[8,2,8,128]{3,2,1,0:T(8,128)}), f32[8,2,8,128]{3,2,1,0:T(8,128)S(1)}, u32[]{:S(2)}, u32[]{:S(2)}) %all-to-all-start) | async-done | bytes 65568 | tf_op jit(solution)/shard_map/all_to_all | solution.py:389
  41.2 2.0 %copy-done.2 = bf16[3584,512]{1,0:T(8,128)(2,1)S(1)} copy-done((bf16[3584,512]{1,0:T(8,128)(2,1)S(1)}, bf16[3584,512]{1,0:T(8,128)(2,1)}, u32[]{:S(2)}) %copy-start.2) | copy-done | bytes 3670040
  43.3 2.0 %copy-done.4 = bf16[3584,512]{1,0:T(8,128)(2,1)S(1)} copy-done((bf16[3584,512]{1,0:T(8,128)(2,1)S(1)}, bf16[3584,512]{1,0:T(8,128)(2,1)}, u32[]{:S(2)}) %copy-start.4) | copy-done | bytes 3670040
  45.3 4.4 %back_rows.1 = (bf16[256,512]{1,0:T(8,128)(2,1)S(1)}, bf16[256,512]{1,0:T(8,128)(2,1)S(1)}, bf16[128,1152]{1,0:T(8,128)(2,1)S(1)}, bf16[128,1152]{1,0:T(8,128)(2...) custom-call(s32[4]{0:T(128)S(1)} %get-tuple-element.52.refs_0_, ...), custom_call_target="tpu_custom_call" | custom-call | flops 1879048192 | bytes 7340032 | tf_op jit(solution)/shard_map/back_rows/pallas_call | solution.py:267
  49.7 0.1 collective-permute-start.11
  49.8 0.5 collective-permute-start.12
  50.3 0.2 collective-permute-start.15
  50.5 0.5 collective-permute-start.13
  51.0 1.0 %collective-permute-start.14 = (bf16[128,1152]{1,0:T(8,128)(2,1)S(1)}, bf16[128,1152]{1,0:T(8,128)(2,1)S(1)}, u32[]{:S(2)}, u32[]{:S(2)}) collective-permute-start(bf16[128,1152]{1,0:T(8,128)(2,1)S(1)} %get-tuple-element.94), channel_id=1, source_target_pairs={{0,1},{1,0},{2,3},{3,2},{4,5},{5,4},{6,7},{7,6},{8,9},{9,8},{10,11... | collective-permute-start | bytes 884744 | tf_op jit(solution)/shard_map/ppermute | solution.py:320
  52.0 0.6 collective-permute-done.12.theirs_ref
  52.6 5.2 %head_gradient.1 = bf16[3584,512]{1,0:T(8,128)(2,1)} custom-call(bf16[128,3584]{1,0:T(8,128)(2,1)S(1)} %copy-done.5, bf16[128,3584]{1,0:T(8,128)(2,1)S(1)} %copy-done.9, bf16[128,3584]{1,0:T(8,128)(2,1)S(1)} %copy-done.7, bf16[128,3584]{1,0:T(8,128)(2,1)S(1)} %collective-permute-done.11.r3, bf16[256,512]{1,0:T(8,128)(2,1)S(1)} %get-tuple-element.92.mine_ref, ...), custom_call_target="tpu_custom_call" | custom-call | flops 1879048192 | bytes 7340032 | tf_op jit(solution)/shard_map/head_gradient/pallas_call | solution.py:295
  57.8 1.4 %collective-permute-done.13 = bf16[128,1152]{1,0:T(8,128)(2,1)S(1)} collective-permute-done((bf16[128,1152]{1,0:T(8,128)(2,1)S(1)}, bf16[128,1152]{1,0:T(8,128)(2,1)S(1)}, u32[]{:S(2)}, u32[]{:S(2)}) %collective-permute-start.13) | collective-permute-done | bytes 294944 | tf_op jit(solution)/shard_map/ppermute | solution.py:320
  59.3 0.3 collective-permute-done.14
  59.5 0.4 collective-permute-done.15
  60.0 0.6 collective-permute-start.16
  60.7 1.3 %collective-permute-start.19 = (bf16[2,2,1,1,16,1152]{5,4,3,2,1,0:T(8,128)(2,1)S(1)}, bf16[2,2,1,1,16,1152]{5,4,3,2,1,0:T(8,128)(2,1)S(1)}, u32[]{:S(2)}, u32[]{:S(2)}) collective-permute-start(bf16[2,2,1,1,16,1152]{5,4,3,2,1,0:T(8,128)(2,1)S(1)} %fusion), channel_id=1, source_target_pairs={{0,2},{1,3},{2,0},{3,1},{4,6},{5,7},{6,4},{7,5},{8,10},{9,11},{10,... | collective-permute-start | bytes 442376 | tf_op jit(solution)/shard_map/ppermute | solution.py:320
  61.9 1.5 %collective-permute-start.22 = (bf16[1,2,1,2,16,1280]{5,4,3,2,1,0:T(8,128)(2,1)S(1)}, bf16[1,2,1,2,16,1280]{5,4,3,2,1,0:T(8,128)(2,1)S(1)}, u32[]{:S(2)}, u32[]{:S(2)}) collective-permute-start(bf16[1,2,1,2,16,1280]{5,4,3,2,1,0:T(8,128)(2,1)S(1)} %bitcast.59), channel_id=1, source_target_pairs={{0,16},{1,17},{2,18},{3,19},{4,20},{5,21},{6,22},{7,23},{8,24},{9,... | collective-permute-start | bytes 491528 | tf_op jit(solution)/shard_map/ppermute | solution.py:320
  63.4 1.8 %collective-permute-done.16 = bf16[1,2,2,1,16,1152]{5,4,3,2,1,0:T(8,128)(2,1)S(1)} collective-permute-done((bf16[1,2,2,1,16,1152]{5,4,3,2,1,0:T(8,128)(2,1)S(1)}, bf16[1,2,2,1,16,1152]{5,4,3,2,1,0:T(8,128)(2,1)S(1)}, u32[]{:S(2)}, u32[]{:S(2)}) %collective-permute-start.16) | collective-permute-done | bytes 147488 | tf_op jit(solution)/shard_map/ppermute | solution.py:320
  65.2 1.4 %collective-permute-start.17 = (bf16[1,2,1,1,16,1152]{5,4,3,2,1,0:T(8,128)(2,1)S(1)}, bf16[1,2,1,1,16,1152]{5,4,3,2,1,0:T(8,128)(2,1)S(1)}, u32[]{:S(2)}, u32[]{:S(2)}) collective-permute-start(bf16[1,2,1,1,16,1152]{5,4,3,2,1,0:T(8,128)(2,1)S(1)} %fusion.7), channel_id=1, source_target_pairs={{0,2},{1,3},{2,0},{3,1},{4,6},{5,7},{6,4},{7,5},{8,10},{9,11},{10,... | collective-permute-start | bytes 221192 | tf_op jit(solution)/shard_map/ppermute | solution.py:320
  66.6 1.6 %collective-permute-start.20 = (bf16[1,2,1,1,16,1152]{5,4,3,2,1,0:T(8,128)(2,1)S(1)}, bf16[1,2,1,1,16,1152]{5,4,3,2,1,0:T(8,128)(2,1)S(1)}, u32[]{:S(2)}, u32[]{:S(2)}) collective-permute-start(bf16[1,2,1,1,16,1152]{5,4,3,2,1,0:T(8,128)(2,1)S(1)} %fusion.5), channel_id=1, source_target_pairs={{0,16},{1,17},{2,18},{3,19},{4,20},{5,21},{6,22},{7,23},{8,24},{9,... | collective-permute-start | bytes 221192 | tf_op jit(solution)/shard_map/ppermute | solution.py:320
  68.3 1.4 %collective-permute-start.23 = (bf16[1,2,1,1,16,1280]{5,4,3,2,1,0:T(8,128)(2,1)S(1)}, bf16[1,2,1,1,16,1280]{5,4,3,2,1,0:T(8,128)(2,1)S(1)}, u32[]{:S(2)}, u32[]{:S(2)}) collective-permute-start(bf16[1,2,1,1,16,1280]{5,4,3,2,1,0:T(8,128)(2,1)S(1)} %fusion.3), channel_id=1, source_target_pairs={{0,1},{1,0},{2,3},{3,2},{4,5},{5,4},{6,7},{7,6},{8,9},{9,8},{10,11... | collective-permute-start | bytes 245768 | tf_op jit(solution)/shard_map/ppermute | solution.py:320
  69.7 0.7 collective-permute-start.18
  70.4 0.7 collective-permute-done.20
  71.1 1.7 %collective-permute-start.21 = (bf16[1,1,1,1,16,1152]{5,4,3,2,1,0:T(8,128)(2,1)S(1)}, bf16[1,1,1,1,16,1152]{5,4,3,2,1,0:T(8,128)(2,1)S(1)}, u32[]{:S(2)}, u32[]{:S(2)}) collective-permute-start(bf16[1,1,1,1,16,1152]{5,4,3,2,1,0:T(8,128)(2,1)S(1)} %fusion.16), channel_id=1, source_target_pairs={{0,4},{1,5},{2,6},{3,7},{4,0},{5,1},{6,2},{7,3},{8,12},{9,13},{10,... | collective-permute-start | bytes 110600 | tf_op jit(solution)/shard_map/ppermute | solution.py:320
  72.8 0.0 collective-permute-done.23
  72.8 1.4 %collective-permute-start.24 = (bf16[1,1,1,1,16,1280]{5,4,3,2,1,0:T(8,128)(2,1)S(1)}, bf16[1,1,1,1,16,1280]{5,4,3,2,1,0:T(8,128)(2,1)S(1)}, u32[]{:S(2)}, u32[]{:S(2)}) collective-permute-start(bf16[1,1,1,1,16,1280]{5,4,3,2,1,0:T(8,128)(2,1)S(1)} %fusion.10), channel_id=1, source_target_pairs={{0,4},{1,5},{2,6},{3,7},{4,0},{5,1},{6,2},{7,3},{8,12},{9,13},{10,... | collective-permute-start | bytes 122888 | tf_op jit(solution)/shard_map/ppermute | solution.py:320
  74.2 0.4 collective-permute-done.18
  74.6 1.9 %collective-permute-done.21 = bf16[1,1,1,1,16,1152]{5,4,3,2,1,0:T(8,128)(2,1)S(1)} collective-permute-done((bf16[1,1,1,1,16,1152]{5,4,3,2,1,0:T(8,128)(2,1)S(1)}, bf16[1,1,1,1,16,1152]{5,4,3,2,1,0:T(8,128)(2,1)S(1)}, u32[]{:S(2)}, u32[]{:S(2)}) %collective-permute-start.21) | collective-permute-done | bytes 36896 | tf_op jit(solution)/shard_map/ppermute | solution.py:320
  76.6 1.2 %collective-permute-done.24 = bf16[1,1,1,1,16,1280]{5,4,3,2,1,0:T(8,128)(2,1)S(1)} collective-permute-done((bf16[1,1,1,1,16,1280]{5,4,3,2,1,0:T(8,128)(2,1)S(1)}, bf16[1,1,1,1,16,1280]{5,4,3,2,1,0:T(8,128)(2,1)S(1)}, u32[]{:S(2)}, u32[]{:S(2)}) %collective-permute-start.24) | collective-permute-done | bytes 40992 | tf_op jit(solution)/shard_map/ppermute | solution.py:320
  77.8 0.7 maximum_bitcast_fusion
  (44 shorter events, 0.5 us)
Async XLA Ops:
  0.6 7.6 %copy-start.5 = (bf16[128,3584]{1,0:T(8,128)(2,1)S(1)}, bf16[128,3584]{1,0:T(8,128)(2,1)}, u32[]{:S(2)}) copy-start(bf16[128,3584]{1,0:T(8,128)(2,1)} %r0.1) | copy-start | bytes 2752516
  1.9 13.1 %collective-permute-start = (bf16[3584,512]{1,0:T(8,128)(2,1)}, bf16[3584,512]{1,0:T(8,128)(2,1)S(1)}, u32[]{:S(2)}, u32[]{:S(2)}) collective-permute-start(bf16[3584,512]{1,0:T(8,128)(2,1)} %refs_1_), channel_id=1, source_target_pairs={{0,8},{1,9},{2,10},{3,11},{4,12},{5,13},{6,14},{7,15},{8,0},{9,1},... | collective-permute-start | bytes 11010056 | tf_op jit(solution)/shard_map/ppermute | solution.py:320
  2.4 9.0 %collective-permute-start.2 = (bf16[32,3584]{1,0:T(8,128)(2,1)S(1)}, bf16[32,3584]{1,0:T(8,128)(2,1)S(1)}, u32[]{:S(2)}, u32[]{:S(2)}) collective-permute-start(bf16[32,3584]{1,0:T(8,128)(2,1)S(1)} %constant_dynamic-slice_fusion.1), channel_id=1, source_target_pairs={{0,16},{1,17},{2,18},{3,19},{4,20},{5,21},{6,22},{7,23},{8,24},{9,... | collective-permute-start | bytes 688136 | tf_op jit(solution)/shard_map/ppermute | solution.py:320
  5.0 17.2 %collective-permute-start.1 = (bf16[128,3584]{1,0:T(8,128)(2,1)}, bf16[128,3584]{1,0:T(8,128)(2,1)S(1)}, u32[]{:S(2)}, u32[]{:S(2)}) collective-permute-start(bf16[128,3584]{1,0:T(8,128)(2,1)} %r0.1), channel_id=1, source_target_pairs={{0,8},{1,9},{2,10},{3,11},{4,12},{5,13},{6,14},{7,15},{8,0},{9,1},... | collective-permute-start | bytes 2752520 | tf_op jit(solution)/shard_map/ppermute | solution.py:320
  6.2 9.9 %collective-permute-start.7 = (bf16[32,3584]{1,0:T(8,128)(2,1)S(1)}, bf16[32,3584]{1,0:T(8,128)(2,1)S(1)}, u32[]{:S(2)}, u32[]{:S(2)}) collective-permute-start(bf16[32,3584]{1,0:T(8,128)(2,1)S(1)} %constant_dynamic-slice_fusion), channel_id=1, source_target_pairs={{0,16},{1,17},{2,18},{3,19},{4,20},{5,21},{6,22},{7,23},{8,24},{9,... | collective-permute-start | bytes 688136 | tf_op jit(solution)/shard_map/ppermute | solution.py:320
  8.1 3.0 %collective-permute-start.3 = (f32[8,128]{1,0:T(8,128)S(1)}, f32[8,128]{1,0:T(8,128)S(1)}, u32[]{:S(2)}, u32[]{:S(2)}) collective-permute-start(f32[8,128]{1,0:T(8,128)S(1)} %taught_stats.1.refs_9_), channel_id=1, source_target_pairs={{0,8},{1,9},{2,10},{3,11},{4,12},{5,13},{6,14},{7,15},{8,0},{9,1},... | collective-permute-start | bytes 12296 | tf_op jit(solution)/shard_map/ppermute | solution.py:320
  8.2 2.0 %copy-start = (bf16[3584,512]{1,0:T(8,128)(2,1)S(1)}, bf16[3584,512]{1,0:T(8,128)(2,1)}, u32[]{:S(2)}) copy-start(bf16[3584,512]{1,0:T(8,128)(2,1)} %refs_1_) | copy-start | bytes 11010052
  10.2 12.9 %copy-start.1 = (bf16[3584,512]{1,0:T(8,128)(2,1)S(1)}, bf16[3584,512]{1,0:T(8,128)(2,1)}, u32[]{:S(2)}) copy-start(bf16[3584,512]{1,0:T(8,128)(2,1)} %refs_1_) | copy-start | bytes 11010052
  10.2 12.9 %copy-start.13 = (s32[128]{0:T(128)S(1)}, s32[128]{0:T(128)}, u32[]{:S(2)}) copy-start(s32[128]{0:T(128)} %param.6) | copy-start | bytes 1540
  11.5 7.7 %collective-permute-start.6 = (bf16[32,3584]{1,0:T(8,128)(2,1)S(1)}, bf16[32,3584]{1,0:T(8,128)(2,1)S(1)}, u32[]{:S(2)}, u32[]{:S(2)}) collective-permute-start(bf16[32,3584]{1,0:T(8,128)(2,1)S(1)} %collective-permute-done.2.refs_0_.refs_1_), channel_id=1, source_target_pairs={{0,2},{1,3},{2,0},{3,1},{4,6},{5,7},{6,4},{7,5},{8,10},{9,11},{10,... | collective-permute-start | bytes 688136 | tf_op jit(solution)/shard_map/ppermute | solution.py:320
  13.5 7.2 %collective-permute-start.5 = (bf16[32,3584]{1,0:T(8,128)(2,1)S(1)}, bf16[32,3584]{1,0:T(8,128)(2,1)S(1)}, u32[]{:S(2)}, u32[]{:S(2)}) collective-permute-start(bf16[32,3584]{1,0:T(8,128)(2,1)S(1)} %collective-permute-done.2.refs_0_.refs_1_), channel_id=1, source_target_pairs={{0,1},{1,0},{2,3},{3,2},{4,5},{5,4},{6,7},{7,6},{8,9},{9,8},{10,11... | collective-permute-start | bytes 688136 | tf_op jit(solution)/shard_map/ppermute | solution.py:320
  15.0 10.1 %copy-start.3 = (bf16[3584,512]{1,0:T(8,128)(2,1)}, bf16[3584,512]{1,0:T(8,128)(2,1)S(1)}, u32[]{:S(2)}) copy-start(bf16[3584,512]{1,0:T(8,128)(2,1)S(1)} %collective-permute-done.w_ref.refs_6_.refs_2_) | copy-start | bytes 11010052
  15.0 7.2 %collective-permute-start.4 = (bf16[2,128,512]{2,1,0:T(8,128)(2,1)S(1)}, bf16[2,128,512]{2,1,0:T(8,128)(2,1)S(1)}, u32[]{:S(2)}, u32[]{:S(2)}) collective-permute-start(bf16[2,128,512]{2,1,0:T(8,128)(2,1)S(1)} %get-tuple-element.63.kept_ref.a0), channel_id=1, source_target_pairs={{0,8},{1,9},{2,10},{3,11},{4,12},{5,13},{6,14},{7,15},{8,0},{9,1},... | collective-permute-start | bytes 786440 | tf_op jit(solution)/shard_map/ppermute | solution.py:320
  20.7 8.8 %collective-permute-start.9 = (bf16[2,128,512]{2,1,0:T(8,128)(2,1)S(1)}, bf16[2,128,512]{2,1,0:T(8,128)(2,1)S(1)}, u32[]{:S(2)}, u32[]{:S(2)}) collective-permute-start(bf16[2,128,512]{2,1,0:T(8,128)(2,1)S(1)} %get-tuple-element.85.gone_ref), channel_id=1, source_target_pairs={{0,16},{1,17},{2,18},{3,19},{4,20},{5,21},{6,22},{7,23},{8,24},{9,... | collective-permute-start | bytes 786440 | tf_op jit(solution)/shard_map/ppermute | solution.py:320
  22.2 0.9 %copy-start.6 = (bf16[128,3584]{1,0:T(8,128)(2,1)}, bf16[128,3584]{1,0:T(8,128)(2,1)S(1)}, u32[]{:S(2)}) copy-start(bf16[128,3584]{1,0:T(8,128)(2,1)S(1)} %collective-permute-done.1.r2) | copy-start | bytes 2752516
  25.1 4.4 %copy-start.8 = (bf16[128,3584]{1,0:T(8,128)(2,1)}, bf16[128,3584]{1,0:T(8,128)(2,1)S(1)}, u32[]{:S(2)}) copy-start(bf16[128,3584]{1,0:T(8,128)(2,1)S(1)} %get-tuple-element.91.r1) | copy-start | bytes 2752516
  25.1 9.9 %copy-start.12 = (s32[512]{0:T(512)S(1)}, s32[512]{0:T(512)}, u32[]{:S(2)}) copy-start(s32[512]{0:T(512)} %param.7) | copy-start | bytes 6148
  25.1 3.7 %collective-permute-start.8 = (f32[2,8,128]{2,1,0:T(8,128)S(1)}, f32[2,8,128]{2,1,0:T(8,128)S(1)}, u32[]{:S(2)}, u32[]{:S(2)}) collective-permute-start(f32[2,8,128]{2,1,0:T(8,128)S(1)} %get-tuple-element.78.mine_ref), channel_id=1, source_target_pairs={{0,16},{1,17},{2,18},{3,19},{4,20},{5,21},{6,22},{7,23},{8,24},{9,... | collective-permute-start | bytes 24584 | tf_op jit(solution)/shard_map/ppermute | solution.py:320
  29.5 4.8 %collective-permute-start.10 = (bf16[2,128,512]{2,1,0:T(8,128)(2,1)S(1)}, bf16[2,128,512]{2,1,0:T(8,128)(2,1)S(1)}, u32[]{:S(2)}, u32[]{:S(2)}) collective-permute-start(bf16[2,128,512]{2,1,0:T(8,128)(2,1)S(1)} %collective-permute-done.9.a2), channel_id=1, source_target_pairs={{0,8},{1,9},{2,10},{3,11},{4,12},{5,13},{6,14},{7,15},{8,0},{9,1},... | collective-permute-start | bytes 786440 | tf_op jit(solution)/shard_map/ppermute | solution.py:320
  29.5 11.7 %all-to-all-start = ((f32[8,2,8,128]{3,2,1,0:T(8,128)}), f32[8,2,8,128]{3,2,1,0:T(8,128)S(1)}, u32[]{:S(2)}, u32[]{:S(2)}) async-start(f32[8,2,8,128]{3,2,1,0:T(8,128)} %merge_stats.1), calls=%async_computation | async-start | bytes 131072 | tf_op jit(solution)/shard_map/all_to_all | solution.py:389
  34.3 0.7 copy-start.10
  35.0 1.0 %copy-start.11 = (bf16[2,128,512]{2,1,0:T(8,128)(2,1)S(1)}, bf16[2,128,512]{2,1,0:T(8,128)(2,1)}, u32[]{:S(2)}) copy-start(bf16[2,128,512]{2,1,0:T(8,128)(2,1)} %copy-done.10) | copy-start | bytes 786436
  41.2 2.0 %copy-start.2 = (bf16[3584,512]{1,0:T(8,128)(2,1)S(1)}, bf16[3584,512]{1,0:T(8,128)(2,1)}, u32[]{:S(2)}) copy-start(bf16[3584,512]{1,0:T(8,128)(2,1)} %refs_1_) | copy-start | bytes 11010052
  43.3 2.0 %copy-start.4 = (bf16[3584,512]{1,0:T(8,128)(2,1)S(1)}, bf16[3584,512]{1,0:T(8,128)(2,1)}, u32[]{:S(2)}) copy-start(bf16[3584,512]{1,0:T(8,128)(2,1)} %copy-done.3) | copy-start | bytes 11010052
  45.3 4.4 %copy-start.9 = (bf16[128,3584]{1,0:T(8,128)(2,1)S(1)}, bf16[128,3584]{1,0:T(8,128)(2,1)}, u32[]{:S(2)}) copy-start(bf16[128,3584]{1,0:T(8,128)(2,1)} %copy-done.8) | copy-start | bytes 2752516
  45.3 7.3 %copy-start.7 = (bf16[128,3584]{1,0:T(8,128)(2,1)S(1)}, bf16[128,3584]{1,0:T(8,128)(2,1)}, u32[]{:S(2)}) copy-start(bf16[128,3584]{1,0:T(8,128)(2,1)} %copy-done.6) | copy-start | bytes 2752516
  49.7 2.9 %collective-permute-start.11 = (bf16[128,3584]{1,0:T(8,128)(2,1)S(1)}, bf16[128,3584]{1,0:T(8,128)(2,1)S(1)}, u32[]{:S(2)}, u32[]{:S(2)}) collective-permute-start(bf16[128,3584]{1,0:T(8,128)(2,1)S(1)} %copy-done.9), channel_id=1, source_target_pairs={{0,8},{1,9},{2,10},{3,11},{4,12},{5,13},{6,14},{7,15},{8,0},{9,1},... | collective-permute-start | bytes 2752520 | tf_op jit(solution)/shard_map/ppermute | solution.py:320
  49.8 2.8 %collective-permute-start.12 = (bf16[256,512]{1,0:T(8,128)(2,1)S(1)}, bf16[256,512]{1,0:T(8,128)(2,1)S(1)}, u32[]{:S(2)}, u32[]{:S(2)}) collective-permute-start(bf16[256,512]{1,0:T(8,128)(2,1)S(1)} %get-tuple-element.90), channel_id=1, source_target_pairs={{0,8},{1,9},{2,10},{3,11},{4,12},{5,13},{6,14},{7,15},{8,0},{9,1},... | collective-permute-start | bytes 786440 | tf_op jit(solution)/shard_map/ppermute | solution.py:320
  50.3 9.7 %collective-permute-start.15 = (bf16[128,1280]{1,0:T(8,128)(2,1)S(1)}, bf16[128,1280]{1,0:T(8,128)(2,1)S(1)}, u32[]{:S(2)}, u32[]{:S(2)}) collective-permute-start(bf16[128,1280]{1,0:T(8,128)(2,1)S(1)} %get-tuple-element.95), channel_id=1, source_target_pairs={{0,2},{1,3},{2,0},{3,1},{4,6},{5,7},{6,4},{7,5},{8,10},{9,11},{10,... | collective-permute-start | bytes 983048 | tf_op jit(solution)/shard_map/ppermute | solution.py:320
  50.5 8.8 %collective-permute-start.13 = (bf16[128,1152]{1,0:T(8,128)(2,1)S(1)}, bf16[128,1152]{1,0:T(8,128)(2,1)S(1)}, u32[]{:S(2)}, u32[]{:S(2)}) collective-permute-start(bf16[128,1152]{1,0:T(8,128)(2,1)S(1)} %get-tuple-element.93), channel_id=1, source_target_pairs={{0,16},{1,17},{2,18},{3,19},{4,20},{5,21},{6,22},{7,23},{8,24},{9,... | collective-permute-start | bytes 884744 | tf_op jit(solution)/shard_map/ppermute | solution.py:320
  51.0 8.5 %collective-permute-start.14 = (bf16[128,1152]{1,0:T(8,128)(2,1)S(1)}, bf16[128,1152]{1,0:T(8,128)(2,1)S(1)}, u32[]{:S(2)}, u32[]{:S(2)}) collective-permute-start(bf16[128,1152]{1,0:T(8,128)(2,1)S(1)} %get-tuple-element.94), channel_id=1, source_target_pairs={{0,1},{1,0},{2,3},{3,2},{4,5},{5,4},{6,7},{7,6},{8,9},{9,8},{10,11... | collective-permute-start | bytes 884744 | tf_op jit(solution)/shard_map/ppermute | solution.py:320
  60.0 5.2 %collective-permute-start.16 = (bf16[1,2,2,1,16,1152]{5,4,3,2,1,0:T(8,128)(2,1)S(1)}, bf16[1,2,2,1,16,1152]{5,4,3,2,1,0:T(8,128)(2,1)S(1)}, u32[]{:S(2)}, u32[]{:S(2)}) collective-permute-start(bf16[1,2,2,1,16,1152]{5,4,3,2,1,0:T(8,128)(2,1)S(1)} %fusion.1), channel_id=1, source_target_pairs={{0,1},{1,0},{2,3},{3,2},{4,5},{5,4},{6,7},{7,6},{8,9},{9,8},{10,11... | collective-permute-start | bytes 442376 | tf_op jit(solution)/shard_map/ppermute | solution.py:320
  60.7 6.0 %collective-permute-start.19 = (bf16[2,2,1,1,16,1152]{5,4,3,2,1,0:T(8,128)(2,1)S(1)}, bf16[2,2,1,1,16,1152]{5,4,3,2,1,0:T(8,128)(2,1)S(1)}, u32[]{:S(2)}, u32[]{:S(2)}) collective-permute-start(bf16[2,2,1,1,16,1152]{5,4,3,2,1,0:T(8,128)(2,1)S(1)} %fusion), channel_id=1, source_target_pairs={{0,2},{1,3},{2,0},{3,1},{4,6},{5,7},{6,4},{7,5},{8,10},{9,11},{10,... | collective-permute-start | bytes 442376 | tf_op jit(solution)/shard_map/ppermute | solution.py:320
  61.9 6.3 %collective-permute-start.22 = (bf16[1,2,1,2,16,1280]{5,4,3,2,1,0:T(8,128)(2,1)S(1)}, bf16[1,2,1,2,16,1280]{5,4,3,2,1,0:T(8,128)(2,1)S(1)}, u32[]{:S(2)}, u32[]{:S(2)}) collective-permute-start(bf16[1,2,1,2,16,1280]{5,4,3,2,1,0:T(8,128)(2,1)S(1)} %bitcast.59), channel_id=1, source_target_pairs={{0,16},{1,17},{2,18},{3,19},{4,20},{5,21},{6,22},{7,23},{8,24},{9,... | collective-permute-start | bytes 491528 | tf_op jit(solution)/shard_map/ppermute | solution.py:320
  65.2 4.4 %collective-permute-start.17 = (bf16[1,2,1,1,16,1152]{5,4,3,2,1,0:T(8,128)(2,1)S(1)}, bf16[1,2,1,1,16,1152]{5,4,3,2,1,0:T(8,128)(2,1)S(1)}, u32[]{:S(2)}, u32[]{:S(2)}) collective-permute-start(bf16[1,2,1,1,16,1152]{5,4,3,2,1,0:T(8,128)(2,1)S(1)} %fusion.7), channel_id=1, source_target_pairs={{0,2},{1,3},{2,0},{3,1},{4,6},{5,7},{6,4},{7,5},{8,10},{9,11},{10,... | collective-permute-start | bytes 221192 | tf_op jit(solution)/shard_map/ppermute | solution.py:320
  66.6 4.4 %collective-permute-start.20 = (bf16[1,2,1,1,16,1152]{5,4,3,2,1,0:T(8,128)(2,1)S(1)}, bf16[1,2,1,1,16,1152]{5,4,3,2,1,0:T(8,128)(2,1)S(1)}, u32[]{:S(2)}, u32[]{:S(2)}) collective-permute-start(bf16[1,2,1,1,16,1152]{5,4,3,2,1,0:T(8,128)(2,1)S(1)} %fusion.5), channel_id=1, source_target_pairs={{0,16},{1,17},{2,18},{3,19},{4,20},{5,21},{6,22},{7,23},{8,24},{9,... | collective-permute-start | bytes 221192 | tf_op jit(solution)/shard_map/ppermute | solution.py:320
  68.3 4.5 %collective-permute-start.23 = (bf16[1,2,1,1,16,1280]{5,4,3,2,1,0:T(8,128)(2,1)S(1)}, bf16[1,2,1,1,16,1280]{5,4,3,2,1,0:T(8,128)(2,1)S(1)}, u32[]{:S(2)}, u32[]{:S(2)}) collective-permute-start(bf16[1,2,1,1,16,1280]{5,4,3,2,1,0:T(8,128)(2,1)S(1)} %fusion.3), channel_id=1, source_target_pairs={{0,1},{1,0},{2,3},{3,2},{4,5},{5,4},{6,7},{7,6},{8,9},{9,8},{10,11... | collective-permute-start | bytes 245768 | tf_op jit(solution)/shard_map/ppermute | solution.py:320
  69.7 4.9 %collective-permute-start.18 = (bf16[1,1,1,1,16,1152]{5,4,3,2,1,0:T(8,128)(2,1)S(1)}, bf16[1,1,1,1,16,1152]{5,4,3,2,1,0:T(8,128)(2,1)S(1)}, u32[]{:S(2)}, u32[]{:S(2)}) collective-permute-start(bf16[1,1,1,1,16,1152]{5,4,3,2,1,0:T(8,128)(2,1)S(1)} %fusion.22), channel_id=1, source_target_pairs={{0,4},{1,5},{2,6},{3,7},{4,0},{5,1},{6,2},{7,3},{8,12},{9,13},{10,... | collective-permute-start | bytes 110600 | tf_op jit(solution)/shard_map/ppermute | solution.py:320
  71.1 5.4 %collective-permute-start.21 = (bf16[1,1,1,1,16,1152]{5,4,3,2,1,0:T(8,128)(2,1)S(1)}, bf16[1,1,1,1,16,1152]{5,4,3,2,1,0:T(8,128)(2,1)S(1)}, u32[]{:S(2)}, u32[]{:S(2)}) collective-permute-start(bf16[1,1,1,1,16,1152]{5,4,3,2,1,0:T(8,128)(2,1)S(1)} %fusion.16), channel_id=1, source_target_pairs={{0,4},{1,5},{2,6},{3,7},{4,0},{5,1},{6,2},{7,3},{8,12},{9,13},{10,... | collective-permute-start | bytes 110600 | tf_op jit(solution)/shard_map/ppermute | solution.py:320
  72.8 5.0 %collective-permute-start.24 = (bf16[1,1,1,1,16,1280]{5,4,3,2,1,0:T(8,128)(2,1)S(1)}, bf16[1,1,1,1,16,1280]{5,4,3,2,1,0:T(8,128)(2,1)S(1)}, u32[]{:S(2)}, u32[]{:S(2)}) collective-permute-start(bf16[1,1,1,1,16,1280]{5,4,3,2,1,0:T(8,128)(2,1)S(1)} %fusion.10), channel_id=1, source_target_pairs={{0,4},{1,5},{2,6},{3,7},{4,0},{5,1},{6,2},{7,3},{8,12},{9,13},{10,... | collective-permute-start | bytes 122888 | tf_op jit(solution)/shard_map/ppermute | solution.py:320

commit v11 on v10

--- a/solution.py
+++ b/solution.py
@@ -181,24 +181,22 @@
     return top[0:1], hard, soft, top[3:4], top[4:5], taught0, top[6:7], taught1
 
 
-def merge_kernel(mine_ref, got_ref, *refs):
+def merge_kernel(flips, *refs):
     out_ref = refs[-1]
     for j in range(2):
-        rows = jnp.concatenate(merged([mine_ref[j], got_ref[j ^ 1]]))
-        for copy in range(out_ref.shape[0]):
-            out_ref[copy, j] = rows
-
-
-def merge(mine, got, held, copies):
-    return pl.pallas_call(
-        merge_kernel,
-        out_shape=shape((copies,) + mine.shape, F32),
-        in_specs=[VMEM] * (2 + len(held)),
+        out_ref[j] = jnp.concatenate(merged([ref[j ^ f] for ref, f in zip(refs, flips)]))
+
+
+def merge(parts, flips, held):
+    return pl.pallas_call(
+        lambda *refs: merge_kernel(flips, *refs),
+        out_shape=shape(parts[0].shape, F32),
+        in_specs=[VMEM] * (len(parts) + len(held)),
         out_specs=VMEM,
         compiler_params=params(6),
-        cost_estimate=cost(0, (copies + 2) * mine.size * 4),
+        cost_estimate=cost(0, 5 * parts[0].size * 4),
         name="merge_stats",
-    )(mine, got, *held)
+    )(*parts, *held)
 
 
 def picker(bit, flip, total):
@@ -210,11 +208,12 @@
     return (lax.broadcasted_iota(jnp.int32, (total, total), 1) == (row ^ flip)).astype(BF16)
 
 
-def grads_kernel(at_ref, stats_ref, *refs):
+def grads_kernel(n, at_ref, *refs):
+    stats_refs, refs = refs[:n], refs[n:]
     logits_refs, (serving_ref, aligned_ref), g_refs = refs[:4], refs[4:6], refs[6:]
     me = at_ref[3]
     per, cols = logits_refs[0].shape
-    stats = [merged([stats_ref[i, j] for i in range(stats_ref.shape[0])]) for j in range(2)]
+    stats = [merged([ref[j] for ref in stats_refs]) for j in range(2)]
     lane = lax.broadcasted_iota(jnp.int32, (per, per), 1)
     for j in range(2):
         rows = stats[j][:4] + (serving_ref[me ^ (2 * j)].astype(F32),)
@@ -240,9 +239,9 @@
             g_ref[j * per : (j + 1) * per, :] = grad.astype(BF16)
 
 
-def back_kernel(bits, edges, at_ref, *refs):
+def back_kernel(bits, edges, n, at_ref, *refs):
     w_refs, g_refs, send_refs, keep_refs = refs[:2], refs[-8:-6], refs[-6:-3], refs[-3:]
-    grads_kernel(at_ref, *refs[2:-6])
+    grads_kernel(n, at_ref, *refs[2:-6])
     for p in range(3):
         per = send_refs[p].shape[0]
         pick = picker(bits[p], at_ref[0], 2 * per)
@@ -265,16 +264,16 @@
     per = logits[0].shape[0]
     parts = [(per, edges[p + 1] - edges[p]) for p in range(3)]
     got = pl.pallas_call(
-        lambda *refs: back_kernel(bits, edges, *refs),
+        lambda *refs: back_kernel(bits, edges, len(stats), *refs),
         out_shape=[shape((2 * per, cols), BF16)] * 2
         + [shape(part, BF16) for part in parts]
         + [shape(part, F32) for part in parts],
-        in_specs=[SMEM] + [VMEM] * 9,
+        in_specs=[SMEM] + [VMEM] * (len(stats) + 8),
         out_specs=[VMEM] * 8,
         compiler_params=params(20),
         cost_estimate=cost(8 * per * depth * cols, 2 * cols * depth * 2, 4 * per * cols),
         name="back_rows",
-    )(at, own, other, stats, *logits, serving, aligned)
+    )(at, own, other, *stats, *logits, serving, aligned)
     return got[0], got[1], got[2:5], got[5:8]
 
 
@@ -382,11 +381,18 @@
     served = serving.reshape(groups, 1, per)
     logits = [near_a, near_b, far_a, far_b]
     held = logits + [weight]
-    stats = merge(stats, swap(stats, X), held, shards)
+    stats = merge([stats, swap(stats, X), swap(stats, Y), swap(stats, X + Y)], (0, 1, 0, 1), held)
     _, taught_x = tie(stats, taught_x)
     taught_far = swap(taught_x, CORE)
     aligned = teacher_rows(who, served, [kept, kept_core, taught_x, taught_far])
-    stats = lax.all_to_all(stats, "vocab", split_axis=0, concat_axis=0, tiled=True)
+    mask = W
+    while True:
+        masks = [mask, 2 * mask, 3 * mask] if 2 * mask < shards else [mask]
+        parts = [stats] + [swap(stats, m) for m in masks]
+        mask *= 4
+        if mask >= shards:
+            break
+        stats = merge(parts, (0,) * len(parts), held)
 
     bits = shards.bit_length() - 1
     masks = {0: X}
@@ -400,7 +406,7 @@
     row_bit = {0: low + bits, ydim: low, wdim: low + 1}
     first_bits = tuple(row_bit[order[0]] for order in orders)
     gown, gother, sents, keeps = back_rows(
-        at, weight, other_weight, stats, logits, served, aligned, first_bits, edges
+        at, weight, other_weight, parts, logits, served, aligned, first_bits, edges
     )
     gots = [swap(sents[p], masks[orders[p][0]]) for p in range(3)]
     theirs = swap(gother, CORE)

time: 79 us -> 72.9 us (0.923)
  local copies, waits for them, and re-layouts: 12 us -> 5.35 us
  starting transfers between devices: 27.9 us -> 32.1 us
  waiting for transfers between devices: 21 us -> 18.2 us
    ppermute x25 -> x30, starting transfers between devices: 23.1 us -> 32.1 us  [swap(): return lax.ppermute(value, AXES, [(i, i ^ mask) for i in range(count)])]
    unnamed x28 -> x10, local copies, waits for them, and re-layouts: 8.73 us -> 2.06 us
    all_to_all x1 -> x0, starting transfers between devices: 4.81 us -> none  [body(): lax.all_to_all(stats, 'vocab', split_axis=0, concat_axis=0, tiled=True)]
    all_to_all x1 -> x0, waiting for transfers between devices: 3.97 us -> none  [body(): lax.all_to_all(stats, 'vocab', split_axis=0, concat_axis=0, tiled=True)]
    ppermute x25 -> x30, waiting for transfers between devices: 17 us -> 18.2 us  [swap(): return lax.ppermute(value, AXES, [(i, i ^ mask) for i in range(count)])]
  transfers between devices with their start and end apart: 26 -> 30, of which waited for: 15 -> 17; matrix products, arithmetic and copies ran while one was open for 3% -> 3% of each run, Pallas kernels for 14% -> 15%
where the time goes in v11:
time: 72.9 us; the launch traced here: 72.7 us
  starting transfers between devices  32.1 us (44%)
  waiting for transfers between devices  18.2 us (25%)
  Pallas kernels  15 us (21%)
  local copies, waits for them, and re-layouts  5.35 us (7%)
  other arithmetic  1.2 us (2%)
  between operations  0.84 us (1%)
    ppermute x30, starting transfers between devices, swap(): return lax.ppermute(value, AXES, [(i, i ^ mask) for i in range(count)])  32.1 us
    ppermute x30, waiting for transfers between devices, swap(): return lax.ppermute(value, AXES, [(i, i ^ mask) for i in range(count)])  18.2 us
    pallas_call x1, Pallas kernels, head_gradient(): pl.pallas_call(head_kernel, grid=(depth // tile,), out_shape=shape((depth...  5.23 us
    pallas_call x1, Pallas kernels, back_rows(): pl.pallas_call(lambda *refs: back_kernel(bits, edges, len(stats), *refs),...  4.39 us
    dynamic_slice x2, local copies, waits for them, and re-layouts, cut(): return lax.dynamic_slice(value, indices, sizes)  2.1 us
    unnamed x10, local copies, waits for them, and re-layouts  2.06 us
    pallas_call x1, Pallas kernels, far_logits(): pl.pallas_call(lambda *refs: far_kernel(len(pieces), *refs), out_shape=(s...  1.96 us
    pallas_call x2, Pallas kernels, near_logits(): pl.pallas_call(near_kernel, out_shape=(shape((per, cols), F32), shape((ST...  1.72 us
  transfers between devices with their start and end apart: 30, of which 17 were waited for; matrix products, arithmetic and copies ran while one was open for 3% of the time, Pallas kernels for 15%

profile of v11, /device:TPU:0, one launch (start us, length us, event | category | flops | bytes accessed | tf_op | source)
XLA Modules:
  0.0 72.7 jit_solution(14268106260273108024)
XLA Ops:
  0.6 0.0 copy-start.2
  0.7 0.1 pad_add_fusion.2.at_ref
  0.7 0.1 pad_add_fusion
  0.8 1.1 %constant_dynamic-slice_fusion.1 = bf16[32,3584]{1,0:T(8,128)(2,1)S(1)} fusion(bf16[128,3584]{1,0:T(8,128)(2,1)} %r0.1, u32[]{:T(128)S(6)} %convert_element_type.149), kind=kLoop, calls=%fused_computation.42 | loop fusion | bytes 458756 | tf_op jit(solution)/shard_map/dynamic_slice | solution.py:346
  1.9 0.5 collective-permute-start
  2.4 2.6 %collective-permute-start.2 = (bf16[32,3584]{1,0:T(8,128)(2,1)S(1)}, bf16[32,3584]{1,0:T(8,128)(2,1)S(1)}, u32[]{:S(2)}, u32[]{:S(2)}) collective-permute-start(bf16[32,3584]{1,0:T(8,128)(2,1)S(1)} %constant_dynamic-slice_fusion.1), channel_id=1, source_target_pairs={{0,16},{1,17},{2,18},{3,19},{4,20},{5,21},{6,22},{7,23},{8,24},{9,... | collective-permute-start | bytes 688136 | tf_op jit(solution)/shard_map/ppermute | solution.py:319
  5.0 0.2 collective-permute-start.1
  5.2 1.0 %constant_dynamic-slice_fusion = bf16[32,3584]{1,0:T(8,128)(2,1)S(1)} fusion(bf16[128,3584]{1,0:T(8,128)(2,1)} %r0.1, u32[]{:T(128)S(6)} %convert_element_type.150), kind=kLoop, calls=%fused_computation.41 | loop fusion | bytes 458756 | tf_op jit(solution)/shard_map/dynamic_slice | solution.py:346
  6.2 0.3 collective-permute-start.7
  6.5 1.1 %copy.7 = bf16[128,4,512]{2,0,1:T(8,128)(2,1)S(1)} copy(bf16[128,4,512]{2,1,0:T(4,128)(2,1)} %param.9) | data formatting | bytes 1048576 | tf_op jit(solution)/shard_map/optimization_barrier | solution.py:322
  7.7 0.4 taught_stats.1.refs_9_
  8.1 0.1 collective-permute-start.3
  8.2 2.0 %copy-done = bf16[3584,512]{1,0:T(8,128)(2,1)S(1)} copy-done((bf16[3584,512]{1,0:T(8,128)(2,1)S(1)}, bf16[3584,512]{1,0:T(8,128)(2,1)}, u32[]{:S(2)}) %copy-start) | copy-done | bytes 3670040
  10.2 0.9 %near_logits.2 = (f32[128,512]{1,0:T(8,128)S(1)}, f32[8,128]{1,0:T(8,128)S(1)}) custom-call(bf16[128,3584]{1,0:T(8,128)(2,1)S(1)} %copy-done.2, bf16[3584,512]{1,0:T(8,128)(2,1)S(1)} %copy-done), custom_call_target="tpu_custom_call" | custom-call | flops 469762048 | bytes 4587520 | tf_op jit(solution)/shard_map/near_logits/pallas_call | solution.py:108
  11.1 0.4 collective-permute-done.2.refs_0_.refs_1_
  11.5 2.0 %collective-permute-start.6 = (bf16[32,3584]{1,0:T(8,128)(2,1)S(1)}, bf16[32,3584]{1,0:T(8,128)(2,1)S(1)}, u32[]{:S(2)}, u32[]{:S(2)}) collective-permute-start(bf16[32,3584]{1,0:T(8,128)(2,1)S(1)} %collective-permute-done.2.refs_0_.refs_1_), channel_id=1, source_target_pairs={{0,2},{1,3},{2,0},{3,1},{4,6},{5,7},{6,4},{7,5},{8,10},{9,11},{10,... | collective-permute-start | bytes 688136 | tf_op jit(solution)/shard_map/ppermute | solution.py:319
  13.5 1.5 %collective-permute-start.5 = (bf16[32,3584]{1,0:T(8,128)(2,1)S(1)}, bf16[32,3584]{1,0:T(8,128)(2,1)S(1)}, u32[]{:S(2)}, u32[]{:S(2)}) collective-permute-start(bf16[32,3584]{1,0:T(8,128)(2,1)S(1)} %collective-permute-done.2.refs_0_.refs_1_), channel_id=1, source_target_pairs={{0,1},{1,0},{2,3},{3,2},{4,5},{5,4},{6,7},{7,6},{8,9},{9,8},{10,11... | collective-permute-start | bytes 688136 | tf_op jit(solution)/shard_map/ppermute | solution.py:319
  15.0 0.0 collective-permute-start.4
  15.0 0.9 %near_logits.3 = (f32[128,512]{1,0:T(8,128)S(1)}, f32[8,128]{1,0:T(8,128)S(1)}) custom-call(bf16[128,3584]{1,0:T(8,128)(2,1)S(1)} %copy-done.2, bf16[3584,512]{1,0:T(8,128)(2,1)S(1)} %collective-permute-done.w_ref.refs_6_.refs_2_, bf16[32,3584]{1,0:T(8,128)(2,1)S(1)} %collective-permute-done.2.refs_0_.refs_1_), custom_call_target="tpu_custom_call" | custom-call | flops 469762048 | bytes 4587520 | tf_op jit(solution)/shard_map/near_logits/pallas_call | solution.py:108
  15.9 0.3 collective-permute-done.7.refs_4_
  16.1 3.1 %collective-permute-done.6.refs_3_ = bf16[32,3584]{1,0:T(8,128)(2,1)S(1)} collective-permute-done((bf16[32,3584]{1,0:T(8,128)(2,1)S(1)}, bf16[32,3584]{1,0:T(8,128)(2,1)S(1)}, u32[]{:S(2)}, u32[]{:S(2)}) %collective-permute-start.6) | collective-permute-done | bytes 229408 | tf_op jit(solution)/shard_map/ppermute | solution.py:319
  19.2 1.5 %collective-permute-done.5.refs_2_ = bf16[32,3584]{1,0:T(8,128)(2,1)S(1)} collective-permute-done((bf16[32,3584]{1,0:T(8,128)(2,1)S(1)}, bf16[32,3584]{1,0:T(8,128)(2,1)S(1)}, u32[]{:S(2)}, u32[]{:S(2)}) %collective-permute-start.5) | collective-permute-done | bytes 229408 | tf_op jit(solution)/shard_map/ppermute | solution.py:319
  20.7 1.5 %collective-permute-start.14 = (bf16[2,128,512]{2,1,0:T(8,128)(2,1)S(1)}, bf16[2,128,512]{2,1,0:T(8,128)(2,1)S(1)}, u32[]{:S(2)}, u32[]{:S(2)}) collective-permute-start(bf16[2,128,512]{2,1,0:T(8,128)(2,1)S(1)} %get-tuple-element.85.gone_ref), channel_id=1, source_target_pairs={{0,16},{1,17},{2,18},{3,19},{4,20},{5,21},{6,22},{7,23},{8,24},{9,... | collective-permute-start | bytes 786440 | tf_op jit(solution)/shard_map/ppermute | solution.py:319
  22.2 0.0 collective-permute-done.4.a1
  22.2 2.0 %far_logits.1 = (f32[128,512]{1,0:T(8,128)S(1)}, f32[128,512]{1,0:T(8,128)S(1)}, bf16[128,3584]{1,0:T(8,128)(2,1)S(1)}, f32[2,8,128]{2,1,0:T(8,128)S(1)}) custom-call(s32[4]{0:T(128)S(1)} %get-tuple-element.64.refs_0_, bf16[32,3584]{1,0:T(8,128)(2,1)S(1)} %collective-permute-done.2.refs_0_.refs_1_, bf16[32,3584]{1,0:T(8,128)(2,1)S(1)} %collective-permute-done.5.refs_2_, ...), custom_call_target="tpu_custom_call" | custom-call | flops 939524096 | bytes 8257536 | tf_op jit(solution)/shard_map/far_logits/pallas_call | solution.py:153
  24.2 0.0 copy-start.3
  24.2 1.5 %collective-permute-start.10 = (f32[2,8,128]{2,1,0:T(8,128)S(1)}, f32[2,8,128]{2,1,0:T(8,128)S(1)}, u32[]{:S(2)}, u32[]{:S(2)}) collective-permute-start(f32[2,8,128]{2,1,0:T(8,128)S(1)} %get-tuple-element.78.refs_0_), channel_id=1, source_target_pairs={{0,17},{1,16},{2,19},{3,18},{4,21},{5,20},{6,23},{7,22},{8,25},{9,... | collective-permute-start | bytes 24584 | tf_op jit(solution)/shard_map/ppermute | solution.py:319
  25.7 0.5 collective-permute-start.9
  26.2 1.5 %collective-permute-start.8 = (f32[2,8,128]{2,1,0:T(8,128)S(1)}, f32[2,8,128]{2,1,0:T(8,128)S(1)}, u32[]{:S(2)}, u32[]{:S(2)}) collective-permute-start(f32[2,8,128]{2,1,0:T(8,128)S(1)} %get-tuple-element.78.refs_0_), channel_id=1, source_target_pairs={{0,16},{1,17},{2,18},{3,19},{4,20},{5,21},{6,22},{7,23},{8,24},{9,... | collective-permute-start | bytes 24584 | tf_op jit(solution)/shard_map/ppermute | solution.py:319
  27.7 1.1 %collective-permute-done.10.refs_3_ = f32[2,8,128]{2,1,0:T(8,128)S(1)} collective-permute-done((f32[2,8,128]{2,1,0:T(8,128)S(1)}, f32[2,8,128]{2,1,0:T(8,128)S(1)}, u32[]{:S(2)}, u32[]{:S(2)}) %collective-permute-start.10) | collective-permute-done | bytes 8224 | tf_op jit(solution)/shard_map/ppermute | solution.py:319
  28.8 0.5 collective-permute-done.9.refs_2_
  29.4 0.5 collective-permute-done.8.refs_1_
  29.9 0.1 collective-permute-start.15
  30.0 2.5 %collective-permute-start.13 = (f32[2,8,128]{2,1,0:T(8,128)S(1)}, f32[2,8,128]{2,1,0:T(8,128)S(1)}, u32[]{:S(2)}, u32[]{:S(2)}) collective-permute-start(f32[2,8,128]{2,1,0:T(8,128)S(1)} %merge_stats.1.refs_3_), channel_id=1, source_target_pairs={{0,6},{1,7},{2,4},{3,5},{4,2},{5,3},{6,0},{7,1},{8,14},{9,15},{10,... | collective-permute-start | bytes 24584 | tf_op jit(solution)/shard_map/ppermute | solution.py:319
  32.5 0.2 collective-permute-start.12
  32.7 1.7 %collective-permute-start.11 = (f32[2,8,128]{2,1,0:T(8,128)S(1)}, f32[2,8,128]{2,1,0:T(8,128)S(1)}, u32[]{:S(2)}, u32[]{:S(2)}) collective-permute-start(f32[2,8,128]{2,1,0:T(8,128)S(1)} %merge_stats.1.refs_3_), channel_id=1, source_target_pairs={{0,2},{1,3},{2,0},{3,1},{4,6},{5,7},{6,4},{7,5},{8,10},{9,11},{10,... | collective-permute-start | bytes 24584 | tf_op jit(solution)/shard_map/ppermute | solution.py:319
  34.5 1.3 %teacher_rows.1.refs_12_ = bf16[2,128,1024]{2,1,0:T(8,128)(2,1)S(1)} custom-call(s32[2]{0:T(128)S(1)} %pad_add_fusion.2.at_ref, s32[4,1,128]{2,1,0:T(1,128)S(1)} %bitcast.42, bf16[2,128,512]{2,1,0:T(8,128)(2,1)S(1)} %get-tuple-element.63.kept_ref.a0, bf16[2,128,512]{2,1,0:T(8,128)(2,1)S(1)} %collective-permute-done.4.a1, ...), custom_call_target="tpu_custom_call" | custom-call | flops 268435456 | bytes 1572864 | tf_op jit(solution)/shard_map/teacher_rows/pallas_call | solution.py:80
  35.8 1.3 %collective-permute-done.12.refs_5_ = f32[2,8,128]{2,1,0:T(8,128)S(1)} collective-permute-done((f32[2,8,128]{2,1,0:T(8,128)S(1)}, f32[2,8,128]{2,1,0:T(8,128)S(1)}, u32[]{:S(2)}, u32[]{:S(2)}) %collective-permute-start.12) | collective-permute-done | bytes 8224 | tf_op jit(solution)/shard_map/ppermute | solution.py:319
  37.1 4.4 %back_rows.1 = (bf16[256,512]{1,0:T(8,128)(2,1)S(1)}, bf16[256,512]{1,0:T(8,128)(2,1)S(1)}, bf16[128,1152]{1,0:T(8,128)(2,1)S(1)}, bf16[128,1152]{1,0:T(8,128)(2...) custom-call(s32[4]{0:T(128)S(1)} %get-tuple-element.52.refs_0_, ...), custom_call_target="tpu_custom_call" | custom-call | flops 1879048192 | bytes 7340032 | tf_op jit(solution)/shard_map/back_rows/pallas_call | solution.py:266
  41.5 0.1 collective-permute-start.16
  41.5 0.5 collective-permute-start.17
  42.0 1.0 %collective-permute-start.20 = (bf16[128,1280]{1,0:T(8,128)(2,1)S(1)}, bf16[128,1280]{1,0:T(8,128)(2,1)S(1)}, u32[]{:S(2)}, u32[]{:S(2)}) collective-permute-start(bf16[128,1280]{1,0:T(8,128)(2,1)S(1)} %get-tuple-element.95), channel_id=1, source_target_pairs={{0,2},{1,3},{2,0},{3,1},{4,6},{5,7},{6,4},{7,5},{8,10},{9,11},{10,... | collective-permute-start | bytes 983048 | tf_op jit(solution)/shard_map/ppermute | solution.py:319
  43.1 1.5 %collective-permute-start.18 = (bf16[128,1152]{1,0:T(8,128)(2,1)S(1)}, bf16[128,1152]{1,0:T(8,128)(2,1)S(1)}, u32[]{:S(2)}, u32[]{:S(2)}) collective-permute-start(bf16[128,1152]{1,0:T(8,128)(2,1)S(1)} %get-tuple-element.93), channel_id=1, source_target_pairs={{0,16},{1,17},{2,18},{3,19},{4,20},{5,21},{6,22},{7,23},{8,24},{9,... | collective-permute-start | bytes 884744 | tf_op jit(solution)/shard_map/ppermute | solution.py:319
  44.6 1.5 %collective-permute-start.19 = (bf16[128,1152]{1,0:T(8,128)(2,1)S(1)}, bf16[128,1152]{1,0:T(8,128)(2,1)S(1)}, u32[]{:S(2)}, u32[]{:S(2)}) collective-permute-start(bf16[128,1152]{1,0:T(8,128)(2,1)S(1)} %get-tuple-element.94), channel_id=1, source_target_pairs={{0,1},{1,0},{2,3},{3,2},{4,5},{5,4},{6,7},{7,6},{8,9},{9,8},{10,11... | collective-permute-start | bytes 884744 | tf_op jit(solution)/shard_map/ppermute | solution.py:319
  46.1 5.2 %head_gradient.1 = bf16[3584,512]{1,0:T(8,128)(2,1)} custom-call(bf16[128,3584]{1,0:T(8,128)(2,1)S(1)} %copy-done.2, bf16[128,3584]{1,0:T(8,128)(2,1)S(1)} %get-tuple-element.91.r1, bf16[128,3584]{1,0:T(8,128)(2,1)S(1)} %collective-permute-done.1.r2, bf16[128,3584]{1,0:T(8,128)(2,1)S(1)} %collective-permute-done.16.r3, ...), custom_call_target="tpu_custom_call" | custom-call | flops 1879048192 | bytes 7340032 | tf_op jit(solution)/shard_map/head_gradient/pallas_call | solution.py:294
  51.3 0.5 collective-permute-done.18
  51.8 1.2 %collective-permute-done.19 = bf16[128,1152]{1,0:T(8,128)(2,1)S(1)} collective-permute-done((bf16[128,1152]{1,0:T(8,128)(2,1)S(1)}, bf16[128,1152]{1,0:T(8,128)(2,1)S(1)}, u32[]{:S(2)}, u32[]{:S(2)}) %collective-permute-start.19) | collective-permute-done | bytes 294944 | tf_op jit(solution)/shard_map/ppermute | solution.py:319
  53.0 1.6 %collective-permute-start.21 = (bf16[1,2,2,1,16,1152]{5,4,3,2,1,0:T(8,128)(2,1)S(1)}, bf16[1,2,2,1,16,1152]{5,4,3,2,1,0:T(8,128)(2,1)S(1)}, u32[]{:S(2)}, u32[]{:S(2)}) collective-permute-start(bf16[1,2,2,1,16,1152]{5,4,3,2,1,0:T(8,128)(2,1)S(1)} %fusion.1), channel_id=1, source_target_pairs={{0,1},{1,0},{2,3},{3,2},{4,5},{5,4},{6,7},{7,6},{8,9},{9,8},{10,11... | collective-permute-start | bytes 442376 | tf_op jit(solution)/shard_map/ppermute | solution.py:319
  54.7 1.1 %collective-permute-start.24 = (bf16[2,2,1,1,16,1152]{5,4,3,2,1,0:T(8,128)(2,1)S(1)}, bf16[2,2,1,1,16,1152]{5,4,3,2,1,0:T(8,128)(2,1)S(1)}, u32[]{:S(2)}, u32[]{:S(2)}) collective-permute-start(bf16[2,2,1,1,16,1152]{5,4,3,2,1,0:T(8,128)(2,1)S(1)} %fusion), channel_id=1, source_target_pairs={{0,2},{1,3},{2,0},{3,1},{4,6},{5,7},{6,4},{7,5},{8,10},{9,11},{10,... | collective-permute-start | bytes 442376 | tf_op jit(solution)/shard_map/ppermute | solution.py:319
  55.8 0.5 collective-permute-start.27
  56.3 1.9 %collective-permute-done.21 = bf16[1,2,2,1,16,1152]{5,4,3,2,1,0:T(8,128)(2,1)S(1)} collective-permute-done((bf16[1,2,2,1,16,1152]{5,4,3,2,1,0:T(8,128)(2,1)S(1)}, bf16[1,2,2,1,16,1152]{5,4,3,2,1,0:T(8,128)(2,1)S(1)}, u32[]{:S(2)}, u32[]{:S(2)}) %collective-permute-start.21) | collective-permute-done | bytes 147488 | tf_op jit(solution)/shard_map/ppermute | solution.py:319
  58.3 1.1 %collective-permute-start.22 = (bf16[1,2,1,1,16,1152]{5,4,3,2,1,0:T(8,128)(2,1)S(1)}, bf16[1,2,1,1,16,1152]{5,4,3,2,1,0:T(8,128)(2,1)S(1)}, u32[]{:S(2)}, u32[]{:S(2)}) collective-permute-start(bf16[1,2,1,1,16,1152]{5,4,3,2,1,0:T(8,128)(2,1)S(1)} %fusion.7), channel_id=1, source_target_pairs={{0,2},{1,3},{2,0},{3,1},{4,6},{5,7},{6,4},{7,5},{8,10},{9,11},{10,... | collective-permute-start | bytes 221192 | tf_op jit(solution)/shard_map/ppermute | solution.py:319
  59.3 1.4 %collective-permute-done.24 = bf16[2,2,1,1,16,1152]{5,4,3,2,1,0:T(8,128)(2,1)S(1)} collective-permute-done((bf16[2,2,1,1,16,1152]{5,4,3,2,1,0:T(8,128)(2,1)S(1)}, bf16[2,2,1,1,16,1152]{5,4,3,2,1,0:T(8,128)(2,1)S(1)}, u32[]{:S(2)}, u32[]{:S(2)}) %collective-permute-start.24) | collective-permute-done | bytes 147488 | tf_op jit(solution)/shard_map/ppermute | solution.py:319
  60.7 0.6 collective-permute-start.25
  61.3 0.6 collective-permute-done.27
  62.0 0.6 collective-permute-start.28
  62.5 0.2 collective-permute-done.22
  62.7 1.9 %collective-permute-start.23 = (bf16[1,1,1,1,16,1152]{5,4,3,2,1,0:T(8,128)(2,1)S(1)}, bf16[1,1,1,1,16,1152]{5,4,3,2,1,0:T(8,128)(2,1)S(1)}, u32[]{:S(2)}, u32[]{:S(2)}) collective-permute-start(bf16[1,1,1,1,16,1152]{5,4,3,2,1,0:T(8,128)(2,1)S(1)} %fusion.22), channel_id=1, source_target_pairs={{0,4},{1,5},{2,6},{3,7},{4,0},{5,1},{6,2},{7,3},{8,12},{9,13},{10,... | collective-permute-start | bytes 110600 | tf_op jit(solution)/shard_map/ppermute | solution.py:319
  64.6 0.5 collective-permute-done.25
  65.2 1.8 %collective-permute-start.26 = (bf16[1,1,1,1,16,1152]{5,4,3,2,1,0:T(8,128)(2,1)S(1)}, bf16[1,1,1,1,16,1152]{5,4,3,2,1,0:T(8,128)(2,1)S(1)}, u32[]{:S(2)}, u32[]{:S(2)}) collective-permute-start(bf16[1,1,1,1,16,1152]{5,4,3,2,1,0:T(8,128)(2,1)S(1)} %fusion.16), channel_id=1, source_target_pairs={{0,4},{1,5},{2,6},{3,7},{4,0},{5,1},{6,2},{7,3},{8,12},{9,13},{10,... | collective-permute-start | bytes 110600 | tf_op jit(solution)/shard_map/ppermute | solution.py:319
  67.0 1.6 %collective-permute-start.29 = (bf16[1,1,1,1,16,1280]{5,4,3,2,1,0:T(8,128)(2,1)S(1)}, bf16[1,1,1,1,16,1280]{5,4,3,2,1,0:T(8,128)(2,1)S(1)}, u32[]{:S(2)}, u32[]{:S(2)}) collective-permute-start(bf16[1,1,1,1,16,1280]{5,4,3,2,1,0:T(8,128)(2,1)S(1)} %fusion.10), channel_id=1, source_target_pairs={{0,4},{1,5},{2,6},{3,7},{4,0},{5,1},{6,2},{7,3},{8,12},{9,13},{10,... | collective-permute-start | bytes 122888 | tf_op jit(solution)/shard_map/ppermute | solution.py:319
  68.6 1.5 %collective-permute-done.26 = bf16[1,1,1,1,16,1152]{5,4,3,2,1,0:T(8,128)(2,1)S(1)} collective-permute-done((bf16[1,1,1,1,16,1152]{5,4,3,2,1,0:T(8,128)(2,1)S(1)}, bf16[1,1,1,1,16,1152]{5,4,3,2,1,0:T(8,128)(2,1)S(1)}, u32[]{:S(2)}, u32[]{:S(2)}) %collective-permute-start.26) | collective-permute-done | bytes 36896 | tf_op jit(solution)/shard_map/ppermute | solution.py:319
  70.1 1.8 %collective-permute-done.29 = bf16[1,1,1,1,16,1280]{5,4,3,2,1,0:T(8,128)(2,1)S(1)} collective-permute-done((bf16[1,1,1,1,16,1280]{5,4,3,2,1,0:T(8,128)(2,1)S(1)}, bf16[1,1,1,1,16,1280]{5,4,3,2,1,0:T(8,128)(2,1)S(1)}, u32[]{:S(2)}, u32[]{:S(2)}) %collective-permute-start.29) | collective-permute-done | bytes 40992 | tf_op jit(solution)/shard_map/ppermute | solution.py:319
  72.0 0.7 maximum_bitcast_fusion
  (34 shorter events, 0.5 us)
Async XLA Ops:
  0.6 7.6 %copy-start.2 = (bf16[128,3584]{1,0:T(8,128)(2,1)S(1)}, bf16[128,3584]{1,0:T(8,128)(2,1)}, u32[]{:S(2)}) copy-start(bf16[128,3584]{1,0:T(8,128)(2,1)} %r0.1) | copy-start | bytes 2752516
  1.9 13.1 %collective-permute-start = (bf16[3584,512]{1,0:T(8,128)(2,1)}, bf16[3584,512]{1,0:T(8,128)(2,1)S(1)}, u32[]{:S(2)}, u32[]{:S(2)}) collective-permute-start(bf16[3584,512]{1,0:T(8,128)(2,1)} %refs_1_), channel_id=1, source_target_pairs={{0,8},{1,9},{2,10},{3,11},{4,12},{5,13},{6,14},{7,15},{8,0},{9,1},... | collective-permute-start | bytes 11010056 | tf_op jit(solution)/shard_map/ppermute | solution.py:319
  2.4 9.0 %collective-permute-start.2 = (bf16[32,3584]{1,0:T(8,128)(2,1)S(1)}, bf16[32,3584]{1,0:T(8,128)(2,1)S(1)}, u32[]{:S(2)}, u32[]{:S(2)}) collective-permute-start(bf16[32,3584]{1,0:T(8,128)(2,1)S(1)} %constant_dynamic-slice_fusion.1), channel_id=1, source_target_pairs={{0,16},{1,17},{2,18},{3,19},{4,20},{5,21},{6,22},{7,23},{8,24},{9,... | collective-permute-start | bytes 688136 | tf_op jit(solution)/shard_map/ppermute | solution.py:319
  5.0 17.2 %collective-permute-start.1 = (bf16[128,3584]{1,0:T(8,128)(2,1)}, bf16[128,3584]{1,0:T(8,128)(2,1)S(1)}, u32[]{:S(2)}, u32[]{:S(2)}) collective-permute-start(bf16[128,3584]{1,0:T(8,128)(2,1)} %r0.1), channel_id=1, source_target_pairs={{0,8},{1,9},{2,10},{3,11},{4,12},{5,13},{6,14},{7,15},{8,0},{9,1},... | collective-permute-start | bytes 2752520 | tf_op jit(solution)/shard_map/ppermute | solution.py:319
  6.2 9.9 %collective-permute-start.7 = (bf16[32,3584]{1,0:T(8,128)(2,1)S(1)}, bf16[32,3584]{1,0:T(8,128)(2,1)S(1)}, u32[]{:S(2)}, u32[]{:S(2)}) collective-permute-start(bf16[32,3584]{1,0:T(8,128)(2,1)S(1)} %constant_dynamic-slice_fusion), channel_id=1, source_target_pairs={{0,16},{1,17},{2,18},{3,19},{4,20},{5,21},{6,22},{7,23},{8,24},{9,... | collective-permute-start | bytes 688136 | tf_op jit(solution)/shard_map/ppermute | solution.py:319
  8.1 3.0 %collective-permute-start.3 = (f32[8,128]{1,0:T(8,128)S(1)}, f32[8,128]{1,0:T(8,128)S(1)}, u32[]{:S(2)}, u32[]{:S(2)}) collective-permute-start(f32[8,128]{1,0:T(8,128)S(1)} %taught_stats.1.refs_9_), channel_id=1, source_target_pairs={{0,8},{1,9},{2,10},{3,11},{4,12},{5,13},{6,14},{7,15},{8,0},{9,1},... | collective-permute-start | bytes 12296 | tf_op jit(solution)/shard_map/ppermute | solution.py:319
  8.2 2.0 %copy-start = (bf16[3584,512]{1,0:T(8,128)(2,1)S(1)}, bf16[3584,512]{1,0:T(8,128)(2,1)}, u32[]{:S(2)}) copy-start(bf16[3584,512]{1,0:T(8,128)(2,1)} %refs_1_) | copy-start | bytes 11010052
  10.2 11.9 %copy-start.1 = (bf16[3584,512]{1,0:T(8,128)(2,1)S(1)}, bf16[3584,512]{1,0:T(8,128)(2,1)}, u32[]{:S(2)}) copy-start(bf16[3584,512]{1,0:T(8,128)(2,1)} %refs_1_) | copy-start | bytes 11010052
  10.2 11.9 %copy-start.4 = (s32[128]{0:T(128)S(1)}, s32[128]{0:T(128)}, u32[]{:S(2)}) copy-start(s32[128]{0:T(128)} %param.6) | copy-start | bytes 1540
  11.5 7.7 %collective-permute-start.6 = (bf16[32,3584]{1,0:T(8,128)(2,1)S(1)}, bf16[32,3584]{1,0:T(8,128)(2,1)S(1)}, u32[]{:S(2)}, u32[]{:S(2)}) collective-permute-start(bf16[32,3584]{1,0:T(8,128)(2,1)S(1)} %collective-permute-done.2.refs_0_.refs_1_), channel_id=1, source_target_pairs={{0,2},{1,3},{2,0},{3,1},{4,6},{5,7},{6,4},{7,5},{8,10},{9,11},{10,... | collective-permute-start | bytes 688136 | tf_op jit(solution)/shard_map/ppermute | solution.py:319
  13.5 7.2 %collective-permute-start.5 = (bf16[32,3584]{1,0:T(8,128)(2,1)S(1)}, bf16[32,3584]{1,0:T(8,128)(2,1)S(1)}, u32[]{:S(2)}, u32[]{:S(2)}) collective-permute-start(bf16[32,3584]{1,0:T(8,128)(2,1)S(1)} %collective-permute-done.2.refs_0_.refs_1_), channel_id=1, source_target_pairs={{0,1},{1,0},{2,3},{3,2},{4,5},{5,4},{6,7},{7,6},{8,9},{9,8},{10,11... | collective-permute-start | bytes 688136 | tf_op jit(solution)/shard_map/ppermute | solution.py:319
  15.0 7.2 %collective-permute-start.4 = (bf16[2,128,512]{2,1,0:T(8,128)(2,1)S(1)}, bf16[2,128,512]{2,1,0:T(8,128)(2,1)S(1)}, u32[]{:S(2)}, u32[]{:S(2)}) collective-permute-start(bf16[2,128,512]{2,1,0:T(8,128)(2,1)S(1)} %get-tuple-element.63.kept_ref.a0), channel_id=1, source_target_pairs={{0,8},{1,9},{2,10},{3,11},{4,12},{5,13},{6,14},{7,15},{8,0},{9,1},... | collective-permute-start | bytes 786440 | tf_op jit(solution)/shard_map/ppermute | solution.py:319
  20.7 9.2 %collective-permute-start.14 = (bf16[2,128,512]{2,1,0:T(8,128)(2,1)S(1)}, bf16[2,128,512]{2,1,0:T(8,128)(2,1)S(1)}, u32[]{:S(2)}, u32[]{:S(2)}) collective-permute-start(bf16[2,128,512]{2,1,0:T(8,128)(2,1)S(1)} %get-tuple-element.85.gone_ref), channel_id=1, source_target_pairs={{0,16},{1,17},{2,18},{3,19},{4,20},{5,21},{6,22},{7,23},{8,24},{9,... | collective-permute-start | bytes 786440 | tf_op jit(solution)/shard_map/ppermute | solution.py:319
  24.2 10.3 %copy-start.3 = (s32[512]{0:T(512)S(1)}, s32[512]{0:T(512)}, u32[]{:S(2)}) copy-start(s32[512]{0:T(512)} %param.7) | copy-start | bytes 6148
  24.2 4.7 %collective-permute-start.10 = (f32[2,8,128]{2,1,0:T(8,128)S(1)}, f32[2,8,128]{2,1,0:T(8,128)S(1)}, u32[]{:S(2)}, u32[]{:S(2)}) collective-permute-start(f32[2,8,128]{2,1,0:T(8,128)S(1)} %get-tuple-element.78.refs_0_), channel_id=1, source_target_pairs={{0,17},{1,16},{2,19},{3,18},{4,21},{5,20},{6,23},{7,22},{8,25},{9,... | collective-permute-start | bytes 24584 | tf_op jit(solution)/shard_map/ppermute | solution.py:319
  25.7 3.7 %collective-permute-start.9 = (f32[2,8,128]{2,1,0:T(8,128)S(1)}, f32[2,8,128]{2,1,0:T(8,128)S(1)}, u32[]{:S(2)}, u32[]{:S(2)}) collective-permute-start(f32[2,8,128]{2,1,0:T(8,128)S(1)} %get-tuple-element.78.refs_0_), channel_id=1, source_target_pairs={{0,1},{1,0},{2,3},{3,2},{4,5},{5,4},{6,7},{7,6},{8,9},{9,8},{10,11... | collective-permute-start | bytes 24584 | tf_op jit(solution)/shard_map/ppermute | solution.py:319
  26.2 3.7 %collective-permute-start.8 = (f32[2,8,128]{2,1,0:T(8,128)S(1)}, f32[2,8,128]{2,1,0:T(8,128)S(1)}, u32[]{:S(2)}, u32[]{:S(2)}) collective-permute-start(f32[2,8,128]{2,1,0:T(8,128)S(1)} %get-tuple-element.78.refs_0_), channel_id=1, source_target_pairs={{0,16},{1,17},{2,18},{3,19},{4,20},{5,21},{6,22},{7,23},{8,24},{9,... | collective-permute-start | bytes 24584 | tf_op jit(solution)/shard_map/ppermute | solution.py:319
  29.9 4.5 %collective-permute-start.15 = (bf16[2,128,512]{2,1,0:T(8,128)(2,1)S(1)}, bf16[2,128,512]{2,1,0:T(8,128)(2,1)S(1)}, u32[]{:S(2)}, u32[]{:S(2)}) collective-permute-start(bf16[2,128,512]{2,1,0:T(8,128)(2,1)S(1)} %collective-permute-done.14.a2), channel_id=1, source_target_pairs={{0,8},{1,9},{2,10},{3,11},{4,12},{5,13},{6,14},{7,15},{8,0},{9,1},... | collective-permute-start | bytes 786440 | tf_op jit(solution)/shard_map/ppermute | solution.py:319
  30.0 5.7 %collective-permute-start.13 = (f32[2,8,128]{2,1,0:T(8,128)S(1)}, f32[2,8,128]{2,1,0:T(8,128)S(1)}, u32[]{:S(2)}, u32[]{:S(2)}) collective-permute-start(f32[2,8,128]{2,1,0:T(8,128)S(1)} %merge_stats.1.refs_3_), channel_id=1, source_target_pairs={{0,6},{1,7},{2,4},{3,5},{4,2},{5,3},{6,0},{7,1},{8,14},{9,15},{10,... | collective-permute-start | bytes 24584 | tf_op jit(solution)/shard_map/ppermute | solution.py:319
  32.5 4.5 %collective-permute-start.12 = (f32[2,8,128]{2,1,0:T(8,128)S(1)}, f32[2,8,128]{2,1,0:T(8,128)S(1)}, u32[]{:S(2)}, u32[]{:S(2)}) collective-permute-start(f32[2,8,128]{2,1,0:T(8,128)S(1)} %merge_stats.1.refs_3_), channel_id=1, source_target_pairs={{0,4},{1,5},{2,6},{3,7},{4,0},{5,1},{6,2},{7,3},{8,12},{9,13},{10,... | collective-permute-start | bytes 24584 | tf_op jit(solution)/shard_map/ppermute | solution.py:319
  32.7 4.3 %collective-permute-start.11 = (f32[2,8,128]{2,1,0:T(8,128)S(1)}, f32[2,8,128]{2,1,0:T(8,128)S(1)}, u32[]{:S(2)}, u32[]{:S(2)}) collective-permute-start(f32[2,8,128]{2,1,0:T(8,128)S(1)} %merge_stats.1.refs_3_), channel_id=1, source_target_pairs={{0,2},{1,3},{2,0},{3,1},{4,6},{5,7},{6,4},{7,5},{8,10},{9,11},{10,... | collective-permute-start | bytes 24584 | tf_op jit(solution)/shard_map/ppermute | solution.py:319
  41.5 4.6 %collective-permute-start.16 = (bf16[128,3584]{1,0:T(8,128)(2,1)S(1)}, bf16[128,3584]{1,0:T(8,128)(2,1)S(1)}, u32[]{:S(2)}, u32[]{:S(2)}) collective-permute-start(bf16[128,3584]{1,0:T(8,128)(2,1)S(1)} %get-tuple-element.91.r1), channel_id=1, source_target_pairs={{0,8},{1,9},{2,10},{3,11},{4,12},{5,13},{6,14},{7,15},{8,0},{9,1},... | collective-permute-start | bytes 2752520 | tf_op jit(solution)/shard_map/ppermute | solution.py:319
  41.5 4.5 %collective-permute-start.17 = (bf16[256,512]{1,0:T(8,128)(2,1)S(1)}, bf16[256,512]{1,0:T(8,128)(2,1)S(1)}, u32[]{:S(2)}, u32[]{:S(2)}) collective-permute-start(bf16[256,512]{1,0:T(8,128)(2,1)S(1)} %get-tuple-element.90), channel_id=1, source_target_pairs={{0,8},{1,9},{2,10},{3,11},{4,12},{5,13},{6,14},{7,15},{8,0},{9,1},... | collective-permute-start | bytes 786440 | tf_op jit(solution)/shard_map/ppermute | solution.py:319
  42.0 11.0 %collective-permute-start.20 = (bf16[128,1280]{1,0:T(8,128)(2,1)S(1)}, bf16[128,1280]{1,0:T(8,128)(2,1)S(1)}, u32[]{:S(2)}, u32[]{:S(2)}) collective-permute-start(bf16[128,1280]{1,0:T(8,128)(2,1)S(1)} %get-tuple-element.95), channel_id=1, source_target_pairs={{0,2},{1,3},{2,0},{3,1},{4,6},{5,7},{6,4},{7,5},{8,10},{9,11},{10,... | collective-permute-start | bytes 983048 | tf_op jit(solution)/shard_map/ppermute | solution.py:319
  43.1 8.7 %collective-permute-start.18 = (bf16[128,1152]{1,0:T(8,128)(2,1)S(1)}, bf16[128,1152]{1,0:T(8,128)(2,1)S(1)}, u32[]{:S(2)}, u32[]{:S(2)}) collective-permute-start(bf16[128,1152]{1,0:T(8,128)(2,1)S(1)} %get-tuple-element.93), channel_id=1, source_target_pairs={{0,16},{1,17},{2,18},{3,19},{4,20},{5,21},{6,22},{7,23},{8,24},{9,... | collective-permute-start | bytes 884744 | tf_op jit(solution)/shard_map/ppermute | solution.py:319
  44.6 8.4 %collective-permute-start.19 = (bf16[128,1152]{1,0:T(8,128)(2,1)S(1)}, bf16[128,1152]{1,0:T(8,128)(2,1)S(1)}, u32[]{:S(2)}, u32[]{:S(2)}) collective-permute-start(bf16[128,1152]{1,0:T(8,128)(2,1)S(1)} %get-tuple-element.94), channel_id=1, source_target_pairs={{0,1},{1,0},{2,3},{3,2},{4,5},{5,4},{6,7},{7,6},{8,9},{9,8},{10,11... | collective-permute-start | bytes 884744 | tf_op jit(solution)/shard_map/ppermute | solution.py:319
  53.0 5.2 %collective-permute-start.21 = (bf16[1,2,2,1,16,1152]{5,4,3,2,1,0:T(8,128)(2,1)S(1)}, bf16[1,2,2,1,16,1152]{5,4,3,2,1,0:T(8,128)(2,1)S(1)}, u32[]{:S(2)}, u32[]{:S(2)}) collective-permute-start(bf16[1,2,2,1,16,1152]{5,4,3,2,1,0:T(8,128)(2,1)S(1)} %fusion.1), channel_id=1, source_target_pairs={{0,1},{1,0},{2,3},{3,2},{4,5},{5,4},{6,7},{7,6},{8,9},{9,8},{10,11... | collective-permute-start | bytes 442376 | tf_op jit(solution)/shard_map/ppermute | solution.py:319
  54.7 6.0 %collective-permute-start.24 = (bf16[2,2,1,1,16,1152]{5,4,3,2,1,0:T(8,128)(2,1)S(1)}, bf16[2,2,1,1,16,1152]{5,4,3,2,1,0:T(8,128)(2,1)S(1)}, u32[]{:S(2)}, u32[]{:S(2)}) collective-permute-start(bf16[2,2,1,1,16,1152]{5,4,3,2,1,0:T(8,128)(2,1)S(1)} %fusion), channel_id=1, source_target_pairs={{0,2},{1,3},{2,0},{3,1},{4,6},{5,7},{6,4},{7,5},{8,10},{9,11},{10,... | collective-permute-start | bytes 442376 | tf_op jit(solution)/shard_map/ppermute | solution.py:319
  55.8 6.1 %collective-permute-start.27 = (bf16[1,2,1,2,16,1280]{5,4,3,2,1,0:T(8,128)(2,1)S(1)}, bf16[1,2,1,2,16,1280]{5,4,3,2,1,0:T(8,128)(2,1)S(1)}, u32[]{:S(2)}, u32[]{:S(2)}) collective-permute-start(bf16[1,2,1,2,16,1280]{5,4,3,2,1,0:T(8,128)(2,1)S(1)} %bitcast.59), channel_id=1, source_target_pairs={{0,16},{1,17},{2,18},{3,19},{4,20},{5,21},{6,22},{7,23},{8,24},{9,... | collective-permute-start | bytes 491528 | tf_op jit(solution)/shard_map/ppermute | solution.py:319
  58.3 4.4 %collective-permute-start.22 = (bf16[1,2,1,1,16,1152]{5,4,3,2,1,0:T(8,128)(2,1)S(1)}, bf16[1,2,1,1,16,1152]{5,4,3,2,1,0:T(8,128)(2,1)S(1)}, u32[]{:S(2)}, u32[]{:S(2)}) collective-permute-start(bf16[1,2,1,1,16,1152]{5,4,3,2,1,0:T(8,128)(2,1)S(1)} %fusion.7), channel_id=1, source_target_pairs={{0,2},{1,3},{2,0},{3,1},{4,6},{5,7},{6,4},{7,5},{8,10},{9,11},{10,... | collective-permute-start | bytes 221192 | tf_op jit(solution)/shard_map/ppermute | solution.py:319
  60.7 4.4 %collective-permute-start.25 = (bf16[1,2,1,1,16,1152]{5,4,3,2,1,0:T(8,128)(2,1)S(1)}, bf16[1,2,1,1,16,1152]{5,4,3,2,1,0:T(8,128)(2,1)S(1)}, u32[]{:S(2)}, u32[]{:S(2)}) collective-permute-start(bf16[1,2,1,1,16,1152]{5,4,3,2,1,0:T(8,128)(2,1)S(1)} %fusion.5), channel_id=1, source_target_pairs={{0,16},{1,17},{2,18},{3,19},{4,20},{5,21},{6,22},{7,23},{8,24},{9,... | collective-permute-start | bytes 221192 | tf_op jit(solution)/shard_map/ppermute | solution.py:319
  62.0 5.0 %collective-permute-start.28 = (bf16[1,2,1,1,16,1280]{5,4,3,2,1,0:T(8,128)(2,1)S(1)}, bf16[1,2,1,1,16,1280]{5,4,3,2,1,0:T(8,128)(2,1)S(1)}, u32[]{:S(2)}, u32[]{:S(2)}) collective-permute-start(bf16[1,2,1,1,16,1280]{5,4,3,2,1,0:T(8,128)(2,1)S(1)} %fusion.3), channel_id=1, source_target_pairs={{0,1},{1,0},{2,3},{3,2},{4,5},{5,4},{6,7},{7,6},{8,9},{9,8},{10,11... | collective-permute-start | bytes 245768 | tf_op jit(solution)/shard_map/ppermute | solution.py:319
  62.7 5.9 %collective-permute-start.23 = (bf16[1,1,1,1,16,1152]{5,4,3,2,1,0:T(8,128)(2,1)S(1)}, bf16[1,1,1,1,16,1152]{5,4,3,2,1,0:T(8,128)(2,1)S(1)}, u32[]{:S(2)}, u32[]{:S(2)}) collective-permute-start(bf16[1,1,1,1,16,1152]{5,4,3,2,1,0:T(8,128)(2,1)S(1)} %fusion.22), channel_id=1, source_target_pairs={{0,4},{1,5},{2,6},{3,7},{4,0},{5,1},{6,2},{7,3},{8,12},{9,13},{10,... | collective-permute-start | bytes 110600 | tf_op jit(solution)/shard_map/ppermute | solution.py:319
  65.2 4.9 %collective-permute-start.26 = (bf16[1,1,1,1,16,1152]{5,4,3,2,1,0:T(8,128)(2,1)S(1)}, bf16[1,1,1,1,16,1152]{5,4,3,2,1,0:T(8,128)(2,1)S(1)}, u32[]{:S(2)}, u32[]{:S(2)}) collective-permute-start(bf16[1,1,1,1,16,1152]{5,4,3,2,1,0:T(8,128)(2,1)S(1)} %fusion.16), channel_id=1, source_target_pairs={{0,4},{1,5},{2,6},{3,7},{4,0},{5,1},{6,2},{7,3},{8,12},{9,13},{10,... | collective-permute-start | bytes 110600 | tf_op jit(solution)/shard_map/ppermute | solution.py:319
  67.0 5.0 %collective-permute-start.29 = (bf16[1,1,1,1,16,1280]{5,4,3,2,1,0:T(8,128)(2,1)S(1)}, bf16[1,1,1,1,16,1280]{5,4,3,2,1,0:T(8,128)(2,1)S(1)}, u32[]{:S(2)}, u32[]{:S(2)}) collective-permute-start(bf16[1,1,1,1,16,1280]{5,4,3,2,1,0:T(8,128)(2,1)S(1)} %fusion.10), channel_id=1, source_target_pairs={{0,4},{1,5},{2,6},{3,7},{4,0},{5,1},{6,2},{7,3},{8,12},{9,13},{10,... | collective-permute-start | bytes 122888 | tf_op jit(solution)/shard_map/ppermute | solution.py:319

commit v12 on v11

--- a/solution.py
+++ b/solution.py
@@ -199,12 +199,13 @@
     )(*parts, *held)
 
 
-def picker(bit, flip, total):
-    half = total // 2
+def picker(places, low, flip, total):
     row = lax.broadcasted_iota(jnp.int32, (total, total), 0)
-    side = jnp.where(row < half, 1 << bit, 0)
-    row = row & (half - 1)
-    row = ((row >> bit) << (bit + 1)) + side + (row & ((1 << bit) - 1))
+    top = total.bit_length() - 2
+    rest = row & ((1 << (top - 2)) - 1)
+    rest = ((rest >> low) << (low + 2)) | (rest & ((1 << low) - 1))
+    first, second, third = [(row >> (top - k)) & 1 for k in range(3)]
+    row = ((1 - first) << places[0]) | (second << places[1]) | (third << places[2]) | rest
     return (lax.broadcasted_iota(jnp.int32, (total, total), 1) == (row ^ flip)).astype(BF16)
 
 
@@ -239,12 +240,13 @@
             g_ref[j * per : (j + 1) * per, :] = grad.astype(BF16)
 
 
-def back_kernel(bits, edges, n, at_ref, *refs):
-    w_refs, g_refs, send_refs, keep_refs = refs[:2], refs[-8:-6], refs[-6:-3], refs[-3:]
-    grads_kernel(n, at_ref, *refs[2:-6])
-    for p in range(3):
+def back_kernel(low, edges, n, at_ref, *refs):
+    w_refs, g_refs, send_refs, keep_refs = refs[:2], refs[-6:-4], refs[-4:-2], refs[-2:]
+    grads_kernel(n, at_ref, *refs[2:-4])
+    x, y, z = g_refs[0].shape[0].bit_length() - 2, low, low + 1
+    for p, places in enumerate(([at_ref[4], at_ref[5], at_ref[6]], [y, z, x])):
         per = send_refs[p].shape[0]
-        pick = picker(bits[p], at_ref[0], 2 * per)
+        pick = picker(places, low, at_ref[0], 2 * per)
         back = 0.0
         for g_ref, w_ref in zip(g_refs, w_refs):
             rows = jnp.dot(pick, g_ref[...], preferred_element_type=F32).astype(BF16)
@@ -254,27 +256,25 @@
                 (((1,), (1,)), ((), ())),
                 preferred_element_type=F32,
             )
-        back = back.T
-        send_refs[p][...] = back[:per].astype(BF16)
+        back = back.astype(BF16).T
+        send_refs[p][...] = back[:per]
         keep_refs[p][...] = back[per:]
 
 
-def back_rows(at, own, other, stats, logits, serving, aligned, bits, edges):
+def back_rows(at, own, other, stats, logits, serving, aligned, low, edges):
     depth, cols = own.shape
     per = logits[0].shape[0]
-    parts = [(per, edges[p + 1] - edges[p]) for p in range(3)]
+    parts = [shape((per, edges[p + 1] - edges[p]), BF16) for p in range(2)]
     got = pl.pallas_call(
-        lambda *refs: back_kernel(bits, edges, len(stats), *refs),
-        out_shape=[shape((2 * per, cols), BF16)] * 2
-        + [shape(part, BF16) for part in parts]
-        + [shape(part, F32) for part in parts],
+        lambda *refs: back_kernel(low, edges, len(stats), *refs),
+        out_shape=[shape((2 * per, cols), BF16)] * 2 + parts * 2,
         in_specs=[SMEM] + [VMEM] * (len(stats) + 8),
-        out_specs=[VMEM] * 8,
+        out_specs=[VMEM] * 6,
         compiler_params=params(20),
         cost_estimate=cost(8 * per * depth * cols, 2 * cols * depth * 2, 4 * per * cols),
         name="back_rows",
     )(at, own, other, *stats, *logits, serving, aligned)
-    return got[0], got[1], got[2:5], got[5:8]
+    return got[0], got[1], got[2:4], got[4:6]
 
 
 def head_kernel(r0, r1, r2, r3, mine_ref, theirs_ref, out_ref):
@@ -329,8 +329,15 @@
     starts = [(quarter ^ k) * quarter_rows for k in range(4)]
     chip = me_g >> 1
     spots = ints(*starts)
+    low = owned.bit_length() - 1
+    turn = [per.bit_length() - 1, low, low + 1]
+    odd = (me_g & 1) == 1
     at = ints(
-        me_v * owned, (me_g * shards + me_v) * cols, ((me_g ^ 1) * shards + me_v) * cols, me_g
+        me_v * owned,
+        (me_g * shards + me_v) * cols,
+        ((me_g ^ 1) * shards + me_v) * cols,
+        me_g,
+        *[jnp.where(odd, turn[k - 1], turn[k]) for k in range(3)],
     )
     who = ints(me_g, me_g & 1)
     unsigned = [
@@ -394,46 +401,36 @@
             break
         stats = merge(parts, (0,) * len(parts), held)
 
-    bits = shards.bit_length() - 1
-    masks = {0: X}
-    for b in range(bits):
-        masks[1 + b] = shards >> (1 + b)
-    ydim, wdim = bits, bits - 1
-    third = depth // 128 // 3 * 128
-    edges = (0, third, 2 * third, depth)
-    orders = [(0, ydim, wdim), (ydim, wdim, 0), (wdim, 0, ydim)]
-    low = owned.bit_length() - 1
-    row_bit = {0: low + bits, ydim: low, wdim: low + 1}
-    first_bits = tuple(row_bit[order[0]] for order in orders)
+    units = depth // 128
+    edges = (0, units * 19 // 28 * 128, depth)
+    orders = [([X, Y, W], [W, X, Y]), ([Y, W, X], [Y, W, X])]
+
+    def step(value, even, odd):
+        masks = [odd if (i // shards) & 1 else even for i in range(count)]
+        return lax.ppermute(value, AXES, [(i, i ^ masks[i]) for i in range(count)])
+
     gown, gother, sents, keeps = back_rows(
-        at, weight, other_weight, parts, logits, served, aligned, first_bits, edges
-    )
-    gots = [swap(sents[p], masks[orders[p][0]]) for p in range(3)]
+        at, weight, other_weight, parts, logits, served, aligned, low, edges
+    )
+    gots = [step(sents[p], orders[p][0][0], orders[p][1][0]) for p in range(2)]
     theirs = swap(gother, CORE)
     _, x_sent = tie(gother, x_rows)
     grad_head = head_gradient([hidden, x_rows, core_hidden, swap(x_sent, CORE)], gown, theirs)
-    grad_head, *gots = tie(grad_head, *gots)
-
-    def folded(value, p):
-        dims = [2] * (1 + bits)
-        dims[orders[p][0]] = 1
-        return value.reshape(*dims, owned, value.shape[-1])
-
-    terms = [[folded(keeps[p], p), folded(gots[p], p)] for p in range(3)]
-    for stage in (1, 2):
-        sents = [
-            sum(lax.index_in_dim(t, 1, orders[p][stage]).astype(F32) for t in terms[p]).astype(BF16)
-            for p in range(3)
-        ]
-        gots = [swap(sents[p], masks[orders[p][stage]]) for p in range(3)]
-        for p in range(3):
-            terms[p] = [lax.index_in_dim(t, 0, orders[p][stage]) for t in terms[p]] + [gots[p]]
-    for dim in range(1, wdim):
-        for p in range(3):
-            sent = sum(lax.index_in_dim(t, 1, dim).astype(F32) for t in terms[p]).astype(BF16)
-            terms[p] = [lax.index_in_dim(t, 0, dim) for t in terms[p]] + [swap(sent, masks[dim])]
-    total = jnp.concatenate([sum(t.astype(F32) for t in ts) for ts in terms], axis=-1)
-    return (total.reshape(owned, depth), grad_head)
+    for p in range(2):
+        grad_head, gots[p] = tie(grad_head, gots[p])
+    terms = [[keeps[p], gots[p]] for p in range(2)]
+    masks = [(orders[p][0][k], orders[p][1][k]) for k in (1, 2) for p in range(2)]
+    mask = shards // 2
+    while mask > W:
+        masks += [(mask, mask)] * 2
+        mask //= 2
+    for k, pair in enumerate(masks):
+        ours = terms[k % 2]
+        kept = ours[0].shape[0] // 2
+        sent = sum(t[kept:].astype(F32) for t in ours).astype(BF16)
+        terms[k % 2] = [t[:kept] for t in ours] + [step(sent, *pair)]
+    total = jnp.concatenate([sum(t.astype(F32) for t in ours) for ours in terms], axis=-1)
+    return (total, grad_head)
 
 
 def solution(mesh):

time: 72.9 us -> 73.5 us (level)
  waiting for transfers between devices: 18.2 us -> 23 us
  starting transfers between devices: 32.1 us -> 28 us
    ppermute x30 -> x18, starting transfers between devices: 32.1 us -> 16.9 us  [swap(): return lax.ppermute(value, AXES, [(i, i ^ mask) for i in range(count)])]
    ppermute x0 -> x8, waiting for transfers between devices: none -> 14.3 us  [step(): return lax.ppermute(value, AXES, [(i, i ^ masks[i]) for i in range(count)])]
    ppermute x0 -> x8, starting transfers between devices: none -> 11.1 us  [step(): return lax.ppermute(value, AXES, [(i, i ^ masks[i]) for i in range(count)])]
    ppermute x30 -> x18, waiting for transfers between devices: 18.2 us -> 8.68 us  [swap(): return lax.ppermute(value, AXES, [(i, i ^ mask) for i in range(count)])]
  transfers between devices with their start and end apart: 30 -> 26, of which waited for: 17 -> 16; matrix products, arithmetic and copies ran while one was open for 3% -> 3% of each run, Pallas kernels for 15% -> 14%
where the time goes in v12:
time: 73.5 us; the launch traced here: 73.2 us
  starting transfers between devices  28 us (38%)
  waiting for transfers between devices  23 us (31%)
  Pallas kernels  14.9 us (20%)
  local copies, waits for them, and re-layouts  5.33 us (7%)
  other arithmetic  1.2 us (2%)
  between operations  0.82 us (1%)
    ppermute x18, starting transfers between devices, swap(): return lax.ppermute(value, AXES, [(i, i ^ mask) for i in range(count)])  16.9 us
    ppermute x8, waiting for transfers between devices, step(): return lax.ppermute(value, AXES, [(i, i ^ masks[i]) for i in range(count)])  14.3 us
    ppermute x8, starting transfers between devices, step(): return lax.ppermute(value, AXES, [(i, i ^ masks[i]) for i in range(count)])  11.1 us
    ppermute x18, waiting for transfers between devices, swap(): return lax.ppermute(value, AXES, [(i, i ^ mask) for i in range(count)])  8.68 us
    pallas_call x1, Pallas kernels, head_gradient(): pl.pallas_call(head_kernel, grid=(depth // tile,), out_shape=shape((depth...  5.23 us
    pallas_call x1, Pallas kernels, back_rows(): pl.pallas_call(lambda *refs: back_kernel(low, edges, len(stats), *refs),...  4.29 us
    unnamed x10, local copies, waits for them, and re-layouts  2.06 us
    dynamic_slice x2, local copies, waits for them, and re-layouts, cut(): return lax.dynamic_slice(value, indices, sizes)  2.02 us
  transfers between devices with their start and end apart: 26, of which 16 were waited for; matrix products, arithmetic and copies ran while one was open for 3% of the time, Pallas kernels for 14%

profile of v12, /device:TPU:0, one launch (start us, length us, event | category | flops | bytes accessed | tf_op | source)
XLA Modules:
  0.0 73.2 jit_solution(4568712507842991468)
XLA Ops:
  0.6 0.0 copy-start.2
  0.7 0.1 pad_add_fusion.1.at_ref
  0.7 0.1 pad_add_fusion.refs_0_
  0.8 0.1 stack.58.refs_0_
  0.9 1.0 %constant_dynamic-slice_fusion.1 = bf16[32,3584]{1,0:T(8,128)(2,1)S(1)} fusion(bf16[128,3584]{1,0:T(8,128)(2,1)} %r0.1, u32[]{:T(128)S(6)} %convert_element_type.114), kind=kLoop, calls=%fused_computation.12 | loop fusion | bytes 458756 | tf_op jit(solution)/shard_map/dynamic_slice | solution.py:353
  1.9 0.5 collective-permute-start
  2.5 2.6 %collective-permute-start.2 = (bf16[32,3584]{1,0:T(8,128)(2,1)S(1)}, bf16[32,3584]{1,0:T(8,128)(2,1)S(1)}, u32[]{:S(2)}, u32[]{:S(2)}) collective-permute-start(bf16[32,3584]{1,0:T(8,128)(2,1)S(1)} %constant_dynamic-slice_fusion.1), channel_id=1, source_target_pairs={{0,16},{1,17},{2,18},{3,19},{4,20},{5,21},{6,22},{7,23},{8,24},{9,... | collective-permute-start | bytes 688136 | tf_op jit(solution)/shard_map/ppermute | solution.py:319
  5.0 0.2 collective-permute-start.1
  5.2 1.0 %constant_dynamic-slice_fusion = bf16[32,3584]{1,0:T(8,128)(2,1)S(1)} fusion(bf16[128,3584]{1,0:T(8,128)(2,1)} %r0.1, u32[]{:T(128)S(6)} %convert_element_type.115), kind=kLoop, calls=%fused_computation.11 | loop fusion | bytes 458756 | tf_op jit(solution)/shard_map/dynamic_slice | solution.py:353
  6.2 0.3 collective-permute-start.7
  6.5 1.1 %copy.7 = bf16[128,4,512]{2,0,1:T(8,128)(2,1)S(1)} copy(bf16[128,4,512]{2,1,0:T(4,128)(2,1)} %param.9) | data formatting | bytes 1048576 | tf_op jit(solution)/shard_map/optimization_barrier | solution.py:322
  7.7 0.4 taught_stats.1.refs_9_
  8.1 0.1 collective-permute-start.3
  8.2 2.0 %copy-done = bf16[3584,512]{1,0:T(8,128)(2,1)S(1)} copy-done((bf16[3584,512]{1,0:T(8,128)(2,1)S(1)}, bf16[3584,512]{1,0:T(8,128)(2,1)}, u32[]{:S(2)}) %copy-start) | copy-done | bytes 3670040
  10.2 0.9 %near_logits.2 = (f32[128,512]{1,0:T(8,128)S(1)}, f32[8,128]{1,0:T(8,128)S(1)}) custom-call(bf16[128,3584]{1,0:T(8,128)(2,1)S(1)} %copy-done.2, bf16[3584,512]{1,0:T(8,128)(2,1)S(1)} %copy-done), custom_call_target="tpu_custom_call" | custom-call | flops 469762048 | bytes 4587520 | tf_op jit(solution)/shard_map/near_logits/pallas_call | solution.py:108
  11.1 0.4 collective-permute-done.2.refs_0_.refs_1_
  11.5 2.0 %collective-permute-start.6 = (bf16[32,3584]{1,0:T(8,128)(2,1)S(1)}, bf16[32,3584]{1,0:T(8,128)(2,1)S(1)}, u32[]{:S(2)}, u32[]{:S(2)}) collective-permute-start(bf16[32,3584]{1,0:T(8,128)(2,1)S(1)} %collective-permute-done.2.refs_0_.refs_1_), channel_id=1, source_target_pairs={{0,2},{1,3},{2,0},{3,1},{4,6},{5,7},{6,4},{7,5},{8,10},{9,11},{10,... | collective-permute-start | bytes 688136 | tf_op jit(solution)/shard_map/ppermute | solution.py:319
  13.5 1.5 %collective-permute-start.5 = (bf16[32,3584]{1,0:T(8,128)(2,1)S(1)}, bf16[32,3584]{1,0:T(8,128)(2,1)S(1)}, u32[]{:S(2)}, u32[]{:S(2)}) collective-permute-start(bf16[32,3584]{1,0:T(8,128)(2,1)S(1)} %collective-permute-done.2.refs_0_.refs_1_), channel_id=1, source_target_pairs={{0,1},{1,0},{2,3},{3,2},{4,5},{5,4},{6,7},{7,6},{8,9},{9,8},{10,11... | collective-permute-start | bytes 688136 | tf_op jit(solution)/shard_map/ppermute | solution.py:319
  15.0 0.9 %near_logits.3 = (f32[128,512]{1,0:T(8,128)S(1)}, f32[8,128]{1,0:T(8,128)S(1)}) custom-call(bf16[128,3584]{1,0:T(8,128)(2,1)S(1)} %copy-done.2, bf16[3584,512]{1,0:T(8,128)(2,1)S(1)} %collective-permute-done.w_ref.refs_6_.refs_2_, bf16[32,3584]{1,0:T(8,128)(2,1)S(1)} %collective-permute-done.2.refs_0_.refs_1_), custom_call_target="tpu_custom_call" | custom-call | flops 469762048 | bytes 4587520 | tf_op jit(solution)/shard_map/near_logits/pallas_call | solution.py:108
  15.9 0.3 collective-permute-done.7.refs_4_
  16.1 3.1 %collective-permute-done.6.refs_3_ = bf16[32,3584]{1,0:T(8,128)(2,1)S(1)} collective-permute-done((bf16[32,3584]{1,0:T(8,128)(2,1)S(1)}, bf16[32,3584]{1,0:T(8,128)(2,1)S(1)}, u32[]{:S(2)}, u32[]{:S(2)}) %collective-permute-start.6) | collective-permute-done | bytes 229408 | tf_op jit(solution)/shard_map/ppermute | solution.py:319
  19.2 1.5 %collective-permute-done.5.refs_2_ = bf16[32,3584]{1,0:T(8,128)(2,1)S(1)} collective-permute-done((bf16[32,3584]{1,0:T(8,128)(2,1)S(1)}, bf16[32,3584]{1,0:T(8,128)(2,1)S(1)}, u32[]{:S(2)}, u32[]{:S(2)}) %collective-permute-start.5) | collective-permute-done | bytes 229408 | tf_op jit(solution)/shard_map/ppermute | solution.py:319
  20.7 1.5 %collective-permute-start.14 = (bf16[2,128,512]{2,1,0:T(8,128)(2,1)S(1)}, bf16[2,128,512]{2,1,0:T(8,128)(2,1)S(1)}, u32[]{:S(2)}, u32[]{:S(2)}) collective-permute-start(bf16[2,128,512]{2,1,0:T(8,128)(2,1)S(1)} %get-tuple-element.83.gone_ref), channel_id=1, source_target_pairs={{0,16},{1,17},{2,18},{3,19},{4,20},{5,21},{6,22},{7,23},{8,24},{9,... | collective-permute-start | bytes 786440 | tf_op jit(solution)/shard_map/ppermute | solution.py:319
  22.2 0.0 collective-permute-done.4.a1
  22.2 0.0 collective-permute-done.1.r2
  22.2 2.0 %far_logits.1 = (f32[128,512]{1,0:T(8,128)S(1)}, f32[128,512]{1,0:T(8,128)S(1)}, bf16[128,3584]{1,0:T(8,128)(2,1)S(1)}, f32[2,8,128]{2,1,0:T(8,128)S(1)}) custom-call(s32[4]{0:T(128)S(1)} %pad_add_fusion.refs_0_, bf16[32,3584]{1,0:T(8,128)(2,1)S(1)} %collective-permute-done.2.refs_0_.refs_1_, bf16[32,3584]{1,0:T(8,128)(2,1)S(1)} %collective-permute-done.5.refs_2_, ...), custom_call_target="tpu_custom_call" | custom-call | flops 939524096 | bytes 8257536 | tf_op jit(solution)/shard_map/far_logits/pallas_call | solution.py:153
  24.2 0.0 copy-start.3
  24.2 1.5 %collective-permute-start.10 = (f32[2,8,128]{2,1,0:T(8,128)S(1)}, f32[2,8,128]{2,1,0:T(8,128)S(1)}, u32[]{:S(2)}, u32[]{:S(2)}) collective-permute-start(f32[2,8,128]{2,1,0:T(8,128)S(1)} %get-tuple-element.76.refs_0_), channel_id=1, source_target_pairs={{0,17},{1,16},{2,19},{3,18},{4,21},{5,20},{6,23},{7,22},{8,25},{9,... | collective-permute-start | bytes 24584 | tf_op jit(solution)/shard_map/ppermute | solution.py:319
  25.7 0.5 collective-permute-start.9
  26.2 1.5 %collective-permute-start.8 = (f32[2,8,128]{2,1,0:T(8,128)S(1)}, f32[2,8,128]{2,1,0:T(8,128)S(1)}, u32[]{:S(2)}, u32[]{:S(2)}) collective-permute-start(f32[2,8,128]{2,1,0:T(8,128)S(1)} %get-tuple-element.76.refs_0_), channel_id=1, source_target_pairs={{0,16},{1,17},{2,18},{3,19},{4,20},{5,21},{6,22},{7,23},{8,24},{9,... | collective-permute-start | bytes 24584 | tf_op jit(solution)/shard_map/ppermute | solution.py:319
  27.7 1.1 %collective-permute-done.10.refs_3_ = f32[2,8,128]{2,1,0:T(8,128)S(1)} collective-permute-done((f32[2,8,128]{2,1,0:T(8,128)S(1)}, f32[2,8,128]{2,1,0:T(8,128)S(1)}, u32[]{:S(2)}, u32[]{:S(2)}) %collective-permute-start.10) | collective-permute-done | bytes 8224 | tf_op jit(solution)/shard_map/ppermute | solution.py:319
  28.9 0.5 collective-permute-done.9.refs_2_
  29.4 0.5 collective-permute-done.8.refs_1_
  29.9 0.0 collective-permute-done.14.a2
  29.9 0.1 collective-permute-start.15
  30.0 2.5 %collective-permute-start.13 = (f32[2,8,128]{2,1,0:T(8,128)S(1)}, f32[2,8,128]{2,1,0:T(8,128)S(1)}, u32[]{:S(2)}, u32[]{:S(2)}) collective-permute-start(f32[2,8,128]{2,1,0:T(8,128)S(1)} %merge_stats.1.refs_3_), channel_id=1, source_target_pairs={{0,6},{1,7},{2,4},{3,5},{4,2},{5,3},{6,0},{7,1},{8,14},{9,15},{10,... | collective-permute-start | bytes 24584 | tf_op jit(solution)/shard_map/ppermute | solution.py:319
  32.5 0.2 collective-permute-start.12
  32.7 1.7 %collective-permute-start.11 = (f32[2,8,128]{2,1,0:T(8,128)S(1)}, f32[2,8,128]{2,1,0:T(8,128)S(1)}, u32[]{:S(2)}, u32[]{:S(2)}) collective-permute-start(f32[2,8,128]{2,1,0:T(8,128)S(1)} %merge_stats.1.refs_3_), channel_id=1, source_target_pairs={{0,2},{1,3},{2,0},{3,1},{4,6},{5,7},{6,4},{7,5},{8,10},{9,11},{10,... | collective-permute-start | bytes 24584 | tf_op jit(solution)/shard_map/ppermute | solution.py:319
  34.5 1.3 %teacher_rows.1.refs_12_ = bf16[2,128,1024]{2,1,0:T(8,128)(2,1)S(1)} custom-call(s32[2]{0:T(128)S(1)} %pad_add_fusion.1.at_ref, s32[4,1,128]{2,1,0:T(1,128)S(1)} %bitcast.18, bf16[2,128,512]{2,1,0:T(8,128)(2,1)S(1)} %get-tuple-element.61.kept_ref.a0, bf16[2,128,512]{2,1,0:T(8,128)(2,1)S(1)} %collective-permute-done.4.a1, ...), custom_call_target="tpu_custom_call" | custom-call | flops 268435456 | bytes 1572864 | tf_op jit(solution)/shard_map/teacher_rows/pallas_call | solution.py:80
  35.8 1.3 %collective-permute-done.12.refs_5_ = f32[2,8,128]{2,1,0:T(8,128)S(1)} collective-permute-done((f32[2,8,128]{2,1,0:T(8,128)S(1)}, f32[2,8,128]{2,1,0:T(8,128)S(1)}, u32[]{:S(2)}, u32[]{:S(2)}) %collective-permute-start.12) | collective-permute-done | bytes 8224 | tf_op jit(solution)/shard_map/ppermute | solution.py:319
  37.1 4.3 %back_rows.1 = (bf16[256,512]{1,0:T(8,128)(2,1)S(1)}, bf16[256,512]{1,0:T(8,128)(2,1)S(1)}, bf16[128,2432]{1,0:T(8,128)(2,1)S(1)}, bf16[128,1152]{1,0:T(8,128)(2...) custom-call(s32[7]{0:T(128)S(1)} %stack.58.refs_0_, bf16[3584,512]{1,0:T(8,128)(2,1)S(1)} %copy-done.1, ...), custom_call_target="tpu_custom_call" | custom-call | flops 1879048192 | bytes 7340032 | tf_op jit(solution)/shard_map/back_rows/pallas_call | solution.py:268
  41.4 0.1 collective-permute-start.16
  41.5 1.6 %collective-permute-start.18 = (bf16[128,2432]{1,0:T(8,128)(2,1)S(1)}, bf16[128,2432]{1,0:T(8,128)(2,1)S(1)}, u32[]{:S(2)}, u32[]{:S(2)}) collective-permute-start(bf16[128,2432]{1,0:T(8,128)(2,1)S(1)} %get-tuple-element.91), channel_id=1, source_target_pairs={{0,16},{1,17},{2,18},{3,19},{4,20},{5,21},{6,22},{7,23},{8,10},{9,... | collective-permute-start | bytes 1867784 | tf_op jit(solution)/shard_map/ppermute | solution.py:410
  43.0 1.5 %collective-permute-start.22 = (bf16[128,1152]{1,0:T(8,128)(2,1)S(1)}, bf16[128,1152]{1,0:T(8,128)(2,1)S(1)}, u32[]{:S(2)}, u32[]{:S(2)}) collective-permute-start(bf16[128,1152]{1,0:T(8,128)(2,1)S(1)} %get-tuple-element.95), channel_id=1, source_target_pairs={{0,1},{1,0},{2,3},{3,2},{4,5},{5,4},{6,7},{7,6},{8,9},{9,8},{10,11... | collective-permute-start | bytes 884744 | tf_op jit(solution)/shard_map/ppermute | solution.py:410
  44.5 0.0 collective-permute-done.17.theirs_ref
  44.6 5.2 %head_gradient.1 = bf16[3584,512]{1,0:T(8,128)(2,1)} custom-call(bf16[128,3584]{1,0:T(8,128)(2,1)S(1)} %copy-done.2, bf16[128,3584]{1,0:T(8,128)(2,1)S(1)} %get-tuple-element.89.r1, bf16[128,3584]{1,0:T(8,128)(2,1)S(1)} %collective-permute-done.1.r2, bf16[128,3584]{1,0:T(8,128)(2,1)S(1)} %collective-permute-done.16.r3, ...), custom_call_target="tpu_custom_call" | custom-call | flops 1879048192 | bytes 7340032 | tf_op jit(solution)/shard_map/head_gradient/pallas_call | solution.py:294
  49.8 2.0 %collective-permute-done.18 = bf16[128,2432]{1,0:T(8,128)(2,1)S(1)} collective-permute-done((bf16[128,2432]{1,0:T(8,128)(2,1)S(1)}, bf16[128,2432]{1,0:T(8,128)(2,1)S(1)}, u32[]{:S(2)}, u32[]{:S(2)}) %collective-permute-start.18) | collective-permute-done | bytes 622624 | tf_op jit(solution)/shard_map/ppermute | solution.py:410
  51.8 0.7 collective-permute-done.22
  52.5 1.1 %collective-permute-start.23 = (bf16[64,1152]{1,0:T(8,128)(2,1)S(1)}, bf16[64,1152]{1,0:T(8,128)(2,1)S(1)}, u32[]{:S(2)}, u32[]{:S(2)}) collective-permute-start(bf16[64,1152]{1,0:T(8,128)(2,1)S(1)} %add_convert_fusion.2), channel_id=1, source_target_pairs={{0,2},{1,3},{2,0},{3,1},{4,6},{5,7},{6,4},{7,5},{8,10},{9,11},{10,... | collective-permute-start | bytes 442376 | tf_op jit(solution)/shard_map/ppermute | solution.py:410
  53.6 0.1 add_convert_fusion
  53.6 1.6 %collective-permute-start.19 = (bf16[64,2432]{1,0:T(8,128)(2,1)S(1)}, bf16[64,2432]{1,0:T(8,128)(2,1)S(1)}, u32[]{:S(2)}, u32[]{:S(2)}) collective-permute-start(bf16[64,2432]{1,0:T(8,128)(2,1)S(1)} %add_convert_fusion), channel_id=1, source_target_pairs={{0,1},{1,0},{2,3},{3,2},{4,5},{5,4},{6,7},{7,6},{8,24},{9,25},{10,... | collective-permute-start | bytes 933896 | tf_op jit(solution)/shard_map/ppermute | solution.py:410
  55.2 2.8 %collective-permute-done.23 = bf16[64,1152]{1,0:T(8,128)(2,1)S(1)} collective-permute-done((bf16[64,1152]{1,0:T(8,128)(2,1)S(1)}, bf16[64,1152]{1,0:T(8,128)(2,1)S(1)}, u32[]{:S(2)}, u32[]{:S(2)}) %collective-permute-start.23) | collective-permute-done | bytes 147488 | tf_op jit(solution)/shard_map/ppermute | solution.py:410
  58.1 0.7 collective-permute-start.24
  58.8 1.8 %collective-permute-done.19 = bf16[64,2432]{1,0:T(8,128)(2,1)S(1)} collective-permute-done((bf16[64,2432]{1,0:T(8,128)(2,1)S(1)}, bf16[64,2432]{1,0:T(8,128)(2,1)S(1)}, u32[]{:S(2)}, u32[]{:S(2)}) %collective-permute-start.19) | collective-permute-done | bytes 311328 | tf_op jit(solution)/shard_map/ppermute | solution.py:410
  60.6 0.1 add_convert_fusion.1
  60.7 1.1 %collective-permute-start.20 = (bf16[32,2432]{1,0:T(8,128)(2,1)S(1)}, bf16[32,2432]{1,0:T(8,128)(2,1)S(1)}, u32[]{:S(2)}, u32[]{:S(2)}) collective-permute-start(bf16[32,2432]{1,0:T(8,128)(2,1)S(1)} %add_convert_fusion.1), channel_id=1, source_target_pairs={{0,2},{1,3},{2,0},{3,1},{4,6},{5,7},{6,4},{7,5},{8,9},{9,8},{10,11... | collective-permute-start | bytes 466952 | tf_op jit(solution)/shard_map/ppermute | solution.py:410
  61.7 0.7 %collective-permute-done.24 = bf16[32,1152]{1,0:T(8,128)(2,1)S(1)} collective-permute-done((bf16[32,1152]{1,0:T(8,128)(2,1)S(1)}, bf16[32,1152]{1,0:T(8,128)(2,1)S(1)}, u32[]{:S(2)}, u32[]{:S(2)}) %collective-permute-start.24) | collective-permute-done | bytes 73760 | tf_op jit(solution)/shard_map/ppermute | solution.py:410
  62.5 2.1 %collective-permute-start.25 = (bf16[16,1152]{1,0:T(8,128)(2,1)S(1)}, bf16[16,1152]{1,0:T(8,128)(2,1)S(1)}, u32[]{:S(2)}, u32[]{:S(2)}) collective-permute-start(bf16[16,1152]{1,0:T(8,128)(2,1)S(1)} %add_convert_fusion.5), channel_id=1, source_target_pairs={{0,4},{1,5},{2,6},{3,7},{4,0},{5,1},{6,2},{7,3},{8,12},{9,13},{10,... | collective-permute-start | bytes 110600 | tf_op jit(solution)/shard_map/ppermute | solution.py:410
  64.6 1.6 %collective-permute-done.20 = bf16[32,2432]{1,0:T(8,128)(2,1)S(1)} collective-permute-done((bf16[32,2432]{1,0:T(8,128)(2,1)S(1)}, bf16[32,2432]{1,0:T(8,128)(2,1)S(1)}, u32[]{:S(2)}, u32[]{:S(2)}) %collective-permute-start.20) | collective-permute-done | bytes 155680 | tf_op jit(solution)/shard_map/ppermute | solution.py:410
  66.3 1.5 %collective-permute-start.21 = (bf16[16,2432]{1,0:T(8,128)(2,1)S(1)}, bf16[16,2432]{1,0:T(8,128)(2,1)S(1)}, u32[]{:S(2)}, u32[]{:S(2)}) collective-permute-start(bf16[16,2432]{1,0:T(8,128)(2,1)S(1)} %add_convert_fusion.3), channel_id=1, source_target_pairs={{0,4},{1,5},{2,6},{3,7},{4,0},{5,1},{6,2},{7,3},{8,12},{9,13},{10,... | collective-permute-start | bytes 233480 | tf_op jit(solution)/shard_map/ppermute | solution.py:410
  67.8 1.3 %collective-permute-done.25 = bf16[16,1152]{1,0:T(8,128)(2,1)S(1)} collective-permute-done((bf16[16,1152]{1,0:T(8,128)(2,1)S(1)}, bf16[16,1152]{1,0:T(8,128)(2,1)S(1)}, u32[]{:S(2)}, u32[]{:S(2)}) %collective-permute-start.25) | collective-permute-done | bytes 36896 | tf_op jit(solution)/shard_map/ppermute | solution.py:410
  69.1 3.4 %collective-permute-done.21 = bf16[16,2432]{1,0:T(8,128)(2,1)S(1)} collective-permute-done((bf16[16,2432]{1,0:T(8,128)(2,1)S(1)}, bf16[16,2432]{1,0:T(8,128)(2,1)S(1)}, u32[]{:S(2)}, u32[]{:S(2)}) %collective-permute-start.21) | collective-permute-done | bytes 77856 | tf_op jit(solution)/shard_map/ppermute | solution.py:410
  72.4 0.1 convert_add_fusion
  72.5 0.7 pad_maximum_fusion
  (22 shorter events, 0.3 us)
Async XLA Ops:
  0.6 7.6 %copy-start.2 = (bf16[128,3584]{1,0:T(8,128)(2,1)S(1)}, bf16[128,3584]{1,0:T(8,128)(2,1)}, u32[]{:S(2)}) copy-start(bf16[128,3584]{1,0:T(8,128)(2,1)} %r0.1) | copy-start | bytes 2752516
  1.9 13.1 %collective-permute-start = (bf16[3584,512]{1,0:T(8,128)(2,1)}, bf16[3584,512]{1,0:T(8,128)(2,1)S(1)}, u32[]{:S(2)}, u32[]{:S(2)}) collective-permute-start(bf16[3584,512]{1,0:T(8,128)(2,1)} %refs_1_), channel_id=1, source_target_pairs={{0,8},{1,9},{2,10},{3,11},{4,12},{5,13},{6,14},{7,15},{8,0},{9,1},... | collective-permute-start | bytes 11010056 | tf_op jit(solution)/shard_map/ppermute | solution.py:319
  2.5 9.0 %collective-permute-start.2 = (bf16[32,3584]{1,0:T(8,128)(2,1)S(1)}, bf16[32,3584]{1,0:T(8,128)(2,1)S(1)}, u32[]{:S(2)}, u32[]{:S(2)}) collective-permute-start(bf16[32,3584]{1,0:T(8,128)(2,1)S(1)} %constant_dynamic-slice_fusion.1), channel_id=1, source_target_pairs={{0,16},{1,17},{2,18},{3,19},{4,20},{5,21},{6,22},{7,23},{8,24},{9,... | collective-permute-start | bytes 688136 | tf_op jit(solution)/shard_map/ppermute | solution.py:319
  5.0 17.2 %collective-permute-start.1 = (bf16[128,3584]{1,0:T(8,128)(2,1)}, bf16[128,3584]{1,0:T(8,128)(2,1)S(1)}, u32[]{:S(2)}, u32[]{:S(2)}) collective-permute-start(bf16[128,3584]{1,0:T(8,128)(2,1)} %r0.1), channel_id=1, source_target_pairs={{0,8},{1,9},{2,10},{3,11},{4,12},{5,13},{6,14},{7,15},{8,0},{9,1},... | collective-permute-start | bytes 2752520 | tf_op jit(solution)/shard_map/ppermute | solution.py:319
  6.2 9.9 %collective-permute-start.7 = (bf16[32,3584]{1,0:T(8,128)(2,1)S(1)}, bf16[32,3584]{1,0:T(8,128)(2,1)S(1)}, u32[]{:S(2)}, u32[]{:S(2)}) collective-permute-start(bf16[32,3584]{1,0:T(8,128)(2,1)S(1)} %constant_dynamic-slice_fusion), channel_id=1, source_target_pairs={{0,16},{1,17},{2,18},{3,19},{4,20},{5,21},{6,22},{7,23},{8,24},{9,... | collective-permute-start | bytes 688136 | tf_op jit(solution)/shard_map/ppermute | solution.py:319
  8.1 3.0 %collective-permute-start.3 = (f32[8,128]{1,0:T(8,128)S(1)}, f32[8,128]{1,0:T(8,128)S(1)}, u32[]{:S(2)}, u32[]{:S(2)}) collective-permute-start(f32[8,128]{1,0:T(8,128)S(1)} %taught_stats.1.refs_9_), channel_id=1, source_target_pairs={{0,8},{1,9},{2,10},{3,11},{4,12},{5,13},{6,14},{7,15},{8,0},{9,1},... | collective-permute-start | bytes 12296 | tf_op jit(solution)/shard_map/ppermute | solution.py:319
  8.2 2.0 %copy-start = (bf16[3584,512]{1,0:T(8,128)(2,1)S(1)}, bf16[3584,512]{1,0:T(8,128)(2,1)}, u32[]{:S(2)}) copy-start(bf16[3584,512]{1,0:T(8,128)(2,1)} %refs_1_) | copy-start | bytes 11010052
  10.2 11.9 %copy-start.1 = (bf16[3584,512]{1,0:T(8,128)(2,1)S(1)}, bf16[3584,512]{1,0:T(8,128)(2,1)}, u32[]{:S(2)}) copy-start(bf16[3584,512]{1,0:T(8,128)(2,1)} %refs_1_) | copy-start | bytes 11010052
  10.2 11.9 %copy-start.4 = (s32[128]{0:T(128)S(1)}, s32[128]{0:T(128)}, u32[]{:S(2)}) copy-start(s32[128]{0:T(128)} %param.6) | copy-start | bytes 1540
  11.5 7.7 %collective-permute-start.6 = (bf16[32,3584]{1,0:T(8,128)(2,1)S(1)}, bf16[32,3584]{1,0:T(8,128)(2,1)S(1)}, u32[]{:S(2)}, u32[]{:S(2)}) collective-permute-start(bf16[32,3584]{1,0:T(8,128)(2,1)S(1)} %collective-permute-done.2.refs_0_.refs_1_), channel_id=1, source_target_pairs={{0,2},{1,3},{2,0},{3,1},{4,6},{5,7},{6,4},{7,5},{8,10},{9,11},{10,... | collective-permute-start | bytes 688136 | tf_op jit(solution)/shard_map/ppermute | solution.py:319
  13.5 7.2 %collective-permute-start.5 = (bf16[32,3584]{1,0:T(8,128)(2,1)S(1)}, bf16[32,3584]{1,0:T(8,128)(2,1)S(1)}, u32[]{:S(2)}, u32[]{:S(2)}) collective-permute-start(bf16[32,3584]{1,0:T(8,128)(2,1)S(1)} %collective-permute-done.2.refs_0_.refs_1_), channel_id=1, source_target_pairs={{0,1},{1,0},{2,3},{3,2},{4,5},{5,4},{6,7},{7,6},{8,9},{9,8},{10,11... | collective-permute-start | bytes 688136 | tf_op jit(solution)/shard_map/ppermute | solution.py:319
  15.0 7.2 %collective-permute-start.4 = (bf16[2,128,512]{2,1,0:T(8,128)(2,1)S(1)}, bf16[2,128,512]{2,1,0:T(8,128)(2,1)S(1)}, u32[]{:S(2)}, u32[]{:S(2)}) collective-permute-start(bf16[2,128,512]{2,1,0:T(8,128)(2,1)S(1)} %get-tuple-element.61.kept_ref.a0), channel_id=1, source_target_pairs={{0,8},{1,9},{2,10},{3,11},{4,12},{5,13},{6,14},{7,15},{8,0},{9,1},... | collective-permute-start | bytes 786440 | tf_op jit(solution)/shard_map/ppermute | solution.py:319
  20.7 9.2 %collective-permute-start.14 = (bf16[2,128,512]{2,1,0:T(8,128)(2,1)S(1)}, bf16[2,128,512]{2,1,0:T(8,128)(2,1)S(1)}, u32[]{:S(2)}, u32[]{:S(2)}) collective-permute-start(bf16[2,128,512]{2,1,0:T(8,128)(2,1)S(1)} %get-tuple-element.83.gone_ref), channel_id=1, source_target_pairs={{0,16},{1,17},{2,18},{3,19},{4,20},{5,21},{6,22},{7,23},{8,24},{9,... | collective-permute-start | bytes 786440 | tf_op jit(solution)/shard_map/ppermute | solution.py:319
  24.2 10.3 %copy-start.3 = (s32[512]{0:T(512)S(1)}, s32[512]{0:T(512)}, u32[]{:S(2)}) copy-start(s32[512]{0:T(512)} %param.7) | copy-start | bytes 6148
  24.2 4.7 %collective-permute-start.10 = (f32[2,8,128]{2,1,0:T(8,128)S(1)}, f32[2,8,128]{2,1,0:T(8,128)S(1)}, u32[]{:S(2)}, u32[]{:S(2)}) collective-permute-start(f32[2,8,128]{2,1,0:T(8,128)S(1)} %get-tuple-element.76.refs_0_), channel_id=1, source_target_pairs={{0,17},{1,16},{2,19},{3,18},{4,21},{5,20},{6,23},{7,22},{8,25},{9,... | collective-permute-start | bytes 24584 | tf_op jit(solution)/shard_map/ppermute | solution.py:319
  25.7 3.7 %collective-permute-start.9 = (f32[2,8,128]{2,1,0:T(8,128)S(1)}, f32[2,8,128]{2,1,0:T(8,128)S(1)}, u32[]{:S(2)}, u32[]{:S(2)}) collective-permute-start(f32[2,8,128]{2,1,0:T(8,128)S(1)} %get-tuple-element.76.refs_0_), channel_id=1, source_target_pairs={{0,1},{1,0},{2,3},{3,2},{4,5},{5,4},{6,7},{7,6},{8,9},{9,8},{10,11... | collective-permute-start | bytes 24584 | tf_op jit(solution)/shard_map/ppermute | solution.py:319
  26.2 3.7 %collective-permute-start.8 = (f32[2,8,128]{2,1,0:T(8,128)S(1)}, f32[2,8,128]{2,1,0:T(8,128)S(1)}, u32[]{:S(2)}, u32[]{:S(2)}) collective-permute-start(f32[2,8,128]{2,1,0:T(8,128)S(1)} %get-tuple-element.76.refs_0_), channel_id=1, source_target_pairs={{0,16},{1,17},{2,18},{3,19},{4,20},{5,21},{6,22},{7,23},{8,24},{9,... | collective-permute-start | bytes 24584 | tf_op jit(solution)/shard_map/ppermute | solution.py:319
  29.9 4.5 %collective-permute-start.15 = (bf16[2,128,512]{2,1,0:T(8,128)(2,1)S(1)}, bf16[2,128,512]{2,1,0:T(8,128)(2,1)S(1)}, u32[]{:S(2)}, u32[]{:S(2)}) collective-permute-start(bf16[2,128,512]{2,1,0:T(8,128)(2,1)S(1)} %collective-permute-done.14.a2), channel_id=1, source_target_pairs={{0,8},{1,9},{2,10},{3,11},{4,12},{5,13},{6,14},{7,15},{8,0},{9,1},... | collective-permute-start | bytes 786440 | tf_op jit(solution)/shard_map/ppermute | solution.py:319
  30.0 5.7 %collective-permute-start.13 = (f32[2,8,128]{2,1,0:T(8,128)S(1)}, f32[2,8,128]{2,1,0:T(8,128)S(1)}, u32[]{:S(2)}, u32[]{:S(2)}) collective-permute-start(f32[2,8,128]{2,1,0:T(8,128)S(1)} %merge_stats.1.refs_3_), channel_id=1, source_target_pairs={{0,6},{1,7},{2,4},{3,5},{4,2},{5,3},{6,0},{7,1},{8,14},{9,15},{10,... | collective-permute-start | bytes 24584 | tf_op jit(solution)/shard_map/ppermute | solution.py:319
  32.5 4.5 %collective-permute-start.12 = (f32[2,8,128]{2,1,0:T(8,128)S(1)}, f32[2,8,128]{2,1,0:T(8,128)S(1)}, u32[]{:S(2)}, u32[]{:S(2)}) collective-permute-start(f32[2,8,128]{2,1,0:T(8,128)S(1)} %merge_stats.1.refs_3_), channel_id=1, source_target_pairs={{0,4},{1,5},{2,6},{3,7},{4,0},{5,1},{6,2},{7,3},{8,12},{9,13},{10,... | collective-permute-start | bytes 24584 | tf_op jit(solution)/shard_map/ppermute | solution.py:319
  32.7 4.3 %collective-permute-start.11 = (f32[2,8,128]{2,1,0:T(8,128)S(1)}, f32[2,8,128]{2,1,0:T(8,128)S(1)}, u32[]{:S(2)}, u32[]{:S(2)}) collective-permute-start(f32[2,8,128]{2,1,0:T(8,128)S(1)} %merge_stats.1.refs_3_), channel_id=1, source_target_pairs={{0,2},{1,3},{2,0},{3,1},{4,6},{5,7},{6,4},{7,5},{8,10},{9,11},{10,... | collective-permute-start | bytes 24584 | tf_op jit(solution)/shard_map/ppermute | solution.py:319
  41.4 3.2 %collective-permute-start.16 = (bf16[128,3584]{1,0:T(8,128)(2,1)S(1)}, bf16[128,3584]{1,0:T(8,128)(2,1)S(1)}, u32[]{:S(2)}, u32[]{:S(2)}) collective-permute-start(bf16[128,3584]{1,0:T(8,128)(2,1)S(1)} %get-tuple-element.89.r1), channel_id=1, source_target_pairs={{0,8},{1,9},{2,10},{3,11},{4,12},{5,13},{6,14},{7,15},{8,0},{9,1},... | collective-permute-start | bytes 2752520 | tf_op jit(solution)/shard_map/ppermute | solution.py:319
  41.5 10.3 %collective-permute-start.18 = (bf16[128,2432]{1,0:T(8,128)(2,1)S(1)}, bf16[128,2432]{1,0:T(8,128)(2,1)S(1)}, u32[]{:S(2)}, u32[]{:S(2)}) collective-permute-start(bf16[128,2432]{1,0:T(8,128)(2,1)S(1)} %get-tuple-element.91), channel_id=1, source_target_pairs={{0,16},{1,17},{2,18},{3,19},{4,20},{5,21},{6,22},{7,23},{8,10},{9,... | collective-permute-start | bytes 1867784 | tf_op jit(solution)/shard_map/ppermute | solution.py:410
  43.0 1.5 %collective-permute-start.17 = (bf16[256,512]{1,0:T(8,128)(2,1)S(1)}, bf16[256,512]{1,0:T(8,128)(2,1)S(1)}, u32[]{:S(2)}, u32[]{:S(2)}) collective-permute-start(bf16[256,512]{1,0:T(8,128)(2,1)S(1)} %get-tuple-element.88), channel_id=1, source_target_pairs={{0,8},{1,9},{2,10},{3,11},{4,12},{5,13},{6,14},{7,15},{8,0},{9,1},... | collective-permute-start | bytes 786440 | tf_op jit(solution)/shard_map/ppermute | solution.py:319
  43.0 9.4 %collective-permute-start.22 = (bf16[128,1152]{1,0:T(8,128)(2,1)S(1)}, bf16[128,1152]{1,0:T(8,128)(2,1)S(1)}, u32[]{:S(2)}, u32[]{:S(2)}) collective-permute-start(bf16[128,1152]{1,0:T(8,128)(2,1)S(1)} %get-tuple-element.95), channel_id=1, source_target_pairs={{0,1},{1,0},{2,3},{3,2},{4,5},{5,4},{6,7},{7,6},{8,9},{9,8},{10,11... | collective-permute-start | bytes 884744 | tf_op jit(solution)/shard_map/ppermute | solution.py:410
  52.5 5.5 %collective-permute-start.23 = (bf16[64,1152]{1,0:T(8,128)(2,1)S(1)}, bf16[64,1152]{1,0:T(8,128)(2,1)S(1)}, u32[]{:S(2)}, u32[]{:S(2)}) collective-permute-start(bf16[64,1152]{1,0:T(8,128)(2,1)S(1)} %add_convert_fusion.2), channel_id=1, source_target_pairs={{0,2},{1,3},{2,0},{3,1},{4,6},{5,7},{6,4},{7,5},{8,10},{9,11},{10,... | collective-permute-start | bytes 442376 | tf_op jit(solution)/shard_map/ppermute | solution.py:410
  53.6 7.0 %collective-permute-start.19 = (bf16[64,2432]{1,0:T(8,128)(2,1)S(1)}, bf16[64,2432]{1,0:T(8,128)(2,1)S(1)}, u32[]{:S(2)}, u32[]{:S(2)}) collective-permute-start(bf16[64,2432]{1,0:T(8,128)(2,1)S(1)} %add_convert_fusion), channel_id=1, source_target_pairs={{0,1},{1,0},{2,3},{3,2},{4,5},{5,4},{6,7},{7,6},{8,24},{9,25},{10,... | collective-permute-start | bytes 933896 | tf_op jit(solution)/shard_map/ppermute | solution.py:410
  58.1 4.4 %collective-permute-start.24 = (bf16[32,1152]{1,0:T(8,128)(2,1)S(1)}, bf16[32,1152]{1,0:T(8,128)(2,1)S(1)}, u32[]{:S(2)}, u32[]{:S(2)}) collective-permute-start(bf16[32,1152]{1,0:T(8,128)(2,1)S(1)} %add_convert_fusion.4), channel_id=1, source_target_pairs={{0,16},{1,17},{2,18},{3,19},{4,20},{5,21},{6,22},{7,23},{8,24},{9,... | collective-permute-start | bytes 221192 | tf_op jit(solution)/shard_map/ppermute | solution.py:410
  60.7 5.5 %collective-permute-start.20 = (bf16[32,2432]{1,0:T(8,128)(2,1)S(1)}, bf16[32,2432]{1,0:T(8,128)(2,1)S(1)}, u32[]{:S(2)}, u32[]{:S(2)}) collective-permute-start(bf16[32,2432]{1,0:T(8,128)(2,1)S(1)} %add_convert_fusion.1), channel_id=1, source_target_pairs={{0,2},{1,3},{2,0},{3,1},{4,6},{5,7},{6,4},{7,5},{8,9},{9,8},{10,11... | collective-permute-start | bytes 466952 | tf_op jit(solution)/shard_map/ppermute | solution.py:410
  62.5 6.5 %collective-permute-start.25 = (bf16[16,1152]{1,0:T(8,128)(2,1)S(1)}, bf16[16,1152]{1,0:T(8,128)(2,1)S(1)}, u32[]{:S(2)}, u32[]{:S(2)}) collective-permute-start(bf16[16,1152]{1,0:T(8,128)(2,1)S(1)} %add_convert_fusion.5), channel_id=1, source_target_pairs={{0,4},{1,5},{2,6},{3,7},{4,0},{5,1},{6,2},{7,3},{8,12},{9,13},{10,... | collective-permute-start | bytes 110600 | tf_op jit(solution)/shard_map/ppermute | solution.py:410
  66.3 6.2 %collective-permute-start.21 = (bf16[16,2432]{1,0:T(8,128)(2,1)S(1)}, bf16[16,2432]{1,0:T(8,128)(2,1)S(1)}, u32[]{:S(2)}, u32[]{:S(2)}) collective-permute-start(bf16[16,2432]{1,0:T(8,128)(2,1)S(1)} %add_convert_fusion.3), channel_id=1, source_target_pairs={{0,4},{1,5},{2,6},{3,7},{4,0},{5,1},{6,2},{7,3},{8,12},{9,13},{10,... | collective-permute-start | bytes 233480 | tf_op jit(solution)/shard_map/ppermute | solution.py:410

commit v13 on v11

--- a/solution.py
+++ b/solution.py
@@ -181,15 +181,15 @@
     return top[0:1], hard, soft, top[3:4], top[4:5], taught0, top[6:7], taught1
 
 
-def merge_kernel(flips, *refs):
+def merge_kernel(n, *refs):
     out_ref = refs[-1]
     for j in range(2):
-        out_ref[j] = jnp.concatenate(merged([ref[j ^ f] for ref, f in zip(refs, flips)]))
-
-
-def merge(parts, flips, held):
-    return pl.pallas_call(
-        lambda *refs: merge_kernel(flips, *refs),
+        out_ref[j] = jnp.concatenate(merged([ref[j] for ref in refs[:n]]))
+
+
+def merge(parts, held):
+    return pl.pallas_call(
+        lambda *refs: merge_kernel(len(parts), *refs),
         out_shape=shape(parts[0].shape, F32),
         in_specs=[VMEM] * (len(parts) + len(held)),
         out_specs=VMEM,
@@ -213,7 +213,7 @@
     logits_refs, (serving_ref, aligned_ref), g_refs = refs[:4], refs[4:6], refs[6:]
     me = at_ref[3]
     per, cols = logits_refs[0].shape
-    stats = [merged([ref[j] for ref in stats_refs]) for j in range(2)]
+    stats = [merged([ref[j ^ (i & 1)] for i, ref in enumerate(stats_refs)]) for j in range(2)]
     lane = lax.broadcasted_iota(jnp.int32, (per, per), 1)
     for j in range(2):
         rows = stats[j][:4] + (serving_ref[me ^ (2 * j)].astype(F32),)
@@ -381,18 +381,15 @@
     served = serving.reshape(groups, 1, per)
     logits = [near_a, near_b, far_a, far_b]
     held = logits + [weight]
-    stats = merge([stats, swap(stats, X), swap(stats, Y), swap(stats, X + Y)], (0, 1, 0, 1), held)
+    mask = W
+    while mask < shards:
+        masks = [mask, 2 * mask, 3 * mask] if 2 * mask < shards else [mask]
+        stats = merge([stats] + [swap(stats, m) for m in masks], held)
+        mask *= 4
     _, taught_x = tie(stats, taught_x)
     taught_far = swap(taught_x, CORE)
     aligned = teacher_rows(who, served, [kept, kept_core, taught_x, taught_far])
-    mask = W
-    while True:
-        masks = [mask, 2 * mask, 3 * mask] if 2 * mask < shards else [mask]
-        parts = [stats] + [swap(stats, m) for m in masks]
-        mask *= 4
-        if mask >= shards:
-            break
-        stats = merge(parts, (0,) * len(parts), held)
+    parts = [stats] + [swap(stats, mask) for mask in (X, Y, X + Y)]
 
     bits = shards.bit_length() - 1
     masks = {0: X}
@@ -412,7 +409,8 @@
     theirs = swap(gother, CORE)
     _, x_sent = tie(gother, x_rows)
     grad_head = head_gradient([hidden, x_rows, core_hidden, swap(x_sent, CORE)], gown, theirs)
-    grad_head, *gots = tie(grad_head, *gots)
+    for p in range(3):
+        grad_head, gots[p] = tie(grad_head, gots[p])
 
     def folded(value, p):
         dims = [2] * (1 + bits)

time: 72.9 us -> 72.9 us (level)
  no operation moved by 1% of the time
where the time goes in v13:
time: 72.9 us; the launch traced here: 72.7 us
  starting transfers between devices  32.1 us (44%)
  waiting for transfers between devices  18.2 us (25%)
  Pallas kernels  15 us (21%)
  local copies, waits for them, and re-layouts  5.35 us (7%)
  other arithmetic  1.2 us (2%)
  between operations  0.84 us (1%)
    ppermute x30, starting transfers between devices, swap(): return lax.ppermute(value, AXES, [(i, i ^ mask) for i in range(count)])  32.1 us
    ppermute x30, waiting for transfers between devices, swap(): return lax.ppermute(value, AXES, [(i, i ^ mask) for i in range(count)])  18.2 us
    pallas_call x1, Pallas kernels, head_gradient(): pl.pallas_call(head_kernel, grid=(depth // tile,), out_shape=shape((depth...  5.23 us
    pallas_call x1, Pallas kernels, back_rows(): pl.pallas_call(lambda *refs: back_kernel(bits, edges, len(stats), *refs),...  4.39 us
    dynamic_slice x2, local copies, waits for them, and re-layouts, cut(): return lax.dynamic_slice(value, indices, sizes)  2.1 us
    unnamed x10, local copies, waits for them, and re-layouts  2.06 us
    pallas_call x1, Pallas kernels, far_logits(): pl.pallas_call(lambda *refs: far_kernel(len(pieces), *refs), out_shape=(s...  1.96 us
    pallas_call x2, Pallas kernels, near_logits(): pl.pallas_call(near_kernel, out_shape=(shape((per, cols), F32), shape((ST...  1.72 us
  transfers between devices with their start and end apart: 30, of which 17 were waited for; matrix products, arithmetic and copies ran while one was open for 3% of the time, Pallas kernels for 15%

profile of v13, /device:TPU:0, one launch (start us, length us, event | category | flops | bytes accessed | tf_op | source)
XLA Modules:
  0.0 72.7 jit_solution(18123179044442753414)
XLA Ops:
  0.6 0.0 copy-start.2
  0.7 0.1 pad_add_fusion.2.at_ref
  0.7 0.1 pad_add_fusion
  0.8 1.1 %constant_dynamic-slice_fusion.1 = bf16[32,3584]{1,0:T(8,128)(2,1)S(1)} fusion(bf16[128,3584]{1,0:T(8,128)(2,1)} %r0.1, u32[]{:T(128)S(6)} %convert_element_type.149), kind=kLoop, calls=%fused_computation.42 | loop fusion | bytes 458756 | tf_op jit(solution)/shard_map/dynamic_slice | solution.py:346
  1.9 0.5 collective-permute-start
  2.4 2.6 %collective-permute-start.2 = (bf16[32,3584]{1,0:T(8,128)(2,1)S(1)}, bf16[32,3584]{1,0:T(8,128)(2,1)S(1)}, u32[]{:S(2)}, u32[]{:S(2)}) collective-permute-start(bf16[32,3584]{1,0:T(8,128)(2,1)S(1)} %constant_dynamic-slice_fusion.1), channel_id=1, source_target_pairs={{0,16},{1,17},{2,18},{3,19},{4,20},{5,21},{6,22},{7,23},{8,24},{9,... | collective-permute-start | bytes 688136 | tf_op jit(solution)/shard_map/ppermute | solution.py:319
  5.0 0.2 collective-permute-start.1
  5.2 1.0 %constant_dynamic-slice_fusion = bf16[32,3584]{1,0:T(8,128)(2,1)S(1)} fusion(bf16[128,3584]{1,0:T(8,128)(2,1)} %r0.1, u32[]{:T(128)S(6)} %convert_element_type.150), kind=kLoop, calls=%fused_computation.41 | loop fusion | bytes 458756 | tf_op jit(solution)/shard_map/dynamic_slice | solution.py:346
  6.2 0.3 collective-permute-start.7
  6.5 1.1 %copy.7 = bf16[128,4,512]{2,0,1:T(8,128)(2,1)S(1)} copy(bf16[128,4,512]{2,1,0:T(4,128)(2,1)} %param.9) | data formatting | bytes 1048576 | tf_op jit(solution)/shard_map/optimization_barrier | solution.py:322
  7.7 0.4 taught_stats.1.refs_9_
  8.1 0.1 collective-permute-start.3
  8.2 2.0 %copy-done = bf16[3584,512]{1,0:T(8,128)(2,1)S(1)} copy-done((bf16[3584,512]{1,0:T(8,128)(2,1)S(1)}, bf16[3584,512]{1,0:T(8,128)(2,1)}, u32[]{:S(2)}) %copy-start) | copy-done | bytes 3670040
  10.2 0.9 %near_logits.2 = (f32[128,512]{1,0:T(8,128)S(1)}, f32[8,128]{1,0:T(8,128)S(1)}) custom-call(bf16[128,3584]{1,0:T(8,128)(2,1)S(1)} %copy-done.2, bf16[3584,512]{1,0:T(8,128)(2,1)S(1)} %copy-done), custom_call_target="tpu_custom_call" | custom-call | flops 469762048 | bytes 4587520 | tf_op jit(solution)/shard_map/near_logits/pallas_call | solution.py:108
  11.1 0.4 collective-permute-done.2.refs_0_.refs_1_
  11.5 2.0 %collective-permute-start.6 = (bf16[32,3584]{1,0:T(8,128)(2,1)S(1)}, bf16[32,3584]{1,0:T(8,128)(2,1)S(1)}, u32[]{:S(2)}, u32[]{:S(2)}) collective-permute-start(bf16[32,3584]{1,0:T(8,128)(2,1)S(1)} %collective-permute-done.2.refs_0_.refs_1_), channel_id=1, source_target_pairs={{0,2},{1,3},{2,0},{3,1},{4,6},{5,7},{6,4},{7,5},{8,10},{9,11},{10,... | collective-permute-start | bytes 688136 | tf_op jit(solution)/shard_map/ppermute | solution.py:319
  13.5 1.5 %collective-permute-start.5 = (bf16[32,3584]{1,0:T(8,128)(2,1)S(1)}, bf16[32,3584]{1,0:T(8,128)(2,1)S(1)}, u32[]{:S(2)}, u32[]{:S(2)}) collective-permute-start(bf16[32,3584]{1,0:T(8,128)(2,1)S(1)} %collective-permute-done.2.refs_0_.refs_1_), channel_id=1, source_target_pairs={{0,1},{1,0},{2,3},{3,2},{4,5},{5,4},{6,7},{7,6},{8,9},{9,8},{10,11... | collective-permute-start | bytes 688136 | tf_op jit(solution)/shard_map/ppermute | solution.py:319
  15.0 0.0 collective-permute-start.4
  15.0 0.9 %near_logits.3 = (f32[128,512]{1,0:T(8,128)S(1)}, f32[8,128]{1,0:T(8,128)S(1)}) custom-call(bf16[128,3584]{1,0:T(8,128)(2,1)S(1)} %copy-done.2, bf16[3584,512]{1,0:T(8,128)(2,1)S(1)} %collective-permute-done.w_ref.refs_6_.refs_2_, bf16[32,3584]{1,0:T(8,128)(2,1)S(1)} %collective-permute-done.2.refs_0_.refs_1_), custom_call_target="tpu_custom_call" | custom-call | flops 469762048 | bytes 4587520 | tf_op jit(solution)/shard_map/near_logits/pallas_call | solution.py:108
  15.9 0.3 collective-permute-done.7.refs_4_
  16.1 3.1 %collective-permute-done.6.refs_3_ = bf16[32,3584]{1,0:T(8,128)(2,1)S(1)} collective-permute-done((bf16[32,3584]{1,0:T(8,128)(2,1)S(1)}, bf16[32,3584]{1,0:T(8,128)(2,1)S(1)}, u32[]{:S(2)}, u32[]{:S(2)}) %collective-permute-start.6) | collective-permute-done | bytes 229408 | tf_op jit(solution)/shard_map/ppermute | solution.py:319
  19.2 1.5 %collective-permute-done.5.refs_2_ = bf16[32,3584]{1,0:T(8,128)(2,1)S(1)} collective-permute-done((bf16[32,3584]{1,0:T(8,128)(2,1)S(1)}, bf16[32,3584]{1,0:T(8,128)(2,1)S(1)}, u32[]{:S(2)}, u32[]{:S(2)}) %collective-permute-start.5) | collective-permute-done | bytes 229408 | tf_op jit(solution)/shard_map/ppermute | solution.py:319
  20.7 1.5 %collective-permute-start.14 = (bf16[2,128,512]{2,1,0:T(8,128)(2,1)S(1)}, bf16[2,128,512]{2,1,0:T(8,128)(2,1)S(1)}, u32[]{:S(2)}, u32[]{:S(2)}) collective-permute-start(bf16[2,128,512]{2,1,0:T(8,128)(2,1)S(1)} %get-tuple-element.87.gone_ref), channel_id=1, source_target_pairs={{0,16},{1,17},{2,18},{3,19},{4,20},{5,21},{6,22},{7,23},{8,24},{9,... | collective-permute-start | bytes 786440 | tf_op jit(solution)/shard_map/ppermute | solution.py:319
  22.2 0.0 collective-permute-done.4.a1
  22.2 2.0 %far_logits.1 = (f32[128,512]{1,0:T(8,128)S(1)}, f32[128,512]{1,0:T(8,128)S(1)}, bf16[128,3584]{1,0:T(8,128)(2,1)S(1)}, f32[2,8,128]{2,1,0:T(8,128)S(1)}) custom-call(s32[4]{0:T(128)S(1)} %get-tuple-element.66.refs_0_, bf16[32,3584]{1,0:T(8,128)(2,1)S(1)} %collective-permute-done.2.refs_0_.refs_1_, bf16[32,3584]{1,0:T(8,128)(2,1)S(1)} %collective-permute-done.5.refs_2_, ...), custom_call_target="tpu_custom_call" | custom-call | flops 939524096 | bytes 8257536 | tf_op jit(solution)/shard_map/far_logits/pallas_call | solution.py:153
  24.2 0.0 copy-start.3
  24.2 2.5 %collective-permute-start.10 = (f32[2,8,128]{2,1,0:T(8,128)S(1)}, f32[2,8,128]{2,1,0:T(8,128)S(1)}, u32[]{:S(2)}, u32[]{:S(2)}) collective-permute-start(f32[2,8,128]{2,1,0:T(8,128)S(1)} %get-tuple-element.80.refs_0_), channel_id=1, source_target_pairs={{0,6},{1,7},{2,4},{3,5},{4,2},{5,3},{6,0},{7,1},{8,14},{9,15},{10,... | collective-permute-start | bytes 24584 | tf_op jit(solution)/shard_map/ppermute | solution.py:319
  26.7 0.2 collective-permute-start.9
  26.9 1.7 %collective-permute-start.8 = (f32[2,8,128]{2,1,0:T(8,128)S(1)}, f32[2,8,128]{2,1,0:T(8,128)S(1)}, u32[]{:S(2)}, u32[]{:S(2)}) collective-permute-start(f32[2,8,128]{2,1,0:T(8,128)S(1)} %get-tuple-element.80.refs_0_), channel_id=1, source_target_pairs={{0,2},{1,3},{2,0},{3,1},{4,6},{5,7},{6,4},{7,5},{8,10},{9,11},{10,... | collective-permute-start | bytes 24584 | tf_op jit(solution)/shard_map/ppermute | solution.py:319
  28.6 1.1 %collective-permute-done.10.refs_3_ = f32[2,8,128]{2,1,0:T(8,128)S(1)} collective-permute-done((f32[2,8,128]{2,1,0:T(8,128)S(1)}, f32[2,8,128]{2,1,0:T(8,128)S(1)}, u32[]{:S(2)}, u32[]{:S(2)}) %collective-permute-start.10) | collective-permute-done | bytes 8224 | tf_op jit(solution)/shard_map/ppermute | solution.py:319
  29.7 1.6 %collective-permute-done.9.refs_2_ = f32[2,8,128]{2,1,0:T(8,128)S(1)} collective-permute-done((f32[2,8,128]{2,1,0:T(8,128)S(1)}, f32[2,8,128]{2,1,0:T(8,128)S(1)}, u32[]{:S(2)}, u32[]{:S(2)}) %collective-permute-start.9) | collective-permute-done | bytes 8224 | tf_op jit(solution)/shard_map/ppermute | solution.py:319
  31.3 0.1 collective-permute-start.15
  31.4 1.6 %collective-permute-start.13 = (f32[2,8,128]{2,1,0:T(8,128)S(1)}, f32[2,8,128]{2,1,0:T(8,128)S(1)}, u32[]{:S(2)}, u32[]{:S(2)}) collective-permute-start(f32[2,8,128]{2,1,0:T(8,128)S(1)} %merge_stats.1.refs_3_), channel_id=1, source_target_pairs={{0,17},{1,16},{2,19},{3,18},{4,21},{5,20},{6,23},{7,22},{8,25},{9,... | collective-permute-start | bytes 24584 | tf_op jit(solution)/shard_map/ppermute | solution.py:319
  32.9 0.5 collective-permute-start.12
  33.4 1.5 %collective-permute-start.11 = (f32[2,8,128]{2,1,0:T(8,128)S(1)}, f32[2,8,128]{2,1,0:T(8,128)S(1)}, u32[]{:S(2)}, u32[]{:S(2)}) collective-permute-start(f32[2,8,128]{2,1,0:T(8,128)S(1)} %merge_stats.1.refs_3_), channel_id=1, source_target_pairs={{0,16},{1,17},{2,18},{3,19},{4,20},{5,21},{6,22},{7,23},{8,24},{9,... | collective-permute-start | bytes 24584 | tf_op jit(solution)/shard_map/ppermute | solution.py:319
  34.9 1.3 %teacher_rows.1.refs_12_ = bf16[2,128,1024]{2,1,0:T(8,128)(2,1)S(1)} custom-call(s32[2]{0:T(128)S(1)} %pad_add_fusion.2.at_ref, s32[4,1,128]{2,1,0:T(1,128)S(1)} %bitcast.42, bf16[2,128,512]{2,1,0:T(8,128)(2,1)S(1)} %get-tuple-element.65.kept_ref.a0, bf16[2,128,512]{2,1,0:T(8,128)(2,1)S(1)} %collective-permute-done.4.a1, ...), custom_call_target="tpu_custom_call" | custom-call | flops 268435456 | bytes 1572864 | tf_op jit(solution)/shard_map/teacher_rows/pallas_call | solution.py:80
  36.2 0.4 collective-permute-done.12.refs_5_
  36.6 0.5 collective-permute-done.11.refs_4_
  37.1 4.4 %back_rows.1 = (bf16[256,512]{1,0:T(8,128)(2,1)S(1)}, bf16[256,512]{1,0:T(8,128)(2,1)S(1)}, bf16[128,1152]{1,0:T(8,128)(2,1)S(1)}, bf16[128,1152]{1,0:T(8,128)(2...) custom-call(s32[4]{0:T(128)S(1)} %get-tuple-element.54.refs_0_, ...), custom_call_target="tpu_custom_call" | custom-call | flops 1879048192 | bytes 7340032 | tf_op jit(solution)/shard_map/back_rows/pallas_call | solution.py:266
  41.5 0.1 collective-permute-start.16
  41.5 0.5 collective-permute-start.17
  42.0 1.0 %collective-permute-start.26 = (bf16[128,1280]{1,0:T(8,128)(2,1)S(1)}, bf16[128,1280]{1,0:T(8,128)(2,1)S(1)}, u32[]{:S(2)}, u32[]{:S(2)}) collective-permute-start(bf16[128,1280]{1,0:T(8,128)(2,1)S(1)} %get-tuple-element.103), channel_id=1, source_target_pairs={{0,2},{1,3},{2,0},{3,1},{4,6},{5,7},{6,4},{7,5},{8,10},{9,11},{10,... | collective-permute-start | bytes 983048 | tf_op jit(solution)/shard_map/ppermute | solution.py:319
  43.1 1.5 %collective-permute-start.18 = (bf16[128,1152]{1,0:T(8,128)(2,1)S(1)}, bf16[128,1152]{1,0:T(8,128)(2,1)S(1)}, u32[]{:S(2)}, u32[]{:S(2)}) collective-permute-start(bf16[128,1152]{1,0:T(8,128)(2,1)S(1)} %get-tuple-element.95), channel_id=1, source_target_pairs={{0,16},{1,17},{2,18},{3,19},{4,20},{5,21},{6,22},{7,23},{8,24},{9,... | collective-permute-start | bytes 884744 | tf_op jit(solution)/shard_map/ppermute | solution.py:319
  44.6 1.5 %collective-permute-start.22 = (bf16[128,1152]{1,0:T(8,128)(2,1)S(1)}, bf16[128,1152]{1,0:T(8,128)(2,1)S(1)}, u32[]{:S(2)}, u32[]{:S(2)}) collective-permute-start(bf16[128,1152]{1,0:T(8,128)(2,1)S(1)} %get-tuple-element.99), channel_id=1, source_target_pairs={{0,1},{1,0},{2,3},{3,2},{4,5},{5,4},{6,7},{7,6},{8,9},{9,8},{10,11... | collective-permute-start | bytes 884744 | tf_op jit(solution)/shard_map/ppermute | solution.py:319
  46.1 5.2 %head_gradient.1 = bf16[3584,512]{1,0:T(8,128)(2,1)} custom-call(bf16[128,3584]{1,0:T(8,128)(2,1)S(1)} %copy-done.2, bf16[128,3584]{1,0:T(8,128)(2,1)S(1)} %get-tuple-element.93.r1, bf16[128,3584]{1,0:T(8,128)(2,1)S(1)} %collective-permute-done.1.r2, bf16[128,3584]{1,0:T(8,128)(2,1)S(1)} %collective-permute-done.16.r3, ...), custom_call_target="tpu_custom_call" | custom-call | flops 1879048192 | bytes 7340032 | tf_op jit(solution)/shard_map/head_gradient/pallas_call | solution.py:294
  51.3 0.5 collective-permute-done.18
  51.8 1.2 %collective-permute-done.22 = bf16[128,1152]{1,0:T(8,128)(2,1)S(1)} collective-permute-done((bf16[128,1152]{1,0:T(8,128)(2,1)S(1)}, bf16[128,1152]{1,0:T(8,128)(2,1)S(1)}, u32[]{:S(2)}, u32[]{:S(2)}) %collective-permute-start.22) | collective-permute-done | bytes 294944 | tf_op jit(solution)/shard_map/ppermute | solution.py:319
  53.0 1.6 %collective-permute-start.19 = (bf16[1,2,2,1,16,1152]{5,4,3,2,1,0:T(8,128)(2,1)S(1)}, bf16[1,2,2,1,16,1152]{5,4,3,2,1,0:T(8,128)(2,1)S(1)}, u32[]{:S(2)}, u32[]{:S(2)}) collective-permute-start(bf16[1,2,2,1,16,1152]{5,4,3,2,1,0:T(8,128)(2,1)S(1)} %fusion.1), channel_id=1, source_target_pairs={{0,1},{1,0},{2,3},{3,2},{4,5},{5,4},{6,7},{7,6},{8,9},{9,8},{10,11... | collective-permute-start | bytes 442376 | tf_op jit(solution)/shard_map/ppermute | solution.py:319
  54.7 1.1 %collective-permute-start.23 = (bf16[2,2,1,1,16,1152]{5,4,3,2,1,0:T(8,128)(2,1)S(1)}, bf16[2,2,1,1,16,1152]{5,4,3,2,1,0:T(8,128)(2,1)S(1)}, u32[]{:S(2)}, u32[]{:S(2)}) collective-permute-start(bf16[2,2,1,1,16,1152]{5,4,3,2,1,0:T(8,128)(2,1)S(1)} %fusion), channel_id=1, source_target_pairs={{0,2},{1,3},{2,0},{3,1},{4,6},{5,7},{6,4},{7,5},{8,10},{9,11},{10,... | collective-permute-start | bytes 442376 | tf_op jit(solution)/shard_map/ppermute | solution.py:319
  55.8 0.5 collective-permute-start.27
  56.3 1.9 %collective-permute-done.19 = bf16[1,2,2,1,16,1152]{5,4,3,2,1,0:T(8,128)(2,1)S(1)} collective-permute-done((bf16[1,2,2,1,16,1152]{5,4,3,2,1,0:T(8,128)(2,1)S(1)}, bf16[1,2,2,1,16,1152]{5,4,3,2,1,0:T(8,128)(2,1)S(1)}, u32[]{:S(2)}, u32[]{:S(2)}) %collective-permute-start.19) | collective-permute-done | bytes 147488 | tf_op jit(solution)/shard_map/ppermute | solution.py:319
  58.3 1.1 %collective-permute-start.20 = (bf16[1,2,1,1,16,1152]{5,4,3,2,1,0:T(8,128)(2,1)S(1)}, bf16[1,2,1,1,16,1152]{5,4,3,2,1,0:T(8,128)(2,1)S(1)}, u32[]{:S(2)}, u32[]{:S(2)}) collective-permute-start(bf16[1,2,1,1,16,1152]{5,4,3,2,1,0:T(8,128)(2,1)S(1)} %fusion.7), channel_id=1, source_target_pairs={{0,2},{1,3},{2,0},{3,1},{4,6},{5,7},{6,4},{7,5},{8,10},{9,11},{10,... | collective-permute-start | bytes 221192 | tf_op jit(solution)/shard_map/ppermute | solution.py:319
  59.3 1.4 %collective-permute-done.23 = bf16[2,2,1,1,16,1152]{5,4,3,2,1,0:T(8,128)(2,1)S(1)} collective-permute-done((bf16[2,2,1,1,16,1152]{5,4,3,2,1,0:T(8,128)(2,1)S(1)}, bf16[2,2,1,1,16,1152]{5,4,3,2,1,0:T(8,128)(2,1)S(1)}, u32[]{:S(2)}, u32[]{:S(2)}) %collective-permute-start.23) | collective-permute-done | bytes 147488 | tf_op jit(solution)/shard_map/ppermute | solution.py:319
  60.7 0.6 collective-permute-start.24
  61.3 0.6 collective-permute-done.27
  62.0 0.6 collective-permute-start.28
  62.5 0.2 collective-permute-done.20
  62.7 1.9 %collective-permute-start.21 = (bf16[1,1,1,1,16,1152]{5,4,3,2,1,0:T(8,128)(2,1)S(1)}, bf16[1,1,1,1,16,1152]{5,4,3,2,1,0:T(8,128)(2,1)S(1)}, u32[]{:S(2)}, u32[]{:S(2)}) collective-permute-start(bf16[1,1,1,1,16,1152]{5,4,3,2,1,0:T(8,128)(2,1)S(1)} %fusion.22), channel_id=1, source_target_pairs={{0,4},{1,5},{2,6},{3,7},{4,0},{5,1},{6,2},{7,3},{8,12},{9,13},{10,... | collective-permute-start | bytes 110600 | tf_op jit(solution)/shard_map/ppermute | solution.py:319
  64.6 0.5 collective-permute-done.24
  65.2 1.8 %collective-permute-start.25 = (bf16[1,1,1,1,16,1152]{5,4,3,2,1,0:T(8,128)(2,1)S(1)}, bf16[1,1,1,1,16,1152]{5,4,3,2,1,0:T(8,128)(2,1)S(1)}, u32[]{:S(2)}, u32[]{:S(2)}) collective-permute-start(bf16[1,1,1,1,16,1152]{5,4,3,2,1,0:T(8,128)(2,1)S(1)} %fusion.16), channel_id=1, source_target_pairs={{0,4},{1,5},{2,6},{3,7},{4,0},{5,1},{6,2},{7,3},{8,12},{9,13},{10,... | collective-permute-start | bytes 110600 | tf_op jit(solution)/shard_map/ppermute | solution.py:319
  67.0 1.6 %collective-permute-start.29 = (bf16[1,1,1,1,16,1280]{5,4,3,2,1,0:T(8,128)(2,1)S(1)}, bf16[1,1,1,1,16,1280]{5,4,3,2,1,0:T(8,128)(2,1)S(1)}, u32[]{:S(2)}, u32[]{:S(2)}) collective-permute-start(bf16[1,1,1,1,16,1280]{5,4,3,2,1,0:T(8,128)(2,1)S(1)} %fusion.10), channel_id=1, source_target_pairs={{0,4},{1,5},{2,6},{3,7},{4,0},{5,1},{6,2},{7,3},{8,12},{9,13},{10,... | collective-permute-start | bytes 122888 | tf_op jit(solution)/shard_map/ppermute | solution.py:319
  68.6 1.5 %collective-permute-done.25 = bf16[1,1,1,1,16,1152]{5,4,3,2,1,0:T(8,128)(2,1)S(1)} collective-permute-done((bf16[1,1,1,1,16,1152]{5,4,3,2,1,0:T(8,128)(2,1)S(1)}, bf16[1,1,1,1,16,1152]{5,4,3,2,1,0:T(8,128)(2,1)S(1)}, u32[]{:S(2)}, u32[]{:S(2)}) %collective-permute-start.25) | collective-permute-done | bytes 36896 | tf_op jit(solution)/shard_map/ppermute | solution.py:319
  70.1 1.8 %collective-permute-done.29 = bf16[1,1,1,1,16,1280]{5,4,3,2,1,0:T(8,128)(2,1)S(1)} collective-permute-done((bf16[1,1,1,1,16,1280]{5,4,3,2,1,0:T(8,128)(2,1)S(1)}, bf16[1,1,1,1,16,1280]{5,4,3,2,1,0:T(8,128)(2,1)S(1)}, u32[]{:S(2)}, u32[]{:S(2)}) %collective-permute-start.29) | collective-permute-done | bytes 40992 | tf_op jit(solution)/shard_map/ppermute | solution.py:319
  72.0 0.7 maximum_bitcast_fusion
  (34 shorter events, 0.5 us)
Async XLA Ops:
  0.6 7.6 %copy-start.2 = (bf16[128,3584]{1,0:T(8,128)(2,1)S(1)}, bf16[128,3584]{1,0:T(8,128)(2,1)}, u32[]{:S(2)}) copy-start(bf16[128,3584]{1,0:T(8,128)(2,1)} %r0.1) | copy-start | bytes 2752516
  1.9 13.1 %collective-permute-start = (bf16[3584,512]{1,0:T(8,128)(2,1)}, bf16[3584,512]{1,0:T(8,128)(2,1)S(1)}, u32[]{:S(2)}, u32[]{:S(2)}) collective-permute-start(bf16[3584,512]{1,0:T(8,128)(2,1)} %refs_1_), channel_id=1, source_target_pairs={{0,8},{1,9},{2,10},{3,11},{4,12},{5,13},{6,14},{7,15},{8,0},{9,1},... | collective-permute-start | bytes 11010056 | tf_op jit(solution)/shard_map/ppermute | solution.py:319
  2.4 9.0 %collective-permute-start.2 = (bf16[32,3584]{1,0:T(8,128)(2,1)S(1)}, bf16[32,3584]{1,0:T(8,128)(2,1)S(1)}, u32[]{:S(2)}, u32[]{:S(2)}) collective-permute-start(bf16[32,3584]{1,0:T(8,128)(2,1)S(1)} %constant_dynamic-slice_fusion.1), channel_id=1, source_target_pairs={{0,16},{1,17},{2,18},{3,19},{4,20},{5,21},{6,22},{7,23},{8,24},{9,... | collective-permute-start | bytes 688136 | tf_op jit(solution)/shard_map/ppermute | solution.py:319
  5.0 17.2 %collective-permute-start.1 = (bf16[128,3584]{1,0:T(8,128)(2,1)}, bf16[128,3584]{1,0:T(8,128)(2,1)S(1)}, u32[]{:S(2)}, u32[]{:S(2)}) collective-permute-start(bf16[128,3584]{1,0:T(8,128)(2,1)} %r0.1), channel_id=1, source_target_pairs={{0,8},{1,9},{2,10},{3,11},{4,12},{5,13},{6,14},{7,15},{8,0},{9,1},... | collective-permute-start | bytes 2752520 | tf_op jit(solution)/shard_map/ppermute | solution.py:319
  6.2 9.9 %collective-permute-start.7 = (bf16[32,3584]{1,0:T(8,128)(2,1)S(1)}, bf16[32,3584]{1,0:T(8,128)(2,1)S(1)}, u32[]{:S(2)}, u32[]{:S(2)}) collective-permute-start(bf16[32,3584]{1,0:T(8,128)(2,1)S(1)} %constant_dynamic-slice_fusion), channel_id=1, source_target_pairs={{0,16},{1,17},{2,18},{3,19},{4,20},{5,21},{6,22},{7,23},{8,24},{9,... | collective-permute-start | bytes 688136 | tf_op jit(solution)/shard_map/ppermute | solution.py:319
  8.1 3.0 %collective-permute-start.3 = (f32[8,128]{1,0:T(8,128)S(1)}, f32[8,128]{1,0:T(8,128)S(1)}, u32[]{:S(2)}, u32[]{:S(2)}) collective-permute-start(f32[8,128]{1,0:T(8,128)S(1)} %taught_stats.1.refs_9_), channel_id=1, source_target_pairs={{0,8},{1,9},{2,10},{3,11},{4,12},{5,13},{6,14},{7,15},{8,0},{9,1},... | collective-permute-start | bytes 12296 | tf_op jit(solution)/shard_map/ppermute | solution.py:319
  8.2 2.0 %copy-start = (bf16[3584,512]{1,0:T(8,128)(2,1)S(1)}, bf16[3584,512]{1,0:T(8,128)(2,1)}, u32[]{:S(2)}) copy-start(bf16[3584,512]{1,0:T(8,128)(2,1)} %refs_1_) | copy-start | bytes 11010052
  10.2 11.9 %copy-start.1 = (bf16[3584,512]{1,0:T(8,128)(2,1)S(1)}, bf16[3584,512]{1,0:T(8,128)(2,1)}, u32[]{:S(2)}) copy-start(bf16[3584,512]{1,0:T(8,128)(2,1)} %refs_1_) | copy-start | bytes 11010052
  10.2 11.9 %copy-start.4 = (s32[128]{0:T(128)S(1)}, s32[128]{0:T(128)}, u32[]{:S(2)}) copy-start(s32[128]{0:T(128)} %param.6) | copy-start | bytes 1540
  11.5 7.7 %collective-permute-start.6 = (bf16[32,3584]{1,0:T(8,128)(2,1)S(1)}, bf16[32,3584]{1,0:T(8,128)(2,1)S(1)}, u32[]{:S(2)}, u32[]{:S(2)}) collective-permute-start(bf16[32,3584]{1,0:T(8,128)(2,1)S(1)} %collective-permute-done.2.refs_0_.refs_1_), channel_id=1, source_target_pairs={{0,2},{1,3},{2,0},{3,1},{4,6},{5,7},{6,4},{7,5},{8,10},{9,11},{10,... | collective-permute-start | bytes 688136 | tf_op jit(solution)/shard_map/ppermute | solution.py:319
  13.5 7.2 %collective-permute-start.5 = (bf16[32,3584]{1,0:T(8,128)(2,1)S(1)}, bf16[32,3584]{1,0:T(8,128)(2,1)S(1)}, u32[]{:S(2)}, u32[]{:S(2)}) collective-permute-start(bf16[32,3584]{1,0:T(8,128)(2,1)S(1)} %collective-permute-done.2.refs_0_.refs_1_), channel_id=1, source_target_pairs={{0,1},{1,0},{2,3},{3,2},{4,5},{5,4},{6,7},{7,6},{8,9},{9,8},{10,11... | collective-permute-start | bytes 688136 | tf_op jit(solution)/shard_map/ppermute | solution.py:319
  15.0 7.2 %collective-permute-start.4 = (bf16[2,128,512]{2,1,0:T(8,128)(2,1)S(1)}, bf16[2,128,512]{2,1,0:T(8,128)(2,1)S(1)}, u32[]{:S(2)}, u32[]{:S(2)}) collective-permute-start(bf16[2,128,512]{2,1,0:T(8,128)(2,1)S(1)} %get-tuple-element.65.kept_ref.a0), channel_id=1, source_target_pairs={{0,8},{1,9},{2,10},{3,11},{4,12},{5,13},{6,14},{7,15},{8,0},{9,1},... | collective-permute-start | bytes 786440 | tf_op jit(solution)/shard_map/ppermute | solution.py:319
  20.7 10.6 %collective-permute-start.14 = (bf16[2,128,512]{2,1,0:T(8,128)(2,1)S(1)}, bf16[2,128,512]{2,1,0:T(8,128)(2,1)S(1)}, u32[]{:S(2)}, u32[]{:S(2)}) collective-permute-start(bf16[2,128,512]{2,1,0:T(8,128)(2,1)S(1)} %get-tuple-element.87.gone_ref), channel_id=1, source_target_pairs={{0,16},{1,17},{2,18},{3,19},{4,20},{5,21},{6,22},{7,23},{8,24},{9,... | collective-permute-start | bytes 786440 | tf_op jit(solution)/shard_map/ppermute | solution.py:319
  24.2 10.8 %copy-start.3 = (s32[512]{0:T(512)S(1)}, s32[512]{0:T(512)}, u32[]{:S(2)}) copy-start(s32[512]{0:T(512)} %param.7) | copy-start | bytes 6148
  24.2 5.5 %collective-permute-start.10 = (f32[2,8,128]{2,1,0:T(8,128)S(1)}, f32[2,8,128]{2,1,0:T(8,128)S(1)}, u32[]{:S(2)}, u32[]{:S(2)}) collective-permute-start(f32[2,8,128]{2,1,0:T(8,128)S(1)} %get-tuple-element.80.refs_0_), channel_id=1, source_target_pairs={{0,6},{1,7},{2,4},{3,5},{4,2},{5,3},{6,0},{7,1},{8,14},{9,15},{10,... | collective-permute-start | bytes 24584 | tf_op jit(solution)/shard_map/ppermute | solution.py:319
  26.7 4.5 %collective-permute-start.9 = (f32[2,8,128]{2,1,0:T(8,128)S(1)}, f32[2,8,128]{2,1,0:T(8,128)S(1)}, u32[]{:S(2)}, u32[]{:S(2)}) collective-permute-start(f32[2,8,128]{2,1,0:T(8,128)S(1)} %get-tuple-element.80.refs_0_), channel_id=1, source_target_pairs={{0,4},{1,5},{2,6},{3,7},{4,0},{5,1},{6,2},{7,3},{8,12},{9,13},{10,... | collective-permute-start | bytes 24584 | tf_op jit(solution)/shard_map/ppermute | solution.py:319
  26.9 4.3 %collective-permute-start.8 = (f32[2,8,128]{2,1,0:T(8,128)S(1)}, f32[2,8,128]{2,1,0:T(8,128)S(1)}, u32[]{:S(2)}, u32[]{:S(2)}) collective-permute-start(f32[2,8,128]{2,1,0:T(8,128)S(1)} %get-tuple-element.80.refs_0_), channel_id=1, source_target_pairs={{0,2},{1,3},{2,0},{3,1},{4,6},{5,7},{6,4},{7,5},{8,10},{9,11},{10,... | collective-permute-start | bytes 24584 | tf_op jit(solution)/shard_map/ppermute | solution.py:319
  31.3 3.6 %collective-permute-start.15 = (bf16[2,128,512]{2,1,0:T(8,128)(2,1)S(1)}, bf16[2,128,512]{2,1,0:T(8,128)(2,1)S(1)}, u32[]{:S(2)}, u32[]{:S(2)}) collective-permute-start(bf16[2,128,512]{2,1,0:T(8,128)(2,1)S(1)} %collective-permute-done.14.a2), channel_id=1, source_target_pairs={{0,8},{1,9},{2,10},{3,11},{4,12},{5,13},{6,14},{7,15},{8,0},{9,1},... | collective-permute-start | bytes 786440 | tf_op jit(solution)/shard_map/ppermute | solution.py:319
  31.4 4.8 %collective-permute-start.13 = (f32[2,8,128]{2,1,0:T(8,128)S(1)}, f32[2,8,128]{2,1,0:T(8,128)S(1)}, u32[]{:S(2)}, u32[]{:S(2)}) collective-permute-start(f32[2,8,128]{2,1,0:T(8,128)S(1)} %merge_stats.1.refs_3_), channel_id=1, source_target_pairs={{0,17},{1,16},{2,19},{3,18},{4,21},{5,20},{6,23},{7,22},{8,25},{9,... | collective-permute-start | bytes 24584 | tf_op jit(solution)/shard_map/ppermute | solution.py:319
  32.9 3.7 %collective-permute-start.12 = (f32[2,8,128]{2,1,0:T(8,128)S(1)}, f32[2,8,128]{2,1,0:T(8,128)S(1)}, u32[]{:S(2)}, u32[]{:S(2)}) collective-permute-start(f32[2,8,128]{2,1,0:T(8,128)S(1)} %merge_stats.1.refs_3_), channel_id=1, source_target_pairs={{0,1},{1,0},{2,3},{3,2},{4,5},{5,4},{6,7},{7,6},{8,9},{9,8},{10,11... | collective-permute-start | bytes 24584 | tf_op jit(solution)/shard_map/ppermute | solution.py:319
  33.4 3.7 %collective-permute-start.11 = (f32[2,8,128]{2,1,0:T(8,128)S(1)}, f32[2,8,128]{2,1,0:T(8,128)S(1)}, u32[]{:S(2)}, u32[]{:S(2)}) collective-permute-start(f32[2,8,128]{2,1,0:T(8,128)S(1)} %merge_stats.1.refs_3_), channel_id=1, source_target_pairs={{0,16},{1,17},{2,18},{3,19},{4,20},{5,21},{6,22},{7,23},{8,24},{9,... | collective-permute-start | bytes 24584 | tf_op jit(solution)/shard_map/ppermute | solution.py:319
  41.5 4.6 %collective-permute-start.16 = (bf16[128,3584]{1,0:T(8,128)(2,1)S(1)}, bf16[128,3584]{1,0:T(8,128)(2,1)S(1)}, u32[]{:S(2)}, u32[]{:S(2)}) collective-permute-start(bf16[128,3584]{1,0:T(8,128)(2,1)S(1)} %get-tuple-element.93.r1), channel_id=1, source_target_pairs={{0,8},{1,9},{2,10},{3,11},{4,12},{5,13},{6,14},{7,15},{8,0},{9,1},... | collective-permute-start | bytes 2752520 | tf_op jit(solution)/shard_map/ppermute | solution.py:319
  41.5 4.5 %collective-permute-start.17 = (bf16[256,512]{1,0:T(8,128)(2,1)S(1)}, bf16[256,512]{1,0:T(8,128)(2,1)S(1)}, u32[]{:S(2)}, u32[]{:S(2)}) collective-permute-start(bf16[256,512]{1,0:T(8,128)(2,1)S(1)} %get-tuple-element.92), channel_id=1, source_target_pairs={{0,8},{1,9},{2,10},{3,11},{4,12},{5,13},{6,14},{7,15},{8,0},{9,1},... | collective-permute-start | bytes 786440 | tf_op jit(solution)/shard_map/ppermute | solution.py:319
  42.0 11.0 %collective-permute-start.26 = (bf16[128,1280]{1,0:T(8,128)(2,1)S(1)}, bf16[128,1280]{1,0:T(8,128)(2,1)S(1)}, u32[]{:S(2)}, u32[]{:S(2)}) collective-permute-start(bf16[128,1280]{1,0:T(8,128)(2,1)S(1)} %get-tuple-element.103), channel_id=1, source_target_pairs={{0,2},{1,3},{2,0},{3,1},{4,6},{5,7},{6,4},{7,5},{8,10},{9,11},{10,... | collective-permute-start | bytes 983048 | tf_op jit(solution)/shard_map/ppermute | solution.py:319
  43.1 8.7 %collective-permute-start.18 = (bf16[128,1152]{1,0:T(8,128)(2,1)S(1)}, bf16[128,1152]{1,0:T(8,128)(2,1)S(1)}, u32[]{:S(2)}, u32[]{:S(2)}) collective-permute-start(bf16[128,1152]{1,0:T(8,128)(2,1)S(1)} %get-tuple-element.95), channel_id=1, source_target_pairs={{0,16},{1,17},{2,18},{3,19},{4,20},{5,21},{6,22},{7,23},{8,24},{9,... | collective-permute-start | bytes 884744 | tf_op jit(solution)/shard_map/ppermute | solution.py:319
  44.6 8.4 %collective-permute-start.22 = (bf16[128,1152]{1,0:T(8,128)(2,1)S(1)}, bf16[128,1152]{1,0:T(8,128)(2,1)S(1)}, u32[]{:S(2)}, u32[]{:S(2)}) collective-permute-start(bf16[128,1152]{1,0:T(8,128)(2,1)S(1)} %get-tuple-element.99), channel_id=1, source_target_pairs={{0,1},{1,0},{2,3},{3,2},{4,5},{5,4},{6,7},{7,6},{8,9},{9,8},{10,11... | collective-permute-start | bytes 884744 | tf_op jit(solution)/shard_map/ppermute | solution.py:319
  53.0 5.2 %collective-permute-start.19 = (bf16[1,2,2,1,16,1152]{5,4,3,2,1,0:T(8,128)(2,1)S(1)}, bf16[1,2,2,1,16,1152]{5,4,3,2,1,0:T(8,128)(2,1)S(1)}, u32[]{:S(2)}, u32[]{:S(2)}) collective-permute-start(bf16[1,2,2,1,16,1152]{5,4,3,2,1,0:T(8,128)(2,1)S(1)} %fusion.1), channel_id=1, source_target_pairs={{0,1},{1,0},{2,3},{3,2},{4,5},{5,4},{6,7},{7,6},{8,9},{9,8},{10,11... | collective-permute-start | bytes 442376 | tf_op jit(solution)/shard_map/ppermute | solution.py:319
  54.7 6.0 %collective-permute-start.23 = (bf16[2,2,1,1,16,1152]{5,4,3,2,1,0:T(8,128)(2,1)S(1)}, bf16[2,2,1,1,16,1152]{5,4,3,2,1,0:T(8,128)(2,1)S(1)}, u32[]{:S(2)}, u32[]{:S(2)}) collective-permute-start(bf16[2,2,1,1,16,1152]{5,4,3,2,1,0:T(8,128)(2,1)S(1)} %fusion), channel_id=1, source_target_pairs={{0,2},{1,3},{2,0},{3,1},{4,6},{5,7},{6,4},{7,5},{8,10},{9,11},{10,... | collective-permute-start | bytes 442376 | tf_op jit(solution)/shard_map/ppermute | solution.py:319
  55.8 6.1 %collective-permute-start.27 = (bf16[1,2,1,2,16,1280]{5,4,3,2,1,0:T(8,128)(2,1)S(1)}, bf16[1,2,1,2,16,1280]{5,4,3,2,1,0:T(8,128)(2,1)S(1)}, u32[]{:S(2)}, u32[]{:S(2)}) collective-permute-start(bf16[1,2,1,2,16,1280]{5,4,3,2,1,0:T(8,128)(2,1)S(1)} %bitcast.59), channel_id=1, source_target_pairs={{0,16},{1,17},{2,18},{3,19},{4,20},{5,21},{6,22},{7,23},{8,24},{9,... | collective-permute-start | bytes 491528 | tf_op jit(solution)/shard_map/ppermute | solution.py:319
  58.3 4.4 %collective-permute-start.20 = (bf16[1,2,1,1,16,1152]{5,4,3,2,1,0:T(8,128)(2,1)S(1)}, bf16[1,2,1,1,16,1152]{5,4,3,2,1,0:T(8,128)(2,1)S(1)}, u32[]{:S(2)}, u32[]{:S(2)}) collective-permute-start(bf16[1,2,1,1,16,1152]{5,4,3,2,1,0:T(8,128)(2,1)S(1)} %fusion.7), channel_id=1, source_target_pairs={{0,2},{1,3},{2,0},{3,1},{4,6},{5,7},{6,4},{7,5},{8,10},{9,11},{10,... | collective-permute-start | bytes 221192 | tf_op jit(solution)/shard_map/ppermute | solution.py:319
  60.7 4.4 %collective-permute-start.24 = (bf16[1,2,1,1,16,1152]{5,4,3,2,1,0:T(8,128)(2,1)S(1)}, bf16[1,2,1,1,16,1152]{5,4,3,2,1,0:T(8,128)(2,1)S(1)}, u32[]{:S(2)}, u32[]{:S(2)}) collective-permute-start(bf16[1,2,1,1,16,1152]{5,4,3,2,1,0:T(8,128)(2,1)S(1)} %fusion.5), channel_id=1, source_target_pairs={{0,16},{1,17},{2,18},{3,19},{4,20},{5,21},{6,22},{7,23},{8,24},{9,... | collective-permute-start | bytes 221192 | tf_op jit(solution)/shard_map/ppermute | solution.py:319
  62.0 5.0 %collective-permute-start.28 = (bf16[1,2,1,1,16,1280]{5,4,3,2,1,0:T(8,128)(2,1)S(1)}, bf16[1,2,1,1,16,1280]{5,4,3,2,1,0:T(8,128)(2,1)S(1)}, u32[]{:S(2)}, u32[]{:S(2)}) collective-permute-start(bf16[1,2,1,1,16,1280]{5,4,3,2,1,0:T(8,128)(2,1)S(1)} %fusion.3), channel_id=1, source_target_pairs={{0,1},{1,0},{2,3},{3,2},{4,5},{5,4},{6,7},{7,6},{8,9},{9,8},{10,11... | collective-permute-start | bytes 245768 | tf_op jit(solution)/shard_map/ppermute | solution.py:319
  62.7 5.9 %collective-permute-start.21 = (bf16[1,1,1,1,16,1152]{5,4,3,2,1,0:T(8,128)(2,1)S(1)}, bf16[1,1,1,1,16,1152]{5,4,3,2,1,0:T(8,128)(2,1)S(1)}, u32[]{:S(2)}, u32[]{:S(2)}) collective-permute-start(bf16[1,1,1,1,16,1152]{5,4,3,2,1,0:T(8,128)(2,1)S(1)} %fusion.22), channel_id=1, source_target_pairs={{0,4},{1,5},{2,6},{3,7},{4,0},{5,1},{6,2},{7,3},{8,12},{9,13},{10,... | collective-permute-start | bytes 110600 | tf_op jit(solution)/shard_map/ppermute | solution.py:319
  65.2 4.9 %collective-permute-start.25 = (bf16[1,1,1,1,16,1152]{5,4,3,2,1,0:T(8,128)(2,1)S(1)}, bf16[1,1,1,1,16,1152]{5,4,3,2,1,0:T(8,128)(2,1)S(1)}, u32[]{:S(2)}, u32[]{:S(2)}) collective-permute-start(bf16[1,1,1,1,16,1152]{5,4,3,2,1,0:T(8,128)(2,1)S(1)} %fusion.16), channel_id=1, source_target_pairs={{0,4},{1,5},{2,6},{3,7},{4,0},{5,1},{6,2},{7,3},{8,12},{9,13},{10,... | collective-permute-start | bytes 110600 | tf_op jit(solution)/shard_map/ppermute | solution.py:319
  67.0 5.0 %collective-permute-start.29 = (bf16[1,1,1,1,16,1280]{5,4,3,2,1,0:T(8,128)(2,1)S(1)}, bf16[1,1,1,1,16,1280]{5,4,3,2,1,0:T(8,128)(2,1)S(1)}, u32[]{:S(2)}, u32[]{:S(2)}) collective-permute-start(bf16[1,1,1,1,16,1280]{5,4,3,2,1,0:T(8,128)(2,1)S(1)} %fusion.10), channel_id=1, source_target_pairs={{0,4},{1,5},{2,6},{3,7},{4,0},{5,1},{6,2},{7,3},{8,12},{9,13},{10,... | collective-permute-start | bytes 122888 | tf_op jit(solution)/shard_map/ppermute | solution.py:319

commit v14 on v13

--- a/solution.py
+++ b/solution.py
@@ -240,10 +240,10 @@
 
 
 def back_kernel(bits, edges, n, at_ref, *refs):
-    w_refs, g_refs, send_refs, keep_refs = refs[:2], refs[-8:-6], refs[-6:-3], refs[-3:]
-    grads_kernel(n, at_ref, *refs[2:-6])
+    w_refs, g_refs, send_refs, keep_refs, both_ref = refs[:2], refs[-7:-5], refs[-5:-3], refs[-3:-1], refs[-1]
+    grads_kernel(n, at_ref, *refs[2:-5])
     for p in range(3):
-        per = send_refs[p].shape[0]
+        per = g_refs[0].shape[0] // 2
         pick = picker(bits[p], at_ref[0], 2 * per)
         back = 0.0
         for g_ref, w_ref in zip(g_refs, w_refs):
@@ -255,26 +255,30 @@
                 preferred_element_type=F32,
             )
         back = back.T
-        send_refs[p][...] = back[:per].astype(BF16)
-        keep_refs[p][...] = back[per:]
+        if p < 2:
+            send_refs[p][...] = back[:per].astype(BF16)
+            keep_refs[p][...] = back[per:]
+        else:
+            both_ref[...] = back.astype(BF16)
 
 
 def back_rows(at, own, other, stats, logits, serving, aligned, bits, edges):
     depth, cols = own.shape
     per = logits[0].shape[0]
-    parts = [(per, edges[p + 1] - edges[p]) for p in range(3)]
+    parts = [(per, edges[p + 1] - edges[p]) for p in range(2)]
     got = pl.pallas_call(
         lambda *refs: back_kernel(bits, edges, len(stats), *refs),
         out_shape=[shape((2 * per, cols), BF16)] * 2
         + [shape(part, BF16) for part in parts]
-        + [shape(part, F32) for part in parts],
+        + [shape(part, F32) for part in parts]
+        + [shape((2 * per, edges[3] - edges[2]), BF16)],
         in_specs=[SMEM] + [VMEM] * (len(stats) + 8),
-        out_specs=[VMEM] * 8,
+        out_specs=[VMEM] * 7,
         compiler_params=params(20),
         cost_estimate=cost(8 * per * depth * cols, 2 * cols * depth * 2, 4 * per * cols),
         name="back_rows",
     )(at, own, other, *stats, *logits, serving, aligned)
-    return got[0], got[1], got[2:5], got[5:8]
+    return got[0], got[1], list(got[2:4]), list(got[4:6]), got[6]
 
 
 def head_kernel(r0, r1, r2, r3, mine_ref, theirs_ref, out_ref):
@@ -337,7 +341,10 @@
         jnp.asarray(v, jnp.uint32)
         for v in (starts[0], starts[3], 2 * chip, 2 * (chip ^ 1))
     ]
-    rows, weight, spots, at, who, *unsigned = tie(hidden, head_weight, spots, at, who, *unsigned)
+    odd = jnp.broadcast_to((me_g & 1).astype(F32), (owned, depth - depth // 384 * 256))
+    rows, weight, spots, at, who, odd, *unsigned = tie(
+        hidden, head_weight, spots, at, who, odd, *unsigned
+    )
     zero = jnp.uint32(0)
 
     def cut(value, start, size, dim):
@@ -392,46 +399,53 @@
     parts = [stats] + [swap(stats, mask) for mask in (X, Y, X + Y)]
 
     bits = shards.bit_length() - 1
-    masks = {0: X}
+    masks = {1: X}
     for b in range(bits):
-        masks[1 + b] = shards >> (1 + b)
-    ydim, wdim = bits, bits - 1
-    third = depth // 128 // 3 * 128
-    edges = (0, third, 2 * third, depth)
-    orders = [(0, ydim, wdim), (ydim, wdim, 0), (wdim, 0, ydim)]
+        masks[2 + b] = shards >> (1 + b)
+    xdim, ydim, wdim = 1, 1 + bits, bits
+    units = depth // 128
+    edges = (0, units // 3 * 128, units // 3 * 256, depth)
+    orders = [(xdim, ydim, wdim), (ydim, wdim, xdim), (wdim, xdim, ydim)]
+    orders = [order + tuple(range(2, wdim)) for order in orders]
     low = owned.bit_length() - 1
-    row_bit = {0: low + bits, ydim: low, wdim: low + 1}
+    row_bit = {xdim: low + bits, ydim: low, wdim: low + 1}
     first_bits = tuple(row_bit[order[0]] for order in orders)
-    gown, gother, sents, keeps = back_rows(
+    gown, gother, sents, keeps, third = back_rows(
         at, weight, other_weight, parts, logits, served, aligned, first_bits, edges
     )
-    gots = [swap(sents[p], masks[orders[p][0]]) for p in range(3)]
+
+    def step(value, p, dim):
+        movers = [i for i in range(count) if p < 2 or (i // shards) & 1]
+        return lax.ppermute(value, AXES, [(i, i ^ masks[dim]) for i in movers])
+
+    def folded(value, p):
+        dims = [2] * (1 + bits)
+        dims[orders[p][0] - 1] = 1
+        return value.reshape(-1, *dims, owned, value.shape[-1])
+
+    gots = [step(sents[p], p, orders[p][0]) for p in range(2)]
+    third_core = swap(third, CORE)
+    sents = sents + [jnp.stack([third[:per], third_core[:per]])]
+    keeps = keeps + [jnp.stack([third[per:], third_core[per:]])]
+    gots.append(step(sents[2], 2, orders[2][0]))
     theirs = swap(gother, CORE)
     _, x_sent = tie(gother, x_rows)
     grad_head = head_gradient([hidden, x_rows, core_hidden, swap(x_sent, CORE)], gown, theirs)
     for p in range(3):
         grad_head, gots[p] = tie(grad_head, gots[p])
-
-    def folded(value, p):
-        dims = [2] * (1 + bits)
-        dims[orders[p][0]] = 1
-        return value.reshape(*dims, owned, value.shape[-1])
-
     terms = [[folded(keeps[p], p), folded(gots[p], p)] for p in range(3)]
-    for stage in (1, 2):
-        sents = [
-            sum(lax.index_in_dim(t, 1, orders[p][stage]).astype(F32) for t in terms[p]).astype(BF16)
-            for p in range(3)
-        ]
-        gots = [swap(sents[p], masks[orders[p][stage]]) for p in range(3)]
-        for p in range(3):
-            terms[p] = [lax.index_in_dim(t, 0, orders[p][stage]) for t in terms[p]] + [gots[p]]
-    for dim in range(1, wdim):
-        for p in range(3):
+    for stage in range(1, 1 + bits):
+        for p in (2, 0, 1):
+            dim = orders[p][stage]
             sent = sum(lax.index_in_dim(t, 1, dim).astype(F32) for t in terms[p]).astype(BF16)
-            terms[p] = [lax.index_in_dim(t, 0, dim) for t in terms[p]] + [swap(sent, masks[dim])]
-    total = jnp.concatenate([sum(t.astype(F32) for t in ts) for ts in terms], axis=-1)
-    return (total.reshape(owned, depth), grad_head)
+            terms[p] = [lax.index_in_dim(t, 0, dim) for t in terms[p]] + [step(sent, p, dim)]
+    totals = [sum(t.astype(F32) for t in terms[p]) for p in range(3)]
+    totals = [total.reshape(-1, owned, total.shape[-1]) for total in totals]
+    back = swap(totals[2][1], CORE)
+    total = jnp.concatenate(
+        [totals[0][0], totals[1][0], jnp.where(odd > 0.5, totals[2][0], back)], axis=-1
+    )
+    return (total, grad_head)
 
 
 def solution(mesh):

time: 72.9 us -> 83.5 us (1.15)
  starting transfers between devices: 32.1 us -> 43.7 us
  waiting for transfers between devices: 18.2 us -> 16.8 us
    ppermute x0 -> x12, starting transfers between devices: none -> 13.2 us  [step(): return lax.ppermute(value, AXES, [(i, i ^ masks[dim]) for i in movers])]
    ppermute x30 -> x20, waiting for transfers between devices: 18.2 us -> 9.57 us  [swap(): return lax.ppermute(value, AXES, [(i, i ^ mask) for i in range(count)])]
    ppermute x0 -> x12, waiting for transfers between devices: none -> 7.22 us  [step(): return lax.ppermute(value, AXES, [(i, i ^ masks[dim]) for i in movers])]
    ppermute x30 -> x20, starting transfers between devices: 32.1 us -> 30.4 us  [swap(): return lax.ppermute(value, AXES, [(i, i ^ mask) for i in range(count)])]
  transfers between devices with their start and end apart: 30 -> 32, of which waited for: 17 -> 14; matrix products, arithmetic and copies ran while one was open for 3% -> 3% of each run, Pallas kernels for 15% -> 13%
where the time goes in v14:
time: 83.5 us; the launch traced here: 83.1 us
  starting transfers between devices  43.7 us (52%)
  waiting for transfers between devices  16.8 us (20%)
  Pallas kernels  14.9 us (18%)
  local copies, waits for them, and re-layouts  5.42 us (6%)
  other arithmetic  1.39 us (2%)
  between operations  0.93 us (1%)
    ppermute x20, starting transfers between devices, swap(): return lax.ppermute(value, AXES, [(i, i ^ mask) for i in range(count)])  30.4 us
    ppermute x12, starting transfers between devices, step(): return lax.ppermute(value, AXES, [(i, i ^ masks[dim]) for i in movers])  13.2 us
    ppermute x20, waiting for transfers between devices, swap(): return lax.ppermute(value, AXES, [(i, i ^ mask) for i in range(count)])  9.57 us
    ppermute x12, waiting for transfers between devices, step(): return lax.ppermute(value, AXES, [(i, i ^ masks[dim]) for i in movers])  7.22 us
    pallas_call x1, Pallas kernels, head_gradient(): pl.pallas_call(head_kernel, grid=(depth // tile,), out_shape=shape((depth...  5.24 us
    pallas_call x1, Pallas kernels, back_rows(): pl.pallas_call(lambda *refs: back_kernel(bits, edges, len(stats), *refs),...  4.35 us
    dynamic_slice x2, local copies, waits for them, and re-layouts, cut(): return lax.dynamic_slice(value, indices, sizes)  2.09 us
    unnamed x10, local copies, waits for them, and re-layouts  2.06 us
  transfers between devices with their start and end apart: 32, of which 14 were waited for; matrix products, arithmetic and copies ran while one was open for 3% of the time, Pallas kernels for 13%

profile of v14, /device:TPU:0, one launch (start us, length us, event | category | flops | bytes accessed | tf_op | source)
XLA Modules:
  0.0 83.1 jit_solution(13136056354933482341)
XLA Ops:
  0.7 0.1 pad_add_fusion.2.at_ref
  0.7 0.1 pad_add_fusion
  0.8 1.1 %constant_dynamic-slice_fusion.1 = bf16[32,3584]{1,0:T(8,128)(2,1)S(1)} fusion(bf16[128,3584]{1,0:T(8,128)(2,1)} %r0.1, u32[]{:T(128)S(6)} %convert_element_type.145), kind=kLoop, calls=%fused_computation.49 | loop fusion | bytes 458756 | tf_op jit(solution)/shard_map/dynamic_slice | solution.py:353
  1.9 0.5 collective-permute-start
  2.4 2.6 %collective-permute-start.2 = (bf16[32,3584]{1,0:T(8,128)(2,1)S(1)}, bf16[32,3584]{1,0:T(8,128)(2,1)S(1)}, u32[]{:S(2)}, u32[]{:S(2)}) collective-permute-start(bf16[32,3584]{1,0:T(8,128)(2,1)S(1)} %constant_dynamic-slice_fusion.1), channel_id=1, source_target_pairs={{0,16},{1,17},{2,18},{3,19},{4,20},{5,21},{6,22},{7,23},{8,24},{9,... | collective-permute-start | bytes 688136 | tf_op jit(solution)/shard_map/ppermute | solution.py:323
  5.0 0.2 collective-permute-start.1
  5.2 1.0 %constant_dynamic-slice_fusion = bf16[32,3584]{1,0:T(8,128)(2,1)S(1)} fusion(bf16[128,3584]{1,0:T(8,128)(2,1)} %r0.1, u32[]{:T(128)S(6)} %convert_element_type.146), kind=kLoop, calls=%fused_computation.48 | loop fusion | bytes 458756 | tf_op jit(solution)/shard_map/dynamic_slice | solution.py:353
  6.2 0.3 collective-permute-start.7
  6.5 1.1 %copy.7 = bf16[128,4,512]{2,0,1:T(8,128)(2,1)S(1)} copy(bf16[128,4,512]{2,1,0:T(4,128)(2,1)} %param.9) | data formatting | bytes 1048576 | tf_op jit(solution)/shard_map/optimization_barrier | solution.py:326
  7.7 0.4 taught_stats.1.refs_9_
  8.1 0.1 collective-permute-start.3
  8.2 2.0 %copy-done = bf16[3584,512]{1,0:T(8,128)(2,1)S(1)} copy-done((bf16[3584,512]{1,0:T(8,128)(2,1)S(1)}, bf16[3584,512]{1,0:T(8,128)(2,1)}, u32[]{:S(2)}) %copy-start) | copy-done | bytes 3670040
  10.2 0.9 %near_logits.2 = (f32[128,512]{1,0:T(8,128)S(1)}, f32[8,128]{1,0:T(8,128)S(1)}) custom-call(bf16[128,3584]{1,0:T(8,128)(2,1)S(1)} %copy-done.2, bf16[3584,512]{1,0:T(8,128)(2,1)S(1)} %copy-done), custom_call_target="tpu_custom_call" | custom-call | flops 469762048 | bytes 4587520 | tf_op jit(solution)/shard_map/near_logits/pallas_call | solution.py:108
  11.1 0.4 collective-permute-done.2.refs_0_.refs_1_
  11.5 2.0 %collective-permute-start.6 = (bf16[32,3584]{1,0:T(8,128)(2,1)S(1)}, bf16[32,3584]{1,0:T(8,128)(2,1)S(1)}, u32[]{:S(2)}, u32[]{:S(2)}) collective-permute-start(bf16[32,3584]{1,0:T(8,128)(2,1)S(1)} %collective-permute-done.2.refs_0_.refs_1_), channel_id=1, source_target_pairs={{0,2},{1,3},{2,0},{3,1},{4,6},{5,7},{6,4},{7,5},{8,10},{9,11},{10,... | collective-permute-start | bytes 688136 | tf_op jit(solution)/shard_map/ppermute | solution.py:323
  13.5 1.5 %collective-permute-start.5 = (bf16[32,3584]{1,0:T(8,128)(2,1)S(1)}, bf16[32,3584]{1,0:T(8,128)(2,1)S(1)}, u32[]{:S(2)}, u32[]{:S(2)}) collective-permute-start(bf16[32,3584]{1,0:T(8,128)(2,1)S(1)} %collective-permute-done.2.refs_0_.refs_1_), channel_id=1, source_target_pairs={{0,1},{1,0},{2,3},{3,2},{4,5},{5,4},{6,7},{7,6},{8,9},{9,8},{10,11... | collective-permute-start | bytes 688136 | tf_op jit(solution)/shard_map/ppermute | solution.py:323
  15.0 0.9 %near_logits.3 = (f32[128,512]{1,0:T(8,128)S(1)}, f32[8,128]{1,0:T(8,128)S(1)}) custom-call(bf16[128,3584]{1,0:T(8,128)(2,1)S(1)} %copy-done.2, bf16[3584,512]{1,0:T(8,128)(2,1)S(1)} %collective-permute-done.w_ref.refs_6_.refs_2_, bf16[32,3584]{1,0:T(8,128)(2,1)S(1)} %collective-permute-done.2.refs_0_.refs_1_), custom_call_target="tpu_custom_call" | custom-call | flops 469762048 | bytes 4587520 | tf_op jit(solution)/shard_map/near_logits/pallas_call | solution.py:108
  15.9 0.3 collective-permute-done.7.refs_4_
  16.1 3.1 %collective-permute-done.6.refs_3_ = bf16[32,3584]{1,0:T(8,128)(2,1)S(1)} collective-permute-done((bf16[32,3584]{1,0:T(8,128)(2,1)S(1)}, bf16[32,3584]{1,0:T(8,128)(2,1)S(1)}, u32[]{:S(2)}, u32[]{:S(2)}) %collective-permute-start.6) | collective-permute-done | bytes 229408 | tf_op jit(solution)/shard_map/ppermute | solution.py:323
  19.2 1.5 %collective-permute-done.5.refs_2_ = bf16[32,3584]{1,0:T(8,128)(2,1)S(1)} collective-permute-done((bf16[32,3584]{1,0:T(8,128)(2,1)S(1)}, bf16[32,3584]{1,0:T(8,128)(2,1)S(1)}, u32[]{:S(2)}, u32[]{:S(2)}) %collective-permute-start.5) | collective-permute-done | bytes 229408 | tf_op jit(solution)/shard_map/ppermute | solution.py:323
  20.7 1.5 %collective-permute-start.14 = (bf16[2,128,512]{2,1,0:T(8,128)(2,1)S(1)}, bf16[2,128,512]{2,1,0:T(8,128)(2,1)S(1)}, u32[]{:S(2)}, u32[]{:S(2)}) collective-permute-start(bf16[2,128,512]{2,1,0:T(8,128)(2,1)S(1)} %get-tuple-element.87.gone_ref), channel_id=1, source_target_pairs={{0,16},{1,17},{2,18},{3,19},{4,20},{5,21},{6,22},{7,23},{8,24},{9,... | collective-permute-start | bytes 786440 | tf_op jit(solution)/shard_map/ppermute | solution.py:323
  22.2 2.0 %far_logits.1 = (f32[128,512]{1,0:T(8,128)S(1)}, f32[128,512]{1,0:T(8,128)S(1)}, bf16[128,3584]{1,0:T(8,128)(2,1)S(1)}, f32[2,8,128]{2,1,0:T(8,128)S(1)}) custom-call(s32[4]{0:T(128)S(1)} %get-tuple-element.66.refs_0_, bf16[32,3584]{1,0:T(8,128)(2,1)S(1)} %collective-permute-done.2.refs_0_.refs_1_, bf16[32,3584]{1,0:T(8,128)(2,1)S(1)} %collective-permute-done.5.refs_2_, ...), custom_call_target="tpu_custom_call" | custom-call | flops 939524096 | bytes 8257536 | tf_op jit(solution)/shard_map/far_logits/pallas_call | solution.py:153
  24.2 2.5 %collective-permute-start.10 = (f32[2,8,128]{2,1,0:T(8,128)S(1)}, f32[2,8,128]{2,1,0:T(8,128)S(1)}, u32[]{:S(2)}, u32[]{:S(2)}) collective-permute-start(f32[2,8,128]{2,1,0:T(8,128)S(1)} %get-tuple-element.80.refs_0_), channel_id=1, source_target_pairs={{0,6},{1,7},{2,4},{3,5},{4,2},{5,3},{6,0},{7,1},{8,14},{9,15},{10,... | collective-permute-start | bytes 24584 | tf_op jit(solution)/shard_map/ppermute | solution.py:323
  26.7 0.2 collective-permute-start.9
  26.9 1.7 %collective-permute-start.8 = (f32[2,8,128]{2,1,0:T(8,128)S(1)}, f32[2,8,128]{2,1,0:T(8,128)S(1)}, u32[]{:S(2)}, u32[]{:S(2)}) collective-permute-start(f32[2,8,128]{2,1,0:T(8,128)S(1)} %get-tuple-element.80.refs_0_), channel_id=1, source_target_pairs={{0,2},{1,3},{2,0},{3,1},{4,6},{5,7},{6,4},{7,5},{8,10},{9,11},{10,... | collective-permute-start | bytes 24584 | tf_op jit(solution)/shard_map/ppermute | solution.py:323
  28.6 1.1 %collective-permute-done.10.refs_3_ = f32[2,8,128]{2,1,0:T(8,128)S(1)} collective-permute-done((f32[2,8,128]{2,1,0:T(8,128)S(1)}, f32[2,8,128]{2,1,0:T(8,128)S(1)}, u32[]{:S(2)}, u32[]{:S(2)}) %collective-permute-start.10) | collective-permute-done | bytes 8224 | tf_op jit(solution)/shard_map/ppermute | solution.py:323
  29.7 1.6 %collective-permute-done.9.refs_2_ = f32[2,8,128]{2,1,0:T(8,128)S(1)} collective-permute-done((f32[2,8,128]{2,1,0:T(8,128)S(1)}, f32[2,8,128]{2,1,0:T(8,128)S(1)}, u32[]{:S(2)}, u32[]{:S(2)}) %collective-permute-start.9) | collective-permute-done | bytes 8224 | tf_op jit(solution)/shard_map/ppermute | solution.py:323
  31.3 0.1 collective-permute-start.15
  31.4 1.6 %collective-permute-start.13 = (f32[2,8,128]{2,1,0:T(8,128)S(1)}, f32[2,8,128]{2,1,0:T(8,128)S(1)}, u32[]{:S(2)}, u32[]{:S(2)}) collective-permute-start(f32[2,8,128]{2,1,0:T(8,128)S(1)} %merge_stats.1.refs_3_), channel_id=1, source_target_pairs={{0,17},{1,16},{2,19},{3,18},{4,21},{5,20},{6,23},{7,22},{8,25},{9,... | collective-permute-start | bytes 24584 | tf_op jit(solution)/shard_map/ppermute | solution.py:323
  32.9 0.5 collective-permute-start.12
  33.4 1.5 %collective-permute-start.11 = (f32[2,8,128]{2,1,0:T(8,128)S(1)}, f32[2,8,128]{2,1,0:T(8,128)S(1)}, u32[]{:S(2)}, u32[]{:S(2)}) collective-permute-start(f32[2,8,128]{2,1,0:T(8,128)S(1)} %merge_stats.1.refs_3_), channel_id=1, source_target_pairs={{0,16},{1,17},{2,18},{3,19},{4,20},{5,21},{6,22},{7,23},{8,24},{9,... | collective-permute-start | bytes 24584 | tf_op jit(solution)/shard_map/ppermute | solution.py:323
  34.9 1.3 %teacher_rows.1.refs_12_ = bf16[2,128,1024]{2,1,0:T(8,128)(2,1)S(1)} custom-call(s32[2]{0:T(128)S(1)} %pad_add_fusion.2.at_ref, s32[4,1,128]{2,1,0:T(1,128)S(1)} %bitcast.54, bf16[2,128,512]{2,1,0:T(8,128)(2,1)S(1)} %get-tuple-element.65.kept_ref.a0, bf16[2,128,512]{2,1,0:T(8,128)(2,1)S(1)} %collective-permute-done.4.a1, ...), custom_call_target="tpu_custom_call" | custom-call | flops 268435456 | bytes 1572864 | tf_op jit(solution)/shard_map/teacher_rows/pallas_call | solution.py:80
  36.2 0.4 collective-permute-done.12.refs_5_
  36.6 0.5 collective-permute-done.11.refs_4_
  37.1 4.4 %back_rows.1 = (bf16[256,512]{1,0:T(8,128)(2,1)S(1)}, bf16[256,512]{1,0:T(8,128)(2,1)S(1)}, bf16[128,1152]{1,0:T(8,128)(2,1)S(1)}, bf16[128,1152]{1,0:T(8,128)(2...) custom-call(s32[4]{0:T(128)S(1)} %get-tuple-element.54.refs_0_, ...), custom_call_target="tpu_custom_call" | custom-call | flops 1879048192 | bytes 7340032 | tf_op jit(solution)/shard_map/back_rows/pallas_call | solution.py:269
  41.4 0.1 collective-permute-start.26
  41.5 0.5 collective-permute-start.17
  42.0 0.1 collective-permute-start.16
  42.1 1.6 %collective-permute-start.18 = (bf16[128,1152]{1,0:T(8,128)(2,1)S(1)}, bf16[128,1152]{1,0:T(8,128)(2,1)S(1)}, u32[]{:S(2)}, u32[]{:S(2)}) collective-permute-start(bf16[128,1152]{1,0:T(8,128)(2,1)S(1)} %get-tuple-element.95), channel_id=1, source_target_pairs={{0,16},{1,17},{2,18},{3,19},{4,20},{5,21},{6,22},{7,23},{8,24},{9,... | collective-permute-start | bytes 884744 | tf_op jit(solution)/shard_map/ppermute | solution.py:419
  43.7 1.5 %collective-permute-start.22 = (bf16[128,1152]{1,0:T(8,128)(2,1)S(1)}, bf16[128,1152]{1,0:T(8,128)(2,1)S(1)}, u32[]{:S(2)}, u32[]{:S(2)}) collective-permute-start(bf16[128,1152]{1,0:T(8,128)(2,1)S(1)} %get-tuple-element.99), channel_id=1, source_target_pairs={{0,1},{1,0},{2,3},{3,2},{4,5},{5,4},{6,7},{7,6},{8,9},{9,8},{10,11... | collective-permute-start | bytes 884744 | tf_op jit(solution)/shard_map/ppermute | solution.py:419
  45.3 0.1 pad_maximum_fusion
  45.4 0.7 collective-permute-start.27
  46.1 5.2 %head_gradient.1 = bf16[3584,512]{1,0:T(8,128)(2,1)} custom-call(bf16[128,3584]{1,0:T(8,128)(2,1)S(1)} %copy-done.2, bf16[128,3584]{1,0:T(8,128)(2,1)S(1)} %get-tuple-element.93.r1, bf16[128,3584]{1,0:T(8,128)(2,1)S(1)} %collective-permute-done.1.r2, bf16[128,3584]{1,0:T(8,128)(2,1)S(1)} %collective-permute-done.16.r3, ...), custom_call_target="tpu_custom_call" | custom-call | flops 1879048192 | bytes 7340032 | tf_op jit(solution)/shard_map/head_gradient/pallas_call | solution.py:298
  51.3 0.2 collective-permute-done.18
  51.6 1.2 %collective-permute-done.22 = bf16[128,1152]{1,0:T(8,128)(2,1)S(1)} collective-permute-done((bf16[128,1152]{1,0:T(8,128)(2,1)S(1)}, bf16[128,1152]{1,0:T(8,128)(2,1)S(1)}, u32[]{:S(2)}, u32[]{:S(2)}) %collective-permute-start.22) | collective-permute-done | bytes 294944 | tf_op jit(solution)/shard_map/ppermute | solution.py:419
  52.8 1.6 %collective-permute-start.19 = (bf16[1,1,2,2,1,16,1152]{6,5,4,3,2,1,0:T(8,128)(2,1)S(1)}, bf16[1,1,2,2,1,16,1152]{6,5,4,3,2,1,0:T(8,128)(2,1)S(1)}, u32[]{:S(2)}, u32[]{:S(2)}) collective-permute-start(bf16[1,1,2,2,1,16,1152]{6,5,4,3,2,1,0:T(8,128)(2,1)S(1)} %fusion.2), channel_id=1, source_target_pairs={{0,1},{1,0},{2,3},{3,2},{4,5},{5,4},{6,7},{7,6},{8,9},{9,8},{10,11... | collective-permute-start | bytes 442376 | tf_op jit(solution)/shard_map/ppermute | solution.py:419
  54.4 1.1 %collective-permute-start.23 = (bf16[1,2,2,1,1,16,1152]{6,5,4,3,2,1,0:T(8,128)(2,1)S(1)}, bf16[1,2,2,1,1,16,1152]{6,5,4,3,2,1,0:T(8,128)(2,1)S(1)}, u32[]{:S(2)}, u32[]{:S(2)}) collective-permute-start(bf16[1,2,2,1,1,16,1152]{6,5,4,3,2,1,0:T(8,128)(2,1)S(1)} %fusion.1), channel_id=1, source_target_pairs={{0,2},{1,3},{2,0},{3,1},{4,6},{5,7},{6,4},{7,5},{8,10},{9,11},{10,... | collective-permute-start | bytes 442376 | tf_op jit(solution)/shard_map/ppermute | solution.py:419
  55.5 3.5 %collective-permute-done.19 = bf16[1,1,2,2,1,16,1152]{6,5,4,3,2,1,0:T(8,128)(2,1)S(1)} collective-permute-done((bf16[1,1,2,2,1,16,1152]{6,5,4,3,2,1,0:T(8,128)(2,1)S(1)}, bf16[1,1,2,2,1,16,1152]{6,5,4,3,2,1,0:T(8,128)(2,1)S(1)}, u32[]{:S(2)}, u32[]{:S(2)}) %collective-permute-start.19) | collective-permute-done | bytes 147488 | tf_op jit(solution)/shard_map/ppermute | solution.py:419
  59.0 1.1 %collective-permute-start.20 = (bf16[1,1,2,1,1,16,1152]{6,5,4,3,2,1,0:T(8,128)(2,1)S(1)}, bf16[1,1,2,1,1,16,1152]{6,5,4,3,2,1,0:T(8,128)(2,1)S(1)}, u32[]{:S(2)}, u32[]{:S(2)}) collective-permute-start(bf16[1,1,2,1,1,16,1152]{6,5,4,3,2,1,0:T(8,128)(2,1)S(1)} %fusion.7), channel_id=1, source_target_pairs={{0,2},{1,3},{2,0},{3,1},{4,6},{5,7},{6,4},{7,5},{8,10},{9,11},{10,... | collective-permute-start | bytes 221192 | tf_op jit(solution)/shard_map/ppermute | solution.py:419
  60.2 0.6 collective-permute-start.24
  60.8 0.1 add_convert_fusion
  60.8 0.7 collective-permute-start.28
  61.5 1.9 %collective-permute-done.20 = bf16[1,1,2,1,1,16,1152]{6,5,4,3,2,1,0:T(8,128)(2,1)S(1)} collective-permute-done((bf16[1,1,2,1,1,16,1152]{6,5,4,3,2,1,0:T(8,128)(2,1)S(1)}, bf16[1,1,2,1,1,16,1152]{6,5,4,3,2,1,0:T(8,128)(2,1)S(1)}, u32[]{:S(2)}, u32[]{:S(2)}) %collective-permute-start.20) | collective-permute-done | bytes 73760 | tf_op jit(solution)/shard_map/ppermute | solution.py:419
  63.5 1.7 %collective-permute-start.21 = (bf16[1,1,1,1,1,16,1152]{6,5,4,3,2,1,0:T(8,128)(2,1)S(1)}, bf16[1,1,1,1,1,16,1152]{6,5,4,3,2,1,0:T(8,128)(2,1)S(1)}, u32[]{:S(2)}, u32[]{:S(2)}) collective-permute-start(bf16[1,1,1,1,1,16,1152]{6,5,4,3,2,1,0:T(8,128)(2,1)S(1)} %fusion.18), channel_id=1, source_target_pairs={{0,4},{1,5},{2,6},{3,7},{4,0},{5,1},{6,2},{7,3},{8,12},{9,13},{10,... | collective-permute-start | bytes 110600 | tf_op jit(solution)/shard_map/ppermute | solution.py:419
  65.2 0.1 add_convert_fusion.1
  65.3 0.7 collective-permute-start.29
  66.0 1.3 %collective-permute-start.25 = (bf16[1,1,1,1,1,16,1152]{6,5,4,3,2,1,0:T(8,128)(2,1)S(1)}, bf16[1,1,1,1,1,16,1152]{6,5,4,3,2,1,0:T(8,128)(2,1)S(1)}, u32[]{:S(2)}, u32[]{:S(2)}) collective-permute-start(bf16[1,1,1,1,1,16,1152]{6,5,4,3,2,1,0:T(8,128)(2,1)S(1)} %fusion.11), channel_id=1, source_target_pairs={{0,4},{1,5},{2,6},{3,7},{4,0},{5,1},{6,2},{7,3},{8,12},{9,13},{10,... | collective-permute-start | bytes 110600 | tf_op jit(solution)/shard_map/ppermute | solution.py:419
  67.3 0.1 add_convert_fusion.2
  67.4 0.7 collective-permute-start.30
  68.0 0.3 collective-permute-done.21
  68.4 0.1 convert_add_fusion
  68.5 13.0 %collective-permute-start.31 = (f32[16,1280]{1,0:T(8,128)S(1)}, f32[16,1280]{1,0:T(8,128)S(1)}, u32[]{:S(2)}, u32[]{:S(2)}) collective-permute-start(f32[16,1280]{1,0:T(8,128)S(1)} %slice_bitcast_fusion.2), channel_id=1, source_target_pairs={{0,8},{1,9},{2,10},{3,11},{4,12},{5,13},{6,14},{7,15},{8,0},{9,1},... | collective-permute-start | bytes 245768 | tf_op jit(solution)/shard_map/ppermute | solution.py:323
  81.5 0.9 %collective-permute-done.31 = f32[16,1280]{1,0:T(8,128)S(1)} collective-permute-done((f32[16,1280]{1,0:T(8,128)S(1)}, f32[16,1280]{1,0:T(8,128)S(1)}, u32[]{:S(2)}, u32[]{:S(2)}) %collective-permute-start.31) | collective-permute-done | bytes 81952 | tf_op jit(solution)/shard_map/ppermute | solution.py:323
  82.4 0.7 pad_maximum_fusion.1
  (43 shorter events, 0.5 us)
Async XLA Ops:
  0.6 7.6 %copy-start.2 = (bf16[128,3584]{1,0:T(8,128)(2,1)S(1)}, bf16[128,3584]{1,0:T(8,128)(2,1)}, u32[]{:S(2)}) copy-start(bf16[128,3584]{1,0:T(8,128)(2,1)} %r0.1) | copy-start | bytes 2752516
  1.9 13.1 %collective-permute-start = (bf16[3584,512]{1,0:T(8,128)(2,1)}, bf16[3584,512]{1,0:T(8,128)(2,1)S(1)}, u32[]{:S(2)}, u32[]{:S(2)}) collective-permute-start(bf16[3584,512]{1,0:T(8,128)(2,1)} %refs_1_), channel_id=1, source_target_pairs={{0,8},{1,9},{2,10},{3,11},{4,12},{5,13},{6,14},{7,15},{8,0},{9,1},... | collective-permute-start | bytes 11010056 | tf_op jit(solution)/shard_map/ppermute | solution.py:323
  2.4 9.0 %collective-permute-start.2 = (bf16[32,3584]{1,0:T(8,128)(2,1)S(1)}, bf16[32,3584]{1,0:T(8,128)(2,1)S(1)}, u32[]{:S(2)}, u32[]{:S(2)}) collective-permute-start(bf16[32,3584]{1,0:T(8,128)(2,1)S(1)} %constant_dynamic-slice_fusion.1), channel_id=1, source_target_pairs={{0,16},{1,17},{2,18},{3,19},{4,20},{5,21},{6,22},{7,23},{8,24},{9,... | collective-permute-start | bytes 688136 | tf_op jit(solution)/shard_map/ppermute | solution.py:323
  5.0 17.2 %collective-permute-start.1 = (bf16[128,3584]{1,0:T(8,128)(2,1)}, bf16[128,3584]{1,0:T(8,128)(2,1)S(1)}, u32[]{:S(2)}, u32[]{:S(2)}) collective-permute-start(bf16[128,3584]{1,0:T(8,128)(2,1)} %r0.1), channel_id=1, source_target_pairs={{0,8},{1,9},{2,10},{3,11},{4,12},{5,13},{6,14},{7,15},{8,0},{9,1},... | collective-permute-start | bytes 2752520 | tf_op jit(solution)/shard_map/ppermute | solution.py:323
  6.2 9.9 %collective-permute-start.7 = (bf16[32,3584]{1,0:T(8,128)(2,1)S(1)}, bf16[32,3584]{1,0:T(8,128)(2,1)S(1)}, u32[]{:S(2)}, u32[]{:S(2)}) collective-permute-start(bf16[32,3584]{1,0:T(8,128)(2,1)S(1)} %constant_dynamic-slice_fusion), channel_id=1, source_target_pairs={{0,16},{1,17},{2,18},{3,19},{4,20},{5,21},{6,22},{7,23},{8,24},{9,... | collective-permute-start | bytes 688136 | tf_op jit(solution)/shard_map/ppermute | solution.py:323
  8.1 3.0 %collective-permute-start.3 = (f32[8,128]{1,0:T(8,128)S(1)}, f32[8,128]{1,0:T(8,128)S(1)}, u32[]{:S(2)}, u32[]{:S(2)}) collective-permute-start(f32[8,128]{1,0:T(8,128)S(1)} %taught_stats.1.refs_9_), channel_id=1, source_target_pairs={{0,8},{1,9},{2,10},{3,11},{4,12},{5,13},{6,14},{7,15},{8,0},{9,1},... | collective-permute-start | bytes 12296 | tf_op jit(solution)/shard_map/ppermute | solution.py:323
  8.2 2.0 %copy-start = (bf16[3584,512]{1,0:T(8,128)(2,1)S(1)}, bf16[3584,512]{1,0:T(8,128)(2,1)}, u32[]{:S(2)}) copy-start(bf16[3584,512]{1,0:T(8,128)(2,1)} %refs_1_) | copy-start | bytes 11010052
  10.2 11.9 %copy-start.1 = (bf16[3584,512]{1,0:T(8,128)(2,1)S(1)}, bf16[3584,512]{1,0:T(8,128)(2,1)}, u32[]{:S(2)}) copy-start(bf16[3584,512]{1,0:T(8,128)(2,1)} %refs_1_) | copy-start | bytes 11010052
  10.2 11.9 %copy-start.4 = (s32[128]{0:T(128)S(1)}, s32[128]{0:T(128)}, u32[]{:S(2)}) copy-start(s32[128]{0:T(128)} %param.6) | copy-start | bytes 1540
  11.5 7.7 %collective-permute-start.6 = (bf16[32,3584]{1,0:T(8,128)(2,1)S(1)}, bf16[32,3584]{1,0:T(8,128)(2,1)S(1)}, u32[]{:S(2)}, u32[]{:S(2)}) collective-permute-start(bf16[32,3584]{1,0:T(8,128)(2,1)S(1)} %collective-permute-done.2.refs_0_.refs_1_), channel_id=1, source_target_pairs={{0,2},{1,3},{2,0},{3,1},{4,6},{5,7},{6,4},{7,5},{8,10},{9,11},{10,... | collective-permute-start | bytes 688136 | tf_op jit(solution)/shard_map/ppermute | solution.py:323
  13.5 7.2 %collective-permute-start.5 = (bf16[32,3584]{1,0:T(8,128)(2,1)S(1)}, bf16[32,3584]{1,0:T(8,128)(2,1)S(1)}, u32[]{:S(2)}, u32[]{:S(2)}) collective-permute-start(bf16[32,3584]{1,0:T(8,128)(2,1)S(1)} %collective-permute-done.2.refs_0_.refs_1_), channel_id=1, source_target_pairs={{0,1},{1,0},{2,3},{3,2},{4,5},{5,4},{6,7},{7,6},{8,9},{9,8},{10,11... | collective-permute-start | bytes 688136 | tf_op jit(solution)/shard_map/ppermute | solution.py:323
  15.0 7.2 %collective-permute-start.4 = (bf16[2,128,512]{2,1,0:T(8,128)(2,1)S(1)}, bf16[2,128,512]{2,1,0:T(8,128)(2,1)S(1)}, u32[]{:S(2)}, u32[]{:S(2)}) collective-permute-start(bf16[2,128,512]{2,1,0:T(8,128)(2,1)S(1)} %get-tuple-element.65.kept_ref.a0), channel_id=1, source_target_pairs={{0,8},{1,9},{2,10},{3,11},{4,12},{5,13},{6,14},{7,15},{8,0},{9,1},... | collective-permute-start | bytes 786440 | tf_op jit(solution)/shard_map/ppermute | solution.py:323
  20.7 10.6 %collective-permute-start.14 = (bf16[2,128,512]{2,1,0:T(8,128)(2,1)S(1)}, bf16[2,128,512]{2,1,0:T(8,128)(2,1)S(1)}, u32[]{:S(2)}, u32[]{:S(2)}) collective-permute-start(bf16[2,128,512]{2,1,0:T(8,128)(2,1)S(1)} %get-tuple-element.87.gone_ref), channel_id=1, source_target_pairs={{0,16},{1,17},{2,18},{3,19},{4,20},{5,21},{6,22},{7,23},{8,24},{9,... | collective-permute-start | bytes 786440 | tf_op jit(solution)/shard_map/ppermute | solution.py:323
  24.2 10.8 %copy-start.3 = (s32[512]{0:T(512)S(1)}, s32[512]{0:T(512)}, u32[]{:S(2)}) copy-start(s32[512]{0:T(512)} %param.7) | copy-start | bytes 6148
  24.2 5.5 %collective-permute-start.10 = (f32[2,8,128]{2,1,0:T(8,128)S(1)}, f32[2,8,128]{2,1,0:T(8,128)S(1)}, u32[]{:S(2)}, u32[]{:S(2)}) collective-permute-start(f32[2,8,128]{2,1,0:T(8,128)S(1)} %get-tuple-element.80.refs_0_), channel_id=1, source_target_pairs={{0,6},{1,7},{2,4},{3,5},{4,2},{5,3},{6,0},{7,1},{8,14},{9,15},{10,... | collective-permute-start | bytes 24584 | tf_op jit(solution)/shard_map/ppermute | solution.py:323
  26.7 4.5 %collective-permute-start.9 = (f32[2,8,128]{2,1,0:T(8,128)S(1)}, f32[2,8,128]{2,1,0:T(8,128)S(1)}, u32[]{:S(2)}, u32[]{:S(2)}) collective-permute-start(f32[2,8,128]{2,1,0:T(8,128)S(1)} %get-tuple-element.80.refs_0_), channel_id=1, source_target_pairs={{0,4},{1,5},{2,6},{3,7},{4,0},{5,1},{6,2},{7,3},{8,12},{9,13},{10,... | collective-permute-start | bytes 24584 | tf_op jit(solution)/shard_map/ppermute | solution.py:323
  26.9 4.3 %collective-permute-start.8 = (f32[2,8,128]{2,1,0:T(8,128)S(1)}, f32[2,8,128]{2,1,0:T(8,128)S(1)}, u32[]{:S(2)}, u32[]{:S(2)}) collective-permute-start(f32[2,8,128]{2,1,0:T(8,128)S(1)} %get-tuple-element.80.refs_0_), channel_id=1, source_target_pairs={{0,2},{1,3},{2,0},{3,1},{4,6},{5,7},{6,4},{7,5},{8,10},{9,11},{10,... | collective-permute-start | bytes 24584 | tf_op jit(solution)/shard_map/ppermute | solution.py:323
  31.3 3.6 %collective-permute-start.15 = (bf16[2,128,512]{2,1,0:T(8,128)(2,1)S(1)}, bf16[2,128,512]{2,1,0:T(8,128)(2,1)S(1)}, u32[]{:S(2)}, u32[]{:S(2)}) collective-permute-start(bf16[2,128,512]{2,1,0:T(8,128)(2,1)S(1)} %collective-permute-done.14.a2), channel_id=1, source_target_pairs={{0,8},{1,9},{2,10},{3,11},{4,12},{5,13},{6,14},{7,15},{8,0},{9,1},... | collective-permute-start | bytes 786440 | tf_op jit(solution)/shard_map/ppermute | solution.py:323
  31.4 4.8 %collective-permute-start.13 = (f32[2,8,128]{2,1,0:T(8,128)S(1)}, f32[2,8,128]{2,1,0:T(8,128)S(1)}, u32[]{:S(2)}, u32[]{:S(2)}) collective-permute-start(f32[2,8,128]{2,1,0:T(8,128)S(1)} %merge_stats.1.refs_3_), channel_id=1, source_target_pairs={{0,17},{1,16},{2,19},{3,18},{4,21},{5,20},{6,23},{7,22},{8,25},{9,... | collective-permute-start | bytes 24584 | tf_op jit(solution)/shard_map/ppermute | solution.py:323
  32.9 3.7 %collective-permute-start.12 = (f32[2,8,128]{2,1,0:T(8,128)S(1)}, f32[2,8,128]{2,1,0:T(8,128)S(1)}, u32[]{:S(2)}, u32[]{:S(2)}) collective-permute-start(f32[2,8,128]{2,1,0:T(8,128)S(1)} %merge_stats.1.refs_3_), channel_id=1, source_target_pairs={{0,1},{1,0},{2,3},{3,2},{4,5},{5,4},{6,7},{7,6},{8,9},{9,8},{10,11... | collective-permute-start | bytes 24584 | tf_op jit(solution)/shard_map/ppermute | solution.py:323
  33.4 3.7 %collective-permute-start.11 = (f32[2,8,128]{2,1,0:T(8,128)S(1)}, f32[2,8,128]{2,1,0:T(8,128)S(1)}, u32[]{:S(2)}, u32[]{:S(2)}) collective-permute-start(f32[2,8,128]{2,1,0:T(8,128)S(1)} %merge_stats.1.refs_3_), channel_id=1, source_target_pairs={{0,16},{1,17},{2,18},{3,19},{4,20},{5,21},{6,22},{7,23},{8,24},{9,... | collective-permute-start | bytes 24584 | tf_op jit(solution)/shard_map/ppermute | solution.py:323
  41.4 3.8 %collective-permute-start.26 = (bf16[256,1280]{1,0:T(8,128)(2,1)S(1)}, bf16[256,1280]{1,0:T(8,128)(2,1)S(1)}, u32[]{:S(2)}, u32[]{:S(2)}) collective-permute-start(bf16[256,1280]{1,0:T(8,128)(2,1)S(1)} %get-tuple-element.102), channel_id=1, source_target_pairs={{0,8},{1,9},{2,10},{3,11},{4,12},{5,13},{6,14},{7,15},{8,0},{9,1},... | collective-permute-start | bytes 1966088 | tf_op jit(solution)/shard_map/ppermute | solution.py:323
  41.5 4.6 %collective-permute-start.17 = (bf16[256,512]{1,0:T(8,128)(2,1)S(1)}, bf16[256,512]{1,0:T(8,128)(2,1)S(1)}, u32[]{:S(2)}, u32[]{:S(2)}) collective-permute-start(bf16[256,512]{1,0:T(8,128)(2,1)S(1)} %get-tuple-element.92), channel_id=1, source_target_pairs={{0,8},{1,9},{2,10},{3,11},{4,12},{5,13},{6,14},{7,15},{8,0},{9,1},... | collective-permute-start | bytes 786440 | tf_op jit(solution)/shard_map/ppermute | solution.py:323
  42.0 4.1 %collective-permute-start.16 = (bf16[128,3584]{1,0:T(8,128)(2,1)S(1)}, bf16[128,3584]{1,0:T(8,128)(2,1)S(1)}, u32[]{:S(2)}, u32[]{:S(2)}) collective-permute-start(bf16[128,3584]{1,0:T(8,128)(2,1)S(1)} %get-tuple-element.93.r1), channel_id=1, source_target_pairs={{0,8},{1,9},{2,10},{3,11},{4,12},{5,13},{6,14},{7,15},{8,0},{9,1},... | collective-permute-start | bytes 2752520 | tf_op jit(solution)/shard_map/ppermute | solution.py:323
  42.1 9.4 %collective-permute-start.18 = (bf16[128,1152]{1,0:T(8,128)(2,1)S(1)}, bf16[128,1152]{1,0:T(8,128)(2,1)S(1)}, u32[]{:S(2)}, u32[]{:S(2)}) collective-permute-start(bf16[128,1152]{1,0:T(8,128)(2,1)S(1)} %get-tuple-element.95), channel_id=1, source_target_pairs={{0,16},{1,17},{2,18},{3,19},{4,20},{5,21},{6,22},{7,23},{8,24},{9,... | collective-permute-start | bytes 884744 | tf_op jit(solution)/shard_map/ppermute | solution.py:419
  43.7 9.1 %collective-permute-start.22 = (bf16[128,1152]{1,0:T(8,128)(2,1)S(1)}, bf16[128,1152]{1,0:T(8,128)(2,1)S(1)}, u32[]{:S(2)}, u32[]{:S(2)}) collective-permute-start(bf16[128,1152]{1,0:T(8,128)(2,1)S(1)} %get-tuple-element.99), channel_id=1, source_target_pairs={{0,1},{1,0},{2,3},{3,2},{4,5},{5,4},{6,7},{7,6},{8,9},{9,8},{10,11... | collective-permute-start | bytes 884744 | tf_op jit(solution)/shard_map/ppermute | solution.py:419
  45.4 15.4 %collective-permute-start.27 = (bf16[2,128,1280]{2,1,0:T(8,128)(2,1)S(1)}, bf16[2,128,1280]{2,1,0:T(8,128)(2,1)S(1)}, u32[]{:S(2)}, u32[]{:S(2)}) collective-permute-start(bf16[2,128,1280]{2,1,0:T(8,128)(2,1)S(1)} %pad_maximum_fusion), channel_id=1, source_target_pairs={{8,10},{9,11},{10,8},{11,9},{12,14},{13,15},{14,12},{15,13},{24,26... | collective-permute-start | bytes 1966088 | tf_op jit(solution)/shard_map/ppermute | solution.py:419
  52.8 6.2 %collective-permute-start.19 = (bf16[1,1,2,2,1,16,1152]{6,5,4,3,2,1,0:T(8,128)(2,1)S(1)}, bf16[1,1,2,2,1,16,1152]{6,5,4,3,2,1,0:T(8,128)(2,1)S(1)}, u32[]{:S(2)}, u32[]{:S(2)}) collective-permute-start(bf16[1,1,2,2,1,16,1152]{6,5,4,3,2,1,0:T(8,128)(2,1)S(1)} %fusion.2), channel_id=1, source_target_pairs={{0,1},{1,0},{2,3},{3,2},{4,5},{5,4},{6,7},{7,6},{8,9},{9,8},{10,11... | collective-permute-start | bytes 442376 | tf_op jit(solution)/shard_map/ppermute | solution.py:419
  54.4 5.7 %collective-permute-start.23 = (bf16[1,2,2,1,1,16,1152]{6,5,4,3,2,1,0:T(8,128)(2,1)S(1)}, bf16[1,2,2,1,1,16,1152]{6,5,4,3,2,1,0:T(8,128)(2,1)S(1)}, u32[]{:S(2)}, u32[]{:S(2)}) collective-permute-start(bf16[1,2,2,1,1,16,1152]{6,5,4,3,2,1,0:T(8,128)(2,1)S(1)} %fusion.1), channel_id=1, source_target_pairs={{0,2},{1,3},{2,0},{3,1},{4,6},{5,7},{6,4},{7,5},{8,10},{9,11},{10,... | collective-permute-start | bytes 442376 | tf_op jit(solution)/shard_map/ppermute | solution.py:419
  59.0 4.4 %collective-permute-start.20 = (bf16[1,1,2,1,1,16,1152]{6,5,4,3,2,1,0:T(8,128)(2,1)S(1)}, bf16[1,1,2,1,1,16,1152]{6,5,4,3,2,1,0:T(8,128)(2,1)S(1)}, u32[]{:S(2)}, u32[]{:S(2)}) collective-permute-start(bf16[1,1,2,1,1,16,1152]{6,5,4,3,2,1,0:T(8,128)(2,1)S(1)} %fusion.7), channel_id=1, source_target_pairs={{0,2},{1,3},{2,0},{3,1},{4,6},{5,7},{6,4},{7,5},{8,10},{9,11},{10,... | collective-permute-start | bytes 221192 | tf_op jit(solution)/shard_map/ppermute | solution.py:419
  60.2 5.8 %collective-permute-start.24 = (bf16[1,1,2,1,1,16,1152]{6,5,4,3,2,1,0:T(8,128)(2,1)S(1)}, bf16[1,1,2,1,1,16,1152]{6,5,4,3,2,1,0:T(8,128)(2,1)S(1)}, u32[]{:S(2)}, u32[]{:S(2)}) collective-permute-start(bf16[1,1,2,1,1,16,1152]{6,5,4,3,2,1,0:T(8,128)(2,1)S(1)} %fusion.5), channel_id=1, source_target_pairs={{0,16},{1,17},{2,18},{3,19},{4,20},{5,21},{6,22},{7,23},{8,24},{9,... | collective-permute-start | bytes 221192 | tf_op jit(solution)/shard_map/ppermute | solution.py:419
  60.8 4.4 %collective-permute-start.28 = (bf16[2,1,2,1,2,16,1280]{6,5,4,3,2,1,0:T(8,128)(2,1)S(1)}, bf16[2,1,2,1,2,16,1280]{6,5,4,3,2,1,0:T(8,128)(2,1)S(1)}, u32[]{:S(2)}, u32[]{:S(2)}) collective-permute-start(bf16[2,1,2,1,2,16,1280]{6,5,4,3,2,1,0:T(8,128)(2,1)S(1)} %add_convert_fusion), channel_id=1, source_target_pairs={{8,24},{9,25},{10,26},{11,27},{12,28},{13,29},{14,30},{15,31},{24,... | collective-permute-start | bytes 983048 | tf_op jit(solution)/shard_map/ppermute | solution.py:419
  63.5 4.9 %collective-permute-start.21 = (bf16[1,1,1,1,1,16,1152]{6,5,4,3,2,1,0:T(8,128)(2,1)S(1)}, bf16[1,1,1,1,1,16,1152]{6,5,4,3,2,1,0:T(8,128)(2,1)S(1)}, u32[]{:S(2)}, u32[]{:S(2)}) collective-permute-start(bf16[1,1,1,1,1,16,1152]{6,5,4,3,2,1,0:T(8,128)(2,1)S(1)} %fusion.18), channel_id=1, source_target_pairs={{0,4},{1,5},{2,6},{3,7},{4,0},{5,1},{6,2},{7,3},{8,12},{9,13},{10,... | collective-permute-start | bytes 110600 | tf_op jit(solution)/shard_map/ppermute | solution.py:419
  65.3 2.0 %collective-permute-start.29 = (bf16[2,1,2,1,1,16,1280]{6,5,4,3,2,1,0:T(8,128)(2,1)S(1)}, bf16[2,1,2,1,1,16,1280]{6,5,4,3,2,1,0:T(8,128)(2,1)S(1)}, u32[]{:S(2)}, u32[]{:S(2)}) collective-permute-start(bf16[2,1,2,1,1,16,1280]{6,5,4,3,2,1,0:T(8,128)(2,1)S(1)} %add_convert_fusion.1), channel_id=1, source_target_pairs={{8,9},{9,8},{10,11},{11,10},{12,13},{13,12},{14,15},{15,14},{24,25... | collective-permute-start | bytes 491528 | tf_op jit(solution)/shard_map/ppermute | solution.py:419
  66.0 15.5 %collective-permute-start.25 = (bf16[1,1,1,1,1,16,1152]{6,5,4,3,2,1,0:T(8,128)(2,1)S(1)}, bf16[1,1,1,1,1,16,1152]{6,5,4,3,2,1,0:T(8,128)(2,1)S(1)}, u32[]{:S(2)}, u32[]{:S(2)}) collective-permute-start(bf16[1,1,1,1,1,16,1152]{6,5,4,3,2,1,0:T(8,128)(2,1)S(1)} %fusion.11), channel_id=1, source_target_pairs={{0,4},{1,5},{2,6},{3,7},{4,0},{5,1},{6,2},{7,3},{8,12},{9,13},{10,... | collective-permute-start | bytes 110600 | tf_op jit(solution)/shard_map/ppermute | solution.py:419
  67.4 1.0 %collective-permute-start.30 = (bf16[2,1,1,1,1,16,1280]{6,5,4,3,2,1,0:T(8,128)(2,1)S(1)}, bf16[2,1,1,1,1,16,1280]{6,5,4,3,2,1,0:T(8,128)(2,1)S(1)}, u32[]{:S(2)}, u32[]{:S(2)}) collective-permute-start(bf16[2,1,1,1,1,16,1280]{6,5,4,3,2,1,0:T(8,128)(2,1)S(1)} %add_convert_fusion.2), channel_id=1, source_target_pairs={{8,12},{9,13},{10,14},{11,15},{12,8},{13,9},{14,10},{15,11},{24,28... | collective-permute-start | bytes 245768 | tf_op jit(solution)/shard_map/ppermute | solution.py:419
  68.5 13.9 %collective-permute-start.31 = (f32[16,1280]{1,0:T(8,128)S(1)}, f32[16,1280]{1,0:T(8,128)S(1)}, u32[]{:S(2)}, u32[]{:S(2)}) collective-permute-start(f32[16,1280]{1,0:T(8,128)S(1)} %slice_bitcast_fusion.2), channel_id=1, source_target_pairs={{0,8},{1,9},{2,10},{3,11},{4,12},{5,13},{6,14},{7,15},{8,0},{9,1},... | collective-permute-start | bytes 245768 | tf_op jit(solution)/shard_map/ppermute | solution.py:323

commit v15 on v13

--- a/solution.py
+++ b/solution.py
@@ -129,13 +129,17 @@
 
 def far_kernel(n, spots_ref, *refs):
     pieces, refs = refs[:n], refs[n:]
-    own_ref, other_ref, stats_a, stats_b, taught_ref, taught_core_ref, ids_ref = refs[:7]
-    a_ref, b_ref, rows_ref, out_ref = refs[7:]
-    for k, piece in enumerate(pieces):
-        rows_ref[pl.ds(pl.multiple_of(spots_ref[k], 16), piece.shape[0]), :] = piece[...]
-    per = rows_ref.shape[0]
-    a = jnp.dot(rows_ref[...], own_ref[...], preferred_element_type=F32)
-    b = jnp.dot(rows_ref[...], other_ref[...], preferred_element_type=F32)
+    own_ref, other_ref, near_ref, stats_a, stats_b, taught_ref, taught_core_ref, ids_ref = refs[:8]
+    a_ref, b_ref, rows_ref, out_ref, full = refs[8:]
+    share = pieces[0].shape[0]
+    for k, piece in enumerate(pieces[:-1]):
+        full[pl.ds(pl.multiple_of(spots_ref[k], 8), share), :] = piece[...].astype(F32)
+    full[4 * share :, :] = pieces[-1][...].astype(F32)
+    rows_ref[0] = near_ref[...]
+    rows_ref[1] = full[...].astype(BF16)
+    per = rows_ref.shape[1]
+    a = jnp.dot(rows_ref[1], own_ref[...], preferred_element_type=F32)
+    b = jnp.dot(rows_ref[1], other_ref[...], preferred_element_type=F32)
     a_ref[...] = a
     b_ref[...] = b
     out_ref[0, 0:3, :] = both(stats_a[...], stats_b[...])
@@ -155,12 +159,13 @@
         out_shape=(
             shape((per, cols), F32),
             shape((per, cols), F32),
-            shape((per, depth), BF16),
+            shape((2, per, depth), BF16),
             shape((2, STAT_ROWS, per), F32),
         ),
         in_specs=[SMEM] + [VMEM] * (len(pieces) + 2 + len(small)),
         out_specs=(VMEM, VMEM, VMEM, VMEM),
-        compiler_params=params(12),
+        scratch_shapes=[pltpu.VMEM((per, depth), F32)],
+        compiler_params=params(16),
         cost_estimate=cost(4 * per * depth * cols, (per + 2 * cols) * depth * 2, 2 * per * cols),
         name="far_logits",
     )(spots, *pieces, own, other, *small)
@@ -277,30 +282,30 @@
     return got[0], got[1], got[2:5], got[5:8]
 
 
-def head_kernel(r0, r1, r2, r3, mine_ref, theirs_ref, out_ref):
-    rows = jnp.concatenate([r0[...], r1[...], r2[...], r3[...]])
+def head_kernel(rows_ref, core_ref, mine_ref, theirs_ref, out_ref):
+    rows = jnp.concatenate([rows_ref[0], rows_ref[1], core_ref[0], core_ref[1]])
     grads = jnp.concatenate([mine_ref[...], theirs_ref[...]])
     out_ref[...] = lax.dot_general(
         rows, grads, (((0,), (0,)), ((), ())), preferred_element_type=F32
     ).astype(BF16)
 
 
-def head_gradient(rows, mine, theirs):
-    per, depth = rows[0].shape
+def head_gradient(rows, core_rows, mine, theirs):
+    _, per, depth = rows.shape
     cols = mine.shape[1]
     tile = 512 if depth % 512 == 0 else depth
     whole = pl.BlockSpec((2 * per, cols), lambda i: (0, 0))
-    slab = pl.BlockSpec((per, tile), lambda i: (0, i))
+    slab = pl.BlockSpec((2, per, tile), lambda i: (0, 0, i))
     return pl.pallas_call(
         head_kernel,
         grid=(depth // tile,),
         out_shape=shape((depth, cols), BF16),
-        in_specs=[slab] * 4 + [whole] * 2,
+        in_specs=[slab] * 2 + [whole] * 2,
         out_specs=pl.BlockSpec((tile, cols), lambda i: (i, 0)),
         compiler_params=params(6),
         cost_estimate=cost(8 * per * depth * cols, (4 * per + cols) * depth * 2),
         name="head_gradient",
-    )(*rows, mine, theirs)
+    )(rows, core_rows, mine, theirs)
 
 
 def body(hidden, token_ids, serving, head_weight, teacher_logits):
@@ -324,7 +329,7 @@
     def ints(*values):
         return jnp.stack([jnp.asarray(v, jnp.int32) for v in values])
 
-    quarter_rows = per // 4
+    quarter_rows = per * 3 // 16
     quarter = me_v & 3
     starts = [(quarter ^ k) * quarter_rows for k in range(4)]
     chip = me_g >> 1
@@ -349,28 +354,26 @@
     x0 = swap(first, X)
     _, rows, weight, teacher = tie(first, rows, weight, teacher_logits)
     other_weight = swap(weight, CORE)
-    core_hidden = swap(rows, CORE)
     x3 = swap(cut(rows, unsigned[1], quarter_rows, 0), X)
+    rest = swap(rows[4 * quarter_rows :], X)
     kept = cut(teacher, unsigned[2], 2, 1).swapaxes(0, 1)
     gone = cut(teacher, unsigned[3], 2, 1).swapaxes(0, 1)
     taught = taught_stats(kept, gone)
     taught_core = swap(taught, CORE)
-    near_a, stats_a = near_logits(rows, weight)
-    x0, kept, gone, taught, taught_core, near_a, rows = tie(
-        x0, kept, gone, taught, taught_core, near_a, rows
-    )
+    x0, kept, gone, taught, taught_core, rows = tie(x0, kept, gone, taught, taught_core, rows)
     x1 = swap(x0, Y)
     x2 = swap(x0, W)
     kept_core = swap(kept, CORE)
+    near_a, stats_a = near_logits(rows, weight, x0)
     near_b, stats_b = near_logits(rows, other_weight, x0)
-    *pieces, gone, near_b = tie(x0, x1, x2, x3, gone, near_b)
+    *pieces, gone, near_a, near_b = tie(x0, x1, x2, x3, rest, gone, near_a, near_b)
     taught_x = swap(gone, X)
-    spots, core_hidden, kept_core = tie(spots, core_hidden, kept_core)
-    far_a, far_b, x_rows, stats = far_logits(
+    far_a, far_b, both_rows, stats = far_logits(
         spots,
         pieces,
         weight,
         other_weight,
+        rows,
         stats_a,
         stats_b,
         taught,
@@ -407,8 +410,8 @@
     )
     gots = [swap(sents[p], masks[orders[p][0]]) for p in range(3)]
     theirs = swap(gother, CORE)
-    _, x_sent = tie(gother, x_rows)
-    grad_head = head_gradient([hidden, x_rows, core_hidden, swap(x_sent, CORE)], gown, theirs)
+    _, rows_sent = tie(gother, both_rows)
+    grad_head = head_gradient(both_rows, swap(rows_sent, CORE), gown, theirs)
     for p in range(3):
         grad_head, gots[p] = tie(grad_head, gots[p])
 

time: 72.9 us -> 72 us (0.988)
  waiting for transfers between devices: 18.2 us -> 14 us
  starting transfers between devices: 32.1 us -> 35.2 us
    ppermute x30, waiting for transfers between devices: 18.2 us -> 14 us  [swap(): return lax.ppermute(value, AXES, [(i, i ^ mask) for i in range(count)])]
    ppermute x30, starting transfers between devices: 32.1 us -> 35.2 us  [swap(): return lax.ppermute(value, AXES, [(i, i ^ mask) for i in range(count)])]
    slice x0 -> x1, local copies, waits for them, and re-layouts: none -> 0.95 us  [body(): rest = swap(rows[4 * quarter_rows:], X)]
    unnamed x10, local copies, waits for them, and re-layouts: 2.06 us -> 1.2 us
  transfers between devices with their start and end apart: 30 -> 30, of which waited for: 17 -> 13; matrix products, arithmetic and copies ran while one was open for 3% -> 5% of each run, Pallas kernels for 15% -> 15%
where the time goes in v15:
time: 72 us; the launch traced here: 71.8 us
  starting transfers between devices  35.2 us (49%)
  Pallas kernels  15.1 us (21%)
  waiting for transfers between devices  14 us (19%)
  local copies, waits for them, and re-layouts  5.47 us (8%)
  other arithmetic  1.18 us (2%)
  between operations  0.84 us (1%)
    ppermute x30, starting transfers between devices, swap(): return lax.ppermute(value, AXES, [(i, i ^ mask) for i in range(count)])  35.2 us
    ppermute x30, waiting for transfers between devices, swap(): return lax.ppermute(value, AXES, [(i, i ^ mask) for i in range(count)])  14 us
    pallas_call x1, Pallas kernels, head_gradient(): pl.pallas_call(head_kernel, grid=(depth // tile,), out_shape=shape((depth...  5.21 us
    pallas_call x1, Pallas kernels, back_rows(): pl.pallas_call(lambda *refs: back_kernel(bits, edges, len(stats), *refs),...  4.39 us
    dynamic_slice x2, local copies, waits for them, and re-layouts, cut(): return lax.dynamic_slice(value, indices, sizes)  2.13 us
    pallas_call x1, Pallas kernels, far_logits(): pl.pallas_call(lambda *refs: far_kernel(len(pieces), *refs), out_shape=(s...  2.05 us
    pallas_call x2, Pallas kernels, near_logits(): pl.pallas_call(near_kernel, out_shape=(shape((per, cols), F32), shape((ST...  1.73 us
  transfers between devices with their start and end apart: 30, of which 13 were waited for; matrix products, arithmetic and copies ran while one was open for 5% of the time, Pallas kernels for 15%

profile of v15, /device:TPU:0, one launch (start us, length us, event | category | flops | bytes accessed | tf_op | source)
XLA Modules:
  0.0 71.8 jit_solution(14529646133938582480)
XLA Ops:
  0.7 0.0 copy-start
  0.7 0.1 pad_add_fusion.2.at_ref
  0.7 0.1 pad_add_fusion
  0.8 1.1 %constant_dynamic-slice_fusion.1 = bf16[24,3584]{1,0:T(8,128)(2,1)S(1)} fusion(bf16[128,3584]{1,0:T(8,128)(2,1)} %refs_8_, u32[]{:T(128)S(6)} %convert_element_type.149), kind=kLoop, calls=%fused_computation.42 | loop fusion | bytes 344068 | tf_op jit(solution)/shard_map/dynamic_slice | solution.py:351
  2.0 0.5 collective-permute-start
  2.5 2.6 %collective-permute-start.1 = (bf16[24,3584]{1,0:T(8,128)(2,1)S(1)}, bf16[24,3584]{1,0:T(8,128)(2,1)S(1)}, u32[]{:S(2)}, u32[]{:S(2)}) collective-permute-start(bf16[24,3584]{1,0:T(8,128)(2,1)S(1)} %constant_dynamic-slice_fusion.1), channel_id=1, source_target_pairs={{0,16},{1,17},{2,18},{3,19},{4,20},{5,21},{6,22},{7,23},{8,24},{9,... | collective-permute-start | bytes 516104 | tf_op jit(solution)/shard_map/ppermute | solution.py:324
  5.0 1.0 %slice.173 = bf16[32,3584]{1,0:T(8,128)(2,1)S(1)} slice(bf16[128,3584]{1,0:T(8,128)(2,1)} %refs_8_), slice={[96:128], [0:3584]} | slice | bytes 458752 | tf_op jit(solution)/shard_map/slice | solution.py:358
  6.0 0.1 collective-permute-start.6
  6.1 1.1 %copy.7 = bf16[128,4,512]{2,0,1:T(8,128)(2,1)S(1)} copy(bf16[128,4,512]{2,1,0:T(4,128)(2,1)} %param.9) | data formatting | bytes 1048576 | tf_op jit(solution)/shard_map/optimization_barrier | solution.py:327
  7.3 0.4 taught_stats.1.refs_11_
  7.6 0.2 collective-permute-start.2
  7.8 1.0 %constant_dynamic-slice_fusion = bf16[24,3584]{1,0:T(8,128)(2,1)S(1)} fusion(bf16[128,3584]{1,0:T(8,128)(2,1)} %refs_8_, u32[]{:T(128)S(6)} %convert_element_type.150), kind=kLoop, calls=%fused_computation.41 | loop fusion | bytes 344068 | tf_op jit(solution)/shard_map/dynamic_slice | solution.py:351
  8.8 1.9 %collective-permute-start.5 = (bf16[24,3584]{1,0:T(8,128)(2,1)S(1)}, bf16[24,3584]{1,0:T(8,128)(2,1)S(1)}, u32[]{:S(2)}, u32[]{:S(2)}) collective-permute-start(bf16[24,3584]{1,0:T(8,128)(2,1)S(1)} %constant_dynamic-slice_fusion), channel_id=1, source_target_pairs={{0,16},{1,17},{2,18},{3,19},{4,20},{5,21},{6,22},{7,23},{8,24},{9,... | collective-permute-start | bytes 516104 | tf_op jit(solution)/shard_map/ppermute | solution.py:324
  10.8 1.6 %collective-permute-start.4 = (bf16[24,3584]{1,0:T(8,128)(2,1)S(1)}, bf16[24,3584]{1,0:T(8,128)(2,1)S(1)}, u32[]{:S(2)}, u32[]{:S(2)}) collective-permute-start(bf16[24,3584]{1,0:T(8,128)(2,1)S(1)} %collective-permute-done.1.refs_0_.refs_1_), channel_id=1, source_target_pairs={{0,2},{1,3},{2,0},{3,1},{4,6},{5,7},{6,4},{7,5},{8,10},{9,11},{10,... | collective-permute-start | bytes 516104 | tf_op jit(solution)/shard_map/ppermute | solution.py:324
  12.4 1.5 %collective-permute-start.3 = (bf16[24,3584]{1,0:T(8,128)(2,1)S(1)}, bf16[24,3584]{1,0:T(8,128)(2,1)S(1)}, u32[]{:S(2)}, u32[]{:S(2)}) collective-permute-start(bf16[24,3584]{1,0:T(8,128)(2,1)S(1)} %collective-permute-done.1.refs_0_.refs_1_), channel_id=1, source_target_pairs={{0,1},{1,0},{2,3},{3,2},{4,5},{5,4},{6,7},{7,6},{8,9},{9,8},{10,11... | collective-permute-start | bytes 516104 | tf_op jit(solution)/shard_map/ppermute | solution.py:324
  13.9 1.2 %copy-done.1 = bf16[128,3584]{1,0:T(8,128)(2,1)S(1)} copy-done((bf16[128,3584]{1,0:T(8,128)(2,1)S(1)}, bf16[128,3584]{1,0:T(8,128)(2,1)}, u32[]{:S(2)}) %copy-start.1) | copy-done | bytes 917528
  15.1 0.9 %near_logits.2 = (f32[128,512]{1,0:T(8,128)S(1)}, f32[8,128]{1,0:T(8,128)S(1)}) custom-call(bf16[128,3584]{1,0:T(8,128)(2,1)S(1)} %copy-done.1, bf16[3584,512]{1,0:T(8,128)(2,1)S(1)} %copy-done, bf16[24,3584]{1,0:T(8,128)(2,1)S(1)} %collective-permute-done.1.refs_0_.refs_1_), custom_call_target="tpu_custom_call" | custom-call | flops 469762048 | bytes 4587520 | tf_op jit(solution)/shard_map/near_logits/pallas_call | solution.py:108
  15.9 0.9 %near_logits.3 = (f32[128,512]{1,0:T(8,128)S(1)}, f32[8,128]{1,0:T(8,128)S(1)}) custom-call(bf16[128,3584]{1,0:T(8,128)(2,1)S(1)} %copy-done.1, bf16[3584,512]{1,0:T(8,128)(2,1)S(1)} %collective-permute-done.w_ref.refs_7_.refs_2_, bf16[24,3584]{1,0:T(8,128)(2,1)S(1)} %collective-permute-done.1.refs_0_.refs_1_), custom_call_target="tpu_custom_call" | custom-call | flops 469762048 | bytes 4587520 | tf_op jit(solution)/shard_map/near_logits/pallas_call | solution.py:108
  16.8 1.8 %collective-permute-done.5.refs_4_ = bf16[24,3584]{1,0:T(8,128)(2,1)S(1)} collective-permute-done((bf16[24,3584]{1,0:T(8,128)(2,1)S(1)}, bf16[24,3584]{1,0:T(8,128)(2,1)S(1)}, u32[]{:S(2)}, u32[]{:S(2)}) %collective-permute-start.5) | collective-permute-done | bytes 172064 | tf_op jit(solution)/shard_map/ppermute | solution.py:324
  18.6 1.8 %collective-permute-start.14 = (bf16[2,128,512]{2,1,0:T(8,128)(2,1)S(1)}, bf16[2,128,512]{2,1,0:T(8,128)(2,1)S(1)}, u32[]{:S(2)}, u32[]{:S(2)}) collective-permute-start(bf16[2,128,512]{2,1,0:T(8,128)(2,1)S(1)} %get-tuple-element.84.gone_ref), channel_id=1, source_target_pairs={{0,16},{1,17},{2,18},{3,19},{4,20},{5,21},{6,22},{7,23},{8,24},{9,... | collective-permute-start | bytes 786440 | tf_op jit(solution)/shard_map/ppermute | solution.py:324
  20.5 2.1 %far_logits.1 = (f32[128,512]{1,0:T(8,128)S(1)}, f32[128,512]{1,0:T(8,128)S(1)}, bf16[2,128,3584]{2,1,0:T(8,128)(2,1)S(1)}, f32[2,8,128]{2,1,0:T(8,128)S(1)}) custom-call(s32[4]{0:T(128)S(1)} %get-tuple-element.57.refs_0_, bf16[24,3584]{1,0:T(8,128)(2,1)S(1)} %collective-permute-done.1.refs_0_.refs_1_, bf16[24,3584]{1,0:T(8,128)(2,1)S(1)} %collective-permute-done.3.refs_2_, ...), custom_call_target="tpu_custom_call" | custom-call | flops 939524096 | bytes 8257536 | tf_op jit(solution)/shard_map/far_logits/pallas_call | solution.py:157
  22.5 0.0 copy-start.3
  22.5 3.7 %collective-permute-start.9 = (f32[2,8,128]{2,1,0:T(8,128)S(1)}, f32[2,8,128]{2,1,0:T(8,128)S(1)}, u32[]{:S(2)}, u32[]{:S(2)}) collective-permute-start(f32[2,8,128]{2,1,0:T(8,128)S(1)} %get-tuple-element.77.refs_0_), channel_id=1, source_target_pairs={{0,6},{1,7},{2,4},{3,5},{4,2},{5,3},{6,0},{7,1},{8,14},{9,15},{10,... | collective-permute-start | bytes 24584 | tf_op jit(solution)/shard_map/ppermute | solution.py:324
  26.2 0.8 %collective-permute-start.7 = (f32[2,8,128]{2,1,0:T(8,128)S(1)}, f32[2,8,128]{2,1,0:T(8,128)S(1)}, u32[]{:S(2)}, u32[]{:S(2)}) collective-permute-start(f32[2,8,128]{2,1,0:T(8,128)S(1)} %get-tuple-element.77.refs_0_), channel_id=1, source_target_pairs={{0,2},{1,3},{2,0},{3,1},{4,6},{5,7},{6,4},{7,5},{8,10},{9,11},{10,... | collective-permute-start | bytes 24584 | tf_op jit(solution)/shard_map/ppermute | solution.py:324
  27.0 0.0 collective-permute-start.13
  27.0 1.1 %collective-permute-done.9.refs_3_ = f32[2,8,128]{2,1,0:T(8,128)S(1)} collective-permute-done((f32[2,8,128]{2,1,0:T(8,128)S(1)}, f32[2,8,128]{2,1,0:T(8,128)S(1)}, u32[]{:S(2)}, u32[]{:S(2)}) %collective-permute-start.9) | collective-permute-done | bytes 8224 | tf_op jit(solution)/shard_map/ppermute | solution.py:324
  28.1 2.7 %collective-permute-done.8.refs_2_ = f32[2,8,128]{2,1,0:T(8,128)S(1)} collective-permute-done((f32[2,8,128]{2,1,0:T(8,128)S(1)}, f32[2,8,128]{2,1,0:T(8,128)S(1)}, u32[]{:S(2)}, u32[]{:S(2)}) %collective-permute-start.8) | collective-permute-done | bytes 8224 | tf_op jit(solution)/shard_map/ppermute | solution.py:324
  30.8 0.0 collective-permute-done.7.refs_1_
  30.8 0.0 collective-permute-done.14.a2
  30.8 0.1 collective-permute-start.15
  30.9 1.6 %collective-permute-start.12 = (f32[2,8,128]{2,1,0:T(8,128)S(1)}, f32[2,8,128]{2,1,0:T(8,128)S(1)}, u32[]{:S(2)}, u32[]{:S(2)}) collective-permute-start(f32[2,8,128]{2,1,0:T(8,128)S(1)} %merge_stats.1.refs_3_), channel_id=1, source_target_pairs={{0,17},{1,16},{2,19},{3,18},{4,21},{5,20},{6,23},{7,22},{8,25},{9,... | collective-permute-start | bytes 24584 | tf_op jit(solution)/shard_map/ppermute | solution.py:324
  32.4 0.5 collective-permute-start.11
  32.9 1.5 %collective-permute-start.10 = (f32[2,8,128]{2,1,0:T(8,128)S(1)}, f32[2,8,128]{2,1,0:T(8,128)S(1)}, u32[]{:S(2)}, u32[]{:S(2)}) collective-permute-start(f32[2,8,128]{2,1,0:T(8,128)S(1)} %merge_stats.1.refs_3_), channel_id=1, source_target_pairs={{0,16},{1,17},{2,18},{3,19},{4,20},{5,21},{6,22},{7,23},{8,24},{9,... | collective-permute-start | bytes 24584 | tf_op jit(solution)/shard_map/ppermute | solution.py:324
  34.4 0.0 collective-permute-done.13.a1
  34.4 0.0 collective-permute-done.15.a3
  34.4 1.3 %teacher_rows.1.refs_12_ = bf16[2,128,1024]{2,1,0:T(8,128)(2,1)S(1)} custom-call(s32[2]{0:T(128)S(1)} %pad_add_fusion.2.at_ref, s32[4,1,128]{2,1,0:T(1,128)S(1)} %bitcast.42, bf16[2,128,512]{2,1,0:T(8,128)(2,1)S(1)} %get-tuple-element.83.kept_ref.a0, bf16[2,128,512]{2,1,0:T(8,128)(2,1)S(1)} %collective-permute-done.13.a1, ...), custom_call_target="tpu_custom_call" | custom-call | flops 268435456 | bytes 1572864 | tf_op jit(solution)/shard_map/teacher_rows/pallas_call | solution.py:80
  35.7 0.0 collective-permute-done.12.refs_6_
  35.7 0.4 collective-permute-done.11.refs_5_
  36.1 0.5 collective-permute-done.10.refs_4_
  36.6 4.4 %back_rows.1 = (bf16[256,512]{1,0:T(8,128)(2,1)S(1)}, bf16[256,512]{1,0:T(8,128)(2,1)S(1)}, bf16[128,1152]{1,0:T(8,128)(2,1)S(1)}, bf16[128,1152]{1,0:T(8,128)(2...) custom-call(s32[4]{0:T(128)S(1)} %get-tuple-element.52.refs_0_, ...), custom_call_target="tpu_custom_call" | custom-call | flops 1879048192 | bytes 7340032 | tf_op jit(solution)/shard_map/back_rows/pallas_call | solution.py:271
  41.0 0.1 collective-permute-start.16
  41.1 0.5 collective-permute-start.17
  41.6 0.0 collective-permute-start.26
  41.6 1.5 %collective-permute-start.18 = (bf16[128,1152]{1,0:T(8,128)(2,1)S(1)}, bf16[128,1152]{1,0:T(8,128)(2,1)S(1)}, u32[]{:S(2)}, u32[]{:S(2)}) collective-permute-start(bf16[128,1152]{1,0:T(8,128)(2,1)S(1)} %get-tuple-element.91), channel_id=1, source_target_pairs={{0,16},{1,17},{2,18},{3,19},{4,20},{5,21},{6,22},{7,23},{8,24},{9,... | collective-permute-start | bytes 884744 | tf_op jit(solution)/shard_map/ppermute | solution.py:324
  43.1 1.5 %collective-permute-start.22 = (bf16[128,1152]{1,0:T(8,128)(2,1)S(1)}, bf16[128,1152]{1,0:T(8,128)(2,1)S(1)}, u32[]{:S(2)}, u32[]{:S(2)}) collective-permute-start(bf16[128,1152]{1,0:T(8,128)(2,1)S(1)} %get-tuple-element.95), channel_id=1, source_target_pairs={{0,1},{1,0},{2,3},{3,2},{4,5},{5,4},{6,7},{7,6},{8,9},{9,8},{10,11... | collective-permute-start | bytes 884744 | tf_op jit(solution)/shard_map/ppermute | solution.py:324
  44.6 0.6 collective-permute-done.17.theirs_ref
  45.2 5.2 %head_gradient.1 = bf16[3584,512]{1,0:T(8,128)(2,1)} custom-call(bf16[2,128,3584]{2,1,0:T(8,128)(2,1)S(1)} %get-tuple-element.89.rows_ref, bf16[2,128,3584]{2,1,0:T(8,128)(2,1)S(1)} %collective-permute-done.16.core_ref, bf16[256,512]{1,0:T(8,128)(2,1)S(1)} %get-tuple-element.90.mine_ref, bf16[256,512]{1,0:T(8,128)(2,1)S(1)} %collective-permute-done.17.theirs_ref), custom_call_target="tpu_custom_call" | custom-call | flops 1879048192 | bytes 7340032 | tf_op jit(solution)/shard_map/head_gradient/pallas_call | solution.py:299
  50.4 0.1 collective-permute-done.18
  50.6 1.2 %collective-permute-done.22 = bf16[128,1152]{1,0:T(8,128)(2,1)S(1)} collective-permute-done((bf16[128,1152]{1,0:T(8,128)(2,1)S(1)}, bf16[128,1152]{1,0:T(8,128)(2,1)S(1)}, u32[]{:S(2)}, u32[]{:S(2)}) %collective-permute-start.22) | collective-permute-done | bytes 294944 | tf_op jit(solution)/shard_map/ppermute | solution.py:324
  51.8 1.6 %collective-permute-start.19 = (bf16[1,2,2,1,16,1152]{5,4,3,2,1,0:T(8,128)(2,1)S(1)}, bf16[1,2,2,1,16,1152]{5,4,3,2,1,0:T(8,128)(2,1)S(1)}, u32[]{:S(2)}, u32[]{:S(2)}) collective-permute-start(bf16[1,2,2,1,16,1152]{5,4,3,2,1,0:T(8,128)(2,1)S(1)} %fusion.1), channel_id=1, source_target_pairs={{0,1},{1,0},{2,3},{3,2},{4,5},{5,4},{6,7},{7,6},{8,9},{9,8},{10,11... | collective-permute-start | bytes 442376 | tf_op jit(solution)/shard_map/ppermute | solution.py:324
  53.5 1.8 %collective-permute-start.23 = (bf16[2,2,1,1,16,1152]{5,4,3,2,1,0:T(8,128)(2,1)S(1)}, bf16[2,2,1,1,16,1152]{5,4,3,2,1,0:T(8,128)(2,1)S(1)}, u32[]{:S(2)}, u32[]{:S(2)}) collective-permute-start(bf16[2,2,1,1,16,1152]{5,4,3,2,1,0:T(8,128)(2,1)S(1)} %fusion), channel_id=1, source_target_pairs={{0,2},{1,3},{2,0},{3,1},{4,6},{5,7},{6,4},{7,5},{8,10},{9,11},{10,... | collective-permute-start | bytes 442376 | tf_op jit(solution)/shard_map/ppermute | solution.py:324
  55.3 0.5 collective-permute-start.27
  55.8 1.2 %collective-permute-done.19 = bf16[1,2,2,1,16,1152]{5,4,3,2,1,0:T(8,128)(2,1)S(1)} collective-permute-done((bf16[1,2,2,1,16,1152]{5,4,3,2,1,0:T(8,128)(2,1)S(1)}, bf16[1,2,2,1,16,1152]{5,4,3,2,1,0:T(8,128)(2,1)S(1)}, u32[]{:S(2)}, u32[]{:S(2)}) %collective-permute-start.19) | collective-permute-done | bytes 147488 | tf_op jit(solution)/shard_map/ppermute | solution.py:324
  57.0 1.8 %collective-permute-start.20 = (bf16[1,2,1,1,16,1152]{5,4,3,2,1,0:T(8,128)(2,1)S(1)}, bf16[1,2,1,1,16,1152]{5,4,3,2,1,0:T(8,128)(2,1)S(1)}, u32[]{:S(2)}, u32[]{:S(2)}) collective-permute-start(bf16[1,2,1,1,16,1152]{5,4,3,2,1,0:T(8,128)(2,1)S(1)} %fusion.7), channel_id=1, source_target_pairs={{0,2},{1,3},{2,0},{3,1},{4,6},{5,7},{6,4},{7,5},{8,10},{9,11},{10,... | collective-permute-start | bytes 221192 | tf_op jit(solution)/shard_map/ppermute | solution.py:324
  58.8 0.6 collective-permute-done.23
  59.5 1.0 %collective-permute-start.24 = (bf16[1,2,1,1,16,1152]{5,4,3,2,1,0:T(8,128)(2,1)S(1)}, bf16[1,2,1,1,16,1152]{5,4,3,2,1,0:T(8,128)(2,1)S(1)}, u32[]{:S(2)}, u32[]{:S(2)}) collective-permute-start(bf16[1,2,1,1,16,1152]{5,4,3,2,1,0:T(8,128)(2,1)S(1)} %fusion.5), channel_id=1, source_target_pairs={{0,16},{1,17},{2,18},{3,19},{4,20},{5,21},{6,22},{7,23},{8,24},{9,... | collective-permute-start | bytes 221192 | tf_op jit(solution)/shard_map/ppermute | solution.py:324
  60.6 0.8 %collective-permute-done.27 = bf16[1,2,1,2,16,1280]{5,4,3,2,1,0:T(8,128)(2,1)S(1)} collective-permute-done((bf16[1,2,1,2,16,1280]{5,4,3,2,1,0:T(8,128)(2,1)S(1)}, bf16[1,2,1,2,16,1280]{5,4,3,2,1,0:T(8,128)(2,1)S(1)}, u32[]{:S(2)}, u32[]{:S(2)}) %collective-permute-start.27) | collective-permute-done | bytes 163872 | tf_op jit(solution)/shard_map/ppermute | solution.py:324
  61.4 0.6 collective-permute-start.28
  62.0 2.1 %collective-permute-start.21 = (bf16[1,1,1,1,16,1152]{5,4,3,2,1,0:T(8,128)(2,1)S(1)}, bf16[1,1,1,1,16,1152]{5,4,3,2,1,0:T(8,128)(2,1)S(1)}, u32[]{:S(2)}, u32[]{:S(2)}) collective-permute-start(bf16[1,1,1,1,16,1152]{5,4,3,2,1,0:T(8,128)(2,1)S(1)} %fusion.22), channel_id=1, source_target_pairs={{0,4},{1,5},{2,6},{3,7},{4,0},{5,1},{6,2},{7,3},{8,12},{9,13},{10,... | collective-permute-start | bytes 110600 | tf_op jit(solution)/shard_map/ppermute | solution.py:324
  64.2 1.9 %collective-permute-start.25 = (bf16[1,1,1,1,16,1152]{5,4,3,2,1,0:T(8,128)(2,1)S(1)}, bf16[1,1,1,1,16,1152]{5,4,3,2,1,0:T(8,128)(2,1)S(1)}, u32[]{:S(2)}, u32[]{:S(2)}) collective-permute-start(bf16[1,1,1,1,16,1152]{5,4,3,2,1,0:T(8,128)(2,1)S(1)} %fusion.16), channel_id=1, source_target_pairs={{0,4},{1,5},{2,6},{3,7},{4,0},{5,1},{6,2},{7,3},{8,12},{9,13},{10,... | collective-permute-start | bytes 110600 | tf_op jit(solution)/shard_map/ppermute | solution.py:324
  66.1 2.0 %collective-permute-start.29 = (bf16[1,1,1,1,16,1280]{5,4,3,2,1,0:T(8,128)(2,1)S(1)}, bf16[1,1,1,1,16,1280]{5,4,3,2,1,0:T(8,128)(2,1)S(1)}, u32[]{:S(2)}, u32[]{:S(2)}) collective-permute-start(bf16[1,1,1,1,16,1280]{5,4,3,2,1,0:T(8,128)(2,1)S(1)} %fusion.10), channel_id=1, source_target_pairs={{0,4},{1,5},{2,6},{3,7},{4,0},{5,1},{6,2},{7,3},{8,12},{9,13},{10,... | collective-permute-start | bytes 122888 | tf_op jit(solution)/shard_map/ppermute | solution.py:324
  68.1 1.0 %collective-permute-done.25 = bf16[1,1,1,1,16,1152]{5,4,3,2,1,0:T(8,128)(2,1)S(1)} collective-permute-done((bf16[1,1,1,1,16,1152]{5,4,3,2,1,0:T(8,128)(2,1)S(1)}, bf16[1,1,1,1,16,1152]{5,4,3,2,1,0:T(8,128)(2,1)S(1)}, u32[]{:S(2)}, u32[]{:S(2)}) %collective-permute-start.25) | collective-permute-done | bytes 36896 | tf_op jit(solution)/shard_map/ppermute | solution.py:324
  69.1 1.9 %collective-permute-done.29 = bf16[1,1,1,1,16,1280]{5,4,3,2,1,0:T(8,128)(2,1)S(1)} collective-permute-done((bf16[1,1,1,1,16,1280]{5,4,3,2,1,0:T(8,128)(2,1)S(1)}, bf16[1,1,1,1,16,1280]{5,4,3,2,1,0:T(8,128)(2,1)S(1)}, u32[]{:S(2)}, u32[]{:S(2)}) %collective-permute-start.29) | collective-permute-done | bytes 40992 | tf_op jit(solution)/shard_map/ppermute | solution.py:324
  71.1 0.7 maximum_bitcast_fusion
  (35 shorter events, 0.5 us)
Async XLA Ops:
  0.7 13.2 %copy-start = (bf16[3584,512]{1,0:T(8,128)(2,1)S(1)}, bf16[3584,512]{1,0:T(8,128)(2,1)}, u32[]{:S(2)}) copy-start(bf16[3584,512]{1,0:T(8,128)(2,1)} %refs_1_) | copy-start | bytes 11010052
  2.0 14.0 %collective-permute-start = (bf16[3584,512]{1,0:T(8,128)(2,1)}, bf16[3584,512]{1,0:T(8,128)(2,1)S(1)}, u32[]{:S(2)}, u32[]{:S(2)}) collective-permute-start(bf16[3584,512]{1,0:T(8,128)(2,1)} %refs_1_), channel_id=1, source_target_pairs={{0,8},{1,9},{2,10},{3,11},{4,12},{5,13},{6,14},{7,15},{8,0},{9,1},... | collective-permute-start | bytes 11010056 | tf_op jit(solution)/shard_map/ppermute | solution.py:324
  2.5 8.3 %collective-permute-start.1 = (bf16[24,3584]{1,0:T(8,128)(2,1)S(1)}, bf16[24,3584]{1,0:T(8,128)(2,1)S(1)}, u32[]{:S(2)}, u32[]{:S(2)}) collective-permute-start(bf16[24,3584]{1,0:T(8,128)(2,1)S(1)} %constant_dynamic-slice_fusion.1), channel_id=1, source_target_pairs={{0,16},{1,17},{2,18},{3,19},{4,20},{5,21},{6,22},{7,23},{8,24},{9,... | collective-permute-start | bytes 516104 | tf_op jit(solution)/shard_map/ppermute | solution.py:324
  6.0 12.6 %collective-permute-start.6 = (bf16[32,3584]{1,0:T(8,128)(2,1)S(1)}, bf16[32,3584]{1,0:T(8,128)(2,1)S(1)}, u32[]{:S(2)}, u32[]{:S(2)}) collective-permute-start(bf16[32,3584]{1,0:T(8,128)(2,1)S(1)} %slice.173), channel_id=1, source_target_pairs={{0,16},{1,17},{2,18},{3,19},{4,20},{5,21},{6,22},{7,23},{8,24},{9,... | collective-permute-start | bytes 688136 | tf_op jit(solution)/shard_map/ppermute | solution.py:324
  7.6 3.1 %collective-permute-start.2 = (f32[8,128]{1,0:T(8,128)S(1)}, f32[8,128]{1,0:T(8,128)S(1)}, u32[]{:S(2)}, u32[]{:S(2)}) collective-permute-start(f32[8,128]{1,0:T(8,128)S(1)} %taught_stats.1.refs_11_), channel_id=1, source_target_pairs={{0,8},{1,9},{2,10},{3,11},{4,12},{5,13},{6,14},{7,15},{8,0},{9,1},... | collective-permute-start | bytes 12296 | tf_op jit(solution)/shard_map/ppermute | solution.py:324
  7.8 12.6 %copy-start.4 = (s32[128]{0:T(128)S(1)}, s32[128]{0:T(128)}, u32[]{:S(2)}) copy-start(s32[128]{0:T(128)} %param.6) | copy-start | bytes 1540
  8.8 9.8 %collective-permute-start.5 = (bf16[24,3584]{1,0:T(8,128)(2,1)S(1)}, bf16[24,3584]{1,0:T(8,128)(2,1)S(1)}, u32[]{:S(2)}, u32[]{:S(2)}) collective-permute-start(bf16[24,3584]{1,0:T(8,128)(2,1)S(1)} %constant_dynamic-slice_fusion), channel_id=1, source_target_pairs={{0,16},{1,17},{2,18},{3,19},{4,20},{5,21},{6,22},{7,23},{8,24},{9,... | collective-permute-start | bytes 516104 | tf_op jit(solution)/shard_map/ppermute | solution.py:324
  10.8 7.8 %collective-permute-start.4 = (bf16[24,3584]{1,0:T(8,128)(2,1)S(1)}, bf16[24,3584]{1,0:T(8,128)(2,1)S(1)}, u32[]{:S(2)}, u32[]{:S(2)}) collective-permute-start(bf16[24,3584]{1,0:T(8,128)(2,1)S(1)} %collective-permute-done.1.refs_0_.refs_1_), channel_id=1, source_target_pairs={{0,2},{1,3},{2,0},{3,1},{4,6},{5,7},{6,4},{7,5},{8,10},{9,11},{10,... | collective-permute-start | bytes 516104 | tf_op jit(solution)/shard_map/ppermute | solution.py:324
  12.4 6.3 %collective-permute-start.3 = (bf16[24,3584]{1,0:T(8,128)(2,1)S(1)}, bf16[24,3584]{1,0:T(8,128)(2,1)S(1)}, u32[]{:S(2)}, u32[]{:S(2)}) collective-permute-start(bf16[24,3584]{1,0:T(8,128)(2,1)S(1)} %collective-permute-done.1.refs_0_.refs_1_), channel_id=1, source_target_pairs={{0,1},{1,0},{2,3},{3,2},{4,5},{5,4},{6,7},{7,6},{8,9},{9,8},{10,11... | collective-permute-start | bytes 516104 | tf_op jit(solution)/shard_map/ppermute | solution.py:324
  13.9 1.2 %copy-start.1 = (bf16[128,3584]{1,0:T(8,128)(2,1)S(1)}, bf16[128,3584]{1,0:T(8,128)(2,1)}, u32[]{:S(2)}) copy-start(bf16[128,3584]{1,0:T(8,128)(2,1)} %refs_8_) | copy-start | bytes 2752516
  15.1 5.4 %copy-start.2 = (bf16[128,3584]{1,0:T(8,128)(2,1)S(1)}, bf16[128,3584]{1,0:T(8,128)(2,1)}, u32[]{:S(2)}) copy-start(bf16[128,3584]{1,0:T(8,128)(2,1)} %refs_8_) | copy-start | bytes 2752516
  18.6 12.2 %collective-permute-start.14 = (bf16[2,128,512]{2,1,0:T(8,128)(2,1)S(1)}, bf16[2,128,512]{2,1,0:T(8,128)(2,1)S(1)}, u32[]{:S(2)}, u32[]{:S(2)}) collective-permute-start(bf16[2,128,512]{2,1,0:T(8,128)(2,1)S(1)} %get-tuple-element.84.gone_ref), channel_id=1, source_target_pairs={{0,16},{1,17},{2,18},{3,19},{4,20},{5,21},{6,22},{7,23},{8,24},{9,... | collective-permute-start | bytes 786440 | tf_op jit(solution)/shard_map/ppermute | solution.py:324
  22.5 11.9 %copy-start.3 = (s32[512]{0:T(512)S(1)}, s32[512]{0:T(512)}, u32[]{:S(2)}) copy-start(s32[512]{0:T(512)} %param.7) | copy-start | bytes 6148
  22.5 5.5 %collective-permute-start.9 = (f32[2,8,128]{2,1,0:T(8,128)S(1)}, f32[2,8,128]{2,1,0:T(8,128)S(1)}, u32[]{:S(2)}, u32[]{:S(2)}) collective-permute-start(f32[2,8,128]{2,1,0:T(8,128)S(1)} %get-tuple-element.77.refs_0_), channel_id=1, source_target_pairs={{0,6},{1,7},{2,4},{3,5},{4,2},{5,3},{6,0},{7,1},{8,14},{9,15},{10,... | collective-permute-start | bytes 24584 | tf_op jit(solution)/shard_map/ppermute | solution.py:324
  26.2 4.5 %collective-permute-start.8 = (f32[2,8,128]{2,1,0:T(8,128)S(1)}, f32[2,8,128]{2,1,0:T(8,128)S(1)}, u32[]{:S(2)}, u32[]{:S(2)}) collective-permute-start(f32[2,8,128]{2,1,0:T(8,128)S(1)} %get-tuple-element.77.refs_0_), channel_id=1, source_target_pairs={{0,4},{1,5},{2,6},{3,7},{4,0},{5,1},{6,2},{7,3},{8,12},{9,13},{10,... | collective-permute-start | bytes 24584 | tf_op jit(solution)/shard_map/ppermute | solution.py:324
  26.2 4.5 %collective-permute-start.7 = (f32[2,8,128]{2,1,0:T(8,128)S(1)}, f32[2,8,128]{2,1,0:T(8,128)S(1)}, u32[]{:S(2)}, u32[]{:S(2)}) collective-permute-start(f32[2,8,128]{2,1,0:T(8,128)S(1)} %get-tuple-element.77.refs_0_), channel_id=1, source_target_pairs={{0,2},{1,3},{2,0},{3,1},{4,6},{5,7},{6,4},{7,5},{8,10},{9,11},{10,... | collective-permute-start | bytes 24584 | tf_op jit(solution)/shard_map/ppermute | solution.py:324
  27.0 7.5 %collective-permute-start.13 = (bf16[2,128,512]{2,1,0:T(8,128)(2,1)S(1)}, bf16[2,128,512]{2,1,0:T(8,128)(2,1)S(1)}, u32[]{:S(2)}, u32[]{:S(2)}) collective-permute-start(bf16[2,128,512]{2,1,0:T(8,128)(2,1)S(1)} %get-tuple-element.83.kept_ref.a0), channel_id=1, source_target_pairs={{0,8},{1,9},{2,10},{3,11},{4,12},{5,13},{6,14},{7,15},{8,0},{9,1},... | collective-permute-start | bytes 786440 | tf_op jit(solution)/shard_map/ppermute | solution.py:324
  30.8 3.6 %collective-permute-start.15 = (bf16[2,128,512]{2,1,0:T(8,128)(2,1)S(1)}, bf16[2,128,512]{2,1,0:T(8,128)(2,1)S(1)}, u32[]{:S(2)}, u32[]{:S(2)}) collective-permute-start(bf16[2,128,512]{2,1,0:T(8,128)(2,1)S(1)} %collective-permute-done.14.a2), channel_id=1, source_target_pairs={{0,8},{1,9},{2,10},{3,11},{4,12},{5,13},{6,14},{7,15},{8,0},{9,1},... | collective-permute-start | bytes 786440 | tf_op jit(solution)/shard_map/ppermute | solution.py:324
  30.9 4.8 %collective-permute-start.12 = (f32[2,8,128]{2,1,0:T(8,128)S(1)}, f32[2,8,128]{2,1,0:T(8,128)S(1)}, u32[]{:S(2)}, u32[]{:S(2)}) collective-permute-start(f32[2,8,128]{2,1,0:T(8,128)S(1)} %merge_stats.1.refs_3_), channel_id=1, source_target_pairs={{0,17},{1,16},{2,19},{3,18},{4,21},{5,20},{6,23},{7,22},{8,25},{9,... | collective-permute-start | bytes 24584 | tf_op jit(solution)/shard_map/ppermute | solution.py:324
  32.4 3.7 %collective-permute-start.11 = (f32[2,8,128]{2,1,0:T(8,128)S(1)}, f32[2,8,128]{2,1,0:T(8,128)S(1)}, u32[]{:S(2)}, u32[]{:S(2)}) collective-permute-start(f32[2,8,128]{2,1,0:T(8,128)S(1)} %merge_stats.1.refs_3_), channel_id=1, source_target_pairs={{0,1},{1,0},{2,3},{3,2},{4,5},{5,4},{6,7},{7,6},{8,9},{9,8},{10,11... | collective-permute-start | bytes 24584 | tf_op jit(solution)/shard_map/ppermute | solution.py:324
  32.9 3.7 %collective-permute-start.10 = (f32[2,8,128]{2,1,0:T(8,128)S(1)}, f32[2,8,128]{2,1,0:T(8,128)S(1)}, u32[]{:S(2)}, u32[]{:S(2)}) collective-permute-start(f32[2,8,128]{2,1,0:T(8,128)S(1)} %merge_stats.1.refs_3_), channel_id=1, source_target_pairs={{0,16},{1,17},{2,18},{3,19},{4,20},{5,21},{6,22},{7,23},{8,24},{9,... | collective-permute-start | bytes 24584 | tf_op jit(solution)/shard_map/ppermute | solution.py:324
  41.0 4.2 %collective-permute-start.16 = (bf16[2,128,3584]{2,1,0:T(8,128)(2,1)S(1)}, bf16[2,128,3584]{2,1,0:T(8,128)(2,1)S(1)}, u32[]{:S(2)}, u32[]{:S(2)}) collective-permute-start(bf16[2,128,3584]{2,1,0:T(8,128)(2,1)S(1)} %get-tuple-element.89.rows_ref), channel_id=1, source_target_pairs={{0,8},{1,9},{2,10},{3,11},{4,12},{5,13},{6,14},{7,15},{8,0},{9,1},... | collective-permute-start | bytes 5505032 | tf_op jit(solution)/shard_map/ppermute | solution.py:324
  41.1 4.1 %collective-permute-start.17 = (bf16[256,512]{1,0:T(8,128)(2,1)S(1)}, bf16[256,512]{1,0:T(8,128)(2,1)S(1)}, u32[]{:S(2)}, u32[]{:S(2)}) collective-permute-start(bf16[256,512]{1,0:T(8,128)(2,1)S(1)} %get-tuple-element.88), channel_id=1, source_target_pairs={{0,8},{1,9},{2,10},{3,11},{4,12},{5,13},{6,14},{7,15},{8,0},{9,1},... | collective-permute-start | bytes 786440 | tf_op jit(solution)/shard_map/ppermute | solution.py:324
  41.6 10.2 %collective-permute-start.26 = (bf16[128,1280]{1,0:T(8,128)(2,1)S(1)}, bf16[128,1280]{1,0:T(8,128)(2,1)S(1)}, u32[]{:S(2)}, u32[]{:S(2)}) collective-permute-start(bf16[128,1280]{1,0:T(8,128)(2,1)S(1)} %get-tuple-element.99), channel_id=1, source_target_pairs={{0,2},{1,3},{2,0},{3,1},{4,6},{5,7},{6,4},{7,5},{8,10},{9,11},{10,... | collective-permute-start | bytes 983048 | tf_op jit(solution)/shard_map/ppermute | solution.py:324
  41.6 9.0 %collective-permute-start.18 = (bf16[128,1152]{1,0:T(8,128)(2,1)S(1)}, bf16[128,1152]{1,0:T(8,128)(2,1)S(1)}, u32[]{:S(2)}, u32[]{:S(2)}) collective-permute-start(bf16[128,1152]{1,0:T(8,128)(2,1)S(1)} %get-tuple-element.91), channel_id=1, source_target_pairs={{0,16},{1,17},{2,18},{3,19},{4,20},{5,21},{6,22},{7,23},{8,24},{9,... | collective-permute-start | bytes 884744 | tf_op jit(solution)/shard_map/ppermute | solution.py:324
  43.1 8.7 %collective-permute-start.22 = (bf16[128,1152]{1,0:T(8,128)(2,1)S(1)}, bf16[128,1152]{1,0:T(8,128)(2,1)S(1)}, u32[]{:S(2)}, u32[]{:S(2)}) collective-permute-start(bf16[128,1152]{1,0:T(8,128)(2,1)S(1)} %get-tuple-element.95), channel_id=1, source_target_pairs={{0,1},{1,0},{2,3},{3,2},{4,5},{5,4},{6,7},{7,6},{8,9},{9,8},{10,11... | collective-permute-start | bytes 884744 | tf_op jit(solution)/shard_map/ppermute | solution.py:324
  51.8 5.2 %collective-permute-start.19 = (bf16[1,2,2,1,16,1152]{5,4,3,2,1,0:T(8,128)(2,1)S(1)}, bf16[1,2,2,1,16,1152]{5,4,3,2,1,0:T(8,128)(2,1)S(1)}, u32[]{:S(2)}, u32[]{:S(2)}) collective-permute-start(bf16[1,2,2,1,16,1152]{5,4,3,2,1,0:T(8,128)(2,1)S(1)} %fusion.1), channel_id=1, source_target_pairs={{0,1},{1,0},{2,3},{3,2},{4,5},{5,4},{6,7},{7,6},{8,9},{9,8},{10,11... | collective-permute-start | bytes 442376 | tf_op jit(solution)/shard_map/ppermute | solution.py:324
  53.5 6.0 %collective-permute-start.23 = (bf16[2,2,1,1,16,1152]{5,4,3,2,1,0:T(8,128)(2,1)S(1)}, bf16[2,2,1,1,16,1152]{5,4,3,2,1,0:T(8,128)(2,1)S(1)}, u32[]{:S(2)}, u32[]{:S(2)}) collective-permute-start(bf16[2,2,1,1,16,1152]{5,4,3,2,1,0:T(8,128)(2,1)S(1)} %fusion), channel_id=1, source_target_pairs={{0,2},{1,3},{2,0},{3,1},{4,6},{5,7},{6,4},{7,5},{8,10},{9,11},{10,... | collective-permute-start | bytes 442376 | tf_op jit(solution)/shard_map/ppermute | solution.py:324
  55.3 6.1 %collective-permute-start.27 = (bf16[1,2,1,2,16,1280]{5,4,3,2,1,0:T(8,128)(2,1)S(1)}, bf16[1,2,1,2,16,1280]{5,4,3,2,1,0:T(8,128)(2,1)S(1)}, u32[]{:S(2)}, u32[]{:S(2)}) collective-permute-start(bf16[1,2,1,2,16,1280]{5,4,3,2,1,0:T(8,128)(2,1)S(1)} %bitcast.59), channel_id=1, source_target_pairs={{0,16},{1,17},{2,18},{3,19},{4,20},{5,21},{6,22},{7,23},{8,24},{9,... | collective-permute-start | bytes 491528 | tf_op jit(solution)/shard_map/ppermute | solution.py:324
  57.0 5.0 %collective-permute-start.20 = (bf16[1,2,1,1,16,1152]{5,4,3,2,1,0:T(8,128)(2,1)S(1)}, bf16[1,2,1,1,16,1152]{5,4,3,2,1,0:T(8,128)(2,1)S(1)}, u32[]{:S(2)}, u32[]{:S(2)}) collective-permute-start(bf16[1,2,1,1,16,1152]{5,4,3,2,1,0:T(8,128)(2,1)S(1)} %fusion.7), channel_id=1, source_target_pairs={{0,2},{1,3},{2,0},{3,1},{4,6},{5,7},{6,4},{7,5},{8,10},{9,11},{10,... | collective-permute-start | bytes 221192 | tf_op jit(solution)/shard_map/ppermute | solution.py:324
  59.5 4.6 %collective-permute-start.24 = (bf16[1,2,1,1,16,1152]{5,4,3,2,1,0:T(8,128)(2,1)S(1)}, bf16[1,2,1,1,16,1152]{5,4,3,2,1,0:T(8,128)(2,1)S(1)}, u32[]{:S(2)}, u32[]{:S(2)}) collective-permute-start(bf16[1,2,1,1,16,1152]{5,4,3,2,1,0:T(8,128)(2,1)S(1)} %fusion.5), channel_id=1, source_target_pairs={{0,16},{1,17},{2,18},{3,19},{4,20},{5,21},{6,22},{7,23},{8,24},{9,... | collective-permute-start | bytes 221192 | tf_op jit(solution)/shard_map/ppermute | solution.py:324
  61.4 4.6 %collective-permute-start.28 = (bf16[1,2,1,1,16,1280]{5,4,3,2,1,0:T(8,128)(2,1)S(1)}, bf16[1,2,1,1,16,1280]{5,4,3,2,1,0:T(8,128)(2,1)S(1)}, u32[]{:S(2)}, u32[]{:S(2)}) collective-permute-start(bf16[1,2,1,1,16,1280]{5,4,3,2,1,0:T(8,128)(2,1)S(1)} %fusion.3), channel_id=1, source_target_pairs={{0,1},{1,0},{2,3},{3,2},{4,5},{5,4},{6,7},{7,6},{8,9},{9,8},{10,11... | collective-permute-start | bytes 245768 | tf_op jit(solution)/shard_map/ppermute | solution.py:324
  62.0 6.0 %collective-permute-start.21 = (bf16[1,1,1,1,16,1152]{5,4,3,2,1,0:T(8,128)(2,1)S(1)}, bf16[1,1,1,1,16,1152]{5,4,3,2,1,0:T(8,128)(2,1)S(1)}, u32[]{:S(2)}, u32[]{:S(2)}) collective-permute-start(bf16[1,1,1,1,16,1152]{5,4,3,2,1,0:T(8,128)(2,1)S(1)} %fusion.22), channel_id=1, source_target_pairs={{0,4},{1,5},{2,6},{3,7},{4,0},{5,1},{6,2},{7,3},{8,12},{9,13},{10,... | collective-permute-start | bytes 110600 | tf_op jit(solution)/shard_map/ppermute | solution.py:324
  64.2 4.9 %collective-permute-start.25 = (bf16[1,1,1,1,16,1152]{5,4,3,2,1,0:T(8,128)(2,1)S(1)}, bf16[1,1,1,1,16,1152]{5,4,3,2,1,0:T(8,128)(2,1)S(1)}, u32[]{:S(2)}, u32[]{:S(2)}) collective-permute-start(bf16[1,1,1,1,16,1152]{5,4,3,2,1,0:T(8,128)(2,1)S(1)} %fusion.16), channel_id=1, source_target_pairs={{0,4},{1,5},{2,6},{3,7},{4,0},{5,1},{6,2},{7,3},{8,12},{9,13},{10,... | collective-permute-start | bytes 110600 | tf_op jit(solution)/shard_map/ppermute | solution.py:324
  66.1 5.0 %collective-permute-start.29 = (bf16[1,1,1,1,16,1280]{5,4,3,2,1,0:T(8,128)(2,1)S(1)}, bf16[1,1,1,1,16,1280]{5,4,3,2,1,0:T(8,128)(2,1)S(1)}, u32[]{:S(2)}, u32[]{:S(2)}) collective-permute-start(bf16[1,1,1,1,16,1280]{5,4,3,2,1,0:T(8,128)(2,1)S(1)} %fusion.10), channel_id=1, source_target_pairs={{0,4},{1,5},{2,6},{3,7},{4,0},{5,1},{6,2},{7,3},{8,12},{9,13},{10,... | collective-permute-start | bytes 122888 | tf_op jit(solution)/shard_map/ppermute | solution.py:324

commit v16 on v15

--- a/solution.py
+++ b/solution.py
@@ -58,7 +58,7 @@
     )(kept, gone)
 
 
-def teacher_kernel(at_ref, serving_ref, a0, a1, a2, a3, aligned_ref):
+def teacher_kernel(at_ref, serving_ref, a0, a1, a2, a3, soft_ref, peaks_ref):
     me, core = at_ref[0], at_ref[1]
     _, per, cols = a0.shape
     for j in range(2):
@@ -71,19 +71,21 @@
                 sums[c] += lax.dot_general(
                     pick, arrived[core ^ c], (((0,), (0,)), ((), ())), preferred_element_type=F32
                 )
+        peak = jnp.max(jnp.maximum(*sums), axis=1, keepdims=True)
         for c in range(2):
-            aligned_ref[j, :, c * cols : (c + 1) * cols] = sums[c].astype(BF16)
+            soft_ref[j, :, c * cols : (c + 1) * cols] = jnp.exp((sums[c] - peak) * 0.5)
+        peaks_ref[j] = columns_to_rows([peak])
 
 
 def teacher_rows(at, serving, arrived):
     _, per, cols = arrived[0].shape
     return pl.pallas_call(
         teacher_kernel,
-        out_shape=shape((2, per, 2 * cols), BF16),
+        out_shape=(shape((2, per, 2 * cols), F32), shape((2, STAT_ROWS, per), F32)),
         in_specs=[SMEM] + [VMEM] * 5,
-        out_specs=VMEM,
-        compiler_params=params(5),
-        cost_estimate=cost(32 * per * per * cols, 12 * per * cols * 2),
+        out_specs=(VMEM, VMEM),
+        compiler_params=params(8),
+        cost_estimate=cost(32 * per * per * cols, 12 * per * cols * 2, 4 * per * cols),
         name="teacher_rows",
     )(at, serving, *arrived)
 
@@ -92,14 +94,13 @@
     peak = jnp.max(logits, axis=1, keepdims=True)
     soft = jnp.exp((logits - peak) * 0.5)
     hard = jnp.sum(soft * soft, axis=1, keepdims=True)
-    return columns_to_rows([peak, hard, jnp.sum(soft, axis=1, keepdims=True)])
+    return soft, columns_to_rows([peak, hard, jnp.sum(soft, axis=1, keepdims=True)])
 
 
 def near_kernel(rows_ref, w_ref, *refs):
     logits_ref, stats_ref = refs[-2:]
     logits = jnp.dot(rows_ref[...], w_ref[...], preferred_element_type=F32)
-    logits_ref[...] = logits
-    stats_ref[...] = student_stats(logits)
+    logits_ref[...], stats_ref[...] = student_stats(logits)
 
 
 def near_logits(rows, weight, *held):
@@ -130,7 +131,7 @@
 def far_kernel(n, spots_ref, *refs):
     pieces, refs = refs[:n], refs[n:]
     own_ref, other_ref, near_ref, stats_a, stats_b, taught_ref, taught_core_ref, ids_ref = refs[:8]
-    a_ref, b_ref, rows_ref, out_ref, full = refs[8:]
+    a_ref, b_ref, rows_ref, out_ref, peaks_ref, full = refs[8:]
     share = pieces[0].shape[0]
     for k, piece in enumerate(pieces[:-1]):
         full[pl.ds(pl.multiple_of(spots_ref[k], 8), share), :] = piece[...].astype(F32)
@@ -140,13 +141,16 @@
     per = rows_ref.shape[1]
     a = jnp.dot(rows_ref[1], own_ref[...], preferred_element_type=F32)
     b = jnp.dot(rows_ref[1], other_ref[...], preferred_element_type=F32)
-    a_ref[...] = a
-    b_ref[...] = b
+    a_ref[...], a = student_stats(a)
+    b_ref[...], b = student_stats(b)
+    peaks_ref[...] = jnp.concatenate(
+        [stats_a[0:1], stats_b[0:1], a[0:1], b[0:1], jnp.zeros((STAT_ROWS - 4, per), F32)]
+    )
     out_ref[0, 0:3, :] = both(stats_a[...], stats_b[...])
     out_ref[0, 3:4, :] = ids_ref[...].astype(F32)
     out_ref[0, 4:6, :] = taught_ref[0:2, :]
     out_ref[0, 6:8, :] = taught_core_ref[0:2, :]
-    out_ref[1, 0:3, :] = both(student_stats(a), student_stats(b))
+    out_ref[1, 0:3, :] = both(a, b)
     row = lax.broadcasted_iota(jnp.int32, (5, per), 0)
     out_ref[1, 3:8, :] = jnp.where((row == 1) | (row == 3), NOTHING, 0.0)
 
@@ -161,9 +165,10 @@
             shape((per, cols), F32),
             shape((2, per, depth), BF16),
             shape((2, STAT_ROWS, per), F32),
+            shape((STAT_ROWS, per), F32),
         ),
         in_specs=[SMEM] + [VMEM] * (len(pieces) + 2 + len(small)),
-        out_specs=(VMEM, VMEM, VMEM, VMEM),
+        out_specs=(VMEM,) * 5,
         scratch_shapes=[pltpu.VMEM((per, depth), F32)],
         compiler_params=params(16),
         cost_estimate=cost(4 * per * depth * cols, (per + 2 * cols) * depth * 2, 2 * per * cols),
@@ -215,15 +220,19 @@
 
 def grads_kernel(n, at_ref, *refs):
     stats_refs, refs = refs[:n], refs[n:]
-    logits_refs, (serving_ref, aligned_ref), g_refs = refs[:4], refs[4:6], refs[6:]
+    soft_refs, (peaks_ref, serving_ref, taught_ref, tpeaks_ref), g_refs = refs[:4], refs[4:8], refs[8:]
     me = at_ref[3]
-    per, cols = logits_refs[0].shape
+    per, cols = soft_refs[0].shape
     stats = [merged([ref[j ^ (i & 1)] for i, ref in enumerate(stats_refs)]) for j in range(2)]
     lane = lax.broadcasted_iota(jnp.int32, (per, per), 1)
     for j in range(2):
-        rows = stats[j][:4] + (serving_ref[me ^ (2 * j)].astype(F32),)
-        columns = jnp.concatenate(rows + (jnp.zeros((128 - len(rows), per), F32),)).T
-        peak, hard, soft, ids, wanted = [columns[:, i : i + 1] for i in range(len(rows))]
+        rows = stats[j][:4] + (
+            serving_ref[me ^ (2 * j)].astype(F32),
+            tpeaks_ref[j, 0:1, :],
+            peaks_ref[2 * j : 2 * j + 2, :],
+        )
+        columns = jnp.concatenate(rows + (jnp.zeros((128 - 8, per), F32),)).T
+        peak, hard, soft, ids, wanted, tlocal, *local = [columns[:, i : i + 1] for i in range(8)]
         ids, wanted = ids.astype(jnp.int32), wanted.astype(jnp.int32)
         tpeak = total = 0.0
         for k in range(4):
@@ -233,26 +242,40 @@
             total += jnp.where(here, taught[1], 0.0)
         tpeak = jnp.sum(tpeak, axis=1, keepdims=True)
         total = jnp.sum(total, axis=1, keepdims=True)
-        hard, soft, total = 16.0 / hard, 32.0 / soft, 32.0 / total
+        teach = jnp.exp((tlocal - tpeak) * 0.5) * (32.0 / total)
+        hard, soft = 16.0 / hard, 32.0 / soft
         for c, g_ref in enumerate(g_refs):
             part = slice(c * cols, (c + 1) * cols)
             column = at_ref[1 + c] + lax.broadcasted_iota(jnp.int32, (per, cols), 1)
-            half = jnp.exp((logits_refs[2 * j + c][...] - peak) * 0.5)
-            taught = jnp.exp((aligned_ref[j, :, part].astype(F32) - tpeak) * 0.5)
+            scale = jnp.exp((local[c] - peak) * 0.5)
+            own = soft_refs[2 * j + c][...]
             label = jnp.where(column == ids, 16.0, 0.0)
-            grad = (half * soft - taught * total) + (half * half * hard - label)
-            g_ref[j * per : (j + 1) * per, :] = grad.astype(BF16)
-
-
-def back_kernel(bits, edges, n, at_ref, *refs):
-    w_refs, g_refs, send_refs, keep_refs = refs[:2], refs[-8:-6], refs[-6:-3], refs[-3:]
-    grads_kernel(n, at_ref, *refs[2:-6])
+            grad = own * (scale * soft + own * (scale * scale * hard)) - taught_ref[j, :, part] * teach
+            g_ref[j * per : (j + 1) * per, :] = (grad - label).astype(BF16)
+
+
+def back_kernel(bits, edges, low, n, at_ref, *refs):
+    w_refs, refs, mixed = refs[:2], refs[2:-1], refs[-1]
+    g_refs, send_refs, keep_refs = refs[-8:-6], refs[-6:-3], refs[-3:]
+    grads_kernel(n, at_ref, *refs[:-6])
+    total = mixed.shape[1]
+    per = total // 2
+    aligned = (1 << low) % 16 == 0
+    if aligned:
+        row = lax.broadcasted_iota(jnp.int32, (total, total), 0)
+        turn = lax.broadcasted_iota(jnp.int32, (total, total), 1) == (row ^ at_ref[0])
+        for c, g_ref in enumerate(g_refs):
+            mixed[c] = jnp.dot(turn.astype(BF16), g_ref[...], preferred_element_type=F32).astype(BF16)
     for p in range(3):
-        per = send_refs[p].shape[0]
-        pick = picker(bits[p], at_ref[0], 2 * per)
         back = 0.0
-        for g_ref, w_ref in zip(g_refs, w_refs):
-            rows = jnp.dot(pick, g_ref[...], preferred_element_type=F32).astype(BF16)
+        for c, (g_ref, w_ref) in enumerate(zip(g_refs, w_refs)):
+            if aligned:
+                run = 1 << bits[p]
+                starts = [i for side in (run, 0) for i in range(side, total, 2 * run)]
+                rows = jnp.concatenate([mixed[c, i : i + run, :] for i in starts])
+            else:
+                pick = picker(bits[p], at_ref[0], total)
+                rows = jnp.dot(pick, g_ref[...], preferred_element_type=F32).astype(BF16)
             back += lax.dot_general(
                 w_ref[edges[p] : edges[p + 1], :],
                 rows,
@@ -264,21 +287,22 @@
         keep_refs[p][...] = back[per:]
 
 
-def back_rows(at, own, other, stats, logits, serving, aligned, bits, edges):
+def back_rows(at, own, other, stats, soft, small, bits, edges, low):
     depth, cols = own.shape
-    per = logits[0].shape[0]
+    per = soft[0].shape[0]
     parts = [(per, edges[p + 1] - edges[p]) for p in range(3)]
     got = pl.pallas_call(
-        lambda *refs: back_kernel(bits, edges, len(stats), *refs),
+        lambda *refs: back_kernel(bits, edges, low, len(stats), *refs),
         out_shape=[shape((2 * per, cols), BF16)] * 2
         + [shape(part, BF16) for part in parts]
         + [shape(part, F32) for part in parts],
-        in_specs=[SMEM] + [VMEM] * (len(stats) + 8),
+        in_specs=[SMEM] + [VMEM] * (len(stats) + 6 + len(small)),
         out_specs=[VMEM] * 8,
+        scratch_shapes=[pltpu.VMEM((2, 2 * per, cols), BF16)],
         compiler_params=params(20),
-        cost_estimate=cost(8 * per * depth * cols, 2 * cols * depth * 2, 4 * per * cols),
+        cost_estimate=cost(8 * per * depth * cols, 2 * cols * depth * 2),
         name="back_rows",
-    )(at, own, other, *stats, *logits, serving, aligned)
+    )(at, own, other, *stats, *soft, *small)
     return got[0], got[1], got[2:5], got[5:8]
 
 
@@ -368,7 +392,7 @@
     near_b, stats_b = near_logits(rows, other_weight, x0)
     *pieces, gone, near_a, near_b = tie(x0, x1, x2, x3, rest, gone, near_a, near_b)
     taught_x = swap(gone, X)
-    far_a, far_b, both_rows, stats = far_logits(
+    far_a, far_b, both_rows, stats, peaks = far_logits(
         spots,
         pieces,
         weight,
@@ -391,7 +415,9 @@
         mask *= 4
     _, taught_x = tie(stats, taught_x)
     taught_far = swap(taught_x, CORE)
-    aligned = teacher_rows(who, served, [kept, kept_core, taught_x, taught_far])
+    taught_soft, taught_peaks = teacher_rows(
+        who, served, [kept, kept_core, taught_x, taught_far]
+    )
     parts = [stats] + [swap(stats, mask) for mask in (X, Y, X + Y)]
 
     bits = shards.bit_length() - 1
@@ -405,8 +431,9 @@
     low = owned.bit_length() - 1
     row_bit = {0: low + bits, ydim: low, wdim: low + 1}
     first_bits = tuple(row_bit[order[0]] for order in orders)
+    small = (peaks, served, taught_soft, taught_peaks)
     gown, gother, sents, keeps = back_rows(
-        at, weight, other_weight, parts, logits, served, aligned, first_bits, edges
+        at, weight, other_weight, parts, logits, small, first_bits, edges, low
     )
     gots = [swap(sents[p], masks[orders[p][0]]) for p in range(3)]
     theirs = swap(gother, CORE)

time: 72 us -> 72.2 us (level)
  no operation moved by 1% of the time
where the time goes in v16:
time: 72.2 us; the launch traced here: 72 us
  starting transfers between devices  35.2 us (49%)
  Pallas kernels  15.4 us (21%)
  waiting for transfers between devices  13.9 us (19%)
  local copies, waits for them, and re-layouts  5.47 us (8%)
  other arithmetic  1.23 us (2%)
  between operations  0.82 us (1%)
    ppermute x30, starting transfers between devices, swap(): return lax.ppermute(value, AXES, [(i, i ^ mask) for i in range(count)])  35.2 us
    ppermute x30, waiting for transfers between devices, swap(): return lax.ppermute(value, AXES, [(i, i ^ mask) for i in range(count)])  13.9 us
    pallas_call x1, Pallas kernels, head_gradient(): pl.pallas_call(head_kernel, grid=(depth // tile,), out_shape=shape((depth...  5.21 us
    pallas_call x1, Pallas kernels, back_rows(): pl.pallas_call(lambda *refs: back_kernel(bits, edges, low, len(stats), *r...  4.43 us
    pallas_call x1, Pallas kernels, far_logits(): pl.pallas_call(lambda *refs: far_kernel(len(pieces), *refs), out_shape=(s...  2.19 us
    dynamic_slice x2, local copies, waits for them, and re-layouts, cut(): return lax.dynamic_slice(value, indices, sizes)  2.13 us
    pallas_call x2, Pallas kernels, near_logits(): pl.pallas_call(near_kernel, out_shape=(shape((per, cols), F32), shape((ST...  1.74 us
  transfers between devices with their start and end apart: 30, of which 13 were waited for; matrix products, arithmetic and copies ran while one was open for 5% of the time, Pallas kernels for 15%

profile of v16, /device:TPU:0, one launch (start us, length us, event | category | flops | bytes accessed | tf_op | source)
XLA Modules:
  0.0 72.0 jit_solution(11569795933207461277)
XLA Ops:
  0.7 0.0 copy-start
  0.7 0.1 pad_add_fusion.2.at_ref
  0.7 0.1 pad_add_fusion
  0.8 1.1 %constant_dynamic-slice_fusion.1 = bf16[24,3584]{1,0:T(8,128)(2,1)S(1)} fusion(bf16[128,3584]{1,0:T(8,128)(2,1)} %refs_8_, u32[]{:T(128)S(6)} %convert_element_type.149), kind=kLoop, calls=%fused_computation.42 | loop fusion | bytes 344068 | tf_op jit(solution)/shard_map/dynamic_slice | solution.py:375
  2.0 0.5 collective-permute-start
  2.5 2.6 %collective-permute-start.1 = (bf16[24,3584]{1,0:T(8,128)(2,1)S(1)}, bf16[24,3584]{1,0:T(8,128)(2,1)S(1)}, u32[]{:S(2)}, u32[]{:S(2)}) collective-permute-start(bf16[24,3584]{1,0:T(8,128)(2,1)S(1)} %constant_dynamic-slice_fusion.1), channel_id=1, source_target_pairs={{0,16},{1,17},{2,18},{3,19},{4,20},{5,21},{6,22},{7,23},{8,24},{9,... | collective-permute-start | bytes 516104 | tf_op jit(solution)/shard_map/ppermute | solution.py:348
  5.0 1.0 %slice.173 = bf16[32,3584]{1,0:T(8,128)(2,1)S(1)} slice(bf16[128,3584]{1,0:T(8,128)(2,1)} %refs_8_), slice={[96:128], [0:3584]} | slice | bytes 458752 | tf_op jit(solution)/shard_map/slice | solution.py:382
  6.0 0.1 collective-permute-start.6
  6.1 1.1 %copy.7 = bf16[128,4,512]{2,0,1:T(8,128)(2,1)S(1)} copy(bf16[128,4,512]{2,1,0:T(4,128)(2,1)} %param.9) | data formatting | bytes 1048576 | tf_op jit(solution)/shard_map/optimization_barrier | solution.py:351
  7.3 0.4 taught_stats.1.refs_11_
  7.6 0.2 collective-permute-start.2
  7.8 1.0 %constant_dynamic-slice_fusion = bf16[24,3584]{1,0:T(8,128)(2,1)S(1)} fusion(bf16[128,3584]{1,0:T(8,128)(2,1)} %refs_8_, u32[]{:T(128)S(6)} %convert_element_type.150), kind=kLoop, calls=%fused_computation.41 | loop fusion | bytes 344068 | tf_op jit(solution)/shard_map/dynamic_slice | solution.py:375
  8.8 1.9 %collective-permute-start.5 = (bf16[24,3584]{1,0:T(8,128)(2,1)S(1)}, bf16[24,3584]{1,0:T(8,128)(2,1)S(1)}, u32[]{:S(2)}, u32[]{:S(2)}) collective-permute-start(bf16[24,3584]{1,0:T(8,128)(2,1)S(1)} %constant_dynamic-slice_fusion), channel_id=1, source_target_pairs={{0,16},{1,17},{2,18},{3,19},{4,20},{5,21},{6,22},{7,23},{8,24},{9,... | collective-permute-start | bytes 516104 | tf_op jit(solution)/shard_map/ppermute | solution.py:348
  10.8 0.0 collective-permute-done.1.refs_0_.refs_1_
  10.8 1.6 %collective-permute-start.4 = (bf16[24,3584]{1,0:T(8,128)(2,1)S(1)}, bf16[24,3584]{1,0:T(8,128)(2,1)S(1)}, u32[]{:S(2)}, u32[]{:S(2)}) collective-permute-start(bf16[24,3584]{1,0:T(8,128)(2,1)S(1)} %collective-permute-done.1.refs_0_.refs_1_), channel_id=1, source_target_pairs={{0,2},{1,3},{2,0},{3,1},{4,6},{5,7},{6,4},{7,5},{8,10},{9,11},{10,... | collective-permute-start | bytes 516104 | tf_op jit(solution)/shard_map/ppermute | solution.py:348
  12.4 1.5 %collective-permute-start.3 = (bf16[24,3584]{1,0:T(8,128)(2,1)S(1)}, bf16[24,3584]{1,0:T(8,128)(2,1)S(1)}, u32[]{:S(2)}, u32[]{:S(2)}) collective-permute-start(bf16[24,3584]{1,0:T(8,128)(2,1)S(1)} %collective-permute-done.1.refs_0_.refs_1_), channel_id=1, source_target_pairs={{0,1},{1,0},{2,3},{3,2},{4,5},{5,4},{6,7},{7,6},{8,9},{9,8},{10,11... | collective-permute-start | bytes 516104 | tf_op jit(solution)/shard_map/ppermute | solution.py:348
  13.9 1.2 %copy-done.1 = bf16[128,3584]{1,0:T(8,128)(2,1)S(1)} copy-done((bf16[128,3584]{1,0:T(8,128)(2,1)S(1)}, bf16[128,3584]{1,0:T(8,128)(2,1)}, u32[]{:S(2)}) %copy-start.1) | copy-done | bytes 917528
  15.1 0.9 %near_logits.2 = (f32[128,512]{1,0:T(8,128)S(1)}, f32[8,128]{1,0:T(8,128)S(1)}) custom-call(bf16[128,3584]{1,0:T(8,128)(2,1)S(1)} %copy-done.1, bf16[3584,512]{1,0:T(8,128)(2,1)S(1)} %copy-done, bf16[24,3584]{1,0:T(8,128)(2,1)S(1)} %collective-permute-done.1.refs_0_.refs_1_), custom_call_target="tpu_custom_call" | custom-call | flops 469762048 | bytes 4587520 | tf_op jit(solution)/shard_map/near_logits/pallas_call | solution.py:109
  15.9 0.0 collective-permute-done.w_ref.refs_7_.refs_2_
  15.9 0.9 %near_logits.3 = (f32[128,512]{1,0:T(8,128)S(1)}, f32[8,128]{1,0:T(8,128)S(1)}) custom-call(bf16[128,3584]{1,0:T(8,128)(2,1)S(1)} %copy-done.1, bf16[3584,512]{1,0:T(8,128)(2,1)S(1)} %collective-permute-done.w_ref.refs_7_.refs_2_, bf16[24,3584]{1,0:T(8,128)(2,1)S(1)} %collective-permute-done.1.refs_0_.refs_1_), custom_call_target="tpu_custom_call" | custom-call | flops 469762048 | bytes 4587520 | tf_op jit(solution)/shard_map/near_logits/pallas_call | solution.py:109
  16.8 1.8 %collective-permute-done.5.refs_4_ = bf16[24,3584]{1,0:T(8,128)(2,1)S(1)} collective-permute-done((bf16[24,3584]{1,0:T(8,128)(2,1)S(1)}, bf16[24,3584]{1,0:T(8,128)(2,1)S(1)}, u32[]{:S(2)}, u32[]{:S(2)}) %collective-permute-start.5) | collective-permute-done | bytes 172064 | tf_op jit(solution)/shard_map/ppermute | solution.py:348
  18.6 0.0 collective-permute-done.6.refs_5_
  18.6 0.0 collective-permute-done.4.refs_3_
  18.6 0.0 collective-permute-done.3.refs_2_
  18.6 1.8 %collective-permute-start.14 = (bf16[2,128,512]{2,1,0:T(8,128)(2,1)S(1)}, bf16[2,128,512]{2,1,0:T(8,128)(2,1)S(1)}, u32[]{:S(2)}, u32[]{:S(2)}) collective-permute-start(bf16[2,128,512]{2,1,0:T(8,128)(2,1)S(1)} %get-tuple-element.88.gone_ref), channel_id=1, source_target_pairs={{0,16},{1,17},{2,18},{3,19},{4,20},{5,21},{6,22},{7,23},{8,24},{9,... | collective-permute-start | bytes 786440 | tf_op jit(solution)/shard_map/ppermute | solution.py:348
  20.5 2.2 %far_logits.1 = (f32[128,512]{1,0:T(8,128)S(1)}, f32[128,512]{1,0:T(8,128)S(1)}, bf16[2,128,3584]{2,1,0:T(8,128)(2,1)S(1)}, f32[2,8,128]{2,1,0:T(8,128)S(1)}, f32[8,128]{1,0:T(8,128)S(1)}) custom-call(s32[4]{0:T(128)S(1)} %get-tuple-element.60.refs_0_, bf16[24,3584]{1,0:T(8,128)(2,1)S(1)} %collective-permute-done.1.refs_0_.refs_1_, ...), custom_call_target="tpu_custom_call" | custom-call | flops 939524096 | bytes 8257536 | tf_op jit(solution)/shard_map/far_logits/pallas_call | solution.py:161
  22.7 0.0 copy-start.3
  22.7 3.6 %collective-permute-start.9 = (f32[2,8,128]{2,1,0:T(8,128)S(1)}, f32[2,8,128]{2,1,0:T(8,128)S(1)}, u32[]{:S(2)}, u32[]{:S(2)}) collective-permute-start(f32[2,8,128]{2,1,0:T(8,128)S(1)} %get-tuple-element.80.refs_0_), channel_id=1, source_target_pairs={{0,6},{1,7},{2,4},{3,5},{4,2},{5,3},{6,0},{7,1},{8,14},{9,15},{10,... | collective-permute-start | bytes 24584 | tf_op jit(solution)/shard_map/ppermute | solution.py:348
  26.3 0.0 collective-permute-start.8
  26.3 0.8 %collective-permute-start.7 = (f32[2,8,128]{2,1,0:T(8,128)S(1)}, f32[2,8,128]{2,1,0:T(8,128)S(1)}, u32[]{:S(2)}, u32[]{:S(2)}) collective-permute-start(f32[2,8,128]{2,1,0:T(8,128)S(1)} %get-tuple-element.80.refs_0_), channel_id=1, source_target_pairs={{0,2},{1,3},{2,0},{3,1},{4,6},{5,7},{6,4},{7,5},{8,10},{9,11},{10,... | collective-permute-start | bytes 24584 | tf_op jit(solution)/shard_map/ppermute | solution.py:348
  27.1 1.1 %collective-permute-done.9.refs_3_ = f32[2,8,128]{2,1,0:T(8,128)S(1)} collective-permute-done((f32[2,8,128]{2,1,0:T(8,128)S(1)}, f32[2,8,128]{2,1,0:T(8,128)S(1)}, u32[]{:S(2)}, u32[]{:S(2)}) %collective-permute-start.9) | collective-permute-done | bytes 8224 | tf_op jit(solution)/shard_map/ppermute | solution.py:348
  28.2 2.7 %collective-permute-done.8.refs_2_ = f32[2,8,128]{2,1,0:T(8,128)S(1)} collective-permute-done((f32[2,8,128]{2,1,0:T(8,128)S(1)}, f32[2,8,128]{2,1,0:T(8,128)S(1)}, u32[]{:S(2)}, u32[]{:S(2)}) %collective-permute-start.8) | collective-permute-done | bytes 8224 | tf_op jit(solution)/shard_map/ppermute | solution.py:348
  30.9 0.1 collective-permute-start.15
  31.0 1.6 %collective-permute-start.12 = (f32[2,8,128]{2,1,0:T(8,128)S(1)}, f32[2,8,128]{2,1,0:T(8,128)S(1)}, u32[]{:S(2)}, u32[]{:S(2)}) collective-permute-start(f32[2,8,128]{2,1,0:T(8,128)S(1)} %merge_stats.1.refs_3_), channel_id=1, source_target_pairs={{0,17},{1,16},{2,19},{3,18},{4,21},{5,20},{6,23},{7,22},{8,25},{9,... | collective-permute-start | bytes 24584 | tf_op jit(solution)/shard_map/ppermute | solution.py:348
  32.6 0.5 collective-permute-start.11
  33.1 1.5 %collective-permute-start.10 = (f32[2,8,128]{2,1,0:T(8,128)S(1)}, f32[2,8,128]{2,1,0:T(8,128)S(1)}, u32[]{:S(2)}, u32[]{:S(2)}) collective-permute-start(f32[2,8,128]{2,1,0:T(8,128)S(1)} %merge_stats.1.refs_3_), channel_id=1, source_target_pairs={{0,16},{1,17},{2,18},{3,19},{4,20},{5,21},{6,22},{7,23},{8,24},{9,... | collective-permute-start | bytes 24584 | tf_op jit(solution)/shard_map/ppermute | solution.py:348
  34.6 1.4 %teacher_rows.1 = (f32[2,128,1024]{2,1,0:T(8,128)S(1)}, f32[2,8,128]{2,1,0:T(8,128)S(1)}) custom-call(s32[2]{0:T(128)S(1)} %pad_add_fusion.2.at_ref, s32[4,1,128]{2,1,0:T(1,128)S(1)} %bitcast.42, bf16[2,128,512]{2,1,0:T(8,128)(2,1)S(1)} %get-tuple-element.87.kept_ref.a0, bf16[2,128,512]{2,1,0:T(8,128)(2,1)S(1)} %collective-permute-done.13.a1, ...), custom_call_target="tpu_custom_call" | custom-call | flops 268435456 | bytes 1572864 | tf_op jit(solution)/shard_map/teacher_rows/pallas_call | solution.py:82
  36.0 0.2 collective-permute-done.11.refs_5_
  36.2 0.5 collective-permute-done.10.refs_4_
  36.7 4.4 %back_rows.1 = (bf16[256,512]{1,0:T(8,128)(2,1)S(1)}, bf16[256,512]{1,0:T(8,128)(2,1)S(1)}, bf16[128,1152]{1,0:T(8,128)(2,1)S(1)}, bf16[128,1152]{1,0:T(8,128)(2...) custom-call(s32[4]{0:T(128)S(1)} %get-tuple-element.55.refs_0_, ...), custom_call_target="tpu_custom_call" | custom-call | flops 1879048192 | bytes 7340032 | tf_op jit(solution)/shard_map/back_rows/pallas_call | solution.py:294
  41.1 0.1 collective-permute-start.16
  41.2 0.5 collective-permute-start.17
  41.7 1.5 %collective-permute-start.18 = (bf16[128,1152]{1,0:T(8,128)(2,1)S(1)}, bf16[128,1152]{1,0:T(8,128)(2,1)S(1)}, u32[]{:S(2)}, u32[]{:S(2)}) collective-permute-start(bf16[128,1152]{1,0:T(8,128)(2,1)S(1)} %get-tuple-element.97), channel_id=1, source_target_pairs={{0,16},{1,17},{2,18},{3,19},{4,20},{5,21},{6,22},{7,23},{8,24},{9,... | collective-permute-start | bytes 884744 | tf_op jit(solution)/shard_map/ppermute | solution.py:348
  43.2 1.5 %collective-permute-start.22 = (bf16[128,1152]{1,0:T(8,128)(2,1)S(1)}, bf16[128,1152]{1,0:T(8,128)(2,1)S(1)}, u32[]{:S(2)}, u32[]{:S(2)}) collective-permute-start(bf16[128,1152]{1,0:T(8,128)(2,1)S(1)} %get-tuple-element.101), channel_id=1, source_target_pairs={{0,1},{1,0},{2,3},{3,2},{4,5},{5,4},{6,7},{7,6},{8,9},{9,8},{10,11... | collective-permute-start | bytes 884744 | tf_op jit(solution)/shard_map/ppermute | solution.py:348
  44.7 0.6 collective-permute-done.17.theirs_ref
  45.4 5.2 %head_gradient.1 = bf16[3584,512]{1,0:T(8,128)(2,1)} custom-call(bf16[2,128,3584]{2,1,0:T(8,128)(2,1)S(1)} %get-tuple-element.95.rows_ref, bf16[2,128,3584]{2,1,0:T(8,128)(2,1)S(1)} %collective-permute-done.16.core_ref, bf16[256,512]{1,0:T(8,128)(2,1)S(1)} %get-tuple-element.96.mine_ref, bf16[256,512]{1,0:T(8,128)(2,1)S(1)} %collective-permute-done.17.theirs_ref), custom_call_target="tpu_custom_call" | custom-call | flops 1879048192 | bytes 7340032 | tf_op jit(solution)/shard_map/head_gradient/pallas_call | solution.py:323
  50.6 0.1 collective-permute-done.18
  50.7 1.2 %collective-permute-done.22 = bf16[128,1152]{1,0:T(8,128)(2,1)S(1)} collective-permute-done((bf16[128,1152]{1,0:T(8,128)(2,1)S(1)}, bf16[128,1152]{1,0:T(8,128)(2,1)S(1)}, u32[]{:S(2)}, u32[]{:S(2)}) %collective-permute-start.22) | collective-permute-done | bytes 294944 | tf_op jit(solution)/shard_map/ppermute | solution.py:348
  52.0 1.6 %collective-permute-start.19 = (bf16[1,2,2,1,16,1152]{5,4,3,2,1,0:T(8,128)(2,1)S(1)}, bf16[1,2,2,1,16,1152]{5,4,3,2,1,0:T(8,128)(2,1)S(1)}, u32[]{:S(2)}, u32[]{:S(2)}) collective-permute-start(bf16[1,2,2,1,16,1152]{5,4,3,2,1,0:T(8,128)(2,1)S(1)} %fusion.1), channel_id=1, source_target_pairs={{0,1},{1,0},{2,3},{3,2},{4,5},{5,4},{6,7},{7,6},{8,9},{9,8},{10,11... | collective-permute-start | bytes 442376 | tf_op jit(solution)/shard_map/ppermute | solution.py:348
  53.5 0.1 add_convert_fusion
  53.7 1.8 %collective-permute-start.23 = (bf16[2,2,1,1,16,1152]{5,4,3,2,1,0:T(8,128)(2,1)S(1)}, bf16[2,2,1,1,16,1152]{5,4,3,2,1,0:T(8,128)(2,1)S(1)}, u32[]{:S(2)}, u32[]{:S(2)}) collective-permute-start(bf16[2,2,1,1,16,1152]{5,4,3,2,1,0:T(8,128)(2,1)S(1)} %fusion), channel_id=1, source_target_pairs={{0,2},{1,3},{2,0},{3,1},{4,6},{5,7},{6,4},{7,5},{8,10},{9,11},{10,... | collective-permute-start | bytes 442376 | tf_op jit(solution)/shard_map/ppermute | solution.py:348
  55.5 0.5 collective-permute-start.27
  56.0 1.2 %collective-permute-done.19 = bf16[1,2,2,1,16,1152]{5,4,3,2,1,0:T(8,128)(2,1)S(1)} collective-permute-done((bf16[1,2,2,1,16,1152]{5,4,3,2,1,0:T(8,128)(2,1)S(1)}, bf16[1,2,2,1,16,1152]{5,4,3,2,1,0:T(8,128)(2,1)S(1)}, u32[]{:S(2)}, u32[]{:S(2)}) %collective-permute-start.19) | collective-permute-done | bytes 147488 | tf_op jit(solution)/shard_map/ppermute | solution.py:348
  57.2 1.8 %collective-permute-start.20 = (bf16[1,2,1,1,16,1152]{5,4,3,2,1,0:T(8,128)(2,1)S(1)}, bf16[1,2,1,1,16,1152]{5,4,3,2,1,0:T(8,128)(2,1)S(1)}, u32[]{:S(2)}, u32[]{:S(2)}) collective-permute-start(bf16[1,2,1,1,16,1152]{5,4,3,2,1,0:T(8,128)(2,1)S(1)} %fusion.7), channel_id=1, source_target_pairs={{0,2},{1,3},{2,0},{3,1},{4,6},{5,7},{6,4},{7,5},{8,10},{9,11},{10,... | collective-permute-start | bytes 221192 | tf_op jit(solution)/shard_map/ppermute | solution.py:348
  59.0 0.6 collective-permute-done.23
  59.7 1.0 %collective-permute-start.24 = (bf16[1,2,1,1,16,1152]{5,4,3,2,1,0:T(8,128)(2,1)S(1)}, bf16[1,2,1,1,16,1152]{5,4,3,2,1,0:T(8,128)(2,1)S(1)}, u32[]{:S(2)}, u32[]{:S(2)}) collective-permute-start(bf16[1,2,1,1,16,1152]{5,4,3,2,1,0:T(8,128)(2,1)S(1)} %fusion.5), channel_id=1, source_target_pairs={{0,16},{1,17},{2,18},{3,19},{4,20},{5,21},{6,22},{7,23},{8,24},{9,... | collective-permute-start | bytes 221192 | tf_op jit(solution)/shard_map/ppermute | solution.py:348
  60.7 0.8 %collective-permute-done.27 = bf16[1,2,1,2,16,1280]{5,4,3,2,1,0:T(8,128)(2,1)S(1)} collective-permute-done((bf16[1,2,1,2,16,1280]{5,4,3,2,1,0:T(8,128)(2,1)S(1)}, bf16[1,2,1,2,16,1280]{5,4,3,2,1,0:T(8,128)(2,1)S(1)}, u32[]{:S(2)}, u32[]{:S(2)}) %collective-permute-start.27) | collective-permute-done | bytes 163872 | tf_op jit(solution)/shard_map/ppermute | solution.py:348
  61.6 0.6 collective-permute-start.28
  62.2 2.1 %collective-permute-start.21 = (bf16[1,1,1,1,16,1152]{5,4,3,2,1,0:T(8,128)(2,1)S(1)}, bf16[1,1,1,1,16,1152]{5,4,3,2,1,0:T(8,128)(2,1)S(1)}, u32[]{:S(2)}, u32[]{:S(2)}) collective-permute-start(bf16[1,1,1,1,16,1152]{5,4,3,2,1,0:T(8,128)(2,1)S(1)} %fusion.22), channel_id=1, source_target_pairs={{0,4},{1,5},{2,6},{3,7},{4,0},{5,1},{6,2},{7,3},{8,12},{9,13},{10,... | collective-permute-start | bytes 110600 | tf_op jit(solution)/shard_map/ppermute | solution.py:348
  64.3 1.9 %collective-permute-start.25 = (bf16[1,1,1,1,16,1152]{5,4,3,2,1,0:T(8,128)(2,1)S(1)}, bf16[1,1,1,1,16,1152]{5,4,3,2,1,0:T(8,128)(2,1)S(1)}, u32[]{:S(2)}, u32[]{:S(2)}) collective-permute-start(bf16[1,1,1,1,16,1152]{5,4,3,2,1,0:T(8,128)(2,1)S(1)} %fusion.16), channel_id=1, source_target_pairs={{0,4},{1,5},{2,6},{3,7},{4,0},{5,1},{6,2},{7,3},{8,12},{9,13},{10,... | collective-permute-start | bytes 110600 | tf_op jit(solution)/shard_map/ppermute | solution.py:348
  66.3 2.0 %collective-permute-start.29 = (bf16[1,1,1,1,16,1280]{5,4,3,2,1,0:T(8,128)(2,1)S(1)}, bf16[1,1,1,1,16,1280]{5,4,3,2,1,0:T(8,128)(2,1)S(1)}, u32[]{:S(2)}, u32[]{:S(2)}) collective-permute-start(bf16[1,1,1,1,16,1280]{5,4,3,2,1,0:T(8,128)(2,1)S(1)} %fusion.10), channel_id=1, source_target_pairs={{0,4},{1,5},{2,6},{3,7},{4,0},{5,1},{6,2},{7,3},{8,12},{9,13},{10,... | collective-permute-start | bytes 122888 | tf_op jit(solution)/shard_map/ppermute | solution.py:348
  68.3 1.0 %collective-permute-done.25 = bf16[1,1,1,1,16,1152]{5,4,3,2,1,0:T(8,128)(2,1)S(1)} collective-permute-done((bf16[1,1,1,1,16,1152]{5,4,3,2,1,0:T(8,128)(2,1)S(1)}, bf16[1,1,1,1,16,1152]{5,4,3,2,1,0:T(8,128)(2,1)S(1)}, u32[]{:S(2)}, u32[]{:S(2)}) %collective-permute-start.25) | collective-permute-done | bytes 36896 | tf_op jit(solution)/shard_map/ppermute | solution.py:348
  69.3 1.9 %collective-permute-done.29 = bf16[1,1,1,1,16,1280]{5,4,3,2,1,0:T(8,128)(2,1)S(1)} collective-permute-done((bf16[1,1,1,1,16,1280]{5,4,3,2,1,0:T(8,128)(2,1)S(1)}, bf16[1,1,1,1,16,1280]{5,4,3,2,1,0:T(8,128)(2,1)S(1)}, u32[]{:S(2)}, u32[]{:S(2)}) %collective-permute-start.29) | collective-permute-done | bytes 40992 | tf_op jit(solution)/shard_map/ppermute | solution.py:348
  71.3 0.7 maximum_bitcast_fusion
  (35 shorter events, 0.5 us)
Async XLA Ops:
  0.7 13.2 %copy-start = (bf16[3584,512]{1,0:T(8,128)(2,1)S(1)}, bf16[3584,512]{1,0:T(8,128)(2,1)}, u32[]{:S(2)}) copy-start(bf16[3584,512]{1,0:T(8,128)(2,1)} %refs_1_) | copy-start | bytes 11010052
  2.0 14.0 %collective-permute-start = (bf16[3584,512]{1,0:T(8,128)(2,1)}, bf16[3584,512]{1,0:T(8,128)(2,1)S(1)}, u32[]{:S(2)}, u32[]{:S(2)}) collective-permute-start(bf16[3584,512]{1,0:T(8,128)(2,1)} %refs_1_), channel_id=1, source_target_pairs={{0,8},{1,9},{2,10},{3,11},{4,12},{5,13},{6,14},{7,15},{8,0},{9,1},... | collective-permute-start | bytes 11010056 | tf_op jit(solution)/shard_map/ppermute | solution.py:348
  2.5 8.3 %collective-permute-start.1 = (bf16[24,3584]{1,0:T(8,128)(2,1)S(1)}, bf16[24,3584]{1,0:T(8,128)(2,1)S(1)}, u32[]{:S(2)}, u32[]{:S(2)}) collective-permute-start(bf16[24,3584]{1,0:T(8,128)(2,1)S(1)} %constant_dynamic-slice_fusion.1), channel_id=1, source_target_pairs={{0,16},{1,17},{2,18},{3,19},{4,20},{5,21},{6,22},{7,23},{8,24},{9,... | collective-permute-start | bytes 516104 | tf_op jit(solution)/shard_map/ppermute | solution.py:348
  6.0 12.6 %collective-permute-start.6 = (bf16[32,3584]{1,0:T(8,128)(2,1)S(1)}, bf16[32,3584]{1,0:T(8,128)(2,1)S(1)}, u32[]{:S(2)}, u32[]{:S(2)}) collective-permute-start(bf16[32,3584]{1,0:T(8,128)(2,1)S(1)} %slice.173), channel_id=1, source_target_pairs={{0,16},{1,17},{2,18},{3,19},{4,20},{5,21},{6,22},{7,23},{8,24},{9,... | collective-permute-start | bytes 688136 | tf_op jit(solution)/shard_map/ppermute | solution.py:348
  7.6 3.1 %collective-permute-start.2 = (f32[8,128]{1,0:T(8,128)S(1)}, f32[8,128]{1,0:T(8,128)S(1)}, u32[]{:S(2)}, u32[]{:S(2)}) collective-permute-start(f32[8,128]{1,0:T(8,128)S(1)} %taught_stats.1.refs_11_), channel_id=1, source_target_pairs={{0,8},{1,9},{2,10},{3,11},{4,12},{5,13},{6,14},{7,15},{8,0},{9,1},... | collective-permute-start | bytes 12296 | tf_op jit(solution)/shard_map/ppermute | solution.py:348
  7.8 12.6 %copy-start.4 = (s32[128]{0:T(128)S(1)}, s32[128]{0:T(128)}, u32[]{:S(2)}) copy-start(s32[128]{0:T(128)} %param.6) | copy-start | bytes 1540
  8.8 9.8 %collective-permute-start.5 = (bf16[24,3584]{1,0:T(8,128)(2,1)S(1)}, bf16[24,3584]{1,0:T(8,128)(2,1)S(1)}, u32[]{:S(2)}, u32[]{:S(2)}) collective-permute-start(bf16[24,3584]{1,0:T(8,128)(2,1)S(1)} %constant_dynamic-slice_fusion), channel_id=1, source_target_pairs={{0,16},{1,17},{2,18},{3,19},{4,20},{5,21},{6,22},{7,23},{8,24},{9,... | collective-permute-start | bytes 516104 | tf_op jit(solution)/shard_map/ppermute | solution.py:348
  10.8 7.8 %collective-permute-start.4 = (bf16[24,3584]{1,0:T(8,128)(2,1)S(1)}, bf16[24,3584]{1,0:T(8,128)(2,1)S(1)}, u32[]{:S(2)}, u32[]{:S(2)}) collective-permute-start(bf16[24,3584]{1,0:T(8,128)(2,1)S(1)} %collective-permute-done.1.refs_0_.refs_1_), channel_id=1, source_target_pairs={{0,2},{1,3},{2,0},{3,1},{4,6},{5,7},{6,4},{7,5},{8,10},{9,11},{10,... | collective-permute-start | bytes 516104 | tf_op jit(solution)/shard_map/ppermute | solution.py:348
  12.4 6.3 %collective-permute-start.3 = (bf16[24,3584]{1,0:T(8,128)(2,1)S(1)}, bf16[24,3584]{1,0:T(8,128)(2,1)S(1)}, u32[]{:S(2)}, u32[]{:S(2)}) collective-permute-start(bf16[24,3584]{1,0:T(8,128)(2,1)S(1)} %collective-permute-done.1.refs_0_.refs_1_), channel_id=1, source_target_pairs={{0,1},{1,0},{2,3},{3,2},{4,5},{5,4},{6,7},{7,6},{8,9},{9,8},{10,11... | collective-permute-start | bytes 516104 | tf_op jit(solution)/shard_map/ppermute | solution.py:348
  13.9 1.2 %copy-start.1 = (bf16[128,3584]{1,0:T(8,128)(2,1)S(1)}, bf16[128,3584]{1,0:T(8,128)(2,1)}, u32[]{:S(2)}) copy-start(bf16[128,3584]{1,0:T(8,128)(2,1)} %refs_8_) | copy-start | bytes 2752516
  15.1 5.4 %copy-start.2 = (bf16[128,3584]{1,0:T(8,128)(2,1)S(1)}, bf16[128,3584]{1,0:T(8,128)(2,1)}, u32[]{:S(2)}) copy-start(bf16[128,3584]{1,0:T(8,128)(2,1)} %refs_8_) | copy-start | bytes 2752516
  18.6 12.3 %collective-permute-start.14 = (bf16[2,128,512]{2,1,0:T(8,128)(2,1)S(1)}, bf16[2,128,512]{2,1,0:T(8,128)(2,1)S(1)}, u32[]{:S(2)}, u32[]{:S(2)}) collective-permute-start(bf16[2,128,512]{2,1,0:T(8,128)(2,1)S(1)} %get-tuple-element.88.gone_ref), channel_id=1, source_target_pairs={{0,16},{1,17},{2,18},{3,19},{4,20},{5,21},{6,22},{7,23},{8,24},{9,... | collective-permute-start | bytes 786440 | tf_op jit(solution)/shard_map/ppermute | solution.py:348
  22.7 11.9 %copy-start.3 = (s32[512]{0:T(512)S(1)}, s32[512]{0:T(512)}, u32[]{:S(2)}) copy-start(s32[512]{0:T(512)} %param.7) | copy-start | bytes 6148
  22.7 5.5 %collective-permute-start.9 = (f32[2,8,128]{2,1,0:T(8,128)S(1)}, f32[2,8,128]{2,1,0:T(8,128)S(1)}, u32[]{:S(2)}, u32[]{:S(2)}) collective-permute-start(f32[2,8,128]{2,1,0:T(8,128)S(1)} %get-tuple-element.80.refs_0_), channel_id=1, source_target_pairs={{0,6},{1,7},{2,4},{3,5},{4,2},{5,3},{6,0},{7,1},{8,14},{9,15},{10,... | collective-permute-start | bytes 24584 | tf_op jit(solution)/shard_map/ppermute | solution.py:348
  26.3 4.5 %collective-permute-start.8 = (f32[2,8,128]{2,1,0:T(8,128)S(1)}, f32[2,8,128]{2,1,0:T(8,128)S(1)}, u32[]{:S(2)}, u32[]{:S(2)}) collective-permute-start(f32[2,8,128]{2,1,0:T(8,128)S(1)} %get-tuple-element.80.refs_0_), channel_id=1, source_target_pairs={{0,4},{1,5},{2,6},{3,7},{4,0},{5,1},{6,2},{7,3},{8,12},{9,13},{10,... | collective-permute-start | bytes 24584 | tf_op jit(solution)/shard_map/ppermute | solution.py:348
  26.3 4.5 %collective-permute-start.7 = (f32[2,8,128]{2,1,0:T(8,128)S(1)}, f32[2,8,128]{2,1,0:T(8,128)S(1)}, u32[]{:S(2)}, u32[]{:S(2)}) collective-permute-start(f32[2,8,128]{2,1,0:T(8,128)S(1)} %get-tuple-element.80.refs_0_), channel_id=1, source_target_pairs={{0,2},{1,3},{2,0},{3,1},{4,6},{5,7},{6,4},{7,5},{8,10},{9,11},{10,... | collective-permute-start | bytes 24584 | tf_op jit(solution)/shard_map/ppermute | solution.py:348
  27.1 7.4 %collective-permute-start.13 = (bf16[2,128,512]{2,1,0:T(8,128)(2,1)S(1)}, bf16[2,128,512]{2,1,0:T(8,128)(2,1)S(1)}, u32[]{:S(2)}, u32[]{:S(2)}) collective-permute-start(bf16[2,128,512]{2,1,0:T(8,128)(2,1)S(1)} %get-tuple-element.87.kept_ref.a0), channel_id=1, source_target_pairs={{0,8},{1,9},{2,10},{3,11},{4,12},{5,13},{6,14},{7,15},{8,0},{9,1},... | collective-permute-start | bytes 786440 | tf_op jit(solution)/shard_map/ppermute | solution.py:348
  30.9 3.6 %collective-permute-start.15 = (bf16[2,128,512]{2,1,0:T(8,128)(2,1)S(1)}, bf16[2,128,512]{2,1,0:T(8,128)(2,1)S(1)}, u32[]{:S(2)}, u32[]{:S(2)}) collective-permute-start(bf16[2,128,512]{2,1,0:T(8,128)(2,1)S(1)} %collective-permute-done.14.a2), channel_id=1, source_target_pairs={{0,8},{1,9},{2,10},{3,11},{4,12},{5,13},{6,14},{7,15},{8,0},{9,1},... | collective-permute-start | bytes 786440 | tf_op jit(solution)/shard_map/ppermute | solution.py:348
  31.0 5.0 %collective-permute-start.12 = (f32[2,8,128]{2,1,0:T(8,128)S(1)}, f32[2,8,128]{2,1,0:T(8,128)S(1)}, u32[]{:S(2)}, u32[]{:S(2)}) collective-permute-start(f32[2,8,128]{2,1,0:T(8,128)S(1)} %merge_stats.1.refs_3_), channel_id=1, source_target_pairs={{0,17},{1,16},{2,19},{3,18},{4,21},{5,20},{6,23},{7,22},{8,25},{9,... | collective-permute-start | bytes 24584 | tf_op jit(solution)/shard_map/ppermute | solution.py:348
  32.6 3.7 %collective-permute-start.11 = (f32[2,8,128]{2,1,0:T(8,128)S(1)}, f32[2,8,128]{2,1,0:T(8,128)S(1)}, u32[]{:S(2)}, u32[]{:S(2)}) collective-permute-start(f32[2,8,128]{2,1,0:T(8,128)S(1)} %merge_stats.1.refs_3_), channel_id=1, source_target_pairs={{0,1},{1,0},{2,3},{3,2},{4,5},{5,4},{6,7},{7,6},{8,9},{9,8},{10,11... | collective-permute-start | bytes 24584 | tf_op jit(solution)/shard_map/ppermute | solution.py:348
  33.1 3.7 %collective-permute-start.10 = (f32[2,8,128]{2,1,0:T(8,128)S(1)}, f32[2,8,128]{2,1,0:T(8,128)S(1)}, u32[]{:S(2)}, u32[]{:S(2)}) collective-permute-start(f32[2,8,128]{2,1,0:T(8,128)S(1)} %merge_stats.1.refs_3_), channel_id=1, source_target_pairs={{0,16},{1,17},{2,18},{3,19},{4,20},{5,21},{6,22},{7,23},{8,24},{9,... | collective-permute-start | bytes 24584 | tf_op jit(solution)/shard_map/ppermute | solution.py:348
  41.1 4.2 %collective-permute-start.16 = (bf16[2,128,3584]{2,1,0:T(8,128)(2,1)S(1)}, bf16[2,128,3584]{2,1,0:T(8,128)(2,1)S(1)}, u32[]{:S(2)}, u32[]{:S(2)}) collective-permute-start(bf16[2,128,3584]{2,1,0:T(8,128)(2,1)S(1)} %get-tuple-element.95.rows_ref), channel_id=1, source_target_pairs={{0,8},{1,9},{2,10},{3,11},{4,12},{5,13},{6,14},{7,15},{8,0},{9,1},... | collective-permute-start | bytes 5505032 | tf_op jit(solution)/shard_map/ppermute | solution.py:348
  41.2 4.1 %collective-permute-start.17 = (bf16[256,512]{1,0:T(8,128)(2,1)S(1)}, bf16[256,512]{1,0:T(8,128)(2,1)S(1)}, u32[]{:S(2)}, u32[]{:S(2)}) collective-permute-start(bf16[256,512]{1,0:T(8,128)(2,1)S(1)} %get-tuple-element.94), channel_id=1, source_target_pairs={{0,8},{1,9},{2,10},{3,11},{4,12},{5,13},{6,14},{7,15},{8,0},{9,1},... | collective-permute-start | bytes 786440 | tf_op jit(solution)/shard_map/ppermute | solution.py:348
  41.7 10.2 %collective-permute-start.26 = (bf16[128,1280]{1,0:T(8,128)(2,1)S(1)}, bf16[128,1280]{1,0:T(8,128)(2,1)S(1)}, u32[]{:S(2)}, u32[]{:S(2)}) collective-permute-start(bf16[128,1280]{1,0:T(8,128)(2,1)S(1)} %get-tuple-element.105), channel_id=1, source_target_pairs={{0,2},{1,3},{2,0},{3,1},{4,6},{5,7},{6,4},{7,5},{8,10},{9,11},{10,... | collective-permute-start | bytes 983048 | tf_op jit(solution)/shard_map/ppermute | solution.py:348
  41.7 9.0 %collective-permute-start.18 = (bf16[128,1152]{1,0:T(8,128)(2,1)S(1)}, bf16[128,1152]{1,0:T(8,128)(2,1)S(1)}, u32[]{:S(2)}, u32[]{:S(2)}) collective-permute-start(bf16[128,1152]{1,0:T(8,128)(2,1)S(1)} %get-tuple-element.97), channel_id=1, source_target_pairs={{0,16},{1,17},{2,18},{3,19},{4,20},{5,21},{6,22},{7,23},{8,24},{9,... | collective-permute-start | bytes 884744 | tf_op jit(solution)/shard_map/ppermute | solution.py:348
  43.2 8.7 %collective-permute-start.22 = (bf16[128,1152]{1,0:T(8,128)(2,1)S(1)}, bf16[128,1152]{1,0:T(8,128)(2,1)S(1)}, u32[]{:S(2)}, u32[]{:S(2)}) collective-permute-start(bf16[128,1152]{1,0:T(8,128)(2,1)S(1)} %get-tuple-element.101), channel_id=1, source_target_pairs={{0,1},{1,0},{2,3},{3,2},{4,5},{5,4},{6,7},{7,6},{8,9},{9,8},{10,11... | collective-permute-start | bytes 884744 | tf_op jit(solution)/shard_map/ppermute | solution.py:348
  52.0 5.2 %collective-permute-start.19 = (bf16[1,2,2,1,16,1152]{5,4,3,2,1,0:T(8,128)(2,1)S(1)}, bf16[1,2,2,1,16,1152]{5,4,3,2,1,0:T(8,128)(2,1)S(1)}, u32[]{:S(2)}, u32[]{:S(2)}) collective-permute-start(bf16[1,2,2,1,16,1152]{5,4,3,2,1,0:T(8,128)(2,1)S(1)} %fusion.1), channel_id=1, source_target_pairs={{0,1},{1,0},{2,3},{3,2},{4,5},{5,4},{6,7},{7,6},{8,9},{9,8},{10,11... | collective-permute-start | bytes 442376 | tf_op jit(solution)/shard_map/ppermute | solution.py:348
  53.7 6.0 %collective-permute-start.23 = (bf16[2,2,1,1,16,1152]{5,4,3,2,1,0:T(8,128)(2,1)S(1)}, bf16[2,2,1,1,16,1152]{5,4,3,2,1,0:T(8,128)(2,1)S(1)}, u32[]{:S(2)}, u32[]{:S(2)}) collective-permute-start(bf16[2,2,1,1,16,1152]{5,4,3,2,1,0:T(8,128)(2,1)S(1)} %fusion), channel_id=1, source_target_pairs={{0,2},{1,3},{2,0},{3,1},{4,6},{5,7},{6,4},{7,5},{8,10},{9,11},{10,... | collective-permute-start | bytes 442376 | tf_op jit(solution)/shard_map/ppermute | solution.py:348
  55.5 6.1 %collective-permute-start.27 = (bf16[1,2,1,2,16,1280]{5,4,3,2,1,0:T(8,128)(2,1)S(1)}, bf16[1,2,1,2,16,1280]{5,4,3,2,1,0:T(8,128)(2,1)S(1)}, u32[]{:S(2)}, u32[]{:S(2)}) collective-permute-start(bf16[1,2,1,2,16,1280]{5,4,3,2,1,0:T(8,128)(2,1)S(1)} %bitcast.59), channel_id=1, source_target_pairs={{0,16},{1,17},{2,18},{3,19},{4,20},{5,21},{6,22},{7,23},{8,24},{9,... | collective-permute-start | bytes 491528 | tf_op jit(solution)/shard_map/ppermute | solution.py:348
  57.2 5.0 %collective-permute-start.20 = (bf16[1,2,1,1,16,1152]{5,4,3,2,1,0:T(8,128)(2,1)S(1)}, bf16[1,2,1,1,16,1152]{5,4,3,2,1,0:T(8,128)(2,1)S(1)}, u32[]{:S(2)}, u32[]{:S(2)}) collective-permute-start(bf16[1,2,1,1,16,1152]{5,4,3,2,1,0:T(8,128)(2,1)S(1)} %fusion.7), channel_id=1, source_target_pairs={{0,2},{1,3},{2,0},{3,1},{4,6},{5,7},{6,4},{7,5},{8,10},{9,11},{10,... | collective-permute-start | bytes 221192 | tf_op jit(solution)/shard_map/ppermute | solution.py:348
  59.7 4.6 %collective-permute-start.24 = (bf16[1,2,1,1,16,1152]{5,4,3,2,1,0:T(8,128)(2,1)S(1)}, bf16[1,2,1,1,16,1152]{5,4,3,2,1,0:T(8,128)(2,1)S(1)}, u32[]{:S(2)}, u32[]{:S(2)}) collective-permute-start(bf16[1,2,1,1,16,1152]{5,4,3,2,1,0:T(8,128)(2,1)S(1)} %fusion.5), channel_id=1, source_target_pairs={{0,16},{1,17},{2,18},{3,19},{4,20},{5,21},{6,22},{7,23},{8,24},{9,... | collective-permute-start | bytes 221192 | tf_op jit(solution)/shard_map/ppermute | solution.py:348
  61.6 4.6 %collective-permute-start.28 = (bf16[1,2,1,1,16,1280]{5,4,3,2,1,0:T(8,128)(2,1)S(1)}, bf16[1,2,1,1,16,1280]{5,4,3,2,1,0:T(8,128)(2,1)S(1)}, u32[]{:S(2)}, u32[]{:S(2)}) collective-permute-start(bf16[1,2,1,1,16,1280]{5,4,3,2,1,0:T(8,128)(2,1)S(1)} %fusion.3), channel_id=1, source_target_pairs={{0,1},{1,0},{2,3},{3,2},{4,5},{5,4},{6,7},{7,6},{8,9},{9,8},{10,11... | collective-permute-start | bytes 245768 | tf_op jit(solution)/shard_map/ppermute | solution.py:348
  62.2 6.0 %collective-permute-start.21 = (bf16[1,1,1,1,16,1152]{5,4,3,2,1,0:T(8,128)(2,1)S(1)}, bf16[1,1,1,1,16,1152]{5,4,3,2,1,0:T(8,128)(2,1)S(1)}, u32[]{:S(2)}, u32[]{:S(2)}) collective-permute-start(bf16[1,1,1,1,16,1152]{5,4,3,2,1,0:T(8,128)(2,1)S(1)} %fusion.22), channel_id=1, source_target_pairs={{0,4},{1,5},{2,6},{3,7},{4,0},{5,1},{6,2},{7,3},{8,12},{9,13},{10,... | collective-permute-start | bytes 110600 | tf_op jit(solution)/shard_map/ppermute | solution.py:348
  64.3 4.9 %collective-permute-start.25 = (bf16[1,1,1,1,16,1152]{5,4,3,2,1,0:T(8,128)(2,1)S(1)}, bf16[1,1,1,1,16,1152]{5,4,3,2,1,0:T(8,128)(2,1)S(1)}, u32[]{:S(2)}, u32[]{:S(2)}) collective-permute-start(bf16[1,1,1,1,16,1152]{5,4,3,2,1,0:T(8,128)(2,1)S(1)} %fusion.16), channel_id=1, source_target_pairs={{0,4},{1,5},{2,6},{3,7},{4,0},{5,1},{6,2},{7,3},{8,12},{9,13},{10,... | collective-permute-start | bytes 110600 | tf_op jit(solution)/shard_map/ppermute | solution.py:348
  66.3 5.0 %collective-permute-start.29 = (bf16[1,1,1,1,16,1280]{5,4,3,2,1,0:T(8,128)(2,1)S(1)}, bf16[1,1,1,1,16,1280]{5,4,3,2,1,0:T(8,128)(2,1)S(1)}, u32[]{:S(2)}, u32[]{:S(2)}) collective-permute-start(bf16[1,1,1,1,16,1280]{5,4,3,2,1,0:T(8,128)(2,1)S(1)} %fusion.10), channel_id=1, source_target_pairs={{0,4},{1,5},{2,6},{3,7},{4,0},{5,1},{6,2},{7,3},{8,12},{9,13},{10,... | collective-permute-start | bytes 122888 | tf_op jit(solution)/shard_map/ppermute | solution.py:348

commit v17 on v16

--- a/solution.py
+++ b/solution.py
@@ -326,7 +326,9 @@
         out_shape=shape((depth, cols), BF16),
         in_specs=[slab] * 2 + [whole] * 2,
         out_specs=pl.BlockSpec((tile, cols), lambda i: (i, 0)),
-        compiler_params=params(6),
+        compiler_params=pltpu.CompilerParams(
+            vmem_limit_bytes=6 * MIB, fuse_transposed_lhs_in_matmul=True
+        ),
         cost_estimate=cost(8 * per * depth * cols, (4 * per + cols) * depth * 2),
         name="head_gradient",
     )(rows, core_rows, mine, theirs)

time: 72.2 us -> 71.9 us (level)
  waiting for transfers between devices: 13.9 us -> 13.1 us
  Pallas kernels: 15.4 us -> 16.2 us
    pallas_call x1, Pallas kernels: 5.21 us -> 5.98 us  [head_gradient(): pl.pallas_call(head_kernel, grid=(depth // tile,), out_shape=shape((depth...]
    ppermute x30, waiting for transfers between devices: 13.9 us -> 13.1 us  [swap(): return lax.ppermute(value, AXES, [(i, i ^ mask) for i in range(count)])]
  transfers between devices with their start and end apart: 30 -> 30, of which waited for: 13 -> 12; matrix products, arithmetic and copies ran while one was open for 5% -> 5% of each run, Pallas kernels for 15% -> 16%
where the time goes in v17:
time: 71.9 us; the launch traced here: 71.7 us
  starting transfers between devices  34.9 us (49%)
  Pallas kernels  16.2 us (23%)
  waiting for transfers between devices  13.1 us (18%)
  local copies, waits for them, and re-layouts  5.47 us (8%)
  other arithmetic  1.23 us (2%)
  between operations  0.82 us (1%)
    ppermute x30, starting transfers between devices, swap(): return lax.ppermute(value, AXES, [(i, i ^ mask) for i in range(count)])  34.9 us
    ppermute x30, waiting for transfers between devices, swap(): return lax.ppermute(value, AXES, [(i, i ^ mask) for i in range(count)])  13.1 us
    pallas_call x1, Pallas kernels, head_gradient(): pl.pallas_call(head_kernel, grid=(depth // tile,), out_shape=shape((depth...  5.98 us
    pallas_call x1, Pallas kernels, back_rows(): pl.pallas_call(lambda *refs: back_kernel(bits, edges, low, len(stats), *r...  4.43 us
    pallas_call x1, Pallas kernels, far_logits(): pl.pallas_call(lambda *refs: far_kernel(len(pieces), *refs), out_shape=(s...  2.19 us
    dynamic_slice x2, local copies, waits for them, and re-layouts, cut(): return lax.dynamic_slice(value, indices, sizes)  2.13 us
    pallas_call x2, Pallas kernels, near_logits(): pl.pallas_call(near_kernel, out_shape=(shape((per, cols), F32), shape((ST...  1.74 us
  transfers between devices with their start and end apart: 30, of which 12 were waited for; matrix products, arithmetic and copies ran while one was open for 5% of the time, Pallas kernels for 16%

profile of v17, /device:TPU:0, one launch (start us, length us, event | category | flops | bytes accessed | tf_op | source)
XLA Modules:
  0.0 71.7 jit_solution(14365948631146226498)
XLA Ops:
  0.7 0.0 copy-start
  0.7 0.1 pad_add_fusion.2.at_ref
  0.7 0.1 pad_add_fusion
  0.8 1.1 %constant_dynamic-slice_fusion.1 = bf16[24,3584]{1,0:T(8,128)(2,1)S(1)} fusion(bf16[128,3584]{1,0:T(8,128)(2,1)} %refs_8_, u32[]{:T(128)S(6)} %convert_element_type.149), kind=kLoop, calls=%fused_computation.42 | loop fusion | bytes 344068 | tf_op jit(solution)/shard_map/dynamic_slice | solution.py:377
  2.0 0.5 collective-permute-start
  2.5 2.6 %collective-permute-start.1 = (bf16[24,3584]{1,0:T(8,128)(2,1)S(1)}, bf16[24,3584]{1,0:T(8,128)(2,1)S(1)}, u32[]{:S(2)}, u32[]{:S(2)}) collective-permute-start(bf16[24,3584]{1,0:T(8,128)(2,1)S(1)} %constant_dynamic-slice_fusion.1), channel_id=1, source_target_pairs={{0,16},{1,17},{2,18},{3,19},{4,20},{5,21},{6,22},{7,23},{8,24},{9,... | collective-permute-start | bytes 516104 | tf_op jit(solution)/shard_map/ppermute | solution.py:350
  5.0 1.0 %slice.173 = bf16[32,3584]{1,0:T(8,128)(2,1)S(1)} slice(bf16[128,3584]{1,0:T(8,128)(2,1)} %refs_8_), slice={[96:128], [0:3584]} | slice | bytes 458752 | tf_op jit(solution)/shard_map/slice | solution.py:384
  6.0 0.1 collective-permute-start.6
  6.1 1.1 %copy.7 = bf16[128,4,512]{2,0,1:T(8,128)(2,1)S(1)} copy(bf16[128,4,512]{2,1,0:T(4,128)(2,1)} %param.9) | data formatting | bytes 1048576 | tf_op jit(solution)/shard_map/optimization_barrier | solution.py:353
  7.3 0.4 taught_stats.1.refs_11_
  7.6 0.2 collective-permute-start.2
  7.8 1.0 %constant_dynamic-slice_fusion = bf16[24,3584]{1,0:T(8,128)(2,1)S(1)} fusion(bf16[128,3584]{1,0:T(8,128)(2,1)} %refs_8_, u32[]{:T(128)S(6)} %convert_element_type.150), kind=kLoop, calls=%fused_computation.41 | loop fusion | bytes 344068 | tf_op jit(solution)/shard_map/dynamic_slice | solution.py:377
  8.8 1.9 %collective-permute-start.5 = (bf16[24,3584]{1,0:T(8,128)(2,1)S(1)}, bf16[24,3584]{1,0:T(8,128)(2,1)S(1)}, u32[]{:S(2)}, u32[]{:S(2)}) collective-permute-start(bf16[24,3584]{1,0:T(8,128)(2,1)S(1)} %constant_dynamic-slice_fusion), channel_id=1, source_target_pairs={{0,16},{1,17},{2,18},{3,19},{4,20},{5,21},{6,22},{7,23},{8,24},{9,... | collective-permute-start | bytes 516104 | tf_op jit(solution)/shard_map/ppermute | solution.py:350
  10.8 0.0 collective-permute-done.2.refs_12_
  10.8 0.0 collective-permute-done.1.refs_0_.refs_1_
  10.8 1.6 %collective-permute-start.4 = (bf16[24,3584]{1,0:T(8,128)(2,1)S(1)}, bf16[24,3584]{1,0:T(8,128)(2,1)S(1)}, u32[]{:S(2)}, u32[]{:S(2)}) collective-permute-start(bf16[24,3584]{1,0:T(8,128)(2,1)S(1)} %collective-permute-done.1.refs_0_.refs_1_), channel_id=1, source_target_pairs={{0,2},{1,3},{2,0},{3,1},{4,6},{5,7},{6,4},{7,5},{8,10},{9,11},{10,... | collective-permute-start | bytes 516104 | tf_op jit(solution)/shard_map/ppermute | solution.py:350
  12.4 1.5 %collective-permute-start.3 = (bf16[24,3584]{1,0:T(8,128)(2,1)S(1)}, bf16[24,3584]{1,0:T(8,128)(2,1)S(1)}, u32[]{:S(2)}, u32[]{:S(2)}) collective-permute-start(bf16[24,3584]{1,0:T(8,128)(2,1)S(1)} %collective-permute-done.1.refs_0_.refs_1_), channel_id=1, source_target_pairs={{0,1},{1,0},{2,3},{3,2},{4,5},{5,4},{6,7},{7,6},{8,9},{9,8},{10,11... | collective-permute-start | bytes 516104 | tf_op jit(solution)/shard_map/ppermute | solution.py:350
  13.9 1.2 %copy-done.1 = bf16[128,3584]{1,0:T(8,128)(2,1)S(1)} copy-done((bf16[128,3584]{1,0:T(8,128)(2,1)S(1)}, bf16[128,3584]{1,0:T(8,128)(2,1)}, u32[]{:S(2)}) %copy-start.1) | copy-done | bytes 917528
  15.1 0.9 %near_logits.2 = (f32[128,512]{1,0:T(8,128)S(1)}, f32[8,128]{1,0:T(8,128)S(1)}) custom-call(bf16[128,3584]{1,0:T(8,128)(2,1)S(1)} %copy-done.1, bf16[3584,512]{1,0:T(8,128)(2,1)S(1)} %copy-done, bf16[24,3584]{1,0:T(8,128)(2,1)S(1)} %collective-permute-done.1.refs_0_.refs_1_), custom_call_target="tpu_custom_call" | custom-call | flops 469762048 | bytes 4587520 | tf_op jit(solution)/shard_map/near_logits/pallas_call | solution.py:109
  15.9 0.9 %near_logits.3 = (f32[128,512]{1,0:T(8,128)S(1)}, f32[8,128]{1,0:T(8,128)S(1)}) custom-call(bf16[128,3584]{1,0:T(8,128)(2,1)S(1)} %copy-done.1, bf16[3584,512]{1,0:T(8,128)(2,1)S(1)} %collective-permute-done.w_ref.refs_7_.refs_2_, bf16[24,3584]{1,0:T(8,128)(2,1)S(1)} %collective-permute-done.1.refs_0_.refs_1_), custom_call_target="tpu_custom_call" | custom-call | flops 469762048 | bytes 4587520 | tf_op jit(solution)/shard_map/near_logits/pallas_call | solution.py:109
  16.8 1.8 %collective-permute-done.5.refs_4_ = bf16[24,3584]{1,0:T(8,128)(2,1)S(1)} collective-permute-done((bf16[24,3584]{1,0:T(8,128)(2,1)S(1)}, bf16[24,3584]{1,0:T(8,128)(2,1)S(1)}, u32[]{:S(2)}, u32[]{:S(2)}) %collective-permute-start.5) | collective-permute-done | bytes 172064 | tf_op jit(solution)/shard_map/ppermute | solution.py:350
  18.6 0.0 collective-permute-done.6.refs_5_
  18.6 0.0 collective-permute-done.4.refs_3_
  18.6 0.0 collective-permute-done.3.refs_2_
  18.6 1.8 %collective-permute-start.14 = (bf16[2,128,512]{2,1,0:T(8,128)(2,1)S(1)}, bf16[2,128,512]{2,1,0:T(8,128)(2,1)S(1)}, u32[]{:S(2)}, u32[]{:S(2)}) collective-permute-start(bf16[2,128,512]{2,1,0:T(8,128)(2,1)S(1)} %get-tuple-element.88.gone_ref), channel_id=1, source_target_pairs={{0,16},{1,17},{2,18},{3,19},{4,20},{5,21},{6,22},{7,23},{8,24},{9,... | collective-permute-start | bytes 786440 | tf_op jit(solution)/shard_map/ppermute | solution.py:350
  20.5 2.2 %far_logits.1 = (f32[128,512]{1,0:T(8,128)S(1)}, f32[128,512]{1,0:T(8,128)S(1)}, bf16[2,128,3584]{2,1,0:T(8,128)(2,1)S(1)}, f32[2,8,128]{2,1,0:T(8,128)S(1)}, f32[8,128]{1,0:T(8,128)S(1)}) custom-call(s32[4]{0:T(128)S(1)} %get-tuple-element.60.refs_0_, bf16[24,3584]{1,0:T(8,128)(2,1)S(1)} %collective-permute-done.1.refs_0_.refs_1_, ...), custom_call_target="tpu_custom_call" | custom-call | flops 939524096 | bytes 8257536 | tf_op jit(solution)/shard_map/far_logits/pallas_call | solution.py:161
  22.7 0.0 copy-start.3
  22.7 3.6 %collective-permute-start.9 = (f32[2,8,128]{2,1,0:T(8,128)S(1)}, f32[2,8,128]{2,1,0:T(8,128)S(1)}, u32[]{:S(2)}, u32[]{:S(2)}) collective-permute-start(f32[2,8,128]{2,1,0:T(8,128)S(1)} %get-tuple-element.80.refs_0_), channel_id=1, source_target_pairs={{0,6},{1,7},{2,4},{3,5},{4,2},{5,3},{6,0},{7,1},{8,14},{9,15},{10,... | collective-permute-start | bytes 24584 | tf_op jit(solution)/shard_map/ppermute | solution.py:350
  26.3 0.0 collective-permute-start.8
  26.3 0.8 %collective-permute-start.7 = (f32[2,8,128]{2,1,0:T(8,128)S(1)}, f32[2,8,128]{2,1,0:T(8,128)S(1)}, u32[]{:S(2)}, u32[]{:S(2)}) collective-permute-start(f32[2,8,128]{2,1,0:T(8,128)S(1)} %get-tuple-element.80.refs_0_), channel_id=1, source_target_pairs={{0,2},{1,3},{2,0},{3,1},{4,6},{5,7},{6,4},{7,5},{8,10},{9,11},{10,... | collective-permute-start | bytes 24584 | tf_op jit(solution)/shard_map/ppermute | solution.py:350
  27.1 0.0 collective-permute-start.13
  27.1 1.1 %collective-permute-done.9.refs_3_ = f32[2,8,128]{2,1,0:T(8,128)S(1)} collective-permute-done((f32[2,8,128]{2,1,0:T(8,128)S(1)}, f32[2,8,128]{2,1,0:T(8,128)S(1)}, u32[]{:S(2)}, u32[]{:S(2)}) %collective-permute-start.9) | collective-permute-done | bytes 8224 | tf_op jit(solution)/shard_map/ppermute | solution.py:350
  28.2 2.7 %collective-permute-done.8.refs_2_ = f32[2,8,128]{2,1,0:T(8,128)S(1)} collective-permute-done((f32[2,8,128]{2,1,0:T(8,128)S(1)}, f32[2,8,128]{2,1,0:T(8,128)S(1)}, u32[]{:S(2)}, u32[]{:S(2)}) %collective-permute-start.8) | collective-permute-done | bytes 8224 | tf_op jit(solution)/shard_map/ppermute | solution.py:350
  30.9 0.1 collective-permute-start.15
  31.0 1.6 %collective-permute-start.12 = (f32[2,8,128]{2,1,0:T(8,128)S(1)}, f32[2,8,128]{2,1,0:T(8,128)S(1)}, u32[]{:S(2)}, u32[]{:S(2)}) collective-permute-start(f32[2,8,128]{2,1,0:T(8,128)S(1)} %merge_stats.1.refs_3_), channel_id=1, source_target_pairs={{0,17},{1,16},{2,19},{3,18},{4,21},{5,20},{6,23},{7,22},{8,25},{9,... | collective-permute-start | bytes 24584 | tf_op jit(solution)/shard_map/ppermute | solution.py:350
  32.6 0.5 collective-permute-start.11
  33.1 1.5 %collective-permute-start.10 = (f32[2,8,128]{2,1,0:T(8,128)S(1)}, f32[2,8,128]{2,1,0:T(8,128)S(1)}, u32[]{:S(2)}, u32[]{:S(2)}) collective-permute-start(f32[2,8,128]{2,1,0:T(8,128)S(1)} %merge_stats.1.refs_3_), channel_id=1, source_target_pairs={{0,16},{1,17},{2,18},{3,19},{4,20},{5,21},{6,22},{7,23},{8,24},{9,... | collective-permute-start | bytes 24584 | tf_op jit(solution)/shard_map/ppermute | solution.py:350
  34.6 1.4 %teacher_rows.1 = (f32[2,128,1024]{2,1,0:T(8,128)S(1)}, f32[2,8,128]{2,1,0:T(8,128)S(1)}) custom-call(s32[2]{0:T(128)S(1)} %pad_add_fusion.2.at_ref, s32[4,1,128]{2,1,0:T(1,128)S(1)} %bitcast.42, bf16[2,128,512]{2,1,0:T(8,128)(2,1)S(1)} %get-tuple-element.87.kept_ref.a0, bf16[2,128,512]{2,1,0:T(8,128)(2,1)S(1)} %collective-permute-done.13.a1, ...), custom_call_target="tpu_custom_call" | custom-call | flops 268435456 | bytes 1572864 | tf_op jit(solution)/shard_map/teacher_rows/pallas_call | solution.py:82
  36.0 0.2 collective-permute-done.11.refs_5_
  36.2 0.5 collective-permute-done.10.refs_4_
  36.7 4.4 %back_rows.1 = (bf16[256,512]{1,0:T(8,128)(2,1)S(1)}, bf16[256,512]{1,0:T(8,128)(2,1)S(1)}, bf16[128,1152]{1,0:T(8,128)(2,1)S(1)}, bf16[128,1152]{1,0:T(8,128)(2...) custom-call(s32[4]{0:T(128)S(1)} %get-tuple-element.55.refs_0_, ...), custom_call_target="tpu_custom_call" | custom-call | flops 1879048192 | bytes 7340032 | tf_op jit(solution)/shard_map/back_rows/pallas_call | solution.py:294
  41.1 0.1 collective-permute-start.16
  41.2 0.5 collective-permute-start.17
  41.7 1.5 %collective-permute-start.18 = (bf16[128,1152]{1,0:T(8,128)(2,1)S(1)}, bf16[128,1152]{1,0:T(8,128)(2,1)S(1)}, u32[]{:S(2)}, u32[]{:S(2)}) collective-permute-start(bf16[128,1152]{1,0:T(8,128)(2,1)S(1)} %get-tuple-element.97), channel_id=1, source_target_pairs={{0,16},{1,17},{2,18},{3,19},{4,20},{5,21},{6,22},{7,23},{8,24},{9,... | collective-permute-start | bytes 884744 | tf_op jit(solution)/shard_map/ppermute | solution.py:350
  43.2 1.5 %collective-permute-start.22 = (bf16[128,1152]{1,0:T(8,128)(2,1)S(1)}, bf16[128,1152]{1,0:T(8,128)(2,1)S(1)}, u32[]{:S(2)}, u32[]{:S(2)}) collective-permute-start(bf16[128,1152]{1,0:T(8,128)(2,1)S(1)} %get-tuple-element.101), channel_id=1, source_target_pairs={{0,1},{1,0},{2,3},{3,2},{4,5},{5,4},{6,7},{7,6},{8,9},{9,8},{10,11... | collective-permute-start | bytes 884744 | tf_op jit(solution)/shard_map/ppermute | solution.py:350
  44.7 0.6 collective-permute-done.17.theirs_ref
  45.4 6.0 %head_gradient.1 = bf16[3584,512]{1,0:T(8,128)(2,1)} custom-call(bf16[2,128,3584]{2,1,0:T(8,128)(2,1)S(1)} %get-tuple-element.95.rows_ref, bf16[2,128,3584]{2,1,0:T(8,128)(2,1)S(1)} %collective-permute-done.16.core_ref, bf16[256,512]{1,0:T(8,128)(2,1)S(1)} %get-tuple-element.96.mine_ref, bf16[256,512]{1,0:T(8,128)(2,1)S(1)} %collective-permute-done.17.theirs_ref), custom_call_target="tpu_custom_call" | custom-call | flops 1879048192 | bytes 7340032 | tf_op jit(solution)/shard_map/head_gradient/pallas_call | solution.py:323
  51.3 0.6 collective-permute-done.22
  52.0 1.6 %collective-permute-start.19 = (bf16[1,2,2,1,16,1152]{5,4,3,2,1,0:T(8,128)(2,1)S(1)}, bf16[1,2,2,1,16,1152]{5,4,3,2,1,0:T(8,128)(2,1)S(1)}, u32[]{:S(2)}, u32[]{:S(2)}) collective-permute-start(bf16[1,2,2,1,16,1152]{5,4,3,2,1,0:T(8,128)(2,1)S(1)} %fusion.1), channel_id=1, source_target_pairs={{0,1},{1,0},{2,3},{3,2},{4,5},{5,4},{6,7},{7,6},{8,9},{9,8},{10,11... | collective-permute-start | bytes 442376 | tf_op jit(solution)/shard_map/ppermute | solution.py:350
  53.5 0.1 add_convert_fusion
  53.7 1.8 %collective-permute-start.23 = (bf16[2,2,1,1,16,1152]{5,4,3,2,1,0:T(8,128)(2,1)S(1)}, bf16[2,2,1,1,16,1152]{5,4,3,2,1,0:T(8,128)(2,1)S(1)}, u32[]{:S(2)}, u32[]{:S(2)}) collective-permute-start(bf16[2,2,1,1,16,1152]{5,4,3,2,1,0:T(8,128)(2,1)S(1)} %fusion), channel_id=1, source_target_pairs={{0,2},{1,3},{2,0},{3,1},{4,6},{5,7},{6,4},{7,5},{8,10},{9,11},{10,... | collective-permute-start | bytes 442376 | tf_op jit(solution)/shard_map/ppermute | solution.py:350
  55.5 0.5 collective-permute-start.27
  56.0 1.3 %collective-permute-done.19 = bf16[1,2,2,1,16,1152]{5,4,3,2,1,0:T(8,128)(2,1)S(1)} collective-permute-done((bf16[1,2,2,1,16,1152]{5,4,3,2,1,0:T(8,128)(2,1)S(1)}, bf16[1,2,2,1,16,1152]{5,4,3,2,1,0:T(8,128)(2,1)S(1)}, u32[]{:S(2)}, u32[]{:S(2)}) %collective-permute-start.19) | collective-permute-done | bytes 147488 | tf_op jit(solution)/shard_map/ppermute | solution.py:350
  57.4 1.6 %collective-permute-start.20 = (bf16[1,2,1,1,16,1152]{5,4,3,2,1,0:T(8,128)(2,1)S(1)}, bf16[1,2,1,1,16,1152]{5,4,3,2,1,0:T(8,128)(2,1)S(1)}, u32[]{:S(2)}, u32[]{:S(2)}) collective-permute-start(bf16[1,2,1,1,16,1152]{5,4,3,2,1,0:T(8,128)(2,1)S(1)} %fusion.7), channel_id=1, source_target_pairs={{0,2},{1,3},{2,0},{3,1},{4,6},{5,7},{6,4},{7,5},{8,10},{9,11},{10,... | collective-permute-start | bytes 221192 | tf_op jit(solution)/shard_map/ppermute | solution.py:350
  59.1 1.3 %collective-permute-start.24 = (bf16[1,2,1,1,16,1152]{5,4,3,2,1,0:T(8,128)(2,1)S(1)}, bf16[1,2,1,1,16,1152]{5,4,3,2,1,0:T(8,128)(2,1)S(1)}, u32[]{:S(2)}, u32[]{:S(2)}) collective-permute-start(bf16[1,2,1,1,16,1152]{5,4,3,2,1,0:T(8,128)(2,1)S(1)} %fusion.5), channel_id=1, source_target_pairs={{0,16},{1,17},{2,18},{3,19},{4,20},{5,21},{6,22},{7,23},{8,24},{9,... | collective-permute-start | bytes 221192 | tf_op jit(solution)/shard_map/ppermute | solution.py:350
  60.4 1.1 %collective-permute-done.27 = bf16[1,2,1,2,16,1280]{5,4,3,2,1,0:T(8,128)(2,1)S(1)} collective-permute-done((bf16[1,2,1,2,16,1280]{5,4,3,2,1,0:T(8,128)(2,1)S(1)}, bf16[1,2,1,2,16,1280]{5,4,3,2,1,0:T(8,128)(2,1)S(1)}, u32[]{:S(2)}, u32[]{:S(2)}) %collective-permute-start.27) | collective-permute-done | bytes 163872 | tf_op jit(solution)/shard_map/ppermute | solution.py:350
  61.5 0.5 collective-permute-start.28
  62.0 2.1 %collective-permute-start.21 = (bf16[1,1,1,1,16,1152]{5,4,3,2,1,0:T(8,128)(2,1)S(1)}, bf16[1,1,1,1,16,1152]{5,4,3,2,1,0:T(8,128)(2,1)S(1)}, u32[]{:S(2)}, u32[]{:S(2)}) collective-permute-start(bf16[1,1,1,1,16,1152]{5,4,3,2,1,0:T(8,128)(2,1)S(1)} %fusion.22), channel_id=1, source_target_pairs={{0,4},{1,5},{2,6},{3,7},{4,0},{5,1},{6,2},{7,3},{8,12},{9,13},{10,... | collective-permute-start | bytes 110600 | tf_op jit(solution)/shard_map/ppermute | solution.py:350
  64.1 1.4 %collective-permute-start.25 = (bf16[1,1,1,1,16,1152]{5,4,3,2,1,0:T(8,128)(2,1)S(1)}, bf16[1,1,1,1,16,1152]{5,4,3,2,1,0:T(8,128)(2,1)S(1)}, u32[]{:S(2)}, u32[]{:S(2)}) collective-permute-start(bf16[1,1,1,1,16,1152]{5,4,3,2,1,0:T(8,128)(2,1)S(1)} %fusion.16), channel_id=1, source_target_pairs={{0,4},{1,5},{2,6},{3,7},{4,0},{5,1},{6,2},{7,3},{8,12},{9,13},{10,... | collective-permute-start | bytes 110600 | tf_op jit(solution)/shard_map/ppermute | solution.py:350
  65.6 0.4 collective-permute-done.28
  66.0 2.1 %collective-permute-start.29 = (bf16[1,1,1,1,16,1280]{5,4,3,2,1,0:T(8,128)(2,1)S(1)}, bf16[1,1,1,1,16,1280]{5,4,3,2,1,0:T(8,128)(2,1)S(1)}, u32[]{:S(2)}, u32[]{:S(2)}) collective-permute-start(bf16[1,1,1,1,16,1280]{5,4,3,2,1,0:T(8,128)(2,1)S(1)} %fusion.10), channel_id=1, source_target_pairs={{0,4},{1,5},{2,6},{3,7},{4,0},{5,1},{6,2},{7,3},{8,12},{9,13},{10,... | collective-permute-start | bytes 122888 | tf_op jit(solution)/shard_map/ppermute | solution.py:350
  68.1 1.0 %collective-permute-done.25 = bf16[1,1,1,1,16,1152]{5,4,3,2,1,0:T(8,128)(2,1)S(1)} collective-permute-done((bf16[1,1,1,1,16,1152]{5,4,3,2,1,0:T(8,128)(2,1)S(1)}, bf16[1,1,1,1,16,1152]{5,4,3,2,1,0:T(8,128)(2,1)S(1)}, u32[]{:S(2)}, u32[]{:S(2)}) %collective-permute-start.25) | collective-permute-done | bytes 36896 | tf_op jit(solution)/shard_map/ppermute | solution.py:350
  69.1 1.9 %collective-permute-done.29 = bf16[1,1,1,1,16,1280]{5,4,3,2,1,0:T(8,128)(2,1)S(1)} collective-permute-done((bf16[1,1,1,1,16,1280]{5,4,3,2,1,0:T(8,128)(2,1)S(1)}, bf16[1,1,1,1,16,1280]{5,4,3,2,1,0:T(8,128)(2,1)S(1)}, u32[]{:S(2)}, u32[]{:S(2)}) %collective-permute-start.29) | collective-permute-done | bytes 40992 | tf_op jit(solution)/shard_map/ppermute | solution.py:350
  71.0 0.7 maximum_bitcast_fusion
  (35 shorter events, 0.5 us)
Async XLA Ops:
  0.7 13.2 %copy-start = (bf16[3584,512]{1,0:T(8,128)(2,1)S(1)}, bf16[3584,512]{1,0:T(8,128)(2,1)}, u32[]{:S(2)}) copy-start(bf16[3584,512]{1,0:T(8,128)(2,1)} %refs_1_) | copy-start | bytes 11010052
  2.0 14.0 %collective-permute-start = (bf16[3584,512]{1,0:T(8,128)(2,1)}, bf16[3584,512]{1,0:T(8,128)(2,1)S(1)}, u32[]{:S(2)}, u32[]{:S(2)}) collective-permute-start(bf16[3584,512]{1,0:T(8,128)(2,1)} %refs_1_), channel_id=1, source_target_pairs={{0,8},{1,9},{2,10},{3,11},{4,12},{5,13},{6,14},{7,15},{8,0},{9,1},... | collective-permute-start | bytes 11010056 | tf_op jit(solution)/shard_map/ppermute | solution.py:350
  2.5 8.3 %collective-permute-start.1 = (bf16[24,3584]{1,0:T(8,128)(2,1)S(1)}, bf16[24,3584]{1,0:T(8,128)(2,1)S(1)}, u32[]{:S(2)}, u32[]{:S(2)}) collective-permute-start(bf16[24,3584]{1,0:T(8,128)(2,1)S(1)} %constant_dynamic-slice_fusion.1), channel_id=1, source_target_pairs={{0,16},{1,17},{2,18},{3,19},{4,20},{5,21},{6,22},{7,23},{8,24},{9,... | collective-permute-start | bytes 516104 | tf_op jit(solution)/shard_map/ppermute | solution.py:350
  6.0 12.6 %collective-permute-start.6 = (bf16[32,3584]{1,0:T(8,128)(2,1)S(1)}, bf16[32,3584]{1,0:T(8,128)(2,1)S(1)}, u32[]{:S(2)}, u32[]{:S(2)}) collective-permute-start(bf16[32,3584]{1,0:T(8,128)(2,1)S(1)} %slice.173), channel_id=1, source_target_pairs={{0,16},{1,17},{2,18},{3,19},{4,20},{5,21},{6,22},{7,23},{8,24},{9,... | collective-permute-start | bytes 688136 | tf_op jit(solution)/shard_map/ppermute | solution.py:350
  7.6 3.1 %collective-permute-start.2 = (f32[8,128]{1,0:T(8,128)S(1)}, f32[8,128]{1,0:T(8,128)S(1)}, u32[]{:S(2)}, u32[]{:S(2)}) collective-permute-start(f32[8,128]{1,0:T(8,128)S(1)} %taught_stats.1.refs_11_), channel_id=1, source_target_pairs={{0,8},{1,9},{2,10},{3,11},{4,12},{5,13},{6,14},{7,15},{8,0},{9,1},... | collective-permute-start | bytes 12296 | tf_op jit(solution)/shard_map/ppermute | solution.py:350
  7.8 12.6 %copy-start.4 = (s32[128]{0:T(128)S(1)}, s32[128]{0:T(128)}, u32[]{:S(2)}) copy-start(s32[128]{0:T(128)} %param.6) | copy-start | bytes 1540
  8.8 9.8 %collective-permute-start.5 = (bf16[24,3584]{1,0:T(8,128)(2,1)S(1)}, bf16[24,3584]{1,0:T(8,128)(2,1)S(1)}, u32[]{:S(2)}, u32[]{:S(2)}) collective-permute-start(bf16[24,3584]{1,0:T(8,128)(2,1)S(1)} %constant_dynamic-slice_fusion), channel_id=1, source_target_pairs={{0,16},{1,17},{2,18},{3,19},{4,20},{5,21},{6,22},{7,23},{8,24},{9,... | collective-permute-start | bytes 516104 | tf_op jit(solution)/shard_map/ppermute | solution.py:350
  10.8 7.8 %collective-permute-start.4 = (bf16[24,3584]{1,0:T(8,128)(2,1)S(1)}, bf16[24,3584]{1,0:T(8,128)(2,1)S(1)}, u32[]{:S(2)}, u32[]{:S(2)}) collective-permute-start(bf16[24,3584]{1,0:T(8,128)(2,1)S(1)} %collective-permute-done.1.refs_0_.refs_1_), channel_id=1, source_target_pairs={{0,2},{1,3},{2,0},{3,1},{4,6},{5,7},{6,4},{7,5},{8,10},{9,11},{10,... | collective-permute-start | bytes 516104 | tf_op jit(solution)/shard_map/ppermute | solution.py:350
  12.4 6.3 %collective-permute-start.3 = (bf16[24,3584]{1,0:T(8,128)(2,1)S(1)}, bf16[24,3584]{1,0:T(8,128)(2,1)S(1)}, u32[]{:S(2)}, u32[]{:S(2)}) collective-permute-start(bf16[24,3584]{1,0:T(8,128)(2,1)S(1)} %collective-permute-done.1.refs_0_.refs_1_), channel_id=1, source_target_pairs={{0,1},{1,0},{2,3},{3,2},{4,5},{5,4},{6,7},{7,6},{8,9},{9,8},{10,11... | collective-permute-start | bytes 516104 | tf_op jit(solution)/shard_map/ppermute | solution.py:350
  13.9 1.2 %copy-start.1 = (bf16[128,3584]{1,0:T(8,128)(2,1)S(1)}, bf16[128,3584]{1,0:T(8,128)(2,1)}, u32[]{:S(2)}) copy-start(bf16[128,3584]{1,0:T(8,128)(2,1)} %refs_8_) | copy-start | bytes 2752516
  15.1 5.4 %copy-start.2 = (bf16[128,3584]{1,0:T(8,128)(2,1)S(1)}, bf16[128,3584]{1,0:T(8,128)(2,1)}, u32[]{:S(2)}) copy-start(bf16[128,3584]{1,0:T(8,128)(2,1)} %refs_8_) | copy-start | bytes 2752516
  18.6 12.3 %collective-permute-start.14 = (bf16[2,128,512]{2,1,0:T(8,128)(2,1)S(1)}, bf16[2,128,512]{2,1,0:T(8,128)(2,1)S(1)}, u32[]{:S(2)}, u32[]{:S(2)}) collective-permute-start(bf16[2,128,512]{2,1,0:T(8,128)(2,1)S(1)} %get-tuple-element.88.gone_ref), channel_id=1, source_target_pairs={{0,16},{1,17},{2,18},{3,19},{4,20},{5,21},{6,22},{7,23},{8,24},{9,... | collective-permute-start | bytes 786440 | tf_op jit(solution)/shard_map/ppermute | solution.py:350
  22.7 11.9 %copy-start.3 = (s32[512]{0:T(512)S(1)}, s32[512]{0:T(512)}, u32[]{:S(2)}) copy-start(s32[512]{0:T(512)} %param.7) | copy-start | bytes 6148
  22.7 5.5 %collective-permute-start.9 = (f32[2,8,128]{2,1,0:T(8,128)S(1)}, f32[2,8,128]{2,1,0:T(8,128)S(1)}, u32[]{:S(2)}, u32[]{:S(2)}) collective-permute-start(f32[2,8,128]{2,1,0:T(8,128)S(1)} %get-tuple-element.80.refs_0_), channel_id=1, source_target_pairs={{0,6},{1,7},{2,4},{3,5},{4,2},{5,3},{6,0},{7,1},{8,14},{9,15},{10,... | collective-permute-start | bytes 24584 | tf_op jit(solution)/shard_map/ppermute | solution.py:350
  26.3 4.5 %collective-permute-start.8 = (f32[2,8,128]{2,1,0:T(8,128)S(1)}, f32[2,8,128]{2,1,0:T(8,128)S(1)}, u32[]{:S(2)}, u32[]{:S(2)}) collective-permute-start(f32[2,8,128]{2,1,0:T(8,128)S(1)} %get-tuple-element.80.refs_0_), channel_id=1, source_target_pairs={{0,4},{1,5},{2,6},{3,7},{4,0},{5,1},{6,2},{7,3},{8,12},{9,13},{10,... | collective-permute-start | bytes 24584 | tf_op jit(solution)/shard_map/ppermute | solution.py:350
  26.3 4.5 %collective-permute-start.7 = (f32[2,8,128]{2,1,0:T(8,128)S(1)}, f32[2,8,128]{2,1,0:T(8,128)S(1)}, u32[]{:S(2)}, u32[]{:S(2)}) collective-permute-start(f32[2,8,128]{2,1,0:T(8,128)S(1)} %get-tuple-element.80.refs_0_), channel_id=1, source_target_pairs={{0,2},{1,3},{2,0},{3,1},{4,6},{5,7},{6,4},{7,5},{8,10},{9,11},{10,... | collective-permute-start | bytes 24584 | tf_op jit(solution)/shard_map/ppermute | solution.py:350
  27.1 7.4 %collective-permute-start.13 = (bf16[2,128,512]{2,1,0:T(8,128)(2,1)S(1)}, bf16[2,128,512]{2,1,0:T(8,128)(2,1)S(1)}, u32[]{:S(2)}, u32[]{:S(2)}) collective-permute-start(bf16[2,128,512]{2,1,0:T(8,128)(2,1)S(1)} %get-tuple-element.87.kept_ref.a0), channel_id=1, source_target_pairs={{0,8},{1,9},{2,10},{3,11},{4,12},{5,13},{6,14},{7,15},{8,0},{9,1},... | collective-permute-start | bytes 786440 | tf_op jit(solution)/shard_map/ppermute | solution.py:350
  30.9 3.6 %collective-permute-start.15 = (bf16[2,128,512]{2,1,0:T(8,128)(2,1)S(1)}, bf16[2,128,512]{2,1,0:T(8,128)(2,1)S(1)}, u32[]{:S(2)}, u32[]{:S(2)}) collective-permute-start(bf16[2,128,512]{2,1,0:T(8,128)(2,1)S(1)} %collective-permute-done.14.a2), channel_id=1, source_target_pairs={{0,8},{1,9},{2,10},{3,11},{4,12},{5,13},{6,14},{7,15},{8,0},{9,1},... | collective-permute-start | bytes 786440 | tf_op jit(solution)/shard_map/ppermute | solution.py:350
  31.0 5.0 %collective-permute-start.12 = (f32[2,8,128]{2,1,0:T(8,128)S(1)}, f32[2,8,128]{2,1,0:T(8,128)S(1)}, u32[]{:S(2)}, u32[]{:S(2)}) collective-permute-start(f32[2,8,128]{2,1,0:T(8,128)S(1)} %merge_stats.1.refs_3_), channel_id=1, source_target_pairs={{0,17},{1,16},{2,19},{3,18},{4,21},{5,20},{6,23},{7,22},{8,25},{9,... | collective-permute-start | bytes 24584 | tf_op jit(solution)/shard_map/ppermute | solution.py:350
  32.6 3.7 %collective-permute-start.11 = (f32[2,8,128]{2,1,0:T(8,128)S(1)}, f32[2,8,128]{2,1,0:T(8,128)S(1)}, u32[]{:S(2)}, u32[]{:S(2)}) collective-permute-start(f32[2,8,128]{2,1,0:T(8,128)S(1)} %merge_stats.1.refs_3_), channel_id=1, source_target_pairs={{0,1},{1,0},{2,3},{3,2},{4,5},{5,4},{6,7},{7,6},{8,9},{9,8},{10,11... | collective-permute-start | bytes 24584 | tf_op jit(solution)/shard_map/ppermute | solution.py:350
  33.1 3.7 %collective-permute-start.10 = (f32[2,8,128]{2,1,0:T(8,128)S(1)}, f32[2,8,128]{2,1,0:T(8,128)S(1)}, u32[]{:S(2)}, u32[]{:S(2)}) collective-permute-start(f32[2,8,128]{2,1,0:T(8,128)S(1)} %merge_stats.1.refs_3_), channel_id=1, source_target_pairs={{0,16},{1,17},{2,18},{3,19},{4,20},{5,21},{6,22},{7,23},{8,24},{9,... | collective-permute-start | bytes 24584 | tf_op jit(solution)/shard_map/ppermute | solution.py:350
  41.1 4.2 %collective-permute-start.16 = (bf16[2,128,3584]{2,1,0:T(8,128)(2,1)S(1)}, bf16[2,128,3584]{2,1,0:T(8,128)(2,1)S(1)}, u32[]{:S(2)}, u32[]{:S(2)}) collective-permute-start(bf16[2,128,3584]{2,1,0:T(8,128)(2,1)S(1)} %get-tuple-element.95.rows_ref), channel_id=1, source_target_pairs={{0,8},{1,9},{2,10},{3,11},{4,12},{5,13},{6,14},{7,15},{8,0},{9,1},... | collective-permute-start | bytes 5505032 | tf_op jit(solution)/shard_map/ppermute | solution.py:350
  41.2 4.1 %collective-permute-start.17 = (bf16[256,512]{1,0:T(8,128)(2,1)S(1)}, bf16[256,512]{1,0:T(8,128)(2,1)S(1)}, u32[]{:S(2)}, u32[]{:S(2)}) collective-permute-start(bf16[256,512]{1,0:T(8,128)(2,1)S(1)} %get-tuple-element.94), channel_id=1, source_target_pairs={{0,8},{1,9},{2,10},{3,11},{4,12},{5,13},{6,14},{7,15},{8,0},{9,1},... | collective-permute-start | bytes 786440 | tf_op jit(solution)/shard_map/ppermute | solution.py:350
  41.7 10.2 %collective-permute-start.26 = (bf16[128,1280]{1,0:T(8,128)(2,1)S(1)}, bf16[128,1280]{1,0:T(8,128)(2,1)S(1)}, u32[]{:S(2)}, u32[]{:S(2)}) collective-permute-start(bf16[128,1280]{1,0:T(8,128)(2,1)S(1)} %get-tuple-element.105), channel_id=1, source_target_pairs={{0,2},{1,3},{2,0},{3,1},{4,6},{5,7},{6,4},{7,5},{8,10},{9,11},{10,... | collective-permute-start | bytes 983048 | tf_op jit(solution)/shard_map/ppermute | solution.py:350
  41.7 9.6 %collective-permute-start.18 = (bf16[128,1152]{1,0:T(8,128)(2,1)S(1)}, bf16[128,1152]{1,0:T(8,128)(2,1)S(1)}, u32[]{:S(2)}, u32[]{:S(2)}) collective-permute-start(bf16[128,1152]{1,0:T(8,128)(2,1)S(1)} %get-tuple-element.97), channel_id=1, source_target_pairs={{0,16},{1,17},{2,18},{3,19},{4,20},{5,21},{6,22},{7,23},{8,24},{9,... | collective-permute-start | bytes 884744 | tf_op jit(solution)/shard_map/ppermute | solution.py:350
  43.2 8.7 %collective-permute-start.22 = (bf16[128,1152]{1,0:T(8,128)(2,1)S(1)}, bf16[128,1152]{1,0:T(8,128)(2,1)S(1)}, u32[]{:S(2)}, u32[]{:S(2)}) collective-permute-start(bf16[128,1152]{1,0:T(8,128)(2,1)S(1)} %get-tuple-element.101), channel_id=1, source_target_pairs={{0,1},{1,0},{2,3},{3,2},{4,5},{5,4},{6,7},{7,6},{8,9},{9,8},{10,11... | collective-permute-start | bytes 884744 | tf_op jit(solution)/shard_map/ppermute | solution.py:350
  52.0 5.4 %collective-permute-start.19 = (bf16[1,2,2,1,16,1152]{5,4,3,2,1,0:T(8,128)(2,1)S(1)}, bf16[1,2,2,1,16,1152]{5,4,3,2,1,0:T(8,128)(2,1)S(1)}, u32[]{:S(2)}, u32[]{:S(2)}) collective-permute-start(bf16[1,2,2,1,16,1152]{5,4,3,2,1,0:T(8,128)(2,1)S(1)} %fusion.1), channel_id=1, source_target_pairs={{0,1},{1,0},{2,3},{3,2},{4,5},{5,4},{6,7},{7,6},{8,9},{9,8},{10,11... | collective-permute-start | bytes 442376 | tf_op jit(solution)/shard_map/ppermute | solution.py:350
  53.7 5.4 %collective-permute-start.23 = (bf16[2,2,1,1,16,1152]{5,4,3,2,1,0:T(8,128)(2,1)S(1)}, bf16[2,2,1,1,16,1152]{5,4,3,2,1,0:T(8,128)(2,1)S(1)}, u32[]{:S(2)}, u32[]{:S(2)}) collective-permute-start(bf16[2,2,1,1,16,1152]{5,4,3,2,1,0:T(8,128)(2,1)S(1)} %fusion), channel_id=1, source_target_pairs={{0,2},{1,3},{2,0},{3,1},{4,6},{5,7},{6,4},{7,5},{8,10},{9,11},{10,... | collective-permute-start | bytes 442376 | tf_op jit(solution)/shard_map/ppermute | solution.py:350
  55.5 6.0 %collective-permute-start.27 = (bf16[1,2,1,2,16,1280]{5,4,3,2,1,0:T(8,128)(2,1)S(1)}, bf16[1,2,1,2,16,1280]{5,4,3,2,1,0:T(8,128)(2,1)S(1)}, u32[]{:S(2)}, u32[]{:S(2)}) collective-permute-start(bf16[1,2,1,2,16,1280]{5,4,3,2,1,0:T(8,128)(2,1)S(1)} %bitcast.59), channel_id=1, source_target_pairs={{0,16},{1,17},{2,18},{3,19},{4,20},{5,21},{6,22},{7,23},{8,24},{9,... | collective-permute-start | bytes 491528 | tf_op jit(solution)/shard_map/ppermute | solution.py:350
  57.4 4.6 %collective-permute-start.20 = (bf16[1,2,1,1,16,1152]{5,4,3,2,1,0:T(8,128)(2,1)S(1)}, bf16[1,2,1,1,16,1152]{5,4,3,2,1,0:T(8,128)(2,1)S(1)}, u32[]{:S(2)}, u32[]{:S(2)}) collective-permute-start(bf16[1,2,1,1,16,1152]{5,4,3,2,1,0:T(8,128)(2,1)S(1)} %fusion.7), channel_id=1, source_target_pairs={{0,2},{1,3},{2,0},{3,1},{4,6},{5,7},{6,4},{7,5},{8,10},{9,11},{10,... | collective-permute-start | bytes 221192 | tf_op jit(solution)/shard_map/ppermute | solution.py:350
  59.1 5.1 %collective-permute-start.24 = (bf16[1,2,1,1,16,1152]{5,4,3,2,1,0:T(8,128)(2,1)S(1)}, bf16[1,2,1,1,16,1152]{5,4,3,2,1,0:T(8,128)(2,1)S(1)}, u32[]{:S(2)}, u32[]{:S(2)}) collective-permute-start(bf16[1,2,1,1,16,1152]{5,4,3,2,1,0:T(8,128)(2,1)S(1)} %fusion.5), channel_id=1, source_target_pairs={{0,16},{1,17},{2,18},{3,19},{4,20},{5,21},{6,22},{7,23},{8,24},{9,... | collective-permute-start | bytes 221192 | tf_op jit(solution)/shard_map/ppermute | solution.py:350
  61.5 4.5 %collective-permute-start.28 = (bf16[1,2,1,1,16,1280]{5,4,3,2,1,0:T(8,128)(2,1)S(1)}, bf16[1,2,1,1,16,1280]{5,4,3,2,1,0:T(8,128)(2,1)S(1)}, u32[]{:S(2)}, u32[]{:S(2)}) collective-permute-start(bf16[1,2,1,1,16,1280]{5,4,3,2,1,0:T(8,128)(2,1)S(1)} %fusion.3), channel_id=1, source_target_pairs={{0,1},{1,0},{2,3},{3,2},{4,5},{5,4},{6,7},{7,6},{8,9},{9,8},{10,11... | collective-permute-start | bytes 245768 | tf_op jit(solution)/shard_map/ppermute | solution.py:350
  62.0 6.1 %collective-permute-start.21 = (bf16[1,1,1,1,16,1152]{5,4,3,2,1,0:T(8,128)(2,1)S(1)}, bf16[1,1,1,1,16,1152]{5,4,3,2,1,0:T(8,128)(2,1)S(1)}, u32[]{:S(2)}, u32[]{:S(2)}) collective-permute-start(bf16[1,1,1,1,16,1152]{5,4,3,2,1,0:T(8,128)(2,1)S(1)} %fusion.22), channel_id=1, source_target_pairs={{0,4},{1,5},{2,6},{3,7},{4,0},{5,1},{6,2},{7,3},{8,12},{9,13},{10,... | collective-permute-start | bytes 110600 | tf_op jit(solution)/shard_map/ppermute | solution.py:350
  64.1 4.9 %collective-permute-start.25 = (bf16[1,1,1,1,16,1152]{5,4,3,2,1,0:T(8,128)(2,1)S(1)}, bf16[1,1,1,1,16,1152]{5,4,3,2,1,0:T(8,128)(2,1)S(1)}, u32[]{:S(2)}, u32[]{:S(2)}) collective-permute-start(bf16[1,1,1,1,16,1152]{5,4,3,2,1,0:T(8,128)(2,1)S(1)} %fusion.16), channel_id=1, source_target_pairs={{0,4},{1,5},{2,6},{3,7},{4,0},{5,1},{6,2},{7,3},{8,12},{9,13},{10,... | collective-permute-start | bytes 110600 | tf_op jit(solution)/shard_map/ppermute | solution.py:350
  66.0 5.0 %collective-permute-start.29 = (bf16[1,1,1,1,16,1280]{5,4,3,2,1,0:T(8,128)(2,1)S(1)}, bf16[1,1,1,1,16,1280]{5,4,3,2,1,0:T(8,128)(2,1)S(1)}, u32[]{:S(2)}, u32[]{:S(2)}) collective-permute-start(bf16[1,1,1,1,16,1280]{5,4,3,2,1,0:T(8,128)(2,1)S(1)} %fusion.10), channel_id=1, source_target_pairs={{0,4},{1,5},{2,6},{3,7},{4,0},{5,1},{6,2},{7,3},{8,12},{9,13},{10,... | collective-permute-start | bytes 122888 | tf_op jit(solution)/shard_map/ppermute | solution.py:350

commit v18 on v16

--- a/solution.py
+++ b/solution.py
@@ -419,14 +419,16 @@
         who, served, [kept, kept_core, taught_x, taught_far]
     )
     parts = [stats] + [swap(stats, mask) for mask in (X, Y, X + Y)]
+    *parts, taught_soft, rows_sent = tie(*parts, taught_soft, both_rows)
+    core_rows = swap(rows_sent, CORE)
 
     bits = shards.bit_length() - 1
     masks = {0: X}
     for b in range(bits):
         masks[1 + b] = shards >> (1 + b)
     ydim, wdim = bits, bits - 1
-    third = depth // 128 // 3 * 128
-    edges = (0, third, 2 * third, depth)
+    units = depth // 128
+    edges = (0, units // 3 * 128, units // 3 * 256, depth)
     orders = [(0, ydim, wdim), (ydim, wdim, 0), (wdim, 0, ydim)]
     low = owned.bit_length() - 1
     row_bit = {0: low + bits, ydim: low, wdim: low + 1}
@@ -437,8 +439,7 @@
     )
     gots = [swap(sents[p], masks[orders[p][0]]) for p in range(3)]
     theirs = swap(gother, CORE)
-    _, rows_sent = tie(gother, both_rows)
-    grad_head = head_gradient(both_rows, swap(rows_sent, CORE), gown, theirs)
+    grad_head = head_gradient(both_rows, core_rows, gown, theirs)
     for p in range(3):
         grad_head, gots[p] = tie(grad_head, gots[p])
 

time: 72.2 us -> 72.3 us (level)
  transfers between devices with their start and end apart: 30 -> 30, of which waited for: 13 -> 12; matrix products, arithmetic and copies ran while one was open for 5% -> 5% of each run, Pallas kernels for 15% -> 21%
where the time goes in v18:
time: 72.3 us; the launch traced here: 72 us
  starting transfers between devices  35 us (48%)
  Pallas kernels  15.4 us (21%)
  waiting for transfers between devices  14.2 us (20%)
  local copies, waits for them, and re-layouts  5.47 us (8%)
  other arithmetic  1.18 us (2%)
  between operations  0.82 us (1%)
    ppermute x30, starting transfers between devices, swap(): return lax.ppermute(value, AXES, [(i, i ^ mask) for i in range(count)])  35 us
    ppermute x30, waiting for transfers between devices, swap(): return lax.ppermute(value, AXES, [(i, i ^ mask) for i in range(count)])  14.2 us
    pallas_call x1, Pallas kernels, head_gradient(): pl.pallas_call(head_kernel, grid=(depth // tile,), out_shape=shape((depth...  5.21 us
    pallas_call x1, Pallas kernels, back_rows(): pl.pallas_call(lambda *refs: back_kernel(bits, edges, low, len(stats), *r...  4.42 us
    pallas_call x1, Pallas kernels, far_logits(): pl.pallas_call(lambda *refs: far_kernel(len(pieces), *refs), out_shape=(s...  2.19 us
    dynamic_slice x2, local copies, waits for them, and re-layouts, cut(): return lax.dynamic_slice(value, indices, sizes)  2.13 us
    pallas_call x2, Pallas kernels, near_logits(): pl.pallas_call(near_kernel, out_shape=(shape((per, cols), F32), shape((ST...  1.74 us
  transfers between devices with their start and end apart: 30, of which 12 were waited for; matrix products, arithmetic and copies ran while one was open for 5% of the time, Pallas kernels for 21%

profile of v18, /device:TPU:0, one launch (start us, length us, event | category | flops | bytes accessed | tf_op | source)
XLA Modules:
  0.0 72.0 jit_solution(13276150555156045273)
XLA Ops:
  0.7 0.0 copy-start
  0.7 0.1 pad_add_fusion.2.at_ref
  0.7 0.1 pad_add_fusion
  0.8 1.1 %constant_dynamic-slice_fusion.1 = bf16[24,3584]{1,0:T(8,128)(2,1)S(1)} fusion(bf16[128,3584]{1,0:T(8,128)(2,1)} %refs_8_, u32[]{:T(128)S(6)} %convert_element_type.149), kind=kLoop, calls=%fused_computation.42 | loop fusion | bytes 344068 | tf_op jit(solution)/shard_map/dynamic_slice | solution.py:375
  2.0 0.5 collective-permute-start
  2.5 2.6 %collective-permute-start.1 = (bf16[24,3584]{1,0:T(8,128)(2,1)S(1)}, bf16[24,3584]{1,0:T(8,128)(2,1)S(1)}, u32[]{:S(2)}, u32[]{:S(2)}) collective-permute-start(bf16[24,3584]{1,0:T(8,128)(2,1)S(1)} %constant_dynamic-slice_fusion.1), channel_id=1, source_target_pairs={{0,16},{1,17},{2,18},{3,19},{4,20},{5,21},{6,22},{7,23},{8,24},{9,... | collective-permute-start | bytes 516104 | tf_op jit(solution)/shard_map/ppermute | solution.py:348
  5.0 1.0 %slice.173 = bf16[32,3584]{1,0:T(8,128)(2,1)S(1)} slice(bf16[128,3584]{1,0:T(8,128)(2,1)} %refs_8_), slice={[96:128], [0:3584]} | slice | bytes 458752 | tf_op jit(solution)/shard_map/slice | solution.py:382
  6.0 0.1 collective-permute-start.6
  6.1 1.1 %copy.7 = bf16[128,4,512]{2,0,1:T(8,128)(2,1)S(1)} copy(bf16[128,4,512]{2,1,0:T(4,128)(2,1)} %param.9) | data formatting | bytes 1048576 | tf_op jit(solution)/shard_map/optimization_barrier | solution.py:351
  7.3 0.4 taught_stats.1.refs_11_
  7.6 0.2 collective-permute-start.2
  7.8 1.0 %constant_dynamic-slice_fusion = bf16[24,3584]{1,0:T(8,128)(2,1)S(1)} fusion(bf16[128,3584]{1,0:T(8,128)(2,1)} %refs_8_, u32[]{:T(128)S(6)} %convert_element_type.150), kind=kLoop, calls=%fused_computation.41 | loop fusion | bytes 344068 | tf_op jit(solution)/shard_map/dynamic_slice | solution.py:375
  8.8 1.9 %collective-permute-start.5 = (bf16[24,3584]{1,0:T(8,128)(2,1)S(1)}, bf16[24,3584]{1,0:T(8,128)(2,1)S(1)}, u32[]{:S(2)}, u32[]{:S(2)}) collective-permute-start(bf16[24,3584]{1,0:T(8,128)(2,1)S(1)} %constant_dynamic-slice_fusion), channel_id=1, source_target_pairs={{0,16},{1,17},{2,18},{3,19},{4,20},{5,21},{6,22},{7,23},{8,24},{9,... | collective-permute-start | bytes 516104 | tf_op jit(solution)/shard_map/ppermute | solution.py:348
  10.8 1.6 %collective-permute-start.4 = (bf16[24,3584]{1,0:T(8,128)(2,1)S(1)}, bf16[24,3584]{1,0:T(8,128)(2,1)S(1)}, u32[]{:S(2)}, u32[]{:S(2)}) collective-permute-start(bf16[24,3584]{1,0:T(8,128)(2,1)S(1)} %collective-permute-done.1.refs_0_.refs_1_), channel_id=1, source_target_pairs={{0,2},{1,3},{2,0},{3,1},{4,6},{5,7},{6,4},{7,5},{8,10},{9,11},{10,... | collective-permute-start | bytes 516104 | tf_op jit(solution)/shard_map/ppermute | solution.py:348
  12.4 1.5 %collective-permute-start.3 = (bf16[24,3584]{1,0:T(8,128)(2,1)S(1)}, bf16[24,3584]{1,0:T(8,128)(2,1)S(1)}, u32[]{:S(2)}, u32[]{:S(2)}) collective-permute-start(bf16[24,3584]{1,0:T(8,128)(2,1)S(1)} %collective-permute-done.1.refs_0_.refs_1_), channel_id=1, source_target_pairs={{0,1},{1,0},{2,3},{3,2},{4,5},{5,4},{6,7},{7,6},{8,9},{9,8},{10,11... | collective-permute-start | bytes 516104 | tf_op jit(solution)/shard_map/ppermute | solution.py:348
  13.9 1.2 %copy-done.1 = bf16[128,3584]{1,0:T(8,128)(2,1)S(1)} copy-done((bf16[128,3584]{1,0:T(8,128)(2,1)S(1)}, bf16[128,3584]{1,0:T(8,128)(2,1)}, u32[]{:S(2)}) %copy-start.1) | copy-done | bytes 917528
  15.1 0.9 %near_logits.2 = (f32[128,512]{1,0:T(8,128)S(1)}, f32[8,128]{1,0:T(8,128)S(1)}) custom-call(bf16[128,3584]{1,0:T(8,128)(2,1)S(1)} %copy-done.1, bf16[3584,512]{1,0:T(8,128)(2,1)S(1)} %copy-done, bf16[24,3584]{1,0:T(8,128)(2,1)S(1)} %collective-permute-done.1.refs_0_.refs_1_), custom_call_target="tpu_custom_call" | custom-call | flops 469762048 | bytes 4587520 | tf_op jit(solution)/shard_map/near_logits/pallas_call | solution.py:109
  15.9 0.0 collective-permute-done.w_ref.refs_7_.refs_2_
  15.9 0.9 %near_logits.3 = (f32[128,512]{1,0:T(8,128)S(1)}, f32[8,128]{1,0:T(8,128)S(1)}) custom-call(bf16[128,3584]{1,0:T(8,128)(2,1)S(1)} %copy-done.1, bf16[3584,512]{1,0:T(8,128)(2,1)S(1)} %collective-permute-done.w_ref.refs_7_.refs_2_, bf16[24,3584]{1,0:T(8,128)(2,1)S(1)} %collective-permute-done.1.refs_0_.refs_1_), custom_call_target="tpu_custom_call" | custom-call | flops 469762048 | bytes 4587520 | tf_op jit(solution)/shard_map/near_logits/pallas_call | solution.py:109
  16.8 1.8 %collective-permute-done.5.refs_4_ = bf16[24,3584]{1,0:T(8,128)(2,1)S(1)} collective-permute-done((bf16[24,3584]{1,0:T(8,128)(2,1)S(1)}, bf16[24,3584]{1,0:T(8,128)(2,1)S(1)}, u32[]{:S(2)}, u32[]{:S(2)}) %collective-permute-start.5) | collective-permute-done | bytes 172064 | tf_op jit(solution)/shard_map/ppermute | solution.py:348
  18.6 0.0 collective-permute-done.6.refs_5_
  18.6 0.0 collective-permute-done.4.refs_3_
  18.6 0.0 collective-permute-done.3.refs_2_
  18.6 1.8 %collective-permute-start.14 = (bf16[2,128,512]{2,1,0:T(8,128)(2,1)S(1)}, bf16[2,128,512]{2,1,0:T(8,128)(2,1)S(1)}, u32[]{:S(2)}, u32[]{:S(2)}) collective-permute-start(bf16[2,128,512]{2,1,0:T(8,128)(2,1)S(1)} %get-tuple-element.92.gone_ref), channel_id=1, source_target_pairs={{0,16},{1,17},{2,18},{3,19},{4,20},{5,21},{6,22},{7,23},{8,24},{9,... | collective-permute-start | bytes 786440 | tf_op jit(solution)/shard_map/ppermute | solution.py:348
  20.5 2.2 %far_logits.1 = (f32[128,512]{1,0:T(8,128)S(1)}, f32[128,512]{1,0:T(8,128)S(1)}, bf16[2,128,3584]{2,1,0:T(8,128)(2,1)S(1)}, f32[2,8,128]{2,1,0:T(8,128)S(1)}, f32[8,128]{1,0:T(8,128)S(1)}) custom-call(s32[4]{0:T(128)S(1)} %get-tuple-element.65.refs_0_, bf16[24,3584]{1,0:T(8,128)(2,1)S(1)} %collective-permute-done.1.refs_0_.refs_1_, ...), custom_call_target="tpu_custom_call" | custom-call | flops 939524096 | bytes 8257536 | tf_op jit(solution)/shard_map/far_logits/pallas_call | solution.py:161
  22.7 0.0 copy-start.3
  22.7 3.6 %collective-permute-start.9 = (f32[2,8,128]{2,1,0:T(8,128)S(1)}, f32[2,8,128]{2,1,0:T(8,128)S(1)}, u32[]{:S(2)}, u32[]{:S(2)}) collective-permute-start(f32[2,8,128]{2,1,0:T(8,128)S(1)} %get-tuple-element.85.refs_0_), channel_id=1, source_target_pairs={{0,6},{1,7},{2,4},{3,5},{4,2},{5,3},{6,0},{7,1},{8,14},{9,15},{10,... | collective-permute-start | bytes 24584 | tf_op jit(solution)/shard_map/ppermute | solution.py:348
  26.3 0.0 collective-permute-start.8
  26.3 0.8 %collective-permute-start.7 = (f32[2,8,128]{2,1,0:T(8,128)S(1)}, f32[2,8,128]{2,1,0:T(8,128)S(1)}, u32[]{:S(2)}, u32[]{:S(2)}) collective-permute-start(f32[2,8,128]{2,1,0:T(8,128)S(1)} %get-tuple-element.85.refs_0_), channel_id=1, source_target_pairs={{0,2},{1,3},{2,0},{3,1},{4,6},{5,7},{6,4},{7,5},{8,10},{9,11},{10,... | collective-permute-start | bytes 24584 | tf_op jit(solution)/shard_map/ppermute | solution.py:348
  27.1 0.0 collective-permute-start.13
  27.1 1.1 %collective-permute-done.9.refs_3_ = f32[2,8,128]{2,1,0:T(8,128)S(1)} collective-permute-done((f32[2,8,128]{2,1,0:T(8,128)S(1)}, f32[2,8,128]{2,1,0:T(8,128)S(1)}, u32[]{:S(2)}, u32[]{:S(2)}) %collective-permute-start.9) | collective-permute-done | bytes 8224 | tf_op jit(solution)/shard_map/ppermute | solution.py:348
  28.2 2.7 %collective-permute-done.8.refs_2_ = f32[2,8,128]{2,1,0:T(8,128)S(1)} collective-permute-done((f32[2,8,128]{2,1,0:T(8,128)S(1)}, f32[2,8,128]{2,1,0:T(8,128)S(1)}, u32[]{:S(2)}, u32[]{:S(2)}) %collective-permute-start.8) | collective-permute-done | bytes 8224 | tf_op jit(solution)/shard_map/ppermute | solution.py:348
  30.9 0.0 collective-permute-done.7.refs_1_
  30.9 0.0 collective-permute-done.14.a2
  30.9 0.1 collective-permute-start.15
  31.0 1.6 %collective-permute-start.12 = (f32[2,8,128]{2,1,0:T(8,128)S(1)}, f32[2,8,128]{2,1,0:T(8,128)S(1)}, u32[]{:S(2)}, u32[]{:S(2)}) collective-permute-start(f32[2,8,128]{2,1,0:T(8,128)S(1)} %merge_stats.1.refs_3_), channel_id=1, source_target_pairs={{0,17},{1,16},{2,19},{3,18},{4,21},{5,20},{6,23},{7,22},{8,25},{9,... | collective-permute-start | bytes 24584 | tf_op jit(solution)/shard_map/ppermute | solution.py:348
  32.6 0.5 collective-permute-start.11
  33.1 1.5 %collective-permute-start.10 = (f32[2,8,128]{2,1,0:T(8,128)S(1)}, f32[2,8,128]{2,1,0:T(8,128)S(1)}, u32[]{:S(2)}, u32[]{:S(2)}) collective-permute-start(f32[2,8,128]{2,1,0:T(8,128)S(1)} %merge_stats.1.refs_3_), channel_id=1, source_target_pairs={{0,16},{1,17},{2,18},{3,19},{4,20},{5,21},{6,22},{7,23},{8,24},{9,... | collective-permute-start | bytes 24584 | tf_op jit(solution)/shard_map/ppermute | solution.py:348
  34.5 0.0 collective-permute-done.13.a1
  34.6 1.4 %teacher_rows.1 = (f32[2,128,1024]{2,1,0:T(8,128)S(1)}, f32[2,8,128]{2,1,0:T(8,128)S(1)}) custom-call(s32[2]{0:T(128)S(1)} %pad_add_fusion.2.at_ref, s32[4,1,128]{2,1,0:T(1,128)S(1)} %bitcast.42, bf16[2,128,512]{2,1,0:T(8,128)(2,1)S(1)} %get-tuple-element.91.kept_ref.a0, bf16[2,128,512]{2,1,0:T(8,128)(2,1)S(1)} %collective-permute-done.13.a1, ...), custom_call_target="tpu_custom_call" | custom-call | flops 268435456 | bytes 1572864 | tf_op jit(solution)/shard_map/teacher_rows/pallas_call | solution.py:82
  36.0 0.2 collective-permute-done.11.refs_5_
  36.2 0.5 collective-permute-done.10.refs_4_
  36.7 4.4 %back_rows.1 = (bf16[256,512]{1,0:T(8,128)(2,1)S(1)}, bf16[256,512]{1,0:T(8,128)(2,1)S(1)}, bf16[128,1152]{1,0:T(8,128)(2,1)S(1)}, bf16[128,1152]{1,0:T(8,128)(2...) custom-call(s32[4]{0:T(128)S(1)} %get-tuple-element.60.refs_0_, ...), custom_call_target="tpu_custom_call" | custom-call | flops 1879048192 | bytes 7340032 | tf_op jit(solution)/shard_map/back_rows/pallas_call | solution.py:294
  41.1 0.6 collective-permute-start.17
  41.7 1.5 %collective-permute-start.18 = (bf16[128,1152]{1,0:T(8,128)(2,1)S(1)}, bf16[128,1152]{1,0:T(8,128)(2,1)S(1)}, u32[]{:S(2)}, u32[]{:S(2)}) collective-permute-start(bf16[128,1152]{1,0:T(8,128)(2,1)S(1)} %get-tuple-element.107), channel_id=1, source_target_pairs={{0,16},{1,17},{2,18},{3,19},{4,20},{5,21},{6,22},{7,23},{8,24},{9,... | collective-permute-start | bytes 884744 | tf_op jit(solution)/shard_map/ppermute | solution.py:348
  43.2 1.5 %collective-permute-start.22 = (bf16[128,1152]{1,0:T(8,128)(2,1)S(1)}, bf16[128,1152]{1,0:T(8,128)(2,1)S(1)}, u32[]{:S(2)}, u32[]{:S(2)}) collective-permute-start(bf16[128,1152]{1,0:T(8,128)(2,1)S(1)} %get-tuple-element.111), channel_id=1, source_target_pairs={{0,1},{1,0},{2,3},{3,2},{4,5},{5,4},{6,7},{7,6},{8,9},{9,8},{10,11... | collective-permute-start | bytes 884744 | tf_op jit(solution)/shard_map/ppermute | solution.py:348
  44.7 5.2 %head_gradient.1 = bf16[3584,512]{1,0:T(8,128)(2,1)} custom-call(bf16[2,128,3584]{2,1,0:T(8,128)(2,1)S(1)} %get-tuple-element.104.rows_ref, bf16[2,128,3584]{2,1,0:T(8,128)(2,1)S(1)} %collective-permute-done.16.core_ref, bf16[256,512]{1,0:T(8,128)(2,1)S(1)} %get-tuple-element.105.mine_ref, bf16[256,512]{1,0:T(8,128)(2,1)S(1)} %collective-permute-done.17.theirs_ref), custom_call_target="tpu_custom_call" | custom-call | flops 1879048192 | bytes 7340032 | tf_op jit(solution)/shard_map/head_gradient/pallas_call | solution.py:323
  49.9 0.8 %collective-permute-done.18 = bf16[128,1152]{1,0:T(8,128)(2,1)S(1)} collective-permute-done((bf16[128,1152]{1,0:T(8,128)(2,1)S(1)}, bf16[128,1152]{1,0:T(8,128)(2,1)S(1)}, u32[]{:S(2)}, u32[]{:S(2)}) %collective-permute-start.18) | collective-permute-done | bytes 294944 | tf_op jit(solution)/shard_map/ppermute | solution.py:348
  50.8 1.2 %collective-permute-done.22 = bf16[128,1152]{1,0:T(8,128)(2,1)S(1)} collective-permute-done((bf16[128,1152]{1,0:T(8,128)(2,1)S(1)}, bf16[128,1152]{1,0:T(8,128)(2,1)S(1)}, u32[]{:S(2)}, u32[]{:S(2)}) %collective-permute-start.22) | collective-permute-done | bytes 294944 | tf_op jit(solution)/shard_map/ppermute | solution.py:348
  52.0 1.6 %collective-permute-start.19 = (bf16[1,2,2,1,16,1152]{5,4,3,2,1,0:T(8,128)(2,1)S(1)}, bf16[1,2,2,1,16,1152]{5,4,3,2,1,0:T(8,128)(2,1)S(1)}, u32[]{:S(2)}, u32[]{:S(2)}) collective-permute-start(bf16[1,2,2,1,16,1152]{5,4,3,2,1,0:T(8,128)(2,1)S(1)} %fusion.1), channel_id=1, source_target_pairs={{0,1},{1,0},{2,3},{3,2},{4,5},{5,4},{6,7},{7,6},{8,9},{9,8},{10,11... | collective-permute-start | bytes 442376 | tf_op jit(solution)/shard_map/ppermute | solution.py:348
  53.7 1.7 %collective-permute-start.23 = (bf16[2,2,1,1,16,1152]{5,4,3,2,1,0:T(8,128)(2,1)S(1)}, bf16[2,2,1,1,16,1152]{5,4,3,2,1,0:T(8,128)(2,1)S(1)}, u32[]{:S(2)}, u32[]{:S(2)}) collective-permute-start(bf16[2,2,1,1,16,1152]{5,4,3,2,1,0:T(8,128)(2,1)S(1)} %fusion), channel_id=1, source_target_pairs={{0,2},{1,3},{2,0},{3,1},{4,6},{5,7},{6,4},{7,5},{8,10},{9,11},{10,... | collective-permute-start | bytes 442376 | tf_op jit(solution)/shard_map/ppermute | solution.py:348
  55.4 0.5 collective-permute-start.27
  56.0 1.2 %collective-permute-done.19 = bf16[1,2,2,1,16,1152]{5,4,3,2,1,0:T(8,128)(2,1)S(1)} collective-permute-done((bf16[1,2,2,1,16,1152]{5,4,3,2,1,0:T(8,128)(2,1)S(1)}, bf16[1,2,2,1,16,1152]{5,4,3,2,1,0:T(8,128)(2,1)S(1)}, u32[]{:S(2)}, u32[]{:S(2)}) %collective-permute-start.19) | collective-permute-done | bytes 147488 | tf_op jit(solution)/shard_map/ppermute | solution.py:348
  57.3 1.7 %collective-permute-start.20 = (bf16[1,2,1,1,16,1152]{5,4,3,2,1,0:T(8,128)(2,1)S(1)}, bf16[1,2,1,1,16,1152]{5,4,3,2,1,0:T(8,128)(2,1)S(1)}, u32[]{:S(2)}, u32[]{:S(2)}) collective-permute-start(bf16[1,2,1,1,16,1152]{5,4,3,2,1,0:T(8,128)(2,1)S(1)} %fusion.7), channel_id=1, source_target_pairs={{0,2},{1,3},{2,0},{3,1},{4,6},{5,7},{6,4},{7,5},{8,10},{9,11},{10,... | collective-permute-start | bytes 221192 | tf_op jit(solution)/shard_map/ppermute | solution.py:348
  59.0 0.7 %collective-permute-done.23 = bf16[2,2,1,1,16,1152]{5,4,3,2,1,0:T(8,128)(2,1)S(1)} collective-permute-done((bf16[2,2,1,1,16,1152]{5,4,3,2,1,0:T(8,128)(2,1)S(1)}, bf16[2,2,1,1,16,1152]{5,4,3,2,1,0:T(8,128)(2,1)S(1)}, u32[]{:S(2)}, u32[]{:S(2)}) %collective-permute-start.23) | collective-permute-done | bytes 147488 | tf_op jit(solution)/shard_map/ppermute | solution.py:348
  59.7 1.0 %collective-permute-start.24 = (bf16[1,2,1,1,16,1152]{5,4,3,2,1,0:T(8,128)(2,1)S(1)}, bf16[1,2,1,1,16,1152]{5,4,3,2,1,0:T(8,128)(2,1)S(1)}, u32[]{:S(2)}, u32[]{:S(2)}) collective-permute-start(bf16[1,2,1,1,16,1152]{5,4,3,2,1,0:T(8,128)(2,1)S(1)} %fusion.5), channel_id=1, source_target_pairs={{0,16},{1,17},{2,18},{3,19},{4,20},{5,21},{6,22},{7,23},{8,24},{9,... | collective-permute-start | bytes 221192 | tf_op jit(solution)/shard_map/ppermute | solution.py:348
  60.7 0.8 %collective-permute-done.27 = bf16[1,2,1,2,16,1280]{5,4,3,2,1,0:T(8,128)(2,1)S(1)} collective-permute-done((bf16[1,2,1,2,16,1280]{5,4,3,2,1,0:T(8,128)(2,1)S(1)}, bf16[1,2,1,2,16,1280]{5,4,3,2,1,0:T(8,128)(2,1)S(1)}, u32[]{:S(2)}, u32[]{:S(2)}) %collective-permute-start.27) | collective-permute-done | bytes 163872 | tf_op jit(solution)/shard_map/ppermute | solution.py:348
  61.6 0.6 collective-permute-start.28
  62.2 2.1 %collective-permute-start.21 = (bf16[1,1,1,1,16,1152]{5,4,3,2,1,0:T(8,128)(2,1)S(1)}, bf16[1,1,1,1,16,1152]{5,4,3,2,1,0:T(8,128)(2,1)S(1)}, u32[]{:S(2)}, u32[]{:S(2)}) collective-permute-start(bf16[1,1,1,1,16,1152]{5,4,3,2,1,0:T(8,128)(2,1)S(1)} %fusion.22), channel_id=1, source_target_pairs={{0,4},{1,5},{2,6},{3,7},{4,0},{5,1},{6,2},{7,3},{8,12},{9,13},{10,... | collective-permute-start | bytes 110600 | tf_op jit(solution)/shard_map/ppermute | solution.py:348
  64.3 2.0 %collective-permute-start.25 = (bf16[1,1,1,1,16,1152]{5,4,3,2,1,0:T(8,128)(2,1)S(1)}, bf16[1,1,1,1,16,1152]{5,4,3,2,1,0:T(8,128)(2,1)S(1)}, u32[]{:S(2)}, u32[]{:S(2)}) collective-permute-start(bf16[1,1,1,1,16,1152]{5,4,3,2,1,0:T(8,128)(2,1)S(1)} %fusion.16), channel_id=1, source_target_pairs={{0,4},{1,5},{2,6},{3,7},{4,0},{5,1},{6,2},{7,3},{8,12},{9,13},{10,... | collective-permute-start | bytes 110600 | tf_op jit(solution)/shard_map/ppermute | solution.py:348
  66.3 1.9 %collective-permute-start.29 = (bf16[1,1,1,1,16,1280]{5,4,3,2,1,0:T(8,128)(2,1)S(1)}, bf16[1,1,1,1,16,1280]{5,4,3,2,1,0:T(8,128)(2,1)S(1)}, u32[]{:S(2)}, u32[]{:S(2)}) collective-permute-start(bf16[1,1,1,1,16,1280]{5,4,3,2,1,0:T(8,128)(2,1)S(1)} %fusion.10), channel_id=1, source_target_pairs={{0,4},{1,5},{2,6},{3,7},{4,0},{5,1},{6,2},{7,3},{8,12},{9,13},{10,... | collective-permute-start | bytes 122888 | tf_op jit(solution)/shard_map/ppermute | solution.py:348
  68.2 1.0 %collective-permute-done.25 = bf16[1,1,1,1,16,1152]{5,4,3,2,1,0:T(8,128)(2,1)S(1)} collective-permute-done((bf16[1,1,1,1,16,1152]{5,4,3,2,1,0:T(8,128)(2,1)S(1)}, bf16[1,1,1,1,16,1152]{5,4,3,2,1,0:T(8,128)(2,1)S(1)}, u32[]{:S(2)}, u32[]{:S(2)}) %collective-permute-start.25) | collective-permute-done | bytes 36896 | tf_op jit(solution)/shard_map/ppermute | solution.py:348
  69.3 2.0 %collective-permute-done.29 = bf16[1,1,1,1,16,1280]{5,4,3,2,1,0:T(8,128)(2,1)S(1)} collective-permute-done((bf16[1,1,1,1,16,1280]{5,4,3,2,1,0:T(8,128)(2,1)S(1)}, bf16[1,1,1,1,16,1280]{5,4,3,2,1,0:T(8,128)(2,1)S(1)}, u32[]{:S(2)}, u32[]{:S(2)}) %collective-permute-start.29) | collective-permute-done | bytes 40992 | tf_op jit(solution)/shard_map/ppermute | solution.py:348
  71.3 0.7 maximum_bitcast_fusion
  (35 shorter events, 0.5 us)
Async XLA Ops:
  0.7 13.2 %copy-start = (bf16[3584,512]{1,0:T(8,128)(2,1)S(1)}, bf16[3584,512]{1,0:T(8,128)(2,1)}, u32[]{:S(2)}) copy-start(bf16[3584,512]{1,0:T(8,128)(2,1)} %refs_1_) | copy-start | bytes 11010052
  2.0 14.0 %collective-permute-start = (bf16[3584,512]{1,0:T(8,128)(2,1)}, bf16[3584,512]{1,0:T(8,128)(2,1)S(1)}, u32[]{:S(2)}, u32[]{:S(2)}) collective-permute-start(bf16[3584,512]{1,0:T(8,128)(2,1)} %refs_1_), channel_id=1, source_target_pairs={{0,8},{1,9},{2,10},{3,11},{4,12},{5,13},{6,14},{7,15},{8,0},{9,1},... | collective-permute-start | bytes 11010056 | tf_op jit(solution)/shard_map/ppermute | solution.py:348
  2.5 8.3 %collective-permute-start.1 = (bf16[24,3584]{1,0:T(8,128)(2,1)S(1)}, bf16[24,3584]{1,0:T(8,128)(2,1)S(1)}, u32[]{:S(2)}, u32[]{:S(2)}) collective-permute-start(bf16[24,3584]{1,0:T(8,128)(2,1)S(1)} %constant_dynamic-slice_fusion.1), channel_id=1, source_target_pairs={{0,16},{1,17},{2,18},{3,19},{4,20},{5,21},{6,22},{7,23},{8,24},{9,... | collective-permute-start | bytes 516104 | tf_op jit(solution)/shard_map/ppermute | solution.py:348
  6.0 12.6 %collective-permute-start.6 = (bf16[32,3584]{1,0:T(8,128)(2,1)S(1)}, bf16[32,3584]{1,0:T(8,128)(2,1)S(1)}, u32[]{:S(2)}, u32[]{:S(2)}) collective-permute-start(bf16[32,3584]{1,0:T(8,128)(2,1)S(1)} %slice.173), channel_id=1, source_target_pairs={{0,16},{1,17},{2,18},{3,19},{4,20},{5,21},{6,22},{7,23},{8,24},{9,... | collective-permute-start | bytes 688136 | tf_op jit(solution)/shard_map/ppermute | solution.py:348
  7.6 3.1 %collective-permute-start.2 = (f32[8,128]{1,0:T(8,128)S(1)}, f32[8,128]{1,0:T(8,128)S(1)}, u32[]{:S(2)}, u32[]{:S(2)}) collective-permute-start(f32[8,128]{1,0:T(8,128)S(1)} %taught_stats.1.refs_11_), channel_id=1, source_target_pairs={{0,8},{1,9},{2,10},{3,11},{4,12},{5,13},{6,14},{7,15},{8,0},{9,1},... | collective-permute-start | bytes 12296 | tf_op jit(solution)/shard_map/ppermute | solution.py:348
  7.8 12.6 %copy-start.4 = (s32[128]{0:T(128)S(1)}, s32[128]{0:T(128)}, u32[]{:S(2)}) copy-start(s32[128]{0:T(128)} %param.6) | copy-start | bytes 1540
  8.8 9.8 %collective-permute-start.5 = (bf16[24,3584]{1,0:T(8,128)(2,1)S(1)}, bf16[24,3584]{1,0:T(8,128)(2,1)S(1)}, u32[]{:S(2)}, u32[]{:S(2)}) collective-permute-start(bf16[24,3584]{1,0:T(8,128)(2,1)S(1)} %constant_dynamic-slice_fusion), channel_id=1, source_target_pairs={{0,16},{1,17},{2,18},{3,19},{4,20},{5,21},{6,22},{7,23},{8,24},{9,... | collective-permute-start | bytes 516104 | tf_op jit(solution)/shard_map/ppermute | solution.py:348
  10.8 7.8 %collective-permute-start.4 = (bf16[24,3584]{1,0:T(8,128)(2,1)S(1)}, bf16[24,3584]{1,0:T(8,128)(2,1)S(1)}, u32[]{:S(2)}, u32[]{:S(2)}) collective-permute-start(bf16[24,3584]{1,0:T(8,128)(2,1)S(1)} %collective-permute-done.1.refs_0_.refs_1_), channel_id=1, source_target_pairs={{0,2},{1,3},{2,0},{3,1},{4,6},{5,7},{6,4},{7,5},{8,10},{9,11},{10,... | collective-permute-start | bytes 516104 | tf_op jit(solution)/shard_map/ppermute | solution.py:348
  12.4 6.3 %collective-permute-start.3 = (bf16[24,3584]{1,0:T(8,128)(2,1)S(1)}, bf16[24,3584]{1,0:T(8,128)(2,1)S(1)}, u32[]{:S(2)}, u32[]{:S(2)}) collective-permute-start(bf16[24,3584]{1,0:T(8,128)(2,1)S(1)} %collective-permute-done.1.refs_0_.refs_1_), channel_id=1, source_target_pairs={{0,1},{1,0},{2,3},{3,2},{4,5},{5,4},{6,7},{7,6},{8,9},{9,8},{10,11... | collective-permute-start | bytes 516104 | tf_op jit(solution)/shard_map/ppermute | solution.py:348
  13.9 1.2 %copy-start.1 = (bf16[128,3584]{1,0:T(8,128)(2,1)S(1)}, bf16[128,3584]{1,0:T(8,128)(2,1)}, u32[]{:S(2)}) copy-start(bf16[128,3584]{1,0:T(8,128)(2,1)} %refs_8_) | copy-start | bytes 2752516
  15.1 5.4 %copy-start.2 = (bf16[128,3584]{1,0:T(8,128)(2,1)S(1)}, bf16[128,3584]{1,0:T(8,128)(2,1)}, u32[]{:S(2)}) copy-start(bf16[128,3584]{1,0:T(8,128)(2,1)} %refs_8_) | copy-start | bytes 2752516
  18.6 12.3 %collective-permute-start.14 = (bf16[2,128,512]{2,1,0:T(8,128)(2,1)S(1)}, bf16[2,128,512]{2,1,0:T(8,128)(2,1)S(1)}, u32[]{:S(2)}, u32[]{:S(2)}) collective-permute-start(bf16[2,128,512]{2,1,0:T(8,128)(2,1)S(1)} %get-tuple-element.92.gone_ref), channel_id=1, source_target_pairs={{0,16},{1,17},{2,18},{3,19},{4,20},{5,21},{6,22},{7,23},{8,24},{9,... | collective-permute-start | bytes 786440 | tf_op jit(solution)/shard_map/ppermute | solution.py:348
  22.7 11.9 %copy-start.3 = (s32[512]{0:T(512)S(1)}, s32[512]{0:T(512)}, u32[]{:S(2)}) copy-start(s32[512]{0:T(512)} %param.7) | copy-start | bytes 6148
  22.7 5.5 %collective-permute-start.9 = (f32[2,8,128]{2,1,0:T(8,128)S(1)}, f32[2,8,128]{2,1,0:T(8,128)S(1)}, u32[]{:S(2)}, u32[]{:S(2)}) collective-permute-start(f32[2,8,128]{2,1,0:T(8,128)S(1)} %get-tuple-element.85.refs_0_), channel_id=1, source_target_pairs={{0,6},{1,7},{2,4},{3,5},{4,2},{5,3},{6,0},{7,1},{8,14},{9,15},{10,... | collective-permute-start | bytes 24584 | tf_op jit(solution)/shard_map/ppermute | solution.py:348
  26.3 4.5 %collective-permute-start.8 = (f32[2,8,128]{2,1,0:T(8,128)S(1)}, f32[2,8,128]{2,1,0:T(8,128)S(1)}, u32[]{:S(2)}, u32[]{:S(2)}) collective-permute-start(f32[2,8,128]{2,1,0:T(8,128)S(1)} %get-tuple-element.85.refs_0_), channel_id=1, source_target_pairs={{0,4},{1,5},{2,6},{3,7},{4,0},{5,1},{6,2},{7,3},{8,12},{9,13},{10,... | collective-permute-start | bytes 24584 | tf_op jit(solution)/shard_map/ppermute | solution.py:348
  26.3 4.5 %collective-permute-start.7 = (f32[2,8,128]{2,1,0:T(8,128)S(1)}, f32[2,8,128]{2,1,0:T(8,128)S(1)}, u32[]{:S(2)}, u32[]{:S(2)}) collective-permute-start(f32[2,8,128]{2,1,0:T(8,128)S(1)} %get-tuple-element.85.refs_0_), channel_id=1, source_target_pairs={{0,2},{1,3},{2,0},{3,1},{4,6},{5,7},{6,4},{7,5},{8,10},{9,11},{10,... | collective-permute-start | bytes 24584 | tf_op jit(solution)/shard_map/ppermute | solution.py:348
  27.1 7.4 %collective-permute-start.13 = (bf16[2,128,512]{2,1,0:T(8,128)(2,1)S(1)}, bf16[2,128,512]{2,1,0:T(8,128)(2,1)S(1)}, u32[]{:S(2)}, u32[]{:S(2)}) collective-permute-start(bf16[2,128,512]{2,1,0:T(8,128)(2,1)S(1)} %get-tuple-element.91.kept_ref.a0), channel_id=1, source_target_pairs={{0,8},{1,9},{2,10},{3,11},{4,12},{5,13},{6,14},{7,15},{8,0},{9,1},... | collective-permute-start | bytes 786440 | tf_op jit(solution)/shard_map/ppermute | solution.py:348
  30.9 3.6 %collective-permute-start.15 = (bf16[2,128,512]{2,1,0:T(8,128)(2,1)S(1)}, bf16[2,128,512]{2,1,0:T(8,128)(2,1)S(1)}, u32[]{:S(2)}, u32[]{:S(2)}) collective-permute-start(bf16[2,128,512]{2,1,0:T(8,128)(2,1)S(1)} %collective-permute-done.14.a2), channel_id=1, source_target_pairs={{0,8},{1,9},{2,10},{3,11},{4,12},{5,13},{6,14},{7,15},{8,0},{9,1},... | collective-permute-start | bytes 786440 | tf_op jit(solution)/shard_map/ppermute | solution.py:348
  31.0 5.0 %collective-permute-start.12 = (f32[2,8,128]{2,1,0:T(8,128)S(1)}, f32[2,8,128]{2,1,0:T(8,128)S(1)}, u32[]{:S(2)}, u32[]{:S(2)}) collective-permute-start(f32[2,8,128]{2,1,0:T(8,128)S(1)} %merge_stats.1.refs_3_), channel_id=1, source_target_pairs={{0,17},{1,16},{2,19},{3,18},{4,21},{5,20},{6,23},{7,22},{8,25},{9,... | collective-permute-start | bytes 24584 | tf_op jit(solution)/shard_map/ppermute | solution.py:348
  32.6 3.7 %collective-permute-start.11 = (f32[2,8,128]{2,1,0:T(8,128)S(1)}, f32[2,8,128]{2,1,0:T(8,128)S(1)}, u32[]{:S(2)}, u32[]{:S(2)}) collective-permute-start(f32[2,8,128]{2,1,0:T(8,128)S(1)} %merge_stats.1.refs_3_), channel_id=1, source_target_pairs={{0,1},{1,0},{2,3},{3,2},{4,5},{5,4},{6,7},{7,6},{8,9},{9,8},{10,11... | collective-permute-start | bytes 24584 | tf_op jit(solution)/shard_map/ppermute | solution.py:348
  33.1 3.7 %collective-permute-start.10 = (f32[2,8,128]{2,1,0:T(8,128)S(1)}, f32[2,8,128]{2,1,0:T(8,128)S(1)}, u32[]{:S(2)}, u32[]{:S(2)}) collective-permute-start(f32[2,8,128]{2,1,0:T(8,128)S(1)} %merge_stats.1.refs_3_), channel_id=1, source_target_pairs={{0,16},{1,17},{2,18},{3,19},{4,20},{5,21},{6,22},{7,23},{8,24},{9,... | collective-permute-start | bytes 24584 | tf_op jit(solution)/shard_map/ppermute | solution.py:348
  36.7 8.0 %collective-permute-start.16 = (bf16[2,128,3584]{2,1,0:T(8,128)(2,1)S(1)}, bf16[2,128,3584]{2,1,0:T(8,128)(2,1)S(1)}, u32[]{:S(2)}, u32[]{:S(2)}) collective-permute-start(bf16[2,128,3584]{2,1,0:T(8,128)(2,1)S(1)} %get-tuple-element.104.rows_ref), channel_id=1, source_target_pairs={{0,8},{1,9},{2,10},{3,11},{4,12},{5,13},{6,14},{7,15},{8,0},{9,1},... | collective-permute-start | bytes 5505032 | tf_op jit(solution)/shard_map/ppermute | solution.py:348
  41.1 3.6 %collective-permute-start.17 = (bf16[256,512]{1,0:T(8,128)(2,1)S(1)}, bf16[256,512]{1,0:T(8,128)(2,1)S(1)}, u32[]{:S(2)}, u32[]{:S(2)}) collective-permute-start(bf16[256,512]{1,0:T(8,128)(2,1)S(1)} %get-tuple-element.106), channel_id=1, source_target_pairs={{0,8},{1,9},{2,10},{3,11},{4,12},{5,13},{6,14},{7,15},{8,0},{9,1},... | collective-permute-start | bytes 786440 | tf_op jit(solution)/shard_map/ppermute | solution.py:348
  41.7 10.3 %collective-permute-start.26 = (bf16[128,1280]{1,0:T(8,128)(2,1)S(1)}, bf16[128,1280]{1,0:T(8,128)(2,1)S(1)}, u32[]{:S(2)}, u32[]{:S(2)}) collective-permute-start(bf16[128,1280]{1,0:T(8,128)(2,1)S(1)} %get-tuple-element.115), channel_id=1, source_target_pairs={{0,2},{1,3},{2,0},{3,1},{4,6},{5,7},{6,4},{7,5},{8,10},{9,11},{10,... | collective-permute-start | bytes 983048 | tf_op jit(solution)/shard_map/ppermute | solution.py:348
  41.7 9.1 %collective-permute-start.18 = (bf16[128,1152]{1,0:T(8,128)(2,1)S(1)}, bf16[128,1152]{1,0:T(8,128)(2,1)S(1)}, u32[]{:S(2)}, u32[]{:S(2)}) collective-permute-start(bf16[128,1152]{1,0:T(8,128)(2,1)S(1)} %get-tuple-element.107), channel_id=1, source_target_pairs={{0,16},{1,17},{2,18},{3,19},{4,20},{5,21},{6,22},{7,23},{8,24},{9,... | collective-permute-start | bytes 884744 | tf_op jit(solution)/shard_map/ppermute | solution.py:348
  43.2 8.8 %collective-permute-start.22 = (bf16[128,1152]{1,0:T(8,128)(2,1)S(1)}, bf16[128,1152]{1,0:T(8,128)(2,1)S(1)}, u32[]{:S(2)}, u32[]{:S(2)}) collective-permute-start(bf16[128,1152]{1,0:T(8,128)(2,1)S(1)} %get-tuple-element.111), channel_id=1, source_target_pairs={{0,1},{1,0},{2,3},{3,2},{4,5},{5,4},{6,7},{7,6},{8,9},{9,8},{10,11... | collective-permute-start | bytes 884744 | tf_op jit(solution)/shard_map/ppermute | solution.py:348
  52.0 5.2 %collective-permute-start.19 = (bf16[1,2,2,1,16,1152]{5,4,3,2,1,0:T(8,128)(2,1)S(1)}, bf16[1,2,2,1,16,1152]{5,4,3,2,1,0:T(8,128)(2,1)S(1)}, u32[]{:S(2)}, u32[]{:S(2)}) collective-permute-start(bf16[1,2,2,1,16,1152]{5,4,3,2,1,0:T(8,128)(2,1)S(1)} %fusion.1), channel_id=1, source_target_pairs={{0,1},{1,0},{2,3},{3,2},{4,5},{5,4},{6,7},{7,6},{8,9},{9,8},{10,11... | collective-permute-start | bytes 442376 | tf_op jit(solution)/shard_map/ppermute | solution.py:348
  53.7 6.0 %collective-permute-start.23 = (bf16[2,2,1,1,16,1152]{5,4,3,2,1,0:T(8,128)(2,1)S(1)}, bf16[2,2,1,1,16,1152]{5,4,3,2,1,0:T(8,128)(2,1)S(1)}, u32[]{:S(2)}, u32[]{:S(2)}) collective-permute-start(bf16[2,2,1,1,16,1152]{5,4,3,2,1,0:T(8,128)(2,1)S(1)} %fusion), channel_id=1, source_target_pairs={{0,2},{1,3},{2,0},{3,1},{4,6},{5,7},{6,4},{7,5},{8,10},{9,11},{10,... | collective-permute-start | bytes 442376 | tf_op jit(solution)/shard_map/ppermute | solution.py:348
  55.4 6.1 %collective-permute-start.27 = (bf16[1,2,1,2,16,1280]{5,4,3,2,1,0:T(8,128)(2,1)S(1)}, bf16[1,2,1,2,16,1280]{5,4,3,2,1,0:T(8,128)(2,1)S(1)}, u32[]{:S(2)}, u32[]{:S(2)}) collective-permute-start(bf16[1,2,1,2,16,1280]{5,4,3,2,1,0:T(8,128)(2,1)S(1)} %bitcast.59), channel_id=1, source_target_pairs={{0,16},{1,17},{2,18},{3,19},{4,20},{5,21},{6,22},{7,23},{8,24},{9,... | collective-permute-start | bytes 491528 | tf_op jit(solution)/shard_map/ppermute | solution.py:348
  57.3 4.9 %collective-permute-start.20 = (bf16[1,2,1,1,16,1152]{5,4,3,2,1,0:T(8,128)(2,1)S(1)}, bf16[1,2,1,1,16,1152]{5,4,3,2,1,0:T(8,128)(2,1)S(1)}, u32[]{:S(2)}, u32[]{:S(2)}) collective-permute-start(bf16[1,2,1,1,16,1152]{5,4,3,2,1,0:T(8,128)(2,1)S(1)} %fusion.7), channel_id=1, source_target_pairs={{0,2},{1,3},{2,0},{3,1},{4,6},{5,7},{6,4},{7,5},{8,10},{9,11},{10,... | collective-permute-start | bytes 221192 | tf_op jit(solution)/shard_map/ppermute | solution.py:348
  59.7 4.5 %collective-permute-start.24 = (bf16[1,2,1,1,16,1152]{5,4,3,2,1,0:T(8,128)(2,1)S(1)}, bf16[1,2,1,1,16,1152]{5,4,3,2,1,0:T(8,128)(2,1)S(1)}, u32[]{:S(2)}, u32[]{:S(2)}) collective-permute-start(bf16[1,2,1,1,16,1152]{5,4,3,2,1,0:T(8,128)(2,1)S(1)} %fusion.5), channel_id=1, source_target_pairs={{0,16},{1,17},{2,18},{3,19},{4,20},{5,21},{6,22},{7,23},{8,24},{9,... | collective-permute-start | bytes 221192 | tf_op jit(solution)/shard_map/ppermute | solution.py:348
  61.6 4.7 %collective-permute-start.28 = (bf16[1,2,1,1,16,1280]{5,4,3,2,1,0:T(8,128)(2,1)S(1)}, bf16[1,2,1,1,16,1280]{5,4,3,2,1,0:T(8,128)(2,1)S(1)}, u32[]{:S(2)}, u32[]{:S(2)}) collective-permute-start(bf16[1,2,1,1,16,1280]{5,4,3,2,1,0:T(8,128)(2,1)S(1)} %fusion.3), channel_id=1, source_target_pairs={{0,1},{1,0},{2,3},{3,2},{4,5},{5,4},{6,7},{7,6},{8,9},{9,8},{10,11... | collective-permute-start | bytes 245768 | tf_op jit(solution)/shard_map/ppermute | solution.py:348
  62.2 6.0 %collective-permute-start.21 = (bf16[1,1,1,1,16,1152]{5,4,3,2,1,0:T(8,128)(2,1)S(1)}, bf16[1,1,1,1,16,1152]{5,4,3,2,1,0:T(8,128)(2,1)S(1)}, u32[]{:S(2)}, u32[]{:S(2)}) collective-permute-start(bf16[1,1,1,1,16,1152]{5,4,3,2,1,0:T(8,128)(2,1)S(1)} %fusion.22), channel_id=1, source_target_pairs={{0,4},{1,5},{2,6},{3,7},{4,0},{5,1},{6,2},{7,3},{8,12},{9,13},{10,... | collective-permute-start | bytes 110600 | tf_op jit(solution)/shard_map/ppermute | solution.py:348
  64.3 4.9 %collective-permute-start.25 = (bf16[1,1,1,1,16,1152]{5,4,3,2,1,0:T(8,128)(2,1)S(1)}, bf16[1,1,1,1,16,1152]{5,4,3,2,1,0:T(8,128)(2,1)S(1)}, u32[]{:S(2)}, u32[]{:S(2)}) collective-permute-start(bf16[1,1,1,1,16,1152]{5,4,3,2,1,0:T(8,128)(2,1)S(1)} %fusion.16), channel_id=1, source_target_pairs={{0,4},{1,5},{2,6},{3,7},{4,0},{5,1},{6,2},{7,3},{8,12},{9,13},{10,... | collective-permute-start | bytes 110600 | tf_op jit(solution)/shard_map/ppermute | solution.py:348
  66.3 5.0 %collective-permute-start.29 = (bf16[1,1,1,1,16,1280]{5,4,3,2,1,0:T(8,128)(2,1)S(1)}, bf16[1,1,1,1,16,1280]{5,4,3,2,1,0:T(8,128)(2,1)S(1)}, u32[]{:S(2)}, u32[]{:S(2)}) collective-permute-start(bf16[1,1,1,1,16,1280]{5,4,3,2,1,0:T(8,128)(2,1)S(1)} %fusion.10), channel_id=1, source_target_pairs={{0,4},{1,5},{2,6},{3,7},{4,0},{5,1},{6,2},{7,3},{8,12},{9,13},{10,... | collective-permute-start | bytes 122888 | tf_op jit(solution)/shard_map/ppermute | solution.py:348

commit v19 on v16

--- a/solution.py
+++ b/solution.py
@@ -427,7 +427,8 @@
     ydim, wdim = bits, bits - 1
     third = depth // 128 // 3 * 128
     edges = (0, third, 2 * third, depth)
-    orders = [(0, ydim, wdim), (ydim, wdim, 0), (wdim, 0, ydim)]
+    rest = tuple(range(1, wdim))
+    orders = [(0, ydim, wdim) + rest, (ydim, wdim, 0) + rest, (wdim, 0) + rest + (ydim,)]
     low = owned.bit_length() - 1
     row_bit = {0: low + bits, ydim: low, wdim: low + 1}
     first_bits = tuple(row_bit[order[0]] for order in orders)
@@ -448,16 +449,9 @@
         return value.reshape(*dims, owned, value.shape[-1])
 
     terms = [[folded(keeps[p], p), folded(gots[p], p)] for p in range(3)]
-    for stage in (1, 2):
-        sents = [
-            sum(lax.index_in_dim(t, 1, orders[p][stage]).astype(F32) for t in terms[p]).astype(BF16)
-            for p in range(3)
-        ]
-        gots = [swap(sents[p], masks[orders[p][stage]]) for p in range(3)]
+    for stage in range(1, 1 + bits):
         for p in range(3):
-            terms[p] = [lax.index_in_dim(t, 0, orders[p][stage]) for t in terms[p]] + [gots[p]]
-    for dim in range(1, wdim):
-        for p in range(3):
+            dim = orders[p][stage]
             sent = sum(lax.index_in_dim(t, 1, dim).astype(F32) for t in terms[p]).astype(BF16)
             terms[p] = [lax.index_in_dim(t, 0, dim) for t in terms[p]] + [swap(sent, masks[dim])]
     total = jnp.concatenate([sum(t.astype(F32) for t in ts) for ts in terms], axis=-1)

time: 72.2 us -> 72.9 us (level)
  waiting for transfers between devices: 13.9 us -> 15.3 us
  starting transfers between devices: 35.2 us -> 34.4 us
    ppermute x30, waiting for transfers between devices: 13.9 us -> 15.3 us  [swap(): return lax.ppermute(value, AXES, [(i, i ^ mask) for i in range(count)])]
    ppermute x30, starting transfers between devices: 35.2 us -> 34.4 us  [swap(): return lax.ppermute(value, AXES, [(i, i ^ mask) for i in range(count)])]
  transfers between devices with their start and end apart: 30 -> 30, of which waited for: 13 -> 15; matrix products, arithmetic and copies ran while one was open for 5% -> 5% of each run, Pallas kernels for 15% -> 15%
where the time goes in v19:
time: 72.9 us; the launch traced here: 72.6 us
  starting transfers between devices  34.4 us (47%)
  Pallas kernels  15.4 us (21%)
  waiting for transfers between devices  15.3 us (21%)
  local copies, waits for them, and re-layouts  5.47 us (8%)
  other arithmetic  1.23 us (2%)
  between operations  0.82 us (1%)
    ppermute x30, starting transfers between devices, swap(): return lax.ppermute(value, AXES, [(i, i ^ mask) for i in range(count)])  34.4 us
    ppermute x30, waiting for transfers between devices, swap(): return lax.ppermute(value, AXES, [(i, i ^ mask) for i in range(count)])  15.3 us
    pallas_call x1, Pallas kernels, head_gradient(): pl.pallas_call(head_kernel, grid=(depth // tile,), out_shape=shape((depth...  5.21 us
    pallas_call x1, Pallas kernels, back_rows(): pl.pallas_call(lambda *refs: back_kernel(bits, edges, low, len(stats), *r...  4.43 us
    pallas_call x1, Pallas kernels, far_logits(): pl.pallas_call(lambda *refs: far_kernel(len(pieces), *refs), out_shape=(s...  2.19 us
    dynamic_slice x2, local copies, waits for them, and re-layouts, cut(): return lax.dynamic_slice(value, indices, sizes)  2.13 us
    pallas_call x2, Pallas kernels, near_logits(): pl.pallas_call(near_kernel, out_shape=(shape((per, cols), F32), shape((ST...  1.74 us
  transfers between devices with their start and end apart: 30, of which 15 were waited for; matrix products, arithmetic and copies ran while one was open for 5% of the time, Pallas kernels for 15%

profile of v19, /device:TPU:0, one launch (start us, length us, event | category | flops | bytes accessed | tf_op | source)
XLA Modules:
  0.0 72.6 jit_solution(2667128792517782923)
XLA Ops:
  0.7 0.0 copy-start
  0.7 0.1 pad_add_fusion.2.at_ref
  0.7 0.1 pad_add_fusion
  0.8 1.1 %constant_dynamic-slice_fusion.1 = bf16[24,3584]{1,0:T(8,128)(2,1)S(1)} fusion(bf16[128,3584]{1,0:T(8,128)(2,1)} %refs_8_, u32[]{:T(128)S(6)} %convert_element_type.149), kind=kLoop, calls=%fused_computation.42 | loop fusion | bytes 344068 | tf_op jit(solution)/shard_map/dynamic_slice | solution.py:375
  2.0 0.5 collective-permute-start
  2.5 2.6 %collective-permute-start.1 = (bf16[24,3584]{1,0:T(8,128)(2,1)S(1)}, bf16[24,3584]{1,0:T(8,128)(2,1)S(1)}, u32[]{:S(2)}, u32[]{:S(2)}) collective-permute-start(bf16[24,3584]{1,0:T(8,128)(2,1)S(1)} %constant_dynamic-slice_fusion.1), channel_id=1, source_target_pairs={{0,16},{1,17},{2,18},{3,19},{4,20},{5,21},{6,22},{7,23},{8,24},{9,... | collective-permute-start | bytes 516104 | tf_op jit(solution)/shard_map/ppermute | solution.py:348
  5.0 1.0 %slice.173 = bf16[32,3584]{1,0:T(8,128)(2,1)S(1)} slice(bf16[128,3584]{1,0:T(8,128)(2,1)} %refs_8_), slice={[96:128], [0:3584]} | slice | bytes 458752 | tf_op jit(solution)/shard_map/slice | solution.py:382
  6.0 0.1 collective-permute-start.6
  6.1 1.1 %copy.7 = bf16[128,4,512]{2,0,1:T(8,128)(2,1)S(1)} copy(bf16[128,4,512]{2,1,0:T(4,128)(2,1)} %param.9) | data formatting | bytes 1048576 | tf_op jit(solution)/shard_map/optimization_barrier | solution.py:351
  7.3 0.4 taught_stats.1.refs_11_
  7.6 0.2 collective-permute-start.2
  7.8 1.0 %constant_dynamic-slice_fusion = bf16[24,3584]{1,0:T(8,128)(2,1)S(1)} fusion(bf16[128,3584]{1,0:T(8,128)(2,1)} %refs_8_, u32[]{:T(128)S(6)} %convert_element_type.150), kind=kLoop, calls=%fused_computation.41 | loop fusion | bytes 344068 | tf_op jit(solution)/shard_map/dynamic_slice | solution.py:375
  8.8 1.9 %collective-permute-start.5 = (bf16[24,3584]{1,0:T(8,128)(2,1)S(1)}, bf16[24,3584]{1,0:T(8,128)(2,1)S(1)}, u32[]{:S(2)}, u32[]{:S(2)}) collective-permute-start(bf16[24,3584]{1,0:T(8,128)(2,1)S(1)} %constant_dynamic-slice_fusion), channel_id=1, source_target_pairs={{0,16},{1,17},{2,18},{3,19},{4,20},{5,21},{6,22},{7,23},{8,24},{9,... | collective-permute-start | bytes 516104 | tf_op jit(solution)/shard_map/ppermute | solution.py:348
  10.8 0.0 collective-permute-done.2.refs_12_
  10.8 1.6 %collective-permute-start.4 = (bf16[24,3584]{1,0:T(8,128)(2,1)S(1)}, bf16[24,3584]{1,0:T(8,128)(2,1)S(1)}, u32[]{:S(2)}, u32[]{:S(2)}) collective-permute-start(bf16[24,3584]{1,0:T(8,128)(2,1)S(1)} %collective-permute-done.1.refs_0_.refs_1_), channel_id=1, source_target_pairs={{0,2},{1,3},{2,0},{3,1},{4,6},{5,7},{6,4},{7,5},{8,10},{9,11},{10,... | collective-permute-start | bytes 516104 | tf_op jit(solution)/shard_map/ppermute | solution.py:348
  12.4 1.5 %collective-permute-start.3 = (bf16[24,3584]{1,0:T(8,128)(2,1)S(1)}, bf16[24,3584]{1,0:T(8,128)(2,1)S(1)}, u32[]{:S(2)}, u32[]{:S(2)}) collective-permute-start(bf16[24,3584]{1,0:T(8,128)(2,1)S(1)} %collective-permute-done.1.refs_0_.refs_1_), channel_id=1, source_target_pairs={{0,1},{1,0},{2,3},{3,2},{4,5},{5,4},{6,7},{7,6},{8,9},{9,8},{10,11... | collective-permute-start | bytes 516104 | tf_op jit(solution)/shard_map/ppermute | solution.py:348
  13.9 1.2 %copy-done.1 = bf16[128,3584]{1,0:T(8,128)(2,1)S(1)} copy-done((bf16[128,3584]{1,0:T(8,128)(2,1)S(1)}, bf16[128,3584]{1,0:T(8,128)(2,1)}, u32[]{:S(2)}) %copy-start.1) | copy-done | bytes 917528
  15.1 0.9 %near_logits.2 = (f32[128,512]{1,0:T(8,128)S(1)}, f32[8,128]{1,0:T(8,128)S(1)}) custom-call(bf16[128,3584]{1,0:T(8,128)(2,1)S(1)} %copy-done.1, bf16[3584,512]{1,0:T(8,128)(2,1)S(1)} %copy-done, bf16[24,3584]{1,0:T(8,128)(2,1)S(1)} %collective-permute-done.1.refs_0_.refs_1_), custom_call_target="tpu_custom_call" | custom-call | flops 469762048 | bytes 4587520 | tf_op jit(solution)/shard_map/near_logits/pallas_call | solution.py:109
  15.9 0.0 collective-permute-done.w_ref.refs_7_.refs_2_
  15.9 0.9 %near_logits.3 = (f32[128,512]{1,0:T(8,128)S(1)}, f32[8,128]{1,0:T(8,128)S(1)}) custom-call(bf16[128,3584]{1,0:T(8,128)(2,1)S(1)} %copy-done.1, bf16[3584,512]{1,0:T(8,128)(2,1)S(1)} %collective-permute-done.w_ref.refs_7_.refs_2_, bf16[24,3584]{1,0:T(8,128)(2,1)S(1)} %collective-permute-done.1.refs_0_.refs_1_), custom_call_target="tpu_custom_call" | custom-call | flops 469762048 | bytes 4587520 | tf_op jit(solution)/shard_map/near_logits/pallas_call | solution.py:109
  16.8 1.8 %collective-permute-done.5.refs_4_ = bf16[24,3584]{1,0:T(8,128)(2,1)S(1)} collective-permute-done((bf16[24,3584]{1,0:T(8,128)(2,1)S(1)}, bf16[24,3584]{1,0:T(8,128)(2,1)S(1)}, u32[]{:S(2)}, u32[]{:S(2)}) %collective-permute-start.5) | collective-permute-done | bytes 172064 | tf_op jit(solution)/shard_map/ppermute | solution.py:348
  18.6 1.8 %collective-permute-start.14 = (bf16[2,128,512]{2,1,0:T(8,128)(2,1)S(1)}, bf16[2,128,512]{2,1,0:T(8,128)(2,1)S(1)}, u32[]{:S(2)}, u32[]{:S(2)}) collective-permute-start(bf16[2,128,512]{2,1,0:T(8,128)(2,1)S(1)} %get-tuple-element.88.gone_ref), channel_id=1, source_target_pairs={{0,16},{1,17},{2,18},{3,19},{4,20},{5,21},{6,22},{7,23},{8,24},{9,... | collective-permute-start | bytes 786440 | tf_op jit(solution)/shard_map/ppermute | solution.py:348
  20.5 2.2 %far_logits.1 = (f32[128,512]{1,0:T(8,128)S(1)}, f32[128,512]{1,0:T(8,128)S(1)}, bf16[2,128,3584]{2,1,0:T(8,128)(2,1)S(1)}, f32[2,8,128]{2,1,0:T(8,128)S(1)}, f32[8,128]{1,0:T(8,128)S(1)}) custom-call(s32[4]{0:T(128)S(1)} %get-tuple-element.60.refs_0_, bf16[24,3584]{1,0:T(8,128)(2,1)S(1)} %collective-permute-done.1.refs_0_.refs_1_, ...), custom_call_target="tpu_custom_call" | custom-call | flops 939524096 | bytes 8257536 | tf_op jit(solution)/shard_map/far_logits/pallas_call | solution.py:161
  22.7 0.0 copy-start.3
  22.7 3.6 %collective-permute-start.9 = (f32[2,8,128]{2,1,0:T(8,128)S(1)}, f32[2,8,128]{2,1,0:T(8,128)S(1)}, u32[]{:S(2)}, u32[]{:S(2)}) collective-permute-start(f32[2,8,128]{2,1,0:T(8,128)S(1)} %get-tuple-element.80.refs_0_), channel_id=1, source_target_pairs={{0,6},{1,7},{2,4},{3,5},{4,2},{5,3},{6,0},{7,1},{8,14},{9,15},{10,... | collective-permute-start | bytes 24584 | tf_op jit(solution)/shard_map/ppermute | solution.py:348
  26.3 0.0 collective-permute-start.8
  26.3 0.8 %collective-permute-start.7 = (f32[2,8,128]{2,1,0:T(8,128)S(1)}, f32[2,8,128]{2,1,0:T(8,128)S(1)}, u32[]{:S(2)}, u32[]{:S(2)}) collective-permute-start(f32[2,8,128]{2,1,0:T(8,128)S(1)} %get-tuple-element.80.refs_0_), channel_id=1, source_target_pairs={{0,2},{1,3},{2,0},{3,1},{4,6},{5,7},{6,4},{7,5},{8,10},{9,11},{10,... | collective-permute-start | bytes 24584 | tf_op jit(solution)/shard_map/ppermute | solution.py:348
  27.1 1.1 %collective-permute-done.9.refs_3_ = f32[2,8,128]{2,1,0:T(8,128)S(1)} collective-permute-done((f32[2,8,128]{2,1,0:T(8,128)S(1)}, f32[2,8,128]{2,1,0:T(8,128)S(1)}, u32[]{:S(2)}, u32[]{:S(2)}) %collective-permute-start.9) | collective-permute-done | bytes 8224 | tf_op jit(solution)/shard_map/ppermute | solution.py:348
  28.2 2.7 %collective-permute-done.8.refs_2_ = f32[2,8,128]{2,1,0:T(8,128)S(1)} collective-permute-done((f32[2,8,128]{2,1,0:T(8,128)S(1)}, f32[2,8,128]{2,1,0:T(8,128)S(1)}, u32[]{:S(2)}, u32[]{:S(2)}) %collective-permute-start.8) | collective-permute-done | bytes 8224 | tf_op jit(solution)/shard_map/ppermute | solution.py:348
  30.9 0.1 collective-permute-start.15
  31.0 1.6 %collective-permute-start.12 = (f32[2,8,128]{2,1,0:T(8,128)S(1)}, f32[2,8,128]{2,1,0:T(8,128)S(1)}, u32[]{:S(2)}, u32[]{:S(2)}) collective-permute-start(f32[2,8,128]{2,1,0:T(8,128)S(1)} %merge_stats.1.refs_3_), channel_id=1, source_target_pairs={{0,17},{1,16},{2,19},{3,18},{4,21},{5,20},{6,23},{7,22},{8,25},{9,... | collective-permute-start | bytes 24584 | tf_op jit(solution)/shard_map/ppermute | solution.py:348
  32.6 0.5 collective-permute-start.11
  33.1 1.5 %collective-permute-start.10 = (f32[2,8,128]{2,1,0:T(8,128)S(1)}, f32[2,8,128]{2,1,0:T(8,128)S(1)}, u32[]{:S(2)}, u32[]{:S(2)}) collective-permute-start(f32[2,8,128]{2,1,0:T(8,128)S(1)} %merge_stats.1.refs_3_), channel_id=1, source_target_pairs={{0,16},{1,17},{2,18},{3,19},{4,20},{5,21},{6,22},{7,23},{8,24},{9,... | collective-permute-start | bytes 24584 | tf_op jit(solution)/shard_map/ppermute | solution.py:348
  34.6 1.4 %teacher_rows.1 = (f32[2,128,1024]{2,1,0:T(8,128)S(1)}, f32[2,8,128]{2,1,0:T(8,128)S(1)}) custom-call(s32[2]{0:T(128)S(1)} %pad_add_fusion.2.at_ref, s32[4,1,128]{2,1,0:T(1,128)S(1)} %bitcast.42, bf16[2,128,512]{2,1,0:T(8,128)(2,1)S(1)} %get-tuple-element.87.kept_ref.a0, bf16[2,128,512]{2,1,0:T(8,128)(2,1)S(1)} %collective-permute-done.13.a1, ...), custom_call_target="tpu_custom_call" | custom-call | flops 268435456 | bytes 1572864 | tf_op jit(solution)/shard_map/teacher_rows/pallas_call | solution.py:82
  36.0 0.0 collective-permute-done.12.refs_6_
  36.0 0.2 collective-permute-done.11.refs_5_
  36.2 0.5 collective-permute-done.10.refs_4_
  36.7 4.4 %back_rows.1 = (bf16[256,512]{1,0:T(8,128)(2,1)S(1)}, bf16[256,512]{1,0:T(8,128)(2,1)S(1)}, bf16[128,1152]{1,0:T(8,128)(2,1)S(1)}, bf16[128,1152]{1,0:T(8,128)(2...) custom-call(s32[4]{0:T(128)S(1)} %get-tuple-element.55.refs_0_, ...), custom_call_target="tpu_custom_call" | custom-call | flops 1879048192 | bytes 7340032 | tf_op jit(solution)/shard_map/back_rows/pallas_call | solution.py:294
  41.1 0.1 collective-permute-start.16
  41.2 0.5 collective-permute-start.17
  41.7 1.5 %collective-permute-start.18 = (bf16[128,1152]{1,0:T(8,128)(2,1)S(1)}, bf16[128,1152]{1,0:T(8,128)(2,1)S(1)}, u32[]{:S(2)}, u32[]{:S(2)}) collective-permute-start(bf16[128,1152]{1,0:T(8,128)(2,1)S(1)} %get-tuple-element.97), channel_id=1, source_target_pairs={{0,16},{1,17},{2,18},{3,19},{4,20},{5,21},{6,22},{7,23},{8,24},{9,... | collective-permute-start | bytes 884744 | tf_op jit(solution)/shard_map/ppermute | solution.py:348
  43.2 1.5 %collective-permute-start.22 = (bf16[128,1152]{1,0:T(8,128)(2,1)S(1)}, bf16[128,1152]{1,0:T(8,128)(2,1)S(1)}, u32[]{:S(2)}, u32[]{:S(2)}) collective-permute-start(bf16[128,1152]{1,0:T(8,128)(2,1)S(1)} %get-tuple-element.101), channel_id=1, source_target_pairs={{0,1},{1,0},{2,3},{3,2},{4,5},{5,4},{6,7},{7,6},{8,9},{9,8},{10,11... | collective-permute-start | bytes 884744 | tf_op jit(solution)/shard_map/ppermute | solution.py:348
  44.7 0.6 collective-permute-done.17.theirs_ref
  45.4 5.2 %head_gradient.1 = bf16[3584,512]{1,0:T(8,128)(2,1)} custom-call(bf16[2,128,3584]{2,1,0:T(8,128)(2,1)S(1)} %get-tuple-element.95.rows_ref, bf16[2,128,3584]{2,1,0:T(8,128)(2,1)S(1)} %collective-permute-done.16.core_ref, bf16[256,512]{1,0:T(8,128)(2,1)S(1)} %get-tuple-element.96.mine_ref, bf16[256,512]{1,0:T(8,128)(2,1)S(1)} %collective-permute-done.17.theirs_ref), custom_call_target="tpu_custom_call" | custom-call | flops 1879048192 | bytes 7340032 | tf_op jit(solution)/shard_map/head_gradient/pallas_call | solution.py:323
  50.6 0.1 collective-permute-done.18
  50.7 1.2 %collective-permute-done.22 = bf16[128,1152]{1,0:T(8,128)(2,1)S(1)} collective-permute-done((bf16[128,1152]{1,0:T(8,128)(2,1)S(1)}, bf16[128,1152]{1,0:T(8,128)(2,1)S(1)}, u32[]{:S(2)}, u32[]{:S(2)}) %collective-permute-start.22) | collective-permute-done | bytes 294944 | tf_op jit(solution)/shard_map/ppermute | solution.py:348
  52.0 1.6 %collective-permute-start.19 = (bf16[1,2,2,1,16,1152]{5,4,3,2,1,0:T(8,128)(2,1)S(1)}, bf16[1,2,2,1,16,1152]{5,4,3,2,1,0:T(8,128)(2,1)S(1)}, u32[]{:S(2)}, u32[]{:S(2)}) collective-permute-start(bf16[1,2,2,1,16,1152]{5,4,3,2,1,0:T(8,128)(2,1)S(1)} %fusion.1), channel_id=1, source_target_pairs={{0,1},{1,0},{2,3},{3,2},{4,5},{5,4},{6,7},{7,6},{8,9},{9,8},{10,11... | collective-permute-start | bytes 442376 | tf_op jit(solution)/shard_map/ppermute | solution.py:348
  53.5 0.1 add_convert_fusion
  53.7 1.8 %collective-permute-start.23 = (bf16[2,2,1,1,16,1152]{5,4,3,2,1,0:T(8,128)(2,1)S(1)}, bf16[2,2,1,1,16,1152]{5,4,3,2,1,0:T(8,128)(2,1)S(1)}, u32[]{:S(2)}, u32[]{:S(2)}) collective-permute-start(bf16[2,2,1,1,16,1152]{5,4,3,2,1,0:T(8,128)(2,1)S(1)} %fusion), channel_id=1, source_target_pairs={{0,2},{1,3},{2,0},{3,1},{4,6},{5,7},{6,4},{7,5},{8,10},{9,11},{10,... | collective-permute-start | bytes 442376 | tf_op jit(solution)/shard_map/ppermute | solution.py:348
  55.5 0.5 collective-permute-start.27
  56.0 1.2 %collective-permute-done.19 = bf16[1,2,2,1,16,1152]{5,4,3,2,1,0:T(8,128)(2,1)S(1)} collective-permute-done((bf16[1,2,2,1,16,1152]{5,4,3,2,1,0:T(8,128)(2,1)S(1)}, bf16[1,2,2,1,16,1152]{5,4,3,2,1,0:T(8,128)(2,1)S(1)}, u32[]{:S(2)}, u32[]{:S(2)}) %collective-permute-start.19) | collective-permute-done | bytes 147488 | tf_op jit(solution)/shard_map/ppermute | solution.py:348
  57.2 1.8 %collective-permute-start.20 = (bf16[1,2,1,1,16,1152]{5,4,3,2,1,0:T(8,128)(2,1)S(1)}, bf16[1,2,1,1,16,1152]{5,4,3,2,1,0:T(8,128)(2,1)S(1)}, u32[]{:S(2)}, u32[]{:S(2)}) collective-permute-start(bf16[1,2,1,1,16,1152]{5,4,3,2,1,0:T(8,128)(2,1)S(1)} %fusion.7), channel_id=1, source_target_pairs={{0,2},{1,3},{2,0},{3,1},{4,6},{5,7},{6,4},{7,5},{8,10},{9,11},{10,... | collective-permute-start | bytes 221192 | tf_op jit(solution)/shard_map/ppermute | solution.py:348
  59.0 0.6 collective-permute-done.23
  59.7 1.0 %collective-permute-start.24 = (bf16[1,2,1,1,16,1152]{5,4,3,2,1,0:T(8,128)(2,1)S(1)}, bf16[1,2,1,1,16,1152]{5,4,3,2,1,0:T(8,128)(2,1)S(1)}, u32[]{:S(2)}, u32[]{:S(2)}) collective-permute-start(bf16[1,2,1,1,16,1152]{5,4,3,2,1,0:T(8,128)(2,1)S(1)} %fusion.5), channel_id=1, source_target_pairs={{0,16},{1,17},{2,18},{3,19},{4,20},{5,21},{6,22},{7,23},{8,24},{9,... | collective-permute-start | bytes 221192 | tf_op jit(solution)/shard_map/ppermute | solution.py:348
  60.7 0.8 %collective-permute-done.27 = bf16[1,2,1,2,16,1280]{5,4,3,2,1,0:T(8,128)(2,1)S(1)} collective-permute-done((bf16[1,2,1,2,16,1280]{5,4,3,2,1,0:T(8,128)(2,1)S(1)}, bf16[1,2,1,2,16,1280]{5,4,3,2,1,0:T(8,128)(2,1)S(1)}, u32[]{:S(2)}, u32[]{:S(2)}) %collective-permute-start.27) | collective-permute-done | bytes 163872 | tf_op jit(solution)/shard_map/ppermute | solution.py:348
  61.6 2.1 %collective-permute-start.28 = (bf16[1,1,1,2,16,1280]{5,4,3,2,1,0:T(8,128)(2,1)S(1)}, bf16[1,1,1,2,16,1280]{5,4,3,2,1,0:T(8,128)(2,1)S(1)}, u32[]{:S(2)}, u32[]{:S(2)}) collective-permute-start(bf16[1,1,1,2,16,1280]{5,4,3,2,1,0:T(8,128)(2,1)S(1)} %fusion.3), channel_id=1, source_target_pairs={{0,4},{1,5},{2,6},{3,7},{4,0},{5,1},{6,2},{7,3},{8,12},{9,13},{10,... | collective-permute-start | bytes 245768 | tf_op jit(solution)/shard_map/ppermute | solution.py:348
  63.7 1.0 %collective-permute-start.21 = (bf16[1,1,1,1,16,1152]{5,4,3,2,1,0:T(8,128)(2,1)S(1)}, bf16[1,1,1,1,16,1152]{5,4,3,2,1,0:T(8,128)(2,1)S(1)}, u32[]{:S(2)}, u32[]{:S(2)}) collective-permute-start(bf16[1,1,1,1,16,1152]{5,4,3,2,1,0:T(8,128)(2,1)S(1)} %fusion.22), channel_id=1, source_target_pairs={{0,4},{1,5},{2,6},{3,7},{4,0},{5,1},{6,2},{7,3},{8,12},{9,13},{10,... | collective-permute-start | bytes 110600 | tf_op jit(solution)/shard_map/ppermute | solution.py:348
  64.7 2.1 %collective-permute-start.25 = (bf16[1,1,1,1,16,1152]{5,4,3,2,1,0:T(8,128)(2,1)S(1)}, bf16[1,1,1,1,16,1152]{5,4,3,2,1,0:T(8,128)(2,1)S(1)}, u32[]{:S(2)}, u32[]{:S(2)}) collective-permute-start(bf16[1,1,1,1,16,1152]{5,4,3,2,1,0:T(8,128)(2,1)S(1)} %fusion.16), channel_id=1, source_target_pairs={{0,4},{1,5},{2,6},{3,7},{4,0},{5,1},{6,2},{7,3},{8,12},{9,13},{10,... | collective-permute-start | bytes 110600 | tf_op jit(solution)/shard_map/ppermute | solution.py:348
  66.8 1.0 %collective-permute-done.28 = bf16[1,1,1,2,16,1280]{5,4,3,2,1,0:T(8,128)(2,1)S(1)} collective-permute-done((bf16[1,1,1,2,16,1280]{5,4,3,2,1,0:T(8,128)(2,1)S(1)}, bf16[1,1,1,2,16,1280]{5,4,3,2,1,0:T(8,128)(2,1)S(1)}, u32[]{:S(2)}, u32[]{:S(2)}) %collective-permute-start.28) | collective-permute-done | bytes 81952 | tf_op jit(solution)/shard_map/ppermute | solution.py:348
  67.8 0.6 collective-permute-start.29
  68.5 0.5 collective-permute-done.21
  69.0 0.7 collective-permute-done.25
  69.7 2.2 %collective-permute-done.29 = bf16[1,1,1,1,16,1280]{5,4,3,2,1,0:T(8,128)(2,1)S(1)} collective-permute-done((bf16[1,1,1,1,16,1280]{5,4,3,2,1,0:T(8,128)(2,1)S(1)}, bf16[1,1,1,1,16,1280]{5,4,3,2,1,0:T(8,128)(2,1)S(1)}, u32[]{:S(2)}, u32[]{:S(2)}) %collective-permute-start.29) | collective-permute-done | bytes 40992 | tf_op jit(solution)/shard_map/ppermute | solution.py:348
  71.9 0.7 maximum_bitcast_fusion
  (35 shorter events, 0.5 us)
Async XLA Ops:
  0.7 13.2 %copy-start = (bf16[3584,512]{1,0:T(8,128)(2,1)S(1)}, bf16[3584,512]{1,0:T(8,128)(2,1)}, u32[]{:S(2)}) copy-start(bf16[3584,512]{1,0:T(8,128)(2,1)} %refs_1_) | copy-start | bytes 11010052
  2.0 14.0 %collective-permute-start = (bf16[3584,512]{1,0:T(8,128)(2,1)}, bf16[3584,512]{1,0:T(8,128)(2,1)S(1)}, u32[]{:S(2)}, u32[]{:S(2)}) collective-permute-start(bf16[3584,512]{1,0:T(8,128)(2,1)} %refs_1_), channel_id=1, source_target_pairs={{0,8},{1,9},{2,10},{3,11},{4,12},{5,13},{6,14},{7,15},{8,0},{9,1},... | collective-permute-start | bytes 11010056 | tf_op jit(solution)/shard_map/ppermute | solution.py:348
  2.5 8.3 %collective-permute-start.1 = (bf16[24,3584]{1,0:T(8,128)(2,1)S(1)}, bf16[24,3584]{1,0:T(8,128)(2,1)S(1)}, u32[]{:S(2)}, u32[]{:S(2)}) collective-permute-start(bf16[24,3584]{1,0:T(8,128)(2,1)S(1)} %constant_dynamic-slice_fusion.1), channel_id=1, source_target_pairs={{0,16},{1,17},{2,18},{3,19},{4,20},{5,21},{6,22},{7,23},{8,24},{9,... | collective-permute-start | bytes 516104 | tf_op jit(solution)/shard_map/ppermute | solution.py:348
  6.0 12.6 %collective-permute-start.6 = (bf16[32,3584]{1,0:T(8,128)(2,1)S(1)}, bf16[32,3584]{1,0:T(8,128)(2,1)S(1)}, u32[]{:S(2)}, u32[]{:S(2)}) collective-permute-start(bf16[32,3584]{1,0:T(8,128)(2,1)S(1)} %slice.173), channel_id=1, source_target_pairs={{0,16},{1,17},{2,18},{3,19},{4,20},{5,21},{6,22},{7,23},{8,24},{9,... | collective-permute-start | bytes 688136 | tf_op jit(solution)/shard_map/ppermute | solution.py:348
  7.6 3.1 %collective-permute-start.2 = (f32[8,128]{1,0:T(8,128)S(1)}, f32[8,128]{1,0:T(8,128)S(1)}, u32[]{:S(2)}, u32[]{:S(2)}) collective-permute-start(f32[8,128]{1,0:T(8,128)S(1)} %taught_stats.1.refs_11_), channel_id=1, source_target_pairs={{0,8},{1,9},{2,10},{3,11},{4,12},{5,13},{6,14},{7,15},{8,0},{9,1},... | collective-permute-start | bytes 12296 | tf_op jit(solution)/shard_map/ppermute | solution.py:348
  7.8 12.6 %copy-start.4 = (s32[128]{0:T(128)S(1)}, s32[128]{0:T(128)}, u32[]{:S(2)}) copy-start(s32[128]{0:T(128)} %param.6) | copy-start | bytes 1540
  8.8 9.8 %collective-permute-start.5 = (bf16[24,3584]{1,0:T(8,128)(2,1)S(1)}, bf16[24,3584]{1,0:T(8,128)(2,1)S(1)}, u32[]{:S(2)}, u32[]{:S(2)}) collective-permute-start(bf16[24,3584]{1,0:T(8,128)(2,1)S(1)} %constant_dynamic-slice_fusion), channel_id=1, source_target_pairs={{0,16},{1,17},{2,18},{3,19},{4,20},{5,21},{6,22},{7,23},{8,24},{9,... | collective-permute-start | bytes 516104 | tf_op jit(solution)/shard_map/ppermute | solution.py:348
  10.8 7.8 %collective-permute-start.4 = (bf16[24,3584]{1,0:T(8,128)(2,1)S(1)}, bf16[24,3584]{1,0:T(8,128)(2,1)S(1)}, u32[]{:S(2)}, u32[]{:S(2)}) collective-permute-start(bf16[24,3584]{1,0:T(8,128)(2,1)S(1)} %collective-permute-done.1.refs_0_.refs_1_), channel_id=1, source_target_pairs={{0,2},{1,3},{2,0},{3,1},{4,6},{5,7},{6,4},{7,5},{8,10},{9,11},{10,... | collective-permute-start | bytes 516104 | tf_op jit(solution)/shard_map/ppermute | solution.py:348
  12.4 6.3 %collective-permute-start.3 = (bf16[24,3584]{1,0:T(8,128)(2,1)S(1)}, bf16[24,3584]{1,0:T(8,128)(2,1)S(1)}, u32[]{:S(2)}, u32[]{:S(2)}) collective-permute-start(bf16[24,3584]{1,0:T(8,128)(2,1)S(1)} %collective-permute-done.1.refs_0_.refs_1_), channel_id=1, source_target_pairs={{0,1},{1,0},{2,3},{3,2},{4,5},{5,4},{6,7},{7,6},{8,9},{9,8},{10,11... | collective-permute-start | bytes 516104 | tf_op jit(solution)/shard_map/ppermute | solution.py:348
  13.9 1.2 %copy-start.1 = (bf16[128,3584]{1,0:T(8,128)(2,1)S(1)}, bf16[128,3584]{1,0:T(8,128)(2,1)}, u32[]{:S(2)}) copy-start(bf16[128,3584]{1,0:T(8,128)(2,1)} %refs_8_) | copy-start | bytes 2752516
  15.1 5.4 %copy-start.2 = (bf16[128,3584]{1,0:T(8,128)(2,1)S(1)}, bf16[128,3584]{1,0:T(8,128)(2,1)}, u32[]{:S(2)}) copy-start(bf16[128,3584]{1,0:T(8,128)(2,1)} %refs_8_) | copy-start | bytes 2752516
  18.6 12.3 %collective-permute-start.14 = (bf16[2,128,512]{2,1,0:T(8,128)(2,1)S(1)}, bf16[2,128,512]{2,1,0:T(8,128)(2,1)S(1)}, u32[]{:S(2)}, u32[]{:S(2)}) collective-permute-start(bf16[2,128,512]{2,1,0:T(8,128)(2,1)S(1)} %get-tuple-element.88.gone_ref), channel_id=1, source_target_pairs={{0,16},{1,17},{2,18},{3,19},{4,20},{5,21},{6,22},{7,23},{8,24},{9,... | collective-permute-start | bytes 786440 | tf_op jit(solution)/shard_map/ppermute | solution.py:348
  22.7 11.9 %copy-start.3 = (s32[512]{0:T(512)S(1)}, s32[512]{0:T(512)}, u32[]{:S(2)}) copy-start(s32[512]{0:T(512)} %param.7) | copy-start | bytes 6148
  22.7 5.5 %collective-permute-start.9 = (f32[2,8,128]{2,1,0:T(8,128)S(1)}, f32[2,8,128]{2,1,0:T(8,128)S(1)}, u32[]{:S(2)}, u32[]{:S(2)}) collective-permute-start(f32[2,8,128]{2,1,0:T(8,128)S(1)} %get-tuple-element.80.refs_0_), channel_id=1, source_target_pairs={{0,6},{1,7},{2,4},{3,5},{4,2},{5,3},{6,0},{7,1},{8,14},{9,15},{10,... | collective-permute-start | bytes 24584 | tf_op jit(solution)/shard_map/ppermute | solution.py:348
  26.3 4.5 %collective-permute-start.8 = (f32[2,8,128]{2,1,0:T(8,128)S(1)}, f32[2,8,128]{2,1,0:T(8,128)S(1)}, u32[]{:S(2)}, u32[]{:S(2)}) collective-permute-start(f32[2,8,128]{2,1,0:T(8,128)S(1)} %get-tuple-element.80.refs_0_), channel_id=1, source_target_pairs={{0,4},{1,5},{2,6},{3,7},{4,0},{5,1},{6,2},{7,3},{8,12},{9,13},{10,... | collective-permute-start | bytes 24584 | tf_op jit(solution)/shard_map/ppermute | solution.py:348
  26.3 4.5 %collective-permute-start.7 = (f32[2,8,128]{2,1,0:T(8,128)S(1)}, f32[2,8,128]{2,1,0:T(8,128)S(1)}, u32[]{:S(2)}, u32[]{:S(2)}) collective-permute-start(f32[2,8,128]{2,1,0:T(8,128)S(1)} %get-tuple-element.80.refs_0_), channel_id=1, source_target_pairs={{0,2},{1,3},{2,0},{3,1},{4,6},{5,7},{6,4},{7,5},{8,10},{9,11},{10,... | collective-permute-start | bytes 24584 | tf_op jit(solution)/shard_map/ppermute | solution.py:348
  27.1 7.4 %collective-permute-start.13 = (bf16[2,128,512]{2,1,0:T(8,128)(2,1)S(1)}, bf16[2,128,512]{2,1,0:T(8,128)(2,1)S(1)}, u32[]{:S(2)}, u32[]{:S(2)}) collective-permute-start(bf16[2,128,512]{2,1,0:T(8,128)(2,1)S(1)} %get-tuple-element.87.kept_ref.a0), channel_id=1, source_target_pairs={{0,8},{1,9},{2,10},{3,11},{4,12},{5,13},{6,14},{7,15},{8,0},{9,1},... | collective-permute-start | bytes 786440 | tf_op jit(solution)/shard_map/ppermute | solution.py:348
  30.9 3.6 %collective-permute-start.15 = (bf16[2,128,512]{2,1,0:T(8,128)(2,1)S(1)}, bf16[2,128,512]{2,1,0:T(8,128)(2,1)S(1)}, u32[]{:S(2)}, u32[]{:S(2)}) collective-permute-start(bf16[2,128,512]{2,1,0:T(8,128)(2,1)S(1)} %collective-permute-done.14.a2), channel_id=1, source_target_pairs={{0,8},{1,9},{2,10},{3,11},{4,12},{5,13},{6,14},{7,15},{8,0},{9,1},... | collective-permute-start | bytes 786440 | tf_op jit(solution)/shard_map/ppermute | solution.py:348
  31.0 5.0 %collective-permute-start.12 = (f32[2,8,128]{2,1,0:T(8,128)S(1)}, f32[2,8,128]{2,1,0:T(8,128)S(1)}, u32[]{:S(2)}, u32[]{:S(2)}) collective-permute-start(f32[2,8,128]{2,1,0:T(8,128)S(1)} %merge_stats.1.refs_3_), channel_id=1, source_target_pairs={{0,17},{1,16},{2,19},{3,18},{4,21},{5,20},{6,23},{7,22},{8,25},{9,... | collective-permute-start | bytes 24584 | tf_op jit(solution)/shard_map/ppermute | solution.py:348
  32.6 3.7 %collective-permute-start.11 = (f32[2,8,128]{2,1,0:T(8,128)S(1)}, f32[2,8,128]{2,1,0:T(8,128)S(1)}, u32[]{:S(2)}, u32[]{:S(2)}) collective-permute-start(f32[2,8,128]{2,1,0:T(8,128)S(1)} %merge_stats.1.refs_3_), channel_id=1, source_target_pairs={{0,1},{1,0},{2,3},{3,2},{4,5},{5,4},{6,7},{7,6},{8,9},{9,8},{10,11... | collective-permute-start | bytes 24584 | tf_op jit(solution)/shard_map/ppermute | solution.py:348
  33.1 3.7 %collective-permute-start.10 = (f32[2,8,128]{2,1,0:T(8,128)S(1)}, f32[2,8,128]{2,1,0:T(8,128)S(1)}, u32[]{:S(2)}, u32[]{:S(2)}) collective-permute-start(f32[2,8,128]{2,1,0:T(8,128)S(1)} %merge_stats.1.refs_3_), channel_id=1, source_target_pairs={{0,16},{1,17},{2,18},{3,19},{4,20},{5,21},{6,22},{7,23},{8,24},{9,... | collective-permute-start | bytes 24584 | tf_op jit(solution)/shard_map/ppermute | solution.py:348
  41.1 4.2 %collective-permute-start.16 = (bf16[2,128,3584]{2,1,0:T(8,128)(2,1)S(1)}, bf16[2,128,3584]{2,1,0:T(8,128)(2,1)S(1)}, u32[]{:S(2)}, u32[]{:S(2)}) collective-permute-start(bf16[2,128,3584]{2,1,0:T(8,128)(2,1)S(1)} %get-tuple-element.95.rows_ref), channel_id=1, source_target_pairs={{0,8},{1,9},{2,10},{3,11},{4,12},{5,13},{6,14},{7,15},{8,0},{9,1},... | collective-permute-start | bytes 5505032 | tf_op jit(solution)/shard_map/ppermute | solution.py:348
  41.2 4.1 %collective-permute-start.17 = (bf16[256,512]{1,0:T(8,128)(2,1)S(1)}, bf16[256,512]{1,0:T(8,128)(2,1)S(1)}, u32[]{:S(2)}, u32[]{:S(2)}) collective-permute-start(bf16[256,512]{1,0:T(8,128)(2,1)S(1)} %get-tuple-element.94), channel_id=1, source_target_pairs={{0,8},{1,9},{2,10},{3,11},{4,12},{5,13},{6,14},{7,15},{8,0},{9,1},... | collective-permute-start | bytes 786440 | tf_op jit(solution)/shard_map/ppermute | solution.py:348
  41.7 10.2 %collective-permute-start.26 = (bf16[128,1280]{1,0:T(8,128)(2,1)S(1)}, bf16[128,1280]{1,0:T(8,128)(2,1)S(1)}, u32[]{:S(2)}, u32[]{:S(2)}) collective-permute-start(bf16[128,1280]{1,0:T(8,128)(2,1)S(1)} %get-tuple-element.105), channel_id=1, source_target_pairs={{0,2},{1,3},{2,0},{3,1},{4,6},{5,7},{6,4},{7,5},{8,10},{9,11},{10,... | collective-permute-start | bytes 983048 | tf_op jit(solution)/shard_map/ppermute | solution.py:348
  41.7 9.0 %collective-permute-start.18 = (bf16[128,1152]{1,0:T(8,128)(2,1)S(1)}, bf16[128,1152]{1,0:T(8,128)(2,1)S(1)}, u32[]{:S(2)}, u32[]{:S(2)}) collective-permute-start(bf16[128,1152]{1,0:T(8,128)(2,1)S(1)} %get-tuple-element.97), channel_id=1, source_target_pairs={{0,16},{1,17},{2,18},{3,19},{4,20},{5,21},{6,22},{7,23},{8,24},{9,... | collective-permute-start | bytes 884744 | tf_op jit(solution)/shard_map/ppermute | solution.py:348
  43.2 8.7 %collective-permute-start.22 = (bf16[128,1152]{1,0:T(8,128)(2,1)S(1)}, bf16[128,1152]{1,0:T(8,128)(2,1)S(1)}, u32[]{:S(2)}, u32[]{:S(2)}) collective-permute-start(bf16[128,1152]{1,0:T(8,128)(2,1)S(1)} %get-tuple-element.101), channel_id=1, source_target_pairs={{0,1},{1,0},{2,3},{3,2},{4,5},{5,4},{6,7},{7,6},{8,9},{9,8},{10,11... | collective-permute-start | bytes 884744 | tf_op jit(solution)/shard_map/ppermute | solution.py:348
  52.0 5.2 %collective-permute-start.19 = (bf16[1,2,2,1,16,1152]{5,4,3,2,1,0:T(8,128)(2,1)S(1)}, bf16[1,2,2,1,16,1152]{5,4,3,2,1,0:T(8,128)(2,1)S(1)}, u32[]{:S(2)}, u32[]{:S(2)}) collective-permute-start(bf16[1,2,2,1,16,1152]{5,4,3,2,1,0:T(8,128)(2,1)S(1)} %fusion.1), channel_id=1, source_target_pairs={{0,1},{1,0},{2,3},{3,2},{4,5},{5,4},{6,7},{7,6},{8,9},{9,8},{10,11... | collective-permute-start | bytes 442376 | tf_op jit(solution)/shard_map/ppermute | solution.py:348
  53.7 6.0 %collective-permute-start.23 = (bf16[2,2,1,1,16,1152]{5,4,3,2,1,0:T(8,128)(2,1)S(1)}, bf16[2,2,1,1,16,1152]{5,4,3,2,1,0:T(8,128)(2,1)S(1)}, u32[]{:S(2)}, u32[]{:S(2)}) collective-permute-start(bf16[2,2,1,1,16,1152]{5,4,3,2,1,0:T(8,128)(2,1)S(1)} %fusion), channel_id=1, source_target_pairs={{0,2},{1,3},{2,0},{3,1},{4,6},{5,7},{6,4},{7,5},{8,10},{9,11},{10,... | collective-permute-start | bytes 442376 | tf_op jit(solution)/shard_map/ppermute | solution.py:348
  55.5 6.1 %collective-permute-start.27 = (bf16[1,2,1,2,16,1280]{5,4,3,2,1,0:T(8,128)(2,1)S(1)}, bf16[1,2,1,2,16,1280]{5,4,3,2,1,0:T(8,128)(2,1)S(1)}, u32[]{:S(2)}, u32[]{:S(2)}) collective-permute-start(bf16[1,2,1,2,16,1280]{5,4,3,2,1,0:T(8,128)(2,1)S(1)} %bitcast.59), channel_id=1, source_target_pairs={{0,16},{1,17},{2,18},{3,19},{4,20},{5,21},{6,22},{7,23},{8,24},{9,... | collective-permute-start | bytes 491528 | tf_op jit(solution)/shard_map/ppermute | solution.py:348
  57.2 6.5 %collective-permute-start.20 = (bf16[1,2,1,1,16,1152]{5,4,3,2,1,0:T(8,128)(2,1)S(1)}, bf16[1,2,1,1,16,1152]{5,4,3,2,1,0:T(8,128)(2,1)S(1)}, u32[]{:S(2)}, u32[]{:S(2)}) collective-permute-start(bf16[1,2,1,1,16,1152]{5,4,3,2,1,0:T(8,128)(2,1)S(1)} %fusion.7), channel_id=1, source_target_pairs={{0,2},{1,3},{2,0},{3,1},{4,6},{5,7},{6,4},{7,5},{8,10},{9,11},{10,... | collective-permute-start | bytes 221192 | tf_op jit(solution)/shard_map/ppermute | solution.py:348
  59.7 5.0 %collective-permute-start.24 = (bf16[1,2,1,1,16,1152]{5,4,3,2,1,0:T(8,128)(2,1)S(1)}, bf16[1,2,1,1,16,1152]{5,4,3,2,1,0:T(8,128)(2,1)S(1)}, u32[]{:S(2)}, u32[]{:S(2)}) collective-permute-start(bf16[1,2,1,1,16,1152]{5,4,3,2,1,0:T(8,128)(2,1)S(1)} %fusion.5), channel_id=1, source_target_pairs={{0,16},{1,17},{2,18},{3,19},{4,20},{5,21},{6,22},{7,23},{8,24},{9,... | collective-permute-start | bytes 221192 | tf_op jit(solution)/shard_map/ppermute | solution.py:348
  61.6 6.2 %collective-permute-start.28 = (bf16[1,1,1,2,16,1280]{5,4,3,2,1,0:T(8,128)(2,1)S(1)}, bf16[1,1,1,2,16,1280]{5,4,3,2,1,0:T(8,128)(2,1)S(1)}, u32[]{:S(2)}, u32[]{:S(2)}) collective-permute-start(bf16[1,1,1,2,16,1280]{5,4,3,2,1,0:T(8,128)(2,1)S(1)} %fusion.3), channel_id=1, source_target_pairs={{0,4},{1,5},{2,6},{3,7},{4,0},{5,1},{6,2},{7,3},{8,12},{9,13},{10,... | collective-permute-start | bytes 245768 | tf_op jit(solution)/shard_map/ppermute | solution.py:348
  63.7 5.2 %collective-permute-start.21 = (bf16[1,1,1,1,16,1152]{5,4,3,2,1,0:T(8,128)(2,1)S(1)}, bf16[1,1,1,1,16,1152]{5,4,3,2,1,0:T(8,128)(2,1)S(1)}, u32[]{:S(2)}, u32[]{:S(2)}) collective-permute-start(bf16[1,1,1,1,16,1152]{5,4,3,2,1,0:T(8,128)(2,1)S(1)} %fusion.22), channel_id=1, source_target_pairs={{0,4},{1,5},{2,6},{3,7},{4,0},{5,1},{6,2},{7,3},{8,12},{9,13},{10,... | collective-permute-start | bytes 110600 | tf_op jit(solution)/shard_map/ppermute | solution.py:348
  64.7 4.9 %collective-permute-start.25 = (bf16[1,1,1,1,16,1152]{5,4,3,2,1,0:T(8,128)(2,1)S(1)}, bf16[1,1,1,1,16,1152]{5,4,3,2,1,0:T(8,128)(2,1)S(1)}, u32[]{:S(2)}, u32[]{:S(2)}) collective-permute-start(bf16[1,1,1,1,16,1152]{5,4,3,2,1,0:T(8,128)(2,1)S(1)} %fusion.16), channel_id=1, source_target_pairs={{0,4},{1,5},{2,6},{3,7},{4,0},{5,1},{6,2},{7,3},{8,12},{9,13},{10,... | collective-permute-start | bytes 110600 | tf_op jit(solution)/shard_map/ppermute | solution.py:348
  67.8 4.1 %collective-permute-start.29 = (bf16[1,1,1,1,16,1280]{5,4,3,2,1,0:T(8,128)(2,1)S(1)}, bf16[1,1,1,1,16,1280]{5,4,3,2,1,0:T(8,128)(2,1)S(1)}, u32[]{:S(2)}, u32[]{:S(2)}) collective-permute-start(bf16[1,1,1,1,16,1280]{5,4,3,2,1,0:T(8,128)(2,1)S(1)} %fusion.10), channel_id=1, source_target_pairs={{0,1},{1,0},{2,3},{3,2},{4,5},{5,4},{6,7},{7,6},{8,9},{9,8},{10,11... | collective-permute-start | bytes 122888 | tf_op jit(solution)/shard_map/ppermute | solution.py:348

commit v20 on v17

--- a/solution.py
+++ b/solution.py
@@ -428,7 +428,7 @@
         masks[1 + b] = shards >> (1 + b)
     ydim, wdim = bits, bits - 1
     third = depth // 128 // 3 * 128
-    edges = (0, third, 2 * third, depth)
+    edges = (0, depth - 2 * third, depth - third, depth)
     orders = [(0, ydim, wdim), (ydim, wdim, 0), (wdim, 0, ydim)]
     low = owned.bit_length() - 1
     row_bit = {0: low + bits, ydim: low, wdim: low + 1}

time: 71.9 us -> 72.2 us (level)
  waiting for transfers between devices: 13.1 us -> 16.5 us
  starting transfers between devices: 34.9 us -> 31.6 us
    ppermute x30, waiting for transfers between devices: 13.1 us -> 16.5 us  [swap(): return lax.ppermute(value, AXES, [(i, i ^ mask) for i in range(count)])]
    ppermute x30, starting transfers between devices: 34.9 us -> 31.6 us  [swap(): return lax.ppermute(value, AXES, [(i, i ^ mask) for i in range(count)])]
  transfers between devices with their start and end apart: 30 -> 30, of which waited for: 12 -> 14; matrix products, arithmetic and copies ran while one was open for 5% -> 5% of each run, Pallas kernels for 16% -> 16%
where the time goes in v20:
time: 72.2 us; the launch traced here: 71.9 us
  starting transfers between devices  31.6 us (44%)
  waiting for transfers between devices  16.5 us (23%)
  Pallas kernels  16.3 us (23%)
  local copies, waits for them, and re-layouts  5.47 us (8%)
  other arithmetic  1.23 us (2%)
  between operations  0.82 us (1%)
    ppermute x30, starting transfers between devices, swap(): return lax.ppermute(value, AXES, [(i, i ^ mask) for i in range(count)])  31.6 us
    ppermute x30, waiting for transfers between devices, swap(): return lax.ppermute(value, AXES, [(i, i ^ mask) for i in range(count)])  16.5 us
    pallas_call x1, Pallas kernels, head_gradient(): pl.pallas_call(head_kernel, grid=(depth // tile,), out_shape=shape((depth...  5.98 us
    pallas_call x1, Pallas kernels, back_rows(): pl.pallas_call(lambda *refs: back_kernel(bits, edges, low, len(stats), *r...  4.55 us
    pallas_call x1, Pallas kernels, far_logits(): pl.pallas_call(lambda *refs: far_kernel(len(pieces), *refs), out_shape=(s...  2.19 us
    dynamic_slice x2, local copies, waits for them, and re-layouts, cut(): return lax.dynamic_slice(value, indices, sizes)  2.13 us
    pallas_call x2, Pallas kernels, near_logits(): pl.pallas_call(near_kernel, out_shape=(shape((per, cols), F32), shape((ST...  1.74 us
  transfers between devices with their start and end apart: 30, of which 14 were waited for; matrix products, arithmetic and copies ran while one was open for 5% of the time, Pallas kernels for 16%

profile of v20, /device:TPU:0, one launch (start us, length us, event | category | flops | bytes accessed | tf_op | source)
XLA Modules:
  0.0 71.9 jit_solution(4878159082892025075)
XLA Ops:
  0.7 0.0 copy-start
  0.7 0.1 pad_add_fusion.2.at_ref
  0.7 0.1 pad_add_fusion
  0.8 1.1 %constant_dynamic-slice_fusion.1 = bf16[24,3584]{1,0:T(8,128)(2,1)S(1)} fusion(bf16[128,3584]{1,0:T(8,128)(2,1)} %refs_8_, u32[]{:T(128)S(6)} %convert_element_type.149), kind=kLoop, calls=%fused_computation.42 | loop fusion | bytes 344068 | tf_op jit(solution)/shard_map/dynamic_slice | solution.py:377
  2.0 0.5 collective-permute-start
  2.5 2.6 %collective-permute-start.1 = (bf16[24,3584]{1,0:T(8,128)(2,1)S(1)}, bf16[24,3584]{1,0:T(8,128)(2,1)S(1)}, u32[]{:S(2)}, u32[]{:S(2)}) collective-permute-start(bf16[24,3584]{1,0:T(8,128)(2,1)S(1)} %constant_dynamic-slice_fusion.1), channel_id=1, source_target_pairs={{0,16},{1,17},{2,18},{3,19},{4,20},{5,21},{6,22},{7,23},{8,24},{9,... | collective-permute-start | bytes 516104 | tf_op jit(solution)/shard_map/ppermute | solution.py:350
  5.0 1.0 %slice.173 = bf16[32,3584]{1,0:T(8,128)(2,1)S(1)} slice(bf16[128,3584]{1,0:T(8,128)(2,1)} %refs_8_), slice={[96:128], [0:3584]} | slice | bytes 458752 | tf_op jit(solution)/shard_map/slice | solution.py:384
  6.0 0.1 collective-permute-start.6
  6.1 1.1 %copy.7 = bf16[128,4,512]{2,0,1:T(8,128)(2,1)S(1)} copy(bf16[128,4,512]{2,1,0:T(4,128)(2,1)} %param.9) | data formatting | bytes 1048576 | tf_op jit(solution)/shard_map/optimization_barrier | solution.py:353
  7.3 0.4 taught_stats.1.refs_11_
  7.6 0.2 collective-permute-start.2
  7.8 1.0 %constant_dynamic-slice_fusion = bf16[24,3584]{1,0:T(8,128)(2,1)S(1)} fusion(bf16[128,3584]{1,0:T(8,128)(2,1)} %refs_8_, u32[]{:T(128)S(6)} %convert_element_type.150), kind=kLoop, calls=%fused_computation.41 | loop fusion | bytes 344068 | tf_op jit(solution)/shard_map/dynamic_slice | solution.py:377
  8.8 1.9 %collective-permute-start.5 = (bf16[24,3584]{1,0:T(8,128)(2,1)S(1)}, bf16[24,3584]{1,0:T(8,128)(2,1)S(1)}, u32[]{:S(2)}, u32[]{:S(2)}) collective-permute-start(bf16[24,3584]{1,0:T(8,128)(2,1)S(1)} %constant_dynamic-slice_fusion), channel_id=1, source_target_pairs={{0,16},{1,17},{2,18},{3,19},{4,20},{5,21},{6,22},{7,23},{8,24},{9,... | collective-permute-start | bytes 516104 | tf_op jit(solution)/shard_map/ppermute | solution.py:350
  10.8 1.6 %collective-permute-start.4 = (bf16[24,3584]{1,0:T(8,128)(2,1)S(1)}, bf16[24,3584]{1,0:T(8,128)(2,1)S(1)}, u32[]{:S(2)}, u32[]{:S(2)}) collective-permute-start(bf16[24,3584]{1,0:T(8,128)(2,1)S(1)} %collective-permute-done.1.refs_0_.refs_1_), channel_id=1, source_target_pairs={{0,2},{1,3},{2,0},{3,1},{4,6},{5,7},{6,4},{7,5},{8,10},{9,11},{10,... | collective-permute-start | bytes 516104 | tf_op jit(solution)/shard_map/ppermute | solution.py:350
  12.4 1.5 %collective-permute-start.3 = (bf16[24,3584]{1,0:T(8,128)(2,1)S(1)}, bf16[24,3584]{1,0:T(8,128)(2,1)S(1)}, u32[]{:S(2)}, u32[]{:S(2)}) collective-permute-start(bf16[24,3584]{1,0:T(8,128)(2,1)S(1)} %collective-permute-done.1.refs_0_.refs_1_), channel_id=1, source_target_pairs={{0,1},{1,0},{2,3},{3,2},{4,5},{5,4},{6,7},{7,6},{8,9},{9,8},{10,11... | collective-permute-start | bytes 516104 | tf_op jit(solution)/shard_map/ppermute | solution.py:350
  13.9 1.2 %copy-done.1 = bf16[128,3584]{1,0:T(8,128)(2,1)S(1)} copy-done((bf16[128,3584]{1,0:T(8,128)(2,1)S(1)}, bf16[128,3584]{1,0:T(8,128)(2,1)}, u32[]{:S(2)}) %copy-start.1) | copy-done | bytes 917528
  15.1 0.9 %near_logits.2 = (f32[128,512]{1,0:T(8,128)S(1)}, f32[8,128]{1,0:T(8,128)S(1)}) custom-call(bf16[128,3584]{1,0:T(8,128)(2,1)S(1)} %copy-done.1, bf16[3584,512]{1,0:T(8,128)(2,1)S(1)} %copy-done, bf16[24,3584]{1,0:T(8,128)(2,1)S(1)} %collective-permute-done.1.refs_0_.refs_1_), custom_call_target="tpu_custom_call" | custom-call | flops 469762048 | bytes 4587520 | tf_op jit(solution)/shard_map/near_logits/pallas_call | solution.py:109
  15.9 0.0 collective-permute-done.w_ref.refs_7_.refs_2_
  15.9 0.9 %near_logits.3 = (f32[128,512]{1,0:T(8,128)S(1)}, f32[8,128]{1,0:T(8,128)S(1)}) custom-call(bf16[128,3584]{1,0:T(8,128)(2,1)S(1)} %copy-done.1, bf16[3584,512]{1,0:T(8,128)(2,1)S(1)} %collective-permute-done.w_ref.refs_7_.refs_2_, bf16[24,3584]{1,0:T(8,128)(2,1)S(1)} %collective-permute-done.1.refs_0_.refs_1_), custom_call_target="tpu_custom_call" | custom-call | flops 469762048 | bytes 4587520 | tf_op jit(solution)/shard_map/near_logits/pallas_call | solution.py:109
  16.8 1.8 %collective-permute-done.5.refs_4_ = bf16[24,3584]{1,0:T(8,128)(2,1)S(1)} collective-permute-done((bf16[24,3584]{1,0:T(8,128)(2,1)S(1)}, bf16[24,3584]{1,0:T(8,128)(2,1)S(1)}, u32[]{:S(2)}, u32[]{:S(2)}) %collective-permute-start.5) | collective-permute-done | bytes 172064 | tf_op jit(solution)/shard_map/ppermute | solution.py:350
  18.6 0.0 collective-permute-done.3.refs_2_
  18.6 1.8 %collective-permute-start.14 = (bf16[2,128,512]{2,1,0:T(8,128)(2,1)S(1)}, bf16[2,128,512]{2,1,0:T(8,128)(2,1)S(1)}, u32[]{:S(2)}, u32[]{:S(2)}) collective-permute-start(bf16[2,128,512]{2,1,0:T(8,128)(2,1)S(1)} %get-tuple-element.88.gone_ref), channel_id=1, source_target_pairs={{0,16},{1,17},{2,18},{3,19},{4,20},{5,21},{6,22},{7,23},{8,24},{9,... | collective-permute-start | bytes 786440 | tf_op jit(solution)/shard_map/ppermute | solution.py:350
  20.5 2.2 %far_logits.1 = (f32[128,512]{1,0:T(8,128)S(1)}, f32[128,512]{1,0:T(8,128)S(1)}, bf16[2,128,3584]{2,1,0:T(8,128)(2,1)S(1)}, f32[2,8,128]{2,1,0:T(8,128)S(1)}, f32[8,128]{1,0:T(8,128)S(1)}) custom-call(s32[4]{0:T(128)S(1)} %get-tuple-element.60.refs_0_, bf16[24,3584]{1,0:T(8,128)(2,1)S(1)} %collective-permute-done.1.refs_0_.refs_1_, ...), custom_call_target="tpu_custom_call" | custom-call | flops 939524096 | bytes 8257536 | tf_op jit(solution)/shard_map/far_logits/pallas_call | solution.py:161
  22.7 0.0 copy-start.3
  22.7 3.6 %collective-permute-start.9 = (f32[2,8,128]{2,1,0:T(8,128)S(1)}, f32[2,8,128]{2,1,0:T(8,128)S(1)}, u32[]{:S(2)}, u32[]{:S(2)}) collective-permute-start(f32[2,8,128]{2,1,0:T(8,128)S(1)} %get-tuple-element.80.refs_0_), channel_id=1, source_target_pairs={{0,6},{1,7},{2,4},{3,5},{4,2},{5,3},{6,0},{7,1},{8,14},{9,15},{10,... | collective-permute-start | bytes 24584 | tf_op jit(solution)/shard_map/ppermute | solution.py:350
  26.3 0.0 collective-permute-start.8
  26.3 0.8 %collective-permute-start.7 = (f32[2,8,128]{2,1,0:T(8,128)S(1)}, f32[2,8,128]{2,1,0:T(8,128)S(1)}, u32[]{:S(2)}, u32[]{:S(2)}) collective-permute-start(f32[2,8,128]{2,1,0:T(8,128)S(1)} %get-tuple-element.80.refs_0_), channel_id=1, source_target_pairs={{0,2},{1,3},{2,0},{3,1},{4,6},{5,7},{6,4},{7,5},{8,10},{9,11},{10,... | collective-permute-start | bytes 24584 | tf_op jit(solution)/shard_map/ppermute | solution.py:350
  27.1 1.1 %collective-permute-done.9.refs_3_ = f32[2,8,128]{2,1,0:T(8,128)S(1)} collective-permute-done((f32[2,8,128]{2,1,0:T(8,128)S(1)}, f32[2,8,128]{2,1,0:T(8,128)S(1)}, u32[]{:S(2)}, u32[]{:S(2)}) %collective-permute-start.9) | collective-permute-done | bytes 8224 | tf_op jit(solution)/shard_map/ppermute | solution.py:350
  28.2 2.7 %collective-permute-done.8.refs_2_ = f32[2,8,128]{2,1,0:T(8,128)S(1)} collective-permute-done((f32[2,8,128]{2,1,0:T(8,128)S(1)}, f32[2,8,128]{2,1,0:T(8,128)S(1)}, u32[]{:S(2)}, u32[]{:S(2)}) %collective-permute-start.8) | collective-permute-done | bytes 8224 | tf_op jit(solution)/shard_map/ppermute | solution.py:350
  30.9 0.1 collective-permute-start.15
  31.0 1.6 %collective-permute-start.12 = (f32[2,8,128]{2,1,0:T(8,128)S(1)}, f32[2,8,128]{2,1,0:T(8,128)S(1)}, u32[]{:S(2)}, u32[]{:S(2)}) collective-permute-start(f32[2,8,128]{2,1,0:T(8,128)S(1)} %merge_stats.1.refs_3_), channel_id=1, source_target_pairs={{0,17},{1,16},{2,19},{3,18},{4,21},{5,20},{6,23},{7,22},{8,25},{9,... | collective-permute-start | bytes 24584 | tf_op jit(solution)/shard_map/ppermute | solution.py:350
  32.6 0.5 collective-permute-start.11
  33.1 1.5 %collective-permute-start.10 = (f32[2,8,128]{2,1,0:T(8,128)S(1)}, f32[2,8,128]{2,1,0:T(8,128)S(1)}, u32[]{:S(2)}, u32[]{:S(2)}) collective-permute-start(f32[2,8,128]{2,1,0:T(8,128)S(1)} %merge_stats.1.refs_3_), channel_id=1, source_target_pairs={{0,16},{1,17},{2,18},{3,19},{4,20},{5,21},{6,22},{7,23},{8,24},{9,... | collective-permute-start | bytes 24584 | tf_op jit(solution)/shard_map/ppermute | solution.py:350
  34.6 0.0 collective-permute-done.15.a3
  34.6 1.4 %teacher_rows.1 = (f32[2,128,1024]{2,1,0:T(8,128)S(1)}, f32[2,8,128]{2,1,0:T(8,128)S(1)}) custom-call(s32[2]{0:T(128)S(1)} %pad_add_fusion.2.at_ref, s32[4,1,128]{2,1,0:T(1,128)S(1)} %bitcast.42, bf16[2,128,512]{2,1,0:T(8,128)(2,1)S(1)} %get-tuple-element.87.kept_ref.a0, bf16[2,128,512]{2,1,0:T(8,128)(2,1)S(1)} %collective-permute-done.13.a1, ...), custom_call_target="tpu_custom_call" | custom-call | flops 268435456 | bytes 1572864 | tf_op jit(solution)/shard_map/teacher_rows/pallas_call | solution.py:82
  36.0 0.0 collective-permute-done.12.refs_6_
  36.0 0.2 collective-permute-done.11.refs_5_
  36.2 0.5 collective-permute-done.10.refs_4_
  36.7 4.5 %back_rows.1 = (bf16[256,512]{1,0:T(8,128)(2,1)S(1)}, bf16[256,512]{1,0:T(8,128)(2,1)S(1)}, bf16[128,1280]{1,0:T(8,128)(2,1)S(1)}, bf16[128,1152]{1,0:T(8,128)(2...) custom-call(s32[4]{0:T(128)S(1)} %get-tuple-element.55.refs_0_, ...), custom_call_target="tpu_custom_call" | custom-call | flops 1879048192 | bytes 7340032 | tf_op jit(solution)/shard_map/back_rows/pallas_call | solution.py:294
  41.3 0.1 collective-permute-start.16
  41.3 0.5 collective-permute-start.17
  41.8 1.5 %collective-permute-start.18 = (bf16[128,1280]{1,0:T(8,128)(2,1)S(1)}, bf16[128,1280]{1,0:T(8,128)(2,1)S(1)}, u32[]{:S(2)}, u32[]{:S(2)}) collective-permute-start(bf16[128,1280]{1,0:T(8,128)(2,1)S(1)} %get-tuple-element.97), channel_id=1, source_target_pairs={{0,16},{1,17},{2,18},{3,19},{4,20},{5,21},{6,22},{7,23},{8,24},{9,... | collective-permute-start | bytes 983048 | tf_op jit(solution)/shard_map/ppermute | solution.py:350
  43.3 1.5 %collective-permute-start.22 = (bf16[128,1152]{1,0:T(8,128)(2,1)S(1)}, bf16[128,1152]{1,0:T(8,128)(2,1)S(1)}, u32[]{:S(2)}, u32[]{:S(2)}) collective-permute-start(bf16[128,1152]{1,0:T(8,128)(2,1)S(1)} %get-tuple-element.101), channel_id=1, source_target_pairs={{0,1},{1,0},{2,3},{3,2},{4,5},{5,4},{6,7},{7,6},{8,9},{9,8},{10,11... | collective-permute-start | bytes 884744 | tf_op jit(solution)/shard_map/ppermute | solution.py:350
  44.8 0.6 collective-permute-done.17.theirs_ref
  45.5 6.0 %head_gradient.1 = bf16[3584,512]{1,0:T(8,128)(2,1)} custom-call(bf16[2,128,3584]{2,1,0:T(8,128)(2,1)S(1)} %get-tuple-element.95.rows_ref, bf16[2,128,3584]{2,1,0:T(8,128)(2,1)S(1)} %collective-permute-done.16.core_ref, bf16[256,512]{1,0:T(8,128)(2,1)S(1)} %get-tuple-element.96.mine_ref, bf16[256,512]{1,0:T(8,128)(2,1)S(1)} %collective-permute-done.17.theirs_ref), custom_call_target="tpu_custom_call" | custom-call | flops 1879048192 | bytes 7340032 | tf_op jit(solution)/shard_map/head_gradient/pallas_call | solution.py:323
  51.5 0.1 collective-permute-done.18
  51.5 0.5 collective-permute-done.22
  52.0 1.2 %collective-permute-done.26 = bf16[128,1152]{1,0:T(8,128)(2,1)S(1)} collective-permute-done((bf16[128,1152]{1,0:T(8,128)(2,1)S(1)}, bf16[128,1152]{1,0:T(8,128)(2,1)S(1)}, u32[]{:S(2)}, u32[]{:S(2)}) %collective-permute-start.26) | collective-permute-done | bytes 294944 | tf_op jit(solution)/shard_map/ppermute | solution.py:350
  53.3 0.1 add_convert_fusion
  53.4 0.3 collective-permute-start.23
  53.7 0.5 collective-permute-start.27
  54.3 0.6 collective-permute-start.19
  54.9 3.7 %collective-permute-done.23 = bf16[2,2,1,1,16,1152]{5,4,3,2,1,0:T(8,128)(2,1)S(1)} collective-permute-done((bf16[2,2,1,1,16,1152]{5,4,3,2,1,0:T(8,128)(2,1)S(1)}, bf16[2,2,1,1,16,1152]{5,4,3,2,1,0:T(8,128)(2,1)S(1)}, u32[]{:S(2)}, u32[]{:S(2)}) %collective-permute-start.23) | collective-permute-done | bytes 147488 | tf_op jit(solution)/shard_map/ppermute | solution.py:350
  58.6 0.6 collective-permute-start.24
  59.3 1.5 %collective-permute-start.28 = (bf16[1,2,1,1,16,1152]{5,4,3,2,1,0:T(8,128)(2,1)S(1)}, bf16[1,2,1,1,16,1152]{5,4,3,2,1,0:T(8,128)(2,1)S(1)}, u32[]{:S(2)}, u32[]{:S(2)}) collective-permute-start(bf16[1,2,1,1,16,1152]{5,4,3,2,1,0:T(8,128)(2,1)S(1)} %fusion.5), channel_id=1, source_target_pairs={{0,1},{1,0},{2,3},{3,2},{4,5},{5,4},{6,7},{7,6},{8,9},{9,8},{10,11... | collective-permute-start | bytes 221192 | tf_op jit(solution)/shard_map/ppermute | solution.py:350
  60.8 1.0 %collective-permute-start.20 = (bf16[1,2,1,1,16,1280]{5,4,3,2,1,0:T(8,128)(2,1)S(1)}, bf16[1,2,1,1,16,1280]{5,4,3,2,1,0:T(8,128)(2,1)S(1)}, u32[]{:S(2)}, u32[]{:S(2)}) collective-permute-start(bf16[1,2,1,1,16,1280]{5,4,3,2,1,0:T(8,128)(2,1)S(1)} %fusion.3), channel_id=1, source_target_pairs={{0,2},{1,3},{2,0},{3,1},{4,6},{5,7},{6,4},{7,5},{8,10},{9,11},{10,... | collective-permute-start | bytes 245768 | tf_op jit(solution)/shard_map/ppermute | solution.py:350
  61.8 1.2 %collective-permute-done.24 = bf16[1,2,1,1,16,1152]{5,4,3,2,1,0:T(8,128)(2,1)S(1)} collective-permute-done((bf16[1,2,1,1,16,1152]{5,4,3,2,1,0:T(8,128)(2,1)S(1)}, bf16[1,2,1,1,16,1152]{5,4,3,2,1,0:T(8,128)(2,1)S(1)}, u32[]{:S(2)}, u32[]{:S(2)}) %collective-permute-start.24) | collective-permute-done | bytes 73760 | tf_op jit(solution)/shard_map/ppermute | solution.py:350
  63.1 2.1 %collective-permute-start.25 = (bf16[1,1,1,1,16,1152]{5,4,3,2,1,0:T(8,128)(2,1)S(1)}, bf16[1,1,1,1,16,1152]{5,4,3,2,1,0:T(8,128)(2,1)S(1)}, u32[]{:S(2)}, u32[]{:S(2)}) collective-permute-start(bf16[1,1,1,1,16,1152]{5,4,3,2,1,0:T(8,128)(2,1)S(1)} %fusion.22), channel_id=1, source_target_pairs={{0,4},{1,5},{2,6},{3,7},{4,0},{5,1},{6,2},{7,3},{8,12},{9,13},{10,... | collective-permute-start | bytes 110600 | tf_op jit(solution)/shard_map/ppermute | solution.py:350
  65.2 1.0 %collective-permute-start.29 = (bf16[1,1,1,1,16,1152]{5,4,3,2,1,0:T(8,128)(2,1)S(1)}, bf16[1,1,1,1,16,1152]{5,4,3,2,1,0:T(8,128)(2,1)S(1)}, u32[]{:S(2)}, u32[]{:S(2)}) collective-permute-start(bf16[1,1,1,1,16,1152]{5,4,3,2,1,0:T(8,128)(2,1)S(1)} %fusion.16), channel_id=1, source_target_pairs={{0,4},{1,5},{2,6},{3,7},{4,0},{5,1},{6,2},{7,3},{8,12},{9,13},{10,... | collective-permute-start | bytes 110600 | tf_op jit(solution)/shard_map/ppermute | solution.py:350
  66.2 2.1 %collective-permute-start.21 = (bf16[1,1,1,1,16,1280]{5,4,3,2,1,0:T(8,128)(2,1)S(1)}, bf16[1,1,1,1,16,1280]{5,4,3,2,1,0:T(8,128)(2,1)S(1)}, u32[]{:S(2)}, u32[]{:S(2)}) collective-permute-start(bf16[1,1,1,1,16,1280]{5,4,3,2,1,0:T(8,128)(2,1)S(1)} %fusion.10), channel_id=1, source_target_pairs={{0,4},{1,5},{2,6},{3,7},{4,0},{5,1},{6,2},{7,3},{8,12},{9,13},{10,... | collective-permute-start | bytes 122888 | tf_op jit(solution)/shard_map/ppermute | solution.py:350
  68.3 0.2 collective-permute-done.25
  68.5 2.0 %collective-permute-done.29 = bf16[1,1,1,1,16,1152]{5,4,3,2,1,0:T(8,128)(2,1)S(1)} collective-permute-done((bf16[1,1,1,1,16,1152]{5,4,3,2,1,0:T(8,128)(2,1)S(1)}, bf16[1,1,1,1,16,1152]{5,4,3,2,1,0:T(8,128)(2,1)S(1)}, u32[]{:S(2)}, u32[]{:S(2)}) %collective-permute-start.29) | collective-permute-done | bytes 36896 | tf_op jit(solution)/shard_map/ppermute | solution.py:350
  70.5 0.6 collective-permute-done.21
  71.2 0.7 maximum_bitcast_fusion
  (35 shorter events, 0.5 us)
Async XLA Ops:
  0.7 13.2 %copy-start = (bf16[3584,512]{1,0:T(8,128)(2,1)S(1)}, bf16[3584,512]{1,0:T(8,128)(2,1)}, u32[]{:S(2)}) copy-start(bf16[3584,512]{1,0:T(8,128)(2,1)} %refs_1_) | copy-start | bytes 11010052
  2.0 14.0 %collective-permute-start = (bf16[3584,512]{1,0:T(8,128)(2,1)}, bf16[3584,512]{1,0:T(8,128)(2,1)S(1)}, u32[]{:S(2)}, u32[]{:S(2)}) collective-permute-start(bf16[3584,512]{1,0:T(8,128)(2,1)} %refs_1_), channel_id=1, source_target_pairs={{0,8},{1,9},{2,10},{3,11},{4,12},{5,13},{6,14},{7,15},{8,0},{9,1},... | collective-permute-start | bytes 11010056 | tf_op jit(solution)/shard_map/ppermute | solution.py:350
  2.5 8.3 %collective-permute-start.1 = (bf16[24,3584]{1,0:T(8,128)(2,1)S(1)}, bf16[24,3584]{1,0:T(8,128)(2,1)S(1)}, u32[]{:S(2)}, u32[]{:S(2)}) collective-permute-start(bf16[24,3584]{1,0:T(8,128)(2,1)S(1)} %constant_dynamic-slice_fusion.1), channel_id=1, source_target_pairs={{0,16},{1,17},{2,18},{3,19},{4,20},{5,21},{6,22},{7,23},{8,24},{9,... | collective-permute-start | bytes 516104 | tf_op jit(solution)/shard_map/ppermute | solution.py:350
  6.0 12.6 %collective-permute-start.6 = (bf16[32,3584]{1,0:T(8,128)(2,1)S(1)}, bf16[32,3584]{1,0:T(8,128)(2,1)S(1)}, u32[]{:S(2)}, u32[]{:S(2)}) collective-permute-start(bf16[32,3584]{1,0:T(8,128)(2,1)S(1)} %slice.173), channel_id=1, source_target_pairs={{0,16},{1,17},{2,18},{3,19},{4,20},{5,21},{6,22},{7,23},{8,24},{9,... | collective-permute-start | bytes 688136 | tf_op jit(solution)/shard_map/ppermute | solution.py:350
  7.6 3.1 %collective-permute-start.2 = (f32[8,128]{1,0:T(8,128)S(1)}, f32[8,128]{1,0:T(8,128)S(1)}, u32[]{:S(2)}, u32[]{:S(2)}) collective-permute-start(f32[8,128]{1,0:T(8,128)S(1)} %taught_stats.1.refs_11_), channel_id=1, source_target_pairs={{0,8},{1,9},{2,10},{3,11},{4,12},{5,13},{6,14},{7,15},{8,0},{9,1},... | collective-permute-start | bytes 12296 | tf_op jit(solution)/shard_map/ppermute | solution.py:350
  7.8 12.6 %copy-start.4 = (s32[128]{0:T(128)S(1)}, s32[128]{0:T(128)}, u32[]{:S(2)}) copy-start(s32[128]{0:T(128)} %param.6) | copy-start | bytes 1540
  8.8 9.8 %collective-permute-start.5 = (bf16[24,3584]{1,0:T(8,128)(2,1)S(1)}, bf16[24,3584]{1,0:T(8,128)(2,1)S(1)}, u32[]{:S(2)}, u32[]{:S(2)}) collective-permute-start(bf16[24,3584]{1,0:T(8,128)(2,1)S(1)} %constant_dynamic-slice_fusion), channel_id=1, source_target_pairs={{0,16},{1,17},{2,18},{3,19},{4,20},{5,21},{6,22},{7,23},{8,24},{9,... | collective-permute-start | bytes 516104 | tf_op jit(solution)/shard_map/ppermute | solution.py:350
  10.8 7.8 %collective-permute-start.4 = (bf16[24,3584]{1,0:T(8,128)(2,1)S(1)}, bf16[24,3584]{1,0:T(8,128)(2,1)S(1)}, u32[]{:S(2)}, u32[]{:S(2)}) collective-permute-start(bf16[24,3584]{1,0:T(8,128)(2,1)S(1)} %collective-permute-done.1.refs_0_.refs_1_), channel_id=1, source_target_pairs={{0,2},{1,3},{2,0},{3,1},{4,6},{5,7},{6,4},{7,5},{8,10},{9,11},{10,... | collective-permute-start | bytes 516104 | tf_op jit(solution)/shard_map/ppermute | solution.py:350
  12.4 6.3 %collective-permute-start.3 = (bf16[24,3584]{1,0:T(8,128)(2,1)S(1)}, bf16[24,3584]{1,0:T(8,128)(2,1)S(1)}, u32[]{:S(2)}, u32[]{:S(2)}) collective-permute-start(bf16[24,3584]{1,0:T(8,128)(2,1)S(1)} %collective-permute-done.1.refs_0_.refs_1_), channel_id=1, source_target_pairs={{0,1},{1,0},{2,3},{3,2},{4,5},{5,4},{6,7},{7,6},{8,9},{9,8},{10,11... | collective-permute-start | bytes 516104 | tf_op jit(solution)/shard_map/ppermute | solution.py:350
  13.9 1.2 %copy-start.1 = (bf16[128,3584]{1,0:T(8,128)(2,1)S(1)}, bf16[128,3584]{1,0:T(8,128)(2,1)}, u32[]{:S(2)}) copy-start(bf16[128,3584]{1,0:T(8,128)(2,1)} %refs_8_) | copy-start | bytes 2752516
  15.1 5.4 %copy-start.2 = (bf16[128,3584]{1,0:T(8,128)(2,1)S(1)}, bf16[128,3584]{1,0:T(8,128)(2,1)}, u32[]{:S(2)}) copy-start(bf16[128,3584]{1,0:T(8,128)(2,1)} %refs_8_) | copy-start | bytes 2752516
  18.6 12.3 %collective-permute-start.14 = (bf16[2,128,512]{2,1,0:T(8,128)(2,1)S(1)}, bf16[2,128,512]{2,1,0:T(8,128)(2,1)S(1)}, u32[]{:S(2)}, u32[]{:S(2)}) collective-permute-start(bf16[2,128,512]{2,1,0:T(8,128)(2,1)S(1)} %get-tuple-element.88.gone_ref), channel_id=1, source_target_pairs={{0,16},{1,17},{2,18},{3,19},{4,20},{5,21},{6,22},{7,23},{8,24},{9,... | collective-permute-start | bytes 786440 | tf_op jit(solution)/shard_map/ppermute | solution.py:350
  22.7 11.9 %copy-start.3 = (s32[512]{0:T(512)S(1)}, s32[512]{0:T(512)}, u32[]{:S(2)}) copy-start(s32[512]{0:T(512)} %param.7) | copy-start | bytes 6148
  22.7 5.5 %collective-permute-start.9 = (f32[2,8,128]{2,1,0:T(8,128)S(1)}, f32[2,8,128]{2,1,0:T(8,128)S(1)}, u32[]{:S(2)}, u32[]{:S(2)}) collective-permute-start(f32[2,8,128]{2,1,0:T(8,128)S(1)} %get-tuple-element.80.refs_0_), channel_id=1, source_target_pairs={{0,6},{1,7},{2,4},{3,5},{4,2},{5,3},{6,0},{7,1},{8,14},{9,15},{10,... | collective-permute-start | bytes 24584 | tf_op jit(solution)/shard_map/ppermute | solution.py:350
  26.3 4.5 %collective-permute-start.8 = (f32[2,8,128]{2,1,0:T(8,128)S(1)}, f32[2,8,128]{2,1,0:T(8,128)S(1)}, u32[]{:S(2)}, u32[]{:S(2)}) collective-permute-start(f32[2,8,128]{2,1,0:T(8,128)S(1)} %get-tuple-element.80.refs_0_), channel_id=1, source_target_pairs={{0,4},{1,5},{2,6},{3,7},{4,0},{5,1},{6,2},{7,3},{8,12},{9,13},{10,... | collective-permute-start | bytes 24584 | tf_op jit(solution)/shard_map/ppermute | solution.py:350
  26.3 4.5 %collective-permute-start.7 = (f32[2,8,128]{2,1,0:T(8,128)S(1)}, f32[2,8,128]{2,1,0:T(8,128)S(1)}, u32[]{:S(2)}, u32[]{:S(2)}) collective-permute-start(f32[2,8,128]{2,1,0:T(8,128)S(1)} %get-tuple-element.80.refs_0_), channel_id=1, source_target_pairs={{0,2},{1,3},{2,0},{3,1},{4,6},{5,7},{6,4},{7,5},{8,10},{9,11},{10,... | collective-permute-start | bytes 24584 | tf_op jit(solution)/shard_map/ppermute | solution.py:350
  27.1 7.4 %collective-permute-start.13 = (bf16[2,128,512]{2,1,0:T(8,128)(2,1)S(1)}, bf16[2,128,512]{2,1,0:T(8,128)(2,1)S(1)}, u32[]{:S(2)}, u32[]{:S(2)}) collective-permute-start(bf16[2,128,512]{2,1,0:T(8,128)(2,1)S(1)} %get-tuple-element.87.kept_ref.a0), channel_id=1, source_target_pairs={{0,8},{1,9},{2,10},{3,11},{4,12},{5,13},{6,14},{7,15},{8,0},{9,1},... | collective-permute-start | bytes 786440 | tf_op jit(solution)/shard_map/ppermute | solution.py:350
  30.9 3.6 %collective-permute-start.15 = (bf16[2,128,512]{2,1,0:T(8,128)(2,1)S(1)}, bf16[2,128,512]{2,1,0:T(8,128)(2,1)S(1)}, u32[]{:S(2)}, u32[]{:S(2)}) collective-permute-start(bf16[2,128,512]{2,1,0:T(8,128)(2,1)S(1)} %collective-permute-done.14.a2), channel_id=1, source_target_pairs={{0,8},{1,9},{2,10},{3,11},{4,12},{5,13},{6,14},{7,15},{8,0},{9,1},... | collective-permute-start | bytes 786440 | tf_op jit(solution)/shard_map/ppermute | solution.py:350
  31.0 5.0 %collective-permute-start.12 = (f32[2,8,128]{2,1,0:T(8,128)S(1)}, f32[2,8,128]{2,1,0:T(8,128)S(1)}, u32[]{:S(2)}, u32[]{:S(2)}) collective-permute-start(f32[2,8,128]{2,1,0:T(8,128)S(1)} %merge_stats.1.refs_3_), channel_id=1, source_target_pairs={{0,17},{1,16},{2,19},{3,18},{4,21},{5,20},{6,23},{7,22},{8,25},{9,... | collective-permute-start | bytes 24584 | tf_op jit(solution)/shard_map/ppermute | solution.py:350
  32.6 3.7 %collective-permute-start.11 = (f32[2,8,128]{2,1,0:T(8,128)S(1)}, f32[2,8,128]{2,1,0:T(8,128)S(1)}, u32[]{:S(2)}, u32[]{:S(2)}) collective-permute-start(f32[2,8,128]{2,1,0:T(8,128)S(1)} %merge_stats.1.refs_3_), channel_id=1, source_target_pairs={{0,1},{1,0},{2,3},{3,2},{4,5},{5,4},{6,7},{7,6},{8,9},{9,8},{10,11... | collective-permute-start | bytes 24584 | tf_op jit(solution)/shard_map/ppermute | solution.py:350
  33.1 3.7 %collective-permute-start.10 = (f32[2,8,128]{2,1,0:T(8,128)S(1)}, f32[2,8,128]{2,1,0:T(8,128)S(1)}, u32[]{:S(2)}, u32[]{:S(2)}) collective-permute-start(f32[2,8,128]{2,1,0:T(8,128)S(1)} %merge_stats.1.refs_3_), channel_id=1, source_target_pairs={{0,16},{1,17},{2,18},{3,19},{4,20},{5,21},{6,22},{7,23},{8,24},{9,... | collective-permute-start | bytes 24584 | tf_op jit(solution)/shard_map/ppermute | solution.py:350
  41.3 4.2 %collective-permute-start.16 = (bf16[2,128,3584]{2,1,0:T(8,128)(2,1)S(1)}, bf16[2,128,3584]{2,1,0:T(8,128)(2,1)S(1)}, u32[]{:S(2)}, u32[]{:S(2)}) collective-permute-start(bf16[2,128,3584]{2,1,0:T(8,128)(2,1)S(1)} %get-tuple-element.95.rows_ref), channel_id=1, source_target_pairs={{0,8},{1,9},{2,10},{3,11},{4,12},{5,13},{6,14},{7,15},{8,0},{9,1},... | collective-permute-start | bytes 5505032 | tf_op jit(solution)/shard_map/ppermute | solution.py:350
  41.3 4.1 %collective-permute-start.17 = (bf16[256,512]{1,0:T(8,128)(2,1)S(1)}, bf16[256,512]{1,0:T(8,128)(2,1)S(1)}, u32[]{:S(2)}, u32[]{:S(2)}) collective-permute-start(bf16[256,512]{1,0:T(8,128)(2,1)S(1)} %get-tuple-element.94), channel_id=1, source_target_pairs={{0,8},{1,9},{2,10},{3,11},{4,12},{5,13},{6,14},{7,15},{8,0},{9,1},... | collective-permute-start | bytes 786440 | tf_op jit(solution)/shard_map/ppermute | solution.py:350
  41.8 9.7 %collective-permute-start.18 = (bf16[128,1280]{1,0:T(8,128)(2,1)S(1)}, bf16[128,1280]{1,0:T(8,128)(2,1)S(1)}, u32[]{:S(2)}, u32[]{:S(2)}) collective-permute-start(bf16[128,1280]{1,0:T(8,128)(2,1)S(1)} %get-tuple-element.97), channel_id=1, source_target_pairs={{0,16},{1,17},{2,18},{3,19},{4,20},{5,21},{6,22},{7,23},{8,24},{9,... | collective-permute-start | bytes 983048 | tf_op jit(solution)/shard_map/ppermute | solution.py:350
  43.3 8.7 %collective-permute-start.22 = (bf16[128,1152]{1,0:T(8,128)(2,1)S(1)}, bf16[128,1152]{1,0:T(8,128)(2,1)S(1)}, u32[]{:S(2)}, u32[]{:S(2)}) collective-permute-start(bf16[128,1152]{1,0:T(8,128)(2,1)S(1)} %get-tuple-element.101), channel_id=1, source_target_pairs={{0,1},{1,0},{2,3},{3,2},{4,5},{5,4},{6,7},{7,6},{8,9},{9,8},{10,11... | collective-permute-start | bytes 884744 | tf_op jit(solution)/shard_map/ppermute | solution.py:350
  44.8 8.4 %collective-permute-start.26 = (bf16[128,1152]{1,0:T(8,128)(2,1)S(1)}, bf16[128,1152]{1,0:T(8,128)(2,1)S(1)}, u32[]{:S(2)}, u32[]{:S(2)}) collective-permute-start(bf16[128,1152]{1,0:T(8,128)(2,1)S(1)} %get-tuple-element.105), channel_id=1, source_target_pairs={{0,2},{1,3},{2,0},{3,1},{4,6},{5,7},{6,4},{7,5},{8,10},{9,11},{10,... | collective-permute-start | bytes 884744 | tf_op jit(solution)/shard_map/ppermute | solution.py:350
  53.4 5.2 %collective-permute-start.23 = (bf16[2,2,1,1,16,1152]{5,4,3,2,1,0:T(8,128)(2,1)S(1)}, bf16[2,2,1,1,16,1152]{5,4,3,2,1,0:T(8,128)(2,1)S(1)}, u32[]{:S(2)}, u32[]{:S(2)}) collective-permute-start(bf16[2,2,1,1,16,1152]{5,4,3,2,1,0:T(8,128)(2,1)S(1)} %fusion.1), channel_id=1, source_target_pairs={{0,2},{1,3},{2,0},{3,1},{4,6},{5,7},{6,4},{7,5},{8,10},{9,11},{10,... | collective-permute-start | bytes 442376 | tf_op jit(solution)/shard_map/ppermute | solution.py:350
  53.7 5.5 %collective-permute-start.27 = (bf16[1,2,1,2,16,1152]{5,4,3,2,1,0:T(8,128)(2,1)S(1)}, bf16[1,2,1,2,16,1152]{5,4,3,2,1,0:T(8,128)(2,1)S(1)}, u32[]{:S(2)}, u32[]{:S(2)}) collective-permute-start(bf16[1,2,1,2,16,1152]{5,4,3,2,1,0:T(8,128)(2,1)S(1)} %bitcast.59), channel_id=1, source_target_pairs={{0,16},{1,17},{2,18},{3,19},{4,20},{5,21},{6,22},{7,23},{8,24},{9,... | collective-permute-start | bytes 442376 | tf_op jit(solution)/shard_map/ppermute | solution.py:350
  54.3 6.4 %collective-permute-start.19 = (bf16[1,2,2,1,16,1280]{5,4,3,2,1,0:T(8,128)(2,1)S(1)}, bf16[1,2,2,1,16,1280]{5,4,3,2,1,0:T(8,128)(2,1)S(1)}, u32[]{:S(2)}, u32[]{:S(2)}) collective-permute-start(bf16[1,2,2,1,16,1280]{5,4,3,2,1,0:T(8,128)(2,1)S(1)} %fusion), channel_id=1, source_target_pairs={{0,1},{1,0},{2,3},{3,2},{4,5},{5,4},{6,7},{7,6},{8,9},{9,8},{10,11... | collective-permute-start | bytes 491528 | tf_op jit(solution)/shard_map/ppermute | solution.py:350
  58.6 4.4 %collective-permute-start.24 = (bf16[1,2,1,1,16,1152]{5,4,3,2,1,0:T(8,128)(2,1)S(1)}, bf16[1,2,1,1,16,1152]{5,4,3,2,1,0:T(8,128)(2,1)S(1)}, u32[]{:S(2)}, u32[]{:S(2)}) collective-permute-start(bf16[1,2,1,1,16,1152]{5,4,3,2,1,0:T(8,128)(2,1)S(1)} %fusion.7), channel_id=1, source_target_pairs={{0,16},{1,17},{2,18},{3,19},{4,20},{5,21},{6,22},{7,23},{8,24},{9,... | collective-permute-start | bytes 221192 | tf_op jit(solution)/shard_map/ppermute | solution.py:350
  59.3 5.9 %collective-permute-start.28 = (bf16[1,2,1,1,16,1152]{5,4,3,2,1,0:T(8,128)(2,1)S(1)}, bf16[1,2,1,1,16,1152]{5,4,3,2,1,0:T(8,128)(2,1)S(1)}, u32[]{:S(2)}, u32[]{:S(2)}) collective-permute-start(bf16[1,2,1,1,16,1152]{5,4,3,2,1,0:T(8,128)(2,1)S(1)} %fusion.5), channel_id=1, source_target_pairs={{0,1},{1,0},{2,3},{3,2},{4,5},{5,4},{6,7},{7,6},{8,9},{9,8},{10,11... | collective-permute-start | bytes 221192 | tf_op jit(solution)/shard_map/ppermute | solution.py:350
  60.8 5.4 %collective-permute-start.20 = (bf16[1,2,1,1,16,1280]{5,4,3,2,1,0:T(8,128)(2,1)S(1)}, bf16[1,2,1,1,16,1280]{5,4,3,2,1,0:T(8,128)(2,1)S(1)}, u32[]{:S(2)}, u32[]{:S(2)}) collective-permute-start(bf16[1,2,1,1,16,1280]{5,4,3,2,1,0:T(8,128)(2,1)S(1)} %fusion.3), channel_id=1, source_target_pairs={{0,2},{1,3},{2,0},{3,1},{4,6},{5,7},{6,4},{7,5},{8,10},{9,11},{10,... | collective-permute-start | bytes 245768 | tf_op jit(solution)/shard_map/ppermute | solution.py:350
  63.1 5.4 %collective-permute-start.25 = (bf16[1,1,1,1,16,1152]{5,4,3,2,1,0:T(8,128)(2,1)S(1)}, bf16[1,1,1,1,16,1152]{5,4,3,2,1,0:T(8,128)(2,1)S(1)}, u32[]{:S(2)}, u32[]{:S(2)}) collective-permute-start(bf16[1,1,1,1,16,1152]{5,4,3,2,1,0:T(8,128)(2,1)S(1)} %fusion.22), channel_id=1, source_target_pairs={{0,4},{1,5},{2,6},{3,7},{4,0},{5,1},{6,2},{7,3},{8,12},{9,13},{10,... | collective-permute-start | bytes 110600 | tf_op jit(solution)/shard_map/ppermute | solution.py:350
  65.2 5.3 %collective-permute-start.29 = (bf16[1,1,1,1,16,1152]{5,4,3,2,1,0:T(8,128)(2,1)S(1)}, bf16[1,1,1,1,16,1152]{5,4,3,2,1,0:T(8,128)(2,1)S(1)}, u32[]{:S(2)}, u32[]{:S(2)}) collective-permute-start(bf16[1,1,1,1,16,1152]{5,4,3,2,1,0:T(8,128)(2,1)S(1)} %fusion.16), channel_id=1, source_target_pairs={{0,4},{1,5},{2,6},{3,7},{4,0},{5,1},{6,2},{7,3},{8,12},{9,13},{10,... | collective-permute-start | bytes 110600 | tf_op jit(solution)/shard_map/ppermute | solution.py:350
  66.2 5.0 %collective-permute-start.21 = (bf16[1,1,1,1,16,1280]{5,4,3,2,1,0:T(8,128)(2,1)S(1)}, bf16[1,1,1,1,16,1280]{5,4,3,2,1,0:T(8,128)(2,1)S(1)}, u32[]{:S(2)}, u32[]{:S(2)}) collective-permute-start(bf16[1,1,1,1,16,1280]{5,4,3,2,1,0:T(8,128)(2,1)S(1)} %fusion.10), channel_id=1, source_target_pairs={{0,4},{1,5},{2,6},{3,7},{4,0},{5,1},{6,2},{7,3},{8,12},{9,13},{10,... | collective-permute-start | bytes 122888 | tf_op jit(solution)/shard_map/ppermute | solution.py:350

commit v21 on v17

--- a/solution.py
+++ b/solution.py
@@ -282,8 +282,8 @@
                 (((1,), (1,)), ((), ())),
                 preferred_element_type=F32,
             )
-        back = back.T
-        send_refs[p][...] = back[:per].astype(BF16)
+        back = back.astype(BF16).T
+        send_refs[p][...] = back[:per]
         keep_refs[p][...] = back[per:]
 
 
@@ -294,8 +294,7 @@
     got = pl.pallas_call(
         lambda *refs: back_kernel(bits, edges, low, len(stats), *refs),
         out_shape=[shape((2 * per, cols), BF16)] * 2
-        + [shape(part, BF16) for part in parts]
-        + [shape(part, F32) for part in parts],
+        + [shape(part, BF16) for part in parts] * 2,
         in_specs=[SMEM] + [VMEM] * (len(stats) + 6 + len(small)),
         out_specs=[VMEM] * 8,
         scratch_shapes=[pltpu.VMEM((2, 2 * per, cols), BF16)],

time: 71.9 us -> 71.9 us (level)
  no operation moved by 1% of the time
where the time goes in v21:
time: 71.9 us; the launch traced here: 71.6 us
  starting transfers between devices  34.9 us (49%)
  Pallas kernels  16.1 us (22%)
  waiting for transfers between devices  13.1 us (18%)
  local copies, waits for them, and re-layouts  5.49 us (8%)
  other arithmetic  1.24 us (2%)
  between operations  0.84 us (1%)
    ppermute x30, starting transfers between devices, swap(): return lax.ppermute(value, AXES, [(i, i ^ mask) for i in range(count)])  34.9 us
    ppermute x30, waiting for transfers between devices, swap(): return lax.ppermute(value, AXES, [(i, i ^ mask) for i in range(count)])  13.1 us
    pallas_call x1, Pallas kernels, head_gradient(): pl.pallas_call(head_kernel, grid=(depth // tile,), out_shape=shape((depth...  5.98 us
    pallas_call x1, Pallas kernels, back_rows(): pl.pallas_call(lambda *refs: back_kernel(bits, edges, low, len(stats), *r...  4.35 us
    pallas_call x1, Pallas kernels, far_logits(): pl.pallas_call(lambda *refs: far_kernel(len(pieces), *refs), out_shape=(s...  2.19 us
    dynamic_slice x2, local copies, waits for them, and re-layouts, cut(): return lax.dynamic_slice(value, indices, sizes)  2.13 us
    pallas_call x2, Pallas kernels, near_logits(): pl.pallas_call(near_kernel, out_shape=(shape((per, cols), F32), shape((ST...  1.74 us
  transfers between devices with their start and end apart: 30, of which 12 were waited for; matrix products, arithmetic and copies ran while one was open for 5% of the time, Pallas kernels for 16%

profile of v21, /device:TPU:0, one launch (start us, length us, event | category | flops | bytes accessed | tf_op | source)
XLA Modules:
  0.0 71.6 jit_solution(11459922124705058355)
XLA Ops:
  0.7 0.0 copy-start
  0.7 0.1 pad_add_fusion.2.at_ref
  0.7 0.1 pad_add_fusion
  0.8 1.1 %constant_dynamic-slice_fusion.1 = bf16[24,3584]{1,0:T(8,128)(2,1)S(1)} fusion(bf16[128,3584]{1,0:T(8,128)(2,1)} %refs_8_, u32[]{:T(128)S(6)} %convert_element_type.194), kind=kLoop, calls=%fused_computation.16 | loop fusion | bytes 344068 | tf_op jit(solution)/shard_map/dynamic_slice | solution.py:376
  2.0 0.5 collective-permute-start
  2.5 2.6 %collective-permute-start.1 = (bf16[24,3584]{1,0:T(8,128)(2,1)S(1)}, bf16[24,3584]{1,0:T(8,128)(2,1)S(1)}, u32[]{:S(2)}, u32[]{:S(2)}) collective-permute-start(bf16[24,3584]{1,0:T(8,128)(2,1)S(1)} %constant_dynamic-slice_fusion.1), channel_id=1, source_target_pairs={{0,16},{1,17},{2,18},{3,19},{4,20},{5,21},{6,22},{7,23},{8,24},{9,... | collective-permute-start | bytes 516104 | tf_op jit(solution)/shard_map/ppermute | solution.py:349
  5.0 1.0 %slice.173 = bf16[32,3584]{1,0:T(8,128)(2,1)S(1)} slice(bf16[128,3584]{1,0:T(8,128)(2,1)} %refs_8_), slice={[96:128], [0:3584]} | slice | bytes 458752 | tf_op jit(solution)/shard_map/slice | solution.py:383
  6.0 0.1 collective-permute-start.6
  6.1 1.1 %copy.7 = bf16[128,4,512]{2,0,1:T(8,128)(2,1)S(1)} copy(bf16[128,4,512]{2,1,0:T(4,128)(2,1)} %param.9) | data formatting | bytes 1048576 | tf_op jit(solution)/shard_map/optimization_barrier | solution.py:352
  7.3 0.4 taught_stats.1.refs_11_
  7.6 0.2 collective-permute-start.2
  7.8 1.0 %constant_dynamic-slice_fusion = bf16[24,3584]{1,0:T(8,128)(2,1)S(1)} fusion(bf16[128,3584]{1,0:T(8,128)(2,1)} %refs_8_, u32[]{:T(128)S(6)} %convert_element_type.195), kind=kLoop, calls=%fused_computation.15 | loop fusion | bytes 344068 | tf_op jit(solution)/shard_map/dynamic_slice | solution.py:376
  8.8 1.9 %collective-permute-start.5 = (bf16[24,3584]{1,0:T(8,128)(2,1)S(1)}, bf16[24,3584]{1,0:T(8,128)(2,1)S(1)}, u32[]{:S(2)}, u32[]{:S(2)}) collective-permute-start(bf16[24,3584]{1,0:T(8,128)(2,1)S(1)} %constant_dynamic-slice_fusion), channel_id=1, source_target_pairs={{0,16},{1,17},{2,18},{3,19},{4,20},{5,21},{6,22},{7,23},{8,24},{9,... | collective-permute-start | bytes 516104 | tf_op jit(solution)/shard_map/ppermute | solution.py:349
  10.8 0.0 collective-permute-done.2.refs_12_
  10.8 1.6 %collective-permute-start.4 = (bf16[24,3584]{1,0:T(8,128)(2,1)S(1)}, bf16[24,3584]{1,0:T(8,128)(2,1)S(1)}, u32[]{:S(2)}, u32[]{:S(2)}) collective-permute-start(bf16[24,3584]{1,0:T(8,128)(2,1)S(1)} %collective-permute-done.1.refs_0_.refs_1_), channel_id=1, source_target_pairs={{0,2},{1,3},{2,0},{3,1},{4,6},{5,7},{6,4},{7,5},{8,10},{9,11},{10,... | collective-permute-start | bytes 516104 | tf_op jit(solution)/shard_map/ppermute | solution.py:349
  12.4 1.5 %collective-permute-start.3 = (bf16[24,3584]{1,0:T(8,128)(2,1)S(1)}, bf16[24,3584]{1,0:T(8,128)(2,1)S(1)}, u32[]{:S(2)}, u32[]{:S(2)}) collective-permute-start(bf16[24,3584]{1,0:T(8,128)(2,1)S(1)} %collective-permute-done.1.refs_0_.refs_1_), channel_id=1, source_target_pairs={{0,1},{1,0},{2,3},{3,2},{4,5},{5,4},{6,7},{7,6},{8,9},{9,8},{10,11... | collective-permute-start | bytes 516104 | tf_op jit(solution)/shard_map/ppermute | solution.py:349
  13.9 1.2 %copy-done.1 = bf16[128,3584]{1,0:T(8,128)(2,1)S(1)} copy-done((bf16[128,3584]{1,0:T(8,128)(2,1)S(1)}, bf16[128,3584]{1,0:T(8,128)(2,1)}, u32[]{:S(2)}) %copy-start.1) | copy-done | bytes 917528
  15.1 0.9 %near_logits.2 = (f32[128,512]{1,0:T(8,128)S(1)}, f32[8,128]{1,0:T(8,128)S(1)}) custom-call(bf16[128,3584]{1,0:T(8,128)(2,1)S(1)} %copy-done.1, bf16[3584,512]{1,0:T(8,128)(2,1)S(1)} %copy-done, bf16[24,3584]{1,0:T(8,128)(2,1)S(1)} %collective-permute-done.1.refs_0_.refs_1_), custom_call_target="tpu_custom_call" | custom-call | flops 469762048 | bytes 4587520 | tf_op jit(solution)/shard_map/near_logits/pallas_call | solution.py:109
  15.9 0.0 collective-permute-done.w_ref.refs_7_.refs_2_
  15.9 0.9 %near_logits.3 = (f32[128,512]{1,0:T(8,128)S(1)}, f32[8,128]{1,0:T(8,128)S(1)}) custom-call(bf16[128,3584]{1,0:T(8,128)(2,1)S(1)} %copy-done.1, bf16[3584,512]{1,0:T(8,128)(2,1)S(1)} %collective-permute-done.w_ref.refs_7_.refs_2_, bf16[24,3584]{1,0:T(8,128)(2,1)S(1)} %collective-permute-done.1.refs_0_.refs_1_), custom_call_target="tpu_custom_call" | custom-call | flops 469762048 | bytes 4587520 | tf_op jit(solution)/shard_map/near_logits/pallas_call | solution.py:109
  16.8 1.8 %collective-permute-done.5.refs_4_ = bf16[24,3584]{1,0:T(8,128)(2,1)S(1)} collective-permute-done((bf16[24,3584]{1,0:T(8,128)(2,1)S(1)}, bf16[24,3584]{1,0:T(8,128)(2,1)S(1)}, u32[]{:S(2)}, u32[]{:S(2)}) %collective-permute-start.5) | collective-permute-done | bytes 172064 | tf_op jit(solution)/shard_map/ppermute | solution.py:349
  18.6 1.8 %collective-permute-start.14 = (bf16[2,128,512]{2,1,0:T(8,128)(2,1)S(1)}, bf16[2,128,512]{2,1,0:T(8,128)(2,1)S(1)}, u32[]{:S(2)}, u32[]{:S(2)}) collective-permute-start(bf16[2,128,512]{2,1,0:T(8,128)(2,1)S(1)} %get-tuple-element.88.gone_ref), channel_id=1, source_target_pairs={{0,16},{1,17},{2,18},{3,19},{4,20},{5,21},{6,22},{7,23},{8,24},{9,... | collective-permute-start | bytes 786440 | tf_op jit(solution)/shard_map/ppermute | solution.py:349
  20.5 2.2 %far_logits.1 = (f32[128,512]{1,0:T(8,128)S(1)}, f32[128,512]{1,0:T(8,128)S(1)}, bf16[2,128,3584]{2,1,0:T(8,128)(2,1)S(1)}, f32[2,8,128]{2,1,0:T(8,128)S(1)}, f32[8,128]{1,0:T(8,128)S(1)}) custom-call(s32[4]{0:T(128)S(1)} %get-tuple-element.60.refs_0_, bf16[24,3584]{1,0:T(8,128)(2,1)S(1)} %collective-permute-done.1.refs_0_.refs_1_, ...), custom_call_target="tpu_custom_call" | custom-call | flops 939524096 | bytes 8257536 | tf_op jit(solution)/shard_map/far_logits/pallas_call | solution.py:161
  22.7 0.0 copy-start.3
  22.7 3.6 %collective-permute-start.9 = (f32[2,8,128]{2,1,0:T(8,128)S(1)}, f32[2,8,128]{2,1,0:T(8,128)S(1)}, u32[]{:S(2)}, u32[]{:S(2)}) collective-permute-start(f32[2,8,128]{2,1,0:T(8,128)S(1)} %get-tuple-element.80.refs_0_), channel_id=1, source_target_pairs={{0,6},{1,7},{2,4},{3,5},{4,2},{5,3},{6,0},{7,1},{8,14},{9,15},{10,... | collective-permute-start | bytes 24584 | tf_op jit(solution)/shard_map/ppermute | solution.py:349
  26.3 0.0 collective-permute-start.8
  26.3 0.8 %collective-permute-start.7 = (f32[2,8,128]{2,1,0:T(8,128)S(1)}, f32[2,8,128]{2,1,0:T(8,128)S(1)}, u32[]{:S(2)}, u32[]{:S(2)}) collective-permute-start(f32[2,8,128]{2,1,0:T(8,128)S(1)} %get-tuple-element.80.refs_0_), channel_id=1, source_target_pairs={{0,2},{1,3},{2,0},{3,1},{4,6},{5,7},{6,4},{7,5},{8,10},{9,11},{10,... | collective-permute-start | bytes 24584 | tf_op jit(solution)/shard_map/ppermute | solution.py:349
  27.1 1.1 %collective-permute-done.9.refs_3_ = f32[2,8,128]{2,1,0:T(8,128)S(1)} collective-permute-done((f32[2,8,128]{2,1,0:T(8,128)S(1)}, f32[2,8,128]{2,1,0:T(8,128)S(1)}, u32[]{:S(2)}, u32[]{:S(2)}) %collective-permute-start.9) | collective-permute-done | bytes 8224 | tf_op jit(solution)/shard_map/ppermute | solution.py:349
  28.2 2.7 %collective-permute-done.8.refs_2_ = f32[2,8,128]{2,1,0:T(8,128)S(1)} collective-permute-done((f32[2,8,128]{2,1,0:T(8,128)S(1)}, f32[2,8,128]{2,1,0:T(8,128)S(1)}, u32[]{:S(2)}, u32[]{:S(2)}) %collective-permute-start.8) | collective-permute-done | bytes 8224 | tf_op jit(solution)/shard_map/ppermute | solution.py:349
  30.9 0.1 collective-permute-start.15
  31.0 1.6 %collective-permute-start.12 = (f32[2,8,128]{2,1,0:T(8,128)S(1)}, f32[2,8,128]{2,1,0:T(8,128)S(1)}, u32[]{:S(2)}, u32[]{:S(2)}) collective-permute-start(f32[2,8,128]{2,1,0:T(8,128)S(1)} %merge_stats.1.refs_3_), channel_id=1, source_target_pairs={{0,17},{1,16},{2,19},{3,18},{4,21},{5,20},{6,23},{7,22},{8,25},{9,... | collective-permute-start | bytes 24584 | tf_op jit(solution)/shard_map/ppermute | solution.py:349
  32.6 0.5 collective-permute-start.11
  33.1 1.5 %collective-permute-start.10 = (f32[2,8,128]{2,1,0:T(8,128)S(1)}, f32[2,8,128]{2,1,0:T(8,128)S(1)}, u32[]{:S(2)}, u32[]{:S(2)}) collective-permute-start(f32[2,8,128]{2,1,0:T(8,128)S(1)} %merge_stats.1.refs_3_), channel_id=1, source_target_pairs={{0,16},{1,17},{2,18},{3,19},{4,20},{5,21},{6,22},{7,23},{8,24},{9,... | collective-permute-start | bytes 24584 | tf_op jit(solution)/shard_map/ppermute | solution.py:349
  34.6 1.4 %teacher_rows.1 = (f32[2,128,1024]{2,1,0:T(8,128)S(1)}, f32[2,8,128]{2,1,0:T(8,128)S(1)}) custom-call(s32[2]{0:T(128)S(1)} %pad_add_fusion.2.at_ref, s32[4,1,128]{2,1,0:T(1,128)S(1)} %bitcast.42, bf16[2,128,512]{2,1,0:T(8,128)(2,1)S(1)} %get-tuple-element.87.kept_ref.a0, bf16[2,128,512]{2,1,0:T(8,128)(2,1)S(1)} %collective-permute-done.13.a1, ...), custom_call_target="tpu_custom_call" | custom-call | flops 268435456 | bytes 1572864 | tf_op jit(solution)/shard_map/teacher_rows/pallas_call | solution.py:82
  36.0 0.0 collective-permute-done.12.refs_6_
  36.0 0.2 collective-permute-done.11.refs_5_
  36.2 0.5 collective-permute-done.10.refs_4_
  36.7 4.4 %back_rows.1 = (bf16[256,512]{1,0:T(8,128)(2,1)S(1)}, bf16[256,512]{1,0:T(8,128)(2,1)S(1)}, bf16[128,1152]{1,0:T(8,128)(2,1)S(1)}, bf16[128,1152]{1,0:T(8,128)(2...) custom-call(s32[4]{0:T(128)S(1)} %get-tuple-element.55.refs_0_, ...), custom_call_target="tpu_custom_call" | custom-call | flops 1879048192 | bytes 7340032 | tf_op jit(solution)/shard_map/back_rows/pallas_call | solution.py:294
  41.1 0.1 collective-permute-start.16
  41.1 0.5 collective-permute-start.17
  41.6 0.0 collective-permute-start.26
  41.6 1.5 %collective-permute-start.18 = (bf16[128,1152]{1,0:T(8,128)(2,1)S(1)}, bf16[128,1152]{1,0:T(8,128)(2,1)S(1)}, u32[]{:S(2)}, u32[]{:S(2)}) collective-permute-start(bf16[128,1152]{1,0:T(8,128)(2,1)S(1)} %get-tuple-element.97), channel_id=1, source_target_pairs={{0,16},{1,17},{2,18},{3,19},{4,20},{5,21},{6,22},{7,23},{8,24},{9,... | collective-permute-start | bytes 884744 | tf_op jit(solution)/shard_map/ppermute | solution.py:349
  43.1 1.5 %collective-permute-start.22 = (bf16[128,1152]{1,0:T(8,128)(2,1)S(1)}, bf16[128,1152]{1,0:T(8,128)(2,1)S(1)}, u32[]{:S(2)}, u32[]{:S(2)}) collective-permute-start(bf16[128,1152]{1,0:T(8,128)(2,1)S(1)} %get-tuple-element.101), channel_id=1, source_target_pairs={{0,1},{1,0},{2,3},{3,2},{4,5},{5,4},{6,7},{7,6},{8,9},{9,8},{10,11... | collective-permute-start | bytes 884744 | tf_op jit(solution)/shard_map/ppermute | solution.py:349
  44.7 0.6 collective-permute-done.17.theirs_ref
  45.3 0.0 collective-permute-done.16.core_ref
  45.3 6.0 %head_gradient.1 = bf16[3584,512]{1,0:T(8,128)(2,1)} custom-call(bf16[2,128,3584]{2,1,0:T(8,128)(2,1)S(1)} %get-tuple-element.95.rows_ref, bf16[2,128,3584]{2,1,0:T(8,128)(2,1)S(1)} %collective-permute-done.16.core_ref, bf16[256,512]{1,0:T(8,128)(2,1)S(1)} %get-tuple-element.96.mine_ref, bf16[256,512]{1,0:T(8,128)(2,1)S(1)} %collective-permute-done.17.theirs_ref), custom_call_target="tpu_custom_call" | custom-call | flops 1879048192 | bytes 7340032 | tf_op jit(solution)/shard_map/head_gradient/pallas_call | solution.py:322
  51.3 0.0 collective-permute-done.18
  51.3 0.6 collective-permute-done.22
  51.8 0.0 collective-permute-done.26
  51.9 1.6 %collective-permute-start.19 = (bf16[1,2,2,1,16,1152]{5,4,3,2,1,0:T(8,128)(2,1)S(1)}, bf16[1,2,2,1,16,1152]{5,4,3,2,1,0:T(8,128)(2,1)S(1)}, u32[]{:S(2)}, u32[]{:S(2)}) collective-permute-start(bf16[1,2,2,1,16,1152]{5,4,3,2,1,0:T(8,128)(2,1)S(1)} %add_convert_fusion.2), channel_id=1, source_target_pairs={{0,1},{1,0},{2,3},{3,2},{4,5},{5,4},{6,7},{7,6},{8,9},{9,8},{10,11... | collective-permute-start | bytes 442376 | tf_op jit(solution)/shard_map/ppermute | solution.py:349
  53.6 1.8 %collective-permute-start.23 = (bf16[2,2,1,1,16,1152]{5,4,3,2,1,0:T(8,128)(2,1)S(1)}, bf16[2,2,1,1,16,1152]{5,4,3,2,1,0:T(8,128)(2,1)S(1)}, u32[]{:S(2)}, u32[]{:S(2)}) collective-permute-start(bf16[2,2,1,1,16,1152]{5,4,3,2,1,0:T(8,128)(2,1)S(1)} %add_convert_fusion.1), channel_id=1, source_target_pairs={{0,2},{1,3},{2,0},{3,1},{4,6},{5,7},{6,4},{7,5},{8,10},{9,11},{10,... | collective-permute-start | bytes 442376 | tf_op jit(solution)/shard_map/ppermute | solution.py:349
  55.4 0.5 collective-permute-start.27
  55.9 1.4 %collective-permute-done.19 = bf16[1,2,2,1,16,1152]{5,4,3,2,1,0:T(8,128)(2,1)S(1)} collective-permute-done((bf16[1,2,2,1,16,1152]{5,4,3,2,1,0:T(8,128)(2,1)S(1)}, bf16[1,2,2,1,16,1152]{5,4,3,2,1,0:T(8,128)(2,1)S(1)}, u32[]{:S(2)}, u32[]{:S(2)}) %collective-permute-start.19) | collective-permute-done | bytes 147488 | tf_op jit(solution)/shard_map/ppermute | solution.py:349
  57.4 1.6 %collective-permute-start.20 = (bf16[1,2,1,1,16,1152]{5,4,3,2,1,0:T(8,128)(2,1)S(1)}, bf16[1,2,1,1,16,1152]{5,4,3,2,1,0:T(8,128)(2,1)S(1)}, u32[]{:S(2)}, u32[]{:S(2)}) collective-permute-start(bf16[1,2,1,1,16,1152]{5,4,3,2,1,0:T(8,128)(2,1)S(1)} %add_convert_fusion.5), channel_id=1, source_target_pairs={{0,2},{1,3},{2,0},{3,1},{4,6},{5,7},{6,4},{7,5},{8,10},{9,11},{10,... | collective-permute-start | bytes 221192 | tf_op jit(solution)/shard_map/ppermute | solution.py:349
  59.0 1.3 %collective-permute-start.24 = (bf16[1,2,1,1,16,1152]{5,4,3,2,1,0:T(8,128)(2,1)S(1)}, bf16[1,2,1,1,16,1152]{5,4,3,2,1,0:T(8,128)(2,1)S(1)}, u32[]{:S(2)}, u32[]{:S(2)}) collective-permute-start(bf16[1,2,1,1,16,1152]{5,4,3,2,1,0:T(8,128)(2,1)S(1)} %add_convert_fusion.4), channel_id=1, source_target_pairs={{0,16},{1,17},{2,18},{3,19},{4,20},{5,21},{6,22},{7,23},{8,24},{9,... | collective-permute-start | bytes 221192 | tf_op jit(solution)/shard_map/ppermute | solution.py:349
  60.3 1.0 %collective-permute-done.27 = bf16[1,2,1,2,16,1280]{5,4,3,2,1,0:T(8,128)(2,1)S(1)} collective-permute-done((bf16[1,2,1,2,16,1280]{5,4,3,2,1,0:T(8,128)(2,1)S(1)}, bf16[1,2,1,2,16,1280]{5,4,3,2,1,0:T(8,128)(2,1)S(1)}, u32[]{:S(2)}, u32[]{:S(2)}) %collective-permute-start.27) | collective-permute-done | bytes 163872 | tf_op jit(solution)/shard_map/ppermute | solution.py:349
  61.4 0.4 collective-permute-start.28
  61.9 2.1 %collective-permute-start.21 = (bf16[1,1,1,1,16,1152]{5,4,3,2,1,0:T(8,128)(2,1)S(1)}, bf16[1,1,1,1,16,1152]{5,4,3,2,1,0:T(8,128)(2,1)S(1)}, u32[]{:S(2)}, u32[]{:S(2)}) collective-permute-start(bf16[1,1,1,1,16,1152]{5,4,3,2,1,0:T(8,128)(2,1)S(1)} %add_convert_fusion.8), channel_id=1, source_target_pairs={{0,4},{1,5},{2,6},{3,7},{4,0},{5,1},{6,2},{7,3},{8,12},{9,13},{10,... | collective-permute-start | bytes 110600 | tf_op jit(solution)/shard_map/ppermute | solution.py:349
  64.0 1.6 %collective-permute-start.25 = (bf16[1,1,1,1,16,1152]{5,4,3,2,1,0:T(8,128)(2,1)S(1)}, bf16[1,1,1,1,16,1152]{5,4,3,2,1,0:T(8,128)(2,1)S(1)}, u32[]{:S(2)}, u32[]{:S(2)}) collective-permute-start(bf16[1,1,1,1,16,1152]{5,4,3,2,1,0:T(8,128)(2,1)S(1)} %add_convert_fusion.7), channel_id=1, source_target_pairs={{0,4},{1,5},{2,6},{3,7},{4,0},{5,1},{6,2},{7,3},{8,12},{9,13},{10,... | collective-permute-start | bytes 110600 | tf_op jit(solution)/shard_map/ppermute | solution.py:349
  65.6 0.3 collective-permute-done.28
  65.9 2.1 %collective-permute-start.29 = (bf16[1,1,1,1,16,1280]{5,4,3,2,1,0:T(8,128)(2,1)S(1)}, bf16[1,1,1,1,16,1280]{5,4,3,2,1,0:T(8,128)(2,1)S(1)}, u32[]{:S(2)}, u32[]{:S(2)}) collective-permute-start(bf16[1,1,1,1,16,1280]{5,4,3,2,1,0:T(8,128)(2,1)S(1)} %add_convert_fusion.6), channel_id=1, source_target_pairs={{0,4},{1,5},{2,6},{3,7},{4,0},{5,1},{6,2},{7,3},{8,12},{9,13},{10,... | collective-permute-start | bytes 122888 | tf_op jit(solution)/shard_map/ppermute | solution.py:349
  68.0 0.9 %collective-permute-done.25 = bf16[1,1,1,1,16,1152]{5,4,3,2,1,0:T(8,128)(2,1)S(1)} collective-permute-done((bf16[1,1,1,1,16,1152]{5,4,3,2,1,0:T(8,128)(2,1)S(1)}, bf16[1,1,1,1,16,1152]{5,4,3,2,1,0:T(8,128)(2,1)S(1)}, u32[]{:S(2)}, u32[]{:S(2)}) %collective-permute-start.25) | collective-permute-done | bytes 36896 | tf_op jit(solution)/shard_map/ppermute | solution.py:349
  68.9 2.0 %collective-permute-done.29 = bf16[1,1,1,1,16,1280]{5,4,3,2,1,0:T(8,128)(2,1)S(1)} collective-permute-done((bf16[1,1,1,1,16,1280]{5,4,3,2,1,0:T(8,128)(2,1)S(1)}, bf16[1,1,1,1,16,1280]{5,4,3,2,1,0:T(8,128)(2,1)S(1)}, u32[]{:S(2)}, u32[]{:S(2)}) %collective-permute-start.29) | collective-permute-done | bytes 40992 | tf_op jit(solution)/shard_map/ppermute | solution.py:349
  70.9 0.7 maximum_bitcast_fusion
  (36 shorter events, 0.5 us)
Async XLA Ops:
  0.7 13.2 %copy-start = (bf16[3584,512]{1,0:T(8,128)(2,1)S(1)}, bf16[3584,512]{1,0:T(8,128)(2,1)}, u32[]{:S(2)}) copy-start(bf16[3584,512]{1,0:T(8,128)(2,1)} %refs_1_) | copy-start | bytes 11010052
  2.0 14.0 %collective-permute-start = (bf16[3584,512]{1,0:T(8,128)(2,1)}, bf16[3584,512]{1,0:T(8,128)(2,1)S(1)}, u32[]{:S(2)}, u32[]{:S(2)}) collective-permute-start(bf16[3584,512]{1,0:T(8,128)(2,1)} %refs_1_), channel_id=1, source_target_pairs={{0,8},{1,9},{2,10},{3,11},{4,12},{5,13},{6,14},{7,15},{8,0},{9,1},... | collective-permute-start | bytes 11010056 | tf_op jit(solution)/shard_map/ppermute | solution.py:349
  2.5 8.3 %collective-permute-start.1 = (bf16[24,3584]{1,0:T(8,128)(2,1)S(1)}, bf16[24,3584]{1,0:T(8,128)(2,1)S(1)}, u32[]{:S(2)}, u32[]{:S(2)}) collective-permute-start(bf16[24,3584]{1,0:T(8,128)(2,1)S(1)} %constant_dynamic-slice_fusion.1), channel_id=1, source_target_pairs={{0,16},{1,17},{2,18},{3,19},{4,20},{5,21},{6,22},{7,23},{8,24},{9,... | collective-permute-start | bytes 516104 | tf_op jit(solution)/shard_map/ppermute | solution.py:349
  6.0 12.6 %collective-permute-start.6 = (bf16[32,3584]{1,0:T(8,128)(2,1)S(1)}, bf16[32,3584]{1,0:T(8,128)(2,1)S(1)}, u32[]{:S(2)}, u32[]{:S(2)}) collective-permute-start(bf16[32,3584]{1,0:T(8,128)(2,1)S(1)} %slice.173), channel_id=1, source_target_pairs={{0,16},{1,17},{2,18},{3,19},{4,20},{5,21},{6,22},{7,23},{8,24},{9,... | collective-permute-start | bytes 688136 | tf_op jit(solution)/shard_map/ppermute | solution.py:349
  7.6 3.1 %collective-permute-start.2 = (f32[8,128]{1,0:T(8,128)S(1)}, f32[8,128]{1,0:T(8,128)S(1)}, u32[]{:S(2)}, u32[]{:S(2)}) collective-permute-start(f32[8,128]{1,0:T(8,128)S(1)} %taught_stats.1.refs_11_), channel_id=1, source_target_pairs={{0,8},{1,9},{2,10},{3,11},{4,12},{5,13},{6,14},{7,15},{8,0},{9,1},... | collective-permute-start | bytes 12296 | tf_op jit(solution)/shard_map/ppermute | solution.py:349
  7.8 12.6 %copy-start.4 = (s32[128]{0:T(128)S(1)}, s32[128]{0:T(128)}, u32[]{:S(2)}) copy-start(s32[128]{0:T(128)} %param.6) | copy-start | bytes 1540
  8.8 9.8 %collective-permute-start.5 = (bf16[24,3584]{1,0:T(8,128)(2,1)S(1)}, bf16[24,3584]{1,0:T(8,128)(2,1)S(1)}, u32[]{:S(2)}, u32[]{:S(2)}) collective-permute-start(bf16[24,3584]{1,0:T(8,128)(2,1)S(1)} %constant_dynamic-slice_fusion), channel_id=1, source_target_pairs={{0,16},{1,17},{2,18},{3,19},{4,20},{5,21},{6,22},{7,23},{8,24},{9,... | collective-permute-start | bytes 516104 | tf_op jit(solution)/shard_map/ppermute | solution.py:349
  10.8 7.8 %collective-permute-start.4 = (bf16[24,3584]{1,0:T(8,128)(2,1)S(1)}, bf16[24,3584]{1,0:T(8,128)(2,1)S(1)}, u32[]{:S(2)}, u32[]{:S(2)}) collective-permute-start(bf16[24,3584]{1,0:T(8,128)(2,1)S(1)} %collective-permute-done.1.refs_0_.refs_1_), channel_id=1, source_target_pairs={{0,2},{1,3},{2,0},{3,1},{4,6},{5,7},{6,4},{7,5},{8,10},{9,11},{10,... | collective-permute-start | bytes 516104 | tf_op jit(solution)/shard_map/ppermute | solution.py:349
  12.4 6.3 %collective-permute-start.3 = (bf16[24,3584]{1,0:T(8,128)(2,1)S(1)}, bf16[24,3584]{1,0:T(8,128)(2,1)S(1)}, u32[]{:S(2)}, u32[]{:S(2)}) collective-permute-start(bf16[24,3584]{1,0:T(8,128)(2,1)S(1)} %collective-permute-done.1.refs_0_.refs_1_), channel_id=1, source_target_pairs={{0,1},{1,0},{2,3},{3,2},{4,5},{5,4},{6,7},{7,6},{8,9},{9,8},{10,11... | collective-permute-start | bytes 516104 | tf_op jit(solution)/shard_map/ppermute | solution.py:349
  13.9 1.2 %copy-start.1 = (bf16[128,3584]{1,0:T(8,128)(2,1)S(1)}, bf16[128,3584]{1,0:T(8,128)(2,1)}, u32[]{:S(2)}) copy-start(bf16[128,3584]{1,0:T(8,128)(2,1)} %refs_8_) | copy-start | bytes 2752516
  15.1 5.4 %copy-start.2 = (bf16[128,3584]{1,0:T(8,128)(2,1)S(1)}, bf16[128,3584]{1,0:T(8,128)(2,1)}, u32[]{:S(2)}) copy-start(bf16[128,3584]{1,0:T(8,128)(2,1)} %refs_8_) | copy-start | bytes 2752516
  18.6 12.3 %collective-permute-start.14 = (bf16[2,128,512]{2,1,0:T(8,128)(2,1)S(1)}, bf16[2,128,512]{2,1,0:T(8,128)(2,1)S(1)}, u32[]{:S(2)}, u32[]{:S(2)}) collective-permute-start(bf16[2,128,512]{2,1,0:T(8,128)(2,1)S(1)} %get-tuple-element.88.gone_ref), channel_id=1, source_target_pairs={{0,16},{1,17},{2,18},{3,19},{4,20},{5,21},{6,22},{7,23},{8,24},{9,... | collective-permute-start | bytes 786440 | tf_op jit(solution)/shard_map/ppermute | solution.py:349
  22.7 11.9 %copy-start.3 = (s32[512]{0:T(512)S(1)}, s32[512]{0:T(512)}, u32[]{:S(2)}) copy-start(s32[512]{0:T(512)} %param.7) | copy-start | bytes 6148
  22.7 5.5 %collective-permute-start.9 = (f32[2,8,128]{2,1,0:T(8,128)S(1)}, f32[2,8,128]{2,1,0:T(8,128)S(1)}, u32[]{:S(2)}, u32[]{:S(2)}) collective-permute-start(f32[2,8,128]{2,1,0:T(8,128)S(1)} %get-tuple-element.80.refs_0_), channel_id=1, source_target_pairs={{0,6},{1,7},{2,4},{3,5},{4,2},{5,3},{6,0},{7,1},{8,14},{9,15},{10,... | collective-permute-start | bytes 24584 | tf_op jit(solution)/shard_map/ppermute | solution.py:349
  26.3 4.5 %collective-permute-start.8 = (f32[2,8,128]{2,1,0:T(8,128)S(1)}, f32[2,8,128]{2,1,0:T(8,128)S(1)}, u32[]{:S(2)}, u32[]{:S(2)}) collective-permute-start(f32[2,8,128]{2,1,0:T(8,128)S(1)} %get-tuple-element.80.refs_0_), channel_id=1, source_target_pairs={{0,4},{1,5},{2,6},{3,7},{4,0},{5,1},{6,2},{7,3},{8,12},{9,13},{10,... | collective-permute-start | bytes 24584 | tf_op jit(solution)/shard_map/ppermute | solution.py:349
  26.3 4.5 %collective-permute-start.7 = (f32[2,8,128]{2,1,0:T(8,128)S(1)}, f32[2,8,128]{2,1,0:T(8,128)S(1)}, u32[]{:S(2)}, u32[]{:S(2)}) collective-permute-start(f32[2,8,128]{2,1,0:T(8,128)S(1)} %get-tuple-element.80.refs_0_), channel_id=1, source_target_pairs={{0,2},{1,3},{2,0},{3,1},{4,6},{5,7},{6,4},{7,5},{8,10},{9,11},{10,... | collective-permute-start | bytes 24584 | tf_op jit(solution)/shard_map/ppermute | solution.py:349
  27.1 7.4 %collective-permute-start.13 = (bf16[2,128,512]{2,1,0:T(8,128)(2,1)S(1)}, bf16[2,128,512]{2,1,0:T(8,128)(2,1)S(1)}, u32[]{:S(2)}, u32[]{:S(2)}) collective-permute-start(bf16[2,128,512]{2,1,0:T(8,128)(2,1)S(1)} %get-tuple-element.87.kept_ref.a0), channel_id=1, source_target_pairs={{0,8},{1,9},{2,10},{3,11},{4,12},{5,13},{6,14},{7,15},{8,0},{9,1},... | collective-permute-start | bytes 786440 | tf_op jit(solution)/shard_map/ppermute | solution.py:349
  30.9 3.6 %collective-permute-start.15 = (bf16[2,128,512]{2,1,0:T(8,128)(2,1)S(1)}, bf16[2,128,512]{2,1,0:T(8,128)(2,1)S(1)}, u32[]{:S(2)}, u32[]{:S(2)}) collective-permute-start(bf16[2,128,512]{2,1,0:T(8,128)(2,1)S(1)} %collective-permute-done.14.a2), channel_id=1, source_target_pairs={{0,8},{1,9},{2,10},{3,11},{4,12},{5,13},{6,14},{7,15},{8,0},{9,1},... | collective-permute-start | bytes 786440 | tf_op jit(solution)/shard_map/ppermute | solution.py:349
  31.0 5.0 %collective-permute-start.12 = (f32[2,8,128]{2,1,0:T(8,128)S(1)}, f32[2,8,128]{2,1,0:T(8,128)S(1)}, u32[]{:S(2)}, u32[]{:S(2)}) collective-permute-start(f32[2,8,128]{2,1,0:T(8,128)S(1)} %merge_stats.1.refs_3_), channel_id=1, source_target_pairs={{0,17},{1,16},{2,19},{3,18},{4,21},{5,20},{6,23},{7,22},{8,25},{9,... | collective-permute-start | bytes 24584 | tf_op jit(solution)/shard_map/ppermute | solution.py:349
  32.6 3.7 %collective-permute-start.11 = (f32[2,8,128]{2,1,0:T(8,128)S(1)}, f32[2,8,128]{2,1,0:T(8,128)S(1)}, u32[]{:S(2)}, u32[]{:S(2)}) collective-permute-start(f32[2,8,128]{2,1,0:T(8,128)S(1)} %merge_stats.1.refs_3_), channel_id=1, source_target_pairs={{0,1},{1,0},{2,3},{3,2},{4,5},{5,4},{6,7},{7,6},{8,9},{9,8},{10,11... | collective-permute-start | bytes 24584 | tf_op jit(solution)/shard_map/ppermute | solution.py:349
  33.1 3.7 %collective-permute-start.10 = (f32[2,8,128]{2,1,0:T(8,128)S(1)}, f32[2,8,128]{2,1,0:T(8,128)S(1)}, u32[]{:S(2)}, u32[]{:S(2)}) collective-permute-start(f32[2,8,128]{2,1,0:T(8,128)S(1)} %merge_stats.1.refs_3_), channel_id=1, source_target_pairs={{0,16},{1,17},{2,18},{3,19},{4,20},{5,21},{6,22},{7,23},{8,24},{9,... | collective-permute-start | bytes 24584 | tf_op jit(solution)/shard_map/ppermute | solution.py:349
  41.1 4.2 %collective-permute-start.16 = (bf16[2,128,3584]{2,1,0:T(8,128)(2,1)S(1)}, bf16[2,128,3584]{2,1,0:T(8,128)(2,1)S(1)}, u32[]{:S(2)}, u32[]{:S(2)}) collective-permute-start(bf16[2,128,3584]{2,1,0:T(8,128)(2,1)S(1)} %get-tuple-element.95.rows_ref), channel_id=1, source_target_pairs={{0,8},{1,9},{2,10},{3,11},{4,12},{5,13},{6,14},{7,15},{8,0},{9,1},... | collective-permute-start | bytes 5505032 | tf_op jit(solution)/shard_map/ppermute | solution.py:349
  41.1 4.1 %collective-permute-start.17 = (bf16[256,512]{1,0:T(8,128)(2,1)S(1)}, bf16[256,512]{1,0:T(8,128)(2,1)S(1)}, u32[]{:S(2)}, u32[]{:S(2)}) collective-permute-start(bf16[256,512]{1,0:T(8,128)(2,1)S(1)} %get-tuple-element.94), channel_id=1, source_target_pairs={{0,8},{1,9},{2,10},{3,11},{4,12},{5,13},{6,14},{7,15},{8,0},{9,1},... | collective-permute-start | bytes 786440 | tf_op jit(solution)/shard_map/ppermute | solution.py:349
  41.6 10.2 %collective-permute-start.26 = (bf16[128,1280]{1,0:T(8,128)(2,1)S(1)}, bf16[128,1280]{1,0:T(8,128)(2,1)S(1)}, u32[]{:S(2)}, u32[]{:S(2)}) collective-permute-start(bf16[128,1280]{1,0:T(8,128)(2,1)S(1)} %get-tuple-element.105), channel_id=1, source_target_pairs={{0,2},{1,3},{2,0},{3,1},{4,6},{5,7},{6,4},{7,5},{8,10},{9,11},{10,... | collective-permute-start | bytes 983048 | tf_op jit(solution)/shard_map/ppermute | solution.py:349
  41.6 9.6 %collective-permute-start.18 = (bf16[128,1152]{1,0:T(8,128)(2,1)S(1)}, bf16[128,1152]{1,0:T(8,128)(2,1)S(1)}, u32[]{:S(2)}, u32[]{:S(2)}) collective-permute-start(bf16[128,1152]{1,0:T(8,128)(2,1)S(1)} %get-tuple-element.97), channel_id=1, source_target_pairs={{0,16},{1,17},{2,18},{3,19},{4,20},{5,21},{6,22},{7,23},{8,24},{9,... | collective-permute-start | bytes 884744 | tf_op jit(solution)/shard_map/ppermute | solution.py:349
  43.1 8.7 %collective-permute-start.22 = (bf16[128,1152]{1,0:T(8,128)(2,1)S(1)}, bf16[128,1152]{1,0:T(8,128)(2,1)S(1)}, u32[]{:S(2)}, u32[]{:S(2)}) collective-permute-start(bf16[128,1152]{1,0:T(8,128)(2,1)S(1)} %get-tuple-element.101), channel_id=1, source_target_pairs={{0,1},{1,0},{2,3},{3,2},{4,5},{5,4},{6,7},{7,6},{8,9},{9,8},{10,11... | collective-permute-start | bytes 884744 | tf_op jit(solution)/shard_map/ppermute | solution.py:349
  51.9 5.4 %collective-permute-start.19 = (bf16[1,2,2,1,16,1152]{5,4,3,2,1,0:T(8,128)(2,1)S(1)}, bf16[1,2,2,1,16,1152]{5,4,3,2,1,0:T(8,128)(2,1)S(1)}, u32[]{:S(2)}, u32[]{:S(2)}) collective-permute-start(bf16[1,2,2,1,16,1152]{5,4,3,2,1,0:T(8,128)(2,1)S(1)} %add_convert_fusion.2), channel_id=1, source_target_pairs={{0,1},{1,0},{2,3},{3,2},{4,5},{5,4},{6,7},{7,6},{8,9},{9,8},{10,11... | collective-permute-start | bytes 442376 | tf_op jit(solution)/shard_map/ppermute | solution.py:349
  53.6 5.4 %collective-permute-start.23 = (bf16[2,2,1,1,16,1152]{5,4,3,2,1,0:T(8,128)(2,1)S(1)}, bf16[2,2,1,1,16,1152]{5,4,3,2,1,0:T(8,128)(2,1)S(1)}, u32[]{:S(2)}, u32[]{:S(2)}) collective-permute-start(bf16[2,2,1,1,16,1152]{5,4,3,2,1,0:T(8,128)(2,1)S(1)} %add_convert_fusion.1), channel_id=1, source_target_pairs={{0,2},{1,3},{2,0},{3,1},{4,6},{5,7},{6,4},{7,5},{8,10},{9,11},{10,... | collective-permute-start | bytes 442376 | tf_op jit(solution)/shard_map/ppermute | solution.py:349
  55.4 5.9 %collective-permute-start.27 = (bf16[1,2,1,2,16,1280]{5,4,3,2,1,0:T(8,128)(2,1)S(1)}, bf16[1,2,1,2,16,1280]{5,4,3,2,1,0:T(8,128)(2,1)S(1)}, u32[]{:S(2)}, u32[]{:S(2)}) collective-permute-start(bf16[1,2,1,2,16,1280]{5,4,3,2,1,0:T(8,128)(2,1)S(1)} %bitcast.59), channel_id=1, source_target_pairs={{0,16},{1,17},{2,18},{3,19},{4,20},{5,21},{6,22},{7,23},{8,24},{9,... | collective-permute-start | bytes 491528 | tf_op jit(solution)/shard_map/ppermute | solution.py:349
  57.4 4.4 %collective-permute-start.20 = (bf16[1,2,1,1,16,1152]{5,4,3,2,1,0:T(8,128)(2,1)S(1)}, bf16[1,2,1,1,16,1152]{5,4,3,2,1,0:T(8,128)(2,1)S(1)}, u32[]{:S(2)}, u32[]{:S(2)}) collective-permute-start(bf16[1,2,1,1,16,1152]{5,4,3,2,1,0:T(8,128)(2,1)S(1)} %add_convert_fusion.5), channel_id=1, source_target_pairs={{0,2},{1,3},{2,0},{3,1},{4,6},{5,7},{6,4},{7,5},{8,10},{9,11},{10,... | collective-permute-start | bytes 221192 | tf_op jit(solution)/shard_map/ppermute | solution.py:349
  59.0 4.9 %collective-permute-start.24 = (bf16[1,2,1,1,16,1152]{5,4,3,2,1,0:T(8,128)(2,1)S(1)}, bf16[1,2,1,1,16,1152]{5,4,3,2,1,0:T(8,128)(2,1)S(1)}, u32[]{:S(2)}, u32[]{:S(2)}) collective-permute-start(bf16[1,2,1,1,16,1152]{5,4,3,2,1,0:T(8,128)(2,1)S(1)} %add_convert_fusion.4), channel_id=1, source_target_pairs={{0,16},{1,17},{2,18},{3,19},{4,20},{5,21},{6,22},{7,23},{8,24},{9,... | collective-permute-start | bytes 221192 | tf_op jit(solution)/shard_map/ppermute | solution.py:349
  61.4 4.5 %collective-permute-start.28 = (bf16[1,2,1,1,16,1280]{5,4,3,2,1,0:T(8,128)(2,1)S(1)}, bf16[1,2,1,1,16,1280]{5,4,3,2,1,0:T(8,128)(2,1)S(1)}, u32[]{:S(2)}, u32[]{:S(2)}) collective-permute-start(bf16[1,2,1,1,16,1280]{5,4,3,2,1,0:T(8,128)(2,1)S(1)} %add_convert_fusion.3), channel_id=1, source_target_pairs={{0,1},{1,0},{2,3},{3,2},{4,5},{5,4},{6,7},{7,6},{8,9},{9,8},{10,11... | collective-permute-start | bytes 245768 | tf_op jit(solution)/shard_map/ppermute | solution.py:349
  61.9 6.1 %collective-permute-start.21 = (bf16[1,1,1,1,16,1152]{5,4,3,2,1,0:T(8,128)(2,1)S(1)}, bf16[1,1,1,1,16,1152]{5,4,3,2,1,0:T(8,128)(2,1)S(1)}, u32[]{:S(2)}, u32[]{:S(2)}) collective-permute-start(bf16[1,1,1,1,16,1152]{5,4,3,2,1,0:T(8,128)(2,1)S(1)} %add_convert_fusion.8), channel_id=1, source_target_pairs={{0,4},{1,5},{2,6},{3,7},{4,0},{5,1},{6,2},{7,3},{8,12},{9,13},{10,... | collective-permute-start | bytes 110600 | tf_op jit(solution)/shard_map/ppermute | solution.py:349
  64.0 4.9 %collective-permute-start.25 = (bf16[1,1,1,1,16,1152]{5,4,3,2,1,0:T(8,128)(2,1)S(1)}, bf16[1,1,1,1,16,1152]{5,4,3,2,1,0:T(8,128)(2,1)S(1)}, u32[]{:S(2)}, u32[]{:S(2)}) collective-permute-start(bf16[1,1,1,1,16,1152]{5,4,3,2,1,0:T(8,128)(2,1)S(1)} %add_convert_fusion.7), channel_id=1, source_target_pairs={{0,4},{1,5},{2,6},{3,7},{4,0},{5,1},{6,2},{7,3},{8,12},{9,13},{10,... | collective-permute-start | bytes 110600 | tf_op jit(solution)/shard_map/ppermute | solution.py:349
  65.9 5.0 %collective-permute-start.29 = (bf16[1,1,1,1,16,1280]{5,4,3,2,1,0:T(8,128)(2,1)S(1)}, bf16[1,1,1,1,16,1280]{5,4,3,2,1,0:T(8,128)(2,1)S(1)}, u32[]{:S(2)}, u32[]{:S(2)}) collective-permute-start(bf16[1,1,1,1,16,1280]{5,4,3,2,1,0:T(8,128)(2,1)S(1)} %add_convert_fusion.6), channel_id=1, source_target_pairs={{0,4},{1,5},{2,6},{3,7},{4,0},{5,1},{6,2},{7,3},{8,12},{9,13},{10,... | collective-permute-start | bytes 122888 | tf_op jit(solution)/shard_map/ppermute | solution.py:349
